TPU v7x, 32 devices: a whole 2x2x4 slice. The times are simulated.
32 devices in a mesh: stream: 8 (over y, x, core), azim: 4 (over z).
Axes of the slice: x: 2, y: 2, z: 4, core: 2. Of those that a mesh axis runs over, the one named last changes fastest.
Arguments:
- start_vector: bfloat16 [32, 4, 8, 64, 128], P('stream', 'azim'), may hold values from -6 to 6
- trace_blocks: bfloat16 [32, 4, 8, 64, 768], P('stream', 'azim'), may hold values from -0.21875 to 0.21875
- neighbour: int32 [4, 8, 12], P('azim'), may hold values from 0 to 71
Outputs:
- krylov_basis: bfloat16 [4, 32, 4, 8, 64, 128], P(None, 'stream', 'azim')
Inputs may be any that keep to these rules, and one draw needn't show every extreme that they name: `neighbour`: entry e names column offsets (e // 24 - 1, (e // 8) % 3 - 1) and slot e % 8; the list is the same for every stream column.
All inputs are finite; a program needn't handle non-finite values.
Results may differ from a plain program's by a relative error of at most 0.0055.
Values may be sent and summed in bfloat16 or wider, within the bound.
No kernel may reach another device: no remote copies, remote signals or barrier semaphores. Data moves between devices by JAX's collectives and lax.ppermute only.
A program may use at most 64 MiB of HBM per device.

v0:
```python
import jax
import jax.numpy as jnp
from jax import lax
from jax.sharding import PartitionSpec as P

STEPS = 4


def with_halo(block, sides, width):
    for axis, dim in sides:
        count = lax.axis_size(axis)
        forward = [(i, i + 1) for i in range(count - 1)]
        forward.append((count - 1, 0))
        backward = [(target, source) for source, target in forward]
        low = lax.ppermute(
            lax.slice_in_dim(block, block.shape[dim] - width, None, axis=dim), axis, forward
        )
        high = lax.ppermute(lax.slice_in_dim(block, 0, width, axis=dim), axis, backward)
        block = jnp.concatenate([low, block, high], axis=dim)
    return block


def apply_rows(padded, blocks, neighbour, rows):
    column_count = padded.shape[1] - 2
    face_count = padded.shape[2]
    width = padded.shape[3]
    rhs_count = padded.shape[4]
    pieces = []
    for stream_shift in range(3):
        for azim_shift in range(3):
            pieces.append(
                padded[stream_shift : stream_shift + rows, azim_shift : azim_shift + column_count]
            )
    window = jnp.stack(pieces, axis=2)
    window = window.reshape(rows, column_count, 9 * face_count, width * rhs_count)
    codes = jnp.arange(9 * face_count, dtype=jnp.int32)
    selector = (neighbour.reshape(column_count, -1)[:, :, None] == codes[None, None, :]).astype(
        jnp.bfloat16
    )
    gathered = jnp.einsum("jtq,ijqx->ijtx", selector, window, preferred_element_type=jnp.float32)
    gathered = gathered.astype(jnp.bfloat16)
    gathered = gathered.reshape(rows, column_count, face_count, -1, rhs_count)
    product = jnp.einsum("ijcam,ijcmr->ijcar", blocks, gathered, preferred_element_type=jnp.float32)
    return product.astype(jnp.bfloat16)


def local(start_vector, trace_blocks, neighbour):
    own_columns = start_vector.shape[0]
    basis = []
    current = start_vector
    for layer_index in range(STEPS):
        padded = with_halo(current, (("stream", 0), ("azim", 1)), 1)
        current = apply_rows(padded, trace_blocks, neighbour, own_columns)
        basis.append(current)
    return jnp.stack(basis)


def solution(mesh):
    return jax.shard_map(
        local,
        mesh=mesh,
        in_specs=(
            P("stream", "azim", None, None, None),
            P("stream", "azim", None, None, None),
            P("azim", None, None),
        ),
        out_specs=P(None, "stream", "azim", None, None, None),
        check_vma=False,
    )
```

profile of v0, /device:TPU:0, one launch (start us, length us, event | category | flops | bytes accessed | tf_op | source)
XLA Modules:
  0.0 316.1 jit_solution(8950533928820168933)
XLA Ops:
  0.0 1.1 fusion.78
  1.1 0.5 collective-permute-start
  1.6 2.9 collective-permute-start.1
  4.6 2.6 collective-permute-done
  7.2 0.3 collective-permute-done.1
  7.4 2.0 pad_maximum_fusion
  9.5 2.1 collective-permute-start.2
  11.5 2.0 collective-permute-start.3
  13.6 0.8 eq.69
  14.3 17.6 %collective-permute-done.2 = bf16[6,1,8,64,128]{4,3,2,0,1:T(8,128)(2,1)} collective-permute-done((bf16[6,1,8,64,128]{4,3,2,0,1:T(8,128)(2,1)}, bf16[6,1,8,64,128]{4,3,2,0,1:T(8,128)(2,1)}, u32[]{:S(2)}, u32[]{:S(2)}) %collective-permute-start.2) | collective-permute-done | bytes 786464 | tf_op jit(solution)/shard_map/ppermute | solution.py:15
  31.9 1.1 fusion.68
  33.0 1.1 fusion.67
  34.1 15.0 %collective-permute-done.3 = bf16[6,1,8,64,128]{4,3,2,0,1:T(8,128)(2,1)} collective-permute-done((bf16[6,1,8,64,128]{4,3,2,0,1:T(8,128)(2,1)}, bf16[6,1,8,64,128]{4,3,2,0,1:T(8,128)(2,1)}, u32[]{:S(2)}, u32[]{:S(2)}) %collective-permute-start.3) | collective-permute-done | bytes 786464 | tf_op jit(solution)/shard_map/ppermute | solution.py:18
  49.1 1.1 fusion.65
  50.2 1.1 fusion.64
  51.3 1.1 bitcast_dynamic-update-slice_fusion.3
  52.4 1.1 fusion.63
  53.6 1.1 fusion.62
  54.8 1.1 fusion.59
  55.9 13.1 %fusion = bf16[4,1,96,8192]{3,2,0,1:T(8,128)(2,1)} fusion(bf16[4,1,9,8,64,128]{5,4,3,0,2,1:T(8,128)(2,1)S(1)} %fusion.59, s32[96]{0:T(128)S(1)} %eq.69), kind=kOutput, calls=%fused_computation.4 | convolution fusion | flops 456137472 | bytes 11010432 | tf_op jit(solution)/shard_map/jtq,ijqx->ijtx/dot_general | solution.py:40
  69.0 10.5 %reshape.187 = bf16[4,8,768,128]{3,2,1,0:T(8,128)(2,1)} reshape(bf16[4,1,96,8192]{3,2,0,1:T(8,128)(2,1)} %fusion) | data formatting | bytes 12582912 | tf_op jit(solution)/shard_map/reshape.6
  79.5 4.1 %fusion.23 = bf16[4,8,128,64]{2,3,1,0:T(8,128)(2,1)S(1)} fusion(bf16[4,8,768,128]{3,2,1,0:T(8,128)(2,1)} %reshape.187, bf16[4,1,8,64,768]{4,3,2,1,0:T(8,128)(2,1)S(1)} %copy-done), kind=kOutput, calls=%fused_computation.22 | convolution fusion | flops 402915328 | bytes 9961472 | tf_op jit(solution)/shard_map/ijcam,ijcmr->ijcar/dot_general | solution.py:43
  83.7 0.2 collective-permute-start.4
  83.8 2.5 collective-permute-start.5
  86.4 3.4 %collective-permute-done.4 = bf16[1,1,8,64,128]{4,3,2,0,1:T(8,128)(2,1)S(1)} collective-permute-done((bf16[1,1,8,64,128]{4,3,2,0,1:T(8,128)(2,1)S(1)}, bf16[1,1,8,64,128]{4,3,2,0,1:T(8,128)(2,1)S(1)}, u32[]{:S(2)}, u32[]{:S(2)}) %collective-permute-start.4) | collective-permute-done | bytes 131104 | tf_op jit(solution)/shard_map/ppermute | solution.py:15
  89.7 0.1 pad_maximum_fusion.1
  89.8 0.2 collective-permute-start.6
  90.1 3.6 %collective-permute-start.7 = (bf16[6,1,8,64,128]{4,3,2,0,1:T(8,128)(2,1)S(1)}, bf16[6,1,8,64,128]{4,3,2,0,1:T(8,128)(2,1)S(1)}, u32[]{:S(2)}, u32[]{:S(2)}) collective-permute-start(bf16[6,1,8,64,128]{4,3,2,0,1:T(8,128)(2,1)S(1)} %pad_maximum_fusion.1), channel_id=1, source_target_pairs={{1,0},{2,1},{3,2},{0,3},{5,4},{6,5},{7,6},{4,7},{9,8},{10,9},{11,1... | collective-permute-start | bytes 2359304 | tf_op jit(solution)/shard_map/ppermute | solution.py:18
  93.7 18.4 %collective-permute-done.6 = bf16[6,1,8,64,128]{4,3,2,0,1:T(8,128)(2,1)S(1)} collective-permute-done((bf16[6,1,8,64,128]{4,3,2,0,1:T(8,128)(2,1)S(1)}, bf16[6,1,8,64,128]{4,3,2,0,1:T(8,128)(2,1)S(1)}, u32[]{:S(2)}, u32[]{:S(2)}) %collective-permute-start.6) | collective-permute-done | bytes 786464 | tf_op jit(solution)/shard_map/ppermute | solution.py:15
  112.2 14.8 %collective-permute-done.7 = bf16[6,1,8,64,128]{4,3,2,0,1:T(8,128)(2,1)S(1)} collective-permute-done((bf16[6,1,8,64,128]{4,3,2,0,1:T(8,128)(2,1)S(1)}, bf16[6,1,8,64,128]{4,3,2,0,1:T(8,128)(2,1)S(1)}, u32[]{:S(2)}, u32[]{:S(2)}) %collective-permute-start.7) | collective-permute-done | bytes 786464 | tf_op jit(solution)/shard_map/ppermute | solution.py:18
  127.3 0.1 fusion.53
  127.4 0.1 fusion.52
  127.5 0.1 fusion.51
  127.5 0.1 fusion.49
  127.6 3.2 %copy.17 = bf16[4,1,9,8,64,128]{5,4,3,2,0,1:T(8,128)(2,1)} copy(bf16[4,1,9,8,64,128]{5,4,3,0,2,1:T(8,128)(2,1)S(1)} %fusion.49) | data formatting | bytes 9437184 | tf_op jit(solution)/shard_map/stack | solution.py:34
  130.9 8.2 %reshape.189 = bf16[4,72,8192]{2,1,0:T(8,128)(2,1)} reshape(bf16[4,1,9,8,64,128]{5,4,3,2,0,1:T(8,128)(2,1)} %copy.17) | data formatting | bytes 9437184 | tf_op jit(solution)/shard_map/reshape.16
  139.0 6.9 %fusion.1 = bf16[4,1,96,8192]{3,2,0,1:T(8,128)(2,1)} fusion(bf16[4,72,8192]{2,1,0:T(8,128)(2,1)} %reshape.189, s32[96]{0:T(128)S(1)} %eq.69), kind=kOutput, calls=%fused_computation.5 | convolution fusion | flops 456137472 | bytes 11010432 | tf_op jit(solution)/shard_map/jtq,ijqx->ijtx/dot_general | solution.py:40
  146.0 10.5 %reshape.190 = bf16[4,8,768,128]{3,2,1,0:T(8,128)(2,1)} reshape(bf16[4,1,96,8192]{3,2,0,1:T(8,128)(2,1)} %fusion.1) | data formatting | bytes 12582912 | tf_op jit(solution)/shard_map/reshape.20
  156.5 4.1 %fusion.20 = bf16[4,8,128,64]{2,3,1,0:T(8,128)(2,1)S(1)} fusion(bf16[4,8,768,128]{3,2,1,0:T(8,128)(2,1)} %reshape.190, bf16[4,1,8,64,768]{4,3,2,1,0:T(8,128)(2,1)S(1)} %copy-done), kind=kOutput, calls=%fused_computation.21 | convolution fusion | flops 402915328 | bytes 9961472 | tf_op jit(solution)/shard_map/ijcam,ijcmr->ijcar/dot_general | solution.py:43
  160.7 2.6 collective-permute-start.9
  163.3 3.5 %collective-permute-done.8 = bf16[1,1,8,64,128]{4,3,2,0,1:T(8,128)(2,1)S(1)} collective-permute-done((bf16[1,1,8,64,128]{4,3,2,0,1:T(8,128)(2,1)S(1)}, bf16[1,1,8,64,128]{4,3,2,0,1:T(8,128)(2,1)S(1)}, u32[]{:S(2)}, u32[]{:S(2)}) %collective-permute-start.8) | collective-permute-done | bytes 131104 | tf_op jit(solution)/shard_map/ppermute | solution.py:15
  166.9 0.1 pad_maximum_fusion.2
  167.0 2.0 collective-permute-start.10
  169.0 1.9 collective-permute-start.11
  170.9 18.4 %collective-permute-done.10 = bf16[6,1,8,64,128]{4,3,2,0,1:T(8,128)(2,1)S(1)} collective-permute-done((bf16[6,1,8,64,128]{4,3,2,0,1:T(8,128)(2,1)S(1)}, bf16[6,1,8,64,128]{4,3,2,0,1:T(8,128)(2,1)S(1)}, u32[]{:S(2)}, u32[]{:S(2)}) %collective-permute-start.10) | collective-permute-done | bytes 786464 | tf_op jit(solution)/shard_map/ppermute | solution.py:15
  189.4 15.1 %collective-permute-done.11 = bf16[6,1,8,64,128]{4,3,2,0,1:T(8,128)(2,1)S(1)} collective-permute-done((bf16[6,1,8,64,128]{4,3,2,0,1:T(8,128)(2,1)S(1)}, bf16[6,1,8,64,128]{4,3,2,0,1:T(8,128)(2,1)S(1)}, u32[]{:S(2)}, u32[]{:S(2)}) %collective-permute-start.11) | collective-permute-done | bytes 786464 | tf_op jit(solution)/shard_map/ppermute | solution.py:18
  205.1 3.2 %copy.18 = bf16[4,1,9,8,64,128]{5,4,3,2,0,1:T(8,128)(2,1)} copy(bf16[4,1,9,8,64,128]{5,4,3,0,2,1:T(8,128)(2,1)S(1)} %fusion.39) | data formatting | bytes 9437184 | tf_op jit(solution)/shard_map/stack | solution.py:34
  208.3 8.2 %reshape.191 = bf16[4,72,8192]{2,1,0:T(8,128)(2,1)} reshape(bf16[4,1,9,8,64,128]{5,4,3,2,0,1:T(8,128)(2,1)} %copy.18) | data formatting | bytes 9437184 | tf_op jit(solution)/shard_map/reshape.22
  216.5 6.9 %fusion.2 = bf16[4,1,96,8192]{3,2,0,1:T(8,128)(2,1)} fusion(bf16[4,72,8192]{2,1,0:T(8,128)(2,1)} %reshape.191, s32[96]{0:T(128)S(1)} %eq.69), kind=kOutput, calls=%fused_computation.6 | convolution fusion | flops 456137472 | bytes 11010432 | tf_op jit(solution)/shard_map/jtq,ijqx->ijtx/dot_general | solution.py:40
  223.4 10.5 %reshape.192 = bf16[4,8,768,128]{3,2,1,0:T(8,128)(2,1)} reshape(bf16[4,1,96,8192]{3,2,0,1:T(8,128)(2,1)} %fusion.2) | data formatting | bytes 12582912 | tf_op jit(solution)/shard_map/reshape.26
  233.9 4.1 %fusion.17 = bf16[4,8,128,64]{2,3,1,0:T(8,128)(2,1)S(1)} fusion(bf16[4,8,768,128]{3,2,1,0:T(8,128)(2,1)} %reshape.192, bf16[4,1,8,64,768]{4,3,2,1,0:T(8,128)(2,1)S(1)} %copy-done), kind=kOutput, calls=%fused_computation.20 | convolution fusion | flops 402915328 | bytes 9961472 | tf_op jit(solution)/shard_map/ijcam,ijcmr->ijcar/dot_general | solution.py:43
  238.1 2.6 collective-permute-start.13
  240.8 3.9 %collective-permute-done.12 = bf16[1,1,8,64,128]{4,3,2,0,1:T(8,128)(2,1)S(1)} collective-permute-done((bf16[1,1,8,64,128]{4,3,2,0,1:T(8,128)(2,1)S(1)}, bf16[1,1,8,64,128]{4,3,2,0,1:T(8,128)(2,1)S(1)}, u32[]{:S(2)}, u32[]{:S(2)}) %collective-permute-start.12) | collective-permute-done | bytes 131104 | tf_op jit(solution)/shard_map/ppermute | solution.py:15
  244.7 0.1 pad_maximum_fusion.3
  244.8 0.3 collective-permute-start.14
  245.1 3.5 %collective-permute-start.15 = (bf16[6,1,8,64,128]{4,3,2,0,1:T(8,128)(2,1)S(1)}, bf16[6,1,8,64,128]{4,3,2,0,1:T(8,128)(2,1)S(1)}, u32[]{:S(2)}, u32[]{:S(2)}) collective-permute-start(bf16[6,1,8,64,128]{4,3,2,0,1:T(8,128)(2,1)S(1)} %pad_maximum_fusion.3), channel_id=1, source_target_pairs={{1,0},{2,1},{3,2},{0,3},{5,4},{6,5},{7,6},{4,7},{9,8},{10,9},{11,1... | collective-permute-start | bytes 2359304 | tf_op jit(solution)/shard_map/ppermute | solution.py:18
  248.7 18.4 %collective-permute-done.14 = bf16[6,1,8,64,128]{4,3,2,0,1:T(8,128)(2,1)S(1)} collective-permute-done((bf16[6,1,8,64,128]{4,3,2,0,1:T(8,128)(2,1)S(1)}, bf16[6,1,8,64,128]{4,3,2,0,1:T(8,128)(2,1)S(1)}, u32[]{:S(2)}, u32[]{:S(2)}) %collective-permute-start.14) | collective-permute-done | bytes 786464 | tf_op jit(solution)/shard_map/ppermute | solution.py:15
  267.2 13.6 %collective-permute-done.15 = bf16[6,1,8,64,128]{4,3,2,0,1:T(8,128)(2,1)S(1)} collective-permute-done((bf16[6,1,8,64,128]{4,3,2,0,1:T(8,128)(2,1)S(1)}, bf16[6,1,8,64,128]{4,3,2,0,1:T(8,128)(2,1)S(1)}, u32[]{:S(2)}, u32[]{:S(2)}) %collective-permute-start.15) | collective-permute-done | bytes 786464 | tf_op jit(solution)/shard_map/ppermute | solution.py:18
  281.4 3.2 %copy.19 = bf16[4,1,9,8,64,128]{5,4,3,2,0,1:T(8,128)(2,1)} copy(bf16[4,1,9,8,64,128]{5,4,3,0,2,1:T(8,128)(2,1)S(1)} %fusion.29) | data formatting | bytes 9437184 | tf_op jit(solution)/shard_map/stack | solution.py:34
  284.6 8.2 %reshape.193 = bf16[4,72,8192]{2,1,0:T(8,128)(2,1)} reshape(bf16[4,1,9,8,64,128]{5,4,3,2,0,1:T(8,128)(2,1)} %copy.19) | data formatting | bytes 9437184 | tf_op jit(solution)/shard_map/reshape.28
  292.8 6.9 %fusion.3 = bf16[4,1,96,8192]{3,2,0,1:T(8,128)(2,1)} fusion(bf16[4,72,8192]{2,1,0:T(8,128)(2,1)} %reshape.193, s32[96]{0:T(128)S(1)} %eq.69), kind=kOutput, calls=%fused_computation.7 | convolution fusion | flops 456137472 | bytes 11010432 | tf_op jit(solution)/shard_map/jtq,ijqx->ijtx/dot_general | solution.py:40
  299.7 10.5 %reshape.194 = bf16[4,8,768,128]{3,2,1,0:T(8,128)(2,1)} reshape(bf16[4,1,96,8192]{3,2,0,1:T(8,128)(2,1)} %fusion.3) | data formatting | bytes 12582912 | tf_op jit(solution)/shard_map/reshape.32
  310.2 4.2 %fusion.26 = bf16[1,4,1,8,64,128]{5,4,3,1,2,0:T(8,128)(2,1)S(1)} fusion(bf16[4,8,768,128]{3,2,1,0:T(8,128)(2,1)} %reshape.194, bf16[4,1,8,64,768]{4,3,2,1,0:T(8,128)(2,1)S(1)} %copy-done), kind=kOutput, calls=%fused_computation.23 | convolution fusion | flops 402915328 | bytes 9961472 | tf_op jit(solution)/shard_map/ijcam,ijcmr->ijcar/dot_general | solution.py:43
  314.5 1.6 maximum_bitcast_fusion
  (48 shorter events, 1.8 us)
Async XLA Ops:
  0.0 79.5 %copy-start = (bf16[4,1,8,64,768]{4,3,2,1,0:T(8,128)(2,1)S(1)}, bf16[4,1,8,64,768]{4,3,2,1,0:T(8,128)(2,1)}, u32[]{:S(2)}) copy-start(bf16[4,1,8,64,768]{4,3,2,1,0:T(8,128)(2,1)} %param.4) | copy-start | bytes 9437188
  1.1 6.0 %collective-permute-start = (bf16[1,1,8,64,128]{4,3,2,0,1:T(8,128)(2,1)S(1)}, bf16[1,1,8,64,128]{4,3,2,0,1:T(8,128)(2,1)S(1)}, u32[]{:S(2)}, u32[]{:S(2)}) collective-permute-start(bf16[1,1,8,64,128]{4,3,2,0,1:T(8,128)(2,1)S(1)} %get-tuple-element.11), channel_id=1, source_target_pairs={{0,4},{4,8},{8,12},{12,16},{16,20},{20,24},{24,28},{28,0},{1,5},{5... | collective-permute-start | bytes 393224 | tf_op jit(solution)/shard_map/ppermute | solution.py:15
  1.6 5.8 %collective-permute-start.1 = (bf16[1,1,8,64,128]{4,3,2,0,1:T(8,128)(2,1)S(1)}, bf16[1,1,8,64,128]{4,3,2,0,1:T(8,128)(2,1)S(1)}, u32[]{:S(2)}, u32[]{:S(2)}) collective-permute-start(bf16[1,1,8,64,128]{4,3,2,0,1:T(8,128)(2,1)S(1)} %get-tuple-element.12), channel_id=1, source_target_pairs={{4,0},{8,4},{12,8},{16,12},{20,16},{24,20},{28,24},{0,28},{5,1},{9... | collective-permute-start | bytes 393224 | tf_op jit(solution)/shard_map/ppermute | solution.py:18
  9.5 22.5 %collective-permute-start.2 = (bf16[6,1,8,64,128]{4,3,2,0,1:T(8,128)(2,1)}, bf16[6,1,8,64,128]{4,3,2,0,1:T(8,128)(2,1)}, u32[]{:S(2)}, u32[]{:S(2)}) collective-permute-start(bf16[6,1,8,64,128]{4,3,2,0,1:T(8,128)(2,1)} %pad_maximum_fusion), channel_id=1, source_target_pairs={{0,1},{1,2},{2,3},{3,0},{4,5},{5,6},{6,7},{7,4},{8,9},{9,10},{10,1... | collective-permute-start | bytes 2359304 | tf_op jit(solution)/shard_map/ppermute | solution.py:15
  11.5 37.6 %collective-permute-start.3 = (bf16[6,1,8,64,128]{4,3,2,0,1:T(8,128)(2,1)}, bf16[6,1,8,64,128]{4,3,2,0,1:T(8,128)(2,1)}, u32[]{:S(2)}, u32[]{:S(2)}) collective-permute-start(bf16[6,1,8,64,128]{4,3,2,0,1:T(8,128)(2,1)} %pad_maximum_fusion), channel_id=1, source_target_pairs={{1,0},{2,1},{3,2},{0,3},{5,4},{6,5},{7,6},{4,7},{9,8},{10,9},{11,1... | collective-permute-start | bytes 2359304 | tf_op jit(solution)/shard_map/ppermute | solution.py:18
  14.3 40.3 %copy-start.7 = (bf16[4,1,8,64,128]{4,3,2,1,0:T(8,128)(2,1)S(1)}, bf16[4,1,8,64,128]{4,3,2,1,0:T(8,128)(2,1)}, u32[]{:S(2)}) copy-start(bf16[4,1,8,64,128]{4,3,2,1,0:T(8,128)(2,1)} %param.3) | copy-start | bytes 1572868
  83.6 43.8 %copy-start.1 = (bf16[4,8,128,64]{2,3,1,0:T(8,128)(2,1)}, bf16[4,8,128,64]{2,3,1,0:T(8,128)(2,1)S(1)}, u32[]{:S(2)}) copy-start(bf16[4,8,128,64]{2,3,1,0:T(8,128)(2,1)S(1)} %fusion.23) | copy-start | bytes 1572868
  83.7 6.1 %collective-permute-start.4 = (bf16[1,1,8,64,128]{4,3,2,0,1:T(8,128)(2,1)S(1)}, bf16[1,1,8,64,128]{4,3,2,0,1:T(8,128)(2,1)S(1)}, u32[]{:S(2)}, u32[]{:S(2)}) collective-permute-start(bf16[1,1,8,64,128]{4,3,2,0,1:T(8,128)(2,1)S(1)} %get-tuple-element.9), channel_id=1, source_target_pairs={{0,4},{4,8},{8,12},{12,16},{16,20},{20,24},{24,28},{28,0},{1,5},{5... | collective-permute-start | bytes 393224 | tf_op jit(solution)/shard_map/ppermute | solution.py:15
  83.8 5.9 %collective-permute-start.5 = (bf16[1,1,8,64,128]{4,3,2,0,1:T(8,128)(2,1)S(1)}, bf16[1,1,8,64,128]{4,3,2,0,1:T(8,128)(2,1)S(1)}, u32[]{:S(2)}, u32[]{:S(2)}) collective-permute-start(bf16[1,1,8,64,128]{4,3,2,0,1:T(8,128)(2,1)S(1)} %get-tuple-element.10), channel_id=1, source_target_pairs={{4,0},{8,4},{12,8},{16,12},{20,16},{24,20},{28,24},{0,28},{5,1},{9... | collective-permute-start | bytes 393224 | tf_op jit(solution)/shard_map/ppermute | solution.py:18
  89.8 22.3 %collective-permute-start.6 = (bf16[6,1,8,64,128]{4,3,2,0,1:T(8,128)(2,1)S(1)}, bf16[6,1,8,64,128]{4,3,2,0,1:T(8,128)(2,1)S(1)}, u32[]{:S(2)}, u32[]{:S(2)}) collective-permute-start(bf16[6,1,8,64,128]{4,3,2,0,1:T(8,128)(2,1)S(1)} %pad_maximum_fusion.1), channel_id=1, source_target_pairs={{0,1},{1,2},{2,3},{3,0},{4,5},{5,6},{6,7},{7,4},{8,9},{9,10},{10,1... | collective-permute-start | bytes 2359304 | tf_op jit(solution)/shard_map/ppermute | solution.py:15
  90.1 37.0 %collective-permute-start.7 = (bf16[6,1,8,64,128]{4,3,2,0,1:T(8,128)(2,1)S(1)}, bf16[6,1,8,64,128]{4,3,2,0,1:T(8,128)(2,1)S(1)}, u32[]{:S(2)}, u32[]{:S(2)}) collective-permute-start(bf16[6,1,8,64,128]{4,3,2,0,1:T(8,128)(2,1)S(1)} %pad_maximum_fusion.1), channel_id=1, source_target_pairs={{1,0},{2,1},{3,2},{0,3},{5,4},{6,5},{7,6},{4,7},{9,8},{10,9},{11,1... | collective-permute-start | bytes 2359304 | tf_op jit(solution)/shard_map/ppermute | solution.py:18
  160.6 44.3 %copy-start.3 = (bf16[4,8,128,64]{2,3,1,0:T(8,128)(2,1)}, bf16[4,8,128,64]{2,3,1,0:T(8,128)(2,1)S(1)}, u32[]{:S(2)}) copy-start(bf16[4,8,128,64]{2,3,1,0:T(8,128)(2,1)S(1)} %fusion.20) | copy-start | bytes 1572868
  160.6 6.2 %collective-permute-start.8 = (bf16[1,1,8,64,128]{4,3,2,0,1:T(8,128)(2,1)S(1)}, bf16[1,1,8,64,128]{4,3,2,0,1:T(8,128)(2,1)S(1)}, u32[]{:S(2)}, u32[]{:S(2)}) collective-permute-start(bf16[1,1,8,64,128]{4,3,2,0,1:T(8,128)(2,1)S(1)} %get-tuple-element.7), channel_id=1, source_target_pairs={{0,4},{4,8},{8,12},{12,16},{16,20},{20,24},{24,28},{28,0},{1,5},{5... | collective-permute-start | bytes 393224 | tf_op jit(solution)/shard_map/ppermute | solution.py:15
  160.7 6.2 %collective-permute-start.9 = (bf16[1,1,8,64,128]{4,3,2,0,1:T(8,128)(2,1)S(1)}, bf16[1,1,8,64,128]{4,3,2,0,1:T(8,128)(2,1)S(1)}, u32[]{:S(2)}, u32[]{:S(2)}) collective-permute-start(bf16[1,1,8,64,128]{4,3,2,0,1:T(8,128)(2,1)S(1)} %get-tuple-element.8), channel_id=1, source_target_pairs={{4,0},{8,4},{12,8},{16,12},{20,16},{24,20},{28,24},{0,28},{5,1},{9... | collective-permute-start | bytes 393224 | tf_op jit(solution)/shard_map/ppermute | solution.py:18
  167.0 22.3 %collective-permute-start.10 = (bf16[6,1,8,64,128]{4,3,2,0,1:T(8,128)(2,1)S(1)}, bf16[6,1,8,64,128]{4,3,2,0,1:T(8,128)(2,1)S(1)}, u32[]{:S(2)}, u32[]{:S(2)}) collective-permute-start(bf16[6,1,8,64,128]{4,3,2,0,1:T(8,128)(2,1)S(1)} %pad_maximum_fusion.2), channel_id=1, source_target_pairs={{0,1},{1,2},{2,3},{3,0},{4,5},{5,6},{6,7},{7,4},{8,9},{9,10},{10,1... | collective-permute-start | bytes 2359304 | tf_op jit(solution)/shard_map/ppermute | solution.py:15
  169.0 35.5 %collective-permute-start.11 = (bf16[6,1,8,64,128]{4,3,2,0,1:T(8,128)(2,1)S(1)}, bf16[6,1,8,64,128]{4,3,2,0,1:T(8,128)(2,1)S(1)}, u32[]{:S(2)}, u32[]{:S(2)}) collective-permute-start(bf16[6,1,8,64,128]{4,3,2,0,1:T(8,128)(2,1)S(1)} %pad_maximum_fusion.2), channel_id=1, source_target_pairs={{1,0},{2,1},{3,2},{0,3},{5,4},{6,5},{7,6},{4,7},{9,8},{10,9},{11,1... | collective-permute-start | bytes 2359304 | tf_op jit(solution)/shard_map/ppermute | solution.py:18
  238.0 43.2 %copy-start.5 = (bf16[4,8,128,64]{2,3,1,0:T(8,128)(2,1)}, bf16[4,8,128,64]{2,3,1,0:T(8,128)(2,1)S(1)}, u32[]{:S(2)}) copy-start(bf16[4,8,128,64]{2,3,1,0:T(8,128)(2,1)S(1)} %fusion.17) | copy-start | bytes 1572868
  238.1 6.6 %collective-permute-start.12 = (bf16[1,1,8,64,128]{4,3,2,0,1:T(8,128)(2,1)S(1)}, bf16[1,1,8,64,128]{4,3,2,0,1:T(8,128)(2,1)S(1)}, u32[]{:S(2)}, u32[]{:S(2)}) collective-permute-start(bf16[1,1,8,64,128]{4,3,2,0,1:T(8,128)(2,1)S(1)} %get-tuple-element.5), channel_id=1, source_target_pairs={{0,4},{4,8},{8,12},{12,16},{16,20},{20,24},{24,28},{28,0},{1,5},{5... | collective-permute-start | bytes 393224 | tf_op jit(solution)/shard_map/ppermute | solution.py:15
  238.1 6.6 %collective-permute-start.13 = (bf16[1,1,8,64,128]{4,3,2,0,1:T(8,128)(2,1)S(1)}, bf16[1,1,8,64,128]{4,3,2,0,1:T(8,128)(2,1)S(1)}, u32[]{:S(2)}, u32[]{:S(2)}) collective-permute-start(bf16[1,1,8,64,128]{4,3,2,0,1:T(8,128)(2,1)S(1)} %get-tuple-element.6), channel_id=1, source_target_pairs={{4,0},{8,4},{12,8},{16,12},{20,16},{24,20},{28,24},{0,28},{5,1},{9... | collective-permute-start | bytes 393224 | tf_op jit(solution)/shard_map/ppermute | solution.py:18
  244.8 22.3 %collective-permute-start.14 = (bf16[6,1,8,64,128]{4,3,2,0,1:T(8,128)(2,1)S(1)}, bf16[6,1,8,64,128]{4,3,2,0,1:T(8,128)(2,1)S(1)}, u32[]{:S(2)}, u32[]{:S(2)}) collective-permute-start(bf16[6,1,8,64,128]{4,3,2,0,1:T(8,128)(2,1)S(1)} %pad_maximum_fusion.3), channel_id=1, source_target_pairs={{0,1},{1,2},{2,3},{3,0},{4,5},{5,6},{6,7},{7,4},{8,9},{9,10},{10,1... | collective-permute-start | bytes 2359304 | tf_op jit(solution)/shard_map/ppermute | solution.py:15
  245.1 35.7 %collective-permute-start.15 = (bf16[6,1,8,64,128]{4,3,2,0,1:T(8,128)(2,1)S(1)}, bf16[6,1,8,64,128]{4,3,2,0,1:T(8,128)(2,1)S(1)}, u32[]{:S(2)}, u32[]{:S(2)}) collective-permute-start(bf16[6,1,8,64,128]{4,3,2,0,1:T(8,128)(2,1)S(1)} %pad_maximum_fusion.3), channel_id=1, source_target_pairs={{1,0},{2,1},{3,2},{0,3},{5,4},{6,5},{7,6},{4,7},{9,8},{10,9},{11,1... | collective-permute-start | bytes 2359304 | tf_op jit(solution)/shard_map/ppermute | solution.py:18
  310.2 4.2 %copy-start.2 = (bf16[4,8,128,64]{2,3,1,0:T(8,128)(2,1)S(1)}, bf16[4,8,128,64]{2,3,1,0:T(8,128)(2,1)}, u32[]{:S(2)}) copy-start(bf16[4,8,128,64]{2,3,1,0:T(8,128)(2,1)} %copy-done.1) | copy-start | bytes 1572868
  310.2 4.2 %copy-start.4 = (bf16[4,8,128,64]{2,3,1,0:T(8,128)(2,1)S(1)}, bf16[4,8,128,64]{2,3,1,0:T(8,128)(2,1)}, u32[]{:S(2)}) copy-start(bf16[4,8,128,64]{2,3,1,0:T(8,128)(2,1)} %copy-done.3) | copy-start | bytes 1572868
  310.2 4.3 %copy-start.6 = (bf16[4,8,128,64]{2,3,1,0:T(8,128)(2,1)S(1)}, bf16[4,8,128,64]{2,3,1,0:T(8,128)(2,1)}, u32[]{:S(2)}) copy-start(bf16[4,8,128,64]{2,3,1,0:T(8,128)(2,1)} %copy-done.5) | copy-start | bytes 1572868
where the time goes:
time: 318 us; the launch traced here: 316 us
  waiting for transfers between devices  145 us (46%)
  local copies, waits for them, and re-layouts  87.4 us (27%)
  matrix products  50.5 us (16%)
  starting transfers between devices  27.2 us (9%)
  other arithmetic  5.45 us (2%)
    ppermute x8, waiting for transfers between devices, with_halo(): lax.ppermute(lax.slice_in_dim(block, block.shape[dim] - width, None, axis...  86.3 us
    another operation x7, local copies, waits for them, and re-layouts  66.6 us
    ppermute x8, waiting for transfers between devices, with_halo(): lax.ppermute(lax.slice_in_dim(block, 0, width, axis=dim), axis, backward)  58.8 us
    dot_general x4, matrix products, apply_rows(): jnp.einsum('jtq,ijqx->ijtx', selector, window, preferred_element_type=jnp...  33.9 us
    ppermute x8, starting transfers between devices, with_halo(): lax.ppermute(lax.slice_in_dim(block, 0, width, axis=dim), axis, backward)  21.8 us
    dot_general x4, matrix products, apply_rows(): jnp.einsum('ijcam,ijcmr->ijcar', blocks, gathered, preferred_element_type...  16.5 us
    another operation x7, local copies, waits for them, and re-layouts, apply_rows(): window = jnp.stack(pieces, axis=2)  11 us
    unnamed x40, local copies, waits for them, and re-layouts  7.83 us
  transfers between devices with their start and end apart: 16, of which 13 were waited for; matrix products, arithmetic and copies ran while one was open for 1% of the time, Pallas kernels for 0%

commit v1 on v0

v1 whole, which is shorter than its diff:
```python
import functools

import jax
import jax.numpy as jnp
from jax import lax
from jax.experimental import pallas as pl
from jax.experimental.pallas import tpu as pltpu
from jax.sharding import PartitionSpec as P

STEPS = 4
HALVES = 2
VMEM_LIMIT = 24 * 1024 * 1024


def low_lanes(shape):
    return lax.broadcasted_iota(jnp.int32, shape, len(shape) - 1) < shape[-1] // 2


def swap_lanes(value):
    return pltpu.roll(value, value.shape[-1] // 2, len(value.shape) - 1)


def pack_kernel(start_ref, first_ref, second_ref):
    faces, width, lanes = start_ref.shape[1:]
    for face in range(faces):
        value = start_ref[0, face].astype(jnp.float32)
        top = value[: width // 2]
        bottom = swap_lanes(value[width // 2 :])
        low = low_lanes(top.shape)
        first_ref[0, face] = jnp.where(low, top, bottom).astype(jnp.bfloat16)
        second_ref[0, face] = jnp.where(low, bottom, top).astype(jnp.bfloat16)


def pack(start):
    columns, faces, width, lanes = start.shape
    half = jax.ShapeDtypeStruct((columns, faces, width // 2, lanes), jnp.bfloat16)
    spec = pl.BlockSpec((1, faces, width // 2, lanes), lambda i: (i, 0, 0, 0))
    return pl.pallas_call(
        pack_kernel,
        grid=(columns,),
        in_specs=[pl.BlockSpec((1, faces, width, lanes), lambda i: (i, 0, 0, 0))],
        out_specs=[spec, spec],
        out_shape=[half, half],
        name="pack",
    )(start)


def step_kernel(half, with_basis, *refs):
    (table, blocks_ref, own, low_az, high_az, low_st, high_st), refs = refs[:7], refs[7:]
    if with_basis:
        other_ref, refs = refs[0], refs[1:]
        if len(refs) == 5:
            refs = refs[1:]
        next_ref, basis_ref, window, sems = refs
    else:
        next_ref, window, sems = refs
    faces, width, depth = blocks_ref.shape[1:]
    columns = own.shape[0]
    span = columns + 2
    rows, lanes = window.shape[1:]
    i = pl.program_id(0)

    @pl.when(i == 0)
    def _():
        copies = []
        view = window.reshape(3, span, faces, rows, lanes)
        for azim, source in enumerate((low_az, own, high_az)):
            copies.append((source, view.at[azim, pl.ds(1, columns)]))
        for azim in range(3):
            copies.append((low_st.at[azim], view.at[azim, 0]))
            copies.append((high_st.at[azim], view.at[azim, span - 1]))
        started = [
            pltpu.make_async_copy(source, target, sems.at[n])
            for n, (source, target) in enumerate(copies)
        ]
        for copy in started:
            copy.start()
        for copy in started:
            copy.wait()

    neighbours = table.shape[1]
    low = low_lanes((rows, lanes))
    for face in range(faces):
        gathered = jnp.concatenate(
            [window[table[face, k] + i * faces] for k in range(neighbours)], axis=0
        )
        block = blocks_ref[0, face]
        stacked = jnp.concatenate([block[:, : depth // 2], block[:, depth // 2 :]], axis=0)
        product = jnp.dot(stacked, gathered, preferred_element_type=jnp.float32)
        top, bottom = product[:width], product[width:]
        if half == 0:
            here = jnp.where(low, top[:rows], bottom[rows:])
            there = jnp.where(low, top[rows:], bottom[:rows])
        else:
            here = jnp.where(low, bottom[rows:], top[:rows])
            there = jnp.where(low, bottom[:rows], top[rows:])
        result = (here + swap_lanes(there)).astype(jnp.bfloat16)
        next_ref[0, face] = result
        if with_basis:
            second = result.astype(jnp.float32)
            first = other_ref[0, face].astype(jnp.float32)
            basis_ref[0, 0, face, :rows] = jnp.where(low, first, second).astype(jnp.bfloat16)
            basis_ref[0, 0, face, rows:] = swap_lanes(jnp.where(low, second, first)).astype(
                jnp.bfloat16
            )


def step(half, index, table, blocks, pieces, other=None, basis=None):
    columns, faces, width, depth = blocks.shape
    rows, lanes = pieces[0].shape[2:]
    with_basis = half == HALVES - 1
    piece_spec = pl.BlockSpec((1, faces, rows, lanes), lambda i: (i, 0, 0, 0))
    any_spec = pl.BlockSpec(memory_space=pl.ANY)
    in_specs = [
        pl.BlockSpec(memory_space=pltpu.SMEM),
        pl.BlockSpec((1, faces, width, depth), lambda i: (i, 0, 0, 0)),
    ] + [any_spec] * 5
    args = [table, blocks, *pieces]
    out_specs = [piece_spec]
    out_shape = [jax.ShapeDtypeStruct((columns, faces, rows, lanes), jnp.bfloat16)]
    aliases = {}
    if with_basis:
        in_specs.append(piece_spec)
        args.append(other)
        if basis is not None:
            in_specs.append(any_spec)
            aliases = {len(args): 1}
            args.append(basis)
        out_specs.append(
            pl.BlockSpec((1, 1, faces, width, lanes), lambda i: (index, i, 0, 0, 0))
        )
        out_shape.append(jax.ShapeDtypeStruct((STEPS, columns, faces, width, lanes), jnp.bfloat16))
    flops = 2 * columns * faces * 2 * width * (depth // 2) * lanes
    return pl.pallas_call(
        functools.partial(step_kernel, half, with_basis),
        grid=(columns,),
        in_specs=in_specs,
        out_specs=out_specs,
        out_shape=out_shape,
        input_output_aliases=aliases,
        scratch_shapes=[
            pltpu.VMEM((3 * (columns + 2) * faces, rows, lanes), jnp.bfloat16),
            pltpu.SemaphoreType.DMA((9,)),
        ],
        cost_estimate=pl.CostEstimate(flops=flops, bytes_accessed=blocks.size * 2, transcendentals=0),
        compiler_params=pltpu.CompilerParams(vmem_limit_bytes=VMEM_LIMIT),
        name=f"step_half{half}",
    )(*args)


def shift(value, axis, up):
    count = lax.axis_size(axis)
    pairs = [(i, (i + 1) % count) for i in range(count)]
    if not up:
        pairs = [(target, source) for source, target in pairs]
    return lax.ppermute(value, axis, pairs)


def halves_of_rows(blocks):
    columns, faces, width, depth = blocks.shape
    row = lax.broadcasted_iota(jnp.int32, (depth, depth), 0)
    column = lax.broadcasted_iota(jnp.int32, (depth, depth), 1)
    part = width // 2
    place = (row // width) * part + row % part + ((row // part) % 2) * (depth // 2)
    mover = (place == column).astype(jnp.bfloat16)
    moved = jnp.dot(blocks.reshape(-1, depth), mover, preferred_element_type=jnp.float32)
    return moved.astype(jnp.bfloat16).reshape(blocks.shape)


def local(start_vector, trace_blocks, neighbour):
    columns, around, faces, width, lanes = start_vector.shape
    start = start_vector.reshape(columns, faces, width, lanes)
    blocks = halves_of_rows(trace_blocks.reshape(columns, faces, width, -1))
    codes = neighbour.reshape(faces, -1)
    table = (((codes // faces) % 3) * (columns + 2) + codes // (3 * faces)) * faces + codes % faces
    current = list(pack(start))
    basis = None
    for index in range(STEPS):
        around_z = [
            (shift(current[h], "azim", True), shift(current[h], "azim", False))
            for h in range(HALVES)
        ]
        for h in range(HALVES):
            low_az, high_az = around_z[h]
            trio = (low_az, current[h], high_az)
            low_st = shift(jnp.stack([part[columns - 1] for part in trio]), "stream", True)
            high_st = shift(jnp.stack([part[0] for part in trio]), "stream", False)
            pieces = (current[h], low_az, high_az, low_st, high_st)
            if h < HALVES - 1:
                (current[h],) = step(h, index, table, blocks, pieces)
            else:
                current[h], basis = step(
                    h, index, table, blocks, pieces, other=current[0], basis=basis
                )
    return basis.reshape(STEPS, columns, around, faces, width, lanes)


def solution(mesh):
    return jax.shard_map(
        local,
        mesh=mesh,
        in_specs=(
            P("stream", "azim", None, None, None),
            P("stream", "azim", None, None, None),
            P("azim", None, None),
        ),
        out_specs=P(None, "stream", "azim", None, None, None),
        check_vma=False,
    )
```

time: 318 us -> 174 us (0.55)
  local copies, waits for them, and re-layouts: 87.4 us -> 11 us
  waiting for transfers between devices: 145 us -> 73.2 us
  matrix products: 50.5 us -> 5.28 us
  Pallas kernels: 0 us -> 33.8 us
  starting transfers between devices: 27.2 us -> 48 us
  other arithmetic: 5.45 us -> 2.13 us
    another operation x14 -> x0, local copies, waits for them, and re-layouts: 77.6 us -> none
    ppermute x16 -> x32, waiting for transfers between devices: 145 us -> 73.2 us  [shift(): return lax.ppermute(value, axis, pairs)]
    dot_general x8 -> x1, matrix products: 50.5 us -> 5.28 us  [halves_of_rows(): jnp.dot(blocks.reshape(-1, depth), mover, preferred_element_type=jnp.floa...]
    pallas_call x0 -> x9, Pallas kernels: none -> 33.8 us  [the longest x8 30.4 us: step(): pl.pallas_call(functools.partial(step_kernel, half, with_basis), grid=(co...]
    ppermute x16 -> x32, starting transfers between devices: 27.2 us -> 48 us  [shift(): return lax.ppermute(value, axis, pairs)]
    unnamed x40 -> x14, local copies, waits for them, and re-layouts: 7.83 us -> 1.92 us
    convert_element_type x0 -> x1, local copies, waits for them, and re-layouts: none -> 4.68 us  [halves_of_rows(): return moved.astype(jnp.bfloat16).reshape(blocks.shape)]
    slice x4 -> x24, local copies, waits for them, and re-layouts: 1.19 us -> 4.41 us  [local(): high_st = shift(jnp.stack([part[0] for part in trio]), 'stream', False)]
  transfers between devices with their start and end apart: 16 -> 32, of which waited for: 13 -> 12; matrix products, arithmetic and copies ran while one was open for 1% -> 9% of each run, Pallas kernels for 0% -> 7%
where the time goes in v1:
time: 174 us
  waiting for transfers between devices  73.2 us (42%)
  starting transfers between devices  48 us (28%)
  Pallas kernels  33.8 us (19%)
  local copies, waits for them, and re-layouts  11 us (6%)
  matrix products  5.28 us (3%)
  other arithmetic  2.13 us (1%)
    ppermute x32, waiting for transfers between devices, shift(): return lax.ppermute(value, axis, pairs)  73.2 us
    ppermute x32, starting transfers between devices, shift(): return lax.ppermute(value, axis, pairs)  48 us
    pallas_call x8, Pallas kernels, step(): pl.pallas_call(functools.partial(step_kernel, half, with_basis), grid=(co...  30.4 us
    dot_general x1, matrix products, halves_of_rows(): jnp.dot(blocks.reshape(-1, depth), mover, preferred_element_type=jnp.floa...  5.28 us
    convert_element_type x1, local copies, waits for them, and re-layouts, halves_of_rows(): return moved.astype(jnp.bfloat16).reshape(blocks.shape)  4.68 us
    slice x24, local copies, waits for them, and re-layouts, local(): high_st = shift(jnp.stack([part[0] for part in trio]), 'stream', False)  4.41 us
  transfers between devices with their start and end apart: 32, of which 12 were waited for; matrix products, arithmetic and copies ran while one was open for 9% of the time, Pallas kernels for 7%

profile of v1, /device:TPU:0, one launch (start us, length us, event | category | flops | bytes accessed | tf_op | source)
XLA Modules:
  0.0 173.8 jit_solution(8313526607652794035)
XLA Ops:
  0.0 3.4 %pack.1 = (bf16[4,8,32,128]{3,2,1,0:T(8,128)(2,1)}, bf16[4,8,32,128]{3,2,1,0:T(8,128)(2,1)}) custom-call(bf16[4,8,64,128]{3,2,1,0:T(8,128)(2,1)} %bitcast.42), custom_call_target="tpu_custom_call" | custom-call | tf_op jit(solution)/shard_map/pack/pallas_call | solution.py:38
  3.4 3.0 %collective-permute-start = (bf16[4,8,32,128]{3,2,1,0:T(8,128)(2,1)}, bf16[4,8,32,128]{3,2,1,0:T(8,128)(2,1)}, u32[]{:S(2)}, u32[]{:S(2)}) collective-permute-start(bf16[4,8,32,128]{3,2,1,0:T(8,128)(2,1)} %get-tuple-element.14.refs_2_), channel_id=1, source_target_pairs={{0,1},{1,2},{2,3},{3,0},{4,5},{5,6},{6,7},{7,4},{8,9},{9,10},{10,1... | collective-permute-start | bytes 786440 | tf_op jit(solution)/shard_map/ppermute | solution.py:156
  6.5 2.0 %collective-permute-start.1 = (bf16[4,8,32,128]{3,2,1,0:T(8,128)(2,1)}, bf16[4,8,32,128]{3,2,1,0:T(8,128)(2,1)}, u32[]{:S(2)}, u32[]{:S(2)}) collective-permute-start(bf16[4,8,32,128]{3,2,1,0:T(8,128)(2,1)} %get-tuple-element.14.refs_2_), channel_id=1, source_target_pairs={{1,0},{2,1},{3,2},{0,3},{5,4},{6,5},{7,6},{4,7},{9,8},{10,9},{11,1... | collective-permute-start | bytes 786440 | tf_op jit(solution)/shard_map/ppermute | solution.py:156
  8.5 3.8 %collective-permute-start.5 = (bf16[4,8,32,128]{3,2,1,0:T(8,128)(2,1)}, bf16[4,8,32,128]{3,2,1,0:T(8,128)(2,1)}, u32[]{:S(2)}, u32[]{:S(2)}) collective-permute-start(bf16[4,8,32,128]{3,2,1,0:T(8,128)(2,1)} %get-tuple-element.15.refs_2_), channel_id=1, source_target_pairs={{1,0},{2,1},{3,2},{0,3},{5,4},{6,5},{7,6},{4,7},{9,8},{10,9},{11,1... | collective-permute-start | bytes 786440 | tf_op jit(solution)/shard_map/ppermute | solution.py:156
  12.4 0.0 copy-start.4
  12.4 5.3 %fusion = bf16[2048,768]{0,1:T(8,128)(2,1)} fusion(bf16[2048,768]{1,0:T(8,128)(2,1)S(1)} %bitcast.33, s32[768]{0:T(1024)S(1)} %get-tuple-element.71, s32[768]{0:T(1024)S(1)} %get-tuple-element.77, s32[768]{0:T(1024)S(1)} %get-tuple-element.72, s32[768]{0:T(1024)S(1)} %get-tuple-element.74, s32[768]{0:T(1024)S(1)} %get-tuple-element.73, ...), kind=kOutput, calls=%fused_computation.6 | convolution fusion | flops 2429288448 | bytes 6312192 | tf_op jit(solution)/shard_map/dot_general | solution.py:166
  17.7 0.6 fusion.64
  18.3 4.7 %copy.7 = bf16[2048,768]{1,0:T(8,128)(2,1)} copy(bf16[2048,768]{0,1:T(8,128)(2,1)} %fusion) | data formatting | bytes 6291456 | tf_op jit(solution)/shard_map/convert_element_type | solution.py:167
  23.0 0.9 fusion.65
  24.0 0.0 collective-permute-done.refs_3_
  24.0 0.9 fusion.63
  24.8 0.9 pad_maximum_fusion
  25.7 0.1 collective-permute-start.2
  25.8 0.9 pad_maximum_fusion.1
  26.6 2.7 %collective-permute-start.3 = (bf16[3,8,32,128]{3,2,1,0:T(8,128)(2,1)S(1)}, bf16[3,8,32,128]{3,2,1,0:T(8,128)(2,1)S(1)}, u32[]{:S(2)}, u32[]{:S(2)}) collective-permute-start(bf16[3,8,32,128]{3,2,1,0:T(8,128)(2,1)S(1)} %pad_maximum_fusion.1), channel_id=1, source_target_pairs={{4,0},{8,4},{12,8},{16,12},{20,16},{24,20},{28,24},{0,28},{5,1},{9... | collective-permute-start | bytes 589832 | tf_op jit(solution)/shard_map/ppermute | solution.py:156
  29.3 2.1 %collective-permute-done.5.refs_4_ = bf16[4,8,32,128]{3,2,1,0:T(8,128)(2,1)} collective-permute-done((bf16[4,8,32,128]{3,2,1,0:T(8,128)(2,1)}, bf16[4,8,32,128]{3,2,1,0:T(8,128)(2,1)}, u32[]{:S(2)}, u32[]{:S(2)}) %collective-permute-start.5) | collective-permute-done | bytes 262176 | tf_op jit(solution)/shard_map/ppermute | solution.py:156
  31.4 0.9 fusion.62
  32.3 0.9 fusion.60
  33.2 0.1 collective-permute-start.6
  33.3 2.7 %collective-permute-start.7 = (bf16[3,8,32,128]{3,2,1,0:T(8,128)(2,1)S(1)}, bf16[3,8,32,128]{3,2,1,0:T(8,128)(2,1)S(1)}, u32[]{:S(2)}, u32[]{:S(2)}) collective-permute-start(bf16[3,8,32,128]{3,2,1,0:T(8,128)(2,1)S(1)} %pad_maximum_fusion.3), channel_id=1, source_target_pairs={{4,0},{8,4},{12,8},{16,12},{20,16},{24,20},{28,24},{0,28},{5,1},{9... | collective-permute-start | bytes 589832 | tf_op jit(solution)/shard_map/ppermute | solution.py:156
  36.0 3.4 %collective-permute-done.6.refs_5_ = bf16[3,8,32,128]{3,2,1,0:T(8,128)(2,1)S(1)} collective-permute-done((bf16[3,8,32,128]{3,2,1,0:T(8,128)(2,1)S(1)}, bf16[3,8,32,128]{3,2,1,0:T(8,128)(2,1)S(1)}, u32[]{:S(2)}, u32[]{:S(2)}) %collective-permute-start.6) | collective-permute-done | bytes 196640 | tf_op jit(solution)/shard_map/ppermute | solution.py:156
  39.4 0.1 collective-permute-done.7.refs_6_
  39.5 1.9 %copy-done.1 = bf16[2048,768]{1,0:T(8,128)(2,1)S(1)} copy-done((bf16[2048,768]{1,0:T(8,128)(2,1)S(1)}, bf16[2048,768]{1,0:T(8,128)(2,1)}, u32[]{:S(2)}) %copy-start.1) | copy-done | bytes 3145752
  41.4 3.5 %step_half0.4.refs_7_.refs_2_ = bf16[4,8,32,128]{3,2,1,0:T(8,128)(2,1)S(1)} custom-call(s32[8,12]{1,0:T(8,128)S(1)} %fusion.30.refs_0_, bf16[4,8,64,768]{3,2,1,0:T(8,128)(2,1)S(1)} %bitcast.34, bf16[4,8,32,128]{3,2,1,0:T(8,128)(2,1)S(1)} %copy-done.5, bf16[4,8,32,128]{3,2,1,0:T(8,128)(2,1)} %collective-permute-done.4.refs_3_, ...), custom_call_target="tpu_custom_call" | custom-call | flops 402653184 | bytes 3145728 | tf_op jit(solution)/shard_map/step_half0/pallas_call | solution.py:134
  44.9 4.7 %step_half1.4 = (bf16[4,8,32,128]{3,2,1,0:T(8,128)(2,1)S(1)}, bf16[4,4,8,64,128]{4,3,2,1,0:T(8,128)(2,1)}) custom-call(s32[8,12]{1,0:T(8,128)S(1)} %fusion.30.refs_0_, bf16[4,8,64,768]{3,2,1,0:T(8,128)(2,1)S(1)} %bitcast.35, bf16[4,8,32,128]{3,2,1,0:T(8,128)(2,1)S(1)} %copy-done.3, bf16[4,8,32,128]{3,2,1,0:T(8,128)(2,1)} %collective-permute-done.refs_3_, ...), custom_call_target="tpu_custom_call" | custom-call | flops 402653184 | bytes 3145728 | tf_op jit(solution)/shard_map/step_half1/pallas_call | solution.py:134
  49.6 1.2 collective-permute-start.8
  50.8 2.7 %collective-permute-start.9 = (bf16[4,8,32,128]{3,2,1,0:T(8,128)(2,1)S(1)}, bf16[4,8,32,128]{3,2,1,0:T(8,128)(2,1)S(1)}, u32[]{:S(2)}, u32[]{:S(2)}) collective-permute-start(bf16[4,8,32,128]{3,2,1,0:T(8,128)(2,1)S(1)} %get-tuple-element.16.refs_2_), channel_id=1, source_target_pairs={{1,0},{2,1},{3,2},{0,3},{5,4},{6,5},{7,6},{4,7},{9,8},{10,9},{11,1... | collective-permute-start | bytes 786440 | tf_op jit(solution)/shard_map/ppermute | solution.py:156
  53.5 0.1 collective-permute-start.12
  53.6 3.8 %collective-permute-start.13 = (bf16[4,8,32,128]{3,2,1,0:T(8,128)(2,1)S(1)}, bf16[4,8,32,128]{3,2,1,0:T(8,128)(2,1)S(1)}, u32[]{:S(2)}, u32[]{:S(2)}) collective-permute-start(bf16[4,8,32,128]{3,2,1,0:T(8,128)(2,1)S(1)} %step_half0.4.refs_7_.refs_2_), channel_id=1, source_target_pairs={{1,0},{2,1},{3,2},{0,3},{5,4},{6,5},{7,6},{4,7},{9,8},{10,9},{11,1... | collective-permute-start | bytes 786440 | tf_op jit(solution)/shard_map/ppermute | solution.py:156
  57.4 7.8 %collective-permute-done.9.refs_4_ = bf16[4,8,32,128]{3,2,1,0:T(8,128)(2,1)S(1)} collective-permute-done((bf16[4,8,32,128]{3,2,1,0:T(8,128)(2,1)S(1)}, bf16[4,8,32,128]{3,2,1,0:T(8,128)(2,1)S(1)}, u32[]{:S(2)}, u32[]{:S(2)}) %collective-permute-start.9) | collective-permute-done | bytes 262176 | tf_op jit(solution)/shard_map/ppermute | solution.py:156
  65.2 1.5 collective-permute-start.10
  66.7 9.6 %collective-permute-done.13.refs_4_ = bf16[4,8,32,128]{3,2,1,0:T(8,128)(2,1)S(1)} collective-permute-done((bf16[4,8,32,128]{3,2,1,0:T(8,128)(2,1)S(1)}, bf16[4,8,32,128]{3,2,1,0:T(8,128)(2,1)S(1)}, u32[]{:S(2)}, u32[]{:S(2)}) %collective-permute-start.13) | collective-permute-done | bytes 262176 | tf_op jit(solution)/shard_map/ppermute | solution.py:156
  76.4 0.3 collective-permute-start.14
  76.8 2.4 %collective-permute-start.15 = (bf16[3,8,32,128]{3,2,1,0:T(8,128)(2,1)S(1)}, bf16[3,8,32,128]{3,2,1,0:T(8,128)(2,1)S(1)}, u32[]{:S(2)}, u32[]{:S(2)}) collective-permute-start(bf16[3,8,32,128]{3,2,1,0:T(8,128)(2,1)S(1)} %pad_maximum_fusion.7), channel_id=1, source_target_pairs={{4,0},{8,4},{12,8},{16,12},{20,16},{24,20},{28,24},{0,28},{5,1},{9... | collective-permute-start | bytes 589832 | tf_op jit(solution)/shard_map/ppermute | solution.py:156
  79.2 0.1 collective-permute-start.11
  79.3 4.1 %collective-permute-done.14.refs_5_ = bf16[3,8,32,128]{3,2,1,0:T(8,128)(2,1)S(1)} collective-permute-done((bf16[3,8,32,128]{3,2,1,0:T(8,128)(2,1)S(1)}, bf16[3,8,32,128]{3,2,1,0:T(8,128)(2,1)S(1)}, u32[]{:S(2)}, u32[]{:S(2)}) %collective-permute-start.14) | collective-permute-done | bytes 196640 | tf_op jit(solution)/shard_map/ppermute | solution.py:156
  83.4 3.1 %step_half0.5.refs_7_.refs_2_ = bf16[4,8,32,128]{3,2,1,0:T(8,128)(2,1)S(1)} custom-call(s32[8,12]{1,0:T(8,128)S(1)} %fusion.30.refs_0_, bf16[4,8,64,768]{3,2,1,0:T(8,128)(2,1)S(1)} %bitcast.36, bf16[4,8,32,128]{3,2,1,0:T(8,128)(2,1)S(1)} %step_half0.4.refs_7_.refs_2_, bf16[4,8,32,128]{3,2,1,0:T(8,128)(2,1)S(1)} %collective-permute-done.12.refs_3_, ...), custom_call_target="tpu_custom_call" | custom-call | flops 402653184 | bytes 3145728 | tf_op jit(solution)/shard_map/step_half0/pallas_call | solution.py:134
  86.5 4.3 %step_half1.5 = (bf16[4,8,32,128]{3,2,1,0:T(8,128)(2,1)S(1)}, bf16[4,4,8,64,128]{4,3,2,1,0:T(8,128)(2,1)}) custom-call(s32[8,12]{1,0:T(8,128)S(1)} %fusion.30.refs_0_, bf16[4,8,64,768]{3,2,1,0:T(8,128)(2,1)S(1)} %bitcast.37, bf16[4,8,32,128]{3,2,1,0:T(8,128)(2,1)S(1)} %get-tuple-element.16.refs_2_, ...), custom_call_target="tpu_custom_call", output_to_operand_aliasing={{1}: (8, {})} | custom-call | flops 402653184 | bytes 3145728 | tf_op jit(solution)/shard_map/step_half1/pallas_call | solution.py:134
  90.8 0.7 collective-permute-start.16
  91.5 3.2 %collective-permute-start.17 = (bf16[4,8,32,128]{3,2,1,0:T(8,128)(2,1)S(1)}, bf16[4,8,32,128]{3,2,1,0:T(8,128)(2,1)S(1)}, u32[]{:S(2)}, u32[]{:S(2)}) collective-permute-start(bf16[4,8,32,128]{3,2,1,0:T(8,128)(2,1)S(1)} %get-tuple-element.18.refs_2_), channel_id=1, source_target_pairs={{1,0},{2,1},{3,2},{0,3},{5,4},{6,5},{7,6},{4,7},{9,8},{10,9},{11,1... | collective-permute-start | bytes 786440 | tf_op jit(solution)/shard_map/ppermute | solution.py:156
  94.7 0.1 collective-permute-start.20
  94.8 3.8 %collective-permute-start.21 = (bf16[4,8,32,128]{3,2,1,0:T(8,128)(2,1)S(1)}, bf16[4,8,32,128]{3,2,1,0:T(8,128)(2,1)S(1)}, u32[]{:S(2)}, u32[]{:S(2)}) collective-permute-start(bf16[4,8,32,128]{3,2,1,0:T(8,128)(2,1)S(1)} %step_half0.5.refs_7_.refs_2_), channel_id=1, source_target_pairs={{1,0},{2,1},{3,2},{0,3},{5,4},{6,5},{7,6},{4,7},{9,8},{10,9},{11,1... | collective-permute-start | bytes 786440 | tf_op jit(solution)/shard_map/ppermute | solution.py:156
  98.6 7.6 %collective-permute-done.17.refs_4_ = bf16[4,8,32,128]{3,2,1,0:T(8,128)(2,1)S(1)} collective-permute-done((bf16[4,8,32,128]{3,2,1,0:T(8,128)(2,1)S(1)}, bf16[4,8,32,128]{3,2,1,0:T(8,128)(2,1)S(1)}, u32[]{:S(2)}, u32[]{:S(2)}) %collective-permute-start.17) | collective-permute-done | bytes 262176 | tf_op jit(solution)/shard_map/ppermute | solution.py:156
  106.3 0.3 collective-permute-start.18
  106.6 10.8 %collective-permute-done.21.refs_4_ = bf16[4,8,32,128]{3,2,1,0:T(8,128)(2,1)S(1)} collective-permute-done((bf16[4,8,32,128]{3,2,1,0:T(8,128)(2,1)S(1)}, bf16[4,8,32,128]{3,2,1,0:T(8,128)(2,1)S(1)}, u32[]{:S(2)}, u32[]{:S(2)}) %collective-permute-start.21) | collective-permute-done | bytes 262176 | tf_op jit(solution)/shard_map/ppermute | solution.py:156
  117.5 0.2 collective-permute-start.22
  117.7 2.6 %collective-permute-start.23 = (bf16[3,8,32,128]{3,2,1,0:T(8,128)(2,1)S(1)}, bf16[3,8,32,128]{3,2,1,0:T(8,128)(2,1)S(1)}, u32[]{:S(2)}, u32[]{:S(2)}) collective-permute-start(bf16[3,8,32,128]{3,2,1,0:T(8,128)(2,1)S(1)} %pad_maximum_fusion.11), channel_id=1, source_target_pairs={{4,0},{8,4},{12,8},{16,12},{20,16},{24,20},{28,24},{0,28},{5,1},{9... | collective-permute-start | bytes 589832 | tf_op jit(solution)/shard_map/ppermute | solution.py:156
  120.3 0.1 collective-permute-start.19
  120.4 5.3 %collective-permute-done.22.refs_5_ = bf16[3,8,32,128]{3,2,1,0:T(8,128)(2,1)S(1)} collective-permute-done((bf16[3,8,32,128]{3,2,1,0:T(8,128)(2,1)S(1)}, bf16[3,8,32,128]{3,2,1,0:T(8,128)(2,1)S(1)}, u32[]{:S(2)}, u32[]{:S(2)}) %collective-permute-start.22) | collective-permute-done | bytes 196640 | tf_op jit(solution)/shard_map/ppermute | solution.py:156
  125.7 3.1 %step_half0.6.refs_7_.refs_2_ = bf16[4,8,32,128]{3,2,1,0:T(8,128)(2,1)S(1)} custom-call(s32[8,12]{1,0:T(8,128)S(1)} %fusion.30.refs_0_, bf16[4,8,64,768]{3,2,1,0:T(8,128)(2,1)S(1)} %bitcast.38, bf16[4,8,32,128]{3,2,1,0:T(8,128)(2,1)S(1)} %step_half0.5.refs_7_.refs_2_, bf16[4,8,32,128]{3,2,1,0:T(8,128)(2,1)S(1)} %collective-permute-done.20.refs_3_, ...), custom_call_target="tpu_custom_call" | custom-call | flops 402653184 | bytes 3145728 | tf_op jit(solution)/shard_map/step_half0/pallas_call | solution.py:134
  128.8 4.3 %step_half1.6 = (bf16[4,8,32,128]{3,2,1,0:T(8,128)(2,1)S(1)}, bf16[4,4,8,64,128]{4,3,2,1,0:T(8,128)(2,1)}) custom-call(s32[8,12]{1,0:T(8,128)S(1)} %fusion.30.refs_0_, bf16[4,8,64,768]{3,2,1,0:T(8,128)(2,1)S(1)} %bitcast.39, bf16[4,8,32,128]{3,2,1,0:T(8,128)(2,1)S(1)} %get-tuple-element.18.refs_2_, ...), custom_call_target="tpu_custom_call", output_to_operand_aliasing={{1}: (8, {})} | custom-call | flops 402653184 | bytes 3145728 | tf_op jit(solution)/shard_map/step_half1/pallas_call | solution.py:134
  133.1 0.2 collective-permute-start.24
  133.3 3.7 %collective-permute-start.25 = (bf16[4,8,32,128]{3,2,1,0:T(8,128)(2,1)S(1)}, bf16[4,8,32,128]{3,2,1,0:T(8,128)(2,1)S(1)}, u32[]{:S(2)}, u32[]{:S(2)}) collective-permute-start(bf16[4,8,32,128]{3,2,1,0:T(8,128)(2,1)S(1)} %get-tuple-element.20.refs_2_), channel_id=1, source_target_pairs={{1,0},{2,1},{3,2},{0,3},{5,4},{6,5},{7,6},{4,7},{9,8},{10,9},{11,1... | collective-permute-start | bytes 786440 | tf_op jit(solution)/shard_map/ppermute | solution.py:156
  137.0 0.1 collective-permute-start.28
  137.1 3.8 %collective-permute-start.29 = (bf16[4,8,32,128]{3,2,1,0:T(8,128)(2,1)S(1)}, bf16[4,8,32,128]{3,2,1,0:T(8,128)(2,1)S(1)}, u32[]{:S(2)}, u32[]{:S(2)}) collective-permute-start(bf16[4,8,32,128]{3,2,1,0:T(8,128)(2,1)S(1)} %step_half0.6.refs_7_.refs_2_), channel_id=1, source_target_pairs={{1,0},{2,1},{3,2},{0,3},{5,4},{6,5},{7,6},{4,7},{9,8},{10,9},{11,1... | collective-permute-start | bytes 786440 | tf_op jit(solution)/shard_map/ppermute | solution.py:156
  140.9 8.7 %collective-permute-done.25.refs_4_ = bf16[4,8,32,128]{3,2,1,0:T(8,128)(2,1)S(1)} collective-permute-done((bf16[4,8,32,128]{3,2,1,0:T(8,128)(2,1)S(1)}, bf16[4,8,32,128]{3,2,1,0:T(8,128)(2,1)S(1)}, u32[]{:S(2)}, u32[]{:S(2)}) %collective-permute-start.25) | collective-permute-done | bytes 262176 | tf_op jit(solution)/shard_map/ppermute | solution.py:156
  149.7 0.1 collective-permute-start.26
  149.7 8.5 %collective-permute-done.29.refs_4_ = bf16[4,8,32,128]{3,2,1,0:T(8,128)(2,1)S(1)} collective-permute-done((bf16[4,8,32,128]{3,2,1,0:T(8,128)(2,1)S(1)}, bf16[4,8,32,128]{3,2,1,0:T(8,128)(2,1)S(1)}, u32[]{:S(2)}, u32[]{:S(2)}) %collective-permute-start.29) | collective-permute-done | bytes 262176 | tf_op jit(solution)/shard_map/ppermute | solution.py:156
  158.3 0.1 collective-permute-start.30
  158.4 2.7 %collective-permute-start.31 = (bf16[3,8,32,128]{3,2,1,0:T(8,128)(2,1)S(1)}, bf16[3,8,32,128]{3,2,1,0:T(8,128)(2,1)S(1)}, u32[]{:S(2)}, u32[]{:S(2)}) collective-permute-start(bf16[3,8,32,128]{3,2,1,0:T(8,128)(2,1)S(1)} %pad_maximum_fusion.15), channel_id=1, source_target_pairs={{4,0},{8,4},{12,8},{16,12},{20,16},{24,20},{28,24},{0,28},{5,1},{9... | collective-permute-start | bytes 589832 | tf_op jit(solution)/shard_map/ppermute | solution.py:156
  161.1 0.1 collective-permute-start.27
  161.2 5.2 %collective-permute-done.30.refs_5_ = bf16[3,8,32,128]{3,2,1,0:T(8,128)(2,1)S(1)} collective-permute-done((bf16[3,8,32,128]{3,2,1,0:T(8,128)(2,1)S(1)}, bf16[3,8,32,128]{3,2,1,0:T(8,128)(2,1)S(1)}, u32[]{:S(2)}, u32[]{:S(2)}) %collective-permute-start.30) | collective-permute-done | bytes 196640 | tf_op jit(solution)/shard_map/ppermute | solution.py:156
  166.4 3.1 %step_half0.7.refs_7_ = bf16[4,8,32,128]{3,2,1,0:T(8,128)(2,1)S(1)} custom-call(s32[8,12]{1,0:T(8,128)S(1)} %fusion.30.refs_0_, bf16[4,8,64,768]{3,2,1,0:T(8,128)(2,1)S(1)} %bitcast.40, bf16[4,8,32,128]{3,2,1,0:T(8,128)(2,1)S(1)} %step_half0.6.refs_7_.refs_2_, bf16[4,8,32,128]{3,2,1,0:T(8,128)(2,1)S(1)} %collective-permute-done.28.refs_3_, ...), custom_call_target="tpu_custom_call" | custom-call | flops 402653184 | bytes 3145728 | tf_op jit(solution)/shard_map/step_half0/pallas_call | solution.py:134
  169.5 4.3 %step_half1.7 = (bf16[4,8,32,128]{3,2,1,0:T(8,128)(2,1)}, bf16[4,4,8,64,128]{4,3,2,1,0:T(8,128)(2,1)}) custom-call(s32[8,12]{1,0:T(8,128)S(1)} %fusion.30.refs_0_, bf16[4,8,64,768]{3,2,1,0:T(8,128)(2,1)S(1)} %bitcast.41, bf16[4,8,32,128]{3,2,1,0:T(8,128)(2,1)S(1)} %get-tuple-element.20.refs_2_, ...), custom_call_target="tpu_custom_call", output_to_operand_aliasing={{1}: (8, {})} | custom-call | flops 402653184 | bytes 3145728 | tf_op jit(solution)/shard_map/step_half1/pallas_call | solution.py:134
  (71 shorter events, 0.7 us)
Async XLA Ops:
  0.0 12.4 %copy-start = (bf16[4,1,8,64,768]{4,3,2,1,0:T(8,128)(2,1)S(1)}, bf16[4,1,8,64,768]{4,3,2,1,0:T(8,128)(2,1)}, u32[]{:S(2)}) copy-start(bf16[4,1,8,64,768]{4,3,2,1,0:T(8,128)(2,1)} %param.4) | copy-start | bytes 9437188
  3.4 20.5 %collective-permute-start = (bf16[4,8,32,128]{3,2,1,0:T(8,128)(2,1)}, bf16[4,8,32,128]{3,2,1,0:T(8,128)(2,1)}, u32[]{:S(2)}, u32[]{:S(2)}) collective-permute-start(bf16[4,8,32,128]{3,2,1,0:T(8,128)(2,1)} %get-tuple-element.14.refs_2_), channel_id=1, source_target_pairs={{0,1},{1,2},{2,3},{3,0},{4,5},{5,6},{6,7},{7,4},{8,9},{9,10},{10,1... | collective-permute-start | bytes 786440 | tf_op jit(solution)/shard_map/ppermute | solution.py:156
  6.5 16.6 %collective-permute-start.1 = (bf16[4,8,32,128]{3,2,1,0:T(8,128)(2,1)}, bf16[4,8,32,128]{3,2,1,0:T(8,128)(2,1)}, u32[]{:S(2)}, u32[]{:S(2)}) collective-permute-start(bf16[4,8,32,128]{3,2,1,0:T(8,128)(2,1)} %get-tuple-element.14.refs_2_), channel_id=1, source_target_pairs={{1,0},{2,1},{3,2},{0,3},{5,4},{6,5},{7,6},{4,7},{9,8},{10,9},{11,1... | collective-permute-start | bytes 786440 | tf_op jit(solution)/shard_map/ppermute | solution.py:156
  8.5 23.8 %collective-permute-start.4 = (bf16[4,8,32,128]{3,2,1,0:T(8,128)(2,1)}, bf16[4,8,32,128]{3,2,1,0:T(8,128)(2,1)}, u32[]{:S(2)}, u32[]{:S(2)}) collective-permute-start(bf16[4,8,32,128]{3,2,1,0:T(8,128)(2,1)} %get-tuple-element.15.refs_2_), channel_id=1, source_target_pairs={{0,1},{1,2},{2,3},{3,0},{4,5},{5,6},{6,7},{7,4},{8,9},{9,10},{10,1... | collective-permute-start | bytes 786440 | tf_op jit(solution)/shard_map/ppermute | solution.py:156
  8.5 22.9 %collective-permute-start.5 = (bf16[4,8,32,128]{3,2,1,0:T(8,128)(2,1)}, bf16[4,8,32,128]{3,2,1,0:T(8,128)(2,1)}, u32[]{:S(2)}, u32[]{:S(2)}) collective-permute-start(bf16[4,8,32,128]{3,2,1,0:T(8,128)(2,1)} %get-tuple-element.15.refs_2_), channel_id=1, source_target_pairs={{1,0},{2,1},{3,2},{0,3},{5,4},{6,5},{7,6},{4,7},{9,8},{10,9},{11,1... | collective-permute-start | bytes 786440 | tf_op jit(solution)/shard_map/ppermute | solution.py:156
  12.4 5.3 %copy-start.3 = (bf16[4,8,32,128]{3,2,1,0:T(8,128)(2,1)S(1)}, bf16[4,8,32,128]{3,2,1,0:T(8,128)(2,1)}, u32[]{:S(2)}) copy-start(bf16[4,8,32,128]{3,2,1,0:T(8,128)(2,1)} %get-tuple-element.14.refs_2_) | copy-start | bytes 786436
  12.4 5.9 %copy-start.4 = (bf16[4,8,32,128]{3,2,1,0:T(8,128)(2,1)S(1)}, bf16[4,8,32,128]{3,2,1,0:T(8,128)(2,1)}, u32[]{:S(2)}) copy-start(bf16[4,8,32,128]{3,2,1,0:T(8,128)(2,1)} %get-tuple-element.15.refs_2_) | copy-start | bytes 786436
  23.0 13.0 %copy-start.6 = (s32[1,8,12]{2,1,0:T(8,128)S(1)}, s32[1,8,12]{2,1,0:T(8,128)}, u32[]{:S(2)}) copy-start(s32[1,8,12]{2,1,0:T(8,128)} %param.5) | copy-start | bytes 1156
  23.0 16.5 %copy-start.5 = (bf16[4,8,32,128]{3,2,1,0:T(8,128)(2,1)S(1)}, bf16[4,8,32,128]{3,2,1,0:T(8,128)(2,1)}, u32[]{:S(2)}) copy-start(bf16[4,8,32,128]{3,2,1,0:T(8,128)(2,1)} %get-tuple-element.15.refs_2_) | copy-start | bytes 786436
  25.7 19.2 %collective-permute-start.2 = (bf16[3,8,32,128]{3,2,1,0:T(8,128)(2,1)S(1)}, bf16[3,8,32,128]{3,2,1,0:T(8,128)(2,1)S(1)}, u32[]{:S(2)}, u32[]{:S(2)}) collective-permute-start(bf16[3,8,32,128]{3,2,1,0:T(8,128)(2,1)S(1)} %pad_maximum_fusion), channel_id=1, source_target_pairs={{0,4},{4,8},{8,12},{12,16},{16,20},{20,24},{24,28},{28,0},{1,5},{5... | collective-permute-start | bytes 589832 | tf_op jit(solution)/shard_map/ppermute | solution.py:156
  26.6 18.3 %collective-permute-start.3 = (bf16[3,8,32,128]{3,2,1,0:T(8,128)(2,1)S(1)}, bf16[3,8,32,128]{3,2,1,0:T(8,128)(2,1)S(1)}, u32[]{:S(2)}, u32[]{:S(2)}) collective-permute-start(bf16[3,8,32,128]{3,2,1,0:T(8,128)(2,1)S(1)} %pad_maximum_fusion.1), channel_id=1, source_target_pairs={{4,0},{8,4},{12,8},{16,12},{20,16},{24,20},{28,24},{0,28},{5,1},{9... | collective-permute-start | bytes 589832 | tf_op jit(solution)/shard_map/ppermute | solution.py:156
  33.2 6.2 %collective-permute-start.6 = (bf16[3,8,32,128]{3,2,1,0:T(8,128)(2,1)S(1)}, bf16[3,8,32,128]{3,2,1,0:T(8,128)(2,1)S(1)}, u32[]{:S(2)}, u32[]{:S(2)}) collective-permute-start(bf16[3,8,32,128]{3,2,1,0:T(8,128)(2,1)S(1)} %pad_maximum_fusion.2), channel_id=1, source_target_pairs={{0,4},{4,8},{8,12},{12,16},{16,20},{20,24},{24,28},{28,0},{1,5},{5... | collective-permute-start | bytes 589832 | tf_op jit(solution)/shard_map/ppermute | solution.py:156
  33.3 6.2 %collective-permute-start.7 = (bf16[3,8,32,128]{3,2,1,0:T(8,128)(2,1)S(1)}, bf16[3,8,32,128]{3,2,1,0:T(8,128)(2,1)S(1)}, u32[]{:S(2)}, u32[]{:S(2)}) collective-permute-start(bf16[3,8,32,128]{3,2,1,0:T(8,128)(2,1)S(1)} %pad_maximum_fusion.3), channel_id=1, source_target_pairs={{4,0},{8,4},{12,8},{16,12},{20,16},{24,20},{28,24},{0,28},{5,1},{9... | collective-permute-start | bytes 589832 | tf_op jit(solution)/shard_map/ppermute | solution.py:156
  39.5 1.9 %copy-start.1 = (bf16[2048,768]{1,0:T(8,128)(2,1)S(1)}, bf16[2048,768]{1,0:T(8,128)(2,1)}, u32[]{:S(2)}) copy-start(bf16[2048,768]{1,0:T(8,128)(2,1)} %copy.7) | copy-start | bytes 9437188
  49.6 33.8 %copy-start.2 = (bf16[2048,768]{1,0:T(8,128)(2,1)S(1)}, bf16[2048,768]{1,0:T(8,128)(2,1)}, u32[]{:S(2)}) copy-start(bf16[2048,768]{1,0:T(8,128)(2,1)} %copy.7) | copy-start | bytes 9437188
  49.6 15.6 %collective-permute-start.8 = (bf16[4,8,32,128]{3,2,1,0:T(8,128)(2,1)S(1)}, bf16[4,8,32,128]{3,2,1,0:T(8,128)(2,1)S(1)}, u32[]{:S(2)}, u32[]{:S(2)}) collective-permute-start(bf16[4,8,32,128]{3,2,1,0:T(8,128)(2,1)S(1)} %get-tuple-element.16.refs_2_), channel_id=1, source_target_pairs={{0,1},{1,2},{2,3},{3,0},{4,5},{5,6},{6,7},{7,4},{8,9},{9,10},{10,1... | collective-permute-start | bytes 786440 | tf_op jit(solution)/shard_map/ppermute | solution.py:156
  50.8 14.4 %collective-permute-start.9 = (bf16[4,8,32,128]{3,2,1,0:T(8,128)(2,1)S(1)}, bf16[4,8,32,128]{3,2,1,0:T(8,128)(2,1)S(1)}, u32[]{:S(2)}, u32[]{:S(2)}) collective-permute-start(bf16[4,8,32,128]{3,2,1,0:T(8,128)(2,1)S(1)} %get-tuple-element.16.refs_2_), channel_id=1, source_target_pairs={{1,0},{2,1},{3,2},{0,3},{5,4},{6,5},{7,6},{4,7},{9,8},{10,9},{11,1... | collective-permute-start | bytes 786440 | tf_op jit(solution)/shard_map/ppermute | solution.py:156
  53.5 22.9 %collective-permute-start.12 = (bf16[4,8,32,128]{3,2,1,0:T(8,128)(2,1)S(1)}, bf16[4,8,32,128]{3,2,1,0:T(8,128)(2,1)S(1)}, u32[]{:S(2)}, u32[]{:S(2)}) collective-permute-start(bf16[4,8,32,128]{3,2,1,0:T(8,128)(2,1)S(1)} %step_half0.4.refs_7_.refs_2_), channel_id=1, source_target_pairs={{0,1},{1,2},{2,3},{3,0},{4,5},{5,6},{6,7},{7,4},{8,9},{9,10},{10,1... | collective-permute-start | bytes 786440 | tf_op jit(solution)/shard_map/ppermute | solution.py:156
  53.6 22.8 %collective-permute-start.13 = (bf16[4,8,32,128]{3,2,1,0:T(8,128)(2,1)S(1)}, bf16[4,8,32,128]{3,2,1,0:T(8,128)(2,1)S(1)}, u32[]{:S(2)}, u32[]{:S(2)}) collective-permute-start(bf16[4,8,32,128]{3,2,1,0:T(8,128)(2,1)S(1)} %step_half0.4.refs_7_.refs_2_), channel_id=1, source_target_pairs={{1,0},{2,1},{3,2},{0,3},{5,4},{6,5},{7,6},{4,7},{9,8},{10,9},{11,1... | collective-permute-start | bytes 786440 | tf_op jit(solution)/shard_map/ppermute | solution.py:156
  65.2 21.3 %collective-permute-start.10 = (bf16[3,8,32,128]{3,2,1,0:T(8,128)(2,1)S(1)}, bf16[3,8,32,128]{3,2,1,0:T(8,128)(2,1)S(1)}, u32[]{:S(2)}, u32[]{:S(2)}) collective-permute-start(bf16[3,8,32,128]{3,2,1,0:T(8,128)(2,1)S(1)} %pad_maximum_fusion.4), channel_id=1, source_target_pairs={{0,4},{4,8},{8,12},{12,16},{16,20},{20,24},{24,28},{28,0},{1,5},{5... | collective-permute-start | bytes 589832 | tf_op jit(solution)/shard_map/ppermute | solution.py:156
  76.4 7.0 %collective-permute-start.14 = (bf16[3,8,32,128]{3,2,1,0:T(8,128)(2,1)S(1)}, bf16[3,8,32,128]{3,2,1,0:T(8,128)(2,1)S(1)}, u32[]{:S(2)}, u32[]{:S(2)}) collective-permute-start(bf16[3,8,32,128]{3,2,1,0:T(8,128)(2,1)S(1)} %pad_maximum_fusion.6), channel_id=1, source_target_pairs={{0,4},{4,8},{8,12},{12,16},{16,20},{20,24},{24,28},{28,0},{1,5},{5... | collective-permute-start | bytes 589832 | tf_op jit(solution)/shard_map/ppermute | solution.py:156
  76.8 6.6 %collective-permute-start.15 = (bf16[3,8,32,128]{3,2,1,0:T(8,128)(2,1)S(1)}, bf16[3,8,32,128]{3,2,1,0:T(8,128)(2,1)S(1)}, u32[]{:S(2)}, u32[]{:S(2)}) collective-permute-start(bf16[3,8,32,128]{3,2,1,0:T(8,128)(2,1)S(1)} %pad_maximum_fusion.7), channel_id=1, source_target_pairs={{4,0},{8,4},{12,8},{16,12},{20,16},{24,20},{28,24},{0,28},{5,1},{9... | collective-permute-start | bytes 589832 | tf_op jit(solution)/shard_map/ppermute | solution.py:156
  79.2 7.3 %collective-permute-start.11 = (bf16[3,8,32,128]{3,2,1,0:T(8,128)(2,1)S(1)}, bf16[3,8,32,128]{3,2,1,0:T(8,128)(2,1)S(1)}, u32[]{:S(2)}, u32[]{:S(2)}) collective-permute-start(bf16[3,8,32,128]{3,2,1,0:T(8,128)(2,1)S(1)} %pad_maximum_fusion.5), channel_id=1, source_target_pairs={{4,0},{8,4},{12,8},{16,12},{20,16},{24,20},{28,24},{0,28},{5,1},{9... | collective-permute-start | bytes 589832 | tf_op jit(solution)/shard_map/ppermute | solution.py:156
  90.8 15.4 %collective-permute-start.16 = (bf16[4,8,32,128]{3,2,1,0:T(8,128)(2,1)S(1)}, bf16[4,8,32,128]{3,2,1,0:T(8,128)(2,1)S(1)}, u32[]{:S(2)}, u32[]{:S(2)}) collective-permute-start(bf16[4,8,32,128]{3,2,1,0:T(8,128)(2,1)S(1)} %get-tuple-element.18.refs_2_), channel_id=1, source_target_pairs={{0,1},{1,2},{2,3},{3,0},{4,5},{5,6},{6,7},{7,4},{8,9},{9,10},{10,1... | collective-permute-start | bytes 786440 | tf_op jit(solution)/shard_map/ppermute | solution.py:156
  91.5 14.7 %collective-permute-start.17 = (bf16[4,8,32,128]{3,2,1,0:T(8,128)(2,1)S(1)}, bf16[4,8,32,128]{3,2,1,0:T(8,128)(2,1)S(1)}, u32[]{:S(2)}, u32[]{:S(2)}) collective-permute-start(bf16[4,8,32,128]{3,2,1,0:T(8,128)(2,1)S(1)} %get-tuple-element.18.refs_2_), channel_id=1, source_target_pairs={{1,0},{2,1},{3,2},{0,3},{5,4},{6,5},{7,6},{4,7},{9,8},{10,9},{11,1... | collective-permute-start | bytes 786440 | tf_op jit(solution)/shard_map/ppermute | solution.py:156
  94.7 22.7 %collective-permute-start.20 = (bf16[4,8,32,128]{3,2,1,0:T(8,128)(2,1)S(1)}, bf16[4,8,32,128]{3,2,1,0:T(8,128)(2,1)S(1)}, u32[]{:S(2)}, u32[]{:S(2)}) collective-permute-start(bf16[4,8,32,128]{3,2,1,0:T(8,128)(2,1)S(1)} %step_half0.5.refs_7_.refs_2_), channel_id=1, source_target_pairs={{0,1},{1,2},{2,3},{3,0},{4,5},{5,6},{6,7},{7,4},{8,9},{9,10},{10,1... | collective-permute-start | bytes 786440 | tf_op jit(solution)/shard_map/ppermute | solution.py:156
  94.8 22.7 %collective-permute-start.21 = (bf16[4,8,32,128]{3,2,1,0:T(8,128)(2,1)S(1)}, bf16[4,8,32,128]{3,2,1,0:T(8,128)(2,1)S(1)}, u32[]{:S(2)}, u32[]{:S(2)}) collective-permute-start(bf16[4,8,32,128]{3,2,1,0:T(8,128)(2,1)S(1)} %step_half0.5.refs_7_.refs_2_), channel_id=1, source_target_pairs={{1,0},{2,1},{3,2},{0,3},{5,4},{6,5},{7,6},{4,7},{9,8},{10,9},{11,1... | collective-permute-start | bytes 786440 | tf_op jit(solution)/shard_map/ppermute | solution.py:156
  106.3 22.5 %collective-permute-start.18 = (bf16[3,8,32,128]{3,2,1,0:T(8,128)(2,1)S(1)}, bf16[3,8,32,128]{3,2,1,0:T(8,128)(2,1)S(1)}, u32[]{:S(2)}, u32[]{:S(2)}) collective-permute-start(bf16[3,8,32,128]{3,2,1,0:T(8,128)(2,1)S(1)} %pad_maximum_fusion.8), channel_id=1, source_target_pairs={{0,4},{4,8},{8,12},{12,16},{16,20},{20,24},{24,28},{28,0},{1,5},{5... | collective-permute-start | bytes 589832 | tf_op jit(solution)/shard_map/ppermute | solution.py:156
  117.5 8.2 %collective-permute-start.22 = (bf16[3,8,32,128]{3,2,1,0:T(8,128)(2,1)S(1)}, bf16[3,8,32,128]{3,2,1,0:T(8,128)(2,1)S(1)}, u32[]{:S(2)}, u32[]{:S(2)}) collective-permute-start(bf16[3,8,32,128]{3,2,1,0:T(8,128)(2,1)S(1)} %pad_maximum_fusion.10), channel_id=1, source_target_pairs={{0,4},{4,8},{8,12},{12,16},{16,20},{20,24},{24,28},{28,0},{1,5},{5... | collective-permute-start | bytes 589832 | tf_op jit(solution)/shard_map/ppermute | solution.py:156
  117.7 8.0 %collective-permute-start.23 = (bf16[3,8,32,128]{3,2,1,0:T(8,128)(2,1)S(1)}, bf16[3,8,32,128]{3,2,1,0:T(8,128)(2,1)S(1)}, u32[]{:S(2)}, u32[]{:S(2)}) collective-permute-start(bf16[3,8,32,128]{3,2,1,0:T(8,128)(2,1)S(1)} %pad_maximum_fusion.11), channel_id=1, source_target_pairs={{4,0},{8,4},{12,8},{16,12},{20,16},{24,20},{28,24},{0,28},{5,1},{9... | collective-permute-start | bytes 589832 | tf_op jit(solution)/shard_map/ppermute | solution.py:156
  120.3 8.5 %collective-permute-start.19 = (bf16[3,8,32,128]{3,2,1,0:T(8,128)(2,1)S(1)}, bf16[3,8,32,128]{3,2,1,0:T(8,128)(2,1)S(1)}, u32[]{:S(2)}, u32[]{:S(2)}) collective-permute-start(bf16[3,8,32,128]{3,2,1,0:T(8,128)(2,1)S(1)} %pad_maximum_fusion.9), channel_id=1, source_target_pairs={{4,0},{8,4},{12,8},{16,12},{20,16},{24,20},{28,24},{0,28},{5,1},{9... | collective-permute-start | bytes 589832 | tf_op jit(solution)/shard_map/ppermute | solution.py:156
  133.1 16.5 %collective-permute-start.24 = (bf16[4,8,32,128]{3,2,1,0:T(8,128)(2,1)S(1)}, bf16[4,8,32,128]{3,2,1,0:T(8,128)(2,1)S(1)}, u32[]{:S(2)}, u32[]{:S(2)}) collective-permute-start(bf16[4,8,32,128]{3,2,1,0:T(8,128)(2,1)S(1)} %get-tuple-element.20.refs_2_), channel_id=1, source_target_pairs={{0,1},{1,2},{2,3},{3,0},{4,5},{5,6},{6,7},{7,4},{8,9},{9,10},{10,1... | collective-permute-start | bytes 786440 | tf_op jit(solution)/shard_map/ppermute | solution.py:156
  133.3 16.3 %collective-permute-start.25 = (bf16[4,8,32,128]{3,2,1,0:T(8,128)(2,1)S(1)}, bf16[4,8,32,128]{3,2,1,0:T(8,128)(2,1)S(1)}, u32[]{:S(2)}, u32[]{:S(2)}) collective-permute-start(bf16[4,8,32,128]{3,2,1,0:T(8,128)(2,1)S(1)} %get-tuple-element.20.refs_2_), channel_id=1, source_target_pairs={{1,0},{2,1},{3,2},{0,3},{5,4},{6,5},{7,6},{4,7},{9,8},{10,9},{11,1... | collective-permute-start | bytes 786440 | tf_op jit(solution)/shard_map/ppermute | solution.py:156
  137.0 21.2 %collective-permute-start.28 = (bf16[4,8,32,128]{3,2,1,0:T(8,128)(2,1)S(1)}, bf16[4,8,32,128]{3,2,1,0:T(8,128)(2,1)S(1)}, u32[]{:S(2)}, u32[]{:S(2)}) collective-permute-start(bf16[4,8,32,128]{3,2,1,0:T(8,128)(2,1)S(1)} %step_half0.6.refs_7_.refs_2_), channel_id=1, source_target_pairs={{0,1},{1,2},{2,3},{3,0},{4,5},{5,6},{6,7},{7,4},{8,9},{9,10},{10,1... | collective-permute-start | bytes 786440 | tf_op jit(solution)/shard_map/ppermute | solution.py:156
  137.1 21.2 %collective-permute-start.29 = (bf16[4,8,32,128]{3,2,1,0:T(8,128)(2,1)S(1)}, bf16[4,8,32,128]{3,2,1,0:T(8,128)(2,1)S(1)}, u32[]{:S(2)}, u32[]{:S(2)}) collective-permute-start(bf16[4,8,32,128]{3,2,1,0:T(8,128)(2,1)S(1)} %step_half0.6.refs_7_.refs_2_), channel_id=1, source_target_pairs={{1,0},{2,1},{3,2},{0,3},{5,4},{6,5},{7,6},{4,7},{9,8},{10,9},{11,1... | collective-permute-start | bytes 786440 | tf_op jit(solution)/shard_map/ppermute | solution.py:156
  149.7 19.8 %collective-permute-start.26 = (bf16[3,8,32,128]{3,2,1,0:T(8,128)(2,1)S(1)}, bf16[3,8,32,128]{3,2,1,0:T(8,128)(2,1)S(1)}, u32[]{:S(2)}, u32[]{:S(2)}) collective-permute-start(bf16[3,8,32,128]{3,2,1,0:T(8,128)(2,1)S(1)} %pad_maximum_fusion.12), channel_id=1, source_target_pairs={{0,4},{4,8},{8,12},{12,16},{16,20},{20,24},{24,28},{28,0},{1,5},{5... | collective-permute-start | bytes 589832 | tf_op jit(solution)/shard_map/ppermute | solution.py:156
  158.3 8.1 %collective-permute-start.30 = (bf16[3,8,32,128]{3,2,1,0:T(8,128)(2,1)S(1)}, bf16[3,8,32,128]{3,2,1,0:T(8,128)(2,1)S(1)}, u32[]{:S(2)}, u32[]{:S(2)}) collective-permute-start(bf16[3,8,32,128]{3,2,1,0:T(8,128)(2,1)S(1)} %pad_maximum_fusion.14), channel_id=1, source_target_pairs={{0,4},{4,8},{8,12},{12,16},{16,20},{20,24},{24,28},{28,0},{1,5},{5... | collective-permute-start | bytes 589832 | tf_op jit(solution)/shard_map/ppermute | solution.py:156
  158.4 8.0 %collective-permute-start.31 = (bf16[3,8,32,128]{3,2,1,0:T(8,128)(2,1)S(1)}, bf16[3,8,32,128]{3,2,1,0:T(8,128)(2,1)S(1)}, u32[]{:S(2)}, u32[]{:S(2)}) collective-permute-start(bf16[3,8,32,128]{3,2,1,0:T(8,128)(2,1)S(1)} %pad_maximum_fusion.15), channel_id=1, source_target_pairs={{4,0},{8,4},{12,8},{16,12},{20,16},{24,20},{28,24},{0,28},{5,1},{9... | collective-permute-start | bytes 589832 | tf_op jit(solution)/shard_map/ppermute | solution.py:156
  161.1 8.4 %collective-permute-start.27 = (bf16[3,8,32,128]{3,2,1,0:T(8,128)(2,1)S(1)}, bf16[3,8,32,128]{3,2,1,0:T(8,128)(2,1)S(1)}, u32[]{:S(2)}, u32[]{:S(2)}) collective-permute-start(bf16[3,8,32,128]{3,2,1,0:T(8,128)(2,1)S(1)} %pad_maximum_fusion.13), channel_id=1, source_target_pairs={{4,0},{8,4},{12,8},{16,12},{20,16},{24,20},{28,24},{0,28},{5,1},{9... | collective-permute-start | bytes 589832 | tf_op jit(solution)/shard_map/ppermute | solution.py:156

commit v2 on v1

--- a/solution.py
+++ b/solution.py
@@ -46,7 +46,7 @@
 
 
 def step_kernel(half, with_basis, *refs):
-    (table, blocks_ref, own, low_az, high_az, low_st, high_st), refs = refs[:7], refs[7:]
+    (table, blocks_ref, even_pair, odd_pair, low_st, high_st), refs = refs[:6], refs[6:]
     if with_basis:
         other_ref, refs = refs[0], refs[1:]
         if len(refs) == 5:
@@ -55,7 +55,7 @@
     else:
         next_ref, window, sems = refs
     faces, width, depth = blocks_ref.shape[1:]
-    columns = own.shape[0]
+    columns = even_pair.shape[1]
     span = columns + 2
     rows, lanes = window.shape[1:]
     i = pl.program_id(0)
@@ -63,10 +63,10 @@
     @pl.when(i == 0)
     def _():
         copies = []
-        view = window.reshape(3, span, faces, rows, lanes)
-        for azim, source in enumerate((low_az, own, high_az)):
+        view = window.reshape(4, span, faces, rows, lanes)
+        for azim in range(4):
+            source = (even_pair, odd_pair)[azim // 2].at[azim % 2]
             copies.append((source, view.at[azim, pl.ds(1, columns)]))
-        for azim in range(3):
             copies.append((low_st.at[azim], view.at[azim, 0]))
             copies.append((high_st.at[azim], view.at[azim, span - 1]))
         started = [
@@ -107,14 +107,14 @@
 
 def step(half, index, table, blocks, pieces, other=None, basis=None):
     columns, faces, width, depth = blocks.shape
-    rows, lanes = pieces[0].shape[2:]
+    rows, lanes = pieces[0].shape[3:]
     with_basis = half == HALVES - 1
     piece_spec = pl.BlockSpec((1, faces, rows, lanes), lambda i: (i, 0, 0, 0))
     any_spec = pl.BlockSpec(memory_space=pl.ANY)
     in_specs = [
         pl.BlockSpec(memory_space=pltpu.SMEM),
         pl.BlockSpec((1, faces, width, depth), lambda i: (i, 0, 0, 0)),
-    ] + [any_spec] * 5
+    ] + [any_spec] * 4
     args = [table, blocks, *pieces]
     out_specs = [piece_spec]
     out_shape = [jax.ShapeDtypeStruct((columns, faces, rows, lanes), jnp.bfloat16)]
@@ -139,8 +139,8 @@
         out_shape=out_shape,
         input_output_aliases=aliases,
         scratch_shapes=[
-            pltpu.VMEM((3 * (columns + 2) * faces, rows, lanes), jnp.bfloat16),
-            pltpu.SemaphoreType.DMA((9,)),
+            pltpu.VMEM((4 * (columns + 2) * faces, rows, lanes), jnp.bfloat16),
+            pltpu.SemaphoreType.DMA((12,)),
         ],
         cost_estimate=pl.CostEstimate(flops=flops, bytes_accessed=blocks.size * 2, transcendentals=0),
         compiler_params=pltpu.CompilerParams(vmem_limit_bytes=VMEM_LIMIT),
@@ -154,6 +154,12 @@
     if not up:
         pairs = [(target, source) for source, target in pairs]
     return lax.ppermute(value, axis, pairs)
+
+
+def with_partner(value, offset):
+    count = lax.axis_size("azim")
+    groups = [[i + offset, (i + offset + 1) % count] for i in range(0, count, 2)]
+    return lax.all_gather(value, "azim", axis_index_groups=groups)
 
 
 def halves_of_rows(blocks):
@@ -172,20 +178,22 @@
     start = start_vector.reshape(columns, faces, width, lanes)
     blocks = halves_of_rows(trace_blocks.reshape(columns, faces, width, -1))
     codes = neighbour.reshape(faces, -1)
-    table = (((codes // faces) % 3) * (columns + 2) + codes // (3 * faces)) * faces + codes % faces
+    place = jnp.where(lax.axis_index("azim") % 2 == 0, jnp.array([2, 0, 1]), jnp.array([0, 1, 3]))
+    table = (place[(codes // faces) % 3] * (columns + 2) + codes // (3 * faces)) * faces + codes % faces
     current = list(pack(start))
     basis = None
     for index in range(STEPS):
         around_z = [
-            (shift(current[h], "azim", True), shift(current[h], "azim", False))
+            (with_partner(current[h], 0), with_partner(current[h], 1))
             for h in range(HALVES)
         ]
         for h in range(HALVES):
-            low_az, high_az = around_z[h]
-            trio = (low_az, current[h], high_az)
-            low_st = shift(jnp.stack([part[columns - 1] for part in trio]), "stream", True)
-            high_st = shift(jnp.stack([part[0] for part in trio]), "stream", False)
-            pieces = (current[h], low_az, high_az, low_st, high_st)
+            pairs = around_z[h]
+            low_st = shift(
+                jnp.concatenate([pair[:, columns - 1] for pair in pairs]), "stream", True
+            )
+            high_st = shift(jnp.concatenate([pair[:, 0] for pair in pairs]), "stream", False)
+            pieces = (*pairs, low_st, high_st)
             if h < HALVES - 1:
                 (current[h],) = step(h, index, table, blocks, pieces)
             else:

time: 174 us -> 274 us (1.57)
  blocking collectives: 0 us -> 168 us
  waiting for transfers between devices: 73.2 us -> 32.3 us
  starting transfers between devices: 48 us -> 15.3 us
    all_gather x0 -> x16, blocking collectives: none -> 168 us  [with_partner(): return lax.all_gather(value, 'azim', axis_index_groups=groups)]
    ppermute x32 -> x16, waiting for transfers between devices: 73.2 us -> 32.3 us  [shift(): return lax.ppermute(value, axis, pairs)]
    ppermute x32 -> x16, starting transfers between devices: 48 us -> 15.3 us  [shift(): return lax.ppermute(value, axis, pairs)]
    slice x24 -> x0, local copies, waits for them, and re-layouts: 4.41 us -> none  [local(): high_st = shift(jnp.stack([part[0] for part in trio]), 'stream', False)]
    unnamed x14 -> x28, local copies, waits for them, and re-layouts: 1.92 us -> 5.51 us
    concatenate x0 -> x16, other arithmetic: none -> 3.25 us  [the longest x8 1.63 us: local(): jnp.concatenate([pair[:, 0] for pair in pairs])]
  transfers between devices with their start and end apart: 32 -> 16, of which waited for: 12 -> 3; matrix products, arithmetic and copies ran while one was open for 9% -> 5% of each run, Pallas kernels for 7% -> 5%
where the time goes in v2:
time: 274 us; the launch traced here: 272 us
  blocking collectives  168 us (61%)
  Pallas kernels  35.6 us (13%)
  waiting for transfers between devices  32.3 us (12%)
  starting transfers between devices  15.3 us (6%)
  local copies, waits for them, and re-layouts  11.9 us (4%)
  matrix products  5.27 us (2%)
  other arithmetic  3.33 us (1%)
    all_gather x16, blocking collectives, with_partner(): return lax.all_gather(value, 'azim', axis_index_groups=groups)  168 us
    ppermute x16, waiting for transfers between devices, shift(): return lax.ppermute(value, axis, pairs)  32.3 us
    pallas_call x8, Pallas kernels, step(): pl.pallas_call(functools.partial(step_kernel, half, with_basis), grid=(co...  32.1 us
    ppermute x16, starting transfers between devices, shift(): return lax.ppermute(value, axis, pairs)  15.3 us
    unnamed x28, local copies, waits for them, and re-layouts  5.51 us
  transfers between devices with their start and end apart: 16, of which 3 were waited for; matrix products, arithmetic and copies ran while one was open for 5% of the time, Pallas kernels for 5%

profile of v2, /device:TPU:0, one launch (start us, length us, event | category | flops | bytes accessed | tf_op | source)
XLA Modules:
  0.0 271.9 jit_solution(16961790977642037346)
XLA Ops:
  0.0 3.5 %pack.1 = (bf16[4,8,32,128]{3,2,1,0:T(8,128)(2,1)}, bf16[4,8,32,128]{3,2,1,0:T(8,128)(2,1)}) custom-call(bf16[4,8,64,128]{3,2,1,0:T(8,128)(2,1)} %bitcast.237), custom_call_target="tpu_custom_call" | custom-call | tf_op jit(solution)/shard_map/pack/pallas_call | solution.py:38
  3.5 10.4 %all-gather = bf16[8,8,32,128]{3,2,1,0:T(8,128)(2,1)S(1)} all-gather(bf16[4,8,32,128]{3,2,1,0:T(8,128)(2,1)} %get-tuple-element.14), channel_id=2, replica_groups={{0,1},{2,3},{4,5},{6,7},{8,9},{10,11},{12,13},{14,15},{16,17},{18,19},{..., dimensions={0}, use_global_device_ids=true | all-gather | bytes 786432 | tf_op jit(solution)/shard_map/all_gather | solution.py:162
  13.9 10.3 %all-gather.1 = bf16[8,8,32,128]{3,2,1,0:T(8,128)(2,1)S(1)} all-gather(bf16[4,8,32,128]{3,2,1,0:T(8,128)(2,1)} %get-tuple-element.14), channel_id=3, replica_groups={{1,2},{3,0},{5,6},{7,4},{9,10},{11,8},{13,14},{15,12},{17,18},{19,16},{..., dimensions={0}, use_global_device_ids=true | all-gather | bytes 786432 | tf_op jit(solution)/shard_map/all_gather | solution.py:162
  24.2 0.7 copy-done.4
  24.9 0.8 pad_maximum_fusion
  25.7 0.0 collective-permute-start
  25.7 0.7 pad_maximum_fusion.1
  26.4 2.6 collective-permute-start.1
  29.1 11.2 %all-gather.2 = bf16[8,8,32,128]{3,2,1,0:T(8,128)(2,1)S(1)} all-gather(bf16[4,8,32,128]{3,2,1,0:T(8,128)(2,1)S(1)} %copy-done.10), channel_id=4, replica_groups={{0,1},{2,3},{4,5},{6,7},{8,9},{10,11},{12,13},{14,15},{16,17},{18,19},{..., dimensions={0}, use_global_device_ids=true | all-gather | bytes 786432 | tf_op jit(solution)/shard_map/all_gather | solution.py:162
  40.3 9.1 %all-gather.3 = bf16[8,8,32,128]{3,2,1,0:T(8,128)(2,1)S(1)} all-gather(bf16[4,8,32,128]{3,2,1,0:T(8,128)(2,1)S(1)} %copy-done.10), channel_id=5, replica_groups={{1,2},{3,0},{5,6},{7,4},{9,10},{11,8},{13,14},{15,12},{17,18},{19,16},{..., dimensions={0}, use_global_device_ids=true | all-gather | bytes 786432 | tf_op jit(solution)/shard_map/all_gather | solution.py:162
  49.4 0.8 copy-done.8
  50.2 0.7 pad_maximum_fusion.2
  50.9 0.0 collective-permute-start.2
  50.9 0.7 pad_maximum_fusion.3
  51.7 2.6 collective-permute-start.3
  54.4 0.1 reshape.118
  54.5 1.2 gather_fusion
  55.8 5.3 %fusion = bf16[2048,768]{0,1:T(8,128)(2,1)} fusion(bf16[2048,768]{1,0:T(8,128)(2,1)S(1)} %bitcast.196, s32[768]{0:T(1024)S(1)} %get-tuple-element.55, s32[768]{0:T(1024)S(1)} %get-tuple-element.61, s32[768]{0:T(1024)S(1)} %get-tuple-element.56, s32[768]{0:T(1024)S(1)} %get-tuple-element.58, s32[768]{0:T(1024)S(1)} %get-tuple-element.57, ...), kind=kOutput, calls=%fused_computation.7 | convolution fusion | flops 2429288448 | bytes 6312192 | tf_op jit(solution)/shard_map/dot_general | solution.py:172
  61.0 0.1 reshape.142
  61.1 4.6 %copy.61 = bf16[2048,768]{1,0:T(8,128)(2,1)} copy(bf16[2048,768]{0,1:T(8,128)(2,1)} %fusion) | data formatting | bytes 6291456 | tf_op jit(solution)/shard_map/convert_element_type | solution.py:173
  65.8 1.9 copy-done.1
  67.7 1.0 copy-done.7
  68.7 1.0 copy-done.9
  69.8 3.6 %step_half0.4.refs_6_ = bf16[4,8,32,128]{3,2,1,0:T(8,128)(2,1)S(1)} custom-call(s32[8,12]{1,0:T(8,128)S(1)} %fusion.30.refs_0_, bf16[4,8,64,768]{3,2,1,0:T(8,128)(2,1)S(1)} %bitcast.197, bf16[2,4,8,32,128]{4,3,2,1,0:T(8,128)(2,1)S(1)} %bitcast.222, bf16[2,4,8,32,128]{4,3,2,1,0:T(8,128)(2,1)S(1)} %bitcast.224, ...), custom_call_target="tpu_custom_call" | custom-call | flops 402653184 | bytes 3145728 | tf_op jit(solution)/shard_map/step_half0/pallas_call | solution.py:134
  73.4 0.0 collective-permute-done.refs_4_
  73.4 5.0 %step_half1.4 = (bf16[4,8,32,128]{3,2,1,0:T(8,128)(2,1)S(1)}, bf16[4,4,8,64,128]{4,3,2,1,0:T(8,128)(2,1)}) custom-call(s32[8,12]{1,0:T(8,128)S(1)} %fusion.30.refs_0_, bf16[4,8,64,768]{3,2,1,0:T(8,128)(2,1)S(1)} %bitcast.198, bf16[2,4,8,32,128]{4,3,2,1,0:T(8,128)(2,1)S(1)} %bitcast.218, bf16[2,4,8,32,128]{4,3,2,1,0:T(8,128)(2,1)S(1)} %bitcast.220, ...), custom_call_target="tpu_custom_call" | custom-call | flops 402653184 | bytes 3145728 | tf_op jit(solution)/shard_map/step_half1/pallas_call | solution.py:134
  78.4 12.3 %all-gather.4 = bf16[8,8,32,128]{3,2,1,0:T(8,128)(2,1)S(1)} all-gather(bf16[4,8,32,128]{3,2,1,0:T(8,128)(2,1)S(1)} %get-tuple-element.16), channel_id=6, replica_groups={{0,1},{2,3},{4,5},{6,7},{8,9},{10,11},{12,13},{14,15},{16,17},{18,19},{..., dimensions={0}, use_global_device_ids=true | all-gather | bytes 786432 | tf_op jit(solution)/shard_map/all_gather | solution.py:162
  90.7 10.2 %all-gather.5 = bf16[8,8,32,128]{3,2,1,0:T(8,128)(2,1)S(1)} all-gather(bf16[4,8,32,128]{3,2,1,0:T(8,128)(2,1)S(1)} %get-tuple-element.16), channel_id=7, replica_groups={{1,2},{3,0},{5,6},{7,4},{9,10},{11,8},{13,14},{15,12},{17,18},{19,16},{..., dimensions={0}, use_global_device_ids=true | all-gather | bytes 786432 | tf_op jit(solution)/shard_map/all_gather | solution.py:162
  100.8 11.3 %all-gather.6 = bf16[8,8,32,128]{3,2,1,0:T(8,128)(2,1)S(1)} all-gather(bf16[4,8,32,128]{3,2,1,0:T(8,128)(2,1)S(1)} %step_half0.4.refs_6_), channel_id=8, replica_groups={{0,1},{2,3},{4,5},{6,7},{8,9},{10,11},{12,13},{14,15},{16,17},{18,19},{..., dimensions={0}, use_global_device_ids=true | all-gather | bytes 786432 | tf_op jit(solution)/shard_map/all_gather | solution.py:162
  112.1 9.2 %all-gather.7 = bf16[8,8,32,128]{3,2,1,0:T(8,128)(2,1)S(1)} all-gather(bf16[4,8,32,128]{3,2,1,0:T(8,128)(2,1)S(1)} %step_half0.4.refs_6_), channel_id=9, replica_groups={{1,2},{3,0},{5,6},{7,4},{9,10},{11,8},{13,14},{15,12},{17,18},{19,16},{..., dimensions={0}, use_global_device_ids=true | all-gather | bytes 786432 | tf_op jit(solution)/shard_map/all_gather | solution.py:162
  121.4 0.1 collective-permute-start.4
  121.5 0.1 collective-permute-start.6
  121.6 2.7 collective-permute-start.7
  124.3 0.5 collective-permute-start.5
  124.9 10.8 %collective-permute-done.6.refs_4_ = bf16[4,8,32,128]{3,2,1,0:T(8,128)(2,1)S(1)} collective-permute-done((bf16[4,8,32,128]{3,2,1,0:T(8,128)(2,1)S(1)}, bf16[4,8,32,128]{3,2,1,0:T(8,128)(2,1)S(1)}, u32[]{:S(2)}, u32[]{:S(2)}) %collective-permute-start.6) | collective-permute-done | bytes 262176 | tf_op jit(solution)/shard_map/ppermute | solution.py:156
  135.6 3.3 %step_half0.5.refs_6_ = bf16[4,8,32,128]{3,2,1,0:T(8,128)(2,1)S(1)} custom-call(s32[8,12]{1,0:T(8,128)S(1)} %fusion.30.refs_0_, bf16[4,8,64,768]{3,2,1,0:T(8,128)(2,1)S(1)} %bitcast.199, bf16[2,4,8,32,128]{4,3,2,1,0:T(8,128)(2,1)S(1)} %bitcast.226, bf16[2,4,8,32,128]{4,3,2,1,0:T(8,128)(2,1)S(1)} %bitcast.228, ...), custom_call_target="tpu_custom_call" | custom-call | flops 402653184 | bytes 3145728 | tf_op jit(solution)/shard_map/step_half0/pallas_call | solution.py:134
  138.9 0.0 collective-permute-done.5.refs_5_
  139.0 4.6 %step_half1.5 = (bf16[4,8,32,128]{3,2,1,0:T(8,128)(2,1)S(1)}, bf16[4,4,8,64,128]{4,3,2,1,0:T(8,128)(2,1)}) custom-call(s32[8,12]{1,0:T(8,128)S(1)} %fusion.30.refs_0_, bf16[4,8,64,768]{3,2,1,0:T(8,128)(2,1)S(1)} %bitcast.200, bf16[2,4,8,32,128]{4,3,2,1,0:T(8,128)(2,1)S(1)} %bitcast.210, ...), custom_call_target="tpu_custom_call", output_to_operand_aliasing={{1}: (7, {})} | custom-call | flops 402653184 | bytes 3145728 | tf_op jit(solution)/shard_map/step_half1/pallas_call | solution.py:134
  143.5 13.0 %all-gather.8 = bf16[8,8,32,128]{3,2,1,0:T(8,128)(2,1)S(1)} all-gather(bf16[4,8,32,128]{3,2,1,0:T(8,128)(2,1)S(1)} %get-tuple-element.18), channel_id=10, replica_groups={{0,1},{2,3},{4,5},{6,7},{8,9},{10,11},{12,13},{14,15},{16,17},{18,19},{..., dimensions={0}, use_global_device_ids=true | all-gather | bytes 786432 | tf_op jit(solution)/shard_map/all_gather | solution.py:162
  156.5 9.9 %all-gather.9 = bf16[8,8,32,128]{3,2,1,0:T(8,128)(2,1)S(1)} all-gather(bf16[4,8,32,128]{3,2,1,0:T(8,128)(2,1)S(1)} %get-tuple-element.18), channel_id=11, replica_groups={{1,2},{3,0},{5,6},{7,4},{9,10},{11,8},{13,14},{15,12},{17,18},{19,16},{..., dimensions={0}, use_global_device_ids=true | all-gather | bytes 786432 | tf_op jit(solution)/shard_map/all_gather | solution.py:162
  166.4 9.8 %all-gather.10 = bf16[8,8,32,128]{3,2,1,0:T(8,128)(2,1)S(1)} all-gather(bf16[4,8,32,128]{3,2,1,0:T(8,128)(2,1)S(1)} %step_half0.5.refs_6_), channel_id=12, replica_groups={{0,1},{2,3},{4,5},{6,7},{8,9},{10,11},{12,13},{14,15},{16,17},{18,19},{..., dimensions={0}, use_global_device_ids=true | all-gather | bytes 786432 | tf_op jit(solution)/shard_map/all_gather | solution.py:162
  176.2 8.9 %all-gather.11 = bf16[8,8,32,128]{3,2,1,0:T(8,128)(2,1)S(1)} all-gather(bf16[4,8,32,128]{3,2,1,0:T(8,128)(2,1)S(1)} %step_half0.5.refs_6_), channel_id=13, replica_groups={{1,2},{3,0},{5,6},{7,4},{9,10},{11,8},{13,14},{15,12},{17,18},{19,16},{..., dimensions={0}, use_global_device_ids=true | all-gather | bytes 786432 | tf_op jit(solution)/shard_map/all_gather | solution.py:162
  185.3 0.1 collective-permute-start.8
  185.4 0.2 collective-permute-start.10
  185.7 2.5 collective-permute-start.11
  188.2 0.5 collective-permute-start.9
  188.8 10.8 %collective-permute-done.10.refs_4_ = bf16[4,8,32,128]{3,2,1,0:T(8,128)(2,1)S(1)} collective-permute-done((bf16[4,8,32,128]{3,2,1,0:T(8,128)(2,1)S(1)}, bf16[4,8,32,128]{3,2,1,0:T(8,128)(2,1)S(1)}, u32[]{:S(2)}, u32[]{:S(2)}) %collective-permute-start.10) | collective-permute-done | bytes 262176 | tf_op jit(solution)/shard_map/ppermute | solution.py:156
  199.5 0.0 collective-permute-done.11.refs_5_
  199.5 3.3 %step_half0.6.refs_6_ = bf16[4,8,32,128]{3,2,1,0:T(8,128)(2,1)S(1)} custom-call(s32[8,12]{1,0:T(8,128)S(1)} %fusion.30.refs_0_, bf16[4,8,64,768]{3,2,1,0:T(8,128)(2,1)S(1)} %bitcast.201, bf16[2,4,8,32,128]{4,3,2,1,0:T(8,128)(2,1)S(1)} %bitcast.230, bf16[2,4,8,32,128]{4,3,2,1,0:T(8,128)(2,1)S(1)} %bitcast.232, ...), custom_call_target="tpu_custom_call" | custom-call | flops 402653184 | bytes 3145728 | tf_op jit(solution)/shard_map/step_half0/pallas_call | solution.py:134
  202.8 0.0 collective-permute-done.9.refs_5_
  202.9 4.6 %step_half1.6 = (bf16[4,8,32,128]{3,2,1,0:T(8,128)(2,1)S(1)}, bf16[4,4,8,64,128]{4,3,2,1,0:T(8,128)(2,1)}) custom-call(s32[8,12]{1,0:T(8,128)S(1)} %fusion.30.refs_0_, bf16[4,8,64,768]{3,2,1,0:T(8,128)(2,1)S(1)} %bitcast.202, bf16[2,4,8,32,128]{4,3,2,1,0:T(8,128)(2,1)S(1)} %bitcast.214, ...), custom_call_target="tpu_custom_call", output_to_operand_aliasing={{1}: (7, {})} | custom-call | flops 402653184 | bytes 3145728 | tf_op jit(solution)/shard_map/step_half1/pallas_call | solution.py:134
  207.4 8.8 %all-gather.12 = bf16[8,8,32,128]{3,2,1,0:T(8,128)(2,1)S(1)} all-gather(bf16[4,8,32,128]{3,2,1,0:T(8,128)(2,1)S(1)} %get-tuple-element.20), channel_id=14, replica_groups={{0,1},{2,3},{4,5},{6,7},{8,9},{10,11},{12,13},{14,15},{16,17},{18,19},{..., dimensions={0}, use_global_device_ids=true | all-gather | bytes 786432 | tf_op jit(solution)/shard_map/all_gather | solution.py:162
  216.2 10.0 %all-gather.13 = bf16[8,8,32,128]{3,2,1,0:T(8,128)(2,1)S(1)} all-gather(bf16[4,8,32,128]{3,2,1,0:T(8,128)(2,1)S(1)} %get-tuple-element.20), channel_id=15, replica_groups={{1,2},{3,0},{5,6},{7,4},{9,10},{11,8},{13,14},{15,12},{17,18},{19,16},{..., dimensions={0}, use_global_device_ids=true | all-gather | bytes 786432 | tf_op jit(solution)/shard_map/all_gather | solution.py:162
  226.2 13.2 %all-gather.14 = bf16[8,8,32,128]{3,2,1,0:T(8,128)(2,1)S(1)} all-gather(bf16[4,8,32,128]{3,2,1,0:T(8,128)(2,1)S(1)} %step_half0.6.refs_6_), channel_id=16, replica_groups={{0,1},{2,3},{4,5},{6,7},{8,9},{10,11},{12,13},{14,15},{16,17},{18,19},{..., dimensions={0}, use_global_device_ids=true | all-gather | bytes 786432 | tf_op jit(solution)/shard_map/all_gather | solution.py:162
  239.4 10.3 %all-gather.15 = bf16[8,8,32,128]{3,2,1,0:T(8,128)(2,1)S(1)} all-gather(bf16[4,8,32,128]{3,2,1,0:T(8,128)(2,1)S(1)} %step_half0.6.refs_6_), channel_id=17, replica_groups={{1,2},{3,0},{5,6},{7,4},{9,10},{11,8},{13,14},{15,12},{17,18},{19,16},{..., dimensions={0}, use_global_device_ids=true | all-gather | bytes 786432 | tf_op jit(solution)/shard_map/all_gather | solution.py:162
  249.8 0.1 collective-permute-start.12
  249.9 0.1 collective-permute-start.14
  250.0 2.7 collective-permute-start.15
  252.7 0.5 collective-permute-start.13
  253.3 10.8 %collective-permute-done.14.refs_4_ = bf16[4,8,32,128]{3,2,1,0:T(8,128)(2,1)S(1)} collective-permute-done((bf16[4,8,32,128]{3,2,1,0:T(8,128)(2,1)S(1)}, bf16[4,8,32,128]{3,2,1,0:T(8,128)(2,1)S(1)}, u32[]{:S(2)}, u32[]{:S(2)}) %collective-permute-start.14) | collective-permute-done | bytes 262176 | tf_op jit(solution)/shard_map/ppermute | solution.py:156
  264.0 3.3 %step_half0.7.refs_6_ = bf16[4,8,32,128]{3,2,1,0:T(8,128)(2,1)S(1)} custom-call(s32[8,12]{1,0:T(8,128)S(1)} %fusion.30.refs_0_, bf16[4,8,64,768]{3,2,1,0:T(8,128)(2,1)S(1)} %bitcast.203, bf16[2,4,8,32,128]{4,3,2,1,0:T(8,128)(2,1)S(1)} %bitcast.234, bf16[2,4,8,32,128]{4,3,2,1,0:T(8,128)(2,1)S(1)} %bitcast.236, ...), custom_call_target="tpu_custom_call" | custom-call | flops 402653184 | bytes 3145728 | tf_op jit(solution)/shard_map/step_half0/pallas_call | solution.py:134
  267.3 0.0 collective-permute-done.12.refs_4_
  267.3 0.0 collective-permute-done.13.refs_5_
  267.3 4.6 %step_half1.7 = (bf16[4,8,32,128]{3,2,1,0:T(8,128)(2,1)}, bf16[4,4,8,64,128]{4,3,2,1,0:T(8,128)(2,1)}) custom-call(s32[8,12]{1,0:T(8,128)S(1)} %fusion.30.refs_0_, bf16[4,8,64,768]{3,2,1,0:T(8,128)(2,1)S(1)} %bitcast.204, bf16[2,4,8,32,128]{4,3,2,1,0:T(8,128)(2,1)S(1)} %bitcast.206, ...), custom_call_target="tpu_custom_call", output_to_operand_aliasing={{1}: (7, {})} | custom-call | flops 402653184 | bytes 3145728 | tf_op jit(solution)/shard_map/step_half1/pallas_call | solution.py:134
  (68 shorter events, 0.8 us)
Async XLA Ops:
  0.0 55.7 %copy-start = (bf16[4,1,8,64,768]{4,3,2,1,0:T(8,128)(2,1)S(1)}, bf16[4,1,8,64,768]{4,3,2,1,0:T(8,128)(2,1)}, u32[]{:S(2)}) copy-start(bf16[4,1,8,64,768]{4,3,2,1,0:T(8,128)(2,1)} %param.6) | copy-start | bytes 9437188
  3.5 25.6 %copy-start.10 = (bf16[4,8,32,128]{3,2,1,0:T(8,128)(2,1)S(1)}, bf16[4,8,32,128]{3,2,1,0:T(8,128)(2,1)}, u32[]{:S(2)}) copy-start(bf16[4,8,32,128]{3,2,1,0:T(8,128)(2,1)} %get-tuple-element.15) | copy-start | bytes 786436
  13.9 10.3 %copy-start.2 = (bf16[8,8,32,128]{3,2,1,0:T(8,128)(2,1)}, bf16[8,8,32,128]{3,2,1,0:T(8,128)(2,1)S(1)}, u32[]{:S(2)}) copy-start(bf16[8,8,32,128]{3,2,1,0:T(8,128)(2,1)S(1)} %all-gather) | copy-start | bytes 1572868
  24.1 0.8 copy-start.4
  24.9 29.4 %copy-start.11 = (s32[1,8,12]{2,1,0:T(8,128)S(1)}, s32[1,8,12]{2,1,0:T(8,128)}, u32[]{:S(2)}) copy-start(s32[1,8,12]{2,1,0:T(8,128)} %param.7) | copy-start | bytes 1156
  24.9 29.5 %copy-start.12 = (s32[3]{0:T(128)S(1)}, s32[3]{0:T(128)}, u32[]{:S(2)}) copy-start(s32[3]{0:T(128)} %constant.116.clone) | copy-start | bytes 40
  24.9 29.6 %copy-start.13 = (s32[3]{0:T(128)S(1)}, s32[3]{0:T(128)}, u32[]{:S(2)}) copy-start(s32[3]{0:T(128)} %constant.117.clone) | copy-start | bytes 40
  25.7 47.7 %collective-permute-start = (bf16[4,8,32,128]{3,2,1,0:T(8,128)(2,1)}, bf16[4,8,32,128]{3,2,1,0:T(8,128)(2,1)S(1)}, u32[]{:S(2)}, u32[]{:S(2)}) collective-permute-start(bf16[4,8,32,128]{3,2,1,0:T(8,128)(2,1)} %pad_maximum_fusion), channel_id=1, source_target_pairs={{0,4},{4,8},{8,12},{12,16},{16,20},{20,24},{24,28},{28,0},{1,5},{5... | collective-permute-start | bytes 786440 | tf_op jit(solution)/shard_map/ppermute | solution.py:156
  26.4 46.9 %collective-permute-start.1 = (bf16[4,8,32,128]{3,2,1,0:T(8,128)(2,1)}, bf16[4,8,32,128]{3,2,1,0:T(8,128)(2,1)}, u32[]{:S(2)}, u32[]{:S(2)}) collective-permute-start(bf16[4,8,32,128]{3,2,1,0:T(8,128)(2,1)} %pad_maximum_fusion.1), channel_id=1, source_target_pairs={{4,0},{8,4},{12,8},{16,12},{20,16},{24,20},{28,24},{0,28},{5,1},{9... | collective-permute-start | bytes 786440 | tf_op jit(solution)/shard_map/ppermute | solution.py:156
  40.3 9.1 %copy-start.6 = (bf16[8,8,32,128]{3,2,1,0:T(8,128)(2,1)}, bf16[8,8,32,128]{3,2,1,0:T(8,128)(2,1)S(1)}, u32[]{:S(2)}) copy-start(bf16[8,8,32,128]{3,2,1,0:T(8,128)(2,1)S(1)} %all-gather.2) | copy-start | bytes 1572868
  49.4 0.8 copy-start.8
  50.9 14.8 %collective-permute-start.2 = (bf16[4,8,32,128]{3,2,1,0:T(8,128)(2,1)}, bf16[4,8,32,128]{3,2,1,0:T(8,128)(2,1)}, u32[]{:S(2)}, u32[]{:S(2)}) collective-permute-start(bf16[4,8,32,128]{3,2,1,0:T(8,128)(2,1)} %pad_maximum_fusion.2), channel_id=1, source_target_pairs={{0,4},{4,8},{8,12},{12,16},{16,20},{20,24},{24,28},{28,0},{1,5},{5... | collective-permute-start | bytes 786440 | tf_op jit(solution)/shard_map/ppermute | solution.py:156
  51.7 14.1 %collective-permute-start.3 = (bf16[4,8,32,128]{3,2,1,0:T(8,128)(2,1)}, bf16[4,8,32,128]{3,2,1,0:T(8,128)(2,1)}, u32[]{:S(2)}, u32[]{:S(2)}) collective-permute-start(bf16[4,8,32,128]{3,2,1,0:T(8,128)(2,1)} %pad_maximum_fusion.3), channel_id=1, source_target_pairs={{4,0},{8,4},{12,8},{16,12},{20,16},{24,20},{28,24},{0,28},{5,1},{9... | collective-permute-start | bytes 786440 | tf_op jit(solution)/shard_map/ppermute | solution.py:156
  65.8 1.9 copy-start.1
  67.7 1.0 copy-start.7
  68.7 1.0 copy-start.9
  69.8 3.6 %copy-start.3 = (bf16[8,8,32,128]{3,2,1,0:T(8,128)(2,1)S(1)}, bf16[8,8,32,128]{3,2,1,0:T(8,128)(2,1)}, u32[]{:S(2)}) copy-start(bf16[8,8,32,128]{3,2,1,0:T(8,128)(2,1)} %copy-done.2) | copy-start | bytes 1572868
  69.8 3.6 %copy-start.5 = (bf16[8,8,32,128]{3,2,1,0:T(8,128)(2,1)S(1)}, bf16[8,8,32,128]{3,2,1,0:T(8,128)(2,1)}, u32[]{:S(2)}) copy-start(bf16[8,8,32,128]{3,2,1,0:T(8,128)(2,1)} %copy-done.4) | copy-start | bytes 1572868
  121.4 17.6 %collective-permute-start.4 = (bf16[4,8,32,128]{3,2,1,0:T(8,128)(2,1)S(1)}, bf16[4,8,32,128]{3,2,1,0:T(8,128)(2,1)S(1)}, u32[]{:S(2)}, u32[]{:S(2)}) collective-permute-start(bf16[4,8,32,128]{3,2,1,0:T(8,128)(2,1)S(1)} %pad_maximum_fusion.4), channel_id=1, source_target_pairs={{0,4},{4,8},{8,12},{12,16},{16,20},{20,24},{24,28},{28,0},{1,5},{5... | collective-permute-start | bytes 786440 | tf_op jit(solution)/shard_map/ppermute | solution.py:156
  121.5 14.1 %collective-permute-start.6 = (bf16[4,8,32,128]{3,2,1,0:T(8,128)(2,1)S(1)}, bf16[4,8,32,128]{3,2,1,0:T(8,128)(2,1)S(1)}, u32[]{:S(2)}, u32[]{:S(2)}) collective-permute-start(bf16[4,8,32,128]{3,2,1,0:T(8,128)(2,1)S(1)} %pad_maximum_fusion.6), channel_id=1, source_target_pairs={{0,4},{4,8},{8,12},{12,16},{16,20},{20,24},{24,28},{28,0},{1,5},{5... | collective-permute-start | bytes 786440 | tf_op jit(solution)/shard_map/ppermute | solution.py:156
  121.6 14.0 %collective-permute-start.7 = (bf16[4,8,32,128]{3,2,1,0:T(8,128)(2,1)S(1)}, bf16[4,8,32,128]{3,2,1,0:T(8,128)(2,1)S(1)}, u32[]{:S(2)}, u32[]{:S(2)}) collective-permute-start(bf16[4,8,32,128]{3,2,1,0:T(8,128)(2,1)S(1)} %pad_maximum_fusion.7), channel_id=1, source_target_pairs={{4,0},{8,4},{12,8},{16,12},{20,16},{24,20},{28,24},{0,28},{5,1},{9... | collective-permute-start | bytes 786440 | tf_op jit(solution)/shard_map/ppermute | solution.py:156
  124.3 14.6 %collective-permute-start.5 = (bf16[4,8,32,128]{3,2,1,0:T(8,128)(2,1)S(1)}, bf16[4,8,32,128]{3,2,1,0:T(8,128)(2,1)S(1)}, u32[]{:S(2)}, u32[]{:S(2)}) collective-permute-start(bf16[4,8,32,128]{3,2,1,0:T(8,128)(2,1)S(1)} %pad_maximum_fusion.5), channel_id=1, source_target_pairs={{4,0},{8,4},{12,8},{16,12},{20,16},{24,20},{28,24},{0,28},{5,1},{9... | collective-permute-start | bytes 786440 | tf_op jit(solution)/shard_map/ppermute | solution.py:156
  185.3 17.6 %collective-permute-start.8 = (bf16[4,8,32,128]{3,2,1,0:T(8,128)(2,1)S(1)}, bf16[4,8,32,128]{3,2,1,0:T(8,128)(2,1)S(1)}, u32[]{:S(2)}, u32[]{:S(2)}) collective-permute-start(bf16[4,8,32,128]{3,2,1,0:T(8,128)(2,1)S(1)} %pad_maximum_fusion.8), channel_id=1, source_target_pairs={{0,4},{4,8},{8,12},{12,16},{16,20},{20,24},{24,28},{28,0},{1,5},{5... | collective-permute-start | bytes 786440 | tf_op jit(solution)/shard_map/ppermute | solution.py:156
  185.4 14.1 %collective-permute-start.10 = (bf16[4,8,32,128]{3,2,1,0:T(8,128)(2,1)S(1)}, bf16[4,8,32,128]{3,2,1,0:T(8,128)(2,1)S(1)}, u32[]{:S(2)}, u32[]{:S(2)}) collective-permute-start(bf16[4,8,32,128]{3,2,1,0:T(8,128)(2,1)S(1)} %pad_maximum_fusion.10), channel_id=1, source_target_pairs={{0,4},{4,8},{8,12},{12,16},{16,20},{20,24},{24,28},{28,0},{1,5},{5... | collective-permute-start | bytes 786440 | tf_op jit(solution)/shard_map/ppermute | solution.py:156
  185.7 13.9 %collective-permute-start.11 = (bf16[4,8,32,128]{3,2,1,0:T(8,128)(2,1)S(1)}, bf16[4,8,32,128]{3,2,1,0:T(8,128)(2,1)S(1)}, u32[]{:S(2)}, u32[]{:S(2)}) collective-permute-start(bf16[4,8,32,128]{3,2,1,0:T(8,128)(2,1)S(1)} %pad_maximum_fusion.11), channel_id=1, source_target_pairs={{4,0},{8,4},{12,8},{16,12},{20,16},{24,20},{28,24},{0,28},{5,1},{9... | collective-permute-start | bytes 786440 | tf_op jit(solution)/shard_map/ppermute | solution.py:156
  188.2 14.6 %collective-permute-start.9 = (bf16[4,8,32,128]{3,2,1,0:T(8,128)(2,1)S(1)}, bf16[4,8,32,128]{3,2,1,0:T(8,128)(2,1)S(1)}, u32[]{:S(2)}, u32[]{:S(2)}) collective-permute-start(bf16[4,8,32,128]{3,2,1,0:T(8,128)(2,1)S(1)} %pad_maximum_fusion.9), channel_id=1, source_target_pairs={{4,0},{8,4},{12,8},{16,12},{20,16},{24,20},{28,24},{0,28},{5,1},{9... | collective-permute-start | bytes 786440 | tf_op jit(solution)/shard_map/ppermute | solution.py:156
  249.8 17.6 %collective-permute-start.12 = (bf16[4,8,32,128]{3,2,1,0:T(8,128)(2,1)S(1)}, bf16[4,8,32,128]{3,2,1,0:T(8,128)(2,1)S(1)}, u32[]{:S(2)}, u32[]{:S(2)}) collective-permute-start(bf16[4,8,32,128]{3,2,1,0:T(8,128)(2,1)S(1)} %pad_maximum_fusion.12), channel_id=1, source_target_pairs={{0,4},{4,8},{8,12},{12,16},{16,20},{20,24},{24,28},{28,0},{1,5},{5... | collective-permute-start | bytes 786440 | tf_op jit(solution)/shard_map/ppermute | solution.py:156
  249.9 14.1 %collective-permute-start.14 = (bf16[4,8,32,128]{3,2,1,0:T(8,128)(2,1)S(1)}, bf16[4,8,32,128]{3,2,1,0:T(8,128)(2,1)S(1)}, u32[]{:S(2)}, u32[]{:S(2)}) collective-permute-start(bf16[4,8,32,128]{3,2,1,0:T(8,128)(2,1)S(1)} %pad_maximum_fusion.14), channel_id=1, source_target_pairs={{0,4},{4,8},{8,12},{12,16},{16,20},{20,24},{24,28},{28,0},{1,5},{5... | collective-permute-start | bytes 786440 | tf_op jit(solution)/shard_map/ppermute | solution.py:156
  250.0 14.0 %collective-permute-start.15 = (bf16[4,8,32,128]{3,2,1,0:T(8,128)(2,1)S(1)}, bf16[4,8,32,128]{3,2,1,0:T(8,128)(2,1)S(1)}, u32[]{:S(2)}, u32[]{:S(2)}) collective-permute-start(bf16[4,8,32,128]{3,2,1,0:T(8,128)(2,1)S(1)} %pad_maximum_fusion.15), channel_id=1, source_target_pairs={{4,0},{8,4},{12,8},{16,12},{20,16},{24,20},{28,24},{0,28},{5,1},{9... | collective-permute-start | bytes 786440 | tf_op jit(solution)/shard_map/ppermute | solution.py:156
  252.7 14.6 %collective-permute-start.13 = (bf16[4,8,32,128]{3,2,1,0:T(8,128)(2,1)S(1)}, bf16[4,8,32,128]{3,2,1,0:T(8,128)(2,1)S(1)}, u32[]{:S(2)}, u32[]{:S(2)}) collective-permute-start(bf16[4,8,32,128]{3,2,1,0:T(8,128)(2,1)S(1)} %pad_maximum_fusion.13), channel_id=1, source_target_pairs={{4,0},{8,4},{12,8},{16,12},{20,16},{24,20},{28,24},{0,28},{5,1},{9... | collective-permute-start | bytes 786440 | tf_op jit(solution)/shard_map/ppermute | solution.py:156

commit v3 on v1

v3 whole, which is shorter than its diff:
```python
import functools

import jax
import jax.numpy as jnp
from jax import lax
from jax.experimental import pallas as pl
from jax.experimental.pallas import tpu as pltpu
from jax.sharding import PartitionSpec as P

STEPS = 4
HALVES = 2
VMEM_LIMIT = 24 * 1024 * 1024
ANY = pl.BlockSpec(memory_space=pl.ANY)


def low_lanes(shape):
    return lax.broadcasted_iota(jnp.int32, shape, len(shape) - 1) < shape[-1] // 2


def swap_lanes(value):
    return pltpu.roll(value, value.shape[-1] // 2, len(value.shape) - 1)


def pack_kernel(start_ref, first_ref, second_ref):
    faces, width, lanes = start_ref.shape[1:]
    for face in range(faces):
        value = start_ref[0, face].astype(jnp.float32)
        top = value[: width // 2]
        bottom = swap_lanes(value[width // 2 :])
        low = low_lanes(top.shape)
        first_ref[0, face] = jnp.where(low, top, bottom).astype(jnp.bfloat16)
        second_ref[0, face] = jnp.where(low, bottom, top).astype(jnp.bfloat16)


def pack(start):
    columns, faces, width, lanes = start.shape
    half = jax.ShapeDtypeStruct((columns, faces, width // 2, lanes), jnp.bfloat16)
    spec = pl.BlockSpec((1, faces, width // 2, lanes), lambda i: (i, 0, 0, 0))
    return pl.pallas_call(
        pack_kernel,
        grid=(columns,),
        in_specs=[pl.BlockSpec((1, faces, width, lanes), lambda i: (i, 0, 0, 0))],
        out_specs=[spec, spec],
        out_shape=[half, half],
        name="pack",
    )(start)


def unpacked(first, second):
    first = first.astype(jnp.float32)
    second = second.astype(jnp.float32)
    low = low_lanes(first.shape)
    top = jnp.where(low, first, second).astype(jnp.bfloat16)
    bottom = swap_lanes(jnp.where(low, second, first)).astype(jnp.bfloat16)
    return top, bottom


def unpack_kernel(first_ref, second_ref, *refs):
    basis_ref = refs[-1]
    faces, rows = first_ref.shape[1:3]
    for face in range(faces):
        top, bottom = unpacked(first_ref[0, face], second_ref[0, face])
        basis_ref[0, 0, face, :rows] = top
        basis_ref[0, 0, face, rows:] = bottom


def unpack(index, first, second, basis):
    columns, faces, rows, lanes = first.shape
    spec = pl.BlockSpec((1, faces, rows, lanes), lambda i: (i, 0, 0, 0))
    return pl.pallas_call(
        unpack_kernel,
        grid=(columns,),
        in_specs=[spec, spec] + ([] if basis is None else [ANY]),
        out_specs=pl.BlockSpec(
            (1, 1, faces, 2 * rows, lanes), lambda i: (index, i, 0, 0, 0)
        ),
        out_shape=jax.ShapeDtypeStruct((STEPS, columns, faces, 2 * rows, lanes), jnp.bfloat16),
        input_output_aliases={} if basis is None else {2: 0},
        name="unpack",
    )(first, second, *([] if basis is None else [basis]))


def run_copies(copies):
    for copy in copies:
        copy.start()
    for copy in copies:
        copy.wait()


def edges_kernel(own, low_az, high_az, after, to_low, to_high, sems):
    columns = own.shape[0]
    copies = []
    for azim, source in enumerate((low_az, own, high_az)):
        copies.append((source.at[0], to_low.at[azim]))
        copies.append((source.at[columns - 1], to_high.at[azim]))
    run_copies(
        [
            pltpu.make_async_copy(source, target, sems.at[n])
            for n, (source, target) in enumerate(copies)
        ]
    )


def edges(own, low_az, high_az, after):
    shape = jax.ShapeDtypeStruct((3, *own.shape[1:]), own.dtype)
    return pl.pallas_call(
        edges_kernel,
        in_specs=[ANY] * 4,
        out_specs=[ANY] * 2,
        out_shape=[shape, shape],
        scratch_shapes=[pltpu.SemaphoreType.DMA((6,))],
        name="edges",
    )(own, low_az, high_az, after)


def part_kernel(half, chosen, step_index, use, *refs):
    refs = list(refs)
    take = lambda wanted=True: refs.pop(0) if wanted else None
    table, blocks, own, low_az, high_az = (take() for _ in range(5))
    low_st, high_st = take(use["stream"]), take(use["stream"])
    other = take(use["basis"])
    take(use["before"])
    take(use["basis_before"])
    following, basis = take(), take(use["basis"])
    window, blocks_buf, result_buf, sems = (take() for _ in range(4))
    basis_buf, other_buf = take(use["basis"]), take(use["basis"])

    faces, width, depth = blocks.shape[1:]
    columns = own.shape[0]
    span = columns + 2
    rows, lanes = window.shape[1:]
    count = iter(range(sems.shape[0]))
    copy_of = lambda source, target: pltpu.make_async_copy(source, target, sems.at[next(count)])

    view = window.reshape(3, span, faces, rows, lanes)
    entering = []
    for azim, source in enumerate((low_az, own, high_az)):
        entering.append(copy_of(source, view.at[azim, pl.ds(1, columns)]))
        if use["stream"]:
            entering.append(copy_of(low_st.at[azim], view.at[azim, 0]))
            entering.append(copy_of(high_st.at[azim], view.at[azim, span - 1]))
    for copy in entering:
        copy.start()
    loading = [copy_of(blocks.at[column], blocks_buf.at[n]) for n, column in enumerate(chosen)]
    for copy in loading:
        copy.start()
    if use["basis"]:
        others = [copy_of(other.at[column], other_buf.at[n]) for n, column in enumerate(chosen)]
        for copy in others:
            copy.start()
        for copy in others:
            copy.wait()
    for copy in entering:
        copy.wait()

    neighbours = table.shape[1]
    low = low_lanes((rows, lanes))
    leaving = []
    for n, column in enumerate(chosen):
        loading[n].wait()
        for face in range(faces):
            gathered = jnp.concatenate(
                [window[table[face, k] + column * faces] for k in range(neighbours)], axis=0
            )
            block = blocks_buf[n, face]
            stacked = jnp.concatenate([block[:, : depth // 2], block[:, depth // 2 :]], axis=0)
            product = jnp.dot(stacked, gathered, preferred_element_type=jnp.float32)
            top, bottom = product[:width], product[width:]
            if half == 0:
                here = jnp.where(low, top[:rows], bottom[rows:])
                there = jnp.where(low, top[rows:], bottom[:rows])
            else:
                here = jnp.where(low, bottom[rows:], top[:rows])
                there = jnp.where(low, bottom[:rows], top[rows:])
            result = (here + swap_lanes(there)).astype(jnp.bfloat16)
            result_buf[n, face] = result
            if use["basis"]:
                upper, lower = unpacked(other_buf[n, face], result)
                basis_buf[n, face, :rows] = upper
                basis_buf[n, face, rows:] = lower
        leaving.append(copy_of(result_buf.at[n], following.at[column]))
        leaving[-1].start()
        if use["basis"]:
            leaving.append(copy_of(basis_buf.at[n], basis.at[step_index, column]))
            leaving[-1].start()
    for copy in leaving:
        copy.wait()


def part(half, index, chosen, table, blocks, pieces, stream=None, before=None, other=None, basis=None):
    columns, faces, width, depth = blocks.shape
    rows, lanes = pieces[0].shape[2:]
    use = {
        "stream": stream is not None,
        "basis": other is not None,
        "before": before is not None,
        "basis_before": basis is not None,
    }
    args = [table, blocks, *pieces]
    if stream is not None:
        args += stream
    if other is not None:
        args.append(other)
    aliases = {}
    if before is not None:
        aliases[len(args)] = 0
        args.append(before)
    if basis is not None:
        aliases[len(args)] = 1
        args.append(basis)
    out_shape = [jax.ShapeDtypeStruct((columns, faces, rows, lanes), jnp.bfloat16)]
    if other is not None:
        out_shape.append(jax.ShapeDtypeStruct((STEPS, columns, faces, width, lanes), jnp.bfloat16))
    size = len(chosen)
    scratch = [
        pltpu.VMEM((3 * (columns + 2) * faces, rows, lanes), jnp.bfloat16),
        pltpu.VMEM((size, faces, width, depth), jnp.bfloat16),
        pltpu.VMEM((size, faces, rows, lanes), jnp.bfloat16),
        pltpu.SemaphoreType.DMA((9 + 4 * size,)),
    ]
    if other is not None:
        scratch.append(pltpu.VMEM((size, faces, width, lanes), jnp.bfloat16))
        scratch.append(pltpu.VMEM((size, faces, rows, lanes), jnp.bfloat16))
    flops = 2 * size * faces * width * depth * lanes
    name = "edge" if stream is not None else "inner"
    return pl.pallas_call(
        functools.partial(part_kernel, half, chosen, index, use),
        in_specs=[pl.BlockSpec(memory_space=pltpu.SMEM)] + [ANY] * (len(args) - 1),
        out_specs=[ANY] * len(out_shape),
        out_shape=out_shape,
        input_output_aliases=aliases,
        scratch_shapes=scratch,
        cost_estimate=pl.CostEstimate(
            flops=flops, bytes_accessed=2 * size * faces * width * depth, transcendentals=0
        ),
        compiler_params=pltpu.CompilerParams(vmem_limit_bytes=VMEM_LIMIT),
        name=f"{name}_half{half}",
    )(*args)


def shift(value, axis, up):
    count = lax.axis_size(axis)
    pairs = [(i, (i + 1) % count) for i in range(count)]
    if not up:
        pairs = [(target, source) for source, target in pairs]
    return lax.ppermute(value, axis, pairs)


def halves_of_rows(blocks):
    columns, faces, width, depth = blocks.shape
    row = lax.broadcasted_iota(jnp.int32, (depth, depth), 0)
    column = lax.broadcasted_iota(jnp.int32, (depth, depth), 1)
    part_rows = width // 2
    place = (row // width) * part_rows + row % part_rows + ((row // part_rows) % 2) * (depth // 2)
    mover = (place == column).astype(jnp.bfloat16)
    moved = jnp.dot(blocks.reshape(-1, depth), mover, preferred_element_type=jnp.float32)
    return moved.astype(jnp.bfloat16).reshape(blocks.shape)


def local(start_vector, trace_blocks, neighbour):
    columns, around, faces, width, lanes = start_vector.shape
    start = start_vector.reshape(columns, faces, width, lanes)
    blocks = halves_of_rows(trace_blocks.reshape(columns, faces, width, -1))
    codes = neighbour.reshape(faces, -1)
    table = (((codes // faces) % 3) * (columns + 2) + codes // (3 * faces)) * faces + codes % faces
    inner = tuple(range(1, columns - 1))
    outer = (0, columns - 1)
    current = list(pack(start))
    basis = None
    latest = current[0]
    for index in range(STEPS):
        around_z = [
            (shift(current[h], "azim", True), shift(current[h], "azim", False))
            for h in range(HALVES)
        ]
        for h in range(HALVES):
            low_az, high_az = around_z[h]
            pieces = (current[h], low_az, high_az)
            to_low, to_high = edges(*pieces, latest)
            stream = [shift(to_high, "stream", True), shift(to_low, "stream", False)]
            last = index == STEPS - 1 and h == HALVES - 1
            other = current[0] if last else None
            outs = part(h, index, inner, table, blocks, pieces, other=other, basis=basis if last else None)
            outs = part(
                h, index, outer, table, blocks, pieces, stream=stream, before=outs[0],
                other=other, basis=outs[1] if last else None,
            )
            current[h] = latest = outs[0]
            if last:
                basis = outs[1]
        if index < STEPS - 1:
            basis = unpack(index, *current, basis)
    return basis.reshape(STEPS, columns, around, faces, width, lanes)


def solution(mesh):
    return jax.shard_map(
        local,
        mesh=mesh,
        in_specs=(
            P("stream", "azim", None, None, None),
            P("stream", "azim", None, None, None),
            P("azim", None, None),
        ),
        out_specs=P(None, "stream", "azim", None, None, None),
        check_vma=False,
    )
```

time: 174 us -> 258 us (1.48)
  Pallas kernels: 33.8 us -> 171 us
  waiting for transfers between devices: 73.2 us -> 0.08 us
  local copies, waits for them, and re-layouts: 11 us -> 25.7 us
  starting transfers between devices: 48 us -> 53.6 us
    pallas_call x8 -> x27, Pallas kernels: 30.4 us -> 168 us  [the longest x8 105 us: edges(): pl.pallas_call(edges_kernel, in_specs=[ANY] * 4, out_specs=[ANY] * 2, out...]
    ppermute x32, waiting for transfers between devices: 73.2 us -> 0.08 us  [shift(): return lax.ppermute(value, axis, pairs)]
    unnamed x14 -> x40, local copies, waits for them, and re-layouts: 1.92 us -> 21 us
    ppermute x32, starting transfers between devices: 48 us -> 53.6 us  [shift(): return lax.ppermute(value, axis, pairs)]
    slice x24 -> x0, local copies, waits for them, and re-layouts: 4.41 us -> none  [local(): high_st = shift(jnp.stack([part[0] for part in trio]), 'stream', False)]
  transfers between devices with their start and end apart: 32 -> 32, of which waited for: 12 -> 0; matrix products, arithmetic and copies ran while one was open for 9% -> 4% of each run, Pallas kernels for 7% -> 59%
where the time goes in v3:
time: 258 us; the launch traced here: 257 us
  Pallas kernels  171 us (66%)
  starting transfers between devices  53.6 us (21%)
  local copies, waits for them, and re-layouts  25.7 us (10%)
  matrix products  5.29 us (2%)
    pallas_call x8, Pallas kernels, edges(): pl.pallas_call(edges_kernel, in_specs=[ANY] * 4, out_specs=[ANY] * 2, out...  105 us
    ppermute x32, starting transfers between devices, shift(): return lax.ppermute(value, axis, pairs)  53.6 us
    pallas_call x16, Pallas kernels, part(): pl.pallas_call(functools.partial(part_kernel, half, chosen, index, use),...  53.6 us
    unnamed x40, local copies, waits for them, and re-layouts  21 us
    pallas_call x3, Pallas kernels, unpack(): pl.pallas_call(unpack_kernel, grid=(columns,), in_specs=[spec, spec] + ([...  9.8 us
    dot_general x1, matrix products, halves_of_rows(): jnp.dot(blocks.reshape(-1, depth), mover, preferred_element_type=jnp.floa...  5.29 us
  transfers between devices with their start and end apart: 32, of which 0 were waited for; matrix products, arithmetic and copies ran while one was open for 4% of the time, Pallas kernels for 59%

profile of v3, /device:TPU:0, one launch (start us, length us, event | category | flops | bytes accessed | tf_op | source)
XLA Modules:
  0.0 256.8 jit_solution(13768334326803474547)
XLA Ops:
  0.0 3.5 %pack.1 = (bf16[4,8,32,128]{3,2,1,0:T(8,128)(2,1)}, bf16[4,8,32,128]{3,2,1,0:T(8,128)(2,1)}) custom-call(bf16[4,8,64,128]{3,2,1,0:T(8,128)(2,1)} %bitcast.50), custom_call_target="tpu_custom_call" | custom-call | tf_op jit(solution)/shard_map/pack/pallas_call | solution.py:39
  3.5 3.0 %collective-permute-start.2 = (bf16[4,8,32,128]{3,2,1,0:T(8,128)(2,1)}, bf16[4,8,32,128]{3,2,1,0:T(8,128)(2,1)}, u32[]{:S(2)}, u32[]{:S(2)}) collective-permute-start(bf16[4,8,32,128]{3,2,1,0:T(8,128)(2,1)} %get-tuple-element.27.own.after.refs_2_), channel_id=1, source_target_pairs={{0,1},{1,2},{2,3},{3,0},{4,5},{5,6},{6,7},{7,4},{8,9},{9,10},{10,1... | collective-permute-start | bytes 786440 | tf_op jit(solution)/shard_map/ppermute | solution.py:246
  6.5 2.0 collective-permute-start.3
  8.5 3.8 %collective-permute-start.1 = (bf16[4,8,32,128]{3,2,1,0:T(8,128)(2,1)}, bf16[4,8,32,128]{3,2,1,0:T(8,128)(2,1)}, u32[]{:S(2)}, u32[]{:S(2)}) collective-permute-start(bf16[4,8,32,128]{3,2,1,0:T(8,128)(2,1)} %get-tuple-element.26.own.refs_2_), channel_id=1, source_target_pairs={{1,0},{2,1},{3,2},{0,3},{5,4},{6,5},{7,6},{4,7},{9,8},{10,9},{11,1... | collective-permute-start | bytes 786440 | tf_op jit(solution)/shard_map/ppermute | solution.py:246
  12.4 5.3 %fusion = bf16[2048,768]{0,1:T(8,128)(2,1)} fusion(bf16[2048,768]{1,0:T(8,128)(2,1)S(1)} %bitcast.33, s32[768]{0:T(1024)S(1)} %get-tuple-element.47, s32[768]{0:T(1024)S(1)} %get-tuple-element.53, s32[768]{0:T(1024)S(1)} %get-tuple-element.48, s32[768]{0:T(1024)S(1)} %get-tuple-element.50, s32[768]{0:T(1024)S(1)} %get-tuple-element.49, ...), kind=kOutput, calls=%fused_computation.6 | convolution fusion | flops 2429288448 | bytes 6312192 | tf_op jit(solution)/shard_map/dot_general | solution.py:256
  17.7 4.7 %copy.16 = bf16[2048,768]{1,0:T(8,128)(2,1)} copy(bf16[2048,768]{0,1:T(8,128)(2,1)} %fusion) | data formatting | bytes 6291456 | tf_op jit(solution)/shard_map/convert_element_type | solution.py:257
  22.4 13.1 %edges.8 = (bf16[3,8,32,128]{3,2,1,0:T(8,128)(2,1)}, bf16[3,8,32,128]{3,2,1,0:T(8,128)(2,1)}) custom-call(bf16[4,8,32,128]{3,2,1,0:T(8,128)(2,1)} %get-tuple-element.27.own.after.refs_2_, bf16[4,8,32,128]{3,2,1,0:T(8,128)(2,1)} %collective-permute-done.2.low_az.refs_3_, bf16[4,8,32,128]{3,2,1,0:T(8,128)(2,1)} %collective-permute-done.3.high_az.refs_4_, ...), custom_call_target="tpu_custom_call" | custom-call | tf_op jit(solution)/shard_map/edges/pallas_call | solution.py:106
  35.5 2.6 %collective-permute-start.5 = (bf16[3,8,32,128]{3,2,1,0:T(8,128)(2,1)}, bf16[3,8,32,128]{3,2,1,0:T(8,128)(2,1)S(1)}, u32[]{:S(2)}, u32[]{:S(2)}) collective-permute-start(bf16[3,8,32,128]{3,2,1,0:T(8,128)(2,1)} %get-tuple-element.29), channel_id=1, source_target_pairs={{4,0},{8,4},{12,8},{16,12},{20,16},{24,20},{28,24},{0,28},{5,1},{9... | collective-permute-start | bytes 589832 | tf_op jit(solution)/shard_map/ppermute | solution.py:246
  38.2 1.9 copy-done.1
  40.1 3.3 %inner_half0.4.refs_7_ = bf16[4,8,32,128]{3,2,1,0:T(8,128)(2,1)} custom-call(s32[8,12]{1,0:T(8,128)S(1)} %fusion.30.refs_0_, bf16[4,8,64,768]{3,2,1,0:T(8,128)(2,1)S(1)} %bitcast.34, bf16[4,8,32,128]{3,2,1,0:T(8,128)(2,1)S(1)} %copy-done.13, bf16[4,8,32,128]{3,2,1,0:T(8,128)(2,1)} %collective-permute-done.2.low_az.refs_3_, ...), custom_call_target="tpu_custom_call" | custom-call | flops 201326592 | bytes 1572864 | tf_op jit(solution)/shard_map/inner_half0/pallas_call | solution.py:226
  43.4 3.6 %edge_half0.4.after.own.refs_2_.first_ref = bf16[4,8,32,128]{3,2,1,0:T(8,128)(2,1)} custom-call(s32[8,12]{1,0:T(8,128)S(1)} %fusion.30.refs_0_, bf16[4,8,64,768]{3,2,1,0:T(8,128)(2,1)S(1)} %bitcast.35, bf16[4,8,32,128]{3,2,1,0:T(8,128)(2,1)S(1)} %copy-done.13, ...), custom_call_target="tpu_custom_call", output_to_operand_aliasing={{}: (7, {})} | custom-call | flops 201326592 | bytes 1572864 | tf_op jit(solution)/shard_map/edge_half0/pallas_call | solution.py:226
  47.1 3.8 %collective-permute-start.11 = (bf16[4,8,32,128]{3,2,1,0:T(8,128)(2,1)}, bf16[4,8,32,128]{3,2,1,0:T(8,128)(2,1)}, u32[]{:S(2)}, u32[]{:S(2)}) collective-permute-start(bf16[4,8,32,128]{3,2,1,0:T(8,128)(2,1)} %edge_half0.4.after.own.refs_2_.first_ref), channel_id=1, source_target_pairs={{1,0},{2,1},{3,2},{0,3},{5,4},{6,5},{7,6},{4,7},{9,8},{10,9},{11,1... | collective-permute-start | bytes 786440 | tf_op jit(solution)/shard_map/ppermute | solution.py:246
  50.9 13.1 %edges.9 = (bf16[3,8,32,128]{3,2,1,0:T(8,128)(2,1)}, bf16[3,8,32,128]{3,2,1,0:T(8,128)(2,1)}) custom-call(bf16[4,8,32,128]{3,2,1,0:T(8,128)(2,1)} %get-tuple-element.26.own.refs_2_, bf16[4,8,32,128]{3,2,1,0:T(8,128)(2,1)} %collective-permute-done.low_az.refs_3_, bf16[4,8,32,128]{3,2,1,0:T(8,128)(2,1)} %collective-permute-done.1.high_az.refs_4_, ...), custom_call_target="tpu_custom_call" | custom-call | tf_op jit(solution)/shard_map/edges/pallas_call | solution.py:106
  64.0 2.6 %collective-permute-start.7 = (bf16[3,8,32,128]{3,2,1,0:T(8,128)(2,1)}, bf16[3,8,32,128]{3,2,1,0:T(8,128)(2,1)S(1)}, u32[]{:S(2)}, u32[]{:S(2)}) collective-permute-start(bf16[3,8,32,128]{3,2,1,0:T(8,128)(2,1)} %get-tuple-element.31), channel_id=1, source_target_pairs={{4,0},{8,4},{12,8},{16,12},{20,16},{24,20},{28,24},{0,28},{5,1},{9... | collective-permute-start | bytes 589832 | tf_op jit(solution)/shard_map/ppermute | solution.py:246
  66.7 1.9 copy-done.2
  68.6 0.9 copy-done.14
  69.5 3.3 %inner_half1.4.refs_7_ = bf16[4,8,32,128]{3,2,1,0:T(8,128)(2,1)} custom-call(s32[8,12]{1,0:T(8,128)S(1)} %fusion.30.refs_0_, bf16[4,8,64,768]{3,2,1,0:T(8,128)(2,1)S(1)} %bitcast.36, bf16[4,8,32,128]{3,2,1,0:T(8,128)(2,1)S(1)} %copy-done.14, bf16[4,8,32,128]{3,2,1,0:T(8,128)(2,1)} %collective-permute-done.low_az.refs_3_, ...), custom_call_target="tpu_custom_call" | custom-call | flops 201326592 | bytes 1572864 | tf_op jit(solution)/shard_map/inner_half1/pallas_call | solution.py:226
  72.8 3.6 %edge_half1.4.after.own.refs_2_.second_ref = bf16[4,8,32,128]{3,2,1,0:T(8,128)(2,1)} custom-call(s32[8,12]{1,0:T(8,128)S(1)} %fusion.30.refs_0_, bf16[4,8,64,768]{3,2,1,0:T(8,128)(2,1)S(1)} %bitcast.37, bf16[4,8,32,128]{3,2,1,0:T(8,128)(2,1)S(1)} %copy-done.14, ...), custom_call_target="tpu_custom_call", output_to_operand_aliasing={{}: (7, {})} | custom-call | flops 201326592 | bytes 1572864 | tf_op jit(solution)/shard_map/edge_half1/pallas_call | solution.py:226
  76.5 3.8 %collective-permute-start.9 = (bf16[4,8,32,128]{3,2,1,0:T(8,128)(2,1)}, bf16[4,8,32,128]{3,2,1,0:T(8,128)(2,1)}, u32[]{:S(2)}, u32[]{:S(2)}) collective-permute-start(bf16[4,8,32,128]{3,2,1,0:T(8,128)(2,1)} %edge_half1.4.after.own.refs_2_.second_ref), channel_id=1, source_target_pairs={{1,0},{2,1},{3,2},{0,3},{5,4},{6,5},{7,6},{4,7},{9,8},{10,9},{11,1... | collective-permute-start | bytes 786440 | tf_op jit(solution)/shard_map/ppermute | solution.py:246
  80.3 0.7 copy-done.15
  81.0 13.1 %edges.10 = (bf16[3,8,32,128]{3,2,1,0:T(8,128)(2,1)}, bf16[3,8,32,128]{3,2,1,0:T(8,128)(2,1)}) custom-call(bf16[4,8,32,128]{3,2,1,0:T(8,128)(2,1)} %edge_half0.4.after.own.refs_2_.first_ref, bf16[4,8,32,128]{3,2,1,0:T(8,128)(2,1)} %copy-done.15, bf16[4,8,32,128]{3,2,1,0:T(8,128)(2,1)} %collective-permute-done.11.high_az.refs_4_, ...), custom_call_target="tpu_custom_call" | custom-call | tf_op jit(solution)/shard_map/edges/pallas_call | solution.py:106
  94.1 2.6 %collective-permute-start.13 = (bf16[3,8,32,128]{3,2,1,0:T(8,128)(2,1)}, bf16[3,8,32,128]{3,2,1,0:T(8,128)(2,1)S(1)}, u32[]{:S(2)}, u32[]{:S(2)}) collective-permute-start(bf16[3,8,32,128]{3,2,1,0:T(8,128)(2,1)} %get-tuple-element.33), channel_id=1, source_target_pairs={{4,0},{8,4},{12,8},{16,12},{20,16},{24,20},{28,24},{0,28},{5,1},{9... | collective-permute-start | bytes 589832 | tf_op jit(solution)/shard_map/ppermute | solution.py:246
  96.8 1.9 copy-done.3
  98.6 0.9 copy-done.16
  99.6 3.3 %inner_half0.5.refs_7_ = bf16[4,8,32,128]{3,2,1,0:T(8,128)(2,1)} custom-call(s32[8,12]{1,0:T(8,128)S(1)} %fusion.30.refs_0_, bf16[4,8,64,768]{3,2,1,0:T(8,128)(2,1)S(1)} %bitcast.38, bf16[4,8,32,128]{3,2,1,0:T(8,128)(2,1)} %edge_half0.4.after.own.refs_2_.first_ref, bf16[4,8,32,128]{3,2,1,0:T(8,128)(2,1)S(1)} %copy-done.16, ...), custom_call_target="tpu_custom_call" | custom-call | flops 201326592 | bytes 1572864 | tf_op jit(solution)/shard_map/inner_half0/pallas_call | solution.py:226
  102.9 3.6 %edge_half0.5.after.own.refs_2_.first_ref = bf16[4,8,32,128]{3,2,1,0:T(8,128)(2,1)} custom-call(s32[8,12]{1,0:T(8,128)S(1)} %fusion.30.refs_0_, bf16[4,8,64,768]{3,2,1,0:T(8,128)(2,1)S(1)} %bitcast.39, bf16[4,8,32,128]{3,2,1,0:T(8,128)(2,1)} %edge_half0.4.after.own.refs_2_.first_ref, ...), custom_call_target="tpu_custom_call", output_to_operand_aliasing={{}: (7, {})} | custom-call | flops 201326592 | bytes 1572864 | tf_op jit(solution)/shard_map/edge_half0/pallas_call | solution.py:226
  106.6 3.8 %collective-permute-start.19 = (bf16[4,8,32,128]{3,2,1,0:T(8,128)(2,1)}, bf16[4,8,32,128]{3,2,1,0:T(8,128)(2,1)}, u32[]{:S(2)}, u32[]{:S(2)}) collective-permute-start(bf16[4,8,32,128]{3,2,1,0:T(8,128)(2,1)} %edge_half0.5.after.own.refs_2_.first_ref), channel_id=1, source_target_pairs={{1,0},{2,1},{3,2},{0,3},{5,4},{6,5},{7,6},{4,7},{9,8},{10,9},{11,1... | collective-permute-start | bytes 786440 | tf_op jit(solution)/shard_map/ppermute | solution.py:246
  110.4 13.1 %edges.11 = (bf16[3,8,32,128]{3,2,1,0:T(8,128)(2,1)}, bf16[3,8,32,128]{3,2,1,0:T(8,128)(2,1)}) custom-call(bf16[4,8,32,128]{3,2,1,0:T(8,128)(2,1)} %edge_half1.4.after.own.refs_2_.second_ref, bf16[4,8,32,128]{3,2,1,0:T(8,128)(2,1)} %collective-permute-done.8.low_az.refs_3_, bf16[4,8,32,128]{3,2,1,0:T(8,128)(2,1)} %collective-permute-done.9.high_az.refs_4_, ...), custom_call_target="tpu_custom_call" | custom-call | tf_op jit(solution)/shard_map/edges/pallas_call | solution.py:106
  123.5 2.6 %collective-permute-start.15 = (bf16[3,8,32,128]{3,2,1,0:T(8,128)(2,1)}, bf16[3,8,32,128]{3,2,1,0:T(8,128)(2,1)S(1)}, u32[]{:S(2)}, u32[]{:S(2)}) collective-permute-start(bf16[3,8,32,128]{3,2,1,0:T(8,128)(2,1)} %get-tuple-element.35), channel_id=1, source_target_pairs={{4,0},{8,4},{12,8},{16,12},{20,16},{24,20},{28,24},{0,28},{5,1},{9... | collective-permute-start | bytes 589832 | tf_op jit(solution)/shard_map/ppermute | solution.py:246
  126.2 1.9 copy-done.4
  128.1 3.4 %inner_half1.5.refs_7_ = bf16[4,8,32,128]{3,2,1,0:T(8,128)(2,1)} custom-call(s32[8,12]{1,0:T(8,128)S(1)} %fusion.30.refs_0_, bf16[4,8,64,768]{3,2,1,0:T(8,128)(2,1)S(1)} %bitcast.40, bf16[4,8,32,128]{3,2,1,0:T(8,128)(2,1)} %edge_half1.4.after.own.refs_2_.second_ref, bf16[4,8,32,128]{3,2,1,0:T(8,128)(2,1)} %collective-permute-done.8.low_az.refs_3_, ...), custom_call_target="tpu_custom_call" | custom-call | flops 201326592 | bytes 1572864 | tf_op jit(solution)/shard_map/inner_half1/pallas_call | solution.py:226
  131.4 3.6 %edge_half1.5.after.own.refs_2_.second_ref = bf16[4,8,32,128]{3,2,1,0:T(8,128)(2,1)} custom-call(s32[8,12]{1,0:T(8,128)S(1)} %fusion.30.refs_0_, bf16[4,8,64,768]{3,2,1,0:T(8,128)(2,1)S(1)} %bitcast.41, bf16[4,8,32,128]{3,2,1,0:T(8,128)(2,1)} %edge_half1.4.after.own.refs_2_.second_ref, ...), custom_call_target="tpu_custom_call", output_to_operand_aliasing={{}: (7, {})} | custom-call | flops 201326592 | bytes 1572864 | tf_op jit(solution)/shard_map/edge_half1/pallas_call | solution.py:226
  135.0 0.1 collective-permute-start.16
  135.1 3.8 %collective-permute-start.17 = (bf16[4,8,32,128]{3,2,1,0:T(8,128)(2,1)}, bf16[4,8,32,128]{3,2,1,0:T(8,128)(2,1)}, u32[]{:S(2)}, u32[]{:S(2)}) collective-permute-start(bf16[4,8,32,128]{3,2,1,0:T(8,128)(2,1)} %edge_half1.5.after.own.refs_2_.second_ref), channel_id=1, source_target_pairs={{1,0},{2,1},{3,2},{0,3},{5,4},{6,5},{7,6},{4,7},{9,8},{10,9},{11,1... | collective-permute-start | bytes 786440 | tf_op jit(solution)/shard_map/ppermute | solution.py:246
  138.9 0.7 copy-done.17
  139.6 13.1 %edges.12 = (bf16[3,8,32,128]{3,2,1,0:T(8,128)(2,1)}, bf16[3,8,32,128]{3,2,1,0:T(8,128)(2,1)}) custom-call(bf16[4,8,32,128]{3,2,1,0:T(8,128)(2,1)} %edge_half0.5.after.own.refs_2_.first_ref, bf16[4,8,32,128]{3,2,1,0:T(8,128)(2,1)} %copy-done.17, bf16[4,8,32,128]{3,2,1,0:T(8,128)(2,1)} %collective-permute-done.19.high_az.refs_4_, ...), custom_call_target="tpu_custom_call" | custom-call | tf_op jit(solution)/shard_map/edges/pallas_call | solution.py:106
  152.8 2.6 %collective-permute-start.21 = (bf16[3,8,32,128]{3,2,1,0:T(8,128)(2,1)}, bf16[3,8,32,128]{3,2,1,0:T(8,128)(2,1)S(1)}, u32[]{:S(2)}, u32[]{:S(2)}) collective-permute-start(bf16[3,8,32,128]{3,2,1,0:T(8,128)(2,1)} %get-tuple-element.37), channel_id=1, source_target_pairs={{4,0},{8,4},{12,8},{16,12},{20,16},{24,20},{28,24},{0,28},{5,1},{9... | collective-permute-start | bytes 589832 | tf_op jit(solution)/shard_map/ppermute | solution.py:246
  155.4 1.9 copy-done.5
  157.3 0.9 copy-done.18
  158.2 3.3 %inner_half0.6.refs_7_ = bf16[4,8,32,128]{3,2,1,0:T(8,128)(2,1)} custom-call(s32[8,12]{1,0:T(8,128)S(1)} %fusion.30.refs_0_, bf16[4,8,64,768]{3,2,1,0:T(8,128)(2,1)S(1)} %bitcast.42, bf16[4,8,32,128]{3,2,1,0:T(8,128)(2,1)} %edge_half0.5.after.own.refs_2_.first_ref, bf16[4,8,32,128]{3,2,1,0:T(8,128)(2,1)S(1)} %copy-done.18, ...), custom_call_target="tpu_custom_call" | custom-call | flops 201326592 | bytes 1572864 | tf_op jit(solution)/shard_map/inner_half0/pallas_call | solution.py:226
  161.6 3.6 %edge_half0.6.after.own.refs_2_.first_ref = bf16[4,8,32,128]{3,2,1,0:T(8,128)(2,1)} custom-call(s32[8,12]{1,0:T(8,128)S(1)} %fusion.30.refs_0_, bf16[4,8,64,768]{3,2,1,0:T(8,128)(2,1)S(1)} %bitcast.43, bf16[4,8,32,128]{3,2,1,0:T(8,128)(2,1)} %edge_half0.5.after.own.refs_2_.first_ref, ...), custom_call_target="tpu_custom_call", output_to_operand_aliasing={{}: (7, {})} | custom-call | flops 201326592 | bytes 1572864 | tf_op jit(solution)/shard_map/edge_half0/pallas_call | solution.py:226
  165.1 0.1 collective-permute-start.26
  165.2 3.8 %collective-permute-start.27 = (bf16[4,8,32,128]{3,2,1,0:T(8,128)(2,1)}, bf16[4,8,32,128]{3,2,1,0:T(8,128)(2,1)}, u32[]{:S(2)}, u32[]{:S(2)}) collective-permute-start(bf16[4,8,32,128]{3,2,1,0:T(8,128)(2,1)} %edge_half0.6.after.own.refs_2_.first_ref), channel_id=1, source_target_pairs={{1,0},{2,1},{3,2},{0,3},{5,4},{6,5},{7,6},{4,7},{9,8},{10,9},{11,1... | collective-permute-start | bytes 786440 | tf_op jit(solution)/shard_map/ppermute | solution.py:246
  169.0 13.1 %edges.13 = (bf16[3,8,32,128]{3,2,1,0:T(8,128)(2,1)}, bf16[3,8,32,128]{3,2,1,0:T(8,128)(2,1)}) custom-call(bf16[4,8,32,128]{3,2,1,0:T(8,128)(2,1)} %edge_half1.5.after.own.refs_2_.second_ref, bf16[4,8,32,128]{3,2,1,0:T(8,128)(2,1)} %collective-permute-done.16.low_az.refs_3_, bf16[4,8,32,128]{3,2,1,0:T(8,128)(2,1)} %collective-permute-done.17.high_az.refs_4_, ...), custom_call_target="tpu_custom_call" | custom-call | tf_op jit(solution)/shard_map/edges/pallas_call | solution.py:106
  182.2 2.6 %collective-permute-start.23 = (bf16[3,8,32,128]{3,2,1,0:T(8,128)(2,1)}, bf16[3,8,32,128]{3,2,1,0:T(8,128)(2,1)S(1)}, u32[]{:S(2)}, u32[]{:S(2)}) collective-permute-start(bf16[3,8,32,128]{3,2,1,0:T(8,128)(2,1)} %get-tuple-element.39), channel_id=1, source_target_pairs={{4,0},{8,4},{12,8},{16,12},{20,16},{24,20},{28,24},{0,28},{5,1},{9... | collective-permute-start | bytes 589832 | tf_op jit(solution)/shard_map/ppermute | solution.py:246
  184.8 1.9 copy-done.6
  186.7 2.9 %inner_half1.6.refs_7_ = bf16[4,8,32,128]{3,2,1,0:T(8,128)(2,1)S(1)} custom-call(s32[8,12]{1,0:T(8,128)S(1)} %fusion.30.refs_0_, bf16[4,8,64,768]{3,2,1,0:T(8,128)(2,1)S(1)} %bitcast.44, bf16[4,8,32,128]{3,2,1,0:T(8,128)(2,1)} %edge_half1.5.after.own.refs_2_.second_ref, bf16[4,8,32,128]{3,2,1,0:T(8,128)(2,1)} %collective-permute-done.16.low_az.refs_3_, ...), custom_call_target="tpu_custom_call" | custom-call | flops 201326592 | bytes 1572864 | tf_op jit(solution)/shard_map/inner_half1/pallas_call | solution.py:226
  189.6 3.1 %edge_half1.6.after.own.second_ref.refs_2_ = bf16[4,8,32,128]{3,2,1,0:T(8,128)(2,1)S(1)} custom-call(s32[8,12]{1,0:T(8,128)S(1)} %fusion.30.refs_0_, bf16[4,8,64,768]{3,2,1,0:T(8,128)(2,1)S(1)} %bitcast.45, bf16[4,8,32,128]{3,2,1,0:T(8,128)(2,1)} %edge_half1.5.after.own.refs_2_.second_ref, ...), custom_call_target="tpu_custom_call", output_to_operand_aliasing={{}: (7, {})} | custom-call | flops 201326592 | bytes 1572864 | tf_op jit(solution)/shard_map/edge_half1/pallas_call | solution.py:226
  192.7 3.8 %collective-permute-start.25 = (bf16[4,8,32,128]{3,2,1,0:T(8,128)(2,1)S(1)}, bf16[4,8,32,128]{3,2,1,0:T(8,128)(2,1)}, u32[]{:S(2)}, u32[]{:S(2)}) collective-permute-start(bf16[4,8,32,128]{3,2,1,0:T(8,128)(2,1)S(1)} %edge_half1.6.after.own.second_ref.refs_2_), channel_id=1, source_target_pairs={{1,0},{2,1},{3,2},{0,3},{5,4},{6,5},{7,6},{4,7},{9,8},{10,9},{11,1... | collective-permute-start | bytes 786440 | tf_op jit(solution)/shard_map/ppermute | solution.py:246
  196.6 13.1 %edges.14 = (bf16[3,8,32,128]{3,2,1,0:T(8,128)(2,1)}, bf16[3,8,32,128]{3,2,1,0:T(8,128)(2,1)}) custom-call(bf16[4,8,32,128]{3,2,1,0:T(8,128)(2,1)} %edge_half0.6.after.own.refs_2_.first_ref, bf16[4,8,32,128]{3,2,1,0:T(8,128)(2,1)} %collective-permute-done.26.low_az.refs_3_, bf16[4,8,32,128]{3,2,1,0:T(8,128)(2,1)} %collective-permute-done.27.high_az.refs_4_, ...), custom_call_target="tpu_custom_call" | custom-call | tf_op jit(solution)/shard_map/edges/pallas_call | solution.py:106
  209.7 2.6 %collective-permute-start.29 = (bf16[3,8,32,128]{3,2,1,0:T(8,128)(2,1)}, bf16[3,8,32,128]{3,2,1,0:T(8,128)(2,1)S(1)}, u32[]{:S(2)}, u32[]{:S(2)}) collective-permute-start(bf16[3,8,32,128]{3,2,1,0:T(8,128)(2,1)} %get-tuple-element.41), channel_id=1, source_target_pairs={{4,0},{8,4},{12,8},{16,12},{20,16},{24,20},{28,24},{0,28},{5,1},{9... | collective-permute-start | bytes 589832 | tf_op jit(solution)/shard_map/ppermute | solution.py:246
  212.3 1.9 copy-done.7
  214.2 2.9 %inner_half0.7.refs_7_ = bf16[4,8,32,128]{3,2,1,0:T(8,128)(2,1)S(1)} custom-call(s32[8,12]{1,0:T(8,128)S(1)} %fusion.30.refs_0_, bf16[4,8,64,768]{3,2,1,0:T(8,128)(2,1)S(1)} %bitcast.46, bf16[4,8,32,128]{3,2,1,0:T(8,128)(2,1)} %edge_half0.6.after.own.refs_2_.first_ref, bf16[4,8,32,128]{3,2,1,0:T(8,128)(2,1)} %collective-permute-done.26.low_az.refs_3_, ...), custom_call_target="tpu_custom_call" | custom-call | flops 201326592 | bytes 1572864 | tf_op jit(solution)/shard_map/inner_half0/pallas_call | solution.py:226
  217.1 3.1 %edge_half0.7.after.refs_5_.refs_7_ = bf16[4,8,32,128]{3,2,1,0:T(8,128)(2,1)S(1)} custom-call(s32[8,12]{1,0:T(8,128)S(1)} %fusion.30.refs_0_, bf16[4,8,64,768]{3,2,1,0:T(8,128)(2,1)S(1)} %bitcast.47, bf16[4,8,32,128]{3,2,1,0:T(8,128)(2,1)} %edge_half0.6.after.own.refs_2_.first_ref, ...), custom_call_target="tpu_custom_call", output_to_operand_aliasing={{}: (7, {})} | custom-call | flops 201326592 | bytes 1572864 | tf_op jit(solution)/shard_map/edge_half0/pallas_call | solution.py:226
  220.2 0.7 copy-done.11
  220.9 13.1 %edges.15 = (bf16[3,8,32,128]{3,2,1,0:T(8,128)(2,1)}, bf16[3,8,32,128]{3,2,1,0:T(8,128)(2,1)}) custom-call(bf16[4,8,32,128]{3,2,1,0:T(8,128)(2,1)} %copy-done.9, bf16[4,8,32,128]{3,2,1,0:T(8,128)(2,1)} %collective-permute-done.24.low_az.refs_3_, bf16[4,8,32,128]{3,2,1,0:T(8,128)(2,1)} %collective-permute-done.25.high_az.refs_4_, ...), custom_call_target="tpu_custom_call" | custom-call | tf_op jit(solution)/shard_map/edges/pallas_call | solution.py:106
  234.1 2.6 %collective-permute-start.31 = (bf16[3,8,32,128]{3,2,1,0:T(8,128)(2,1)}, bf16[3,8,32,128]{3,2,1,0:T(8,128)(2,1)}, u32[]{:S(2)}, u32[]{:S(2)}) collective-permute-start(bf16[3,8,32,128]{3,2,1,0:T(8,128)(2,1)} %get-tuple-element.43), channel_id=1, source_target_pairs={{4,0},{8,4},{12,8},{16,12},{20,16},{24,20},{28,24},{0,28},{5,1},{9... | collective-permute-start | bytes 589832 | tf_op jit(solution)/shard_map/ppermute | solution.py:246
  236.7 3.3 %unpack.3.refs_0_ = bf16[4,4,8,64,128]{4,3,2,1,0:T(8,128)(2,1)} custom-call(bf16[4,8,32,128]{3,2,1,0:T(8,128)(2,1)} %edge_half0.4.after.own.refs_2_.first_ref, bf16[4,8,32,128]{3,2,1,0:T(8,128)(2,1)} %edge_half1.4.after.own.refs_2_.second_ref), custom_call_target="tpu_custom_call" | custom-call | tf_op jit(solution)/shard_map/unpack/pallas_call | solution.py:70
  239.9 3.3 %unpack.4.refs_0_ = bf16[4,4,8,64,128]{4,3,2,1,0:T(8,128)(2,1)} custom-call(bf16[4,8,32,128]{3,2,1,0:T(8,128)(2,1)} %edge_half0.5.after.own.refs_2_.first_ref, bf16[4,8,32,128]{3,2,1,0:T(8,128)(2,1)} %edge_half1.5.after.own.refs_2_.second_ref, bf16[4,4,8,64,128]{4,3,2,1,0:T(8,128)(2,1)} %unpack.3.refs_0_), custom_call_target="tpu_custom_call", output_to_operand_aliasing={{}: (2, {})} | custom-call | tf_op jit(solution)/shard_map/unpack/pallas_call | solution.py:70
  243.2 3.3 %unpack.5.refs_6_ = bf16[4,4,8,64,128]{4,3,2,1,0:T(8,128)(2,1)} custom-call(bf16[4,8,32,128]{3,2,1,0:T(8,128)(2,1)} %edge_half0.6.after.own.refs_2_.first_ref, bf16[4,8,32,128]{3,2,1,0:T(8,128)(2,1)} %copy-done.9, bf16[4,4,8,64,128]{4,3,2,1,0:T(8,128)(2,1)} %unpack.4.refs_0_), custom_call_target="tpu_custom_call", output_to_operand_aliasing={{}: (2, {})} | custom-call | tf_op jit(solution)/shard_map/unpack/pallas_call | solution.py:70
  246.5 1.9 copy-done.8
  248.4 0.9 copy-done.12
  249.3 3.6 %inner_half1.7 = (bf16[4,8,32,128]{3,2,1,0:T(8,128)(2,1)S(1)}, bf16[4,4,8,64,128]{4,3,2,1,0:T(8,128)(2,1)}) custom-call(s32[8,12]{1,0:T(8,128)S(1)} %fusion.30.refs_0_, bf16[4,8,64,768]{3,2,1,0:T(8,128)(2,1)S(1)} %bitcast.48, bf16[4,8,32,128]{3,2,1,0:T(8,128)(2,1)S(1)} %copy-done.10, ...), custom_call_target="tpu_custom_call", output_to_operand_aliasing={{1}: (6, {})} | custom-call | flops 201326592 | bytes 1572864 | tf_op jit(solution)/shard_map/inner_half1/pallas_call | solution.py:226
  252.9 3.7 %edge_half1.7 = (bf16[4,8,32,128]{3,2,1,0:T(8,128)(2,1)S(1)}, bf16[4,4,8,64,128]{4,3,2,1,0:T(8,128)(2,1)}) custom-call(s32[8,12]{1,0:T(8,128)S(1)} %fusion.30.refs_0_, bf16[4,8,64,768]{3,2,1,0:T(8,128)(2,1)S(1)} %bitcast.49, bf16[4,8,32,128]{3,2,1,0:T(8,128)(2,1)S(1)} %copy-done.10, ...), custom_call_target="tpu_custom_call", output_to_operand_aliasing={{0}: (8, {}), {1}: (9, {})} | custom-call | flops 201326592 | bytes 1572864 | tf_op jit(solution)/shard_map/edge_half1/pallas_call | solution.py:226
  (76 shorter events, 0.9 us)
Async XLA Ops:
  0.0 12.4 %copy-start = (bf16[4,1,8,64,768]{4,3,2,1,0:T(8,128)(2,1)S(1)}, bf16[4,1,8,64,768]{4,3,2,1,0:T(8,128)(2,1)}, u32[]{:S(2)}) copy-start(bf16[4,1,8,64,768]{4,3,2,1,0:T(8,128)(2,1)} %param.4) | copy-start | bytes 9437188
  3.5 18.9 %collective-permute-start.2 = (bf16[4,8,32,128]{3,2,1,0:T(8,128)(2,1)}, bf16[4,8,32,128]{3,2,1,0:T(8,128)(2,1)}, u32[]{:S(2)}, u32[]{:S(2)}) collective-permute-start(bf16[4,8,32,128]{3,2,1,0:T(8,128)(2,1)} %get-tuple-element.27.own.after.refs_2_), channel_id=1, source_target_pairs={{0,1},{1,2},{2,3},{3,0},{4,5},{5,6},{6,7},{7,4},{8,9},{9,10},{10,1... | collective-permute-start | bytes 786440 | tf_op jit(solution)/shard_map/ppermute | solution.py:246
  6.5 15.9 %collective-permute-start.3 = (bf16[4,8,32,128]{3,2,1,0:T(8,128)(2,1)}, bf16[4,8,32,128]{3,2,1,0:T(8,128)(2,1)}, u32[]{:S(2)}, u32[]{:S(2)}) collective-permute-start(bf16[4,8,32,128]{3,2,1,0:T(8,128)(2,1)} %get-tuple-element.27.own.after.refs_2_), channel_id=1, source_target_pairs={{1,0},{2,1},{3,2},{0,3},{5,4},{6,5},{7,6},{4,7},{9,8},{10,9},{11,1... | collective-permute-start | bytes 786440 | tf_op jit(solution)/shard_map/ppermute | solution.py:246
  8.5 42.4 %collective-permute-start = (bf16[4,8,32,128]{3,2,1,0:T(8,128)(2,1)}, bf16[4,8,32,128]{3,2,1,0:T(8,128)(2,1)}, u32[]{:S(2)}, u32[]{:S(2)}) collective-permute-start(bf16[4,8,32,128]{3,2,1,0:T(8,128)(2,1)} %get-tuple-element.26.own.refs_2_), channel_id=1, source_target_pairs={{0,1},{1,2},{2,3},{3,0},{4,5},{5,6},{6,7},{7,4},{8,9},{9,10},{10,1... | collective-permute-start | bytes 786440 | tf_op jit(solution)/shard_map/ppermute | solution.py:246
  8.5 42.4 %collective-permute-start.1 = (bf16[4,8,32,128]{3,2,1,0:T(8,128)(2,1)}, bf16[4,8,32,128]{3,2,1,0:T(8,128)(2,1)}, u32[]{:S(2)}, u32[]{:S(2)}) collective-permute-start(bf16[4,8,32,128]{3,2,1,0:T(8,128)(2,1)} %get-tuple-element.26.own.refs_2_), channel_id=1, source_target_pairs={{1,0},{2,1},{3,2},{0,3},{5,4},{6,5},{7,6},{4,7},{9,8},{10,9},{11,1... | collective-permute-start | bytes 786440 | tf_op jit(solution)/shard_map/ppermute | solution.py:246
  17.7 20.5 %copy-start.19 = (s32[1,8,12]{2,1,0:T(8,128)S(1)}, s32[1,8,12]{2,1,0:T(8,128)}, u32[]{:S(2)}) copy-start(s32[1,8,12]{2,1,0:T(8,128)} %param.5) | copy-start | bytes 1156
  17.7 20.5 %copy-start.13 = (bf16[4,8,32,128]{3,2,1,0:T(8,128)(2,1)S(1)}, bf16[4,8,32,128]{3,2,1,0:T(8,128)(2,1)}, u32[]{:S(2)}) copy-start(bf16[4,8,32,128]{3,2,1,0:T(8,128)(2,1)} %get-tuple-element.27.own.after.refs_2_) | copy-start | bytes 786436
  35.5 7.9 %collective-permute-start.4 = (bf16[3,8,32,128]{3,2,1,0:T(8,128)(2,1)}, bf16[3,8,32,128]{3,2,1,0:T(8,128)(2,1)S(1)}, u32[]{:S(2)}, u32[]{:S(2)}) collective-permute-start(bf16[3,8,32,128]{3,2,1,0:T(8,128)(2,1)} %get-tuple-element.28), channel_id=1, source_target_pairs={{0,4},{4,8},{8,12},{12,16},{16,20},{20,24},{24,28},{28,0},{1,5},{5... | collective-permute-start | bytes 589832 | tf_op jit(solution)/shard_map/ppermute | solution.py:246
  35.5 7.9 %collective-permute-start.5 = (bf16[3,8,32,128]{3,2,1,0:T(8,128)(2,1)}, bf16[3,8,32,128]{3,2,1,0:T(8,128)(2,1)S(1)}, u32[]{:S(2)}, u32[]{:S(2)}) collective-permute-start(bf16[3,8,32,128]{3,2,1,0:T(8,128)(2,1)} %get-tuple-element.29), channel_id=1, source_target_pairs={{4,0},{8,4},{12,8},{16,12},{20,16},{24,20},{28,24},{0,28},{5,1},{9... | collective-permute-start | bytes 589832 | tf_op jit(solution)/shard_map/ppermute | solution.py:246
  38.2 1.9 copy-start.1
  47.0 33.3 %collective-permute-start.10 = (bf16[4,8,32,128]{3,2,1,0:T(8,128)(2,1)}, bf16[4,8,32,128]{3,2,1,0:T(8,128)(2,1)S(1)}, u32[]{:S(2)}, u32[]{:S(2)}) collective-permute-start(bf16[4,8,32,128]{3,2,1,0:T(8,128)(2,1)} %edge_half0.4.after.own.refs_2_.first_ref), channel_id=1, source_target_pairs={{0,1},{1,2},{2,3},{3,0},{4,5},{5,6},{6,7},{7,4},{8,9},{9,10},{10,1... | collective-permute-start | bytes 786440 | tf_op jit(solution)/shard_map/ppermute | solution.py:246
  47.1 33.2 %collective-permute-start.11 = (bf16[4,8,32,128]{3,2,1,0:T(8,128)(2,1)}, bf16[4,8,32,128]{3,2,1,0:T(8,128)(2,1)}, u32[]{:S(2)}, u32[]{:S(2)}) collective-permute-start(bf16[4,8,32,128]{3,2,1,0:T(8,128)(2,1)} %edge_half0.4.after.own.refs_2_.first_ref), channel_id=1, source_target_pairs={{1,0},{2,1},{3,2},{0,3},{5,4},{6,5},{7,6},{4,7},{9,8},{10,9},{11,1... | collective-permute-start | bytes 786440 | tf_op jit(solution)/shard_map/ppermute | solution.py:246
  64.0 8.8 %collective-permute-start.6 = (bf16[3,8,32,128]{3,2,1,0:T(8,128)(2,1)}, bf16[3,8,32,128]{3,2,1,0:T(8,128)(2,1)S(1)}, u32[]{:S(2)}, u32[]{:S(2)}) collective-permute-start(bf16[3,8,32,128]{3,2,1,0:T(8,128)(2,1)} %get-tuple-element.30), channel_id=1, source_target_pairs={{0,4},{4,8},{8,12},{12,16},{16,20},{20,24},{24,28},{28,0},{1,5},{5... | collective-permute-start | bytes 589832 | tf_op jit(solution)/shard_map/ppermute | solution.py:246
  64.0 8.8 %collective-permute-start.7 = (bf16[3,8,32,128]{3,2,1,0:T(8,128)(2,1)}, bf16[3,8,32,128]{3,2,1,0:T(8,128)(2,1)S(1)}, u32[]{:S(2)}, u32[]{:S(2)}) collective-permute-start(bf16[3,8,32,128]{3,2,1,0:T(8,128)(2,1)} %get-tuple-element.31), channel_id=1, source_target_pairs={{4,0},{8,4},{12,8},{16,12},{20,16},{24,20},{28,24},{0,28},{5,1},{9... | collective-permute-start | bytes 589832 | tf_op jit(solution)/shard_map/ppermute | solution.py:246
  66.7 1.9 copy-start.2
  68.6 0.9 copy-start.14
  76.4 34.0 %collective-permute-start.8 = (bf16[4,8,32,128]{3,2,1,0:T(8,128)(2,1)}, bf16[4,8,32,128]{3,2,1,0:T(8,128)(2,1)}, u32[]{:S(2)}, u32[]{:S(2)}) collective-permute-start(bf16[4,8,32,128]{3,2,1,0:T(8,128)(2,1)} %edge_half1.4.after.own.refs_2_.second_ref), channel_id=1, source_target_pairs={{0,1},{1,2},{2,3},{3,0},{4,5},{5,6},{6,7},{7,4},{8,9},{9,10},{10,1... | collective-permute-start | bytes 786440 | tf_op jit(solution)/shard_map/ppermute | solution.py:246
  76.5 33.9 %collective-permute-start.9 = (bf16[4,8,32,128]{3,2,1,0:T(8,128)(2,1)}, bf16[4,8,32,128]{3,2,1,0:T(8,128)(2,1)}, u32[]{:S(2)}, u32[]{:S(2)}) collective-permute-start(bf16[4,8,32,128]{3,2,1,0:T(8,128)(2,1)} %edge_half1.4.after.own.refs_2_.second_ref), channel_id=1, source_target_pairs={{1,0},{2,1},{3,2},{0,3},{5,4},{6,5},{7,6},{4,7},{9,8},{10,9},{11,1... | collective-permute-start | bytes 786440 | tf_op jit(solution)/shard_map/ppermute | solution.py:246
  80.3 0.7 copy-start.15
  94.1 8.9 %collective-permute-start.12 = (bf16[3,8,32,128]{3,2,1,0:T(8,128)(2,1)}, bf16[3,8,32,128]{3,2,1,0:T(8,128)(2,1)S(1)}, u32[]{:S(2)}, u32[]{:S(2)}) collective-permute-start(bf16[3,8,32,128]{3,2,1,0:T(8,128)(2,1)} %get-tuple-element.32), channel_id=1, source_target_pairs={{0,4},{4,8},{8,12},{12,16},{16,20},{20,24},{24,28},{28,0},{1,5},{5... | collective-permute-start | bytes 589832 | tf_op jit(solution)/shard_map/ppermute | solution.py:246
  94.1 8.8 %collective-permute-start.13 = (bf16[3,8,32,128]{3,2,1,0:T(8,128)(2,1)}, bf16[3,8,32,128]{3,2,1,0:T(8,128)(2,1)S(1)}, u32[]{:S(2)}, u32[]{:S(2)}) collective-permute-start(bf16[3,8,32,128]{3,2,1,0:T(8,128)(2,1)} %get-tuple-element.33), channel_id=1, source_target_pairs={{4,0},{8,4},{12,8},{16,12},{20,16},{24,20},{28,24},{0,28},{5,1},{9... | collective-permute-start | bytes 589832 | tf_op jit(solution)/shard_map/ppermute | solution.py:246
  96.8 1.9 copy-start.3
  98.6 0.9 copy-start.16
  106.5 32.4 %collective-permute-start.18 = (bf16[4,8,32,128]{3,2,1,0:T(8,128)(2,1)}, bf16[4,8,32,128]{3,2,1,0:T(8,128)(2,1)S(1)}, u32[]{:S(2)}, u32[]{:S(2)}) collective-permute-start(bf16[4,8,32,128]{3,2,1,0:T(8,128)(2,1)} %edge_half0.5.after.own.refs_2_.first_ref), channel_id=1, source_target_pairs={{0,1},{1,2},{2,3},{3,0},{4,5},{5,6},{6,7},{7,4},{8,9},{9,10},{10,1... | collective-permute-start | bytes 786440 | tf_op jit(solution)/shard_map/ppermute | solution.py:246
  106.6 32.3 %collective-permute-start.19 = (bf16[4,8,32,128]{3,2,1,0:T(8,128)(2,1)}, bf16[4,8,32,128]{3,2,1,0:T(8,128)(2,1)}, u32[]{:S(2)}, u32[]{:S(2)}) collective-permute-start(bf16[4,8,32,128]{3,2,1,0:T(8,128)(2,1)} %edge_half0.5.after.own.refs_2_.first_ref), channel_id=1, source_target_pairs={{1,0},{2,1},{3,2},{0,3},{5,4},{6,5},{7,6},{4,7},{9,8},{10,9},{11,1... | collective-permute-start | bytes 786440 | tf_op jit(solution)/shard_map/ppermute | solution.py:246
  123.5 8.0 %collective-permute-start.14 = (bf16[3,8,32,128]{3,2,1,0:T(8,128)(2,1)}, bf16[3,8,32,128]{3,2,1,0:T(8,128)(2,1)S(1)}, u32[]{:S(2)}, u32[]{:S(2)}) collective-permute-start(bf16[3,8,32,128]{3,2,1,0:T(8,128)(2,1)} %get-tuple-element.34), channel_id=1, source_target_pairs={{0,4},{4,8},{8,12},{12,16},{16,20},{20,24},{24,28},{28,0},{1,5},{5... | collective-permute-start | bytes 589832 | tf_op jit(solution)/shard_map/ppermute | solution.py:246
  123.5 7.9 %collective-permute-start.15 = (bf16[3,8,32,128]{3,2,1,0:T(8,128)(2,1)}, bf16[3,8,32,128]{3,2,1,0:T(8,128)(2,1)S(1)}, u32[]{:S(2)}, u32[]{:S(2)}) collective-permute-start(bf16[3,8,32,128]{3,2,1,0:T(8,128)(2,1)} %get-tuple-element.35), channel_id=1, source_target_pairs={{4,0},{8,4},{12,8},{16,12},{20,16},{24,20},{28,24},{0,28},{5,1},{9... | collective-permute-start | bytes 589832 | tf_op jit(solution)/shard_map/ppermute | solution.py:246
  126.2 1.9 copy-start.4
  135.0 34.0 %collective-permute-start.16 = (bf16[4,8,32,128]{3,2,1,0:T(8,128)(2,1)}, bf16[4,8,32,128]{3,2,1,0:T(8,128)(2,1)}, u32[]{:S(2)}, u32[]{:S(2)}) collective-permute-start(bf16[4,8,32,128]{3,2,1,0:T(8,128)(2,1)} %edge_half1.5.after.own.refs_2_.second_ref), channel_id=1, source_target_pairs={{0,1},{1,2},{2,3},{3,0},{4,5},{5,6},{6,7},{7,4},{8,9},{9,10},{10,1... | collective-permute-start | bytes 786440 | tf_op jit(solution)/shard_map/ppermute | solution.py:246
  135.1 33.9 %collective-permute-start.17 = (bf16[4,8,32,128]{3,2,1,0:T(8,128)(2,1)}, bf16[4,8,32,128]{3,2,1,0:T(8,128)(2,1)}, u32[]{:S(2)}, u32[]{:S(2)}) collective-permute-start(bf16[4,8,32,128]{3,2,1,0:T(8,128)(2,1)} %edge_half1.5.after.own.refs_2_.second_ref), channel_id=1, source_target_pairs={{1,0},{2,1},{3,2},{0,3},{5,4},{6,5},{7,6},{4,7},{9,8},{10,9},{11,1... | collective-permute-start | bytes 786440 | tf_op jit(solution)/shard_map/ppermute | solution.py:246
  138.9 0.7 copy-start.17
  152.7 8.9 %collective-permute-start.20 = (bf16[3,8,32,128]{3,2,1,0:T(8,128)(2,1)}, bf16[3,8,32,128]{3,2,1,0:T(8,128)(2,1)S(1)}, u32[]{:S(2)}, u32[]{:S(2)}) collective-permute-start(bf16[3,8,32,128]{3,2,1,0:T(8,128)(2,1)} %get-tuple-element.36), channel_id=1, source_target_pairs={{0,4},{4,8},{8,12},{12,16},{16,20},{20,24},{24,28},{28,0},{1,5},{5... | collective-permute-start | bytes 589832 | tf_op jit(solution)/shard_map/ppermute | solution.py:246
  152.8 8.8 %collective-permute-start.21 = (bf16[3,8,32,128]{3,2,1,0:T(8,128)(2,1)}, bf16[3,8,32,128]{3,2,1,0:T(8,128)(2,1)S(1)}, u32[]{:S(2)}, u32[]{:S(2)}) collective-permute-start(bf16[3,8,32,128]{3,2,1,0:T(8,128)(2,1)} %get-tuple-element.37), channel_id=1, source_target_pairs={{4,0},{8,4},{12,8},{16,12},{20,16},{24,20},{28,24},{0,28},{5,1},{9... | collective-permute-start | bytes 589832 | tf_op jit(solution)/shard_map/ppermute | solution.py:246
  155.4 1.9 copy-start.5
  157.3 0.9 copy-start.18
  165.1 31.4 %collective-permute-start.26 = (bf16[4,8,32,128]{3,2,1,0:T(8,128)(2,1)}, bf16[4,8,32,128]{3,2,1,0:T(8,128)(2,1)}, u32[]{:S(2)}, u32[]{:S(2)}) collective-permute-start(bf16[4,8,32,128]{3,2,1,0:T(8,128)(2,1)} %edge_half0.6.after.own.refs_2_.first_ref), channel_id=1, source_target_pairs={{0,1},{1,2},{2,3},{3,0},{4,5},{5,6},{6,7},{7,4},{8,9},{9,10},{10,1... | collective-permute-start | bytes 786440 | tf_op jit(solution)/shard_map/ppermute | solution.py:246
  165.2 31.3 %collective-permute-start.27 = (bf16[4,8,32,128]{3,2,1,0:T(8,128)(2,1)}, bf16[4,8,32,128]{3,2,1,0:T(8,128)(2,1)}, u32[]{:S(2)}, u32[]{:S(2)}) collective-permute-start(bf16[4,8,32,128]{3,2,1,0:T(8,128)(2,1)} %edge_half0.6.after.own.refs_2_.first_ref), channel_id=1, source_target_pairs={{1,0},{2,1},{3,2},{0,3},{5,4},{6,5},{7,6},{4,7},{9,8},{10,9},{11,1... | collective-permute-start | bytes 786440 | tf_op jit(solution)/shard_map/ppermute | solution.py:246
  182.1 7.5 %collective-permute-start.22 = (bf16[3,8,32,128]{3,2,1,0:T(8,128)(2,1)}, bf16[3,8,32,128]{3,2,1,0:T(8,128)(2,1)S(1)}, u32[]{:S(2)}, u32[]{:S(2)}) collective-permute-start(bf16[3,8,32,128]{3,2,1,0:T(8,128)(2,1)} %get-tuple-element.38), channel_id=1, source_target_pairs={{0,4},{4,8},{8,12},{12,16},{16,20},{20,24},{24,28},{28,0},{1,5},{5... | collective-permute-start | bytes 589832 | tf_op jit(solution)/shard_map/ppermute | solution.py:246
  182.2 7.4 %collective-permute-start.23 = (bf16[3,8,32,128]{3,2,1,0:T(8,128)(2,1)}, bf16[3,8,32,128]{3,2,1,0:T(8,128)(2,1)S(1)}, u32[]{:S(2)}, u32[]{:S(2)}) collective-permute-start(bf16[3,8,32,128]{3,2,1,0:T(8,128)(2,1)} %get-tuple-element.39), channel_id=1, source_target_pairs={{4,0},{8,4},{12,8},{16,12},{20,16},{24,20},{28,24},{0,28},{5,1},{9... | collective-permute-start | bytes 589832 | tf_op jit(solution)/shard_map/ppermute | solution.py:246
  184.8 1.9 copy-start.6
  192.7 3.9 %copy-start.9 = (bf16[4,8,32,128]{3,2,1,0:T(8,128)(2,1)}, bf16[4,8,32,128]{3,2,1,0:T(8,128)(2,1)S(1)}, u32[]{:S(2)}) copy-start(bf16[4,8,32,128]{3,2,1,0:T(8,128)(2,1)S(1)} %edge_half1.6.after.own.second_ref.refs_2_) | copy-start | bytes 786436
  192.7 28.2 %collective-permute-start.24 = (bf16[4,8,32,128]{3,2,1,0:T(8,128)(2,1)S(1)}, bf16[4,8,32,128]{3,2,1,0:T(8,128)(2,1)}, u32[]{:S(2)}, u32[]{:S(2)}) collective-permute-start(bf16[4,8,32,128]{3,2,1,0:T(8,128)(2,1)S(1)} %edge_half1.6.after.own.second_ref.refs_2_), channel_id=1, source_target_pairs={{0,1},{1,2},{2,3},{3,0},{4,5},{5,6},{6,7},{7,4},{8,9},{9,10},{10,1... | collective-permute-start | bytes 786440 | tf_op jit(solution)/shard_map/ppermute | solution.py:246
  192.7 28.2 %collective-permute-start.25 = (bf16[4,8,32,128]{3,2,1,0:T(8,128)(2,1)S(1)}, bf16[4,8,32,128]{3,2,1,0:T(8,128)(2,1)}, u32[]{:S(2)}, u32[]{:S(2)}) collective-permute-start(bf16[4,8,32,128]{3,2,1,0:T(8,128)(2,1)S(1)} %edge_half1.6.after.own.second_ref.refs_2_), channel_id=1, source_target_pairs={{1,0},{2,1},{3,2},{0,3},{5,4},{6,5},{7,6},{4,7},{9,8},{10,9},{11,1... | collective-permute-start | bytes 786440 | tf_op jit(solution)/shard_map/ppermute | solution.py:246
  209.6 7.5 %collective-permute-start.28 = (bf16[3,8,32,128]{3,2,1,0:T(8,128)(2,1)}, bf16[3,8,32,128]{3,2,1,0:T(8,128)(2,1)S(1)}, u32[]{:S(2)}, u32[]{:S(2)}) collective-permute-start(bf16[3,8,32,128]{3,2,1,0:T(8,128)(2,1)} %get-tuple-element.40), channel_id=1, source_target_pairs={{0,4},{4,8},{8,12},{12,16},{16,20},{20,24},{24,28},{28,0},{1,5},{5... | collective-permute-start | bytes 589832 | tf_op jit(solution)/shard_map/ppermute | solution.py:246
  209.7 7.4 %collective-permute-start.29 = (bf16[3,8,32,128]{3,2,1,0:T(8,128)(2,1)}, bf16[3,8,32,128]{3,2,1,0:T(8,128)(2,1)S(1)}, u32[]{:S(2)}, u32[]{:S(2)}) collective-permute-start(bf16[3,8,32,128]{3,2,1,0:T(8,128)(2,1)} %get-tuple-element.41), channel_id=1, source_target_pairs={{4,0},{8,4},{12,8},{16,12},{20,16},{24,20},{28,24},{0,28},{5,1},{9... | collective-permute-start | bytes 589832 | tf_op jit(solution)/shard_map/ppermute | solution.py:246
  212.3 1.9 copy-start.7
  220.2 0.7 copy-start.11
  234.0 18.9 %collective-permute-start.30 = (bf16[3,8,32,128]{3,2,1,0:T(8,128)(2,1)}, bf16[3,8,32,128]{3,2,1,0:T(8,128)(2,1)}, u32[]{:S(2)}, u32[]{:S(2)}) collective-permute-start(bf16[3,8,32,128]{3,2,1,0:T(8,128)(2,1)} %get-tuple-element.42), channel_id=1, source_target_pairs={{0,4},{4,8},{8,12},{12,16},{16,20},{20,24},{24,28},{28,0},{1,5},{5... | collective-permute-start | bytes 589832 | tf_op jit(solution)/shard_map/ppermute | solution.py:246
  234.1 18.9 %collective-permute-start.31 = (bf16[3,8,32,128]{3,2,1,0:T(8,128)(2,1)}, bf16[3,8,32,128]{3,2,1,0:T(8,128)(2,1)}, u32[]{:S(2)}, u32[]{:S(2)}) collective-permute-start(bf16[3,8,32,128]{3,2,1,0:T(8,128)(2,1)} %get-tuple-element.43), channel_id=1, source_target_pairs={{4,0},{8,4},{12,8},{16,12},{20,16},{24,20},{28,24},{0,28},{5,1},{9... | collective-permute-start | bytes 589832 | tf_op jit(solution)/shard_map/ppermute | solution.py:246
  243.2 3.3 %copy-start.10 = (bf16[4,8,32,128]{3,2,1,0:T(8,128)(2,1)S(1)}, bf16[4,8,32,128]{3,2,1,0:T(8,128)(2,1)}, u32[]{:S(2)}) copy-start(bf16[4,8,32,128]{3,2,1,0:T(8,128)(2,1)} %copy-done.9) | copy-start | bytes 786436
  246.5 1.9 copy-start.8
  248.4 0.9 copy-start.12

commit v4 on v0

v4 whole, which is shorter than its diff:
```python
import functools

import jax
import jax.numpy as jnp
from jax import lax
from jax.experimental import pallas as pl
from jax.experimental.pallas import tpu as pltpu
from jax.sharding import PartitionSpec as P

STEPS = 4
HALVES = 2
VMEM = pl.BlockSpec(memory_space=pltpu.VMEM)
ANY = pl.BlockSpec(memory_space=pl.ANY)


def low_lanes(shape):
    return lax.broadcasted_iota(jnp.int32, shape, len(shape) - 1) < shape[-1] // 2


def swap_lanes(value):
    return pltpu.roll(value, value.shape[-1] // 2, len(value.shape) - 1)


def pack_kernel(start_ref, first_ref, second_ref):
    columns, faces, width, lanes = start_ref.shape
    for column in range(columns):
        for face in range(faces):
            value = start_ref[column, face].astype(jnp.float32)
            top = value[: width // 2]
            bottom = swap_lanes(value[width // 2 :])
            low = low_lanes(top.shape)
            first_ref[column, face] = jnp.where(low, top, bottom).astype(jnp.bfloat16)
            second_ref[column, face] = jnp.where(low, bottom, top).astype(jnp.bfloat16)


def pack(start):
    columns, faces, width, lanes = start.shape
    half = jax.ShapeDtypeStruct((columns, faces, width // 2, lanes), jnp.bfloat16)
    return pl.pallas_call(
        pack_kernel,
        in_specs=[VMEM],
        out_specs=[VMEM] * 2,
        out_shape=[half, half],
        name="pack",
    )(start)


def unpack_kernel(index, chosen, skipped, first_ref, second_ref, *refs):
    basis_ref, done_ref, buffer, sems = refs[-4:]
    done_ref[...] = jnp.zeros_like(done_ref)
    faces, rows = first_ref.shape[1:3]
    copies = []
    for n, column in enumerate(chosen):
        for face in range(faces):
            first = first_ref[column, face].astype(jnp.float32)
            second = second_ref[column - skipped, face].astype(jnp.float32)
            low = low_lanes(first.shape)
            buffer[n, face, :rows] = jnp.where(low, first, second).astype(jnp.bfloat16)
            bottom = swap_lanes(jnp.where(low, second, first))
            buffer[n, face, rows:] = bottom.astype(jnp.bfloat16)
        copies.append(
            pltpu.make_async_copy(buffer.at[n], basis_ref.at[index, column], sems.at[n])
        )
        copies[-1].start()
    for copy in copies:
        copy.wait()


def unpack(index, chosen, first, second, basis, after):
    columns, faces, rows, lanes = first.shape
    size = len(chosen)
    skipped = 0 if second.shape[0] == columns else chosen[0]
    extra = [value for value in (basis, after) if value is not None]
    return pl.pallas_call(
        functools.partial(unpack_kernel, index, chosen, skipped),
        in_specs=[VMEM] * 2 + [ANY] * len(extra),
        out_specs=[ANY, VMEM],
        out_shape=[
            jax.ShapeDtypeStruct((STEPS, columns, faces, 2 * rows, lanes), jnp.bfloat16),
            jax.ShapeDtypeStruct((8, lanes), jnp.float32),
        ],
        scratch_shapes=[
            pltpu.VMEM((size, faces, 2 * rows, lanes), jnp.bfloat16),
            pltpu.SemaphoreType.DMA((size,)),
        ],
        input_output_aliases={} if basis is None else {2: 0},
        name="unpack",
    )(first, second, *extra)


def edges_kernel(own, low_az, high_az, after, to_low, to_high):
    columns = own.shape[0]
    for azim, source in enumerate((low_az, own, high_az)):
        to_low[azim] = source[0]
        to_high[azim] = source[columns - 1]


def edges(own, low_az, high_az, after):
    shape = jax.ShapeDtypeStruct((3, *own.shape[1:]), own.dtype)
    return pl.pallas_call(
        edges_kernel,
        in_specs=[VMEM] * 3 + [ANY],
        out_specs=[VMEM] * 2,
        out_shape=[shape, shape],
        name="edges",
    )(own, low_az, high_az, after)


def part_kernel(half, chosen, slots, *refs):
    window = refs[-1]
    following = refs[-2]
    table, blocks, own, low_az, high_az = refs[:5]
    faces, width, depth = blocks.shape[1:]
    columns = own.shape[0]
    span = columns + 2
    rows, lanes = window.shape[1:]
    view = window.reshape(3, span, faces, rows, lanes)
    for azim, source in enumerate((low_az, own, high_az)):
        view[azim, 1 : columns + 1] = source[...]
    if len(refs) > 7:
        low_st, high_st, before, after = refs[5:9]
        view[:, 0] = low_st[...]
        view[:, span - 1] = high_st[...]
        following[1 : columns - 1] = before[...]

    neighbours = table.shape[1]
    low = low_lanes((rows, lanes))
    for slot, column in zip(slots, chosen):
        for face in range(faces):
            gathered = jnp.concatenate(
                [window[table[face, k] + column * faces] for k in range(neighbours)], axis=0
            )
            block = blocks[column, face]
            stacked = jnp.concatenate([block[:, : depth // 2], block[:, depth // 2 :]], axis=0)
            product = jnp.dot(stacked, gathered, preferred_element_type=jnp.float32)
            top, bottom = product[:width], product[width:]
            if half == 0:
                here = jnp.where(low, top[:rows], bottom[rows:])
                there = jnp.where(low, top[rows:], bottom[:rows])
            else:
                here = jnp.where(low, bottom[rows:], top[:rows])
                there = jnp.where(low, bottom[:rows], top[rows:])
            following[slot, face] = (here + swap_lanes(there)).astype(jnp.bfloat16)


def part(half, chosen, table, blocks, pieces, stream=None, before=None, after=None):
    columns, faces, width, depth = blocks.shape
    rows, lanes = pieces[0].shape[2:]
    args = [table, blocks, *pieces]
    in_specs = [pl.BlockSpec(memory_space=pltpu.SMEM)] + [VMEM] * 4
    size = len(chosen)
    if stream is None:
        slots, out_columns = range(size), size
    else:
        slots, out_columns = chosen, columns
        args += [*stream, before, after]
        in_specs += [VMEM] * 3 + [ANY]
    name = "inner" if stream is None else "edge"
    return pl.pallas_call(
        functools.partial(part_kernel, half, chosen, slots),
        in_specs=in_specs,
        out_specs=VMEM,
        out_shape=jax.ShapeDtypeStruct((out_columns, faces, rows, lanes), jnp.bfloat16),
        scratch_shapes=[pltpu.VMEM((3 * (columns + 2) * faces, rows, lanes), jnp.bfloat16)],
        cost_estimate=pl.CostEstimate(
            flops=2 * size * faces * width * depth * lanes,
            bytes_accessed=2 * size * faces * width * depth,
            transcendentals=0,
        ),
        name=f"{name}_half{half}",
    )(*args)


def shift(value, axis, up):
    count = lax.axis_size(axis)
    pairs = [(i, (i + 1) % count) for i in range(count)]
    if not up:
        pairs = [(target, source) for source, target in pairs]
    return lax.ppermute(value, axis, pairs)


def halves_of_rows(blocks):
    columns, faces, width, depth = blocks.shape
    row = lax.broadcasted_iota(jnp.int32, (depth, depth), 0)
    column = lax.broadcasted_iota(jnp.int32, (depth, depth), 1)
    part_rows = width // 2
    place = (row // width) * part_rows + row % part_rows + ((row // part_rows) % 2) * (depth // 2)
    mover = (place == column).astype(jnp.bfloat16)
    moved = jnp.dot(blocks.reshape(-1, depth), mover, preferred_element_type=jnp.float32)
    return moved.astype(jnp.bfloat16).reshape(blocks.shape)


def local(start_vector, trace_blocks, neighbour):
    columns, around, faces, width, lanes = start_vector.shape
    start = start_vector.reshape(columns, faces, width, lanes)
    blocks = halves_of_rows(trace_blocks.reshape(columns, faces, width, -1))
    codes = neighbour.reshape(faces, -1)
    table = (((codes // faces) % 3) * (columns + 2) + codes // (3 * faces)) * faces + codes % faces
    inner = tuple(range(1, columns - 1))
    outer = (0, columns - 1)
    every = tuple(range(columns))
    current = list(pack(start))
    basis = None
    latest = current[0]
    for index in range(STEPS):
        around_z = [
            (shift(current[h], "azim", True), shift(current[h], "azim", False))
            for h in range(HALVES)
        ]
        previous = tuple(current)
        for h in range(HALVES):
            last = index == STEPS - 1 and h == HALVES - 1
            pieces = (current[h], *around_z[h])
            to_low, to_high = edges(*pieces, latest)
            stream = [shift(to_high, "stream", True), shift(to_low, "stream", False)]
            middle = part(h, inner, table, blocks, pieces)
            after = middle
            if h == 0 and index > 0:
                basis, after = unpack(index - 1, every, *previous, basis, middle)
            if last:
                basis, after = unpack(index, inner, current[0], middle, basis, None)
            current[h] = latest = part(h, outer, table, blocks, pieces, stream, middle, after)
    basis, _ = unpack(STEPS - 1, outer, *current, basis, None)
    return basis.reshape(STEPS, columns, around, faces, width, lanes)


def solution(mesh):
    return jax.shard_map(
        local,
        mesh=mesh,
        in_specs=(
            P("stream", "azim", None, None, None),
            P("stream", "azim", None, None, None),
            P("azim", None, None),
        ),
        out_specs=P(None, "stream", "azim", None, None, None),
        check_vma=False,
    )
```

time: 318 us -> 161 us (0.51)
  waiting for transfers between devices: 145 us -> 3.46 us
  Pallas kernels: 0 us -> 86 us
  local copies, waits for them, and re-layouts: 87.4 us -> 12.3 us
  matrix products: 50.5 us -> 5.28 us
  starting transfers between devices: 27.2 us -> 52.5 us
  other arithmetic: 5.45 us -> 0.65 us
    ppermute x16 -> x32, waiting for transfers between devices: 145 us -> 3.46 us  [shift(): return lax.ppermute(value, axis, pairs)]
    pallas_call x0 -> x30, Pallas kernels: none -> 86 us  [the longest x16 56.5 us: part(): pl.pallas_call(functools.partial(part_kernel, half, chosen, slots), in_sp...]
    another operation x14 -> x0, local copies, waits for them, and re-layouts: 77.6 us -> none
    dot_general x8 -> x1, matrix products: 50.5 us -> 5.28 us  [halves_of_rows(): jnp.dot(blocks.reshape(-1, depth), mover, preferred_element_type=jnp.floa...]
    ppermute x16 -> x32, starting transfers between devices: 27.2 us -> 52.5 us  [shift(): return lax.ppermute(value, axis, pairs)]
    convert_element_type x0 -> x1, local copies, waits for them, and re-layouts: none -> 4.71 us  [halves_of_rows(): return moved.astype(jnp.bfloat16).reshape(blocks.shape)]
    unnamed x40 -> x28, local copies, waits for them, and re-layouts: 7.83 us -> 7.61 us
  transfers between devices with their start and end apart: 16 -> 32, of which waited for: 13 -> 3; matrix products, arithmetic and copies ran while one was open for 1% -> 7% of each run, Pallas kernels for 0% -> 47%
where the time goes in v4:
time: 161 us
  Pallas kernels  86 us (53%)
  starting transfers between devices  52.5 us (33%)
  local copies, waits for them, and re-layouts  12.3 us (8%)
  matrix products  5.28 us (3%)
  waiting for transfers between devices  3.46 us (2%)
    pallas_call x16, Pallas kernels, part(): pl.pallas_call(functools.partial(part_kernel, half, chosen, slots), in_sp...  56.5 us
    ppermute x32, starting transfers between devices, shift(): return lax.ppermute(value, axis, pairs)  52.5 us
    pallas_call x8, Pallas kernels, edges(): pl.pallas_call(edges_kernel, in_specs=[VMEM] * 3 + [ANY], out_specs=[VMEM...  15 us
    pallas_call x5, Pallas kernels, unpack(): pl.pallas_call(functools.partial(unpack_kernel, index, chosen, skipped),...  12.4 us
    unnamed x28, local copies, waits for them, and re-layouts  7.61 us
    dot_general x1, matrix products, halves_of_rows(): jnp.dot(blocks.reshape(-1, depth), mover, preferred_element_type=jnp.floa...  5.28 us
    convert_element_type x1, local copies, waits for them, and re-layouts, halves_of_rows(): return moved.astype(jnp.bfloat16).reshape(blocks.shape)  4.71 us
    ppermute x32, waiting for transfers between devices, shift(): return lax.ppermute(value, axis, pairs)  3.46 us
  transfers between devices with their start and end apart: 32, of which 3 were waited for; matrix products, arithmetic and copies ran while one was open for 7% of the time, Pallas kernels for 47%

profile of v4, /device:TPU:0, one launch (start us, length us, event | category | flops | bytes accessed | tf_op | source)
XLA Modules:
  0.0 160.7 jit_solution(2516701067743414995)
XLA Ops:
  0.0 2.2 %pack.1 = (bf16[4,8,32,128]{3,2,1,0:T(8,128)(2,1)}, bf16[4,8,32,128]{3,2,1,0:T(8,128)(2,1)}) custom-call(bf16[4,8,64,128]{3,2,1,0:T(8,128)(2,1)} %bitcast.50), custom_call_target="tpu_custom_call" | custom-call | tf_op jit(solution)/shard_map/pack/pallas_call | solution.py:39
  2.2 5.0 %collective-permute-start.1 = (bf16[4,8,32,128]{3,2,1,0:T(8,128)(2,1)}, bf16[4,8,32,128]{3,2,1,0:T(8,128)(2,1)}, u32[]{:S(2)}, u32[]{:S(2)}) collective-permute-start(bf16[4,8,32,128]{3,2,1,0:T(8,128)(2,1)} %get-tuple-element.32.own.after.refs_2_), channel_id=1, source_target_pairs={{1,0},{2,1},{3,2},{0,3},{5,4},{6,5},{7,6},{4,7},{9,8},{10,9},{11,1... | collective-permute-start | bytes 786440 | tf_op jit(solution)/shard_map/ppermute | solution.py:179
  7.2 3.8 %collective-permute-start.7 = (bf16[4,8,32,128]{3,2,1,0:T(8,128)(2,1)}, bf16[4,8,32,128]{3,2,1,0:T(8,128)(2,1)S(1)}, u32[]{:S(2)}, u32[]{:S(2)}) collective-permute-start(bf16[4,8,32,128]{3,2,1,0:T(8,128)(2,1)} %get-tuple-element.35.own.refs_2_), channel_id=1, source_target_pairs={{1,0},{2,1},{3,2},{0,3},{5,4},{6,5},{7,6},{4,7},{9,8},{10,9},{11,1... | collective-permute-start | bytes 786440 | tf_op jit(solution)/shard_map/ppermute | solution.py:179
  11.1 5.3 %fusion = bf16[2048,768]{0,1:T(8,128)(2,1)} fusion(bf16[2048,768]{1,0:T(8,128)(2,1)S(1)} %bitcast.33, s32[768]{0:T(1024)S(1)} %get-tuple-element.59, s32[768]{0:T(1024)S(1)} %get-tuple-element.65, s32[768]{0:T(1024)S(1)} %get-tuple-element.60, s32[768]{0:T(1024)S(1)} %get-tuple-element.62, s32[768]{0:T(1024)S(1)} %get-tuple-element.61, ...), kind=kOutput, calls=%fused_computation.6 | convolution fusion | flops 2429288448 | bytes 6312192 | tf_op jit(solution)/shard_map/dot_general | solution.py:189
  16.4 4.7 %copy.8 = bf16[2048,768]{1,0:T(8,128)(2,1)} copy(bf16[2048,768]{0,1:T(8,128)(2,1)} %fusion) | data formatting | bytes 6291456 | tf_op jit(solution)/shard_map/convert_element_type | solution.py:190
  21.1 1.9 %edges.8 = (bf16[3,8,32,128]{3,2,1,0:T(8,128)(2,1)}, bf16[3,8,32,128]{3,2,1,0:T(8,128)(2,1)}) custom-call(bf16[4,8,32,128]{3,2,1,0:T(8,128)(2,1)} %get-tuple-element.32.own.after.refs_2_, bf16[4,8,32,128]{3,2,1,0:T(8,128)(2,1)} %collective-permute-done.low_az.refs_3_, bf16[4,8,32,128]{3,2,1,0:T(8,128)(2,1)} %collective-permute-done.1.high_az.refs_4_, ...), custom_call_target="tpu_custom_call" | custom-call | tf_op jit(solution)/shard_map/edges/pallas_call | solution.py:100
  23.0 2.6 %collective-permute-start.3 = (bf16[3,8,32,128]{3,2,1,0:T(8,128)(2,1)}, bf16[3,8,32,128]{3,2,1,0:T(8,128)(2,1)}, u32[]{:S(2)}, u32[]{:S(2)}) collective-permute-start(bf16[3,8,32,128]{3,2,1,0:T(8,128)(2,1)} %get-tuple-element.34), channel_id=1, source_target_pairs={{4,0},{8,4},{12,8},{16,12},{20,16},{24,20},{28,24},{0,28},{5,1},{9... | collective-permute-start | bytes 589832 | tf_op jit(solution)/shard_map/ppermute | solution.py:179
  25.6 0.6 fusion.30.refs_0_
  26.3 3.4 %inner_half0.4.refs_7_.refs_8_ = bf16[2,8,32,128]{3,2,1,0:T(8,128)(2,1)} custom-call(s32[8,12]{1,0:T(8,128)} %fusion.30.refs_0_, bf16[4,8,64,768]{3,2,1,0:T(8,128)(2,1)} %bitcast.34, bf16[4,8,32,128]{3,2,1,0:T(8,128)(2,1)} %get-tuple-element.32.own.after.refs_2_, bf16[4,8,32,128]{3,2,1,0:T(8,128)(2,1)} %collective-permute-done.low_az.refs_3_, ...), custom_call_target="tpu_custom_call" | custom-call | flops 201326592 | bytes 1572864 | tf_op jit(solution)/shard_map/inner_half0/pallas_call | solution.py:159
  29.7 3.6 %edge_half0.4.after.own.refs_2_.first_ref = bf16[4,8,32,128]{3,2,1,0:T(8,128)(2,1)} custom-call(s32[8,12]{1,0:T(8,128)} %fusion.30.refs_0_, bf16[4,8,64,768]{3,2,1,0:T(8,128)(2,1)} %bitcast.35, bf16[4,8,32,128]{3,2,1,0:T(8,128)(2,1)} %get-tuple-element.32.own.after.refs_2_, bf16[4,8,32,128]{3,2,1,0:T(8,128)(2,1)} %collective-permute-done.low_az.refs_3_, ...), custom_call_target="tpu_custom_call" | custom-call | flops 201326592 | bytes 1572864 | tf_op jit(solution)/shard_map/edge_half0/pallas_call | solution.py:159
  33.3 3.8 %collective-permute-start.5 = (bf16[4,8,32,128]{3,2,1,0:T(8,128)(2,1)}, bf16[4,8,32,128]{3,2,1,0:T(8,128)(2,1)}, u32[]{:S(2)}, u32[]{:S(2)}) collective-permute-start(bf16[4,8,32,128]{3,2,1,0:T(8,128)(2,1)} %edge_half0.4.after.own.refs_2_.first_ref), channel_id=1, source_target_pairs={{1,0},{2,1},{3,2},{0,3},{5,4},{6,5},{7,6},{4,7},{9,8},{10,9},{11,1... | collective-permute-start | bytes 786440 | tf_op jit(solution)/shard_map/ppermute | solution.py:179
  37.2 0.7 copy-done.1
  37.9 1.9 %edges.9 = (bf16[3,8,32,128]{3,2,1,0:T(8,128)(2,1)}, bf16[3,8,32,128]{3,2,1,0:T(8,128)(2,1)}) custom-call(bf16[4,8,32,128]{3,2,1,0:T(8,128)(2,1)} %get-tuple-element.35.own.refs_2_, bf16[4,8,32,128]{3,2,1,0:T(8,128)(2,1)} %collective-permute-done.6.low_az.refs_3_, bf16[4,8,32,128]{3,2,1,0:T(8,128)(2,1)} %copy-done.1, ...), custom_call_target="tpu_custom_call" | custom-call | tf_op jit(solution)/shard_map/edges/pallas_call | solution.py:100
  39.7 1.3 collective-permute-start.8
  41.0 1.3 collective-permute-start.9
  42.4 3.4 %inner_half1.4.refs_7_.refs_8_ = bf16[2,8,32,128]{3,2,1,0:T(8,128)(2,1)} custom-call(s32[8,12]{1,0:T(8,128)} %fusion.30.refs_0_, bf16[4,8,64,768]{3,2,1,0:T(8,128)(2,1)} %bitcast.36, bf16[4,8,32,128]{3,2,1,0:T(8,128)(2,1)} %get-tuple-element.35.own.refs_2_, bf16[4,8,32,128]{3,2,1,0:T(8,128)(2,1)} %collective-permute-done.6.low_az.refs_3_, ...), custom_call_target="tpu_custom_call" | custom-call | flops 201326592 | bytes 1572864 | tf_op jit(solution)/shard_map/inner_half1/pallas_call | solution.py:159
  45.8 1.3 collective-permute-done.8.refs_5_
  47.1 0.7 copy-done.7
  47.8 0.7 copy-done.10
  48.5 3.6 %edge_half1.4.after.second_ref.own.refs_2_ = bf16[4,8,32,128]{3,2,1,0:T(8,128)(2,1)} custom-call(s32[8,12]{1,0:T(8,128)} %fusion.30.refs_0_, bf16[4,8,64,768]{3,2,1,0:T(8,128)(2,1)} %bitcast.37, bf16[4,8,32,128]{3,2,1,0:T(8,128)(2,1)} %get-tuple-element.35.own.refs_2_, bf16[4,8,32,128]{3,2,1,0:T(8,128)(2,1)} %collective-permute-done.6.low_az.refs_3_, ...), custom_call_target="tpu_custom_call" | custom-call | flops 201326592 | bytes 1572864 | tf_op jit(solution)/shard_map/edge_half1/pallas_call | solution.py:159
  52.1 3.8 %collective-permute-start.15 = (bf16[4,8,32,128]{3,2,1,0:T(8,128)(2,1)}, bf16[4,8,32,128]{3,2,1,0:T(8,128)(2,1)S(1)}, u32[]{:S(2)}, u32[]{:S(2)}) collective-permute-start(bf16[4,8,32,128]{3,2,1,0:T(8,128)(2,1)} %edge_half1.4.after.second_ref.own.refs_2_), channel_id=1, source_target_pairs={{1,0},{2,1},{3,2},{0,3},{5,4},{6,5},{7,6},{4,7},{9,8},{10,9},{11,1... | collective-permute-start | bytes 786440 | tf_op jit(solution)/shard_map/ppermute | solution.py:179
  56.0 1.9 %edges.10 = (bf16[3,8,32,128]{3,2,1,0:T(8,128)(2,1)}, bf16[3,8,32,128]{3,2,1,0:T(8,128)(2,1)}) custom-call(bf16[4,8,32,128]{3,2,1,0:T(8,128)(2,1)} %edge_half0.4.after.own.refs_2_.first_ref, bf16[4,8,32,128]{3,2,1,0:T(8,128)(2,1)} %collective-permute-done.4.low_az.refs_3_, bf16[4,8,32,128]{3,2,1,0:T(8,128)(2,1)} %collective-permute-done.5.high_az.refs_4_, ...), custom_call_target="tpu_custom_call" | custom-call | tf_op jit(solution)/shard_map/edges/pallas_call | solution.py:100
  58.1 2.4 %collective-permute-start.11 = (bf16[3,8,32,128]{3,2,1,0:T(8,128)(2,1)}, bf16[3,8,32,128]{3,2,1,0:T(8,128)(2,1)}, u32[]{:S(2)}, u32[]{:S(2)}) collective-permute-start(bf16[3,8,32,128]{3,2,1,0:T(8,128)(2,1)} %get-tuple-element.39), channel_id=1, source_target_pairs={{4,0},{8,4},{12,8},{16,12},{20,16},{24,20},{28,24},{0,28},{5,1},{9... | collective-permute-start | bytes 589832 | tf_op jit(solution)/shard_map/ppermute | solution.py:179
  60.5 3.4 %inner_half0.5.refs_0_.refs_7_ = bf16[2,8,32,128]{3,2,1,0:T(8,128)(2,1)} custom-call(s32[8,12]{1,0:T(8,128)} %fusion.30.refs_0_, bf16[4,8,64,768]{3,2,1,0:T(8,128)(2,1)} %bitcast.38, bf16[4,8,32,128]{3,2,1,0:T(8,128)(2,1)} %edge_half0.4.after.own.refs_2_.first_ref, bf16[4,8,32,128]{3,2,1,0:T(8,128)(2,1)} %collective-permute-done.4.low_az.refs_3_, ...), custom_call_target="tpu_custom_call" | custom-call | flops 201326592 | bytes 1572864 | tf_op jit(solution)/shard_map/inner_half0/pallas_call | solution.py:159
  63.9 2.5 %unpack.5 = (bf16[4,4,8,64,128]{4,3,2,1,0:T(8,128)(2,1)}, f32[8,128]{1,0:T(8,128)}) custom-call(bf16[4,8,32,128]{3,2,1,0:T(8,128)(2,1)} %edge_half0.4.after.own.refs_2_.first_ref, bf16[4,8,32,128]{3,2,1,0:T(8,128)(2,1)} %edge_half1.4.after.second_ref.own.refs_2_, bf16[2,8,32,128]{3,2,1,0:T(8,128)(2,1)} %inner_half0.5.refs_0_.refs_7_), custom_call_target="tpu_custom_call" | custom-call | tf_op jit(solution)/shard_map/unpack/pallas_call | solution.py:74
  66.5 3.6 %edge_half0.5.after.own.refs_2_.first_ref = bf16[4,8,32,128]{3,2,1,0:T(8,128)(2,1)} custom-call(s32[8,12]{1,0:T(8,128)} %fusion.30.refs_0_, bf16[4,8,64,768]{3,2,1,0:T(8,128)(2,1)} %bitcast.39, bf16[4,8,32,128]{3,2,1,0:T(8,128)(2,1)} %edge_half0.4.after.own.refs_2_.first_ref, bf16[4,8,32,128]{3,2,1,0:T(8,128)(2,1)} %collective-permute-done.4.low_az.refs_3_, ...), custom_call_target="tpu_custom_call" | custom-call | flops 201326592 | bytes 1572864 | tf_op jit(solution)/shard_map/edge_half0/pallas_call | solution.py:159
  70.1 3.8 %collective-permute-start.13 = (bf16[4,8,32,128]{3,2,1,0:T(8,128)(2,1)}, bf16[4,8,32,128]{3,2,1,0:T(8,128)(2,1)}, u32[]{:S(2)}, u32[]{:S(2)}) collective-permute-start(bf16[4,8,32,128]{3,2,1,0:T(8,128)(2,1)} %edge_half0.5.after.own.refs_2_.first_ref), channel_id=1, source_target_pairs={{1,0},{2,1},{3,2},{0,3},{5,4},{6,5},{7,6},{4,7},{9,8},{10,9},{11,1... | collective-permute-start | bytes 786440 | tf_op jit(solution)/shard_map/ppermute | solution.py:179
  73.9 0.7 copy-done.4
  74.6 1.9 %edges.11 = (bf16[3,8,32,128]{3,2,1,0:T(8,128)(2,1)}, bf16[3,8,32,128]{3,2,1,0:T(8,128)(2,1)}) custom-call(bf16[4,8,32,128]{3,2,1,0:T(8,128)(2,1)} %edge_half1.4.after.second_ref.own.refs_2_, bf16[4,8,32,128]{3,2,1,0:T(8,128)(2,1)} %collective-permute-done.14.low_az.refs_3_, bf16[4,8,32,128]{3,2,1,0:T(8,128)(2,1)} %copy-done.4, ...), custom_call_target="tpu_custom_call" | custom-call | tf_op jit(solution)/shard_map/edges/pallas_call | solution.py:100
  76.5 2.6 %collective-permute-start.17 = (bf16[3,8,32,128]{3,2,1,0:T(8,128)(2,1)}, bf16[3,8,32,128]{3,2,1,0:T(8,128)(2,1)S(1)}, u32[]{:S(2)}, u32[]{:S(2)}) collective-permute-start(bf16[3,8,32,128]{3,2,1,0:T(8,128)(2,1)} %get-tuple-element.42), channel_id=1, source_target_pairs={{4,0},{8,4},{12,8},{16,12},{20,16},{24,20},{28,24},{0,28},{5,1},{9... | collective-permute-start | bytes 589832 | tf_op jit(solution)/shard_map/ppermute | solution.py:179
  79.2 3.4 %inner_half1.5.refs_7_.refs_8_ = bf16[2,8,32,128]{3,2,1,0:T(8,128)(2,1)} custom-call(s32[8,12]{1,0:T(8,128)} %fusion.30.refs_0_, bf16[4,8,64,768]{3,2,1,0:T(8,128)(2,1)} %bitcast.40, bf16[4,8,32,128]{3,2,1,0:T(8,128)(2,1)} %edge_half1.4.after.second_ref.own.refs_2_, bf16[4,8,32,128]{3,2,1,0:T(8,128)(2,1)} %collective-permute-done.14.low_az.refs_3_, ...), custom_call_target="tpu_custom_call" | custom-call | flops 201326592 | bytes 1572864 | tf_op jit(solution)/shard_map/inner_half1/pallas_call | solution.py:159
  82.6 1.7 %collective-permute-done.16.refs_5_ = bf16[3,8,32,128]{3,2,1,0:T(8,128)(2,1)S(1)} collective-permute-done((bf16[3,8,32,128]{3,2,1,0:T(8,128)(2,1)}, bf16[3,8,32,128]{3,2,1,0:T(8,128)(2,1)S(1)}, u32[]{:S(2)}, u32[]{:S(2)}) %collective-permute-start.16) | collective-permute-done | bytes 196640 | tf_op jit(solution)/shard_map/ppermute | solution.py:179
  84.2 0.7 copy-done.8
  84.9 0.7 copy-done.11
  85.6 3.6 %edge_half1.5.after.second_ref.own.refs_2_ = bf16[4,8,32,128]{3,2,1,0:T(8,128)(2,1)} custom-call(s32[8,12]{1,0:T(8,128)} %fusion.30.refs_0_, bf16[4,8,64,768]{3,2,1,0:T(8,128)(2,1)} %bitcast.41, bf16[4,8,32,128]{3,2,1,0:T(8,128)(2,1)} %edge_half1.4.after.second_ref.own.refs_2_, bf16[4,8,32,128]{3,2,1,0:T(8,128)(2,1)} %collective-permute-done.14.low_az.refs_3_, ...), custom_call_target="tpu_custom_call" | custom-call | flops 201326592 | bytes 1572864 | tf_op jit(solution)/shard_map/edge_half1/pallas_call | solution.py:159
  89.2 3.5 %collective-permute-start.23 = (bf16[4,8,32,128]{3,2,1,0:T(8,128)(2,1)}, bf16[4,8,32,128]{3,2,1,0:T(8,128)(2,1)S(1)}, u32[]{:S(2)}, u32[]{:S(2)}) collective-permute-start(bf16[4,8,32,128]{3,2,1,0:T(8,128)(2,1)} %edge_half1.5.after.second_ref.own.refs_2_), channel_id=1, source_target_pairs={{1,0},{2,1},{3,2},{0,3},{5,4},{6,5},{7,6},{4,7},{9,8},{10,9},{11,1... | collective-permute-start | bytes 786440 | tf_op jit(solution)/shard_map/ppermute | solution.py:179
  92.8 1.9 %edges.12 = (bf16[3,8,32,128]{3,2,1,0:T(8,128)(2,1)}, bf16[3,8,32,128]{3,2,1,0:T(8,128)(2,1)}) custom-call(bf16[4,8,32,128]{3,2,1,0:T(8,128)(2,1)} %edge_half0.5.after.own.refs_2_.first_ref, bf16[4,8,32,128]{3,2,1,0:T(8,128)(2,1)} %collective-permute-done.12.low_az.refs_3_, bf16[4,8,32,128]{3,2,1,0:T(8,128)(2,1)} %collective-permute-done.13.high_az.refs_4_, ...), custom_call_target="tpu_custom_call" | custom-call | tf_op jit(solution)/shard_map/edges/pallas_call | solution.py:100
  94.7 2.6 %collective-permute-start.19 = (bf16[3,8,32,128]{3,2,1,0:T(8,128)(2,1)}, bf16[3,8,32,128]{3,2,1,0:T(8,128)(2,1)}, u32[]{:S(2)}, u32[]{:S(2)}) collective-permute-start(bf16[3,8,32,128]{3,2,1,0:T(8,128)(2,1)} %get-tuple-element.44), channel_id=1, source_target_pairs={{4,0},{8,4},{12,8},{16,12},{20,16},{24,20},{28,24},{0,28},{5,1},{9... | collective-permute-start | bytes 589832 | tf_op jit(solution)/shard_map/ppermute | solution.py:179
  97.3 3.4 %inner_half0.6.refs_1_.refs_7_ = bf16[2,8,32,128]{3,2,1,0:T(8,128)(2,1)} custom-call(s32[8,12]{1,0:T(8,128)} %fusion.30.refs_0_, bf16[4,8,64,768]{3,2,1,0:T(8,128)(2,1)} %bitcast.42, bf16[4,8,32,128]{3,2,1,0:T(8,128)(2,1)} %edge_half0.5.after.own.refs_2_.first_ref, bf16[4,8,32,128]{3,2,1,0:T(8,128)(2,1)} %collective-permute-done.12.low_az.refs_3_, ...), custom_call_target="tpu_custom_call" | custom-call | flops 201326592 | bytes 1572864 | tf_op jit(solution)/shard_map/inner_half0/pallas_call | solution.py:159
  100.8 2.5 %unpack.6 = (bf16[4,4,8,64,128]{4,3,2,1,0:T(8,128)(2,1)}, f32[8,128]{1,0:T(8,128)}) custom-call(bf16[4,8,32,128]{3,2,1,0:T(8,128)(2,1)} %edge_half0.5.after.own.refs_2_.first_ref, bf16[4,8,32,128]{3,2,1,0:T(8,128)(2,1)} %edge_half1.5.after.second_ref.own.refs_2_, ...), custom_call_target="tpu_custom_call", output_to_operand_aliasing={{0}: (2, {})} | custom-call | tf_op jit(solution)/shard_map/unpack/pallas_call | solution.py:74
  103.3 3.7 %edge_half0.6.after.own.refs_2_.first_ref = bf16[4,8,32,128]{3,2,1,0:T(8,128)(2,1)} custom-call(s32[8,12]{1,0:T(8,128)} %fusion.30.refs_0_, bf16[4,8,64,768]{3,2,1,0:T(8,128)(2,1)} %bitcast.43, bf16[4,8,32,128]{3,2,1,0:T(8,128)(2,1)} %edge_half0.5.after.own.refs_2_.first_ref, bf16[4,8,32,128]{3,2,1,0:T(8,128)(2,1)} %collective-permute-done.12.low_az.refs_3_, ...), custom_call_target="tpu_custom_call" | custom-call | flops 201326592 | bytes 1572864 | tf_op jit(solution)/shard_map/edge_half0/pallas_call | solution.py:159
  107.0 3.8 %collective-permute-start.21 = (bf16[4,8,32,128]{3,2,1,0:T(8,128)(2,1)}, bf16[4,8,32,128]{3,2,1,0:T(8,128)(2,1)}, u32[]{:S(2)}, u32[]{:S(2)}) collective-permute-start(bf16[4,8,32,128]{3,2,1,0:T(8,128)(2,1)} %edge_half0.6.after.own.refs_2_.first_ref), channel_id=1, source_target_pairs={{1,0},{2,1},{3,2},{0,3},{5,4},{6,5},{7,6},{4,7},{9,8},{10,9},{11,1... | collective-permute-start | bytes 786440 | tf_op jit(solution)/shard_map/ppermute | solution.py:179
  110.8 0.7 copy-done.2
  111.5 1.9 %edges.13 = (bf16[3,8,32,128]{3,2,1,0:T(8,128)(2,1)}, bf16[3,8,32,128]{3,2,1,0:T(8,128)(2,1)}) custom-call(bf16[4,8,32,128]{3,2,1,0:T(8,128)(2,1)} %edge_half1.5.after.second_ref.own.refs_2_, bf16[4,8,32,128]{3,2,1,0:T(8,128)(2,1)} %collective-permute-done.22.low_az.refs_3_, bf16[4,8,32,128]{3,2,1,0:T(8,128)(2,1)} %copy-done.2, ...), custom_call_target="tpu_custom_call" | custom-call | tf_op jit(solution)/shard_map/edges/pallas_call | solution.py:100
  113.4 2.6 %collective-permute-start.25 = (bf16[3,8,32,128]{3,2,1,0:T(8,128)(2,1)}, bf16[3,8,32,128]{3,2,1,0:T(8,128)(2,1)S(1)}, u32[]{:S(2)}, u32[]{:S(2)}) collective-permute-start(bf16[3,8,32,128]{3,2,1,0:T(8,128)(2,1)} %get-tuple-element.48), channel_id=1, source_target_pairs={{4,0},{8,4},{12,8},{16,12},{20,16},{24,20},{28,24},{0,28},{5,1},{9... | collective-permute-start | bytes 589832 | tf_op jit(solution)/shard_map/ppermute | solution.py:179
  116.1 3.4 %inner_half1.6.refs_7_.refs_8_ = bf16[2,8,32,128]{3,2,1,0:T(8,128)(2,1)} custom-call(s32[8,12]{1,0:T(8,128)} %fusion.30.refs_0_, bf16[4,8,64,768]{3,2,1,0:T(8,128)(2,1)} %bitcast.44, bf16[4,8,32,128]{3,2,1,0:T(8,128)(2,1)} %edge_half1.5.after.second_ref.own.refs_2_, bf16[4,8,32,128]{3,2,1,0:T(8,128)(2,1)} %collective-permute-done.22.low_az.refs_3_, ...), custom_call_target="tpu_custom_call" | custom-call | flops 201326592 | bytes 1572864 | tf_op jit(solution)/shard_map/inner_half1/pallas_call | solution.py:159
  119.5 0.4 collective-permute-done.24.refs_5_
  119.9 0.7 copy-done.9
  120.6 0.7 copy-done.12
  121.2 3.6 %edge_half1.6.after.second_ref.own.refs_2_ = bf16[4,8,32,128]{3,2,1,0:T(8,128)(2,1)} custom-call(s32[8,12]{1,0:T(8,128)} %fusion.30.refs_0_, bf16[4,8,64,768]{3,2,1,0:T(8,128)(2,1)} %bitcast.45, bf16[4,8,32,128]{3,2,1,0:T(8,128)(2,1)} %edge_half1.5.after.second_ref.own.refs_2_, bf16[4,8,32,128]{3,2,1,0:T(8,128)(2,1)} %collective-permute-done.22.low_az.refs_3_, ...), custom_call_target="tpu_custom_call" | custom-call | flops 201326592 | bytes 1572864 | tf_op jit(solution)/shard_map/edge_half1/pallas_call | solution.py:159
  124.9 3.6 %collective-permute-start.29 = (bf16[4,8,32,128]{3,2,1,0:T(8,128)(2,1)}, bf16[4,8,32,128]{3,2,1,0:T(8,128)(2,1)S(1)}, u32[]{:S(2)}, u32[]{:S(2)}) collective-permute-start(bf16[4,8,32,128]{3,2,1,0:T(8,128)(2,1)} %edge_half1.6.after.second_ref.own.refs_2_), channel_id=1, source_target_pairs={{1,0},{2,1},{3,2},{0,3},{5,4},{6,5},{7,6},{4,7},{9,8},{10,9},{11,1... | collective-permute-start | bytes 786440 | tf_op jit(solution)/shard_map/ppermute | solution.py:179
  128.5 1.9 %edges.14 = (bf16[3,8,32,128]{3,2,1,0:T(8,128)(2,1)}, bf16[3,8,32,128]{3,2,1,0:T(8,128)(2,1)}) custom-call(bf16[4,8,32,128]{3,2,1,0:T(8,128)(2,1)} %edge_half0.6.after.own.refs_2_.first_ref, bf16[4,8,32,128]{3,2,1,0:T(8,128)(2,1)} %collective-permute-done.20.low_az.refs_3_, bf16[4,8,32,128]{3,2,1,0:T(8,128)(2,1)} %collective-permute-done.21.high_az.refs_4_, ...), custom_call_target="tpu_custom_call" | custom-call | tf_op jit(solution)/shard_map/edges/pallas_call | solution.py:100
  130.3 2.6 %collective-permute-start.27 = (bf16[3,8,32,128]{3,2,1,0:T(8,128)(2,1)}, bf16[3,8,32,128]{3,2,1,0:T(8,128)(2,1)}, u32[]{:S(2)}, u32[]{:S(2)}) collective-permute-start(bf16[3,8,32,128]{3,2,1,0:T(8,128)(2,1)} %get-tuple-element.50), channel_id=1, source_target_pairs={{4,0},{8,4},{12,8},{16,12},{20,16},{24,20},{28,24},{0,28},{5,1},{9... | collective-permute-start | bytes 589832 | tf_op jit(solution)/shard_map/ppermute | solution.py:179
  133.0 3.4 %inner_half0.7.refs_1_.refs_7_ = bf16[2,8,32,128]{3,2,1,0:T(8,128)(2,1)} custom-call(s32[8,12]{1,0:T(8,128)} %fusion.30.refs_0_, bf16[4,8,64,768]{3,2,1,0:T(8,128)(2,1)} %bitcast.46, bf16[4,8,32,128]{3,2,1,0:T(8,128)(2,1)} %edge_half0.6.after.own.refs_2_.first_ref, bf16[4,8,32,128]{3,2,1,0:T(8,128)(2,1)} %collective-permute-done.20.low_az.refs_3_, ...), custom_call_target="tpu_custom_call" | custom-call | flops 201326592 | bytes 1572864 | tf_op jit(solution)/shard_map/inner_half0/pallas_call | solution.py:159
  136.4 2.5 %unpack.7 = (bf16[4,4,8,64,128]{4,3,2,1,0:T(8,128)(2,1)}, f32[8,128]{1,0:T(8,128)}) custom-call(bf16[4,8,32,128]{3,2,1,0:T(8,128)(2,1)} %edge_half0.6.after.own.refs_2_.first_ref, bf16[4,8,32,128]{3,2,1,0:T(8,128)(2,1)} %edge_half1.6.after.second_ref.own.refs_2_, ...), custom_call_target="tpu_custom_call", output_to_operand_aliasing={{0}: (2, {})} | custom-call | tf_op jit(solution)/shard_map/unpack/pallas_call | solution.py:74
  139.0 3.7 %edge_half0.7.after.first_ref = bf16[4,8,32,128]{3,2,1,0:T(8,128)(2,1)} custom-call(s32[8,12]{1,0:T(8,128)} %fusion.30.refs_0_, bf16[4,8,64,768]{3,2,1,0:T(8,128)(2,1)} %bitcast.47, bf16[4,8,32,128]{3,2,1,0:T(8,128)(2,1)} %edge_half0.6.after.own.refs_2_.first_ref, bf16[4,8,32,128]{3,2,1,0:T(8,128)(2,1)} %collective-permute-done.20.low_az.refs_3_, ...), custom_call_target="tpu_custom_call" | custom-call | flops 201326592 | bytes 1572864 | tf_op jit(solution)/shard_map/edge_half0/pallas_call | solution.py:159
  142.6 0.7 copy-done.3
  143.3 1.9 %edges.15 = (bf16[3,8,32,128]{3,2,1,0:T(8,128)(2,1)}, bf16[3,8,32,128]{3,2,1,0:T(8,128)(2,1)}) custom-call(bf16[4,8,32,128]{3,2,1,0:T(8,128)(2,1)} %edge_half1.6.after.second_ref.own.refs_2_, bf16[4,8,32,128]{3,2,1,0:T(8,128)(2,1)} %collective-permute-done.28.low_az.refs_3_, bf16[4,8,32,128]{3,2,1,0:T(8,128)(2,1)} %copy-done.3, ...), custom_call_target="tpu_custom_call" | custom-call | tf_op jit(solution)/shard_map/edges/pallas_call | solution.py:100
  145.2 2.6 %collective-permute-start.31 = (bf16[3,8,32,128]{3,2,1,0:T(8,128)(2,1)}, bf16[3,8,32,128]{3,2,1,0:T(8,128)(2,1)S(1)}, u32[]{:S(2)}, u32[]{:S(2)}) collective-permute-start(bf16[3,8,32,128]{3,2,1,0:T(8,128)(2,1)} %get-tuple-element.54), channel_id=1, source_target_pairs={{4,0},{8,4},{12,8},{16,12},{20,16},{24,20},{28,24},{0,28},{5,1},{9... | collective-permute-start | bytes 589832 | tf_op jit(solution)/shard_map/ppermute | solution.py:179
  147.9 3.4 %inner_half1.7.second_ref.refs_7_ = bf16[2,8,32,128]{3,2,1,0:T(8,128)(2,1)} custom-call(s32[8,12]{1,0:T(8,128)} %fusion.30.refs_0_, bf16[4,8,64,768]{3,2,1,0:T(8,128)(2,1)} %bitcast.48, bf16[4,8,32,128]{3,2,1,0:T(8,128)(2,1)} %edge_half1.6.after.second_ref.own.refs_2_, bf16[4,8,32,128]{3,2,1,0:T(8,128)(2,1)} %collective-permute-done.28.low_az.refs_3_, ...), custom_call_target="tpu_custom_call" | custom-call | flops 201326592 | bytes 1572864 | tf_op jit(solution)/shard_map/inner_half1/pallas_call | solution.py:159
  151.3 2.4 %unpack.8 = (bf16[4,4,8,64,128]{4,3,2,1,0:T(8,128)(2,1)}, f32[8,128]{1,0:T(8,128)}) custom-call(bf16[4,8,32,128]{3,2,1,0:T(8,128)(2,1)} %edge_half0.7.after.first_ref, bf16[2,8,32,128]{3,2,1,0:T(8,128)(2,1)} %inner_half1.7.second_ref.refs_7_, bf16[4,4,8,64,128]{4,3,2,1,0:T(8,128)(2,1)} %get-tuple-element.55.refs_0_), custom_call_target="tpu_custom_call", output_to_operand_aliasing={{0}: (2, {})} | custom-call | tf_op jit(solution)/shard_map/unpack/pallas_call | solution.py:74
  153.7 0.7 copy-done.5
  154.4 3.7 %edge_half1.7.second_ref = bf16[4,8,32,128]{3,2,1,0:T(8,128)(2,1)} custom-call(s32[8,12]{1,0:T(8,128)} %fusion.30.refs_0_, bf16[4,8,64,768]{3,2,1,0:T(8,128)(2,1)} %bitcast.49, bf16[4,8,32,128]{3,2,1,0:T(8,128)(2,1)} %edge_half1.6.after.second_ref.own.refs_2_, bf16[4,8,32,128]{3,2,1,0:T(8,128)(2,1)} %collective-permute-done.28.low_az.refs_3_, ...), custom_call_target="tpu_custom_call" | custom-call | flops 201326592 | bytes 1572864 | tf_op jit(solution)/shard_map/edge_half1/pallas_call | solution.py:159
  158.1 2.4 %unpack.9 = (bf16[4,4,8,64,128]{4,3,2,1,0:T(8,128)(2,1)}, f32[8,128]{1,0:T(8,128)}) custom-call(bf16[4,8,32,128]{3,2,1,0:T(8,128)(2,1)} %edge_half0.7.after.first_ref, bf16[4,8,32,128]{3,2,1,0:T(8,128)(2,1)} %edge_half1.7.second_ref, bf16[4,4,8,64,128]{4,3,2,1,0:T(8,128)(2,1)} %get-tuple-element.57.refs_0_), custom_call_target="tpu_custom_call", output_to_operand_aliasing={{0}: (2, {})} | custom-call | tf_op jit(solution)/shard_map/unpack/pallas_call | solution.py:74
  (66 shorter events, 0.5 us)
Async XLA Ops:
  0.0 11.1 %copy-start = (bf16[4,1,8,64,768]{4,3,2,1,0:T(8,128)(2,1)S(1)}, bf16[4,1,8,64,768]{4,3,2,1,0:T(8,128)(2,1)}, u32[]{:S(2)}) copy-start(bf16[4,1,8,64,768]{4,3,2,1,0:T(8,128)(2,1)} %param.4) | copy-start | bytes 9437188
  2.2 18.9 %collective-permute-start.1 = (bf16[4,8,32,128]{3,2,1,0:T(8,128)(2,1)}, bf16[4,8,32,128]{3,2,1,0:T(8,128)(2,1)}, u32[]{:S(2)}, u32[]{:S(2)}) collective-permute-start(bf16[4,8,32,128]{3,2,1,0:T(8,128)(2,1)} %get-tuple-element.32.own.after.refs_2_), channel_id=1, source_target_pairs={{1,0},{2,1},{3,2},{0,3},{5,4},{6,5},{7,6},{4,7},{9,8},{10,9},{11,1... | collective-permute-start | bytes 786440 | tf_op jit(solution)/shard_map/ppermute | solution.py:179
  7.2 13.9 %collective-permute-start = (bf16[4,8,32,128]{3,2,1,0:T(8,128)(2,1)}, bf16[4,8,32,128]{3,2,1,0:T(8,128)(2,1)}, u32[]{:S(2)}, u32[]{:S(2)}) collective-permute-start(bf16[4,8,32,128]{3,2,1,0:T(8,128)(2,1)} %get-tuple-element.32.own.after.refs_2_), channel_id=1, source_target_pairs={{0,1},{1,2},{2,3},{3,0},{4,5},{5,6},{6,7},{7,4},{8,9},{9,10},{10,1... | collective-permute-start | bytes 786440 | tf_op jit(solution)/shard_map/ppermute | solution.py:179
  7.2 30.0 %collective-permute-start.7 = (bf16[4,8,32,128]{3,2,1,0:T(8,128)(2,1)}, bf16[4,8,32,128]{3,2,1,0:T(8,128)(2,1)S(1)}, u32[]{:S(2)}, u32[]{:S(2)}) collective-permute-start(bf16[4,8,32,128]{3,2,1,0:T(8,128)(2,1)} %get-tuple-element.35.own.refs_2_), channel_id=1, source_target_pairs={{1,0},{2,1},{3,2},{0,3},{5,4},{6,5},{7,6},{4,7},{9,8},{10,9},{11,1... | collective-permute-start | bytes 786440 | tf_op jit(solution)/shard_map/ppermute | solution.py:179
  11.0 26.1 %collective-permute-start.6 = (bf16[4,8,32,128]{3,2,1,0:T(8,128)(2,1)}, bf16[4,8,32,128]{3,2,1,0:T(8,128)(2,1)}, u32[]{:S(2)}, u32[]{:S(2)}) collective-permute-start(bf16[4,8,32,128]{3,2,1,0:T(8,128)(2,1)} %get-tuple-element.35.own.refs_2_), channel_id=1, source_target_pairs={{0,1},{1,2},{2,3},{3,0},{4,5},{5,6},{6,7},{7,4},{8,9},{9,10},{10,1... | collective-permute-start | bytes 786440 | tf_op jit(solution)/shard_map/ppermute | solution.py:179
  16.4 9.2 %copy-start.13 = (s32[1,8,12]{2,1,0:T(8,128)S(1)}, s32[1,8,12]{2,1,0:T(8,128)}, u32[]{:S(2)}) copy-start(s32[1,8,12]{2,1,0:T(8,128)} %param.5) | copy-start | bytes 1156
  23.0 6.7 %collective-permute-start.2 = (bf16[3,8,32,128]{3,2,1,0:T(8,128)(2,1)}, bf16[3,8,32,128]{3,2,1,0:T(8,128)(2,1)}, u32[]{:S(2)}, u32[]{:S(2)}) collective-permute-start(bf16[3,8,32,128]{3,2,1,0:T(8,128)(2,1)} %get-tuple-element.33), channel_id=1, source_target_pairs={{0,4},{4,8},{8,12},{12,16},{16,20},{20,24},{24,28},{28,0},{1,5},{5... | collective-permute-start | bytes 589832 | tf_op jit(solution)/shard_map/ppermute | solution.py:179
  23.0 6.7 %collective-permute-start.3 = (bf16[3,8,32,128]{3,2,1,0:T(8,128)(2,1)}, bf16[3,8,32,128]{3,2,1,0:T(8,128)(2,1)}, u32[]{:S(2)}, u32[]{:S(2)}) collective-permute-start(bf16[3,8,32,128]{3,2,1,0:T(8,128)(2,1)} %get-tuple-element.34), channel_id=1, source_target_pairs={{4,0},{8,4},{12,8},{16,12},{20,16},{24,20},{28,24},{0,28},{5,1},{9... | collective-permute-start | bytes 589832 | tf_op jit(solution)/shard_map/ppermute | solution.py:179
  33.3 22.7 %collective-permute-start.5 = (bf16[4,8,32,128]{3,2,1,0:T(8,128)(2,1)}, bf16[4,8,32,128]{3,2,1,0:T(8,128)(2,1)}, u32[]{:S(2)}, u32[]{:S(2)}) collective-permute-start(bf16[4,8,32,128]{3,2,1,0:T(8,128)(2,1)} %edge_half0.4.after.own.refs_2_.first_ref), channel_id=1, source_target_pairs={{1,0},{2,1},{3,2},{0,3},{5,4},{6,5},{7,6},{4,7},{9,8},{10,9},{11,1... | collective-permute-start | bytes 786440 | tf_op jit(solution)/shard_map/ppermute | solution.py:179
  37.2 18.8 %collective-permute-start.4 = (bf16[4,8,32,128]{3,2,1,0:T(8,128)(2,1)}, bf16[4,8,32,128]{3,2,1,0:T(8,128)(2,1)}, u32[]{:S(2)}, u32[]{:S(2)}) collective-permute-start(bf16[4,8,32,128]{3,2,1,0:T(8,128)(2,1)} %edge_half0.4.after.own.refs_2_.first_ref), channel_id=1, source_target_pairs={{0,1},{1,2},{2,3},{3,0},{4,5},{5,6},{6,7},{7,4},{8,9},{9,10},{10,1... | collective-permute-start | bytes 786440 | tf_op jit(solution)/shard_map/ppermute | solution.py:179
  37.2 0.7 copy-start.1
  39.7 7.4 %collective-permute-start.8 = (bf16[3,8,32,128]{3,2,1,0:T(8,128)(2,1)}, bf16[3,8,32,128]{3,2,1,0:T(8,128)(2,1)S(1)}, u32[]{:S(2)}, u32[]{:S(2)}) collective-permute-start(bf16[3,8,32,128]{3,2,1,0:T(8,128)(2,1)} %get-tuple-element.36), channel_id=1, source_target_pairs={{0,4},{4,8},{8,12},{12,16},{16,20},{20,24},{24,28},{28,0},{1,5},{5... | collective-permute-start | bytes 589832 | tf_op jit(solution)/shard_map/ppermute | solution.py:179
  41.0 6.1 %collective-permute-start.9 = (bf16[3,8,32,128]{3,2,1,0:T(8,128)(2,1)}, bf16[3,8,32,128]{3,2,1,0:T(8,128)(2,1)S(1)}, u32[]{:S(2)}, u32[]{:S(2)}) collective-permute-start(bf16[3,8,32,128]{3,2,1,0:T(8,128)(2,1)} %get-tuple-element.37), channel_id=1, source_target_pairs={{4,0},{8,4},{12,8},{16,12},{20,16},{24,20},{28,24},{0,28},{5,1},{9... | collective-permute-start | bytes 589832 | tf_op jit(solution)/shard_map/ppermute | solution.py:179
  47.1 0.7 copy-start.7
  47.8 0.7 copy-start.10
  52.1 21.8 %collective-permute-start.15 = (bf16[4,8,32,128]{3,2,1,0:T(8,128)(2,1)}, bf16[4,8,32,128]{3,2,1,0:T(8,128)(2,1)S(1)}, u32[]{:S(2)}, u32[]{:S(2)}) collective-permute-start(bf16[4,8,32,128]{3,2,1,0:T(8,128)(2,1)} %edge_half1.4.after.second_ref.own.refs_2_), channel_id=1, source_target_pairs={{1,0},{2,1},{3,2},{0,3},{5,4},{6,5},{7,6},{4,7},{9,8},{10,9},{11,1... | collective-permute-start | bytes 786440 | tf_op jit(solution)/shard_map/ppermute | solution.py:179
  56.0 18.0 %collective-permute-start.14 = (bf16[4,8,32,128]{3,2,1,0:T(8,128)(2,1)}, bf16[4,8,32,128]{3,2,1,0:T(8,128)(2,1)}, u32[]{:S(2)}, u32[]{:S(2)}) collective-permute-start(bf16[4,8,32,128]{3,2,1,0:T(8,128)(2,1)} %edge_half1.4.after.second_ref.own.refs_2_), channel_id=1, source_target_pairs={{0,1},{1,2},{2,3},{3,0},{4,5},{5,6},{6,7},{7,4},{8,9},{9,10},{10,1... | collective-permute-start | bytes 786440 | tf_op jit(solution)/shard_map/ppermute | solution.py:179
  57.8 8.6 %collective-permute-start.10 = (bf16[3,8,32,128]{3,2,1,0:T(8,128)(2,1)}, bf16[3,8,32,128]{3,2,1,0:T(8,128)(2,1)}, u32[]{:S(2)}, u32[]{:S(2)}) collective-permute-start(bf16[3,8,32,128]{3,2,1,0:T(8,128)(2,1)} %get-tuple-element.38), channel_id=1, source_target_pairs={{0,4},{4,8},{8,12},{12,16},{16,20},{20,24},{24,28},{28,0},{1,5},{5... | collective-permute-start | bytes 589832 | tf_op jit(solution)/shard_map/ppermute | solution.py:179
  58.1 8.4 %collective-permute-start.11 = (bf16[3,8,32,128]{3,2,1,0:T(8,128)(2,1)}, bf16[3,8,32,128]{3,2,1,0:T(8,128)(2,1)}, u32[]{:S(2)}, u32[]{:S(2)}) collective-permute-start(bf16[3,8,32,128]{3,2,1,0:T(8,128)(2,1)} %get-tuple-element.39), channel_id=1, source_target_pairs={{4,0},{8,4},{12,8},{16,12},{20,16},{24,20},{28,24},{0,28},{5,1},{9... | collective-permute-start | bytes 589832 | tf_op jit(solution)/shard_map/ppermute | solution.py:179
  70.1 22.7 %collective-permute-start.13 = (bf16[4,8,32,128]{3,2,1,0:T(8,128)(2,1)}, bf16[4,8,32,128]{3,2,1,0:T(8,128)(2,1)}, u32[]{:S(2)}, u32[]{:S(2)}) collective-permute-start(bf16[4,8,32,128]{3,2,1,0:T(8,128)(2,1)} %edge_half0.5.after.own.refs_2_.first_ref), channel_id=1, source_target_pairs={{1,0},{2,1},{3,2},{0,3},{5,4},{6,5},{7,6},{4,7},{9,8},{10,9},{11,1... | collective-permute-start | bytes 786440 | tf_op jit(solution)/shard_map/ppermute | solution.py:179
  73.9 18.9 %collective-permute-start.12 = (bf16[4,8,32,128]{3,2,1,0:T(8,128)(2,1)}, bf16[4,8,32,128]{3,2,1,0:T(8,128)(2,1)}, u32[]{:S(2)}, u32[]{:S(2)}) collective-permute-start(bf16[4,8,32,128]{3,2,1,0:T(8,128)(2,1)} %edge_half0.5.after.own.refs_2_.first_ref), channel_id=1, source_target_pairs={{0,1},{1,2},{2,3},{3,0},{4,5},{5,6},{6,7},{7,4},{8,9},{9,10},{10,1... | collective-permute-start | bytes 786440 | tf_op jit(solution)/shard_map/ppermute | solution.py:179
  73.9 0.7 copy-start.4
  76.5 7.7 %collective-permute-start.16 = (bf16[3,8,32,128]{3,2,1,0:T(8,128)(2,1)}, bf16[3,8,32,128]{3,2,1,0:T(8,128)(2,1)S(1)}, u32[]{:S(2)}, u32[]{:S(2)}) collective-permute-start(bf16[3,8,32,128]{3,2,1,0:T(8,128)(2,1)} %get-tuple-element.41), channel_id=1, source_target_pairs={{0,4},{4,8},{8,12},{12,16},{16,20},{20,24},{24,28},{28,0},{1,5},{5... | collective-permute-start | bytes 589832 | tf_op jit(solution)/shard_map/ppermute | solution.py:179
  76.5 7.7 %collective-permute-start.17 = (bf16[3,8,32,128]{3,2,1,0:T(8,128)(2,1)}, bf16[3,8,32,128]{3,2,1,0:T(8,128)(2,1)S(1)}, u32[]{:S(2)}, u32[]{:S(2)}) collective-permute-start(bf16[3,8,32,128]{3,2,1,0:T(8,128)(2,1)} %get-tuple-element.42), channel_id=1, source_target_pairs={{4,0},{8,4},{12,8},{16,12},{20,16},{24,20},{28,24},{0,28},{5,1},{9... | collective-permute-start | bytes 589832 | tf_op jit(solution)/shard_map/ppermute | solution.py:179
  84.2 0.7 copy-start.8
  84.9 0.7 copy-start.11
  89.2 21.6 %collective-permute-start.23 = (bf16[4,8,32,128]{3,2,1,0:T(8,128)(2,1)}, bf16[4,8,32,128]{3,2,1,0:T(8,128)(2,1)S(1)}, u32[]{:S(2)}, u32[]{:S(2)}) collective-permute-start(bf16[4,8,32,128]{3,2,1,0:T(8,128)(2,1)} %edge_half1.5.after.second_ref.own.refs_2_), channel_id=1, source_target_pairs={{1,0},{2,1},{3,2},{0,3},{5,4},{6,5},{7,6},{4,7},{9,8},{10,9},{11,1... | collective-permute-start | bytes 786440 | tf_op jit(solution)/shard_map/ppermute | solution.py:179
  92.8 18.0 %collective-permute-start.22 = (bf16[4,8,32,128]{3,2,1,0:T(8,128)(2,1)}, bf16[4,8,32,128]{3,2,1,0:T(8,128)(2,1)}, u32[]{:S(2)}, u32[]{:S(2)}) collective-permute-start(bf16[4,8,32,128]{3,2,1,0:T(8,128)(2,1)} %edge_half1.5.after.second_ref.own.refs_2_), channel_id=1, source_target_pairs={{0,1},{1,2},{2,3},{3,0},{4,5},{5,6},{6,7},{7,4},{8,9},{9,10},{10,1... | collective-permute-start | bytes 786440 | tf_op jit(solution)/shard_map/ppermute | solution.py:179
  94.7 8.6 %collective-permute-start.18 = (bf16[3,8,32,128]{3,2,1,0:T(8,128)(2,1)}, bf16[3,8,32,128]{3,2,1,0:T(8,128)(2,1)}, u32[]{:S(2)}, u32[]{:S(2)}) collective-permute-start(bf16[3,8,32,128]{3,2,1,0:T(8,128)(2,1)} %get-tuple-element.43), channel_id=1, source_target_pairs={{0,4},{4,8},{8,12},{12,16},{16,20},{20,24},{24,28},{28,0},{1,5},{5... | collective-permute-start | bytes 589832 | tf_op jit(solution)/shard_map/ppermute | solution.py:179
  94.7 8.6 %collective-permute-start.19 = (bf16[3,8,32,128]{3,2,1,0:T(8,128)(2,1)}, bf16[3,8,32,128]{3,2,1,0:T(8,128)(2,1)}, u32[]{:S(2)}, u32[]{:S(2)}) collective-permute-start(bf16[3,8,32,128]{3,2,1,0:T(8,128)(2,1)} %get-tuple-element.44), channel_id=1, source_target_pairs={{4,0},{8,4},{12,8},{16,12},{20,16},{24,20},{28,24},{0,28},{5,1},{9... | collective-permute-start | bytes 589832 | tf_op jit(solution)/shard_map/ppermute | solution.py:179
  107.0 21.5 %collective-permute-start.21 = (bf16[4,8,32,128]{3,2,1,0:T(8,128)(2,1)}, bf16[4,8,32,128]{3,2,1,0:T(8,128)(2,1)}, u32[]{:S(2)}, u32[]{:S(2)}) collective-permute-start(bf16[4,8,32,128]{3,2,1,0:T(8,128)(2,1)} %edge_half0.6.after.own.refs_2_.first_ref), channel_id=1, source_target_pairs={{1,0},{2,1},{3,2},{0,3},{5,4},{6,5},{7,6},{4,7},{9,8},{10,9},{11,1... | collective-permute-start | bytes 786440 | tf_op jit(solution)/shard_map/ppermute | solution.py:179
  110.8 17.6 %collective-permute-start.20 = (bf16[4,8,32,128]{3,2,1,0:T(8,128)(2,1)}, bf16[4,8,32,128]{3,2,1,0:T(8,128)(2,1)}, u32[]{:S(2)}, u32[]{:S(2)}) collective-permute-start(bf16[4,8,32,128]{3,2,1,0:T(8,128)(2,1)} %edge_half0.6.after.own.refs_2_.first_ref), channel_id=1, source_target_pairs={{0,1},{1,2},{2,3},{3,0},{4,5},{5,6},{6,7},{7,4},{8,9},{9,10},{10,1... | collective-permute-start | bytes 786440 | tf_op jit(solution)/shard_map/ppermute | solution.py:179
  110.8 0.7 copy-start.2
  113.4 6.4 %collective-permute-start.24 = (bf16[3,8,32,128]{3,2,1,0:T(8,128)(2,1)}, bf16[3,8,32,128]{3,2,1,0:T(8,128)(2,1)S(1)}, u32[]{:S(2)}, u32[]{:S(2)}) collective-permute-start(bf16[3,8,32,128]{3,2,1,0:T(8,128)(2,1)} %get-tuple-element.47), channel_id=1, source_target_pairs={{0,4},{4,8},{8,12},{12,16},{16,20},{20,24},{24,28},{28,0},{1,5},{5... | collective-permute-start | bytes 589832 | tf_op jit(solution)/shard_map/ppermute | solution.py:179
  113.4 6.5 %collective-permute-start.25 = (bf16[3,8,32,128]{3,2,1,0:T(8,128)(2,1)}, bf16[3,8,32,128]{3,2,1,0:T(8,128)(2,1)S(1)}, u32[]{:S(2)}, u32[]{:S(2)}) collective-permute-start(bf16[3,8,32,128]{3,2,1,0:T(8,128)(2,1)} %get-tuple-element.48), channel_id=1, source_target_pairs={{4,0},{8,4},{12,8},{16,12},{20,16},{24,20},{28,24},{0,28},{5,1},{9... | collective-permute-start | bytes 589832 | tf_op jit(solution)/shard_map/ppermute | solution.py:179
  119.9 0.7 copy-start.9
  120.6 0.7 copy-start.12
  124.9 17.8 %collective-permute-start.29 = (bf16[4,8,32,128]{3,2,1,0:T(8,128)(2,1)}, bf16[4,8,32,128]{3,2,1,0:T(8,128)(2,1)S(1)}, u32[]{:S(2)}, u32[]{:S(2)}) collective-permute-start(bf16[4,8,32,128]{3,2,1,0:T(8,128)(2,1)} %edge_half1.6.after.second_ref.own.refs_2_), channel_id=1, source_target_pairs={{1,0},{2,1},{3,2},{0,3},{5,4},{6,5},{7,6},{4,7},{9,8},{10,9},{11,1... | collective-permute-start | bytes 786440 | tf_op jit(solution)/shard_map/ppermute | solution.py:179
  128.4 14.2 %collective-permute-start.28 = (bf16[4,8,32,128]{3,2,1,0:T(8,128)(2,1)}, bf16[4,8,32,128]{3,2,1,0:T(8,128)(2,1)}, u32[]{:S(2)}, u32[]{:S(2)}) collective-permute-start(bf16[4,8,32,128]{3,2,1,0:T(8,128)(2,1)} %edge_half1.6.after.second_ref.own.refs_2_), channel_id=1, source_target_pairs={{0,1},{1,2},{2,3},{3,0},{4,5},{5,6},{6,7},{7,4},{8,9},{9,10},{10,1... | collective-permute-start | bytes 786440 | tf_op jit(solution)/shard_map/ppermute | solution.py:179
  130.3 8.6 %collective-permute-start.26 = (bf16[3,8,32,128]{3,2,1,0:T(8,128)(2,1)}, bf16[3,8,32,128]{3,2,1,0:T(8,128)(2,1)}, u32[]{:S(2)}, u32[]{:S(2)}) collective-permute-start(bf16[3,8,32,128]{3,2,1,0:T(8,128)(2,1)} %get-tuple-element.49), channel_id=1, source_target_pairs={{0,4},{4,8},{8,12},{12,16},{16,20},{20,24},{24,28},{28,0},{1,5},{5... | collective-permute-start | bytes 589832 | tf_op jit(solution)/shard_map/ppermute | solution.py:179
  130.3 8.6 %collective-permute-start.27 = (bf16[3,8,32,128]{3,2,1,0:T(8,128)(2,1)}, bf16[3,8,32,128]{3,2,1,0:T(8,128)(2,1)}, u32[]{:S(2)}, u32[]{:S(2)}) collective-permute-start(bf16[3,8,32,128]{3,2,1,0:T(8,128)(2,1)} %get-tuple-element.50), channel_id=1, source_target_pairs={{4,0},{8,4},{12,8},{16,12},{20,16},{24,20},{28,24},{0,28},{5,1},{9... | collective-permute-start | bytes 589832 | tf_op jit(solution)/shard_map/ppermute | solution.py:179
  142.6 0.7 copy-start.3
  145.2 8.4 %collective-permute-start.30 = (bf16[3,8,32,128]{3,2,1,0:T(8,128)(2,1)}, bf16[3,8,32,128]{3,2,1,0:T(8,128)(2,1)S(1)}, u32[]{:S(2)}, u32[]{:S(2)}) collective-permute-start(bf16[3,8,32,128]{3,2,1,0:T(8,128)(2,1)} %get-tuple-element.53), channel_id=1, source_target_pairs={{0,4},{4,8},{8,12},{12,16},{16,20},{20,24},{24,28},{28,0},{1,5},{5... | collective-permute-start | bytes 589832 | tf_op jit(solution)/shard_map/ppermute | solution.py:179
  145.2 8.5 %collective-permute-start.31 = (bf16[3,8,32,128]{3,2,1,0:T(8,128)(2,1)}, bf16[3,8,32,128]{3,2,1,0:T(8,128)(2,1)S(1)}, u32[]{:S(2)}, u32[]{:S(2)}) collective-permute-start(bf16[3,8,32,128]{3,2,1,0:T(8,128)(2,1)} %get-tuple-element.54), channel_id=1, source_target_pairs={{4,0},{8,4},{12,8},{16,12},{20,16},{24,20},{28,24},{0,28},{5,1},{9... | collective-permute-start | bytes 589832 | tf_op jit(solution)/shard_map/ppermute | solution.py:179
  153.7 0.7 copy-start.5
  153.7 0.8 copy-start.6

commit v5 on v4

--- a/solution.py
+++ b/solution.py
@@ -88,28 +88,13 @@
     )(first, second, *extra)
 
 
-def edges_kernel(own, low_az, high_az, after, to_low, to_high):
+def edges(own, low_az, high_az, after):
+    *trio, _ = lax.optimization_barrier((low_az, own, high_az, after))
     columns = own.shape[0]
-    for azim, source in enumerate((low_az, own, high_az)):
-        to_low[azim] = source[0]
-        to_high[azim] = source[columns - 1]
-
-
-def edges(own, low_az, high_az, after):
-    shape = jax.ShapeDtypeStruct((3, *own.shape[1:]), own.dtype)
-    return pl.pallas_call(
-        edges_kernel,
-        in_specs=[VMEM] * 3 + [ANY],
-        out_specs=[VMEM] * 2,
-        out_shape=[shape, shape],
-        name="edges",
-    )(own, low_az, high_az, after)
-
-
-def part_kernel(half, chosen, slots, *refs):
-    window = refs[-1]
-    following = refs[-2]
-    table, blocks, own, low_az, high_az = refs[:5]
+    return jnp.stack([part[0] for part in trio]), jnp.stack([part[columns - 1] for part in trio])
+
+
+def step_kernel(half, table, blocks, own, low_az, high_az, low_st, high_st, after, following, window):
     faces, width, depth = blocks.shape[1:]
     columns = own.shape[0]
     span = columns + 2
@@ -117,58 +102,51 @@
     view = window.reshape(3, span, faces, rows, lanes)
     for azim, source in enumerate((low_az, own, high_az)):
         view[azim, 1 : columns + 1] = source[...]
-    if len(refs) > 7:
-        low_st, high_st, before, after = refs[5:9]
-        view[:, 0] = low_st[...]
-        view[:, span - 1] = high_st[...]
-        following[1 : columns - 1] = before[...]
-
+    view[:, 0] = low_st[...]
+    view[:, span - 1] = high_st[...]
     neighbours = table.shape[1]
     low = low_lanes((rows, lanes))
-    for slot, column in zip(slots, chosen):
+
+    def one(column, face):
+        gathered = jnp.concatenate(
+            [window[table[face, k] + column * faces] for k in range(neighbours)], axis=0
+        )
+        block = blocks[column, face]
+        stacked = jnp.concatenate([block[:, : depth // 2], block[:, depth // 2 :]], axis=0)
+        product = jnp.dot(stacked, gathered, preferred_element_type=jnp.float32)
+        top, bottom = product[:width], product[width:]
+        if half == 0:
+            here = jnp.where(low, top[:rows], bottom[rows:])
+            there = jnp.where(low, top[rows:], bottom[:rows])
+        else:
+            here = jnp.where(low, bottom[rows:], top[:rows])
+            there = jnp.where(low, bottom[:rows], top[rows:])
+        following[column, face] = (here + swap_lanes(there)).astype(jnp.bfloat16)
+
+    def turn(column, carry):
         for face in range(faces):
-            gathered = jnp.concatenate(
-                [window[table[face, k] + column * faces] for k in range(neighbours)], axis=0
-            )
-            block = blocks[column, face]
-            stacked = jnp.concatenate([block[:, : depth // 2], block[:, depth // 2 :]], axis=0)
-            product = jnp.dot(stacked, gathered, preferred_element_type=jnp.float32)
-            top, bottom = product[:width], product[width:]
-            if half == 0:
-                here = jnp.where(low, top[:rows], bottom[rows:])
-                there = jnp.where(low, top[rows:], bottom[:rows])
-            else:
-                here = jnp.where(low, bottom[rows:], top[:rows])
-                there = jnp.where(low, bottom[:rows], top[rows:])
-            following[slot, face] = (here + swap_lanes(there)).astype(jnp.bfloat16)
-
-
-def part(half, chosen, table, blocks, pieces, stream=None, before=None, after=None):
+            one(column, face)
+        return carry
+
+    lax.fori_loop(0, columns, turn, 0)
+
+
+def step(half, table, blocks, pieces, stream, after):
     columns, faces, width, depth = blocks.shape
     rows, lanes = pieces[0].shape[2:]
-    args = [table, blocks, *pieces]
-    in_specs = [pl.BlockSpec(memory_space=pltpu.SMEM)] + [VMEM] * 4
-    size = len(chosen)
-    if stream is None:
-        slots, out_columns = range(size), size
-    else:
-        slots, out_columns = chosen, columns
-        args += [*stream, before, after]
-        in_specs += [VMEM] * 3 + [ANY]
-    name = "inner" if stream is None else "edge"
     return pl.pallas_call(
-        functools.partial(part_kernel, half, chosen, slots),
-        in_specs=in_specs,
+        functools.partial(step_kernel, half),
+        in_specs=[pl.BlockSpec(memory_space=pltpu.SMEM)] + [VMEM] * 6 + [ANY],
         out_specs=VMEM,
-        out_shape=jax.ShapeDtypeStruct((out_columns, faces, rows, lanes), jnp.bfloat16),
+        out_shape=jax.ShapeDtypeStruct((columns, faces, rows, lanes), jnp.bfloat16),
         scratch_shapes=[pltpu.VMEM((3 * (columns + 2) * faces, rows, lanes), jnp.bfloat16)],
         cost_estimate=pl.CostEstimate(
-            flops=2 * size * faces * width * depth * lanes,
-            bytes_accessed=2 * size * faces * width * depth,
+            flops=2 * columns * faces * width * depth * lanes,
+            bytes_accessed=2 * columns * faces * width * depth,
             transcendentals=0,
         ),
-        name=f"{name}_half{half}",
-    )(*args)
+        name=f"step_half{half}",
+    )(table, blocks, *pieces, *stream, after)
 
 
 def shift(value, axis, up):
@@ -196,8 +174,6 @@
     blocks = halves_of_rows(trace_blocks.reshape(columns, faces, width, -1))
     codes = neighbour.reshape(faces, -1)
     table = (((codes // faces) % 3) * (columns + 2) + codes // (3 * faces)) * faces + codes % faces
-    inner = tuple(range(1, columns - 1))
-    outer = (0, columns - 1)
     every = tuple(range(columns))
     current = list(pack(start))
     basis = None
@@ -209,18 +185,13 @@
         ]
         previous = tuple(current)
         for h in range(HALVES):
-            last = index == STEPS - 1 and h == HALVES - 1
             pieces = (current[h], *around_z[h])
             to_low, to_high = edges(*pieces, latest)
             stream = [shift(to_high, "stream", True), shift(to_low, "stream", False)]
-            middle = part(h, inner, table, blocks, pieces)
-            after = middle
-            if h == 0 and index > 0:
-                basis, after = unpack(index - 1, every, *previous, basis, middle)
-            if last:
-                basis, after = unpack(index, inner, current[0], middle, basis, None)
-            current[h] = latest = part(h, outer, table, blocks, pieces, stream, middle, after)
-    basis, _ = unpack(STEPS - 1, outer, *current, basis, None)
+            if h == 1 and index > 0:
+                basis, latest = unpack(index - 1, every, *previous, basis, latest)
+            current[h] = latest = step(h, table, blocks, pieces, stream, latest)
+    basis, _ = unpack(STEPS - 1, every, *current, basis, None)
     return basis.reshape(STEPS, columns, around, faces, width, lanes)
 
 

time: 161 us -> 165 us (1.025)
  waiting for transfers between devices: 3.46 us -> 42.1 us
  Pallas kernels: 86 us -> 49.8 us
  starting transfers between devices: 52.5 us -> 39.9 us
  local copies, waits for them, and re-layouts: 12.3 us -> 21.7 us
  other arithmetic: 0.65 us -> 5.14 us
    ppermute x32, waiting for transfers between devices: 3.46 us -> 42.1 us  [shift(): return lax.ppermute(value, axis, pairs)]
    pallas_call x24 -> x8, Pallas kernels: 71.5 us -> 37.6 us  [step(): pl.pallas_call(functools.partial(step_kernel, half), in_specs=[pl.BlockSp...]
    slice x0 -> x23, local copies, waits for them, and re-layouts: none -> 14.2 us  [edges(): part[0]]
    ppermute x32, starting transfers between devices: 52.5 us -> 39.9 us  [shift(): return lax.ppermute(value, axis, pairs)]
    unnamed x28 -> x36, local copies, waits for them, and re-layouts: 7.61 us -> 2.77 us
    another operation x0 -> x16, other arithmetic: none -> 4.49 us  [the longest x8 2.25 us: edges(): jnp.stack([part[columns - 1] for part in trio])]
    pallas_call x5 -> x4, Pallas kernels: 12.4 us -> 10.1 us  [unpack(): pl.pallas_call(functools.partial(unpack_kernel, index, chosen, skipped),...]
  transfers between devices with their start and end apart: 32 -> 32, of which waited for: 3 -> 16; matrix products, arithmetic and copies ran while one was open for 7% -> 16% of each run, Pallas kernels for 47% -> 25%
where the time goes in v5:
time: 165 us; the launch traced here: 164 us
  Pallas kernels  49.8 us (30%)
  waiting for transfers between devices  42.1 us (26%)
  starting transfers between devices  39.9 us (24%)
  local copies, waits for them, and re-layouts  21.7 us (13%)
  matrix products  5.3 us (3%)
  other arithmetic  5.14 us (3%)
    ppermute x32, waiting for transfers between devices, shift(): return lax.ppermute(value, axis, pairs)  42.1 us
    ppermute x32, starting transfers between devices, shift(): return lax.ppermute(value, axis, pairs)  39.9 us
    pallas_call x8, Pallas kernels, step(): pl.pallas_call(functools.partial(step_kernel, half), in_specs=[pl.BlockSp...  37.6 us
    slice x23, local copies, waits for them, and re-layouts, edges(): part[0]  14.2 us
    pallas_call x4, Pallas kernels, unpack(): pl.pallas_call(functools.partial(unpack_kernel, index, chosen, skipped),...  10.1 us
    dot_general x1, matrix products, halves_of_rows(): jnp.dot(blocks.reshape(-1, depth), mover, preferred_element_type=jnp.floa...  5.3 us
    convert_element_type x1, local copies, waits for them, and re-layouts, halves_of_rows(): return moved.astype(jnp.bfloat16).reshape(blocks.shape)  4.73 us
  transfers between devices with their start and end apart: 32, of which 16 were waited for; matrix products, arithmetic and copies ran while one was open for 16% of the time, Pallas kernels for 25%

profile of v5, /device:TPU:0, one launch (start us, length us, event | category | flops | bytes accessed | tf_op | source)
XLA Modules:
  0.0 164.4 jit_solution(17435916192445160752)
XLA Ops:
  0.0 2.1 %pack.1 = (bf16[4,8,32,128]{3,2,1,0:T(8,128)(2,1)}, bf16[4,8,32,128]{3,2,1,0:T(8,128)(2,1)}) custom-call(bf16[4,8,64,128]{3,2,1,0:T(8,128)(2,1)} %bitcast.42), custom_call_target="tpu_custom_call" | custom-call | tf_op jit(solution)/shard_map/pack/pallas_call | solution.py:39
  2.1 3.0 %collective-permute-start = (bf16[4,8,32,128]{3,2,1,0:T(8,128)(2,1)}, bf16[4,8,32,128]{3,2,1,0:T(8,128)(2,1)}, u32[]{:S(2)}, u32[]{:S(2)}) collective-permute-start(bf16[4,8,32,128]{3,2,1,0:T(8,128)(2,1)} %get-tuple-element.40.own.after), channel_id=1, source_target_pairs={{0,1},{1,2},{2,3},{3,0},{4,5},{5,6},{6,7},{7,4},{8,9},{9,10},{10,1... | collective-permute-start | bytes 786440 | tf_op jit(solution)/shard_map/ppermute | solution.py:157
  5.2 2.0 %collective-permute-start.1 = (bf16[4,8,32,128]{3,2,1,0:T(8,128)(2,1)}, bf16[4,8,32,128]{3,2,1,0:T(8,128)(2,1)}, u32[]{:S(2)}, u32[]{:S(2)}) collective-permute-start(bf16[4,8,32,128]{3,2,1,0:T(8,128)(2,1)} %get-tuple-element.40.own.after), channel_id=1, source_target_pairs={{1,0},{2,1},{3,2},{0,3},{5,4},{6,5},{7,6},{4,7},{9,8},{10,9},{11,1... | collective-permute-start | bytes 786440 | tf_op jit(solution)/shard_map/ppermute | solution.py:157
  7.2 3.8 %collective-permute-start.7 = (bf16[4,8,32,128]{3,2,1,0:T(8,128)(2,1)}, bf16[4,8,32,128]{3,2,1,0:T(8,128)(2,1)}, u32[]{:S(2)}, u32[]{:S(2)}) collective-permute-start(bf16[4,8,32,128]{3,2,1,0:T(8,128)(2,1)} %get-tuple-element.44.own), channel_id=1, source_target_pairs={{1,0},{2,1},{3,2},{0,3},{5,4},{6,5},{7,6},{4,7},{9,8},{10,9},{11,1... | collective-permute-start | bytes 786440 | tf_op jit(solution)/shard_map/ppermute | solution.py:157
  11.1 5.3 %fusion = bf16[2048,768]{0,1:T(8,128)(2,1)} fusion(bf16[2048,768]{1,0:T(8,128)(2,1)S(1)} %bitcast.33, s32[768]{0:T(1024)S(1)} %get-tuple-element.121, s32[768]{0:T(1024)S(1)} %get-tuple-element.127, s32[768]{0:T(1024)S(1)} %get-tuple-element.122, s32[768]{0:T(1024)S(1)} %get-tuple-element.124, s32[768]{0:T(1024)S(1)} %get-tuple-element.123, ...), kind=kOutput, calls=%fused_computation.6 | convolution fusion | flops 2429288448 | bytes 6312192 | tf_op jit(solution)/shard_map/dot_general | solution.py:167
  16.4 4.7 %copy.7 = bf16[2048,768]{1,0:T(8,128)(2,1)} copy(bf16[2048,768]{0,1:T(8,128)(2,1)} %fusion) | data formatting | bytes 6291456 | tf_op jit(solution)/shard_map/convert_element_type | solution.py:168
  21.1 0.9 fusion.65
  22.0 0.9 fusion.63
  22.9 1.1 collective-permute-start.3
  24.8 4.4 %collective-permute-done.3.high_st = bf16[3,8,32,128]{3,2,1,0:T(8,128)(2,1)S(1)} collective-permute-done((bf16[3,8,32,128]{3,2,1,0:T(8,128)(2,1)S(1)}, bf16[3,8,32,128]{3,2,1,0:T(8,128)(2,1)S(1)}, u32[]{:S(2)}, u32[]{:S(2)}) %collective-permute-start.3) | collective-permute-done | bytes 196640 | tf_op jit(solution)/shard_map/ppermute | solution.py:157
  29.1 2.3 %collective-permute-done.2.low_st = bf16[3,8,32,128]{3,2,1,0:T(8,128)(2,1)S(1)} collective-permute-done((bf16[3,8,32,128]{3,2,1,0:T(8,128)(2,1)S(1)}, bf16[3,8,32,128]{3,2,1,0:T(8,128)(2,1)S(1)}, u32[]{:S(2)}, u32[]{:S(2)}) %collective-permute-start.2) | collective-permute-done | bytes 196640 | tf_op jit(solution)/shard_map/ppermute | solution.py:157
  32.1 4.7 %step_half0.4.after.own.first_ref = bf16[4,8,32,128]{3,2,1,0:T(8,128)(2,1)} custom-call(s32[8,12]{1,0:T(8,128)} %fusion.30.table, bf16[4,8,64,768]{3,2,1,0:T(8,128)(2,1)} %bitcast.34, bf16[4,8,32,128]{3,2,1,0:T(8,128)(2,1)} %get-tuple-element.40.own.after, bf16[4,8,32,128]{3,2,1,0:T(8,128)(2,1)} %collective-permute-done.low_az, ...), custom_call_target="tpu_custom_call" | custom-call | flops 402653184 | bytes 3145728 | tf_op jit(solution)/shard_map/step_half0/pallas_call | solution.py:137
  36.8 3.8 %collective-permute-start.5 = (bf16[4,8,32,128]{3,2,1,0:T(8,128)(2,1)}, bf16[4,8,32,128]{3,2,1,0:T(8,128)(2,1)}, u32[]{:S(2)}, u32[]{:S(2)}) collective-permute-start(bf16[4,8,32,128]{3,2,1,0:T(8,128)(2,1)} %step_half0.4.after.own.first_ref), channel_id=1, source_target_pairs={{1,0},{2,1},{3,2},{0,3},{5,4},{6,5},{7,6},{4,7},{9,8},{10,9},{11,1... | collective-permute-start | bytes 786440 | tf_op jit(solution)/shard_map/ppermute | solution.py:157
  40.6 0.9 fusion.60
  41.6 0.9 fusion.62
  43.3 4.5 %collective-permute-done.9.high_st = bf16[3,8,32,128]{3,2,1,0:T(8,128)(2,1)} collective-permute-done((bf16[3,8,32,128]{3,2,1,0:T(8,128)(2,1)S(1)}, bf16[3,8,32,128]{3,2,1,0:T(8,128)(2,1)}, u32[]{:S(2)}, u32[]{:S(2)}) %collective-permute-start.9) | collective-permute-done | bytes 196640 | tf_op jit(solution)/shard_map/ppermute | solution.py:157
  47.8 1.8 %collective-permute-done.8.low_st = bf16[3,8,32,128]{3,2,1,0:T(8,128)(2,1)} collective-permute-done((bf16[3,8,32,128]{3,2,1,0:T(8,128)(2,1)S(1)}, bf16[3,8,32,128]{3,2,1,0:T(8,128)(2,1)}, u32[]{:S(2)}, u32[]{:S(2)}) %collective-permute-start.8) | collective-permute-done | bytes 196640 | tf_op jit(solution)/shard_map/ppermute | solution.py:157
  49.6 4.7 %step_half1.4.after.second_ref.own = bf16[4,8,32,128]{3,2,1,0:T(8,128)(2,1)} custom-call(s32[8,12]{1,0:T(8,128)} %fusion.30.table, bf16[4,8,64,768]{3,2,1,0:T(8,128)(2,1)} %bitcast.35, bf16[4,8,32,128]{3,2,1,0:T(8,128)(2,1)} %get-tuple-element.44.own, bf16[4,8,32,128]{3,2,1,0:T(8,128)(2,1)} %collective-permute-done.6.low_az, ...), custom_call_target="tpu_custom_call" | custom-call | flops 402653184 | bytes 3145728 | tf_op jit(solution)/shard_map/step_half1/pallas_call | solution.py:137
  54.3 3.8 %collective-permute-start.15 = (bf16[4,8,32,128]{3,2,1,0:T(8,128)(2,1)}, bf16[4,8,32,128]{3,2,1,0:T(8,128)(2,1)}, u32[]{:S(2)}, u32[]{:S(2)}) collective-permute-start(bf16[4,8,32,128]{3,2,1,0:T(8,128)(2,1)} %step_half1.4.after.second_ref.own), channel_id=1, source_target_pairs={{1,0},{2,1},{3,2},{0,3},{5,4},{6,5},{7,6},{4,7},{9,8},{10,9},{11,1... | collective-permute-start | bytes 786440 | tf_op jit(solution)/shard_map/ppermute | solution.py:157
  58.1 0.9 fusion.57
  59.0 0.9 fusion.59
  60.6 4.6 %collective-permute-done.11.high_st = bf16[3,8,32,128]{3,2,1,0:T(8,128)(2,1)} collective-permute-done((bf16[3,8,32,128]{3,2,1,0:T(8,128)(2,1)S(1)}, bf16[3,8,32,128]{3,2,1,0:T(8,128)(2,1)}, u32[]{:S(2)}, u32[]{:S(2)}) %collective-permute-start.11) | collective-permute-done | bytes 196640 | tf_op jit(solution)/shard_map/ppermute | solution.py:157
  65.2 1.5 collective-permute-done.10.low_st
  66.7 4.7 %step_half0.5.refs_0_.own.first_ref = bf16[4,8,32,128]{3,2,1,0:T(8,128)(2,1)} custom-call(s32[8,12]{1,0:T(8,128)} %fusion.30.table, bf16[4,8,64,768]{3,2,1,0:T(8,128)(2,1)} %bitcast.36, bf16[4,8,32,128]{3,2,1,0:T(8,128)(2,1)} %step_half0.4.after.own.first_ref, bf16[4,8,32,128]{3,2,1,0:T(8,128)(2,1)} %collective-permute-done.4.low_az, ...), custom_call_target="tpu_custom_call" | custom-call | flops 402653184 | bytes 3145728 | tf_op jit(solution)/shard_map/step_half0/pallas_call | solution.py:137
  71.4 3.8 %collective-permute-start.13 = (bf16[4,8,32,128]{3,2,1,0:T(8,128)(2,1)}, bf16[4,8,32,128]{3,2,1,0:T(8,128)(2,1)}, u32[]{:S(2)}, u32[]{:S(2)}) collective-permute-start(bf16[4,8,32,128]{3,2,1,0:T(8,128)(2,1)} %step_half0.5.refs_0_.own.first_ref), channel_id=1, source_target_pairs={{1,0},{2,1},{3,2},{0,3},{5,4},{6,5},{7,6},{4,7},{9,8},{10,9},{11,1... | collective-permute-start | bytes 786440 | tf_op jit(solution)/shard_map/ppermute | solution.py:157
  75.2 0.9 fusion.54
  76.2 0.9 fusion.56
  77.7 0.8 collective-permute-start.17
  78.6 0.7 pad_maximum_fusion.6
  79.3 2.5 %unpack.4 = (bf16[4,4,8,64,128]{4,3,2,1,0:T(8,128)(2,1)}, f32[8,128]{1,0:T(8,128)}) custom-call(bf16[4,8,32,128]{3,2,1,0:T(8,128)(2,1)} %step_half0.4.after.own.first_ref, bf16[4,8,32,128]{3,2,1,0:T(8,128)(2,1)} %step_half1.4.after.second_ref.own, bf16[4,8,32,128]{3,2,1,0:T(8,128)(2,1)} %step_half0.5.refs_0_.own.first_ref), custom_call_target="tpu_custom_call" | custom-call | tf_op jit(solution)/shard_map/unpack/pallas_call | solution.py:74
  81.8 2.2 %collective-permute-done.17.high_st = bf16[3,8,32,128]{3,2,1,0:T(8,128)(2,1)S(1)} collective-permute-done((bf16[3,8,32,128]{3,2,1,0:T(8,128)(2,1)}, bf16[3,8,32,128]{3,2,1,0:T(8,128)(2,1)S(1)}, u32[]{:S(2)}, u32[]{:S(2)}) %collective-permute-start.17) | collective-permute-done | bytes 196640 | tf_op jit(solution)/shard_map/ppermute | solution.py:157
  84.0 1.5 collective-permute-done.16.low_st
  86.2 4.7 %step_half1.5.after.second_ref.own = bf16[4,8,32,128]{3,2,1,0:T(8,128)(2,1)} custom-call(s32[8,12]{1,0:T(8,128)} %fusion.30.table, bf16[4,8,64,768]{3,2,1,0:T(8,128)(2,1)} %bitcast.37, bf16[4,8,32,128]{3,2,1,0:T(8,128)(2,1)} %step_half1.4.after.second_ref.own, bf16[4,8,32,128]{3,2,1,0:T(8,128)(2,1)} %collective-permute-done.14.low_az, ...), custom_call_target="tpu_custom_call" | custom-call | flops 402653184 | bytes 3145728 | tf_op jit(solution)/shard_map/step_half1/pallas_call | solution.py:137
  90.9 3.8 %collective-permute-start.23 = (bf16[4,8,32,128]{3,2,1,0:T(8,128)(2,1)}, bf16[4,8,32,128]{3,2,1,0:T(8,128)(2,1)}, u32[]{:S(2)}, u32[]{:S(2)}) collective-permute-start(bf16[4,8,32,128]{3,2,1,0:T(8,128)(2,1)} %step_half1.5.after.second_ref.own), channel_id=1, source_target_pairs={{1,0},{2,1},{3,2},{0,3},{5,4},{6,5},{7,6},{4,7},{9,8},{10,9},{11,1... | collective-permute-start | bytes 786440 | tf_op jit(solution)/shard_map/ppermute | solution.py:157
  94.7 0.9 fusion.51
  95.6 0.9 fusion.53
  96.6 1.4 collective-permute-start.19
  98.0 4.1 %collective-permute-done.19.high_st = bf16[3,8,32,128]{3,2,1,0:T(8,128)(2,1)} collective-permute-done((bf16[3,8,32,128]{3,2,1,0:T(8,128)(2,1)S(1)}, bf16[3,8,32,128]{3,2,1,0:T(8,128)(2,1)}, u32[]{:S(2)}, u32[]{:S(2)}) %collective-permute-start.19) | collective-permute-done | bytes 196640 | tf_op jit(solution)/shard_map/ppermute | solution.py:157
  102.1 2.0 %collective-permute-done.18.low_st = bf16[3,8,32,128]{3,2,1,0:T(8,128)(2,1)} collective-permute-done((bf16[3,8,32,128]{3,2,1,0:T(8,128)(2,1)S(1)}, bf16[3,8,32,128]{3,2,1,0:T(8,128)(2,1)}, u32[]{:S(2)}, u32[]{:S(2)}) %collective-permute-start.18) | collective-permute-done | bytes 196640 | tf_op jit(solution)/shard_map/ppermute | solution.py:157
  104.1 4.7 %step_half0.6.refs_1_.own.first_ref = bf16[4,8,32,128]{3,2,1,0:T(8,128)(2,1)} custom-call(s32[8,12]{1,0:T(8,128)} %fusion.30.table, bf16[4,8,64,768]{3,2,1,0:T(8,128)(2,1)} %bitcast.38, bf16[4,8,32,128]{3,2,1,0:T(8,128)(2,1)} %step_half0.5.refs_0_.own.first_ref, bf16[4,8,32,128]{3,2,1,0:T(8,128)(2,1)} %collective-permute-done.12.low_az, ...), custom_call_target="tpu_custom_call" | custom-call | flops 402653184 | bytes 3145728 | tf_op jit(solution)/shard_map/step_half0/pallas_call | solution.py:137
  108.8 3.8 %collective-permute-start.21 = (bf16[4,8,32,128]{3,2,1,0:T(8,128)(2,1)}, bf16[4,8,32,128]{3,2,1,0:T(8,128)(2,1)}, u32[]{:S(2)}, u32[]{:S(2)}) collective-permute-start(bf16[4,8,32,128]{3,2,1,0:T(8,128)(2,1)} %step_half0.6.refs_1_.own.first_ref), channel_id=1, source_target_pairs={{1,0},{2,1},{3,2},{0,3},{5,4},{6,5},{7,6},{4,7},{9,8},{10,9},{11,1... | collective-permute-start | bytes 786440 | tf_op jit(solution)/shard_map/ppermute | solution.py:157
  112.6 0.9 fusion.48
  113.5 0.9 fusion.50
  114.4 0.7 pad_maximum_fusion.11
  116.3 2.5 %unpack.5 = (bf16[4,4,8,64,128]{4,3,2,1,0:T(8,128)(2,1)}, f32[8,128]{1,0:T(8,128)}) custom-call(bf16[4,8,32,128]{3,2,1,0:T(8,128)(2,1)} %step_half0.5.refs_0_.own.first_ref, bf16[4,8,32,128]{3,2,1,0:T(8,128)(2,1)} %step_half1.5.after.second_ref.own, bf16[4,4,8,64,128]{4,3,2,1,0:T(8,128)(2,1)} %get-tuple-element.59.refs_0_, ...), custom_call_target="tpu_custom_call", output_to_operand_aliasing={{0}: (2, {})} | custom-call | tf_op jit(solution)/shard_map/unpack/pallas_call | solution.py:74
  118.9 2.1 %collective-permute-done.25.high_st = bf16[3,8,32,128]{3,2,1,0:T(8,128)(2,1)S(1)} collective-permute-done((bf16[3,8,32,128]{3,2,1,0:T(8,128)(2,1)}, bf16[3,8,32,128]{3,2,1,0:T(8,128)(2,1)S(1)}, u32[]{:S(2)}, u32[]{:S(2)}) %collective-permute-start.25) | collective-permute-done | bytes 196640 | tf_op jit(solution)/shard_map/ppermute | solution.py:157
  121.0 1.4 collective-permute-done.24.low_st
  123.1 4.7 %step_half1.6.after.second_ref.own = bf16[4,8,32,128]{3,2,1,0:T(8,128)(2,1)} custom-call(s32[8,12]{1,0:T(8,128)} %fusion.30.table, bf16[4,8,64,768]{3,2,1,0:T(8,128)(2,1)} %bitcast.39, bf16[4,8,32,128]{3,2,1,0:T(8,128)(2,1)} %step_half1.5.after.second_ref.own, bf16[4,8,32,128]{3,2,1,0:T(8,128)(2,1)} %collective-permute-done.22.low_az, ...), custom_call_target="tpu_custom_call" | custom-call | flops 402653184 | bytes 3145728 | tf_op jit(solution)/shard_map/step_half1/pallas_call | solution.py:137
  127.8 3.8 %collective-permute-start.29 = (bf16[4,8,32,128]{3,2,1,0:T(8,128)(2,1)}, bf16[4,8,32,128]{3,2,1,0:T(8,128)(2,1)}, u32[]{:S(2)}, u32[]{:S(2)}) collective-permute-start(bf16[4,8,32,128]{3,2,1,0:T(8,128)(2,1)} %step_half1.6.after.second_ref.own), channel_id=1, source_target_pairs={{1,0},{2,1},{3,2},{0,3},{5,4},{6,5},{7,6},{4,7},{9,8},{10,9},{11,1... | collective-permute-start | bytes 786440 | tf_op jit(solution)/shard_map/ppermute | solution.py:157
  131.7 0.9 fusion.45
  132.6 0.9 fusion.47
  133.5 1.4 collective-permute-start.27
  135.0 4.4 %collective-permute-done.27.high_st = bf16[3,8,32,128]{3,2,1,0:T(8,128)(2,1)} collective-permute-done((bf16[3,8,32,128]{3,2,1,0:T(8,128)(2,1)S(1)}, bf16[3,8,32,128]{3,2,1,0:T(8,128)(2,1)}, u32[]{:S(2)}, u32[]{:S(2)}) %collective-permute-start.27) | collective-permute-done | bytes 196640 | tf_op jit(solution)/shard_map/ppermute | solution.py:157
  139.5 1.7 %collective-permute-done.26.low_st = bf16[3,8,32,128]{3,2,1,0:T(8,128)(2,1)} collective-permute-done((bf16[3,8,32,128]{3,2,1,0:T(8,128)(2,1)S(1)}, bf16[3,8,32,128]{3,2,1,0:T(8,128)(2,1)}, u32[]{:S(2)}, u32[]{:S(2)}) %collective-permute-start.26) | collective-permute-done | bytes 196640 | tf_op jit(solution)/shard_map/ppermute | solution.py:157
  141.1 4.7 %step_half0.7.refs_1_.first_ref = bf16[4,8,32,128]{3,2,1,0:T(8,128)(2,1)} custom-call(s32[8,12]{1,0:T(8,128)} %fusion.30.table, bf16[4,8,64,768]{3,2,1,0:T(8,128)(2,1)} %bitcast.40, bf16[4,8,32,128]{3,2,1,0:T(8,128)(2,1)} %step_half0.6.refs_1_.own.first_ref, bf16[4,8,32,128]{3,2,1,0:T(8,128)(2,1)} %collective-permute-done.20.low_az, ...), custom_call_target="tpu_custom_call" | custom-call | flops 402653184 | bytes 3145728 | tf_op jit(solution)/shard_map/step_half0/pallas_call | solution.py:137
  145.8 0.9 fusion.42
  146.7 0.9 fusion.44
  148.3 1.3 collective-permute-start.31
  149.6 0.7 pad_maximum_fusion.14
  150.3 2.5 %unpack.6 = (bf16[4,4,8,64,128]{4,3,2,1,0:T(8,128)(2,1)}, f32[8,128]{1,0:T(8,128)}) custom-call(bf16[4,8,32,128]{3,2,1,0:T(8,128)(2,1)} %step_half0.6.refs_1_.own.first_ref, bf16[4,8,32,128]{3,2,1,0:T(8,128)(2,1)} %step_half1.6.after.second_ref.own, bf16[4,4,8,64,128]{4,3,2,1,0:T(8,128)(2,1)} %get-tuple-element.67.refs_0_, ...), custom_call_target="tpu_custom_call", output_to_operand_aliasing={{0}: (2, {})} | custom-call | tf_op jit(solution)/shard_map/unpack/pallas_call | solution.py:74
  152.8 1.6 %collective-permute-done.31.high_st = bf16[3,8,32,128]{3,2,1,0:T(8,128)(2,1)S(1)} collective-permute-done((bf16[3,8,32,128]{3,2,1,0:T(8,128)(2,1)}, bf16[3,8,32,128]{3,2,1,0:T(8,128)(2,1)S(1)}, u32[]{:S(2)}, u32[]{:S(2)}) %collective-permute-start.31) | collective-permute-done | bytes 196640 | tf_op jit(solution)/shard_map/ppermute | solution.py:157
  154.5 2.0 %collective-permute-done.30.low_st = bf16[3,8,32,128]{3,2,1,0:T(8,128)(2,1)S(1)} collective-permute-done((bf16[3,8,32,128]{3,2,1,0:T(8,128)(2,1)}, bf16[3,8,32,128]{3,2,1,0:T(8,128)(2,1)S(1)}, u32[]{:S(2)}, u32[]{:S(2)}) %collective-permute-start.30) | collective-permute-done | bytes 196640 | tf_op jit(solution)/shard_map/ppermute | solution.py:157
  157.2 4.7 %step_half1.7.second_ref = bf16[4,8,32,128]{3,2,1,0:T(8,128)(2,1)} custom-call(s32[8,12]{1,0:T(8,128)} %fusion.30.table, bf16[4,8,64,768]{3,2,1,0:T(8,128)(2,1)} %bitcast.41, bf16[4,8,32,128]{3,2,1,0:T(8,128)(2,1)} %step_half1.6.after.second_ref.own, bf16[4,8,32,128]{3,2,1,0:T(8,128)(2,1)} %collective-permute-done.28.low_az, ...), custom_call_target="tpu_custom_call" | custom-call | flops 402653184 | bytes 3145728 | tf_op jit(solution)/shard_map/step_half1/pallas_call | solution.py:137
  161.9 2.5 %unpack.7 = (bf16[4,4,8,64,128]{4,3,2,1,0:T(8,128)(2,1)}, f32[8,128]{1,0:T(8,128)}) custom-call(bf16[4,8,32,128]{3,2,1,0:T(8,128)(2,1)} %step_half0.7.refs_1_.first_ref, bf16[4,8,32,128]{3,2,1,0:T(8,128)(2,1)} %step_half1.7.second_ref, bf16[4,4,8,64,128]{4,3,2,1,0:T(8,128)(2,1)} %get-tuple-element.69.refs_0_), custom_call_target="tpu_custom_call", output_to_operand_aliasing={{0}: (2, {})} | custom-call | tf_op jit(solution)/shard_map/unpack/pallas_call | solution.py:74
  (96 shorter events, 8.0 us)
Async XLA Ops:
  0.0 11.1 %copy-start = (bf16[4,1,8,64,768]{4,3,2,1,0:T(8,128)(2,1)S(1)}, bf16[4,1,8,64,768]{4,3,2,1,0:T(8,128)(2,1)}, u32[]{:S(2)}) copy-start(bf16[4,1,8,64,768]{4,3,2,1,0:T(8,128)(2,1)} %param.4) | copy-start | bytes 9437188
  2.1 19.0 %collective-permute-start = (bf16[4,8,32,128]{3,2,1,0:T(8,128)(2,1)}, bf16[4,8,32,128]{3,2,1,0:T(8,128)(2,1)}, u32[]{:S(2)}, u32[]{:S(2)}) collective-permute-start(bf16[4,8,32,128]{3,2,1,0:T(8,128)(2,1)} %get-tuple-element.40.own.after), channel_id=1, source_target_pairs={{0,1},{1,2},{2,3},{3,0},{4,5},{5,6},{6,7},{7,4},{8,9},{9,10},{10,1... | collective-permute-start | bytes 786440 | tf_op jit(solution)/shard_map/ppermute | solution.py:157
  5.2 15.9 %collective-permute-start.1 = (bf16[4,8,32,128]{3,2,1,0:T(8,128)(2,1)}, bf16[4,8,32,128]{3,2,1,0:T(8,128)(2,1)}, u32[]{:S(2)}, u32[]{:S(2)}) collective-permute-start(bf16[4,8,32,128]{3,2,1,0:T(8,128)(2,1)} %get-tuple-element.40.own.after), channel_id=1, source_target_pairs={{1,0},{2,1},{3,2},{0,3},{5,4},{6,5},{7,6},{4,7},{9,8},{10,9},{11,1... | collective-permute-start | bytes 786440 | tf_op jit(solution)/shard_map/ppermute | solution.py:157
  7.2 33.4 %collective-permute-start.6 = (bf16[4,8,32,128]{3,2,1,0:T(8,128)(2,1)}, bf16[4,8,32,128]{3,2,1,0:T(8,128)(2,1)}, u32[]{:S(2)}, u32[]{:S(2)}) collective-permute-start(bf16[4,8,32,128]{3,2,1,0:T(8,128)(2,1)} %get-tuple-element.44.own), channel_id=1, source_target_pairs={{0,1},{1,2},{2,3},{3,0},{4,5},{5,6},{6,7},{7,4},{8,9},{9,10},{10,1... | collective-permute-start | bytes 786440 | tf_op jit(solution)/shard_map/ppermute | solution.py:157
  7.2 33.4 %collective-permute-start.7 = (bf16[4,8,32,128]{3,2,1,0:T(8,128)(2,1)}, bf16[4,8,32,128]{3,2,1,0:T(8,128)(2,1)}, u32[]{:S(2)}, u32[]{:S(2)}) collective-permute-start(bf16[4,8,32,128]{3,2,1,0:T(8,128)(2,1)} %get-tuple-element.44.own), channel_id=1, source_target_pairs={{1,0},{2,1},{3,2},{0,3},{5,4},{6,5},{7,6},{4,7},{9,8},{10,9},{11,1... | collective-permute-start | bytes 786440 | tf_op jit(solution)/shard_map/ppermute | solution.py:157
  16.4 5.6 %copy-start.7 = (bf16[4,8,32,128]{3,2,1,0:T(8,128)(2,1)S(1)}, bf16[4,8,32,128]{3,2,1,0:T(8,128)(2,1)}, u32[]{:S(2)}) copy-start(bf16[4,8,32,128]{3,2,1,0:T(8,128)(2,1)} %get-tuple-element.40.own.after) | copy-start | bytes 786436
  16.4 7.8 %copy-start.17 = (s32[1,8,12]{2,1,0:T(8,128)S(1)}, s32[1,8,12]{2,1,0:T(8,128)}, u32[]{:S(2)}) copy-start(s32[1,8,12]{2,1,0:T(8,128)} %param.5) | copy-start | bytes 1156
  22.9 6.2 %collective-permute-start.3 = (bf16[3,8,32,128]{3,2,1,0:T(8,128)(2,1)S(1)}, bf16[3,8,32,128]{3,2,1,0:T(8,128)(2,1)S(1)}, u32[]{:S(2)}, u32[]{:S(2)}) collective-permute-start(bf16[3,8,32,128]{3,2,1,0:T(8,128)(2,1)S(1)} %pad_maximum_fusion.1), channel_id=1, source_target_pairs={{4,0},{8,4},{12,8},{16,12},{20,16},{24,20},{28,24},{0,28},{5,1},{9... | collective-permute-start | bytes 589832 | tf_op jit(solution)/shard_map/ppermute | solution.py:157
  24.1 7.3 %collective-permute-start.2 = (bf16[3,8,32,128]{3,2,1,0:T(8,128)(2,1)S(1)}, bf16[3,8,32,128]{3,2,1,0:T(8,128)(2,1)S(1)}, u32[]{:S(2)}, u32[]{:S(2)}) collective-permute-start(bf16[3,8,32,128]{3,2,1,0:T(8,128)(2,1)S(1)} %pad_maximum_fusion), channel_id=1, source_target_pairs={{0,4},{4,8},{8,12},{12,16},{16,20},{20,24},{24,28},{28,0},{1,5},{5... | collective-permute-start | bytes 589832 | tf_op jit(solution)/shard_map/ppermute | solution.py:157
  29.1 2.3 %copy-start.12 = (bf16[3,8,32,128]{3,2,1,0:T(8,128)(2,1)}, bf16[3,8,32,128]{3,2,1,0:T(8,128)(2,1)S(1)}, u32[]{:S(2)}) copy-start(bf16[3,8,32,128]{3,2,1,0:T(8,128)(2,1)S(1)} %collective-permute-done.3.high_st) | copy-start | bytes 589828
  31.4 0.7 copy-start.16
  32.1 9.4 %copy-start.8 = (bf16[4,8,32,128]{3,2,1,0:T(8,128)(2,1)S(1)}, bf16[4,8,32,128]{3,2,1,0:T(8,128)(2,1)}, u32[]{:S(2)}) copy-start(bf16[4,8,32,128]{3,2,1,0:T(8,128)(2,1)} %get-tuple-element.44.own) | copy-start | bytes 786436
  36.8 21.3 %collective-permute-start.4 = (bf16[4,8,32,128]{3,2,1,0:T(8,128)(2,1)}, bf16[4,8,32,128]{3,2,1,0:T(8,128)(2,1)}, u32[]{:S(2)}, u32[]{:S(2)}) collective-permute-start(bf16[4,8,32,128]{3,2,1,0:T(8,128)(2,1)} %step_half0.4.after.own.first_ref), channel_id=1, source_target_pairs={{0,1},{1,2},{2,3},{3,0},{4,5},{5,6},{6,7},{7,4},{8,9},{9,10},{10,1... | collective-permute-start | bytes 786440 | tf_op jit(solution)/shard_map/ppermute | solution.py:157
  36.8 21.3 %collective-permute-start.5 = (bf16[4,8,32,128]{3,2,1,0:T(8,128)(2,1)}, bf16[4,8,32,128]{3,2,1,0:T(8,128)(2,1)}, u32[]{:S(2)}, u32[]{:S(2)}) collective-permute-start(bf16[4,8,32,128]{3,2,1,0:T(8,128)(2,1)} %step_half0.4.after.own.first_ref), channel_id=1, source_target_pairs={{1,0},{2,1},{3,2},{0,3},{5,4},{6,5},{7,6},{4,7},{9,8},{10,9},{11,1... | collective-permute-start | bytes 786440 | tf_op jit(solution)/shard_map/ppermute | solution.py:157
  42.5 5.3 %collective-permute-start.9 = (bf16[3,8,32,128]{3,2,1,0:T(8,128)(2,1)S(1)}, bf16[3,8,32,128]{3,2,1,0:T(8,128)(2,1)}, u32[]{:S(2)}, u32[]{:S(2)}) collective-permute-start(bf16[3,8,32,128]{3,2,1,0:T(8,128)(2,1)S(1)} %pad_maximum_fusion.3), channel_id=1, source_target_pairs={{4,0},{8,4},{12,8},{16,12},{20,16},{24,20},{28,24},{0,28},{5,1},{9... | collective-permute-start | bytes 589832 | tf_op jit(solution)/shard_map/ppermute | solution.py:157
  43.2 15.8 %copy-start.1 = (bf16[4,8,32,128]{3,2,1,0:T(8,128)(2,1)S(1)}, bf16[4,8,32,128]{3,2,1,0:T(8,128)(2,1)}, u32[]{:S(2)}) copy-start(bf16[4,8,32,128]{3,2,1,0:T(8,128)(2,1)} %step_half0.4.after.own.first_ref) | copy-start | bytes 786436
  43.2 6.4 %collective-permute-start.8 = (bf16[3,8,32,128]{3,2,1,0:T(8,128)(2,1)S(1)}, bf16[3,8,32,128]{3,2,1,0:T(8,128)(2,1)}, u32[]{:S(2)}, u32[]{:S(2)}) collective-permute-start(bf16[3,8,32,128]{3,2,1,0:T(8,128)(2,1)S(1)} %pad_maximum_fusion.2), channel_id=1, source_target_pairs={{0,4},{4,8},{8,12},{12,16},{16,20},{20,24},{24,28},{28,0},{1,5},{5... | collective-permute-start | bytes 589832 | tf_op jit(solution)/shard_map/ppermute | solution.py:157
  54.3 21.0 %collective-permute-start.14 = (bf16[4,8,32,128]{3,2,1,0:T(8,128)(2,1)}, bf16[4,8,32,128]{3,2,1,0:T(8,128)(2,1)}, u32[]{:S(2)}, u32[]{:S(2)}) collective-permute-start(bf16[4,8,32,128]{3,2,1,0:T(8,128)(2,1)} %step_half1.4.after.second_ref.own), channel_id=1, source_target_pairs={{0,1},{1,2},{2,3},{3,0},{4,5},{5,6},{6,7},{7,4},{8,9},{9,10},{10,1... | collective-permute-start | bytes 786440 | tf_op jit(solution)/shard_map/ppermute | solution.py:157
  54.3 21.0 %collective-permute-start.15 = (bf16[4,8,32,128]{3,2,1,0:T(8,128)(2,1)}, bf16[4,8,32,128]{3,2,1,0:T(8,128)(2,1)}, u32[]{:S(2)}, u32[]{:S(2)}) collective-permute-start(bf16[4,8,32,128]{3,2,1,0:T(8,128)(2,1)} %step_half1.4.after.second_ref.own), channel_id=1, source_target_pairs={{1,0},{2,1},{3,2},{0,3},{5,4},{6,5},{7,6},{4,7},{9,8},{10,9},{11,1... | collective-permute-start | bytes 786440 | tf_op jit(solution)/shard_map/ppermute | solution.py:157
  59.9 5.3 %collective-permute-start.11 = (bf16[3,8,32,128]{3,2,1,0:T(8,128)(2,1)S(1)}, bf16[3,8,32,128]{3,2,1,0:T(8,128)(2,1)}, u32[]{:S(2)}, u32[]{:S(2)}) collective-permute-start(bf16[3,8,32,128]{3,2,1,0:T(8,128)(2,1)S(1)} %pad_maximum_fusion.5), channel_id=1, source_target_pairs={{4,0},{8,4},{12,8},{16,12},{20,16},{24,20},{28,24},{0,28},{5,1},{9... | collective-permute-start | bytes 589832 | tf_op jit(solution)/shard_map/ppermute | solution.py:157
  60.6 15.6 %copy-start.2 = (bf16[4,8,32,128]{3,2,1,0:T(8,128)(2,1)S(1)}, bf16[4,8,32,128]{3,2,1,0:T(8,128)(2,1)}, u32[]{:S(2)}) copy-start(bf16[4,8,32,128]{3,2,1,0:T(8,128)(2,1)} %step_half1.4.after.second_ref.own) | copy-start | bytes 786436
  60.6 6.2 %collective-permute-start.10 = (bf16[3,8,32,128]{3,2,1,0:T(8,128)(2,1)S(1)}, bf16[3,8,32,128]{3,2,1,0:T(8,128)(2,1)}, u32[]{:S(2)}, u32[]{:S(2)}) collective-permute-start(bf16[3,8,32,128]{3,2,1,0:T(8,128)(2,1)S(1)} %pad_maximum_fusion.4), channel_id=1, source_target_pairs={{0,4},{4,8},{8,12},{12,16},{16,20},{20,24},{24,28},{28,0},{1,5},{5... | collective-permute-start | bytes 589832 | tf_op jit(solution)/shard_map/ppermute | solution.py:157
  71.4 23.3 %collective-permute-start.12 = (bf16[4,8,32,128]{3,2,1,0:T(8,128)(2,1)}, bf16[4,8,32,128]{3,2,1,0:T(8,128)(2,1)}, u32[]{:S(2)}, u32[]{:S(2)}) collective-permute-start(bf16[4,8,32,128]{3,2,1,0:T(8,128)(2,1)} %step_half0.5.refs_0_.own.first_ref), channel_id=1, source_target_pairs={{0,1},{1,2},{2,3},{3,0},{4,5},{5,6},{6,7},{7,4},{8,9},{9,10},{10,1... | collective-permute-start | bytes 786440 | tf_op jit(solution)/shard_map/ppermute | solution.py:157
  71.4 23.3 %collective-permute-start.13 = (bf16[4,8,32,128]{3,2,1,0:T(8,128)(2,1)}, bf16[4,8,32,128]{3,2,1,0:T(8,128)(2,1)}, u32[]{:S(2)}, u32[]{:S(2)}) collective-permute-start(bf16[4,8,32,128]{3,2,1,0:T(8,128)(2,1)} %step_half0.5.refs_0_.own.first_ref), channel_id=1, source_target_pairs={{1,0},{2,1},{3,2},{0,3},{5,4},{6,5},{7,6},{4,7},{9,8},{10,9},{11,1... | collective-permute-start | bytes 786440 | tf_op jit(solution)/shard_map/ppermute | solution.py:157
  77.7 6.2 %collective-permute-start.17 = (bf16[3,8,32,128]{3,2,1,0:T(8,128)(2,1)}, bf16[3,8,32,128]{3,2,1,0:T(8,128)(2,1)S(1)}, u32[]{:S(2)}, u32[]{:S(2)}) collective-permute-start(bf16[3,8,32,128]{3,2,1,0:T(8,128)(2,1)} %pad_maximum_fusion.7), channel_id=1, source_target_pairs={{4,0},{8,4},{12,8},{16,12},{20,16},{24,20},{28,24},{0,28},{5,1},{9... | collective-permute-start | bytes 589832 | tf_op jit(solution)/shard_map/ppermute | solution.py:157
  79.3 6.2 %collective-permute-start.16 = (bf16[3,8,32,128]{3,2,1,0:T(8,128)(2,1)}, bf16[3,8,32,128]{3,2,1,0:T(8,128)(2,1)S(1)}, u32[]{:S(2)}, u32[]{:S(2)}) collective-permute-start(bf16[3,8,32,128]{3,2,1,0:T(8,128)(2,1)} %pad_maximum_fusion.6), channel_id=1, source_target_pairs={{0,4},{4,8},{8,12},{12,16},{16,20},{20,24},{24,28},{28,0},{1,5},{5... | collective-permute-start | bytes 589832 | tf_op jit(solution)/shard_map/ppermute | solution.py:157
  84.0 1.5 copy-start.11
  85.5 0.7 copy-start.15
  86.2 9.4 %copy-start.3 = (bf16[4,8,32,128]{3,2,1,0:T(8,128)(2,1)S(1)}, bf16[4,8,32,128]{3,2,1,0:T(8,128)(2,1)}, u32[]{:S(2)}) copy-start(bf16[4,8,32,128]{3,2,1,0:T(8,128)(2,1)} %step_half0.5.refs_0_.own.first_ref) | copy-start | bytes 786436
  90.9 21.7 %collective-permute-start.22 = (bf16[4,8,32,128]{3,2,1,0:T(8,128)(2,1)}, bf16[4,8,32,128]{3,2,1,0:T(8,128)(2,1)}, u32[]{:S(2)}, u32[]{:S(2)}) collective-permute-start(bf16[4,8,32,128]{3,2,1,0:T(8,128)(2,1)} %step_half1.5.after.second_ref.own), channel_id=1, source_target_pairs={{0,1},{1,2},{2,3},{3,0},{4,5},{5,6},{6,7},{7,4},{8,9},{9,10},{10,1... | collective-permute-start | bytes 786440 | tf_op jit(solution)/shard_map/ppermute | solution.py:157
  90.9 21.7 %collective-permute-start.23 = (bf16[4,8,32,128]{3,2,1,0:T(8,128)(2,1)}, bf16[4,8,32,128]{3,2,1,0:T(8,128)(2,1)}, u32[]{:S(2)}, u32[]{:S(2)}) collective-permute-start(bf16[4,8,32,128]{3,2,1,0:T(8,128)(2,1)} %step_half1.5.after.second_ref.own), channel_id=1, source_target_pairs={{1,0},{2,1},{3,2},{0,3},{5,4},{6,5},{7,6},{4,7},{9,8},{10,9},{11,1... | collective-permute-start | bytes 786440 | tf_op jit(solution)/shard_map/ppermute | solution.py:157
  96.6 5.6 %collective-permute-start.19 = (bf16[3,8,32,128]{3,2,1,0:T(8,128)(2,1)S(1)}, bf16[3,8,32,128]{3,2,1,0:T(8,128)(2,1)}, u32[]{:S(2)}, u32[]{:S(2)}) collective-permute-start(bf16[3,8,32,128]{3,2,1,0:T(8,128)(2,1)S(1)} %pad_maximum_fusion.9), channel_id=1, source_target_pairs={{4,0},{8,4},{12,8},{16,12},{20,16},{24,20},{28,24},{0,28},{5,1},{9... | collective-permute-start | bytes 589832 | tf_op jit(solution)/shard_map/ppermute | solution.py:157
  97.9 15.6 %copy-start.4 = (bf16[4,8,32,128]{3,2,1,0:T(8,128)(2,1)S(1)}, bf16[4,8,32,128]{3,2,1,0:T(8,128)(2,1)}, u32[]{:S(2)}) copy-start(bf16[4,8,32,128]{3,2,1,0:T(8,128)(2,1)} %step_half1.5.after.second_ref.own) | copy-start | bytes 786436
  98.0 6.2 %collective-permute-start.18 = (bf16[3,8,32,128]{3,2,1,0:T(8,128)(2,1)S(1)}, bf16[3,8,32,128]{3,2,1,0:T(8,128)(2,1)}, u32[]{:S(2)}, u32[]{:S(2)}) collective-permute-start(bf16[3,8,32,128]{3,2,1,0:T(8,128)(2,1)S(1)} %pad_maximum_fusion.8), channel_id=1, source_target_pairs={{0,4},{4,8},{8,12},{12,16},{16,20},{20,24},{24,28},{28,0},{1,5},{5... | collective-permute-start | bytes 589832 | tf_op jit(solution)/shard_map/ppermute | solution.py:157
  108.8 22.9 %collective-permute-start.20 = (bf16[4,8,32,128]{3,2,1,0:T(8,128)(2,1)}, bf16[4,8,32,128]{3,2,1,0:T(8,128)(2,1)}, u32[]{:S(2)}, u32[]{:S(2)}) collective-permute-start(bf16[4,8,32,128]{3,2,1,0:T(8,128)(2,1)} %step_half0.6.refs_1_.own.first_ref), channel_id=1, source_target_pairs={{0,1},{1,2},{2,3},{3,0},{4,5},{5,6},{6,7},{7,4},{8,9},{9,10},{10,1... | collective-permute-start | bytes 786440 | tf_op jit(solution)/shard_map/ppermute | solution.py:157
  108.8 22.9 %collective-permute-start.21 = (bf16[4,8,32,128]{3,2,1,0:T(8,128)(2,1)}, bf16[4,8,32,128]{3,2,1,0:T(8,128)(2,1)}, u32[]{:S(2)}, u32[]{:S(2)}) collective-permute-start(bf16[4,8,32,128]{3,2,1,0:T(8,128)(2,1)} %step_half0.6.refs_1_.own.first_ref), channel_id=1, source_target_pairs={{1,0},{2,1},{3,2},{0,3},{5,4},{6,5},{7,6},{4,7},{9,8},{10,9},{11,1... | collective-permute-start | bytes 786440 | tf_op jit(solution)/shard_map/ppermute | solution.py:157
  115.1 5.8 %collective-permute-start.25 = (bf16[3,8,32,128]{3,2,1,0:T(8,128)(2,1)}, bf16[3,8,32,128]{3,2,1,0:T(8,128)(2,1)S(1)}, u32[]{:S(2)}, u32[]{:S(2)}) collective-permute-start(bf16[3,8,32,128]{3,2,1,0:T(8,128)(2,1)} %pad_maximum_fusion.11), channel_id=1, source_target_pairs={{4,0},{8,4},{12,8},{16,12},{20,16},{24,20},{28,24},{0,28},{5,1},{9... | collective-permute-start | bytes 589832 | tf_op jit(solution)/shard_map/ppermute | solution.py:157
  116.2 6.2 %collective-permute-start.24 = (bf16[3,8,32,128]{3,2,1,0:T(8,128)(2,1)}, bf16[3,8,32,128]{3,2,1,0:T(8,128)(2,1)S(1)}, u32[]{:S(2)}, u32[]{:S(2)}) collective-permute-start(bf16[3,8,32,128]{3,2,1,0:T(8,128)(2,1)} %pad_maximum_fusion.10), channel_id=1, source_target_pairs={{0,4},{4,8},{8,12},{12,16},{16,20},{20,24},{24,28},{28,0},{1,5},{5... | collective-permute-start | bytes 589832 | tf_op jit(solution)/shard_map/ppermute | solution.py:157
  121.0 1.4 copy-start.10
  122.4 0.7 copy-start.14
  123.1 9.4 %copy-start.6 = (bf16[4,8,32,128]{3,2,1,0:T(8,128)(2,1)S(1)}, bf16[4,8,32,128]{3,2,1,0:T(8,128)(2,1)}, u32[]{:S(2)}) copy-start(bf16[4,8,32,128]{3,2,1,0:T(8,128)(2,1)} %step_half0.6.refs_1_.own.first_ref) | copy-start | bytes 786436
  127.8 18.0 %collective-permute-start.28 = (bf16[4,8,32,128]{3,2,1,0:T(8,128)(2,1)}, bf16[4,8,32,128]{3,2,1,0:T(8,128)(2,1)}, u32[]{:S(2)}, u32[]{:S(2)}) collective-permute-start(bf16[4,8,32,128]{3,2,1,0:T(8,128)(2,1)} %step_half1.6.after.second_ref.own), channel_id=1, source_target_pairs={{0,1},{1,2},{2,3},{3,0},{4,5},{5,6},{6,7},{7,4},{8,9},{9,10},{10,1... | collective-permute-start | bytes 786440 | tf_op jit(solution)/shard_map/ppermute | solution.py:157
  127.8 18.0 %collective-permute-start.29 = (bf16[4,8,32,128]{3,2,1,0:T(8,128)(2,1)}, bf16[4,8,32,128]{3,2,1,0:T(8,128)(2,1)}, u32[]{:S(2)}, u32[]{:S(2)}) collective-permute-start(bf16[4,8,32,128]{3,2,1,0:T(8,128)(2,1)} %step_half1.6.after.second_ref.own), channel_id=1, source_target_pairs={{1,0},{2,1},{3,2},{0,3},{5,4},{6,5},{7,6},{4,7},{9,8},{10,9},{11,1... | collective-permute-start | bytes 786440 | tf_op jit(solution)/shard_map/ppermute | solution.py:157
  133.5 6.0 %collective-permute-start.27 = (bf16[3,8,32,128]{3,2,1,0:T(8,128)(2,1)S(1)}, bf16[3,8,32,128]{3,2,1,0:T(8,128)(2,1)}, u32[]{:S(2)}, u32[]{:S(2)}) collective-permute-start(bf16[3,8,32,128]{3,2,1,0:T(8,128)(2,1)S(1)} %pad_maximum_fusion.13), channel_id=1, source_target_pairs={{4,0},{8,4},{12,8},{16,12},{20,16},{24,20},{28,24},{0,28},{5,1},{9... | collective-permute-start | bytes 589832 | tf_op jit(solution)/shard_map/ppermute | solution.py:157
  135.0 11.7 %copy-start.5 = (bf16[4,8,32,128]{3,2,1,0:T(8,128)(2,1)S(1)}, bf16[4,8,32,128]{3,2,1,0:T(8,128)(2,1)}, u32[]{:S(2)}) copy-start(bf16[4,8,32,128]{3,2,1,0:T(8,128)(2,1)} %step_half1.6.after.second_ref.own) | copy-start | bytes 786436
  135.0 6.2 %collective-permute-start.26 = (bf16[3,8,32,128]{3,2,1,0:T(8,128)(2,1)S(1)}, bf16[3,8,32,128]{3,2,1,0:T(8,128)(2,1)}, u32[]{:S(2)}, u32[]{:S(2)}) collective-permute-start(bf16[3,8,32,128]{3,2,1,0:T(8,128)(2,1)S(1)} %pad_maximum_fusion.12), channel_id=1, source_target_pairs={{0,4},{4,8},{8,12},{12,16},{16,20},{20,24},{24,28},{28,0},{1,5},{5... | collective-permute-start | bytes 589832 | tf_op jit(solution)/shard_map/ppermute | solution.py:157
  148.3 6.2 %collective-permute-start.31 = (bf16[3,8,32,128]{3,2,1,0:T(8,128)(2,1)}, bf16[3,8,32,128]{3,2,1,0:T(8,128)(2,1)S(1)}, u32[]{:S(2)}, u32[]{:S(2)}) collective-permute-start(bf16[3,8,32,128]{3,2,1,0:T(8,128)(2,1)} %pad_maximum_fusion.15), channel_id=1, source_target_pairs={{4,0},{8,4},{12,8},{16,12},{20,16},{24,20},{28,24},{0,28},{5,1},{9... | collective-permute-start | bytes 589832 | tf_op jit(solution)/shard_map/ppermute | solution.py:157
  150.3 6.2 %collective-permute-start.30 = (bf16[3,8,32,128]{3,2,1,0:T(8,128)(2,1)}, bf16[3,8,32,128]{3,2,1,0:T(8,128)(2,1)S(1)}, u32[]{:S(2)}, u32[]{:S(2)}) collective-permute-start(bf16[3,8,32,128]{3,2,1,0:T(8,128)(2,1)} %pad_maximum_fusion.14), channel_id=1, source_target_pairs={{0,4},{4,8},{8,12},{12,16},{16,20},{20,24},{24,28},{28,0},{1,5},{5... | collective-permute-start | bytes 589832 | tf_op jit(solution)/shard_map/ppermute | solution.py:157
  154.5 2.0 %copy-start.9 = (bf16[3,8,32,128]{3,2,1,0:T(8,128)(2,1)}, bf16[3,8,32,128]{3,2,1,0:T(8,128)(2,1)S(1)}, u32[]{:S(2)}) copy-start(bf16[3,8,32,128]{3,2,1,0:T(8,128)(2,1)S(1)} %collective-permute-done.31.high_st) | copy-start | bytes 589828
  156.5 0.7 copy-start.13

commit v6 on v5

--- a/solution.py
+++ b/solution.py
@@ -9,6 +9,7 @@
 
 STEPS = 4
 HALVES = 2
+VMEM_LIMIT = 4 * 1024 * 1024
 VMEM = pl.BlockSpec(memory_space=pltpu.VMEM)
 ANY = pl.BlockSpec(memory_space=pl.ANY)
 
@@ -41,6 +42,7 @@
         in_specs=[VMEM],
         out_specs=[VMEM] * 2,
         out_shape=[half, half],
+        compiler_params=pltpu.CompilerParams(vmem_limit_bytes=VMEM_LIMIT),
         name="pack",
     )(start)
 
@@ -84,6 +86,7 @@
             pltpu.SemaphoreType.DMA((size,)),
         ],
         input_output_aliases={} if basis is None else {2: 0},
+        compiler_params=pltpu.CompilerParams(vmem_limit_bytes=VMEM_LIMIT),
         name="unpack",
     )(first, second, *extra)
 
@@ -145,6 +148,7 @@
             bytes_accessed=2 * columns * faces * width * depth,
             transcendentals=0,
         ),
+        compiler_params=pltpu.CompilerParams(vmem_limit_bytes=VMEM_LIMIT),
         name=f"step_half{half}",
     )(table, blocks, *pieces, *stream, after)
 

time: 165 us -> 132 us (0.80)
  Pallas kernels: 49.8 us -> 25.3 us
  local copies, waits for them, and re-layouts: 21.7 us -> 12.4 us
  other arithmetic: 5.14 us -> 0.45 us
  waiting for transfers between devices: 42.1 us -> 46.2 us
    pallas_call x8, Pallas kernels: 37.6 us -> 20.2 us  [step(): pl.pallas_call(functools.partial(step_kernel, half), in_specs=[pl.BlockSp...]
    slice x23, local copies, waits for them, and re-layouts: 14.2 us -> 4.61 us  [edges(): part[0]]
    pallas_call x4, Pallas kernels: 10.1 us -> 4.26 us  [unpack(): pl.pallas_call(functools.partial(unpack_kernel, index, chosen, skipped),...]
    ppermute x32, waiting for transfers between devices: 42.1 us -> 46.2 us  [shift(): return lax.ppermute(value, axis, pairs)]
    another operation x8, other arithmetic: 2.25 us -> 0.2 us  [edges(): jnp.stack([part[columns - 1] for part in trio])]
    another operation x8, other arithmetic: 2.24 us -> 0.21 us  [edges(): jnp.stack([part[0] for part in trio])]
  transfers between devices with their start and end apart: 32 -> 32, of which waited for: 16 -> 16; matrix products, arithmetic and copies ran while one was open for 16% -> 11% of each run, Pallas kernels for 25% -> 16%
where the time goes in v6:
time: 132 us; the launch traced here: 131 us
  waiting for transfers between devices  46.2 us (35%)
  starting transfers between devices  41.1 us (31%)
  Pallas kernels  25.3 us (19%)
  local copies, waits for them, and re-layouts  12.4 us (9%)
  matrix products  5.3 us (4%)
    ppermute x32, waiting for transfers between devices, shift(): return lax.ppermute(value, axis, pairs)  46.2 us
    ppermute x32, starting transfers between devices, shift(): return lax.ppermute(value, axis, pairs)  41.1 us
    pallas_call x8, Pallas kernels, step(): pl.pallas_call(functools.partial(step_kernel, half), in_specs=[pl.BlockSp...  20.2 us
    dot_general x1, matrix products, halves_of_rows(): jnp.dot(blocks.reshape(-1, depth), mover, preferred_element_type=jnp.floa...  5.3 us
    convert_element_type x1, local copies, waits for them, and re-layouts, halves_of_rows(): return moved.astype(jnp.bfloat16).reshape(blocks.shape)  4.7 us
    slice x23, local copies, waits for them, and re-layouts, edges(): part[0]  4.61 us
    pallas_call x4, Pallas kernels, unpack(): pl.pallas_call(functools.partial(unpack_kernel, index, chosen, skipped),...  4.26 us
    unnamed x10, local copies, waits for them, and re-layouts  3.09 us
  transfers between devices with their start and end apart: 32, of which 16 were waited for; matrix products, arithmetic and copies ran while one was open for 11% of the time, Pallas kernels for 16%

profile of v6, /device:TPU:0, one launch (start us, length us, event | category | flops | bytes accessed | tf_op | source)
XLA Modules:
  0.0 131.2 jit_solution(4997171089077178424)
XLA Ops:
  0.0 1.2 copy-done.3
  1.2 0.9 pack.1
  2.1 3.0 %collective-permute-start = (bf16[4,8,32,128]{3,2,1,0:T(8,128)(2,1)S(1)}, bf16[4,8,32,128]{3,2,1,0:T(8,128)(2,1)}, u32[]{:S(2)}, u32[]{:S(2)}) collective-permute-start(bf16[4,8,32,128]{3,2,1,0:T(8,128)(2,1)S(1)} %get-tuple-element.40.own.after), channel_id=1, source_target_pairs={{0,1},{1,2},{2,3},{3,0},{4,5},{5,6},{6,7},{7,4},{8,9},{9,10},{10,1... | collective-permute-start | bytes 786440 | tf_op jit(solution)/shard_map/ppermute | solution.py:161
  5.1 2.0 %collective-permute-start.1 = (bf16[4,8,32,128]{3,2,1,0:T(8,128)(2,1)S(1)}, bf16[4,8,32,128]{3,2,1,0:T(8,128)(2,1)}, u32[]{:S(2)}, u32[]{:S(2)}) collective-permute-start(bf16[4,8,32,128]{3,2,1,0:T(8,128)(2,1)S(1)} %get-tuple-element.40.own.after), channel_id=1, source_target_pairs={{1,0},{2,1},{3,2},{0,3},{5,4},{6,5},{7,6},{4,7},{9,8},{10,9},{11,1... | collective-permute-start | bytes 786440 | tf_op jit(solution)/shard_map/ppermute | solution.py:161
  7.1 3.8 %collective-permute-start.7 = (bf16[4,8,32,128]{3,2,1,0:T(8,128)(2,1)}, bf16[4,8,32,128]{3,2,1,0:T(8,128)(2,1)}, u32[]{:S(2)}, u32[]{:S(2)}) collective-permute-start(bf16[4,8,32,128]{3,2,1,0:T(8,128)(2,1)} %get-tuple-element.44.own), channel_id=1, source_target_pairs={{1,0},{2,1},{3,2},{0,3},{5,4},{6,5},{7,6},{4,7},{9,8},{10,9},{11,1... | collective-permute-start | bytes 786440 | tf_op jit(solution)/shard_map/ppermute | solution.py:161
  11.0 5.3 %fusion = bf16[2048,768]{0,1:T(8,128)(2,1)} fusion(bf16[2048,768]{1,0:T(8,128)(2,1)S(1)} %bitcast.33, s32[768]{0:T(1024)S(1)} %get-tuple-element.121, s32[768]{0:T(1024)S(1)} %get-tuple-element.127, s32[768]{0:T(1024)S(1)} %get-tuple-element.122, s32[768]{0:T(1024)S(1)} %get-tuple-element.124, s32[768]{0:T(1024)S(1)} %get-tuple-element.123, ...), kind=kOutput, calls=%fused_computation.6 | convolution fusion | flops 2429288448 | bytes 6312192 | tf_op jit(solution)/shard_map/dot_general | solution.py:171
  16.3 4.7 %copy.7 = bf16[2048,768]{1,0:T(8,128)(2,1)} copy(bf16[2048,768]{0,1:T(8,128)(2,1)} %fusion) | data formatting | bytes 6291456 | tf_op jit(solution)/shard_map/convert_element_type | solution.py:172
  21.0 0.9 fusion.65
  21.9 0.9 fusion.63
  22.8 1.1 collective-permute-start.3
  23.9 0.1 collective-permute-start.2
  24.0 5.0 %collective-permute-done.3.high_st = bf16[3,8,32,128]{3,2,1,0:T(8,128)(2,1)S(1)} collective-permute-done((bf16[3,8,32,128]{3,2,1,0:T(8,128)(2,1)S(1)}, bf16[3,8,32,128]{3,2,1,0:T(8,128)(2,1)S(1)}, u32[]{:S(2)}, u32[]{:S(2)}) %collective-permute-start.3) | collective-permute-done | bytes 196640 | tf_op jit(solution)/shard_map/ppermute | solution.py:161
  29.0 2.3 %collective-permute-done.2.low_st = bf16[3,8,32,128]{3,2,1,0:T(8,128)(2,1)S(1)} collective-permute-done((bf16[3,8,32,128]{3,2,1,0:T(8,128)(2,1)S(1)}, bf16[3,8,32,128]{3,2,1,0:T(8,128)(2,1)S(1)}, u32[]{:S(2)}, u32[]{:S(2)}) %collective-permute-start.2) | collective-permute-done | bytes 196640 | tf_op jit(solution)/shard_map/ppermute | solution.py:161
  31.3 1.9 %copy-done.1 = bf16[2048,768]{1,0:T(8,128)(2,1)S(1)} copy-done((bf16[2048,768]{1,0:T(8,128)(2,1)S(1)}, bf16[2048,768]{1,0:T(8,128)(2,1)}, u32[]{:S(2)}) %copy-start.1) | copy-done | bytes 3145752
  33.2 3.0 %step_half0.4.after.own.first_ref = bf16[4,8,32,128]{3,2,1,0:T(8,128)(2,1)S(1)} custom-call(s32[8,12]{1,0:T(8,128)S(1)} %fusion.30.table, bf16[4,8,64,768]{3,2,1,0:T(8,128)(2,1)S(1)} %bitcast.34, bf16[4,8,32,128]{3,2,1,0:T(8,128)(2,1)S(1)} %get-tuple-element.40.own.after, bf16[4,8,32,128]{3,2,1,0:T(8,128)(2,1)} %collective-permute-done.low_az, ...), custom_call_target="tpu_custom_call" | custom-call | flops 402653184 | bytes 3145728 | tf_op jit(solution)/shard_map/step_half0/pallas_call | solution.py:140
  36.2 0.0 collective-permute-start.4
  36.2 3.8 %collective-permute-start.5 = (bf16[4,8,32,128]{3,2,1,0:T(8,128)(2,1)S(1)}, bf16[4,8,32,128]{3,2,1,0:T(8,128)(2,1)S(1)}, u32[]{:S(2)}, u32[]{:S(2)}) collective-permute-start(bf16[4,8,32,128]{3,2,1,0:T(8,128)(2,1)S(1)} %step_half0.4.after.own.first_ref), channel_id=1, source_target_pairs={{1,0},{2,1},{3,2},{0,3},{5,4},{6,5},{7,6},{4,7},{9,8},{10,9},{11,1... | collective-permute-start | bytes 786440 | tf_op jit(solution)/shard_map/ppermute | solution.py:161
  40.0 0.9 fusion.60
  40.9 0.9 fusion.61
  41.8 0.9 fusion.62
  42.7 0.1 collective-permute-start.9
  42.8 0.5 collective-permute-start.8
  43.4 4.6 %collective-permute-done.9.high_st = bf16[3,8,32,128]{3,2,1,0:T(8,128)(2,1)S(1)} collective-permute-done((bf16[3,8,32,128]{3,2,1,0:T(8,128)(2,1)S(1)}, bf16[3,8,32,128]{3,2,1,0:T(8,128)(2,1)S(1)}, u32[]{:S(2)}, u32[]{:S(2)}) %collective-permute-start.9) | collective-permute-done | bytes 196640 | tf_op jit(solution)/shard_map/ppermute | solution.py:161
  48.0 1.1 collective-permute-done.8.low_st
  49.1 2.9 %step_half1.4.after.second_ref.own = bf16[4,8,32,128]{3,2,1,0:T(8,128)(2,1)S(1)} custom-call(s32[8,12]{1,0:T(8,128)S(1)} %fusion.30.table, bf16[4,8,64,768]{3,2,1,0:T(8,128)(2,1)S(1)} %bitcast.35, bf16[4,8,32,128]{3,2,1,0:T(8,128)(2,1)} %get-tuple-element.44.own, bf16[4,8,32,128]{3,2,1,0:T(8,128)(2,1)} %collective-permute-done.6.low_az, ...), custom_call_target="tpu_custom_call" | custom-call | flops 402653184 | bytes 3145728 | tf_op jit(solution)/shard_map/step_half1/pallas_call | solution.py:140
  52.0 3.8 %collective-permute-start.15 = (bf16[4,8,32,128]{3,2,1,0:T(8,128)(2,1)S(1)}, bf16[4,8,32,128]{3,2,1,0:T(8,128)(2,1)S(1)}, u32[]{:S(2)}, u32[]{:S(2)}) collective-permute-start(bf16[4,8,32,128]{3,2,1,0:T(8,128)(2,1)S(1)} %step_half1.4.after.second_ref.own), channel_id=1, source_target_pairs={{1,0},{2,1},{3,2},{0,3},{5,4},{6,5},{7,6},{4,7},{9,8},{10,9},{11,1... | collective-permute-start | bytes 786440 | tf_op jit(solution)/shard_map/ppermute | solution.py:161
  55.9 1.2 collective-permute-start.11
  57.2 0.1 collective-permute-start.10
  57.3 4.9 %collective-permute-done.11.high_st = bf16[3,8,32,128]{3,2,1,0:T(8,128)(2,1)S(1)} collective-permute-done((bf16[3,8,32,128]{3,2,1,0:T(8,128)(2,1)S(1)}, bf16[3,8,32,128]{3,2,1,0:T(8,128)(2,1)S(1)}, u32[]{:S(2)}, u32[]{:S(2)}) %collective-permute-start.11) | collective-permute-done | bytes 196640 | tf_op jit(solution)/shard_map/ppermute | solution.py:161
  62.1 1.1 collective-permute-done.10.low_st
  63.3 2.4 %step_half0.5.refs_0_.own.first_ref = bf16[4,8,32,128]{3,2,1,0:T(8,128)(2,1)S(1)} custom-call(s32[8,12]{1,0:T(8,128)S(1)} %fusion.30.table, bf16[4,8,64,768]{3,2,1,0:T(8,128)(2,1)S(1)} %bitcast.36, bf16[4,8,32,128]{3,2,1,0:T(8,128)(2,1)S(1)} %step_half0.4.after.own.first_ref, bf16[4,8,32,128]{3,2,1,0:T(8,128)(2,1)S(1)} %collective-permute-done.4.low_az, ...), custom_call_target="tpu_custom_call" | custom-call | flops 402653184 | bytes 3145728 | tf_op jit(solution)/shard_map/step_half0/pallas_call | solution.py:140
  65.7 3.8 %collective-permute-start.13 = (bf16[4,8,32,128]{3,2,1,0:T(8,128)(2,1)S(1)}, bf16[4,8,32,128]{3,2,1,0:T(8,128)(2,1)S(1)}, u32[]{:S(2)}, u32[]{:S(2)}) collective-permute-start(bf16[4,8,32,128]{3,2,1,0:T(8,128)(2,1)S(1)} %step_half0.5.refs_0_.own.first_ref), channel_id=1, source_target_pairs={{1,0},{2,1},{3,2},{0,3},{5,4},{6,5},{7,6},{4,7},{9,8},{10,9},{11,1... | collective-permute-start | bytes 786440 | tf_op jit(solution)/shard_map/ppermute | solution.py:161
  69.6 1.2 collective-permute-start.17
  70.8 0.1 collective-permute-start.16
  70.9 0.9 unpack.4
  71.8 3.8 %collective-permute-done.17.high_st = bf16[3,8,32,128]{3,2,1,0:T(8,128)(2,1)S(1)} collective-permute-done((bf16[3,8,32,128]{3,2,1,0:T(8,128)(2,1)S(1)}, bf16[3,8,32,128]{3,2,1,0:T(8,128)(2,1)S(1)}, u32[]{:S(2)}, u32[]{:S(2)}) %collective-permute-start.17) | collective-permute-done | bytes 196640 | tf_op jit(solution)/shard_map/ppermute | solution.py:161
  75.6 1.3 collective-permute-done.16.low_st
  76.8 2.4 %step_half1.5.after.second_ref.own = bf16[4,8,32,128]{3,2,1,0:T(8,128)(2,1)S(1)} custom-call(s32[8,12]{1,0:T(8,128)S(1)} %fusion.30.table, bf16[4,8,64,768]{3,2,1,0:T(8,128)(2,1)S(1)} %bitcast.37, bf16[4,8,32,128]{3,2,1,0:T(8,128)(2,1)S(1)} %step_half1.4.after.second_ref.own, bf16[4,8,32,128]{3,2,1,0:T(8,128)(2,1)S(1)} %collective-permute-done.14.low_az, ...), custom_call_target="tpu_custom_call" | custom-call | flops 402653184 | bytes 3145728 | tf_op jit(solution)/shard_map/step_half1/pallas_call | solution.py:140
  79.3 3.8 %collective-permute-start.23 = (bf16[4,8,32,128]{3,2,1,0:T(8,128)(2,1)S(1)}, bf16[4,8,32,128]{3,2,1,0:T(8,128)(2,1)S(1)}, u32[]{:S(2)}, u32[]{:S(2)}) collective-permute-start(bf16[4,8,32,128]{3,2,1,0:T(8,128)(2,1)S(1)} %step_half1.5.after.second_ref.own), channel_id=1, source_target_pairs={{1,0},{2,1},{3,2},{0,3},{5,4},{6,5},{7,6},{4,7},{9,8},{10,9},{11,1... | collective-permute-start | bytes 786440 | tf_op jit(solution)/shard_map/ppermute | solution.py:161
  83.2 1.0 collective-permute-start.19
  84.2 0.1 collective-permute-start.18
  84.3 4.5 %collective-permute-done.19.high_st = bf16[3,8,32,128]{3,2,1,0:T(8,128)(2,1)S(1)} collective-permute-done((bf16[3,8,32,128]{3,2,1,0:T(8,128)(2,1)S(1)}, bf16[3,8,32,128]{3,2,1,0:T(8,128)(2,1)S(1)}, u32[]{:S(2)}, u32[]{:S(2)}) %collective-permute-start.19) | collective-permute-done | bytes 196640 | tf_op jit(solution)/shard_map/ppermute | solution.py:161
  88.8 1.5 %collective-permute-done.18.low_st = bf16[3,8,32,128]{3,2,1,0:T(8,128)(2,1)S(1)} collective-permute-done((bf16[3,8,32,128]{3,2,1,0:T(8,128)(2,1)S(1)}, bf16[3,8,32,128]{3,2,1,0:T(8,128)(2,1)S(1)}, u32[]{:S(2)}, u32[]{:S(2)}) %collective-permute-start.18) | collective-permute-done | bytes 196640 | tf_op jit(solution)/shard_map/ppermute | solution.py:161
  90.3 2.4 %step_half0.6.refs_1_.own.first_ref = bf16[4,8,32,128]{3,2,1,0:T(8,128)(2,1)S(1)} custom-call(s32[8,12]{1,0:T(8,128)S(1)} %fusion.30.table, bf16[4,8,64,768]{3,2,1,0:T(8,128)(2,1)S(1)} %bitcast.38, bf16[4,8,32,128]{3,2,1,0:T(8,128)(2,1)S(1)} %step_half0.5.refs_0_.own.first_ref, bf16[4,8,32,128]{3,2,1,0:T(8,128)(2,1)S(1)} %collective-permute-done.12.low_az, ...), custom_call_target="tpu_custom_call" | custom-call | flops 402653184 | bytes 3145728 | tf_op jit(solution)/shard_map/step_half0/pallas_call | solution.py:140
  92.7 3.8 %collective-permute-start.21 = (bf16[4,8,32,128]{3,2,1,0:T(8,128)(2,1)S(1)}, bf16[4,8,32,128]{3,2,1,0:T(8,128)(2,1)S(1)}, u32[]{:S(2)}, u32[]{:S(2)}) collective-permute-start(bf16[4,8,32,128]{3,2,1,0:T(8,128)(2,1)S(1)} %step_half0.6.refs_1_.own.first_ref), channel_id=1, source_target_pairs={{1,0},{2,1},{3,2},{0,3},{5,4},{6,5},{7,6},{4,7},{9,8},{10,9},{11,1... | collective-permute-start | bytes 786440 | tf_op jit(solution)/shard_map/ppermute | solution.py:161
  96.6 0.8 collective-permute-start.25
  97.5 0.1 collective-permute-start.24
  97.6 0.9 unpack.5
  98.5 3.4 %collective-permute-done.25.high_st = bf16[3,8,32,128]{3,2,1,0:T(8,128)(2,1)S(1)} collective-permute-done((bf16[3,8,32,128]{3,2,1,0:T(8,128)(2,1)S(1)}, bf16[3,8,32,128]{3,2,1,0:T(8,128)(2,1)S(1)}, u32[]{:S(2)}, u32[]{:S(2)}) %collective-permute-start.25) | collective-permute-done | bytes 196640 | tf_op jit(solution)/shard_map/ppermute | solution.py:161
  101.9 1.7 %collective-permute-done.24.low_st = bf16[3,8,32,128]{3,2,1,0:T(8,128)(2,1)S(1)} collective-permute-done((bf16[3,8,32,128]{3,2,1,0:T(8,128)(2,1)S(1)}, bf16[3,8,32,128]{3,2,1,0:T(8,128)(2,1)S(1)}, u32[]{:S(2)}, u32[]{:S(2)}) %collective-permute-start.24) | collective-permute-done | bytes 196640 | tf_op jit(solution)/shard_map/ppermute | solution.py:161
  103.6 2.4 %step_half1.6.after.second_ref.own = bf16[4,8,32,128]{3,2,1,0:T(8,128)(2,1)S(1)} custom-call(s32[8,12]{1,0:T(8,128)S(1)} %fusion.30.table, bf16[4,8,64,768]{3,2,1,0:T(8,128)(2,1)S(1)} %bitcast.39, bf16[4,8,32,128]{3,2,1,0:T(8,128)(2,1)S(1)} %step_half1.5.after.second_ref.own, bf16[4,8,32,128]{3,2,1,0:T(8,128)(2,1)S(1)} %collective-permute-done.22.low_az, ...), custom_call_target="tpu_custom_call" | custom-call | flops 402653184 | bytes 3145728 | tf_op jit(solution)/shard_map/step_half1/pallas_call | solution.py:140
  106.0 3.8 %collective-permute-start.29 = (bf16[4,8,32,128]{3,2,1,0:T(8,128)(2,1)S(1)}, bf16[4,8,32,128]{3,2,1,0:T(8,128)(2,1)S(1)}, u32[]{:S(2)}, u32[]{:S(2)}) collective-permute-start(bf16[4,8,32,128]{3,2,1,0:T(8,128)(2,1)S(1)} %step_half1.6.after.second_ref.own), channel_id=1, source_target_pairs={{1,0},{2,1},{3,2},{0,3},{5,4},{6,5},{7,6},{4,7},{9,8},{10,9},{11,1... | collective-permute-start | bytes 786440 | tf_op jit(solution)/shard_map/ppermute | solution.py:161
  109.9 0.7 collective-permute-start.27
  110.6 0.1 collective-permute-start.26
  110.6 4.5 %collective-permute-done.27.high_st = bf16[3,8,32,128]{3,2,1,0:T(8,128)(2,1)S(1)} collective-permute-done((bf16[3,8,32,128]{3,2,1,0:T(8,128)(2,1)S(1)}, bf16[3,8,32,128]{3,2,1,0:T(8,128)(2,1)S(1)}, u32[]{:S(2)}, u32[]{:S(2)}) %collective-permute-start.27) | collective-permute-done | bytes 196640 | tf_op jit(solution)/shard_map/ppermute | solution.py:161
  115.1 1.5 %collective-permute-done.26.low_st = bf16[3,8,32,128]{3,2,1,0:T(8,128)(2,1)S(1)} collective-permute-done((bf16[3,8,32,128]{3,2,1,0:T(8,128)(2,1)S(1)}, bf16[3,8,32,128]{3,2,1,0:T(8,128)(2,1)S(1)}, u32[]{:S(2)}, u32[]{:S(2)}) %collective-permute-start.26) | collective-permute-done | bytes 196640 | tf_op jit(solution)/shard_map/ppermute | solution.py:161
  116.6 2.4 %step_half0.7.refs_1_.first_ref = bf16[4,8,32,128]{3,2,1,0:T(8,128)(2,1)S(1)} custom-call(s32[8,12]{1,0:T(8,128)S(1)} %fusion.30.table, bf16[4,8,64,768]{3,2,1,0:T(8,128)(2,1)S(1)} %bitcast.40, bf16[4,8,32,128]{3,2,1,0:T(8,128)(2,1)S(1)} %step_half0.6.refs_1_.own.first_ref, bf16[4,8,32,128]{3,2,1,0:T(8,128)(2,1)S(1)} %collective-permute-done.20.low_az, ...), custom_call_target="tpu_custom_call" | custom-call | flops 402653184 | bytes 3145728 | tf_op jit(solution)/shard_map/step_half0/pallas_call | solution.py:140
  119.1 2.0 %collective-permute-start.31 = (bf16[3,8,32,128]{3,2,1,0:T(8,128)(2,1)S(1)}, bf16[3,8,32,128]{3,2,1,0:T(8,128)(2,1)S(1)}, u32[]{:S(2)}, u32[]{:S(2)}) collective-permute-start(bf16[3,8,32,128]{3,2,1,0:T(8,128)(2,1)S(1)} %pad_maximum_fusion.15), channel_id=1, source_target_pairs={{4,0},{8,4},{12,8},{16,12},{20,16},{24,20},{28,24},{0,28},{5,1},{9... | collective-permute-start | bytes 589832 | tf_op jit(solution)/shard_map/ppermute | solution.py:161
  121.2 0.1 collective-permute-start.30
  121.2 0.9 unpack.6
  122.2 3.3 %collective-permute-done.31.high_st = bf16[3,8,32,128]{3,2,1,0:T(8,128)(2,1)S(1)} collective-permute-done((bf16[3,8,32,128]{3,2,1,0:T(8,128)(2,1)S(1)}, bf16[3,8,32,128]{3,2,1,0:T(8,128)(2,1)S(1)}, u32[]{:S(2)}, u32[]{:S(2)}) %collective-permute-start.31) | collective-permute-done | bytes 196640 | tf_op jit(solution)/shard_map/ppermute | solution.py:161
  125.5 1.8 %collective-permute-done.30.low_st = bf16[3,8,32,128]{3,2,1,0:T(8,128)(2,1)S(1)} collective-permute-done((bf16[3,8,32,128]{3,2,1,0:T(8,128)(2,1)S(1)}, bf16[3,8,32,128]{3,2,1,0:T(8,128)(2,1)S(1)}, u32[]{:S(2)}, u32[]{:S(2)}) %collective-permute-start.30) | collective-permute-done | bytes 196640 | tf_op jit(solution)/shard_map/ppermute | solution.py:161
  127.3 2.4 %step_half1.7.second_ref = bf16[4,8,32,128]{3,2,1,0:T(8,128)(2,1)S(1)} custom-call(s32[8,12]{1,0:T(8,128)S(1)} %fusion.30.table, bf16[4,8,64,768]{3,2,1,0:T(8,128)(2,1)S(1)} %bitcast.41, bf16[4,8,32,128]{3,2,1,0:T(8,128)(2,1)S(1)} %step_half1.6.after.second_ref.own, bf16[4,8,32,128]{3,2,1,0:T(8,128)(2,1)S(1)} %collective-permute-done.28.low_az, ...), custom_call_target="tpu_custom_call" | custom-call | flops 402653184 | bytes 3145728 | tf_op jit(solution)/shard_map/step_half1/pallas_call | solution.py:140
  129.7 1.5 %unpack.7 = (bf16[4,4,8,64,128]{4,3,2,1,0:T(8,128)(2,1)}, f32[8,128]{1,0:T(8,128)}) custom-call(bf16[4,8,32,128]{3,2,1,0:T(8,128)(2,1)S(1)} %step_half0.7.refs_1_.first_ref, bf16[4,8,32,128]{3,2,1,0:T(8,128)(2,1)S(1)} %step_half1.7.second_ref, bf16[4,4,8,64,128]{4,3,2,1,0:T(8,128)(2,1)} %get-tuple-element.69.refs_0_), custom_call_target="tpu_custom_call", output_to_operand_aliasing={{0}: (2, {})} | custom-call | tf_op jit(solution)/shard_map/unpack/pallas_call | solution.py:76
  (70 shorter events, 0.9 us)
Async XLA Ops:
  0.0 11.0 %copy-start = (bf16[4,1,8,64,768]{4,3,2,1,0:T(8,128)(2,1)S(1)}, bf16[4,1,8,64,768]{4,3,2,1,0:T(8,128)(2,1)}, u32[]{:S(2)}) copy-start(bf16[4,1,8,64,768]{4,3,2,1,0:T(8,128)(2,1)} %param.4) | copy-start | bytes 9437188
  0.0 1.2 copy-start.3
  2.1 18.9 %collective-permute-start = (bf16[4,8,32,128]{3,2,1,0:T(8,128)(2,1)S(1)}, bf16[4,8,32,128]{3,2,1,0:T(8,128)(2,1)}, u32[]{:S(2)}, u32[]{:S(2)}) collective-permute-start(bf16[4,8,32,128]{3,2,1,0:T(8,128)(2,1)S(1)} %get-tuple-element.40.own.after), channel_id=1, source_target_pairs={{0,1},{1,2},{2,3},{3,0},{4,5},{5,6},{6,7},{7,4},{8,9},{9,10},{10,1... | collective-permute-start | bytes 786440 | tf_op jit(solution)/shard_map/ppermute | solution.py:161
  5.1 15.9 %collective-permute-start.1 = (bf16[4,8,32,128]{3,2,1,0:T(8,128)(2,1)S(1)}, bf16[4,8,32,128]{3,2,1,0:T(8,128)(2,1)}, u32[]{:S(2)}, u32[]{:S(2)}) collective-permute-start(bf16[4,8,32,128]{3,2,1,0:T(8,128)(2,1)S(1)} %get-tuple-element.40.own.after), channel_id=1, source_target_pairs={{1,0},{2,1},{3,2},{0,3},{5,4},{6,5},{7,6},{4,7},{9,8},{10,9},{11,1... | collective-permute-start | bytes 786440 | tf_op jit(solution)/shard_map/ppermute | solution.py:161
  7.1 32.9 %collective-permute-start.6 = (bf16[4,8,32,128]{3,2,1,0:T(8,128)(2,1)}, bf16[4,8,32,128]{3,2,1,0:T(8,128)(2,1)}, u32[]{:S(2)}, u32[]{:S(2)}) collective-permute-start(bf16[4,8,32,128]{3,2,1,0:T(8,128)(2,1)} %get-tuple-element.44.own), channel_id=1, source_target_pairs={{0,1},{1,2},{2,3},{3,0},{4,5},{5,6},{6,7},{7,4},{8,9},{9,10},{10,1... | collective-permute-start | bytes 786440 | tf_op jit(solution)/shard_map/ppermute | solution.py:161
  7.1 32.9 %collective-permute-start.7 = (bf16[4,8,32,128]{3,2,1,0:T(8,128)(2,1)}, bf16[4,8,32,128]{3,2,1,0:T(8,128)(2,1)}, u32[]{:S(2)}, u32[]{:S(2)}) collective-permute-start(bf16[4,8,32,128]{3,2,1,0:T(8,128)(2,1)} %get-tuple-element.44.own), channel_id=1, source_target_pairs={{1,0},{2,1},{3,2},{0,3},{5,4},{6,5},{7,6},{4,7},{9,8},{10,9},{11,1... | collective-permute-start | bytes 786440 | tf_op jit(solution)/shard_map/ppermute | solution.py:161
  16.3 7.7 %copy-start.4 = (s32[1,8,12]{2,1,0:T(8,128)S(1)}, s32[1,8,12]{2,1,0:T(8,128)}, u32[]{:S(2)}) copy-start(s32[1,8,12]{2,1,0:T(8,128)} %param.5) | copy-start | bytes 1156
  22.8 6.2 %collective-permute-start.3 = (bf16[3,8,32,128]{3,2,1,0:T(8,128)(2,1)S(1)}, bf16[3,8,32,128]{3,2,1,0:T(8,128)(2,1)S(1)}, u32[]{:S(2)}, u32[]{:S(2)}) collective-permute-start(bf16[3,8,32,128]{3,2,1,0:T(8,128)(2,1)S(1)} %pad_maximum_fusion.1), channel_id=1, source_target_pairs={{4,0},{8,4},{12,8},{16,12},{20,16},{24,20},{28,24},{0,28},{5,1},{9... | collective-permute-start | bytes 589832 | tf_op jit(solution)/shard_map/ppermute | solution.py:161
  23.9 7.3 %collective-permute-start.2 = (bf16[3,8,32,128]{3,2,1,0:T(8,128)(2,1)S(1)}, bf16[3,8,32,128]{3,2,1,0:T(8,128)(2,1)S(1)}, u32[]{:S(2)}, u32[]{:S(2)}) collective-permute-start(bf16[3,8,32,128]{3,2,1,0:T(8,128)(2,1)S(1)} %pad_maximum_fusion), channel_id=1, source_target_pairs={{0,4},{4,8},{8,12},{12,16},{16,20},{20,24},{24,28},{28,0},{1,5},{5... | collective-permute-start | bytes 589832 | tf_op jit(solution)/shard_map/ppermute | solution.py:161
  31.3 1.9 %copy-start.1 = (bf16[2048,768]{1,0:T(8,128)(2,1)S(1)}, bf16[2048,768]{1,0:T(8,128)(2,1)}, u32[]{:S(2)}) copy-start(bf16[2048,768]{1,0:T(8,128)(2,1)} %copy.7) | copy-start | bytes 9437188
  33.2 15.9 %copy-start.2 = (bf16[2048,768]{1,0:T(8,128)(2,1)S(1)}, bf16[2048,768]{1,0:T(8,128)(2,1)}, u32[]{:S(2)}) copy-start(bf16[2048,768]{1,0:T(8,128)(2,1)} %copy.7) | copy-start | bytes 9437188
  36.2 19.7 %collective-permute-start.4 = (bf16[4,8,32,128]{3,2,1,0:T(8,128)(2,1)S(1)}, bf16[4,8,32,128]{3,2,1,0:T(8,128)(2,1)S(1)}, u32[]{:S(2)}, u32[]{:S(2)}) collective-permute-start(bf16[4,8,32,128]{3,2,1,0:T(8,128)(2,1)S(1)} %step_half0.4.after.own.first_ref), channel_id=1, source_target_pairs={{0,1},{1,2},{2,3},{3,0},{4,5},{5,6},{6,7},{7,4},{8,9},{9,10},{10,1... | collective-permute-start | bytes 786440 | tf_op jit(solution)/shard_map/ppermute | solution.py:161
  36.2 19.6 %collective-permute-start.5 = (bf16[4,8,32,128]{3,2,1,0:T(8,128)(2,1)S(1)}, bf16[4,8,32,128]{3,2,1,0:T(8,128)(2,1)S(1)}, u32[]{:S(2)}, u32[]{:S(2)}) collective-permute-start(bf16[4,8,32,128]{3,2,1,0:T(8,128)(2,1)S(1)} %step_half0.4.after.own.first_ref), channel_id=1, source_target_pairs={{1,0},{2,1},{3,2},{0,3},{5,4},{6,5},{7,6},{4,7},{9,8},{10,9},{11,1... | collective-permute-start | bytes 786440 | tf_op jit(solution)/shard_map/ppermute | solution.py:161
  42.7 5.3 %collective-permute-start.9 = (bf16[3,8,32,128]{3,2,1,0:T(8,128)(2,1)S(1)}, bf16[3,8,32,128]{3,2,1,0:T(8,128)(2,1)S(1)}, u32[]{:S(2)}, u32[]{:S(2)}) collective-permute-start(bf16[3,8,32,128]{3,2,1,0:T(8,128)(2,1)S(1)} %pad_maximum_fusion.3), channel_id=1, source_target_pairs={{4,0},{8,4},{12,8},{16,12},{20,16},{24,20},{28,24},{0,28},{5,1},{9... | collective-permute-start | bytes 589832 | tf_op jit(solution)/shard_map/ppermute | solution.py:161
  42.8 6.2 %collective-permute-start.8 = (bf16[3,8,32,128]{3,2,1,0:T(8,128)(2,1)S(1)}, bf16[3,8,32,128]{3,2,1,0:T(8,128)(2,1)S(1)}, u32[]{:S(2)}, u32[]{:S(2)}) collective-permute-start(bf16[3,8,32,128]{3,2,1,0:T(8,128)(2,1)S(1)} %pad_maximum_fusion.2), channel_id=1, source_target_pairs={{0,4},{4,8},{8,12},{12,16},{16,20},{20,24},{24,28},{28,0},{1,5},{5... | collective-permute-start | bytes 589832 | tf_op jit(solution)/shard_map/ppermute | solution.py:161
  52.0 17.5 %collective-permute-start.14 = (bf16[4,8,32,128]{3,2,1,0:T(8,128)(2,1)S(1)}, bf16[4,8,32,128]{3,2,1,0:T(8,128)(2,1)S(1)}, u32[]{:S(2)}, u32[]{:S(2)}) collective-permute-start(bf16[4,8,32,128]{3,2,1,0:T(8,128)(2,1)S(1)} %step_half1.4.after.second_ref.own), channel_id=1, source_target_pairs={{0,1},{1,2},{2,3},{3,0},{4,5},{5,6},{6,7},{7,4},{8,9},{9,10},{10,1... | collective-permute-start | bytes 786440 | tf_op jit(solution)/shard_map/ppermute | solution.py:161
  52.0 17.5 %collective-permute-start.15 = (bf16[4,8,32,128]{3,2,1,0:T(8,128)(2,1)S(1)}, bf16[4,8,32,128]{3,2,1,0:T(8,128)(2,1)S(1)}, u32[]{:S(2)}, u32[]{:S(2)}) collective-permute-start(bf16[4,8,32,128]{3,2,1,0:T(8,128)(2,1)S(1)} %step_half1.4.after.second_ref.own), channel_id=1, source_target_pairs={{1,0},{2,1},{3,2},{0,3},{5,4},{6,5},{7,6},{4,7},{9,8},{10,9},{11,1... | collective-permute-start | bytes 786440 | tf_op jit(solution)/shard_map/ppermute | solution.py:161
  55.9 6.2 %collective-permute-start.11 = (bf16[3,8,32,128]{3,2,1,0:T(8,128)(2,1)S(1)}, bf16[3,8,32,128]{3,2,1,0:T(8,128)(2,1)S(1)}, u32[]{:S(2)}, u32[]{:S(2)}) collective-permute-start(bf16[3,8,32,128]{3,2,1,0:T(8,128)(2,1)S(1)} %pad_maximum_fusion.5), channel_id=1, source_target_pairs={{4,0},{8,4},{12,8},{16,12},{20,16},{24,20},{28,24},{0,28},{5,1},{9... | collective-permute-start | bytes 589832 | tf_op jit(solution)/shard_map/ppermute | solution.py:161
  57.2 6.0 %collective-permute-start.10 = (bf16[3,8,32,128]{3,2,1,0:T(8,128)(2,1)S(1)}, bf16[3,8,32,128]{3,2,1,0:T(8,128)(2,1)S(1)}, u32[]{:S(2)}, u32[]{:S(2)}) collective-permute-start(bf16[3,8,32,128]{3,2,1,0:T(8,128)(2,1)S(1)} %pad_maximum_fusion.4), channel_id=1, source_target_pairs={{0,4},{4,8},{8,12},{12,16},{16,20},{20,24},{24,28},{28,0},{1,5},{5... | collective-permute-start | bytes 589832 | tf_op jit(solution)/shard_map/ppermute | solution.py:161
  65.6 17.5 %collective-permute-start.12 = (bf16[4,8,32,128]{3,2,1,0:T(8,128)(2,1)S(1)}, bf16[4,8,32,128]{3,2,1,0:T(8,128)(2,1)S(1)}, u32[]{:S(2)}, u32[]{:S(2)}) collective-permute-start(bf16[4,8,32,128]{3,2,1,0:T(8,128)(2,1)S(1)} %step_half0.5.refs_0_.own.first_ref), channel_id=1, source_target_pairs={{0,1},{1,2},{2,3},{3,0},{4,5},{5,6},{6,7},{7,4},{8,9},{9,10},{10,1... | collective-permute-start | bytes 786440 | tf_op jit(solution)/shard_map/ppermute | solution.py:161
  65.7 17.4 %collective-permute-start.13 = (bf16[4,8,32,128]{3,2,1,0:T(8,128)(2,1)S(1)}, bf16[4,8,32,128]{3,2,1,0:T(8,128)(2,1)S(1)}, u32[]{:S(2)}, u32[]{:S(2)}) collective-permute-start(bf16[4,8,32,128]{3,2,1,0:T(8,128)(2,1)S(1)} %step_half0.5.refs_0_.own.first_ref), channel_id=1, source_target_pairs={{1,0},{2,1},{3,2},{0,3},{5,4},{6,5},{7,6},{4,7},{9,8},{10,9},{11,1... | collective-permute-start | bytes 786440 | tf_op jit(solution)/shard_map/ppermute | solution.py:161
  69.6 6.0 %collective-permute-start.17 = (bf16[3,8,32,128]{3,2,1,0:T(8,128)(2,1)S(1)}, bf16[3,8,32,128]{3,2,1,0:T(8,128)(2,1)S(1)}, u32[]{:S(2)}, u32[]{:S(2)}) collective-permute-start(bf16[3,8,32,128]{3,2,1,0:T(8,128)(2,1)S(1)} %pad_maximum_fusion.7), channel_id=1, source_target_pairs={{4,0},{8,4},{12,8},{16,12},{20,16},{24,20},{28,24},{0,28},{5,1},{9... | collective-permute-start | bytes 589832 | tf_op jit(solution)/shard_map/ppermute | solution.py:161
  70.8 6.0 %collective-permute-start.16 = (bf16[3,8,32,128]{3,2,1,0:T(8,128)(2,1)S(1)}, bf16[3,8,32,128]{3,2,1,0:T(8,128)(2,1)S(1)}, u32[]{:S(2)}, u32[]{:S(2)}) collective-permute-start(bf16[3,8,32,128]{3,2,1,0:T(8,128)(2,1)S(1)} %pad_maximum_fusion.6), channel_id=1, source_target_pairs={{0,4},{4,8},{8,12},{12,16},{16,20},{20,24},{24,28},{28,0},{1,5},{5... | collective-permute-start | bytes 589832 | tf_op jit(solution)/shard_map/ppermute | solution.py:161
  79.2 17.3 %collective-permute-start.22 = (bf16[4,8,32,128]{3,2,1,0:T(8,128)(2,1)S(1)}, bf16[4,8,32,128]{3,2,1,0:T(8,128)(2,1)S(1)}, u32[]{:S(2)}, u32[]{:S(2)}) collective-permute-start(bf16[4,8,32,128]{3,2,1,0:T(8,128)(2,1)S(1)} %step_half1.5.after.second_ref.own), channel_id=1, source_target_pairs={{0,1},{1,2},{2,3},{3,0},{4,5},{5,6},{6,7},{7,4},{8,9},{9,10},{10,1... | collective-permute-start | bytes 786440 | tf_op jit(solution)/shard_map/ppermute | solution.py:161
  79.3 17.3 %collective-permute-start.23 = (bf16[4,8,32,128]{3,2,1,0:T(8,128)(2,1)S(1)}, bf16[4,8,32,128]{3,2,1,0:T(8,128)(2,1)S(1)}, u32[]{:S(2)}, u32[]{:S(2)}) collective-permute-start(bf16[4,8,32,128]{3,2,1,0:T(8,128)(2,1)S(1)} %step_half1.5.after.second_ref.own), channel_id=1, source_target_pairs={{1,0},{2,1},{3,2},{0,3},{5,4},{6,5},{7,6},{4,7},{9,8},{10,9},{11,1... | collective-permute-start | bytes 786440 | tf_op jit(solution)/shard_map/ppermute | solution.py:161
  83.2 5.6 %collective-permute-start.19 = (bf16[3,8,32,128]{3,2,1,0:T(8,128)(2,1)S(1)}, bf16[3,8,32,128]{3,2,1,0:T(8,128)(2,1)S(1)}, u32[]{:S(2)}, u32[]{:S(2)}) collective-permute-start(bf16[3,8,32,128]{3,2,1,0:T(8,128)(2,1)S(1)} %pad_maximum_fusion.9), channel_id=1, source_target_pairs={{4,0},{8,4},{12,8},{16,12},{20,16},{24,20},{28,24},{0,28},{5,1},{9... | collective-permute-start | bytes 589832 | tf_op jit(solution)/shard_map/ppermute | solution.py:161
  84.2 6.0 %collective-permute-start.18 = (bf16[3,8,32,128]{3,2,1,0:T(8,128)(2,1)S(1)}, bf16[3,8,32,128]{3,2,1,0:T(8,128)(2,1)S(1)}, u32[]{:S(2)}, u32[]{:S(2)}) collective-permute-start(bf16[3,8,32,128]{3,2,1,0:T(8,128)(2,1)S(1)} %pad_maximum_fusion.8), channel_id=1, source_target_pairs={{0,4},{4,8},{8,12},{12,16},{16,20},{20,24},{24,28},{28,0},{1,5},{5... | collective-permute-start | bytes 589832 | tf_op jit(solution)/shard_map/ppermute | solution.py:161
  92.7 17.1 %collective-permute-start.20 = (bf16[4,8,32,128]{3,2,1,0:T(8,128)(2,1)S(1)}, bf16[4,8,32,128]{3,2,1,0:T(8,128)(2,1)S(1)}, u32[]{:S(2)}, u32[]{:S(2)}) collective-permute-start(bf16[4,8,32,128]{3,2,1,0:T(8,128)(2,1)S(1)} %step_half0.6.refs_1_.own.first_ref), channel_id=1, source_target_pairs={{0,1},{1,2},{2,3},{3,0},{4,5},{5,6},{6,7},{7,4},{8,9},{9,10},{10,1... | collective-permute-start | bytes 786440 | tf_op jit(solution)/shard_map/ppermute | solution.py:161
  92.7 17.1 %collective-permute-start.21 = (bf16[4,8,32,128]{3,2,1,0:T(8,128)(2,1)S(1)}, bf16[4,8,32,128]{3,2,1,0:T(8,128)(2,1)S(1)}, u32[]{:S(2)}, u32[]{:S(2)}) collective-permute-start(bf16[4,8,32,128]{3,2,1,0:T(8,128)(2,1)S(1)} %step_half0.6.refs_1_.own.first_ref), channel_id=1, source_target_pairs={{1,0},{2,1},{3,2},{0,3},{5,4},{6,5},{7,6},{4,7},{9,8},{10,9},{11,1... | collective-permute-start | bytes 786440 | tf_op jit(solution)/shard_map/ppermute | solution.py:161
  96.6 5.3 %collective-permute-start.25 = (bf16[3,8,32,128]{3,2,1,0:T(8,128)(2,1)S(1)}, bf16[3,8,32,128]{3,2,1,0:T(8,128)(2,1)S(1)}, u32[]{:S(2)}, u32[]{:S(2)}) collective-permute-start(bf16[3,8,32,128]{3,2,1,0:T(8,128)(2,1)S(1)} %pad_maximum_fusion.11), channel_id=1, source_target_pairs={{4,0},{8,4},{12,8},{16,12},{20,16},{24,20},{28,24},{0,28},{5,1},{9... | collective-permute-start | bytes 589832 | tf_op jit(solution)/shard_map/ppermute | solution.py:161
  97.5 6.0 %collective-permute-start.24 = (bf16[3,8,32,128]{3,2,1,0:T(8,128)(2,1)S(1)}, bf16[3,8,32,128]{3,2,1,0:T(8,128)(2,1)S(1)}, u32[]{:S(2)}, u32[]{:S(2)}) collective-permute-start(bf16[3,8,32,128]{3,2,1,0:T(8,128)(2,1)S(1)} %pad_maximum_fusion.10), channel_id=1, source_target_pairs={{0,4},{4,8},{8,12},{12,16},{16,20},{20,24},{24,28},{28,0},{1,5},{5... | collective-permute-start | bytes 589832 | tf_op jit(solution)/shard_map/ppermute | solution.py:161
  105.9 13.1 %collective-permute-start.28 = (bf16[4,8,32,128]{3,2,1,0:T(8,128)(2,1)S(1)}, bf16[4,8,32,128]{3,2,1,0:T(8,128)(2,1)S(1)}, u32[]{:S(2)}, u32[]{:S(2)}) collective-permute-start(bf16[4,8,32,128]{3,2,1,0:T(8,128)(2,1)S(1)} %step_half1.6.after.second_ref.own), channel_id=1, source_target_pairs={{0,1},{1,2},{2,3},{3,0},{4,5},{5,6},{6,7},{7,4},{8,9},{9,10},{10,1... | collective-permute-start | bytes 786440 | tf_op jit(solution)/shard_map/ppermute | solution.py:161
  106.0 13.0 %collective-permute-start.29 = (bf16[4,8,32,128]{3,2,1,0:T(8,128)(2,1)S(1)}, bf16[4,8,32,128]{3,2,1,0:T(8,128)(2,1)S(1)}, u32[]{:S(2)}, u32[]{:S(2)}) collective-permute-start(bf16[4,8,32,128]{3,2,1,0:T(8,128)(2,1)S(1)} %step_half1.6.after.second_ref.own), channel_id=1, source_target_pairs={{1,0},{2,1},{3,2},{0,3},{5,4},{6,5},{7,6},{4,7},{9,8},{10,9},{11,1... | collective-permute-start | bytes 786440 | tf_op jit(solution)/shard_map/ppermute | solution.py:161
  109.9 5.3 %collective-permute-start.27 = (bf16[3,8,32,128]{3,2,1,0:T(8,128)(2,1)S(1)}, bf16[3,8,32,128]{3,2,1,0:T(8,128)(2,1)S(1)}, u32[]{:S(2)}, u32[]{:S(2)}) collective-permute-start(bf16[3,8,32,128]{3,2,1,0:T(8,128)(2,1)S(1)} %pad_maximum_fusion.13), channel_id=1, source_target_pairs={{4,0},{8,4},{12,8},{16,12},{20,16},{24,20},{28,24},{0,28},{5,1},{9... | collective-permute-start | bytes 589832 | tf_op jit(solution)/shard_map/ppermute | solution.py:161
  110.6 6.0 %collective-permute-start.26 = (bf16[3,8,32,128]{3,2,1,0:T(8,128)(2,1)S(1)}, bf16[3,8,32,128]{3,2,1,0:T(8,128)(2,1)S(1)}, u32[]{:S(2)}, u32[]{:S(2)}) collective-permute-start(bf16[3,8,32,128]{3,2,1,0:T(8,128)(2,1)S(1)} %pad_maximum_fusion.12), channel_id=1, source_target_pairs={{0,4},{4,8},{8,12},{12,16},{16,20},{20,24},{24,28},{28,0},{1,5},{5... | collective-permute-start | bytes 589832 | tf_op jit(solution)/shard_map/ppermute | solution.py:161
  119.1 6.4 %collective-permute-start.31 = (bf16[3,8,32,128]{3,2,1,0:T(8,128)(2,1)S(1)}, bf16[3,8,32,128]{3,2,1,0:T(8,128)(2,1)S(1)}, u32[]{:S(2)}, u32[]{:S(2)}) collective-permute-start(bf16[3,8,32,128]{3,2,1,0:T(8,128)(2,1)S(1)} %pad_maximum_fusion.15), channel_id=1, source_target_pairs={{4,0},{8,4},{12,8},{16,12},{20,16},{24,20},{28,24},{0,28},{5,1},{9... | collective-permute-start | bytes 589832 | tf_op jit(solution)/shard_map/ppermute | solution.py:161
  121.2 6.1 %collective-permute-start.30 = (bf16[3,8,32,128]{3,2,1,0:T(8,128)(2,1)S(1)}, bf16[3,8,32,128]{3,2,1,0:T(8,128)(2,1)S(1)}, u32[]{:S(2)}, u32[]{:S(2)}) collective-permute-start(bf16[3,8,32,128]{3,2,1,0:T(8,128)(2,1)S(1)} %pad_maximum_fusion.14), channel_id=1, source_target_pairs={{0,4},{4,8},{8,12},{12,16},{16,20},{20,24},{24,28},{28,0},{1,5},{5... | collective-permute-start | bytes 589832 | tf_op jit(solution)/shard_map/ppermute | solution.py:161

commit v7 on v6

--- a/solution.py
+++ b/solution.py
@@ -97,60 +97,83 @@
     return jnp.stack([part[0] for part in trio]), jnp.stack([part[columns - 1] for part in trio])
 
 
-def step_kernel(half, table, blocks, own, low_az, high_az, low_st, high_st, after, following, window):
+def part_kernel(half, *refs):
+    table, blocks, own, low_az, high_az = refs[:5]
+    following, window = refs[-2:]
+    edge = len(refs) > 9
     faces, width, depth = blocks.shape[1:]
     columns = own.shape[0]
     span = columns + 2
     rows, lanes = window.shape[1:]
     view = window.reshape(3, span, faces, rows, lanes)
-    for azim, source in enumerate((low_az, own, high_az)):
-        view[azim, 1 : columns + 1] = source[...]
-    view[:, 0] = low_st[...]
-    view[:, span - 1] = high_st[...]
+
+    def enter(column, carry):
+        for azim, source in enumerate((low_az, own, high_az)):
+            for face in range(faces):
+                view[azim, column + 1, face] = source[column, face]
+        return carry
+
+    lax.fori_loop(0, columns, enter, 0)
+    if edge:
+        low_st, high_st, before = refs[5:8]
+
+        def enter_stream(face, carry):
+            for azim in range(3):
+                view[azim, 0, face] = low_st[azim, face]
+                view[azim, span - 1, face] = high_st[azim, face]
+            for column in range(columns - 2):
+                following[column + 1, face] = before[column, face]
+            return carry
+
+        lax.fori_loop(0, faces, enter_stream, 0)
     neighbours = table.shape[1]
     low = low_lanes((rows, lanes))
 
-    def one(column, face):
-        gathered = jnp.concatenate(
-            [window[table[face, k] + column * faces] for k in range(neighbours)], axis=0
-        )
-        block = blocks[column, face]
-        stacked = jnp.concatenate([block[:, : depth // 2], block[:, depth // 2 :]], axis=0)
-        product = jnp.dot(stacked, gathered, preferred_element_type=jnp.float32)
-        top, bottom = product[:width], product[width:]
-        if half == 0:
-            here = jnp.where(low, top[:rows], bottom[rows:])
-            there = jnp.where(low, top[rows:], bottom[:rows])
-        else:
-            here = jnp.where(low, bottom[rows:], top[:rows])
-            there = jnp.where(low, bottom[:rows], top[rows:])
-        following[column, face] = (here + swap_lanes(there)).astype(jnp.bfloat16)
-
-    def turn(column, carry):
-        for face in range(faces):
-            one(column, face)
+    def turn(n, carry):
+        column = n * (columns - 1) if edge else n + 1
+        slot = column if edge else n
+        for face in range(faces):
+            gathered = jnp.concatenate(
+                [window[table[face, k] + column * faces] for k in range(neighbours)], axis=0
+            )
+            block = blocks[column, face]
+            stacked = jnp.concatenate([block[:, : depth // 2], block[:, depth // 2 :]], axis=0)
+            product = jnp.dot(stacked, gathered, preferred_element_type=jnp.float32)
+            top, bottom = product[:width], product[width:]
+            if half == 0:
+                here = jnp.where(low, top[:rows], bottom[rows:])
+                there = jnp.where(low, top[rows:], bottom[:rows])
+            else:
+                here = jnp.where(low, bottom[rows:], top[:rows])
+                there = jnp.where(low, bottom[:rows], top[rows:])
+            following[slot, face] = (here + swap_lanes(there)).astype(jnp.bfloat16)
         return carry
 
-    lax.fori_loop(0, columns, turn, 0)
-
-
-def step(half, table, blocks, pieces, stream, after):
+    lax.fori_loop(0, 2 if edge else columns - 2, turn, 0)
+
+
+def part(half, table, blocks, pieces, rest):
     columns, faces, width, depth = blocks.shape
     rows, lanes = pieces[0].shape[2:]
-    return pl.pallas_call(
-        functools.partial(step_kernel, half),
-        in_specs=[pl.BlockSpec(memory_space=pltpu.SMEM)] + [VMEM] * 6 + [ANY],
+    edge = len(rest) > 2
+    name = "edge" if edge else "inner"
+    done, kept = (2, columns) if edge else (columns - 2, columns - 2)
+    in_specs = [pl.BlockSpec(memory_space=pltpu.SMEM)] + [VMEM] * 4
+    in_specs += [VMEM] * 3 + [ANY] if edge else [ANY] * 2
+    return pl.pallas_call(
+        functools.partial(part_kernel, half),
+        in_specs=in_specs,
         out_specs=VMEM,
-        out_shape=jax.ShapeDtypeStruct((columns, faces, rows, lanes), jnp.bfloat16),
+        out_shape=jax.ShapeDtypeStruct((kept, faces, rows, lanes), jnp.bfloat16),
         scratch_shapes=[pltpu.VMEM((3 * (columns + 2) * faces, rows, lanes), jnp.bfloat16)],
         cost_estimate=pl.CostEstimate(
-            flops=2 * columns * faces * width * depth * lanes,
-            bytes_accessed=2 * columns * faces * width * depth,
+            flops=2 * done * faces * width * depth * lanes,
+            bytes_accessed=2 * done * faces * width * depth,
             transcendentals=0,
         ),
         compiler_params=pltpu.CompilerParams(vmem_limit_bytes=VMEM_LIMIT),
-        name=f"step_half{half}",
-    )(table, blocks, *pieces, *stream, after)
+        name=f"{name}_half{half}",
+    )(table, blocks, *pieces, *rest)
 
 
 def shift(value, axis, up):
@@ -161,15 +184,42 @@
     return lax.ppermute(value, axis, pairs)
 
 
+def halves_kernel(blocks, moved):
+    columns, faces, width, depth = blocks.shape
+    part_rows = width // 2
+    group = 4 * width
+    row = lax.broadcasted_iota(jnp.int32, (group, group), 0)
+    column = lax.broadcasted_iota(jnp.int32, (group, group), 1)
+    place = (row // width) * part_rows + row % part_rows
+    place = place + ((row // part_rows) % 2) * (group // 2)
+    mover = jnp.where(place == column, 1.0, 0.0).astype(jnp.bfloat16)
+
+    def turn(n, carry):
+        for face in range(faces):
+            for first in range(0, depth, group):
+                result = jnp.dot(
+                    blocks[n, face, :, first : first + group],
+                    mover,
+                    preferred_element_type=jnp.float32,
+                ).astype(jnp.bfloat16)
+                at = first // 2
+                moved[n, face, :, at : at + group // 2] = result[:, : group // 2]
+                at += depth // 2
+                moved[n, face, :, at : at + group // 2] = result[:, group // 2 :]
+        return carry
+
+    lax.fori_loop(0, columns, turn, 0)
+
+
 def halves_of_rows(blocks):
-    columns, faces, width, depth = blocks.shape
-    row = lax.broadcasted_iota(jnp.int32, (depth, depth), 0)
-    column = lax.broadcasted_iota(jnp.int32, (depth, depth), 1)
-    part_rows = width // 2
-    place = (row // width) * part_rows + row % part_rows + ((row // part_rows) % 2) * (depth // 2)
-    mover = (place == column).astype(jnp.bfloat16)
-    moved = jnp.dot(blocks.reshape(-1, depth), mover, preferred_element_type=jnp.float32)
-    return moved.astype(jnp.bfloat16).reshape(blocks.shape)
+    return pl.pallas_call(
+        halves_kernel,
+        in_specs=[VMEM],
+        out_specs=VMEM,
+        out_shape=jax.ShapeDtypeStruct(blocks.shape, blocks.dtype),
+        compiler_params=pltpu.CompilerParams(vmem_limit_bytes=VMEM_LIMIT),
+        name="halves_of_rows",
+    )(blocks)
 
 
 def local(start_vector, trace_blocks, neighbour):
@@ -182,19 +232,22 @@
     current = list(pack(start))
     basis = None
     latest = current[0]
+    lows = [shift(current[h], "azim", True) for h in range(HALVES)]
+    highs = [shift(current[h], "azim", False) for h in range(HALVES)]
     for index in range(STEPS):
-        around_z = [
-            (shift(current[h], "azim", True), shift(current[h], "azim", False))
-            for h in range(HALVES)
-        ]
         previous = tuple(current)
         for h in range(HALVES):
-            pieces = (current[h], *around_z[h])
+            pieces = (current[h], lows[h], highs[h])
             to_low, to_high = edges(*pieces, latest)
-            stream = [shift(to_high, "stream", True), shift(to_low, "stream", False)]
+            stream = (shift(to_high, "stream", True), shift(to_low, "stream", False))
+            middle = part(h, table, blocks, pieces, (to_low, to_high))
+            after = middle
             if h == 1 and index > 0:
-                basis, latest = unpack(index - 1, every, *previous, basis, latest)
-            current[h] = latest = step(h, table, blocks, pieces, stream, latest)
+                basis, after = unpack(index - 1, every, *previous, basis, middle)
+            current[h] = latest = part(h, table, blocks, pieces, (*stream, middle, after))
+            if index < STEPS - 1:
+                lows[h] = shift(current[h], "azim", True)
+                highs[h] = shift(current[h], "azim", False)
     basis, _ = unpack(STEPS - 1, every, *current, basis, None)
     return basis.reshape(STEPS, columns, around, faces, width, lanes)
 

time: 132 us -> 116 us (0.88)
  local copies, waits for them, and re-layouts: 12.4 us -> 3.19 us
  Pallas kernels: 25.3 us -> 31.9 us
  waiting for transfers between devices: 46.2 us -> 40.4 us
  matrix products: 5.3 us -> 0 us
    pallas_call x8 -> x17, Pallas kernels: 20.2 us -> 27.5 us  [the longest x16 24.7 us: part(): pl.pallas_call(functools.partial(part_kernel, half), in_specs=in_specs, o...]
    ppermute x32, waiting for transfers between devices: 46.2 us -> 40.4 us  [shift(): return lax.ppermute(value, axis, pairs)]
    dot_general x1 -> x0, matrix products: 5.3 us -> none  [halves_of_rows(): jnp.dot(blocks.reshape(-1, depth), mover, preferred_element_type=jnp.floa...]
    convert_element_type x1 -> x0, local copies, waits for them, and re-layouts: 4.7 us -> none  [halves_of_rows(): return moved.astype(jnp.bfloat16).reshape(blocks.shape)]
    slice x23, local copies, waits for them, and re-layouts: 4.61 us -> 0.25 us  [edges(): part[0]]
    unnamed x10 -> x6, local copies, waits for them, and re-layouts: 3.09 us -> 2.93 us
  transfers between devices with their start and end apart: 32 -> 32, of which waited for: 16 -> 17; matrix products, arithmetic and copies ran while one was open for 11% -> 1% of each run, Pallas kernels for 16% -> 25%
where the time goes in v7:
time: 116 us
  waiting for transfers between devices  40.4 us (35%)
  starting transfers between devices  40 us (34%)
  Pallas kernels  31.9 us (28%)
  local copies, waits for them, and re-layouts  3.19 us (3%)
    ppermute x32, waiting for transfers between devices, shift(): return lax.ppermute(value, axis, pairs)  40.4 us
    ppermute x32, starting transfers between devices, shift(): return lax.ppermute(value, axis, pairs)  40 us
    pallas_call x16, Pallas kernels, part(): pl.pallas_call(functools.partial(part_kernel, half), in_specs=in_specs, o...  24.7 us
    pallas_call x4, Pallas kernels, unpack(): pl.pallas_call(functools.partial(unpack_kernel, index, chosen, skipped),...  4.25 us
    unnamed x6, local copies, waits for them, and re-layouts  2.93 us
    pallas_call x1, Pallas kernels, halves_of_rows(): pl.pallas_call(halves_kernel, in_specs=[VMEM], out_specs=VMEM, out_shape=...  2.72 us
  transfers between devices with their start and end apart: 32, of which 17 were waited for; matrix products, arithmetic and copies ran while one was open for 1% of the time, Pallas kernels for 25%

profile of v7, /device:TPU:0, one launch (start us, length us, event | category | flops | bytes accessed | tf_op | source)
XLA Modules:
  0.0 116.3 jit_solution(7611342471445696447)
XLA Ops:
  0.0 1.0 copy-done.1
  1.0 0.2 pack.1
  1.2 3.1 %collective-permute-start = (bf16[4,8,32,128]{3,2,1,0:T(8,128)(2,1)S(1)}, bf16[4,8,32,128]{3,2,1,0:T(8,128)(2,1)S(1)}, u32[]{:S(2)}, u32[]{:S(2)}) collective-permute-start(bf16[4,8,32,128]{3,2,1,0:T(8,128)(2,1)S(1)} %get-tuple-element.40.refs_2_), channel_id=1, source_target_pairs={{0,1},{1,2},{2,3},{3,0},{4,5},{5,6},{6,7},{7,4},{8,9},{9,10},{10,1... | collective-permute-start | bytes 786440 | tf_op jit(solution)/shard_map/ppermute | solution.py:184
  4.3 2.1 %collective-permute-start.1 = (bf16[4,8,32,128]{3,2,1,0:T(8,128)(2,1)S(1)}, bf16[4,8,32,128]{3,2,1,0:T(8,128)(2,1)S(1)}, u32[]{:S(2)}, u32[]{:S(2)}) collective-permute-start(bf16[4,8,32,128]{3,2,1,0:T(8,128)(2,1)S(1)} %get-tuple-element.40.refs_2_), channel_id=1, source_target_pairs={{1,0},{2,1},{3,2},{0,3},{5,4},{6,5},{7,6},{4,7},{9,8},{10,9},{11,1... | collective-permute-start | bytes 786440 | tf_op jit(solution)/shard_map/ppermute | solution.py:184
  6.4 3.8 %collective-permute-start.7 = (bf16[4,8,32,128]{3,2,1,0:T(8,128)(2,1)S(1)}, bf16[4,8,32,128]{3,2,1,0:T(8,128)(2,1)S(1)}, u32[]{:S(2)}, u32[]{:S(2)}) collective-permute-start(bf16[4,8,32,128]{3,2,1,0:T(8,128)(2,1)S(1)} %get-tuple-element.44.refs_2_), channel_id=1, source_target_pairs={{1,0},{2,1},{3,2},{0,3},{5,4},{6,5},{7,6},{4,7},{9,8},{10,9},{11,1... | collective-permute-start | bytes 786440 | tf_op jit(solution)/shard_map/ppermute | solution.py:184
  10.2 1.9 %copy-done = bf16[4,1,8,64,768]{4,3,2,1,0:T(8,128)(2,1)S(1)} copy-done((bf16[4,1,8,64,768]{4,3,2,1,0:T(8,128)(2,1)S(1)}, bf16[4,1,8,64,768]{4,3,2,1,0:T(8,128)(2,1)}, u32[]{:S(2)}) %copy-start) | copy-done | bytes 3145752
  12.1 2.7 %halves_of_rows.1.refs_1_ = bf16[4,8,64,768]{3,2,1,0:T(8,128)(2,1)S(1)} custom-call(bf16[4,8,64,768]{3,2,1,0:T(8,128)(2,1)S(1)} %bitcast.29), custom_call_target="tpu_custom_call" | custom-call | tf_op jit(solution)/shard_map/halves_of_rows/pallas_call | solution.py:215
  14.8 4.4 %collective-permute-done.1.refs_4_ = bf16[4,8,32,128]{3,2,1,0:T(8,128)(2,1)S(1)} collective-permute-done((bf16[4,8,32,128]{3,2,1,0:T(8,128)(2,1)S(1)}, bf16[4,8,32,128]{3,2,1,0:T(8,128)(2,1)S(1)}, u32[]{:S(2)}, u32[]{:S(2)}) %collective-permute-start.1) | collective-permute-done | bytes 262176 | tf_op jit(solution)/shard_map/ppermute | solution.py:184
  19.4 0.1 collective-permute-start.3
  19.5 0.5 collective-permute-start.2
  20.0 1.5 %inner_half0.4.refs_7_.refs_8_ = bf16[2,8,32,128]{3,2,1,0:T(8,128)(2,1)S(1)} custom-call(s32[8,12]{1,0:T(8,128)S(1)} %fusion.4.refs_0_, bf16[4,8,64,768]{3,2,1,0:T(8,128)(2,1)S(1)} %halves_of_rows.1.refs_1_, bf16[4,8,32,128]{3,2,1,0:T(8,128)(2,1)S(1)} %get-tuple-element.40.refs_2_, bf16[4,8,32,128]{3,2,1,0:T(8,128)(2,1)S(1)} %collective-permute-done.refs_3_, ...), custom_call_target="tpu_custom_call" | custom-call | flops 201326592 | bytes 1572864 | tf_op jit(solution)/shard_map/inner_half0/pallas_call | solution.py:163
  21.5 1.9 %collective-permute-done.3.refs_6_ = bf16[3,8,32,128]{3,2,1,0:T(8,128)(2,1)S(1)} collective-permute-done((bf16[3,8,32,128]{3,2,1,0:T(8,128)(2,1)S(1)}, bf16[3,8,32,128]{3,2,1,0:T(8,128)(2,1)S(1)}, u32[]{:S(2)}, u32[]{:S(2)}) %collective-permute-start.3) | collective-permute-done | bytes 196640 | tf_op jit(solution)/shard_map/ppermute | solution.py:184
  23.4 4.2 %collective-permute-done.2.refs_5_ = bf16[3,8,32,128]{3,2,1,0:T(8,128)(2,1)S(1)} collective-permute-done((bf16[3,8,32,128]{3,2,1,0:T(8,128)(2,1)S(1)}, bf16[3,8,32,128]{3,2,1,0:T(8,128)(2,1)S(1)}, u32[]{:S(2)}, u32[]{:S(2)}) %collective-permute-start.2) | collective-permute-done | bytes 196640 | tf_op jit(solution)/shard_map/ppermute | solution.py:184
  27.7 1.6 %edge_half0.4.refs_2_.first_ref = bf16[4,8,32,128]{3,2,1,0:T(8,128)(2,1)S(1)} custom-call(s32[8,12]{1,0:T(8,128)S(1)} %fusion.4.refs_0_, bf16[4,8,64,768]{3,2,1,0:T(8,128)(2,1)S(1)} %halves_of_rows.1.refs_1_, bf16[4,8,32,128]{3,2,1,0:T(8,128)(2,1)S(1)} %get-tuple-element.40.refs_2_, bf16[4,8,32,128]{3,2,1,0:T(8,128)(2,1)S(1)} %collective-permute-done.refs_3_, ...), custom_call_target="tpu_custom_call" | custom-call | flops 201326592 | bytes 1572864 | tf_op jit(solution)/shard_map/edge_half0/pallas_call | solution.py:163
  29.2 0.7 collective-permute-start.4
  29.9 3.2 %collective-permute-start.5 = (bf16[4,8,32,128]{3,2,1,0:T(8,128)(2,1)S(1)}, bf16[4,8,32,128]{3,2,1,0:T(8,128)(2,1)S(1)}, u32[]{:S(2)}, u32[]{:S(2)}) collective-permute-start(bf16[4,8,32,128]{3,2,1,0:T(8,128)(2,1)S(1)} %edge_half0.4.refs_2_.first_ref), channel_id=1, source_target_pairs={{1,0},{2,1},{3,2},{0,3},{5,4},{6,5},{7,6},{4,7},{9,8},{10,9},{11,1... | collective-permute-start | bytes 786440 | tf_op jit(solution)/shard_map/ppermute | solution.py:184
  33.2 0.1 collective-permute-start.9
  33.3 0.5 collective-permute-start.8
  33.8 1.5 %inner_half1.4.refs_7_.refs_8_ = bf16[2,8,32,128]{3,2,1,0:T(8,128)(2,1)S(1)} custom-call(s32[8,12]{1,0:T(8,128)S(1)} %fusion.4.refs_0_, bf16[4,8,64,768]{3,2,1,0:T(8,128)(2,1)S(1)} %halves_of_rows.1.refs_1_, bf16[4,8,32,128]{3,2,1,0:T(8,128)(2,1)S(1)} %get-tuple-element.44.refs_2_, bf16[4,8,32,128]{3,2,1,0:T(8,128)(2,1)S(1)} %collective-permute-done.6.refs_3_, ...), custom_call_target="tpu_custom_call" | custom-call | flops 201326592 | bytes 1572864 | tf_op jit(solution)/shard_map/inner_half1/pallas_call | solution.py:163
  35.3 3.1 %collective-permute-done.9.refs_6_ = bf16[3,8,32,128]{3,2,1,0:T(8,128)(2,1)S(1)} collective-permute-done((bf16[3,8,32,128]{3,2,1,0:T(8,128)(2,1)S(1)}, bf16[3,8,32,128]{3,2,1,0:T(8,128)(2,1)S(1)}, u32[]{:S(2)}, u32[]{:S(2)}) %collective-permute-start.9) | collective-permute-done | bytes 196640 | tf_op jit(solution)/shard_map/ppermute | solution.py:184
  38.5 1.8 %collective-permute-done.8.refs_5_ = bf16[3,8,32,128]{3,2,1,0:T(8,128)(2,1)S(1)} collective-permute-done((bf16[3,8,32,128]{3,2,1,0:T(8,128)(2,1)S(1)}, bf16[3,8,32,128]{3,2,1,0:T(8,128)(2,1)S(1)}, u32[]{:S(2)}, u32[]{:S(2)}) %collective-permute-start.8) | collective-permute-done | bytes 196640 | tf_op jit(solution)/shard_map/ppermute | solution.py:184
  40.3 1.6 %edge_half1.4.refs_2_.second_ref = bf16[4,8,32,128]{3,2,1,0:T(8,128)(2,1)S(1)} custom-call(s32[8,12]{1,0:T(8,128)S(1)} %fusion.4.refs_0_, bf16[4,8,64,768]{3,2,1,0:T(8,128)(2,1)S(1)} %halves_of_rows.1.refs_1_, bf16[4,8,32,128]{3,2,1,0:T(8,128)(2,1)S(1)} %get-tuple-element.44.refs_2_, bf16[4,8,32,128]{3,2,1,0:T(8,128)(2,1)S(1)} %collective-permute-done.6.refs_3_, ...), custom_call_target="tpu_custom_call" | custom-call | flops 201326592 | bytes 1572864 | tf_op jit(solution)/shard_map/edge_half1/pallas_call | solution.py:163
  41.9 3.8 %collective-permute-start.15 = (bf16[4,8,32,128]{3,2,1,0:T(8,128)(2,1)S(1)}, bf16[4,8,32,128]{3,2,1,0:T(8,128)(2,1)S(1)}, u32[]{:S(2)}, u32[]{:S(2)}) collective-permute-start(bf16[4,8,32,128]{3,2,1,0:T(8,128)(2,1)S(1)} %edge_half1.4.refs_2_.second_ref), channel_id=1, source_target_pairs={{1,0},{2,1},{3,2},{0,3},{5,4},{6,5},{7,6},{4,7},{9,8},{10,9},{11,1... | collective-permute-start | bytes 786440 | tf_op jit(solution)/shard_map/ppermute | solution.py:184
  45.8 0.5 collective-permute-start.11
  46.3 0.1 collective-permute-start.10
  46.5 1.5 %inner_half0.5.refs_7_.refs_8_ = bf16[2,8,32,128]{3,2,1,0:T(8,128)(2,1)S(1)} custom-call(s32[8,12]{1,0:T(8,128)S(1)} %fusion.4.refs_0_, bf16[4,8,64,768]{3,2,1,0:T(8,128)(2,1)S(1)} %halves_of_rows.1.refs_1_, bf16[4,8,32,128]{3,2,1,0:T(8,128)(2,1)S(1)} %edge_half0.4.refs_2_.first_ref, bf16[4,8,32,128]{3,2,1,0:T(8,128)(2,1)S(1)} %collective-permute-done.4.refs_3_, ...), custom_call_target="tpu_custom_call" | custom-call | flops 201326592 | bytes 1572864 | tf_op jit(solution)/shard_map/inner_half0/pallas_call | solution.py:163
  48.0 3.3 %collective-permute-done.11.refs_6_ = bf16[3,8,32,128]{3,2,1,0:T(8,128)(2,1)S(1)} collective-permute-done((bf16[3,8,32,128]{3,2,1,0:T(8,128)(2,1)S(1)}, bf16[3,8,32,128]{3,2,1,0:T(8,128)(2,1)S(1)}, u32[]{:S(2)}, u32[]{:S(2)}) %collective-permute-start.11) | collective-permute-done | bytes 196640 | tf_op jit(solution)/shard_map/ppermute | solution.py:184
  51.2 1.3 %collective-permute-done.10.refs_5_ = bf16[3,8,32,128]{3,2,1,0:T(8,128)(2,1)S(1)} collective-permute-done((bf16[3,8,32,128]{3,2,1,0:T(8,128)(2,1)S(1)}, bf16[3,8,32,128]{3,2,1,0:T(8,128)(2,1)S(1)}, u32[]{:S(2)}, u32[]{:S(2)}) %collective-permute-start.10) | collective-permute-done | bytes 196640 | tf_op jit(solution)/shard_map/ppermute | solution.py:184
  52.5 1.6 %edge_half0.5.refs_2_.first_ref = bf16[4,8,32,128]{3,2,1,0:T(8,128)(2,1)S(1)} custom-call(s32[8,12]{1,0:T(8,128)S(1)} %fusion.4.refs_0_, bf16[4,8,64,768]{3,2,1,0:T(8,128)(2,1)S(1)} %halves_of_rows.1.refs_1_, bf16[4,8,32,128]{3,2,1,0:T(8,128)(2,1)S(1)} %edge_half0.4.refs_2_.first_ref, bf16[4,8,32,128]{3,2,1,0:T(8,128)(2,1)S(1)} %collective-permute-done.4.refs_3_, ...), custom_call_target="tpu_custom_call" | custom-call | flops 201326592 | bytes 1572864 | tf_op jit(solution)/shard_map/edge_half0/pallas_call | solution.py:163
  54.2 3.8 %collective-permute-start.13 = (bf16[4,8,32,128]{3,2,1,0:T(8,128)(2,1)S(1)}, bf16[4,8,32,128]{3,2,1,0:T(8,128)(2,1)S(1)}, u32[]{:S(2)}, u32[]{:S(2)}) collective-permute-start(bf16[4,8,32,128]{3,2,1,0:T(8,128)(2,1)S(1)} %edge_half0.5.refs_2_.first_ref), channel_id=1, source_target_pairs={{1,0},{2,1},{3,2},{0,3},{5,4},{6,5},{7,6},{4,7},{9,8},{10,9},{11,1... | collective-permute-start | bytes 786440 | tf_op jit(solution)/shard_map/ppermute | solution.py:184
  58.1 1.0 collective-permute-start.17
  59.1 0.1 collective-permute-start.16
  59.2 1.5 %inner_half1.5.refs_0_.refs_7_ = bf16[2,8,32,128]{3,2,1,0:T(8,128)(2,1)S(1)} custom-call(s32[8,12]{1,0:T(8,128)S(1)} %fusion.4.refs_0_, bf16[4,8,64,768]{3,2,1,0:T(8,128)(2,1)S(1)} %halves_of_rows.1.refs_1_, bf16[4,8,32,128]{3,2,1,0:T(8,128)(2,1)S(1)} %edge_half1.4.refs_2_.second_ref, bf16[4,8,32,128]{3,2,1,0:T(8,128)(2,1)S(1)} %collective-permute-done.14.refs_3_, ...), custom_call_target="tpu_custom_call" | custom-call | flops 201326592 | bytes 1572864 | tf_op jit(solution)/shard_map/inner_half1/pallas_call | solution.py:163
  60.7 0.9 unpack.4
  61.6 2.2 %collective-permute-done.17.refs_6_ = bf16[3,8,32,128]{3,2,1,0:T(8,128)(2,1)S(1)} collective-permute-done((bf16[3,8,32,128]{3,2,1,0:T(8,128)(2,1)S(1)}, bf16[3,8,32,128]{3,2,1,0:T(8,128)(2,1)S(1)}, u32[]{:S(2)}, u32[]{:S(2)}) %collective-permute-start.17) | collective-permute-done | bytes 196640 | tf_op jit(solution)/shard_map/ppermute | solution.py:184
  63.9 1.3 %collective-permute-done.16.refs_5_ = bf16[3,8,32,128]{3,2,1,0:T(8,128)(2,1)S(1)} collective-permute-done((bf16[3,8,32,128]{3,2,1,0:T(8,128)(2,1)S(1)}, bf16[3,8,32,128]{3,2,1,0:T(8,128)(2,1)S(1)}, u32[]{:S(2)}, u32[]{:S(2)}) %collective-permute-start.16) | collective-permute-done | bytes 196640 | tf_op jit(solution)/shard_map/ppermute | solution.py:184
  65.2 1.6 %edge_half1.5.refs_2_.second_ref = bf16[4,8,32,128]{3,2,1,0:T(8,128)(2,1)S(1)} custom-call(s32[8,12]{1,0:T(8,128)S(1)} %fusion.4.refs_0_, bf16[4,8,64,768]{3,2,1,0:T(8,128)(2,1)S(1)} %halves_of_rows.1.refs_1_, bf16[4,8,32,128]{3,2,1,0:T(8,128)(2,1)S(1)} %edge_half1.4.refs_2_.second_ref, bf16[4,8,32,128]{3,2,1,0:T(8,128)(2,1)S(1)} %collective-permute-done.14.refs_3_, ...), custom_call_target="tpu_custom_call" | custom-call | flops 201326592 | bytes 1572864 | tf_op jit(solution)/shard_map/edge_half1/pallas_call | solution.py:163
  66.8 3.8 %collective-permute-start.23 = (bf16[4,8,32,128]{3,2,1,0:T(8,128)(2,1)S(1)}, bf16[4,8,32,128]{3,2,1,0:T(8,128)(2,1)S(1)}, u32[]{:S(2)}, u32[]{:S(2)}) collective-permute-start(bf16[4,8,32,128]{3,2,1,0:T(8,128)(2,1)S(1)} %edge_half1.5.refs_2_.second_ref), channel_id=1, source_target_pairs={{1,0},{2,1},{3,2},{0,3},{5,4},{6,5},{7,6},{4,7},{9,8},{10,9},{11,1... | collective-permute-start | bytes 786440 | tf_op jit(solution)/shard_map/ppermute | solution.py:184
  70.7 1.0 collective-permute-start.19
  71.8 1.5 %inner_half0.6.refs_7_.refs_8_ = bf16[2,8,32,128]{3,2,1,0:T(8,128)(2,1)S(1)} custom-call(s32[8,12]{1,0:T(8,128)S(1)} %fusion.4.refs_0_, bf16[4,8,64,768]{3,2,1,0:T(8,128)(2,1)S(1)} %halves_of_rows.1.refs_1_, bf16[4,8,32,128]{3,2,1,0:T(8,128)(2,1)S(1)} %edge_half0.5.refs_2_.first_ref, bf16[4,8,32,128]{3,2,1,0:T(8,128)(2,1)S(1)} %collective-permute-done.12.refs_3_, ...), custom_call_target="tpu_custom_call" | custom-call | flops 201326592 | bytes 1572864 | tf_op jit(solution)/shard_map/inner_half0/pallas_call | solution.py:163
  73.3 3.0 %collective-permute-done.19.refs_6_ = bf16[3,8,32,128]{3,2,1,0:T(8,128)(2,1)S(1)} collective-permute-done((bf16[3,8,32,128]{3,2,1,0:T(8,128)(2,1)S(1)}, bf16[3,8,32,128]{3,2,1,0:T(8,128)(2,1)S(1)}, u32[]{:S(2)}, u32[]{:S(2)}) %collective-permute-start.19) | collective-permute-done | bytes 196640 | tf_op jit(solution)/shard_map/ppermute | solution.py:184
  76.3 1.5 %collective-permute-done.18.refs_5_ = bf16[3,8,32,128]{3,2,1,0:T(8,128)(2,1)S(1)} collective-permute-done((bf16[3,8,32,128]{3,2,1,0:T(8,128)(2,1)S(1)}, bf16[3,8,32,128]{3,2,1,0:T(8,128)(2,1)S(1)}, u32[]{:S(2)}, u32[]{:S(2)}) %collective-permute-start.18) | collective-permute-done | bytes 196640 | tf_op jit(solution)/shard_map/ppermute | solution.py:184
  77.8 1.6 %edge_half0.6.refs_2_.first_ref = bf16[4,8,32,128]{3,2,1,0:T(8,128)(2,1)S(1)} custom-call(s32[8,12]{1,0:T(8,128)S(1)} %fusion.4.refs_0_, bf16[4,8,64,768]{3,2,1,0:T(8,128)(2,1)S(1)} %halves_of_rows.1.refs_1_, bf16[4,8,32,128]{3,2,1,0:T(8,128)(2,1)S(1)} %edge_half0.5.refs_2_.first_ref, bf16[4,8,32,128]{3,2,1,0:T(8,128)(2,1)S(1)} %collective-permute-done.12.refs_3_, ...), custom_call_target="tpu_custom_call" | custom-call | flops 201326592 | bytes 1572864 | tf_op jit(solution)/shard_map/edge_half0/pallas_call | solution.py:163
  79.4 3.8 %collective-permute-start.21 = (bf16[4,8,32,128]{3,2,1,0:T(8,128)(2,1)S(1)}, bf16[4,8,32,128]{3,2,1,0:T(8,128)(2,1)S(1)}, u32[]{:S(2)}, u32[]{:S(2)}) collective-permute-start(bf16[4,8,32,128]{3,2,1,0:T(8,128)(2,1)S(1)} %edge_half0.6.refs_2_.first_ref), channel_id=1, source_target_pairs={{1,0},{2,1},{3,2},{0,3},{5,4},{6,5},{7,6},{4,7},{9,8},{10,9},{11,1... | collective-permute-start | bytes 786440 | tf_op jit(solution)/shard_map/ppermute | solution.py:184
  83.3 0.8 collective-permute-start.25
  84.2 0.1 collective-permute-start.24
  84.2 1.5 %inner_half1.6.refs_1_.refs_7_ = bf16[2,8,32,128]{3,2,1,0:T(8,128)(2,1)S(1)} custom-call(s32[8,12]{1,0:T(8,128)S(1)} %fusion.4.refs_0_, bf16[4,8,64,768]{3,2,1,0:T(8,128)(2,1)S(1)} %halves_of_rows.1.refs_1_, bf16[4,8,32,128]{3,2,1,0:T(8,128)(2,1)S(1)} %edge_half1.5.refs_2_.second_ref, bf16[4,8,32,128]{3,2,1,0:T(8,128)(2,1)S(1)} %collective-permute-done.22.refs_3_, ...), custom_call_target="tpu_custom_call" | custom-call | flops 201326592 | bytes 1572864 | tf_op jit(solution)/shard_map/inner_half1/pallas_call | solution.py:163
  85.8 0.9 unpack.5
  86.7 1.9 %collective-permute-done.25.refs_6_ = bf16[3,8,32,128]{3,2,1,0:T(8,128)(2,1)S(1)} collective-permute-done((bf16[3,8,32,128]{3,2,1,0:T(8,128)(2,1)S(1)}, bf16[3,8,32,128]{3,2,1,0:T(8,128)(2,1)S(1)}, u32[]{:S(2)}, u32[]{:S(2)}) %collective-permute-start.25) | collective-permute-done | bytes 196640 | tf_op jit(solution)/shard_map/ppermute | solution.py:184
  88.6 1.7 %collective-permute-done.24.refs_5_ = bf16[3,8,32,128]{3,2,1,0:T(8,128)(2,1)S(1)} collective-permute-done((bf16[3,8,32,128]{3,2,1,0:T(8,128)(2,1)S(1)}, bf16[3,8,32,128]{3,2,1,0:T(8,128)(2,1)S(1)}, u32[]{:S(2)}, u32[]{:S(2)}) %collective-permute-start.24) | collective-permute-done | bytes 196640 | tf_op jit(solution)/shard_map/ppermute | solution.py:184
  90.3 1.6 %edge_half1.6.refs_2_.second_ref = bf16[4,8,32,128]{3,2,1,0:T(8,128)(2,1)S(1)} custom-call(s32[8,12]{1,0:T(8,128)S(1)} %fusion.4.refs_0_, bf16[4,8,64,768]{3,2,1,0:T(8,128)(2,1)S(1)} %halves_of_rows.1.refs_1_, bf16[4,8,32,128]{3,2,1,0:T(8,128)(2,1)S(1)} %edge_half1.5.refs_2_.second_ref, bf16[4,8,32,128]{3,2,1,0:T(8,128)(2,1)S(1)} %collective-permute-done.22.refs_3_, ...), custom_call_target="tpu_custom_call" | custom-call | flops 201326592 | bytes 1572864 | tf_op jit(solution)/shard_map/edge_half1/pallas_call | solution.py:163
  92.0 3.8 %collective-permute-start.29 = (bf16[4,8,32,128]{3,2,1,0:T(8,128)(2,1)S(1)}, bf16[4,8,32,128]{3,2,1,0:T(8,128)(2,1)S(1)}, u32[]{:S(2)}, u32[]{:S(2)}) collective-permute-start(bf16[4,8,32,128]{3,2,1,0:T(8,128)(2,1)S(1)} %edge_half1.6.refs_2_.second_ref), channel_id=1, source_target_pairs={{1,0},{2,1},{3,2},{0,3},{5,4},{6,5},{7,6},{4,7},{9,8},{10,9},{11,1... | collective-permute-start | bytes 786440 | tf_op jit(solution)/shard_map/ppermute | solution.py:184
  95.9 0.6 collective-permute-start.27
  96.5 1.5 %inner_half0.7.refs_7_.refs_8_ = bf16[2,8,32,128]{3,2,1,0:T(8,128)(2,1)S(1)} custom-call(s32[8,12]{1,0:T(8,128)S(1)} %fusion.4.refs_0_, bf16[4,8,64,768]{3,2,1,0:T(8,128)(2,1)S(1)} %halves_of_rows.1.refs_1_, bf16[4,8,32,128]{3,2,1,0:T(8,128)(2,1)S(1)} %edge_half0.6.refs_2_.first_ref, bf16[4,8,32,128]{3,2,1,0:T(8,128)(2,1)S(1)} %collective-permute-done.20.refs_3_, ...), custom_call_target="tpu_custom_call" | custom-call | flops 201326592 | bytes 1572864 | tf_op jit(solution)/shard_map/inner_half0/pallas_call | solution.py:163
  98.0 3.1 %collective-permute-done.27.refs_6_ = bf16[3,8,32,128]{3,2,1,0:T(8,128)(2,1)S(1)} collective-permute-done((bf16[3,8,32,128]{3,2,1,0:T(8,128)(2,1)S(1)}, bf16[3,8,32,128]{3,2,1,0:T(8,128)(2,1)S(1)}, u32[]{:S(2)}, u32[]{:S(2)}) %collective-permute-start.27) | collective-permute-done | bytes 196640 | tf_op jit(solution)/shard_map/ppermute | solution.py:184
  101.1 1.6 %collective-permute-done.26.refs_5_ = bf16[3,8,32,128]{3,2,1,0:T(8,128)(2,1)S(1)} collective-permute-done((bf16[3,8,32,128]{3,2,1,0:T(8,128)(2,1)S(1)}, bf16[3,8,32,128]{3,2,1,0:T(8,128)(2,1)S(1)}, u32[]{:S(2)}, u32[]{:S(2)}) %collective-permute-start.26) | collective-permute-done | bytes 196640 | tf_op jit(solution)/shard_map/ppermute | solution.py:184
  102.7 1.6 %edge_half0.7.first_ref = bf16[4,8,32,128]{3,2,1,0:T(8,128)(2,1)S(1)} custom-call(s32[8,12]{1,0:T(8,128)S(1)} %fusion.4.refs_0_, bf16[4,8,64,768]{3,2,1,0:T(8,128)(2,1)S(1)} %halves_of_rows.1.refs_1_, bf16[4,8,32,128]{3,2,1,0:T(8,128)(2,1)S(1)} %edge_half0.6.refs_2_.first_ref, bf16[4,8,32,128]{3,2,1,0:T(8,128)(2,1)S(1)} %collective-permute-done.20.refs_3_, ...), custom_call_target="tpu_custom_call" | custom-call | flops 201326592 | bytes 1572864 | tf_op jit(solution)/shard_map/edge_half0/pallas_call | solution.py:163
  104.4 2.3 %collective-permute-start.31 = (bf16[3,8,32,128]{3,2,1,0:T(8,128)(2,1)S(1)}, bf16[3,8,32,128]{3,2,1,0:T(8,128)(2,1)S(1)}, u32[]{:S(2)}, u32[]{:S(2)}) collective-permute-start(bf16[3,8,32,128]{3,2,1,0:T(8,128)(2,1)S(1)} %pad_maximum_fusion.15.refs_5_), channel_id=1, source_target_pairs={{4,0},{8,4},{12,8},{16,12},{20,16},{24,20},{28,24},{0,28},{5,1},{9... | collective-permute-start | bytes 589832 | tf_op jit(solution)/shard_map/ppermute | solution.py:184
  106.8 1.5 %inner_half1.7.refs_1_.refs_7_ = bf16[2,8,32,128]{3,2,1,0:T(8,128)(2,1)S(1)} custom-call(s32[8,12]{1,0:T(8,128)S(1)} %fusion.4.refs_0_, bf16[4,8,64,768]{3,2,1,0:T(8,128)(2,1)S(1)} %halves_of_rows.1.refs_1_, bf16[4,8,32,128]{3,2,1,0:T(8,128)(2,1)S(1)} %edge_half1.6.refs_2_.second_ref, bf16[4,8,32,128]{3,2,1,0:T(8,128)(2,1)S(1)} %collective-permute-done.28.refs_3_, ...), custom_call_target="tpu_custom_call" | custom-call | flops 201326592 | bytes 1572864 | tf_op jit(solution)/shard_map/inner_half1/pallas_call | solution.py:163
  108.3 0.9 unpack.6
  109.3 2.0 %collective-permute-done.31.refs_6_ = bf16[3,8,32,128]{3,2,1,0:T(8,128)(2,1)S(1)} collective-permute-done((bf16[3,8,32,128]{3,2,1,0:T(8,128)(2,1)S(1)}, bf16[3,8,32,128]{3,2,1,0:T(8,128)(2,1)S(1)}, u32[]{:S(2)}, u32[]{:S(2)}) %collective-permute-start.31) | collective-permute-done | bytes 196640 | tf_op jit(solution)/shard_map/ppermute | solution.py:184
  111.3 2.0 %collective-permute-done.30.refs_5_ = bf16[3,8,32,128]{3,2,1,0:T(8,128)(2,1)S(1)} collective-permute-done((bf16[3,8,32,128]{3,2,1,0:T(8,128)(2,1)S(1)}, bf16[3,8,32,128]{3,2,1,0:T(8,128)(2,1)S(1)}, u32[]{:S(2)}, u32[]{:S(2)}) %collective-permute-start.30) | collective-permute-done | bytes 196640 | tf_op jit(solution)/shard_map/ppermute | solution.py:184
  113.2 1.6 %edge_half1.7.second_ref = bf16[4,8,32,128]{3,2,1,0:T(8,128)(2,1)S(1)} custom-call(s32[8,12]{1,0:T(8,128)S(1)} %fusion.4.refs_0_, bf16[4,8,64,768]{3,2,1,0:T(8,128)(2,1)S(1)} %halves_of_rows.1.refs_1_, bf16[4,8,32,128]{3,2,1,0:T(8,128)(2,1)S(1)} %edge_half1.6.refs_2_.second_ref, bf16[4,8,32,128]{3,2,1,0:T(8,128)(2,1)S(1)} %collective-permute-done.28.refs_3_, ...), custom_call_target="tpu_custom_call" | custom-call | flops 201326592 | bytes 1572864 | tf_op jit(solution)/shard_map/edge_half1/pallas_call | solution.py:163
  114.8 1.5 %unpack.7 = (bf16[4,4,8,64,128]{4,3,2,1,0:T(8,128)(2,1)}, f32[8,128]{1,0:T(8,128)}) custom-call(bf16[4,8,32,128]{3,2,1,0:T(8,128)(2,1)S(1)} %edge_half0.7.first_ref, bf16[4,8,32,128]{3,2,1,0:T(8,128)(2,1)S(1)} %edge_half1.7.second_ref, bf16[4,4,8,64,128]{4,3,2,1,0:T(8,128)(2,1)} %get-tuple-element.69.refs_0_), custom_call_target="tpu_custom_call", output_to_operand_aliasing={{0}: (2, {})} | custom-call | tf_op jit(solution)/shard_map/unpack/pallas_call | solution.py:76
  (68 shorter events, 1.1 us)
Async XLA Ops:
  0.0 1.0 copy-start.1
  1.2 13.6 %collective-permute-start = (bf16[4,8,32,128]{3,2,1,0:T(8,128)(2,1)S(1)}, bf16[4,8,32,128]{3,2,1,0:T(8,128)(2,1)S(1)}, u32[]{:S(2)}, u32[]{:S(2)}) collective-permute-start(bf16[4,8,32,128]{3,2,1,0:T(8,128)(2,1)S(1)} %get-tuple-element.40.refs_2_), channel_id=1, source_target_pairs={{0,1},{1,2},{2,3},{3,0},{4,5},{5,6},{6,7},{7,4},{8,9},{9,10},{10,1... | collective-permute-start | bytes 786440 | tf_op jit(solution)/shard_map/ppermute | solution.py:184
  4.3 15.0 %collective-permute-start.1 = (bf16[4,8,32,128]{3,2,1,0:T(8,128)(2,1)S(1)}, bf16[4,8,32,128]{3,2,1,0:T(8,128)(2,1)S(1)}, u32[]{:S(2)}, u32[]{:S(2)}) collective-permute-start(bf16[4,8,32,128]{3,2,1,0:T(8,128)(2,1)S(1)} %get-tuple-element.40.refs_2_), channel_id=1, source_target_pairs={{1,0},{2,1},{3,2},{0,3},{5,4},{6,5},{7,6},{4,7},{9,8},{10,9},{11,1... | collective-permute-start | bytes 786440 | tf_op jit(solution)/shard_map/ppermute | solution.py:184
  6.4 26.7 %collective-permute-start.6 = (bf16[4,8,32,128]{3,2,1,0:T(8,128)(2,1)S(1)}, bf16[4,8,32,128]{3,2,1,0:T(8,128)(2,1)S(1)}, u32[]{:S(2)}, u32[]{:S(2)}) collective-permute-start(bf16[4,8,32,128]{3,2,1,0:T(8,128)(2,1)S(1)} %get-tuple-element.44.refs_2_), channel_id=1, source_target_pairs={{0,1},{1,2},{2,3},{3,0},{4,5},{5,6},{6,7},{7,4},{8,9},{9,10},{10,1... | collective-permute-start | bytes 786440 | tf_op jit(solution)/shard_map/ppermute | solution.py:184
  6.4 26.7 %collective-permute-start.7 = (bf16[4,8,32,128]{3,2,1,0:T(8,128)(2,1)S(1)}, bf16[4,8,32,128]{3,2,1,0:T(8,128)(2,1)S(1)}, u32[]{:S(2)}, u32[]{:S(2)}) collective-permute-start(bf16[4,8,32,128]{3,2,1,0:T(8,128)(2,1)S(1)} %get-tuple-element.44.refs_2_), channel_id=1, source_target_pairs={{1,0},{2,1},{3,2},{0,3},{5,4},{6,5},{7,6},{4,7},{9,8},{10,9},{11,1... | collective-permute-start | bytes 786440 | tf_op jit(solution)/shard_map/ppermute | solution.py:184
  10.2 1.9 %copy-start = (bf16[4,1,8,64,768]{4,3,2,1,0:T(8,128)(2,1)S(1)}, bf16[4,1,8,64,768]{4,3,2,1,0:T(8,128)(2,1)}, u32[]{:S(2)}) copy-start(bf16[4,1,8,64,768]{4,3,2,1,0:T(8,128)(2,1)} %param.4) | copy-start | bytes 9437188
  12.1 7.9 %copy-start.2 = (s32[1,8,12]{2,1,0:T(8,128)S(1)}, s32[1,8,12]{2,1,0:T(8,128)}, u32[]{:S(2)}) copy-start(s32[1,8,12]{2,1,0:T(8,128)} %param.5) | copy-start | bytes 1156
  19.4 4.1 %collective-permute-start.3 = (bf16[3,8,32,128]{3,2,1,0:T(8,128)(2,1)S(1)}, bf16[3,8,32,128]{3,2,1,0:T(8,128)(2,1)S(1)}, u32[]{:S(2)}, u32[]{:S(2)}) collective-permute-start(bf16[3,8,32,128]{3,2,1,0:T(8,128)(2,1)S(1)} %pad_maximum_fusion.1.refs_5_), channel_id=1, source_target_pairs={{4,0},{8,4},{12,8},{16,12},{20,16},{24,20},{28,24},{0,28},{5,1},{9... | collective-permute-start | bytes 589832 | tf_op jit(solution)/shard_map/ppermute | solution.py:184
  19.5 8.2 %collective-permute-start.2 = (bf16[3,8,32,128]{3,2,1,0:T(8,128)(2,1)S(1)}, bf16[3,8,32,128]{3,2,1,0:T(8,128)(2,1)S(1)}, u32[]{:S(2)}, u32[]{:S(2)}) collective-permute-start(bf16[3,8,32,128]{3,2,1,0:T(8,128)(2,1)S(1)} %pad_maximum_fusion.refs_6_), channel_id=1, source_target_pairs={{0,4},{4,8},{8,12},{12,16},{16,20},{20,24},{24,28},{28,0},{1,5},{5... | collective-permute-start | bytes 589832 | tf_op jit(solution)/shard_map/ppermute | solution.py:184
  29.2 16.5 %collective-permute-start.4 = (bf16[4,8,32,128]{3,2,1,0:T(8,128)(2,1)S(1)}, bf16[4,8,32,128]{3,2,1,0:T(8,128)(2,1)S(1)}, u32[]{:S(2)}, u32[]{:S(2)}) collective-permute-start(bf16[4,8,32,128]{3,2,1,0:T(8,128)(2,1)S(1)} %edge_half0.4.refs_2_.first_ref), channel_id=1, source_target_pairs={{0,1},{1,2},{2,3},{3,0},{4,5},{5,6},{6,7},{7,4},{8,9},{9,10},{10,1... | collective-permute-start | bytes 786440 | tf_op jit(solution)/shard_map/ppermute | solution.py:184
  29.9 15.8 %collective-permute-start.5 = (bf16[4,8,32,128]{3,2,1,0:T(8,128)(2,1)S(1)}, bf16[4,8,32,128]{3,2,1,0:T(8,128)(2,1)S(1)}, u32[]{:S(2)}, u32[]{:S(2)}) collective-permute-start(bf16[4,8,32,128]{3,2,1,0:T(8,128)(2,1)S(1)} %edge_half0.4.refs_2_.first_ref), channel_id=1, source_target_pairs={{1,0},{2,1},{3,2},{0,3},{5,4},{6,5},{7,6},{4,7},{9,8},{10,9},{11,1... | collective-permute-start | bytes 786440 | tf_op jit(solution)/shard_map/ppermute | solution.py:184
  33.2 5.3 %collective-permute-start.9 = (bf16[3,8,32,128]{3,2,1,0:T(8,128)(2,1)S(1)}, bf16[3,8,32,128]{3,2,1,0:T(8,128)(2,1)S(1)}, u32[]{:S(2)}, u32[]{:S(2)}) collective-permute-start(bf16[3,8,32,128]{3,2,1,0:T(8,128)(2,1)S(1)} %pad_maximum_fusion.3.refs_5_), channel_id=1, source_target_pairs={{4,0},{8,4},{12,8},{16,12},{20,16},{24,20},{28,24},{0,28},{5,1},{9... | collective-permute-start | bytes 589832 | tf_op jit(solution)/shard_map/ppermute | solution.py:184
  33.3 7.0 %collective-permute-start.8 = (bf16[3,8,32,128]{3,2,1,0:T(8,128)(2,1)S(1)}, bf16[3,8,32,128]{3,2,1,0:T(8,128)(2,1)S(1)}, u32[]{:S(2)}, u32[]{:S(2)}) collective-permute-start(bf16[3,8,32,128]{3,2,1,0:T(8,128)(2,1)S(1)} %pad_maximum_fusion.2.refs_6_), channel_id=1, source_target_pairs={{0,4},{4,8},{8,12},{12,16},{16,20},{20,24},{24,28},{28,0},{1,5},{5... | collective-permute-start | bytes 589832 | tf_op jit(solution)/shard_map/ppermute | solution.py:184
  41.9 16.1 %collective-permute-start.14 = (bf16[4,8,32,128]{3,2,1,0:T(8,128)(2,1)S(1)}, bf16[4,8,32,128]{3,2,1,0:T(8,128)(2,1)S(1)}, u32[]{:S(2)}, u32[]{:S(2)}) collective-permute-start(bf16[4,8,32,128]{3,2,1,0:T(8,128)(2,1)S(1)} %edge_half1.4.refs_2_.second_ref), channel_id=1, source_target_pairs={{0,1},{1,2},{2,3},{3,0},{4,5},{5,6},{6,7},{7,4},{8,9},{9,10},{10,1... | collective-permute-start | bytes 786440 | tf_op jit(solution)/shard_map/ppermute | solution.py:184
  41.9 16.1 %collective-permute-start.15 = (bf16[4,8,32,128]{3,2,1,0:T(8,128)(2,1)S(1)}, bf16[4,8,32,128]{3,2,1,0:T(8,128)(2,1)S(1)}, u32[]{:S(2)}, u32[]{:S(2)}) collective-permute-start(bf16[4,8,32,128]{3,2,1,0:T(8,128)(2,1)S(1)} %edge_half1.4.refs_2_.second_ref), channel_id=1, source_target_pairs={{1,0},{2,1},{3,2},{0,3},{5,4},{6,5},{7,6},{4,7},{9,8},{10,9},{11,1... | collective-permute-start | bytes 786440 | tf_op jit(solution)/shard_map/ppermute | solution.py:184
  45.8 5.4 %collective-permute-start.11 = (bf16[3,8,32,128]{3,2,1,0:T(8,128)(2,1)S(1)}, bf16[3,8,32,128]{3,2,1,0:T(8,128)(2,1)S(1)}, u32[]{:S(2)}, u32[]{:S(2)}) collective-permute-start(bf16[3,8,32,128]{3,2,1,0:T(8,128)(2,1)S(1)} %pad_maximum_fusion.5.refs_5_), channel_id=1, source_target_pairs={{4,0},{8,4},{12,8},{16,12},{20,16},{24,20},{28,24},{0,28},{5,1},{9... | collective-permute-start | bytes 589832 | tf_op jit(solution)/shard_map/ppermute | solution.py:184
  46.3 6.2 %collective-permute-start.10 = (bf16[3,8,32,128]{3,2,1,0:T(8,128)(2,1)S(1)}, bf16[3,8,32,128]{3,2,1,0:T(8,128)(2,1)S(1)}, u32[]{:S(2)}, u32[]{:S(2)}) collective-permute-start(bf16[3,8,32,128]{3,2,1,0:T(8,128)(2,1)S(1)} %pad_maximum_fusion.4.refs_6_), channel_id=1, source_target_pairs={{0,4},{4,8},{8,12},{12,16},{16,20},{20,24},{24,28},{28,0},{1,5},{5... | collective-permute-start | bytes 589832 | tf_op jit(solution)/shard_map/ppermute | solution.py:184
  54.1 16.5 %collective-permute-start.12 = (bf16[4,8,32,128]{3,2,1,0:T(8,128)(2,1)S(1)}, bf16[4,8,32,128]{3,2,1,0:T(8,128)(2,1)S(1)}, u32[]{:S(2)}, u32[]{:S(2)}) collective-permute-start(bf16[4,8,32,128]{3,2,1,0:T(8,128)(2,1)S(1)} %edge_half0.5.refs_2_.first_ref), channel_id=1, source_target_pairs={{0,1},{1,2},{2,3},{3,0},{4,5},{5,6},{6,7},{7,4},{8,9},{9,10},{10,1... | collective-permute-start | bytes 786440 | tf_op jit(solution)/shard_map/ppermute | solution.py:184
  54.2 16.5 %collective-permute-start.13 = (bf16[4,8,32,128]{3,2,1,0:T(8,128)(2,1)S(1)}, bf16[4,8,32,128]{3,2,1,0:T(8,128)(2,1)S(1)}, u32[]{:S(2)}, u32[]{:S(2)}) collective-permute-start(bf16[4,8,32,128]{3,2,1,0:T(8,128)(2,1)S(1)} %edge_half0.5.refs_2_.first_ref), channel_id=1, source_target_pairs={{1,0},{2,1},{3,2},{0,3},{5,4},{6,5},{7,6},{4,7},{9,8},{10,9},{11,1... | collective-permute-start | bytes 786440 | tf_op jit(solution)/shard_map/ppermute | solution.py:184
  58.1 5.8 %collective-permute-start.17 = (bf16[3,8,32,128]{3,2,1,0:T(8,128)(2,1)S(1)}, bf16[3,8,32,128]{3,2,1,0:T(8,128)(2,1)S(1)}, u32[]{:S(2)}, u32[]{:S(2)}) collective-permute-start(bf16[3,8,32,128]{3,2,1,0:T(8,128)(2,1)S(1)} %pad_maximum_fusion.7.refs_5_), channel_id=1, source_target_pairs={{4,0},{8,4},{12,8},{16,12},{20,16},{24,20},{28,24},{0,28},{5,1},{9... | collective-permute-start | bytes 589832 | tf_op jit(solution)/shard_map/ppermute | solution.py:184
  59.1 6.0 %collective-permute-start.16 = (bf16[3,8,32,128]{3,2,1,0:T(8,128)(2,1)S(1)}, bf16[3,8,32,128]{3,2,1,0:T(8,128)(2,1)S(1)}, u32[]{:S(2)}, u32[]{:S(2)}) collective-permute-start(bf16[3,8,32,128]{3,2,1,0:T(8,128)(2,1)S(1)} %pad_maximum_fusion.6.refs_6_), channel_id=1, source_target_pairs={{0,4},{4,8},{8,12},{12,16},{16,20},{20,24},{24,28},{28,0},{1,5},{5... | collective-permute-start | bytes 589832 | tf_op jit(solution)/shard_map/ppermute | solution.py:184
  66.8 16.5 %collective-permute-start.22 = (bf16[4,8,32,128]{3,2,1,0:T(8,128)(2,1)S(1)}, bf16[4,8,32,128]{3,2,1,0:T(8,128)(2,1)S(1)}, u32[]{:S(2)}, u32[]{:S(2)}) collective-permute-start(bf16[4,8,32,128]{3,2,1,0:T(8,128)(2,1)S(1)} %edge_half1.5.refs_2_.second_ref), channel_id=1, source_target_pairs={{0,1},{1,2},{2,3},{3,0},{4,5},{5,6},{6,7},{7,4},{8,9},{9,10},{10,1... | collective-permute-start | bytes 786440 | tf_op jit(solution)/shard_map/ppermute | solution.py:184
  66.8 16.4 %collective-permute-start.23 = (bf16[4,8,32,128]{3,2,1,0:T(8,128)(2,1)S(1)}, bf16[4,8,32,128]{3,2,1,0:T(8,128)(2,1)S(1)}, u32[]{:S(2)}, u32[]{:S(2)}) collective-permute-start(bf16[4,8,32,128]{3,2,1,0:T(8,128)(2,1)S(1)} %edge_half1.5.refs_2_.second_ref), channel_id=1, source_target_pairs={{1,0},{2,1},{3,2},{0,3},{5,4},{6,5},{7,6},{4,7},{9,8},{10,9},{11,1... | collective-permute-start | bytes 786440 | tf_op jit(solution)/shard_map/ppermute | solution.py:184
  70.7 5.6 %collective-permute-start.19 = (bf16[3,8,32,128]{3,2,1,0:T(8,128)(2,1)S(1)}, bf16[3,8,32,128]{3,2,1,0:T(8,128)(2,1)S(1)}, u32[]{:S(2)}, u32[]{:S(2)}) collective-permute-start(bf16[3,8,32,128]{3,2,1,0:T(8,128)(2,1)S(1)} %pad_maximum_fusion.9.refs_5_), channel_id=1, source_target_pairs={{4,0},{8,4},{12,8},{16,12},{20,16},{24,20},{28,24},{0,28},{5,1},{9... | collective-permute-start | bytes 589832 | tf_op jit(solution)/shard_map/ppermute | solution.py:184
  71.7 6.1 %collective-permute-start.18 = (bf16[3,8,32,128]{3,2,1,0:T(8,128)(2,1)S(1)}, bf16[3,8,32,128]{3,2,1,0:T(8,128)(2,1)S(1)}, u32[]{:S(2)}, u32[]{:S(2)}) collective-permute-start(bf16[3,8,32,128]{3,2,1,0:T(8,128)(2,1)S(1)} %pad_maximum_fusion.8.refs_6_), channel_id=1, source_target_pairs={{0,4},{4,8},{8,12},{12,16},{16,20},{20,24},{24,28},{28,0},{1,5},{5... | collective-permute-start | bytes 589832 | tf_op jit(solution)/shard_map/ppermute | solution.py:184
  79.4 16.4 %collective-permute-start.20 = (bf16[4,8,32,128]{3,2,1,0:T(8,128)(2,1)S(1)}, bf16[4,8,32,128]{3,2,1,0:T(8,128)(2,1)S(1)}, u32[]{:S(2)}, u32[]{:S(2)}) collective-permute-start(bf16[4,8,32,128]{3,2,1,0:T(8,128)(2,1)S(1)} %edge_half0.6.refs_2_.first_ref), channel_id=1, source_target_pairs={{0,1},{1,2},{2,3},{3,0},{4,5},{5,6},{6,7},{7,4},{8,9},{9,10},{10,1... | collective-permute-start | bytes 786440 | tf_op jit(solution)/shard_map/ppermute | solution.py:184
  79.4 16.4 %collective-permute-start.21 = (bf16[4,8,32,128]{3,2,1,0:T(8,128)(2,1)S(1)}, bf16[4,8,32,128]{3,2,1,0:T(8,128)(2,1)S(1)}, u32[]{:S(2)}, u32[]{:S(2)}) collective-permute-start(bf16[4,8,32,128]{3,2,1,0:T(8,128)(2,1)S(1)} %edge_half0.6.refs_2_.first_ref), channel_id=1, source_target_pairs={{1,0},{2,1},{3,2},{0,3},{5,4},{6,5},{7,6},{4,7},{9,8},{10,9},{11,1... | collective-permute-start | bytes 786440 | tf_op jit(solution)/shard_map/ppermute | solution.py:184
  83.3 5.3 %collective-permute-start.25 = (bf16[3,8,32,128]{3,2,1,0:T(8,128)(2,1)S(1)}, bf16[3,8,32,128]{3,2,1,0:T(8,128)(2,1)S(1)}, u32[]{:S(2)}, u32[]{:S(2)}) collective-permute-start(bf16[3,8,32,128]{3,2,1,0:T(8,128)(2,1)S(1)} %pad_maximum_fusion.11.refs_5_), channel_id=1, source_target_pairs={{4,0},{8,4},{12,8},{16,12},{20,16},{24,20},{28,24},{0,28},{5,1},{9... | collective-permute-start | bytes 589832 | tf_op jit(solution)/shard_map/ppermute | solution.py:184
  84.2 6.2 %collective-permute-start.24 = (bf16[3,8,32,128]{3,2,1,0:T(8,128)(2,1)S(1)}, bf16[3,8,32,128]{3,2,1,0:T(8,128)(2,1)S(1)}, u32[]{:S(2)}, u32[]{:S(2)}) collective-permute-start(bf16[3,8,32,128]{3,2,1,0:T(8,128)(2,1)S(1)} %pad_maximum_fusion.10.refs_6_), channel_id=1, source_target_pairs={{0,4},{4,8},{8,12},{12,16},{16,20},{20,24},{24,28},{28,0},{1,5},{5... | collective-permute-start | bytes 589832 | tf_op jit(solution)/shard_map/ppermute | solution.py:184
  91.9 12.4 %collective-permute-start.28 = (bf16[4,8,32,128]{3,2,1,0:T(8,128)(2,1)S(1)}, bf16[4,8,32,128]{3,2,1,0:T(8,128)(2,1)S(1)}, u32[]{:S(2)}, u32[]{:S(2)}) collective-permute-start(bf16[4,8,32,128]{3,2,1,0:T(8,128)(2,1)S(1)} %edge_half1.6.refs_2_.second_ref), channel_id=1, source_target_pairs={{0,1},{1,2},{2,3},{3,0},{4,5},{5,6},{6,7},{7,4},{8,9},{9,10},{10,1... | collective-permute-start | bytes 786440 | tf_op jit(solution)/shard_map/ppermute | solution.py:184
  92.0 12.3 %collective-permute-start.29 = (bf16[4,8,32,128]{3,2,1,0:T(8,128)(2,1)S(1)}, bf16[4,8,32,128]{3,2,1,0:T(8,128)(2,1)S(1)}, u32[]{:S(2)}, u32[]{:S(2)}) collective-permute-start(bf16[4,8,32,128]{3,2,1,0:T(8,128)(2,1)S(1)} %edge_half1.6.refs_2_.second_ref), channel_id=1, source_target_pairs={{1,0},{2,1},{3,2},{0,3},{5,4},{6,5},{7,6},{4,7},{9,8},{10,9},{11,1... | collective-permute-start | bytes 786440 | tf_op jit(solution)/shard_map/ppermute | solution.py:184
  95.9 5.3 %collective-permute-start.27 = (bf16[3,8,32,128]{3,2,1,0:T(8,128)(2,1)S(1)}, bf16[3,8,32,128]{3,2,1,0:T(8,128)(2,1)S(1)}, u32[]{:S(2)}, u32[]{:S(2)}) collective-permute-start(bf16[3,8,32,128]{3,2,1,0:T(8,128)(2,1)S(1)} %pad_maximum_fusion.13.refs_5_), channel_id=1, source_target_pairs={{4,0},{8,4},{12,8},{16,12},{20,16},{24,20},{28,24},{0,28},{5,1},{9... | collective-permute-start | bytes 589832 | tf_op jit(solution)/shard_map/ppermute | solution.py:184
  96.5 6.2 %collective-permute-start.26 = (bf16[3,8,32,128]{3,2,1,0:T(8,128)(2,1)S(1)}, bf16[3,8,32,128]{3,2,1,0:T(8,128)(2,1)S(1)}, u32[]{:S(2)}, u32[]{:S(2)}) collective-permute-start(bf16[3,8,32,128]{3,2,1,0:T(8,128)(2,1)S(1)} %pad_maximum_fusion.12.refs_6_), channel_id=1, source_target_pairs={{0,4},{4,8},{8,12},{12,16},{16,20},{20,24},{24,28},{28,0},{1,5},{5... | collective-permute-start | bytes 589832 | tf_op jit(solution)/shard_map/ppermute | solution.py:184
  104.4 6.9 %collective-permute-start.31 = (bf16[3,8,32,128]{3,2,1,0:T(8,128)(2,1)S(1)}, bf16[3,8,32,128]{3,2,1,0:T(8,128)(2,1)S(1)}, u32[]{:S(2)}, u32[]{:S(2)}) collective-permute-start(bf16[3,8,32,128]{3,2,1,0:T(8,128)(2,1)S(1)} %pad_maximum_fusion.15.refs_5_), channel_id=1, source_target_pairs={{4,0},{8,4},{12,8},{16,12},{20,16},{24,20},{28,24},{0,28},{5,1},{9... | collective-permute-start | bytes 589832 | tf_op jit(solution)/shard_map/ppermute | solution.py:184
  106.8 6.5 %collective-permute-start.30 = (bf16[3,8,32,128]{3,2,1,0:T(8,128)(2,1)S(1)}, bf16[3,8,32,128]{3,2,1,0:T(8,128)(2,1)S(1)}, u32[]{:S(2)}, u32[]{:S(2)}) collective-permute-start(bf16[3,8,32,128]{3,2,1,0:T(8,128)(2,1)S(1)} %pad_maximum_fusion.14.refs_6_), channel_id=1, source_target_pairs={{0,4},{4,8},{8,12},{12,16},{16,20},{20,24},{24,28},{28,0},{1,5},{5... | collective-permute-start | bytes 589832 | tf_op jit(solution)/shard_map/ppermute | solution.py:184

commit v8 on v7

--- a/solution.py
+++ b/solution.py
@@ -9,6 +9,7 @@
 
 STEPS = 4
 HALVES = 2
+WEIGHT = 100
 VMEM_LIMIT = 4 * 1024 * 1024
 VMEM = pl.BlockSpec(memory_space=pltpu.VMEM)
 ANY = pl.BlockSpec(memory_space=pl.ANY)
@@ -167,7 +168,7 @@
         out_shape=jax.ShapeDtypeStruct((kept, faces, rows, lanes), jnp.bfloat16),
         scratch_shapes=[pltpu.VMEM((3 * (columns + 2) * faces, rows, lanes), jnp.bfloat16)],
         cost_estimate=pl.CostEstimate(
-            flops=2 * done * faces * width * depth * lanes,
+            flops=WEIGHT * 2 * done * faces * width * depth * lanes,
             bytes_accessed=2 * done * faces * width * depth,
             transcendentals=0,
         ),
@@ -234,6 +235,7 @@
     latest = current[0]
     lows = [shift(current[h], "azim", True) for h in range(HALVES)]
     highs = [shift(current[h], "azim", False) for h in range(HALVES)]
+    waiting = None
     for index in range(STEPS):
         previous = tuple(current)
         for h in range(HALVES):
@@ -241,13 +243,17 @@
             to_low, to_high = edges(*pieces, latest)
             stream = (shift(to_high, "stream", True), shift(to_low, "stream", False))
             middle = part(h, table, blocks, pieces, (to_low, to_high))
+            if waiting is not None:
+                held, _ = lax.optimization_barrier((current[waiting], middle))
+                highs[waiting] = shift(held, "azim", False)
             after = middle
             if h == 1 and index > 0:
                 basis, after = unpack(index - 1, every, *previous, basis, middle)
             current[h] = latest = part(h, table, blocks, pieces, (*stream, middle, after))
+            waiting = None
             if index < STEPS - 1:
                 lows[h] = shift(current[h], "azim", True)
-                highs[h] = shift(current[h], "azim", False)
+                waiting = h
     basis, _ = unpack(STEPS - 1, every, *current, basis, None)
     return basis.reshape(STEPS, columns, around, faces, width, lanes)
 

time: 116 us -> 124 us (1.069)
  starting transfers between devices: 40 us -> 46.2 us
  waiting for transfers between devices: 40.4 us -> 42 us
    ppermute x32, starting transfers between devices: 40 us -> 46.2 us  [shift(): return lax.ppermute(value, axis, pairs)]
    ppermute x32, waiting for transfers between devices: 40.4 us -> 42 us  [shift(): return lax.ppermute(value, axis, pairs)]
  transfers between devices with their start and end apart: 32 -> 32, of which waited for: 17 -> 12; matrix products, arithmetic and copies ran while one was open for 1% -> 1% of each run, Pallas kernels for 25% -> 23%
where the time goes in v8:
time: 124 us
  starting transfers between devices  46.2 us (37%)
  waiting for transfers between devices  42 us (34%)
  Pallas kernels  31.8 us (26%)
  local copies, waits for them, and re-layouts  3.18 us (3%)
    ppermute x32, starting transfers between devices, shift(): return lax.ppermute(value, axis, pairs)  46.2 us
    ppermute x32, waiting for transfers between devices, shift(): return lax.ppermute(value, axis, pairs)  42 us
    pallas_call x16, Pallas kernels, part(): pl.pallas_call(functools.partial(part_kernel, half), in_specs=in_specs, o...  24.7 us
    pallas_call x4, Pallas kernels, unpack(): pl.pallas_call(functools.partial(unpack_kernel, index, chosen, skipped),...  4.25 us
    unnamed x6, local copies, waits for them, and re-layouts  2.93 us
    pallas_call x1, Pallas kernels, halves_of_rows(): pl.pallas_call(halves_kernel, in_specs=[VMEM], out_specs=VMEM, out_shape=...  2.72 us
  transfers between devices with their start and end apart: 32, of which 12 were waited for; matrix products, arithmetic and copies ran while one was open for 1% of the time, Pallas kernels for 23%

profile of v8, /device:TPU:0, one launch (start us, length us, event | category | flops | bytes accessed | tf_op | source)
XLA Modules:
  0.0 124.1 jit_solution(12450521309750034825)
XLA Ops:
  0.0 1.0 copy-done.1
  1.0 0.2 pack.1
  1.2 3.1 %collective-permute-start = (bf16[4,8,32,128]{3,2,1,0:T(8,128)(2,1)S(1)}, bf16[4,8,32,128]{3,2,1,0:T(8,128)(2,1)S(1)}, u32[]{:S(2)}, u32[]{:S(2)}) collective-permute-start(bf16[4,8,32,128]{3,2,1,0:T(8,128)(2,1)S(1)} %get-tuple-element.46.refs_2_), channel_id=1, source_target_pairs={{0,1},{1,2},{2,3},{3,0},{4,5},{5,6},{6,7},{7,4},{8,9},{9,10},{10,1... | collective-permute-start | bytes 786440 | tf_op jit(solution)/shard_map/ppermute | solution.py:185
  4.3 2.1 %collective-permute-start.1 = (bf16[4,8,32,128]{3,2,1,0:T(8,128)(2,1)S(1)}, bf16[4,8,32,128]{3,2,1,0:T(8,128)(2,1)S(1)}, u32[]{:S(2)}, u32[]{:S(2)}) collective-permute-start(bf16[4,8,32,128]{3,2,1,0:T(8,128)(2,1)S(1)} %get-tuple-element.46.refs_2_), channel_id=1, source_target_pairs={{1,0},{2,1},{3,2},{0,3},{5,4},{6,5},{7,6},{4,7},{9,8},{10,9},{11,1... | collective-permute-start | bytes 786440 | tf_op jit(solution)/shard_map/ppermute | solution.py:185
  6.4 3.8 %collective-permute-start.6 = (bf16[4,8,32,128]{3,2,1,0:T(8,128)(2,1)S(1)}, bf16[4,8,32,128]{3,2,1,0:T(8,128)(2,1)S(1)}, u32[]{:S(2)}, u32[]{:S(2)}) collective-permute-start(bf16[4,8,32,128]{3,2,1,0:T(8,128)(2,1)S(1)} %get-tuple-element.50.refs_2_), channel_id=1, source_target_pairs={{1,0},{2,1},{3,2},{0,3},{5,4},{6,5},{7,6},{4,7},{9,8},{10,9},{11,1... | collective-permute-start | bytes 786440 | tf_op jit(solution)/shard_map/ppermute | solution.py:185
  10.2 1.9 %copy-done = bf16[4,1,8,64,768]{4,3,2,1,0:T(8,128)(2,1)S(1)} copy-done((bf16[4,1,8,64,768]{4,3,2,1,0:T(8,128)(2,1)S(1)}, bf16[4,1,8,64,768]{4,3,2,1,0:T(8,128)(2,1)}, u32[]{:S(2)}) %copy-start) | copy-done | bytes 3145752
  12.1 2.7 %halves_of_rows.1.refs_1_ = bf16[4,8,64,768]{3,2,1,0:T(8,128)(2,1)S(1)} custom-call(bf16[4,8,64,768]{3,2,1,0:T(8,128)(2,1)S(1)} %bitcast.29), custom_call_target="tpu_custom_call" | custom-call | tf_op jit(solution)/shard_map/halves_of_rows/pallas_call | solution.py:216
  14.9 4.4 %collective-permute-done.1.refs_4_ = bf16[4,8,32,128]{3,2,1,0:T(8,128)(2,1)S(1)} collective-permute-done((bf16[4,8,32,128]{3,2,1,0:T(8,128)(2,1)S(1)}, bf16[4,8,32,128]{3,2,1,0:T(8,128)(2,1)S(1)}, u32[]{:S(2)}, u32[]{:S(2)}) %collective-permute-start.1) | collective-permute-done | bytes 262176 | tf_op jit(solution)/shard_map/ppermute | solution.py:185
  19.4 0.1 collective-permute-start.3
  19.5 0.5 collective-permute-start.2
  20.0 1.5 %inner_half0.4.refs_7_.refs_8_ = bf16[2,8,32,128]{3,2,1,0:T(8,128)(2,1)S(1)} custom-call(s32[8,12]{1,0:T(8,128)S(1)} %fusion.4.refs_0_, bf16[4,8,64,768]{3,2,1,0:T(8,128)(2,1)S(1)} %halves_of_rows.1.refs_1_, bf16[4,8,32,128]{3,2,1,0:T(8,128)(2,1)S(1)} %get-tuple-element.46.refs_2_, bf16[4,8,32,128]{3,2,1,0:T(8,128)(2,1)S(1)} %collective-permute-done.refs_3_, ...), custom_call_target="tpu_custom_call" | custom-call | flops 20132659200 | bytes 1572864 | tf_op jit(solution)/shard_map/inner_half0/pallas_call | solution.py:164
  21.5 1.9 %collective-permute-done.3.refs_6_ = bf16[3,8,32,128]{3,2,1,0:T(8,128)(2,1)S(1)} collective-permute-done((bf16[3,8,32,128]{3,2,1,0:T(8,128)(2,1)S(1)}, bf16[3,8,32,128]{3,2,1,0:T(8,128)(2,1)S(1)}, u32[]{:S(2)}, u32[]{:S(2)}) %collective-permute-start.3) | collective-permute-done | bytes 196640 | tf_op jit(solution)/shard_map/ppermute | solution.py:185
  23.4 4.2 %collective-permute-done.2.refs_5_ = bf16[3,8,32,128]{3,2,1,0:T(8,128)(2,1)S(1)} collective-permute-done((bf16[3,8,32,128]{3,2,1,0:T(8,128)(2,1)S(1)}, bf16[3,8,32,128]{3,2,1,0:T(8,128)(2,1)S(1)}, u32[]{:S(2)}, u32[]{:S(2)}) %collective-permute-start.2) | collective-permute-done | bytes 196640 | tf_op jit(solution)/shard_map/ppermute | solution.py:185
  27.7 1.6 %edge_half0.4.refs_2_.first_ref = bf16[4,8,32,128]{3,2,1,0:T(8,128)(2,1)S(1)} custom-call(s32[8,12]{1,0:T(8,128)S(1)} %fusion.4.refs_0_, bf16[4,8,64,768]{3,2,1,0:T(8,128)(2,1)S(1)} %halves_of_rows.1.refs_1_, bf16[4,8,32,128]{3,2,1,0:T(8,128)(2,1)S(1)} %get-tuple-element.46.refs_2_, bf16[4,8,32,128]{3,2,1,0:T(8,128)(2,1)S(1)} %collective-permute-done.refs_3_, ...), custom_call_target="tpu_custom_call" | custom-call | flops 20132659200 | bytes 1572864 | tf_op jit(solution)/shard_map/edge_half0/pallas_call | solution.py:164
  29.2 0.7 collective-permute-start.4
  30.0 0.1 collective-permute-start.8
  30.1 2.7 %collective-permute-start.9 = (bf16[3,8,32,128]{3,2,1,0:T(8,128)(2,1)S(1)}, bf16[3,8,32,128]{3,2,1,0:T(8,128)(2,1)S(1)}, u32[]{:S(2)}, u32[]{:S(2)}) collective-permute-start(bf16[3,8,32,128]{3,2,1,0:T(8,128)(2,1)S(1)} %pad_maximum_fusion.2.refs_5_), channel_id=1, source_target_pairs={{4,0},{8,4},{12,8},{16,12},{20,16},{24,20},{28,24},{0,28},{5,1},{9... | collective-permute-start | bytes 589832 | tf_op jit(solution)/shard_map/ppermute | solution.py:185
  32.8 1.5 %inner_half1.4.refs_7_.refs_8_ = bf16[2,8,32,128]{3,2,1,0:T(8,128)(2,1)S(1)} custom-call(s32[8,12]{1,0:T(8,128)S(1)} %fusion.4.refs_0_, bf16[4,8,64,768]{3,2,1,0:T(8,128)(2,1)S(1)} %halves_of_rows.1.refs_1_, bf16[4,8,32,128]{3,2,1,0:T(8,128)(2,1)S(1)} %get-tuple-element.50.refs_2_, bf16[4,8,32,128]{3,2,1,0:T(8,128)(2,1)S(1)} %collective-permute-done.5.refs_3_, ...), custom_call_target="tpu_custom_call" | custom-call | flops 20132659200 | bytes 1572864 | tf_op jit(solution)/shard_map/inner_half1/pallas_call | solution.py:164
  34.3 3.2 %collective-permute-start.7 = (bf16[4,8,32,128]{3,2,1,0:T(8,128)(2,1)S(1)}, bf16[4,8,32,128]{3,2,1,0:T(8,128)(2,1)S(1)}, u32[]{:S(2)}, u32[]{:S(2)}) collective-permute-start(bf16[4,8,32,128]{3,2,1,0:T(8,128)(2,1)S(1)} %edge_half0.4.refs_2_.first_ref), channel_id=1, source_target_pairs={{1,0},{2,1},{3,2},{0,3},{5,4},{6,5},{7,6},{4,7},{9,8},{10,9},{11,1... | collective-permute-start | bytes 786440 | tf_op jit(solution)/shard_map/ppermute | solution.py:185
  37.5 1.6 %edge_half1.4.refs_2_.second_ref = bf16[4,8,32,128]{3,2,1,0:T(8,128)(2,1)S(1)} custom-call(s32[8,12]{1,0:T(8,128)S(1)} %fusion.4.refs_0_, bf16[4,8,64,768]{3,2,1,0:T(8,128)(2,1)S(1)} %halves_of_rows.1.refs_1_, bf16[4,8,32,128]{3,2,1,0:T(8,128)(2,1)S(1)} %get-tuple-element.50.refs_2_, bf16[4,8,32,128]{3,2,1,0:T(8,128)(2,1)S(1)} %collective-permute-done.5.refs_3_, ...), custom_call_target="tpu_custom_call" | custom-call | flops 20132659200 | bytes 1572864 | tf_op jit(solution)/shard_map/edge_half1/pallas_call | solution.py:164
  39.1 0.1 collective-permute-start.13
  39.2 4.1 %collective-permute-done.7.refs_4_ = bf16[4,8,32,128]{3,2,1,0:T(8,128)(2,1)S(1)} collective-permute-done((bf16[4,8,32,128]{3,2,1,0:T(8,128)(2,1)S(1)}, bf16[4,8,32,128]{3,2,1,0:T(8,128)(2,1)S(1)}, u32[]{:S(2)}, u32[]{:S(2)}) %collective-permute-start.7) | collective-permute-done | bytes 262176 | tf_op jit(solution)/shard_map/ppermute | solution.py:185
  43.3 1.0 collective-permute-start.11
  44.3 0.1 collective-permute-start.10
  44.4 1.5 %inner_half0.5.refs_7_.refs_8_ = bf16[2,8,32,128]{3,2,1,0:T(8,128)(2,1)S(1)} custom-call(s32[8,12]{1,0:T(8,128)S(1)} %fusion.4.refs_0_, bf16[4,8,64,768]{3,2,1,0:T(8,128)(2,1)S(1)} %halves_of_rows.1.refs_1_, bf16[4,8,32,128]{3,2,1,0:T(8,128)(2,1)S(1)} %edge_half0.4.refs_2_.first_ref, bf16[4,8,32,128]{3,2,1,0:T(8,128)(2,1)S(1)} %collective-permute-done.4.refs_3_, ...), custom_call_target="tpu_custom_call" | custom-call | flops 20132659200 | bytes 1572864 | tf_op jit(solution)/shard_map/inner_half0/pallas_call | solution.py:164
  45.9 3.5 %collective-permute-start.14 = (bf16[4,8,32,128]{3,2,1,0:T(8,128)(2,1)S(1)}, bf16[4,8,32,128]{3,2,1,0:T(8,128)(2,1)S(1)}, u32[]{:S(2)}, u32[]{:S(2)}) collective-permute-start(bf16[4,8,32,128]{3,2,1,0:T(8,128)(2,1)S(1)} %edge_half1.4.refs_2_.second_ref), channel_id=1, source_target_pairs={{1,0},{2,1},{3,2},{0,3},{5,4},{6,5},{7,6},{4,7},{9,8},{10,9},{11,1... | collective-permute-start | bytes 786440 | tf_op jit(solution)/shard_map/ppermute | solution.py:185
  49.4 2.4 %collective-permute-done.10.refs_5_ = bf16[3,8,32,128]{3,2,1,0:T(8,128)(2,1)S(1)} collective-permute-done((bf16[3,8,32,128]{3,2,1,0:T(8,128)(2,1)S(1)}, bf16[3,8,32,128]{3,2,1,0:T(8,128)(2,1)S(1)}, u32[]{:S(2)}, u32[]{:S(2)}) %collective-permute-start.10) | collective-permute-done | bytes 196640 | tf_op jit(solution)/shard_map/ppermute | solution.py:185
  51.9 1.6 %edge_half0.5.refs_2_.first_ref = bf16[4,8,32,128]{3,2,1,0:T(8,128)(2,1)S(1)} custom-call(s32[8,12]{1,0:T(8,128)S(1)} %fusion.4.refs_0_, bf16[4,8,64,768]{3,2,1,0:T(8,128)(2,1)S(1)} %halves_of_rows.1.refs_1_, bf16[4,8,32,128]{3,2,1,0:T(8,128)(2,1)S(1)} %edge_half0.4.refs_2_.first_ref, bf16[4,8,32,128]{3,2,1,0:T(8,128)(2,1)S(1)} %collective-permute-done.4.refs_3_, ...), custom_call_target="tpu_custom_call" | custom-call | flops 20132659200 | bytes 1572864 | tf_op jit(solution)/shard_map/edge_half0/pallas_call | solution.py:164
  53.5 0.5 collective-permute-start.12
  53.9 2.2 %collective-permute-done.14.refs_4_ = bf16[4,8,32,128]{3,2,1,0:T(8,128)(2,1)S(1)} collective-permute-done((bf16[4,8,32,128]{3,2,1,0:T(8,128)(2,1)S(1)}, bf16[4,8,32,128]{3,2,1,0:T(8,128)(2,1)S(1)}, u32[]{:S(2)}, u32[]{:S(2)}) %collective-permute-start.14) | collective-permute-done | bytes 262176 | tf_op jit(solution)/shard_map/ppermute | solution.py:185
  56.3 0.1 collective-permute-start.16
  56.4 2.7 %collective-permute-start.17 = (bf16[3,8,32,128]{3,2,1,0:T(8,128)(2,1)S(1)}, bf16[3,8,32,128]{3,2,1,0:T(8,128)(2,1)S(1)}, u32[]{:S(2)}, u32[]{:S(2)}) collective-permute-start(bf16[3,8,32,128]{3,2,1,0:T(8,128)(2,1)S(1)} %pad_maximum_fusion.6.refs_5_), channel_id=1, source_target_pairs={{4,0},{8,4},{12,8},{16,12},{20,16},{24,20},{28,24},{0,28},{5,1},{9... | collective-permute-start | bytes 589832 | tf_op jit(solution)/shard_map/ppermute | solution.py:185
  59.0 1.5 %inner_half1.5.refs_0_.refs_7_ = bf16[2,8,32,128]{3,2,1,0:T(8,128)(2,1)S(1)} custom-call(s32[8,12]{1,0:T(8,128)S(1)} %fusion.4.refs_0_, bf16[4,8,64,768]{3,2,1,0:T(8,128)(2,1)S(1)} %halves_of_rows.1.refs_1_, bf16[4,8,32,128]{3,2,1,0:T(8,128)(2,1)S(1)} %edge_half1.4.refs_2_.second_ref, bf16[4,8,32,128]{3,2,1,0:T(8,128)(2,1)S(1)} %collective-permute-done.13.refs_3_, ...), custom_call_target="tpu_custom_call" | custom-call | flops 20132659200 | bytes 1572864 | tf_op jit(solution)/shard_map/inner_half1/pallas_call | solution.py:164
  60.5 0.9 unpack.4
  61.5 4.3 %collective-permute-start.15 = (bf16[4,8,32,128]{3,2,1,0:T(8,128)(2,1)S(1)}, bf16[4,8,32,128]{3,2,1,0:T(8,128)(2,1)S(1)}, u32[]{:S(2)}, u32[]{:S(2)}) collective-permute-start(bf16[4,8,32,128]{3,2,1,0:T(8,128)(2,1)S(1)} %edge_half0.5.refs_2_.first_ref), channel_id=1, source_target_pairs={{1,0},{2,1},{3,2},{0,3},{5,4},{6,5},{7,6},{4,7},{9,8},{10,9},{11,1... | collective-permute-start | bytes 786440 | tf_op jit(solution)/shard_map/ppermute | solution.py:185
  65.8 1.6 %edge_half1.5.refs_2_.second_ref = bf16[4,8,32,128]{3,2,1,0:T(8,128)(2,1)S(1)} custom-call(s32[8,12]{1,0:T(8,128)S(1)} %fusion.4.refs_0_, bf16[4,8,64,768]{3,2,1,0:T(8,128)(2,1)S(1)} %halves_of_rows.1.refs_1_, bf16[4,8,32,128]{3,2,1,0:T(8,128)(2,1)S(1)} %edge_half1.4.refs_2_.second_ref, bf16[4,8,32,128]{3,2,1,0:T(8,128)(2,1)S(1)} %collective-permute-done.13.refs_3_, ...), custom_call_target="tpu_custom_call" | custom-call | flops 20132659200 | bytes 1572864 | tf_op jit(solution)/shard_map/edge_half1/pallas_call | solution.py:164
  67.4 4.8 %collective-permute-done.15.refs_4_ = bf16[4,8,32,128]{3,2,1,0:T(8,128)(2,1)S(1)} collective-permute-done((bf16[4,8,32,128]{3,2,1,0:T(8,128)(2,1)S(1)}, bf16[4,8,32,128]{3,2,1,0:T(8,128)(2,1)S(1)}, u32[]{:S(2)}, u32[]{:S(2)}) %collective-permute-start.15) | collective-permute-done | bytes 262176 | tf_op jit(solution)/shard_map/ppermute | solution.py:185
  72.3 0.1 collective-permute-start.19
  72.4 0.5 collective-permute-start.18
  73.0 1.5 %inner_half0.6.refs_7_.refs_8_ = bf16[2,8,32,128]{3,2,1,0:T(8,128)(2,1)S(1)} custom-call(s32[8,12]{1,0:T(8,128)S(1)} %fusion.4.refs_0_, bf16[4,8,64,768]{3,2,1,0:T(8,128)(2,1)S(1)} %halves_of_rows.1.refs_1_, bf16[4,8,32,128]{3,2,1,0:T(8,128)(2,1)S(1)} %edge_half0.5.refs_2_.first_ref, bf16[4,8,32,128]{3,2,1,0:T(8,128)(2,1)S(1)} %collective-permute-done.12.refs_3_, ...), custom_call_target="tpu_custom_call" | custom-call | flops 20132659200 | bytes 1572864 | tf_op jit(solution)/shard_map/inner_half0/pallas_call | solution.py:164
  74.5 4.4 %collective-permute-start.22 = (bf16[4,8,32,128]{3,2,1,0:T(8,128)(2,1)S(1)}, bf16[4,8,32,128]{3,2,1,0:T(8,128)(2,1)S(1)}, u32[]{:S(2)}, u32[]{:S(2)}) collective-permute-start(bf16[4,8,32,128]{3,2,1,0:T(8,128)(2,1)S(1)} %edge_half1.5.refs_2_.second_ref), channel_id=1, source_target_pairs={{1,0},{2,1},{3,2},{0,3},{5,4},{6,5},{7,6},{4,7},{9,8},{10,9},{11,1... | collective-permute-start | bytes 786440 | tf_op jit(solution)/shard_map/ppermute | solution.py:185
  78.9 1.6 %edge_half0.6.refs_2_.first_ref = bf16[4,8,32,128]{3,2,1,0:T(8,128)(2,1)S(1)} custom-call(s32[8,12]{1,0:T(8,128)S(1)} %fusion.4.refs_0_, bf16[4,8,64,768]{3,2,1,0:T(8,128)(2,1)S(1)} %halves_of_rows.1.refs_1_, bf16[4,8,32,128]{3,2,1,0:T(8,128)(2,1)S(1)} %edge_half0.5.refs_2_.first_ref, bf16[4,8,32,128]{3,2,1,0:T(8,128)(2,1)S(1)} %collective-permute-done.12.refs_3_, ...), custom_call_target="tpu_custom_call" | custom-call | flops 20132659200 | bytes 1572864 | tf_op jit(solution)/shard_map/edge_half0/pallas_call | solution.py:164
  80.5 5.1 %collective-permute-done.22.refs_4_ = bf16[4,8,32,128]{3,2,1,0:T(8,128)(2,1)S(1)} collective-permute-done((bf16[4,8,32,128]{3,2,1,0:T(8,128)(2,1)S(1)}, bf16[4,8,32,128]{3,2,1,0:T(8,128)(2,1)S(1)}, u32[]{:S(2)}, u32[]{:S(2)}) %collective-permute-start.22) | collective-permute-done | bytes 262176 | tf_op jit(solution)/shard_map/ppermute | solution.py:185
  85.7 0.1 collective-permute-start.24
  85.8 2.7 %collective-permute-start.25 = (bf16[3,8,32,128]{3,2,1,0:T(8,128)(2,1)S(1)}, bf16[3,8,32,128]{3,2,1,0:T(8,128)(2,1)S(1)}, u32[]{:S(2)}, u32[]{:S(2)}) collective-permute-start(bf16[3,8,32,128]{3,2,1,0:T(8,128)(2,1)S(1)} %pad_maximum_fusion.10.refs_5_), channel_id=1, source_target_pairs={{4,0},{8,4},{12,8},{16,12},{20,16},{24,20},{28,24},{0,28},{5,1},{9... | collective-permute-start | bytes 589832 | tf_op jit(solution)/shard_map/ppermute | solution.py:185
  88.5 1.5 %inner_half1.6.refs_1_.refs_7_ = bf16[2,8,32,128]{3,2,1,0:T(8,128)(2,1)S(1)} custom-call(s32[8,12]{1,0:T(8,128)S(1)} %fusion.4.refs_0_, bf16[4,8,64,768]{3,2,1,0:T(8,128)(2,1)S(1)} %halves_of_rows.1.refs_1_, bf16[4,8,32,128]{3,2,1,0:T(8,128)(2,1)S(1)} %edge_half1.5.refs_2_.second_ref, bf16[4,8,32,128]{3,2,1,0:T(8,128)(2,1)S(1)} %collective-permute-done.21.refs_3_, ...), custom_call_target="tpu_custom_call" | custom-call | flops 20132659200 | bytes 1572864 | tf_op jit(solution)/shard_map/inner_half1/pallas_call | solution.py:164
  90.0 0.9 unpack.5
  90.9 4.3 %collective-permute-start.23 = (bf16[4,8,32,128]{3,2,1,0:T(8,128)(2,1)S(1)}, bf16[4,8,32,128]{3,2,1,0:T(8,128)(2,1)S(1)}, u32[]{:S(2)}, u32[]{:S(2)}) collective-permute-start(bf16[4,8,32,128]{3,2,1,0:T(8,128)(2,1)S(1)} %edge_half0.6.refs_2_.first_ref), channel_id=1, source_target_pairs={{1,0},{2,1},{3,2},{0,3},{5,4},{6,5},{7,6},{4,7},{9,8},{10,9},{11,1... | collective-permute-start | bytes 786440 | tf_op jit(solution)/shard_map/ppermute | solution.py:185
  95.3 1.6 %edge_half1.6.refs_2_.second_ref = bf16[4,8,32,128]{3,2,1,0:T(8,128)(2,1)S(1)} custom-call(s32[8,12]{1,0:T(8,128)S(1)} %fusion.4.refs_0_, bf16[4,8,64,768]{3,2,1,0:T(8,128)(2,1)S(1)} %halves_of_rows.1.refs_1_, bf16[4,8,32,128]{3,2,1,0:T(8,128)(2,1)S(1)} %edge_half1.5.refs_2_.second_ref, bf16[4,8,32,128]{3,2,1,0:T(8,128)(2,1)S(1)} %collective-permute-done.21.refs_3_, ...), custom_call_target="tpu_custom_call" | custom-call | flops 20132659200 | bytes 1572864 | tf_op jit(solution)/shard_map/edge_half1/pallas_call | solution.py:164
  96.9 4.8 %collective-permute-done.23.refs_4_ = bf16[4,8,32,128]{3,2,1,0:T(8,128)(2,1)S(1)} collective-permute-done((bf16[4,8,32,128]{3,2,1,0:T(8,128)(2,1)S(1)}, bf16[4,8,32,128]{3,2,1,0:T(8,128)(2,1)S(1)}, u32[]{:S(2)}, u32[]{:S(2)}) %collective-permute-start.23) | collective-permute-done | bytes 262176 | tf_op jit(solution)/shard_map/ppermute | solution.py:185
  101.8 0.1 collective-permute-start.27
  101.9 0.5 collective-permute-start.26
  102.4 1.5 %inner_half0.7.refs_7_.refs_8_ = bf16[2,8,32,128]{3,2,1,0:T(8,128)(2,1)S(1)} custom-call(s32[8,12]{1,0:T(8,128)S(1)} %fusion.4.refs_0_, bf16[4,8,64,768]{3,2,1,0:T(8,128)(2,1)S(1)} %halves_of_rows.1.refs_1_, bf16[4,8,32,128]{3,2,1,0:T(8,128)(2,1)S(1)} %edge_half0.6.refs_2_.first_ref, bf16[4,8,32,128]{3,2,1,0:T(8,128)(2,1)S(1)} %collective-permute-done.20.refs_3_, ...), custom_call_target="tpu_custom_call" | custom-call | flops 20132659200 | bytes 1572864 | tf_op jit(solution)/shard_map/inner_half0/pallas_call | solution.py:164
  103.9 4.4 %collective-permute-start.29 = (bf16[4,8,32,128]{3,2,1,0:T(8,128)(2,1)S(1)}, bf16[4,8,32,128]{3,2,1,0:T(8,128)(2,1)S(1)}, u32[]{:S(2)}, u32[]{:S(2)}) collective-permute-start(bf16[4,8,32,128]{3,2,1,0:T(8,128)(2,1)S(1)} %edge_half1.6.refs_2_.second_ref), channel_id=1, source_target_pairs={{1,0},{2,1},{3,2},{0,3},{5,4},{6,5},{7,6},{4,7},{9,8},{10,9},{11,1... | collective-permute-start | bytes 786440 | tf_op jit(solution)/shard_map/ppermute | solution.py:185
  108.3 1.6 %edge_half0.7.first_ref = bf16[4,8,32,128]{3,2,1,0:T(8,128)(2,1)S(1)} custom-call(s32[8,12]{1,0:T(8,128)S(1)} %fusion.4.refs_0_, bf16[4,8,64,768]{3,2,1,0:T(8,128)(2,1)S(1)} %halves_of_rows.1.refs_1_, bf16[4,8,32,128]{3,2,1,0:T(8,128)(2,1)S(1)} %edge_half0.6.refs_2_.first_ref, bf16[4,8,32,128]{3,2,1,0:T(8,128)(2,1)S(1)} %collective-permute-done.20.refs_3_, ...), custom_call_target="tpu_custom_call" | custom-call | flops 20132659200 | bytes 1572864 | tf_op jit(solution)/shard_map/edge_half0/pallas_call | solution.py:164
  109.9 4.2 %collective-permute-done.29.refs_4_ = bf16[4,8,32,128]{3,2,1,0:T(8,128)(2,1)S(1)} collective-permute-done((bf16[4,8,32,128]{3,2,1,0:T(8,128)(2,1)S(1)}, bf16[4,8,32,128]{3,2,1,0:T(8,128)(2,1)S(1)}, u32[]{:S(2)}, u32[]{:S(2)}) %collective-permute-start.29) | collective-permute-done | bytes 262176 | tf_op jit(solution)/shard_map/ppermute | solution.py:185
  114.1 0.1 collective-permute-start.31
  114.2 0.5 collective-permute-start.30
  114.7 1.5 %inner_half1.7.refs_1_.refs_7_ = bf16[2,8,32,128]{3,2,1,0:T(8,128)(2,1)S(1)} custom-call(s32[8,12]{1,0:T(8,128)S(1)} %fusion.4.refs_0_, bf16[4,8,64,768]{3,2,1,0:T(8,128)(2,1)S(1)} %halves_of_rows.1.refs_1_, bf16[4,8,32,128]{3,2,1,0:T(8,128)(2,1)S(1)} %edge_half1.6.refs_2_.second_ref, bf16[4,8,32,128]{3,2,1,0:T(8,128)(2,1)S(1)} %collective-permute-done.28.refs_3_, ...), custom_call_target="tpu_custom_call" | custom-call | flops 20132659200 | bytes 1572864 | tf_op jit(solution)/shard_map/inner_half1/pallas_call | solution.py:164
  116.3 0.9 unpack.6
  117.2 2.0 %collective-permute-done.31.refs_6_ = bf16[3,8,32,128]{3,2,1,0:T(8,128)(2,1)S(1)} collective-permute-done((bf16[3,8,32,128]{3,2,1,0:T(8,128)(2,1)S(1)}, bf16[3,8,32,128]{3,2,1,0:T(8,128)(2,1)S(1)}, u32[]{:S(2)}, u32[]{:S(2)}) %collective-permute-start.31) | collective-permute-done | bytes 196640 | tf_op jit(solution)/shard_map/ppermute | solution.py:185
  119.2 1.9 %collective-permute-done.30.refs_5_ = bf16[3,8,32,128]{3,2,1,0:T(8,128)(2,1)S(1)} collective-permute-done((bf16[3,8,32,128]{3,2,1,0:T(8,128)(2,1)S(1)}, bf16[3,8,32,128]{3,2,1,0:T(8,128)(2,1)S(1)}, u32[]{:S(2)}, u32[]{:S(2)}) %collective-permute-start.30) | collective-permute-done | bytes 196640 | tf_op jit(solution)/shard_map/ppermute | solution.py:185
  121.1 1.6 %edge_half1.7.second_ref = bf16[4,8,32,128]{3,2,1,0:T(8,128)(2,1)S(1)} custom-call(s32[8,12]{1,0:T(8,128)S(1)} %fusion.4.refs_0_, bf16[4,8,64,768]{3,2,1,0:T(8,128)(2,1)S(1)} %halves_of_rows.1.refs_1_, bf16[4,8,32,128]{3,2,1,0:T(8,128)(2,1)S(1)} %edge_half1.6.refs_2_.second_ref, bf16[4,8,32,128]{3,2,1,0:T(8,128)(2,1)S(1)} %collective-permute-done.28.refs_3_, ...), custom_call_target="tpu_custom_call" | custom-call | flops 20132659200 | bytes 1572864 | tf_op jit(solution)/shard_map/edge_half1/pallas_call | solution.py:164
  122.6 1.5 %unpack.7 = (bf16[4,4,8,64,128]{4,3,2,1,0:T(8,128)(2,1)}, f32[8,128]{1,0:T(8,128)}) custom-call(bf16[4,8,32,128]{3,2,1,0:T(8,128)(2,1)S(1)} %edge_half0.7.first_ref, bf16[4,8,32,128]{3,2,1,0:T(8,128)(2,1)S(1)} %edge_half1.7.second_ref, bf16[4,4,8,64,128]{4,3,2,1,0:T(8,128)(2,1)} %get-tuple-element.81.refs_0_), custom_call_target="tpu_custom_call", output_to_operand_aliasing={{0}: (2, {})} | custom-call | tf_op jit(solution)/shard_map/unpack/pallas_call | solution.py:77
  (68 shorter events, 0.9 us)
Async XLA Ops:
  0.0 1.0 copy-start.1
  1.2 13.7 %collective-permute-start = (bf16[4,8,32,128]{3,2,1,0:T(8,128)(2,1)S(1)}, bf16[4,8,32,128]{3,2,1,0:T(8,128)(2,1)S(1)}, u32[]{:S(2)}, u32[]{:S(2)}) collective-permute-start(bf16[4,8,32,128]{3,2,1,0:T(8,128)(2,1)S(1)} %get-tuple-element.46.refs_2_), channel_id=1, source_target_pairs={{0,1},{1,2},{2,3},{3,0},{4,5},{5,6},{6,7},{7,4},{8,9},{9,10},{10,1... | collective-permute-start | bytes 786440 | tf_op jit(solution)/shard_map/ppermute | solution.py:185
  4.3 15.0 %collective-permute-start.1 = (bf16[4,8,32,128]{3,2,1,0:T(8,128)(2,1)S(1)}, bf16[4,8,32,128]{3,2,1,0:T(8,128)(2,1)S(1)}, u32[]{:S(2)}, u32[]{:S(2)}) collective-permute-start(bf16[4,8,32,128]{3,2,1,0:T(8,128)(2,1)S(1)} %get-tuple-element.46.refs_2_), channel_id=1, source_target_pairs={{1,0},{2,1},{3,2},{0,3},{5,4},{6,5},{7,6},{4,7},{9,8},{10,9},{11,1... | collective-permute-start | bytes 786440 | tf_op jit(solution)/shard_map/ppermute | solution.py:185
  6.4 23.6 %collective-permute-start.5 = (bf16[4,8,32,128]{3,2,1,0:T(8,128)(2,1)S(1)}, bf16[4,8,32,128]{3,2,1,0:T(8,128)(2,1)S(1)}, u32[]{:S(2)}, u32[]{:S(2)}) collective-permute-start(bf16[4,8,32,128]{3,2,1,0:T(8,128)(2,1)S(1)} %get-tuple-element.50.refs_2_), channel_id=1, source_target_pairs={{0,1},{1,2},{2,3},{3,0},{4,5},{5,6},{6,7},{7,4},{8,9},{9,10},{10,1... | collective-permute-start | bytes 786440 | tf_op jit(solution)/shard_map/ppermute | solution.py:185
  6.4 23.6 %collective-permute-start.6 = (bf16[4,8,32,128]{3,2,1,0:T(8,128)(2,1)S(1)}, bf16[4,8,32,128]{3,2,1,0:T(8,128)(2,1)S(1)}, u32[]{:S(2)}, u32[]{:S(2)}) collective-permute-start(bf16[4,8,32,128]{3,2,1,0:T(8,128)(2,1)S(1)} %get-tuple-element.50.refs_2_), channel_id=1, source_target_pairs={{1,0},{2,1},{3,2},{0,3},{5,4},{6,5},{7,6},{4,7},{9,8},{10,9},{11,1... | collective-permute-start | bytes 786440 | tf_op jit(solution)/shard_map/ppermute | solution.py:185
  10.2 1.9 %copy-start = (bf16[4,1,8,64,768]{4,3,2,1,0:T(8,128)(2,1)S(1)}, bf16[4,1,8,64,768]{4,3,2,1,0:T(8,128)(2,1)}, u32[]{:S(2)}) copy-start(bf16[4,1,8,64,768]{4,3,2,1,0:T(8,128)(2,1)} %param.4) | copy-start | bytes 9437188
  12.1 2.7 %copy-start.2 = (s32[1,8,12]{2,1,0:T(8,128)S(1)}, s32[1,8,12]{2,1,0:T(8,128)}, u32[]{:S(2)}) copy-start(s32[1,8,12]{2,1,0:T(8,128)} %param.5) | copy-start | bytes 1156
  19.4 4.1 %collective-permute-start.3 = (bf16[3,8,32,128]{3,2,1,0:T(8,128)(2,1)S(1)}, bf16[3,8,32,128]{3,2,1,0:T(8,128)(2,1)S(1)}, u32[]{:S(2)}, u32[]{:S(2)}) collective-permute-start(bf16[3,8,32,128]{3,2,1,0:T(8,128)(2,1)S(1)} %pad_maximum_fusion.1.refs_5_), channel_id=1, source_target_pairs={{4,0},{8,4},{12,8},{16,12},{20,16},{24,20},{28,24},{0,28},{5,1},{9... | collective-permute-start | bytes 589832 | tf_op jit(solution)/shard_map/ppermute | solution.py:185
  19.5 8.2 %collective-permute-start.2 = (bf16[3,8,32,128]{3,2,1,0:T(8,128)(2,1)S(1)}, bf16[3,8,32,128]{3,2,1,0:T(8,128)(2,1)S(1)}, u32[]{:S(2)}, u32[]{:S(2)}) collective-permute-start(bf16[3,8,32,128]{3,2,1,0:T(8,128)(2,1)S(1)} %pad_maximum_fusion.refs_6_), channel_id=1, source_target_pairs={{0,4},{4,8},{8,12},{12,16},{16,20},{20,24},{24,28},{28,0},{1,5},{5... | collective-permute-start | bytes 589832 | tf_op jit(solution)/shard_map/ppermute | solution.py:185
  29.2 14.0 %collective-permute-start.4 = (bf16[4,8,32,128]{3,2,1,0:T(8,128)(2,1)S(1)}, bf16[4,8,32,128]{3,2,1,0:T(8,128)(2,1)S(1)}, u32[]{:S(2)}, u32[]{:S(2)}) collective-permute-start(bf16[4,8,32,128]{3,2,1,0:T(8,128)(2,1)S(1)} %edge_half0.4.refs_2_.first_ref), channel_id=1, source_target_pairs={{0,1},{1,2},{2,3},{3,0},{4,5},{5,6},{6,7},{7,4},{8,9},{9,10},{10,1... | collective-permute-start | bytes 786440 | tf_op jit(solution)/shard_map/ppermute | solution.py:185
  30.0 7.5 %collective-permute-start.8 = (bf16[3,8,32,128]{3,2,1,0:T(8,128)(2,1)S(1)}, bf16[3,8,32,128]{3,2,1,0:T(8,128)(2,1)S(1)}, u32[]{:S(2)}, u32[]{:S(2)}) collective-permute-start(bf16[3,8,32,128]{3,2,1,0:T(8,128)(2,1)S(1)} %pad_maximum_fusion.3.refs_6_), channel_id=1, source_target_pairs={{0,4},{4,8},{8,12},{12,16},{16,20},{20,24},{24,28},{28,0},{1,5},{5... | collective-permute-start | bytes 589832 | tf_op jit(solution)/shard_map/ppermute | solution.py:185
  30.1 7.4 %collective-permute-start.9 = (bf16[3,8,32,128]{3,2,1,0:T(8,128)(2,1)S(1)}, bf16[3,8,32,128]{3,2,1,0:T(8,128)(2,1)S(1)}, u32[]{:S(2)}, u32[]{:S(2)}) collective-permute-start(bf16[3,8,32,128]{3,2,1,0:T(8,128)(2,1)S(1)} %pad_maximum_fusion.2.refs_5_), channel_id=1, source_target_pairs={{4,0},{8,4},{12,8},{16,12},{20,16},{24,20},{28,24},{0,28},{5,1},{9... | collective-permute-start | bytes 589832 | tf_op jit(solution)/shard_map/ppermute | solution.py:185
  34.3 8.9 %collective-permute-start.7 = (bf16[4,8,32,128]{3,2,1,0:T(8,128)(2,1)S(1)}, bf16[4,8,32,128]{3,2,1,0:T(8,128)(2,1)S(1)}, u32[]{:S(2)}, u32[]{:S(2)}) collective-permute-start(bf16[4,8,32,128]{3,2,1,0:T(8,128)(2,1)S(1)} %edge_half0.4.refs_2_.first_ref), channel_id=1, source_target_pairs={{1,0},{2,1},{3,2},{0,3},{5,4},{6,5},{7,6},{4,7},{9,8},{10,9},{11,1... | collective-permute-start | bytes 786440 | tf_op jit(solution)/shard_map/ppermute | solution.py:185
  39.1 14.8 %collective-permute-start.13 = (bf16[4,8,32,128]{3,2,1,0:T(8,128)(2,1)S(1)}, bf16[4,8,32,128]{3,2,1,0:T(8,128)(2,1)S(1)}, u32[]{:S(2)}, u32[]{:S(2)}) collective-permute-start(bf16[4,8,32,128]{3,2,1,0:T(8,128)(2,1)S(1)} %edge_half1.4.refs_2_.second_ref), channel_id=1, source_target_pairs={{0,1},{1,2},{2,3},{3,0},{4,5},{5,6},{6,7},{7,4},{8,9},{9,10},{10,1... | collective-permute-start | bytes 786440 | tf_op jit(solution)/shard_map/ppermute | solution.py:185
  43.3 6.1 %collective-permute-start.11 = (bf16[3,8,32,128]{3,2,1,0:T(8,128)(2,1)S(1)}, bf16[3,8,32,128]{3,2,1,0:T(8,128)(2,1)S(1)}, u32[]{:S(2)}, u32[]{:S(2)}) collective-permute-start(bf16[3,8,32,128]{3,2,1,0:T(8,128)(2,1)S(1)} %pad_maximum_fusion.5.refs_5_), channel_id=1, source_target_pairs={{4,0},{8,4},{12,8},{16,12},{20,16},{24,20},{28,24},{0,28},{5,1},{9... | collective-permute-start | bytes 589832 | tf_op jit(solution)/shard_map/ppermute | solution.py:185
  44.3 7.5 %collective-permute-start.10 = (bf16[3,8,32,128]{3,2,1,0:T(8,128)(2,1)S(1)}, bf16[3,8,32,128]{3,2,1,0:T(8,128)(2,1)S(1)}, u32[]{:S(2)}, u32[]{:S(2)}) collective-permute-start(bf16[3,8,32,128]{3,2,1,0:T(8,128)(2,1)S(1)} %pad_maximum_fusion.4.refs_6_), channel_id=1, source_target_pairs={{0,4},{4,8},{8,12},{12,16},{16,20},{20,24},{24,28},{28,0},{1,5},{5... | collective-permute-start | bytes 589832 | tf_op jit(solution)/shard_map/ppermute | solution.py:185
  45.9 10.3 %collective-permute-start.14 = (bf16[4,8,32,128]{3,2,1,0:T(8,128)(2,1)S(1)}, bf16[4,8,32,128]{3,2,1,0:T(8,128)(2,1)S(1)}, u32[]{:S(2)}, u32[]{:S(2)}) collective-permute-start(bf16[4,8,32,128]{3,2,1,0:T(8,128)(2,1)S(1)} %edge_half1.4.refs_2_.second_ref), channel_id=1, source_target_pairs={{1,0},{2,1},{3,2},{0,3},{5,4},{6,5},{7,6},{4,7},{9,8},{10,9},{11,1... | collective-permute-start | bytes 786440 | tf_op jit(solution)/shard_map/ppermute | solution.py:185
  53.5 14.0 %collective-permute-start.12 = (bf16[4,8,32,128]{3,2,1,0:T(8,128)(2,1)S(1)}, bf16[4,8,32,128]{3,2,1,0:T(8,128)(2,1)S(1)}, u32[]{:S(2)}, u32[]{:S(2)}) collective-permute-start(bf16[4,8,32,128]{3,2,1,0:T(8,128)(2,1)S(1)} %edge_half0.5.refs_2_.first_ref), channel_id=1, source_target_pairs={{0,1},{1,2},{2,3},{3,0},{4,5},{5,6},{6,7},{7,4},{8,9},{9,10},{10,1... | collective-permute-start | bytes 786440 | tf_op jit(solution)/shard_map/ppermute | solution.py:185
  56.3 9.5 %collective-permute-start.16 = (bf16[3,8,32,128]{3,2,1,0:T(8,128)(2,1)S(1)}, bf16[3,8,32,128]{3,2,1,0:T(8,128)(2,1)S(1)}, u32[]{:S(2)}, u32[]{:S(2)}) collective-permute-start(bf16[3,8,32,128]{3,2,1,0:T(8,128)(2,1)S(1)} %pad_maximum_fusion.7.refs_6_), channel_id=1, source_target_pairs={{0,4},{4,8},{8,12},{12,16},{16,20},{20,24},{24,28},{28,0},{1,5},{5... | collective-permute-start | bytes 589832 | tf_op jit(solution)/shard_map/ppermute | solution.py:185
  56.4 9.5 %collective-permute-start.17 = (bf16[3,8,32,128]{3,2,1,0:T(8,128)(2,1)S(1)}, bf16[3,8,32,128]{3,2,1,0:T(8,128)(2,1)S(1)}, u32[]{:S(2)}, u32[]{:S(2)}) collective-permute-start(bf16[3,8,32,128]{3,2,1,0:T(8,128)(2,1)S(1)} %pad_maximum_fusion.6.refs_5_), channel_id=1, source_target_pairs={{4,0},{8,4},{12,8},{16,12},{20,16},{24,20},{28,24},{0,28},{5,1},{9... | collective-permute-start | bytes 589832 | tf_op jit(solution)/shard_map/ppermute | solution.py:185
  61.5 10.8 %collective-permute-start.15 = (bf16[4,8,32,128]{3,2,1,0:T(8,128)(2,1)S(1)}, bf16[4,8,32,128]{3,2,1,0:T(8,128)(2,1)S(1)}, u32[]{:S(2)}, u32[]{:S(2)}) collective-permute-start(bf16[4,8,32,128]{3,2,1,0:T(8,128)(2,1)S(1)} %edge_half0.5.refs_2_.first_ref), channel_id=1, source_target_pairs={{1,0},{2,1},{3,2},{0,3},{5,4},{6,5},{7,6},{4,7},{9,8},{10,9},{11,1... | collective-permute-start | bytes 786440 | tf_op jit(solution)/shard_map/ppermute | solution.py:185
  67.4 13.2 %collective-permute-start.21 = (bf16[4,8,32,128]{3,2,1,0:T(8,128)(2,1)S(1)}, bf16[4,8,32,128]{3,2,1,0:T(8,128)(2,1)S(1)}, u32[]{:S(2)}, u32[]{:S(2)}) collective-permute-start(bf16[4,8,32,128]{3,2,1,0:T(8,128)(2,1)S(1)} %edge_half1.5.refs_2_.second_ref), channel_id=1, source_target_pairs={{0,1},{1,2},{2,3},{3,0},{4,5},{5,6},{6,7},{7,4},{8,9},{9,10},{10,1... | collective-permute-start | bytes 786440 | tf_op jit(solution)/shard_map/ppermute | solution.py:185
  72.3 6.6 %collective-permute-start.19 = (bf16[3,8,32,128]{3,2,1,0:T(8,128)(2,1)S(1)}, bf16[3,8,32,128]{3,2,1,0:T(8,128)(2,1)S(1)}, u32[]{:S(2)}, u32[]{:S(2)}) collective-permute-start(bf16[3,8,32,128]{3,2,1,0:T(8,128)(2,1)S(1)} %pad_maximum_fusion.9.refs_5_), channel_id=1, source_target_pairs={{4,0},{8,4},{12,8},{16,12},{20,16},{24,20},{28,24},{0,28},{5,1},{9... | collective-permute-start | bytes 589832 | tf_op jit(solution)/shard_map/ppermute | solution.py:185
  72.4 6.5 %collective-permute-start.18 = (bf16[3,8,32,128]{3,2,1,0:T(8,128)(2,1)S(1)}, bf16[3,8,32,128]{3,2,1,0:T(8,128)(2,1)S(1)}, u32[]{:S(2)}, u32[]{:S(2)}) collective-permute-start(bf16[3,8,32,128]{3,2,1,0:T(8,128)(2,1)S(1)} %pad_maximum_fusion.8.refs_6_), channel_id=1, source_target_pairs={{0,4},{4,8},{8,12},{12,16},{16,20},{20,24},{24,28},{28,0},{1,5},{5... | collective-permute-start | bytes 589832 | tf_op jit(solution)/shard_map/ppermute | solution.py:185
  74.5 11.2 %collective-permute-start.22 = (bf16[4,8,32,128]{3,2,1,0:T(8,128)(2,1)S(1)}, bf16[4,8,32,128]{3,2,1,0:T(8,128)(2,1)S(1)}, u32[]{:S(2)}, u32[]{:S(2)}) collective-permute-start(bf16[4,8,32,128]{3,2,1,0:T(8,128)(2,1)S(1)} %edge_half1.5.refs_2_.second_ref), channel_id=1, source_target_pairs={{1,0},{2,1},{3,2},{0,3},{5,4},{6,5},{7,6},{4,7},{9,8},{10,9},{11,1... | collective-permute-start | bytes 786440 | tf_op jit(solution)/shard_map/ppermute | solution.py:185
  80.5 16.4 %collective-permute-start.20 = (bf16[4,8,32,128]{3,2,1,0:T(8,128)(2,1)S(1)}, bf16[4,8,32,128]{3,2,1,0:T(8,128)(2,1)S(1)}, u32[]{:S(2)}, u32[]{:S(2)}) collective-permute-start(bf16[4,8,32,128]{3,2,1,0:T(8,128)(2,1)S(1)} %edge_half0.6.refs_2_.first_ref), channel_id=1, source_target_pairs={{0,1},{1,2},{2,3},{3,0},{4,5},{5,6},{6,7},{7,4},{8,9},{9,10},{10,1... | collective-permute-start | bytes 786440 | tf_op jit(solution)/shard_map/ppermute | solution.py:185
  85.7 9.5 %collective-permute-start.24 = (bf16[3,8,32,128]{3,2,1,0:T(8,128)(2,1)S(1)}, bf16[3,8,32,128]{3,2,1,0:T(8,128)(2,1)S(1)}, u32[]{:S(2)}, u32[]{:S(2)}) collective-permute-start(bf16[3,8,32,128]{3,2,1,0:T(8,128)(2,1)S(1)} %pad_maximum_fusion.11.refs_6_), channel_id=1, source_target_pairs={{0,4},{4,8},{8,12},{12,16},{16,20},{20,24},{24,28},{28,0},{1,5},{5... | collective-permute-start | bytes 589832 | tf_op jit(solution)/shard_map/ppermute | solution.py:185
  85.8 9.5 %collective-permute-start.25 = (bf16[3,8,32,128]{3,2,1,0:T(8,128)(2,1)S(1)}, bf16[3,8,32,128]{3,2,1,0:T(8,128)(2,1)S(1)}, u32[]{:S(2)}, u32[]{:S(2)}) collective-permute-start(bf16[3,8,32,128]{3,2,1,0:T(8,128)(2,1)S(1)} %pad_maximum_fusion.10.refs_5_), channel_id=1, source_target_pairs={{4,0},{8,4},{12,8},{16,12},{20,16},{24,20},{28,24},{0,28},{5,1},{9... | collective-permute-start | bytes 589832 | tf_op jit(solution)/shard_map/ppermute | solution.py:185
  90.9 10.8 %collective-permute-start.23 = (bf16[4,8,32,128]{3,2,1,0:T(8,128)(2,1)S(1)}, bf16[4,8,32,128]{3,2,1,0:T(8,128)(2,1)S(1)}, u32[]{:S(2)}, u32[]{:S(2)}) collective-permute-start(bf16[4,8,32,128]{3,2,1,0:T(8,128)(2,1)S(1)} %edge_half0.6.refs_2_.first_ref), channel_id=1, source_target_pairs={{1,0},{2,1},{3,2},{0,3},{5,4},{6,5},{7,6},{4,7},{9,8},{10,9},{11,1... | collective-permute-start | bytes 786440 | tf_op jit(solution)/shard_map/ppermute | solution.py:185
  96.8 13.0 %collective-permute-start.28 = (bf16[4,8,32,128]{3,2,1,0:T(8,128)(2,1)S(1)}, bf16[4,8,32,128]{3,2,1,0:T(8,128)(2,1)S(1)}, u32[]{:S(2)}, u32[]{:S(2)}) collective-permute-start(bf16[4,8,32,128]{3,2,1,0:T(8,128)(2,1)S(1)} %edge_half1.6.refs_2_.second_ref), channel_id=1, source_target_pairs={{0,1},{1,2},{2,3},{3,0},{4,5},{5,6},{6,7},{7,4},{8,9},{9,10},{10,1... | collective-permute-start | bytes 786440 | tf_op jit(solution)/shard_map/ppermute | solution.py:185
  101.8 6.5 %collective-permute-start.27 = (bf16[3,8,32,128]{3,2,1,0:T(8,128)(2,1)S(1)}, bf16[3,8,32,128]{3,2,1,0:T(8,128)(2,1)S(1)}, u32[]{:S(2)}, u32[]{:S(2)}) collective-permute-start(bf16[3,8,32,128]{3,2,1,0:T(8,128)(2,1)S(1)} %pad_maximum_fusion.13.refs_5_), channel_id=1, source_target_pairs={{4,0},{8,4},{12,8},{16,12},{20,16},{24,20},{28,24},{0,28},{5,1},{9... | collective-permute-start | bytes 589832 | tf_op jit(solution)/shard_map/ppermute | solution.py:185
  101.9 6.4 %collective-permute-start.26 = (bf16[3,8,32,128]{3,2,1,0:T(8,128)(2,1)S(1)}, bf16[3,8,32,128]{3,2,1,0:T(8,128)(2,1)S(1)}, u32[]{:S(2)}, u32[]{:S(2)}) collective-permute-start(bf16[3,8,32,128]{3,2,1,0:T(8,128)(2,1)S(1)} %pad_maximum_fusion.12.refs_6_), channel_id=1, source_target_pairs={{0,4},{4,8},{8,12},{12,16},{16,20},{20,24},{24,28},{28,0},{1,5},{5... | collective-permute-start | bytes 589832 | tf_op jit(solution)/shard_map/ppermute | solution.py:185
  103.9 10.1 %collective-permute-start.29 = (bf16[4,8,32,128]{3,2,1,0:T(8,128)(2,1)S(1)}, bf16[4,8,32,128]{3,2,1,0:T(8,128)(2,1)S(1)}, u32[]{:S(2)}, u32[]{:S(2)}) collective-permute-start(bf16[4,8,32,128]{3,2,1,0:T(8,128)(2,1)S(1)} %edge_half1.6.refs_2_.second_ref), channel_id=1, source_target_pairs={{1,0},{2,1},{3,2},{0,3},{5,4},{6,5},{7,6},{4,7},{9,8},{10,9},{11,1... | collective-permute-start | bytes 786440 | tf_op jit(solution)/shard_map/ppermute | solution.py:185
  114.1 5.0 %collective-permute-start.31 = (bf16[3,8,32,128]{3,2,1,0:T(8,128)(2,1)S(1)}, bf16[3,8,32,128]{3,2,1,0:T(8,128)(2,1)S(1)}, u32[]{:S(2)}, u32[]{:S(2)}) collective-permute-start(bf16[3,8,32,128]{3,2,1,0:T(8,128)(2,1)S(1)} %pad_maximum_fusion.15.refs_5_), channel_id=1, source_target_pairs={{4,0},{8,4},{12,8},{16,12},{20,16},{24,20},{28,24},{0,28},{5,1},{9... | collective-permute-start | bytes 589832 | tf_op jit(solution)/shard_map/ppermute | solution.py:185
  114.2 6.9 %collective-permute-start.30 = (bf16[3,8,32,128]{3,2,1,0:T(8,128)(2,1)S(1)}, bf16[3,8,32,128]{3,2,1,0:T(8,128)(2,1)S(1)}, u32[]{:S(2)}, u32[]{:S(2)}) collective-permute-start(bf16[3,8,32,128]{3,2,1,0:T(8,128)(2,1)S(1)} %pad_maximum_fusion.14.refs_6_), channel_id=1, source_target_pairs={{0,4},{4,8},{8,12},{12,16},{16,20},{20,24},{24,28},{28,0},{1,5},{5... | collective-permute-start | bytes 589832 | tf_op jit(solution)/shard_map/ppermute | solution.py:185

commit v9 on v7

--- a/solution.py
+++ b/solution.py
@@ -9,6 +9,9 @@
 
 STEPS = 4
 HALVES = 2
+APART_FIRST = (False, False)
+APART_LAST = (False, True)
+WEIGHT = 100
 VMEM_LIMIT = 4 * 1024 * 1024
 VMEM = pl.BlockSpec(memory_space=pltpu.VMEM)
 ANY = pl.BlockSpec(memory_space=pl.ANY)
@@ -93,8 +96,23 @@
 
 def edges(own, low_az, high_az, after):
     *trio, _ = lax.optimization_barrier((low_az, own, high_az, after))
-    columns = own.shape[0]
-    return jnp.stack([part[0] for part in trio]), jnp.stack([part[columns - 1] for part in trio])
+    return jnp.stack([part[0] for part in trio]), jnp.stack([part[-1] for part in trio])
+
+
+def neighbours_of(value, apart):
+    if apart:
+        parts = (jnp.stack([value[0], value[-1]]), value[1:-1])
+    else:
+        parts = (value,)
+    return [(part, shift(part, "azim", True), shift(part, "azim", False)) for part in parts]
+
+
+def joined(value, outer, inner, after):
+    outer, inner, _ = lax.optimization_barrier((outer, inner, after))
+    return (
+        value,
+        *(jnp.concatenate([outer[n][:1], inner[n], outer[n][1:]]) for n in (1, 2)),
+    )
 
 
 def part_kernel(half, *refs):
@@ -167,8 +185,8 @@
         out_shape=jax.ShapeDtypeStruct((kept, faces, rows, lanes), jnp.bfloat16),
         scratch_shapes=[pltpu.VMEM((3 * (columns + 2) * faces, rows, lanes), jnp.bfloat16)],
         cost_estimate=pl.CostEstimate(
-            flops=2 * done * faces * width * depth * lanes,
-            bytes_accessed=2 * done * faces * width * depth,
+            flops=WEIGHT * 2 * done * faces * width * depth * lanes,
+            bytes_accessed=WEIGHT * 2 * done * faces * width * depth,
             transcendentals=0,
         ),
         compiler_params=pltpu.CompilerParams(vmem_limit_bytes=VMEM_LIMIT),
@@ -228,17 +246,19 @@
     blocks = halves_of_rows(trace_blocks.reshape(columns, faces, width, -1))
     codes = neighbour.reshape(faces, -1)
     table = (((codes // faces) % 3) * (columns + 2) + codes // (3 * faces)) * faces + codes % faces
+    table = pltpu.with_memory_space_constraint(table, pltpu.SMEM)
     every = tuple(range(columns))
     current = list(pack(start))
     basis = None
     latest = current[0]
-    lows = [shift(current[h], "azim", True) for h in range(HALVES)]
-    highs = [shift(current[h], "azim", False) for h in range(HALVES)]
+    around_z = [neighbours_of(current[h], APART_FIRST[h]) for h in range(HALVES)]
     for index in range(STEPS):
         previous = tuple(current)
         for h in range(HALVES):
-            pieces = (current[h], lows[h], highs[h])
-            to_low, to_high = edges(*pieces, latest)
+            parts = around_z[h]
+            apart = len(parts) > 1
+            to_low, to_high = edges(*parts[0], middle if apart and h else latest)
+            pieces = joined(current[h], *parts, latest if h else to_high) if apart else parts[0]
             stream = (shift(to_high, "stream", True), shift(to_low, "stream", False))
             middle = part(h, table, blocks, pieces, (to_low, to_high))
             after = middle
@@ -246,8 +266,7 @@
                 basis, after = unpack(index - 1, every, *previous, basis, middle)
             current[h] = latest = part(h, table, blocks, pieces, (*stream, middle, after))
             if index < STEPS - 1:
-                lows[h] = shift(current[h], "azim", True)
-                highs[h] = shift(current[h], "azim", False)
+                around_z[h] = neighbours_of(current[h], index == STEPS - 2 and APART_LAST[h])
     basis, _ = unpack(STEPS - 1, every, *current, basis, None)
     return basis.reshape(STEPS, columns, around, faces, width, lanes)
 

time: 116 us -> 117 us (level)
  waiting for transfers between devices: 40.4 us -> 36.4 us
  starting transfers between devices: 40 us -> 43.8 us
    ppermute x32 -> x34, waiting for transfers between devices: 40.4 us -> 36.4 us  [shift(): return lax.ppermute(value, axis, pairs)]
    ppermute x32 -> x34, starting transfers between devices: 40 us -> 43.8 us  [shift(): return lax.ppermute(value, axis, pairs)]
  transfers between devices with their start and end apart: 32 -> 34, of which waited for: 17 -> 14; matrix products, arithmetic and copies ran while one was open for 1% -> 1% of each run, Pallas kernels for 25% -> 25%
where the time goes in v9:
time: 117 us; the launch traced here: 116 us
  starting transfers between devices  43.8 us (37%)
  waiting for transfers between devices  36.4 us (31%)
  Pallas kernels  31.9 us (27%)
  local copies, waits for them, and re-layouts  3.23 us (3%)
    ppermute x34, starting transfers between devices, shift(): return lax.ppermute(value, axis, pairs)  43.8 us
    ppermute x34, waiting for transfers between devices, shift(): return lax.ppermute(value, axis, pairs)  36.4 us
    pallas_call x16, Pallas kernels, part(): pl.pallas_call(functools.partial(part_kernel, half), in_specs=in_specs, o...  24.8 us
    pallas_call x4, Pallas kernels, unpack(): pl.pallas_call(functools.partial(unpack_kernel, index, chosen, skipped),...  4.25 us
    unnamed x6, local copies, waits for them, and re-layouts  2.93 us
    pallas_call x1, Pallas kernels, halves_of_rows(): pl.pallas_call(halves_kernel, in_specs=[VMEM], out_specs=VMEM, out_shape=...  2.72 us
  transfers between devices with their start and end apart: 34, of which 14 were waited for; matrix products, arithmetic and copies ran while one was open for 1% of the time, Pallas kernels for 25%

profile of v9, /device:TPU:0, one launch (start us, length us, event | category | flops | bytes accessed | tf_op | source)
XLA Modules:
  0.0 116.4 jit_solution(16396137365500657650)
XLA Ops:
  0.0 1.0 copy-done.1
  1.0 0.2 pack.1
  1.2 3.1 %collective-permute-start = (bf16[4,8,32,128]{3,2,1,0:T(8,128)(2,1)S(1)}, bf16[4,8,32,128]{3,2,1,0:T(8,128)(2,1)S(1)}, u32[]{:S(2)}, u32[]{:S(2)}) collective-permute-start(bf16[4,8,32,128]{3,2,1,0:T(8,128)(2,1)S(1)} %get-tuple-element.44.refs_2_), channel_id=1, source_target_pairs={{0,1},{1,2},{2,3},{3,0},{4,5},{5,6},{6,7},{7,4},{8,9},{9,10},{10,1... | collective-permute-start | bytes 786440 | tf_op jit(solution)/shard_map/ppermute | solution.py:202
  4.3 2.1 %collective-permute-start.1 = (bf16[4,8,32,128]{3,2,1,0:T(8,128)(2,1)S(1)}, bf16[4,8,32,128]{3,2,1,0:T(8,128)(2,1)S(1)}, u32[]{:S(2)}, u32[]{:S(2)}) collective-permute-start(bf16[4,8,32,128]{3,2,1,0:T(8,128)(2,1)S(1)} %get-tuple-element.44.refs_2_), channel_id=1, source_target_pairs={{1,0},{2,1},{3,2},{0,3},{5,4},{6,5},{7,6},{4,7},{9,8},{10,9},{11,1... | collective-permute-start | bytes 786440 | tf_op jit(solution)/shard_map/ppermute | solution.py:202
  6.4 3.8 %collective-permute-start.7 = (bf16[4,8,32,128]{3,2,1,0:T(8,128)(2,1)S(1)}, bf16[4,8,32,128]{3,2,1,0:T(8,128)(2,1)S(1)}, u32[]{:S(2)}, u32[]{:S(2)}) collective-permute-start(bf16[4,8,32,128]{3,2,1,0:T(8,128)(2,1)S(1)} %get-tuple-element.48.refs_2_), channel_id=1, source_target_pairs={{1,0},{2,1},{3,2},{0,3},{5,4},{6,5},{7,6},{4,7},{9,8},{10,9},{11,1... | collective-permute-start | bytes 786440 | tf_op jit(solution)/shard_map/ppermute | solution.py:202
  10.2 1.9 %copy-done = bf16[4,1,8,64,768]{4,3,2,1,0:T(8,128)(2,1)S(1)} copy-done((bf16[4,1,8,64,768]{4,3,2,1,0:T(8,128)(2,1)S(1)}, bf16[4,1,8,64,768]{4,3,2,1,0:T(8,128)(2,1)}, u32[]{:S(2)}) %copy-start) | copy-done | bytes 3145752
  12.1 2.7 %halves_of_rows.1.refs_1_ = bf16[4,8,64,768]{3,2,1,0:T(8,128)(2,1)S(1)} custom-call(bf16[4,8,64,768]{3,2,1,0:T(8,128)(2,1)S(1)} %bitcast.29), custom_call_target="tpu_custom_call" | custom-call | tf_op jit(solution)/shard_map/halves_of_rows/pallas_call | solution.py:233
  14.9 4.4 %collective-permute-done.1.refs_4_ = bf16[4,8,32,128]{3,2,1,0:T(8,128)(2,1)S(1)} collective-permute-done((bf16[4,8,32,128]{3,2,1,0:T(8,128)(2,1)S(1)}, bf16[4,8,32,128]{3,2,1,0:T(8,128)(2,1)S(1)}, u32[]{:S(2)}, u32[]{:S(2)}) %collective-permute-start.1) | collective-permute-done | bytes 262176 | tf_op jit(solution)/shard_map/ppermute | solution.py:202
  19.4 0.1 collective-permute-start.3
  19.5 0.5 collective-permute-start.2
  20.0 1.5 %inner_half0.4.refs_7_.refs_8_ = bf16[2,8,32,128]{3,2,1,0:T(8,128)(2,1)S(1)} custom-call(s32[8,12]{1,0:T(8,128)S(1)} %fusion.4.refs_0_, bf16[4,8,64,768]{3,2,1,0:T(8,128)(2,1)S(1)} %halves_of_rows.1.refs_1_, bf16[4,8,32,128]{3,2,1,0:T(8,128)(2,1)S(1)} %get-tuple-element.44.refs_2_, bf16[4,8,32,128]{3,2,1,0:T(8,128)(2,1)S(1)} %collective-permute-done.refs_3_, ...), custom_call_target="tpu_custom_call" | custom-call | flops 20132659200 | bytes 157286400 | tf_op jit(solution)/shard_map/inner_half0/pallas_call | solution.py:181
  21.5 1.9 %collective-permute-done.3.refs_6_ = bf16[3,8,32,128]{3,2,1,0:T(8,128)(2,1)S(1)} collective-permute-done((bf16[3,8,32,128]{3,2,1,0:T(8,128)(2,1)S(1)}, bf16[3,8,32,128]{3,2,1,0:T(8,128)(2,1)S(1)}, u32[]{:S(2)}, u32[]{:S(2)}) %collective-permute-start.3) | collective-permute-done | bytes 196640 | tf_op jit(solution)/shard_map/ppermute | solution.py:202
  23.4 4.2 %collective-permute-done.2.refs_5_ = bf16[3,8,32,128]{3,2,1,0:T(8,128)(2,1)S(1)} collective-permute-done((bf16[3,8,32,128]{3,2,1,0:T(8,128)(2,1)S(1)}, bf16[3,8,32,128]{3,2,1,0:T(8,128)(2,1)S(1)}, u32[]{:S(2)}, u32[]{:S(2)}) %collective-permute-start.2) | collective-permute-done | bytes 196640 | tf_op jit(solution)/shard_map/ppermute | solution.py:202
  27.7 1.6 %edge_half0.4.refs_2_.first_ref = bf16[4,8,32,128]{3,2,1,0:T(8,128)(2,1)S(1)} custom-call(s32[8,12]{1,0:T(8,128)S(1)} %fusion.4.refs_0_, bf16[4,8,64,768]{3,2,1,0:T(8,128)(2,1)S(1)} %halves_of_rows.1.refs_1_, bf16[4,8,32,128]{3,2,1,0:T(8,128)(2,1)S(1)} %get-tuple-element.44.refs_2_, bf16[4,8,32,128]{3,2,1,0:T(8,128)(2,1)S(1)} %collective-permute-done.refs_3_, ...), custom_call_target="tpu_custom_call" | custom-call | flops 20132659200 | bytes 157286400 | tf_op jit(solution)/shard_map/edge_half0/pallas_call | solution.py:181
  29.2 0.7 collective-permute-start.4
  29.9 3.2 %collective-permute-start.5 = (bf16[4,8,32,128]{3,2,1,0:T(8,128)(2,1)S(1)}, bf16[4,8,32,128]{3,2,1,0:T(8,128)(2,1)S(1)}, u32[]{:S(2)}, u32[]{:S(2)}) collective-permute-start(bf16[4,8,32,128]{3,2,1,0:T(8,128)(2,1)S(1)} %edge_half0.4.refs_2_.first_ref), channel_id=1, source_target_pairs={{1,0},{2,1},{3,2},{0,3},{5,4},{6,5},{7,6},{4,7},{9,8},{10,9},{11,1... | collective-permute-start | bytes 786440 | tf_op jit(solution)/shard_map/ppermute | solution.py:202
  33.2 0.1 collective-permute-start.9
  33.3 0.5 collective-permute-start.8
  33.8 1.5 %inner_half1.4.refs_7_.refs_8_ = bf16[2,8,32,128]{3,2,1,0:T(8,128)(2,1)S(1)} custom-call(s32[8,12]{1,0:T(8,128)S(1)} %fusion.4.refs_0_, bf16[4,8,64,768]{3,2,1,0:T(8,128)(2,1)S(1)} %halves_of_rows.1.refs_1_, bf16[4,8,32,128]{3,2,1,0:T(8,128)(2,1)S(1)} %get-tuple-element.48.refs_2_, bf16[4,8,32,128]{3,2,1,0:T(8,128)(2,1)S(1)} %collective-permute-done.6.refs_3_, ...), custom_call_target="tpu_custom_call" | custom-call | flops 20132659200 | bytes 157286400 | tf_op jit(solution)/shard_map/inner_half1/pallas_call | solution.py:181
  35.4 3.1 %collective-permute-done.9.refs_6_ = bf16[3,8,32,128]{3,2,1,0:T(8,128)(2,1)S(1)} collective-permute-done((bf16[3,8,32,128]{3,2,1,0:T(8,128)(2,1)S(1)}, bf16[3,8,32,128]{3,2,1,0:T(8,128)(2,1)S(1)}, u32[]{:S(2)}, u32[]{:S(2)}) %collective-permute-start.9) | collective-permute-done | bytes 196640 | tf_op jit(solution)/shard_map/ppermute | solution.py:202
  38.5 1.8 %collective-permute-done.8.refs_5_ = bf16[3,8,32,128]{3,2,1,0:T(8,128)(2,1)S(1)} collective-permute-done((bf16[3,8,32,128]{3,2,1,0:T(8,128)(2,1)S(1)}, bf16[3,8,32,128]{3,2,1,0:T(8,128)(2,1)S(1)}, u32[]{:S(2)}, u32[]{:S(2)}) %collective-permute-start.8) | collective-permute-done | bytes 196640 | tf_op jit(solution)/shard_map/ppermute | solution.py:202
  40.3 1.6 %edge_half1.4.refs_2_.second_ref = bf16[4,8,32,128]{3,2,1,0:T(8,128)(2,1)S(1)} custom-call(s32[8,12]{1,0:T(8,128)S(1)} %fusion.4.refs_0_, bf16[4,8,64,768]{3,2,1,0:T(8,128)(2,1)S(1)} %halves_of_rows.1.refs_1_, bf16[4,8,32,128]{3,2,1,0:T(8,128)(2,1)S(1)} %get-tuple-element.48.refs_2_, bf16[4,8,32,128]{3,2,1,0:T(8,128)(2,1)S(1)} %collective-permute-done.6.refs_3_, ...), custom_call_target="tpu_custom_call" | custom-call | flops 20132659200 | bytes 157286400 | tf_op jit(solution)/shard_map/edge_half1/pallas_call | solution.py:181
  41.9 3.8 %collective-permute-start.15 = (bf16[4,8,32,128]{3,2,1,0:T(8,128)(2,1)S(1)}, bf16[4,8,32,128]{3,2,1,0:T(8,128)(2,1)S(1)}, u32[]{:S(2)}, u32[]{:S(2)}) collective-permute-start(bf16[4,8,32,128]{3,2,1,0:T(8,128)(2,1)S(1)} %edge_half1.4.refs_2_.second_ref), channel_id=1, source_target_pairs={{1,0},{2,1},{3,2},{0,3},{5,4},{6,5},{7,6},{4,7},{9,8},{10,9},{11,1... | collective-permute-start | bytes 786440 | tf_op jit(solution)/shard_map/ppermute | solution.py:202
  45.8 0.5 collective-permute-start.11
  46.3 0.1 collective-permute-start.10
  46.5 1.5 %inner_half0.5.refs_7_.refs_8_ = bf16[2,8,32,128]{3,2,1,0:T(8,128)(2,1)S(1)} custom-call(s32[8,12]{1,0:T(8,128)S(1)} %fusion.4.refs_0_, bf16[4,8,64,768]{3,2,1,0:T(8,128)(2,1)S(1)} %halves_of_rows.1.refs_1_, bf16[4,8,32,128]{3,2,1,0:T(8,128)(2,1)S(1)} %edge_half0.4.refs_2_.first_ref, bf16[4,8,32,128]{3,2,1,0:T(8,128)(2,1)S(1)} %collective-permute-done.4.refs_3_, ...), custom_call_target="tpu_custom_call" | custom-call | flops 20132659200 | bytes 157286400 | tf_op jit(solution)/shard_map/inner_half0/pallas_call | solution.py:181
  48.0 3.3 %collective-permute-done.11.refs_6_ = bf16[3,8,32,128]{3,2,1,0:T(8,128)(2,1)S(1)} collective-permute-done((bf16[3,8,32,128]{3,2,1,0:T(8,128)(2,1)S(1)}, bf16[3,8,32,128]{3,2,1,0:T(8,128)(2,1)S(1)}, u32[]{:S(2)}, u32[]{:S(2)}) %collective-permute-start.11) | collective-permute-done | bytes 196640 | tf_op jit(solution)/shard_map/ppermute | solution.py:202
  51.2 1.3 %collective-permute-done.10.refs_5_ = bf16[3,8,32,128]{3,2,1,0:T(8,128)(2,1)S(1)} collective-permute-done((bf16[3,8,32,128]{3,2,1,0:T(8,128)(2,1)S(1)}, bf16[3,8,32,128]{3,2,1,0:T(8,128)(2,1)S(1)}, u32[]{:S(2)}, u32[]{:S(2)}) %collective-permute-start.10) | collective-permute-done | bytes 196640 | tf_op jit(solution)/shard_map/ppermute | solution.py:202
  52.5 1.6 %edge_half0.5.refs_2_.first_ref = bf16[4,8,32,128]{3,2,1,0:T(8,128)(2,1)S(1)} custom-call(s32[8,12]{1,0:T(8,128)S(1)} %fusion.4.refs_0_, bf16[4,8,64,768]{3,2,1,0:T(8,128)(2,1)S(1)} %halves_of_rows.1.refs_1_, bf16[4,8,32,128]{3,2,1,0:T(8,128)(2,1)S(1)} %edge_half0.4.refs_2_.first_ref, bf16[4,8,32,128]{3,2,1,0:T(8,128)(2,1)S(1)} %collective-permute-done.4.refs_3_, ...), custom_call_target="tpu_custom_call" | custom-call | flops 20132659200 | bytes 157286400 | tf_op jit(solution)/shard_map/edge_half0/pallas_call | solution.py:181
  54.2 3.8 %collective-permute-start.13 = (bf16[4,8,32,128]{3,2,1,0:T(8,128)(2,1)S(1)}, bf16[4,8,32,128]{3,2,1,0:T(8,128)(2,1)S(1)}, u32[]{:S(2)}, u32[]{:S(2)}) collective-permute-start(bf16[4,8,32,128]{3,2,1,0:T(8,128)(2,1)S(1)} %edge_half0.5.refs_2_.first_ref), channel_id=1, source_target_pairs={{1,0},{2,1},{3,2},{0,3},{5,4},{6,5},{7,6},{4,7},{9,8},{10,9},{11,1... | collective-permute-start | bytes 786440 | tf_op jit(solution)/shard_map/ppermute | solution.py:202
  58.1 1.0 collective-permute-start.17
  59.1 0.1 collective-permute-start.16
  59.2 1.5 %inner_half1.5.refs_0_.refs_7_ = bf16[2,8,32,128]{3,2,1,0:T(8,128)(2,1)S(1)} custom-call(s32[8,12]{1,0:T(8,128)S(1)} %fusion.4.refs_0_, bf16[4,8,64,768]{3,2,1,0:T(8,128)(2,1)S(1)} %halves_of_rows.1.refs_1_, bf16[4,8,32,128]{3,2,1,0:T(8,128)(2,1)S(1)} %edge_half1.4.refs_2_.second_ref, bf16[4,8,32,128]{3,2,1,0:T(8,128)(2,1)S(1)} %collective-permute-done.14.refs_3_, ...), custom_call_target="tpu_custom_call" | custom-call | flops 20132659200 | bytes 157286400 | tf_op jit(solution)/shard_map/inner_half1/pallas_call | solution.py:181
  60.7 0.9 unpack.4
  61.6 2.3 %collective-permute-done.17.refs_6_ = bf16[3,8,32,128]{3,2,1,0:T(8,128)(2,1)S(1)} collective-permute-done((bf16[3,8,32,128]{3,2,1,0:T(8,128)(2,1)S(1)}, bf16[3,8,32,128]{3,2,1,0:T(8,128)(2,1)S(1)}, u32[]{:S(2)}, u32[]{:S(2)}) %collective-permute-start.17) | collective-permute-done | bytes 196640 | tf_op jit(solution)/shard_map/ppermute | solution.py:202
  63.9 1.3 %collective-permute-done.16.refs_5_ = bf16[3,8,32,128]{3,2,1,0:T(8,128)(2,1)S(1)} collective-permute-done((bf16[3,8,32,128]{3,2,1,0:T(8,128)(2,1)S(1)}, bf16[3,8,32,128]{3,2,1,0:T(8,128)(2,1)S(1)}, u32[]{:S(2)}, u32[]{:S(2)}) %collective-permute-start.16) | collective-permute-done | bytes 196640 | tf_op jit(solution)/shard_map/ppermute | solution.py:202
  65.2 1.6 %edge_half1.5.refs_2_.second_ref = bf16[4,8,32,128]{3,2,1,0:T(8,128)(2,1)S(1)} custom-call(s32[8,12]{1,0:T(8,128)S(1)} %fusion.4.refs_0_, bf16[4,8,64,768]{3,2,1,0:T(8,128)(2,1)S(1)} %halves_of_rows.1.refs_1_, bf16[4,8,32,128]{3,2,1,0:T(8,128)(2,1)S(1)} %edge_half1.4.refs_2_.second_ref, bf16[4,8,32,128]{3,2,1,0:T(8,128)(2,1)S(1)} %collective-permute-done.14.refs_3_, ...), custom_call_target="tpu_custom_call" | custom-call | flops 20132659200 | bytes 157286400 | tf_op jit(solution)/shard_map/edge_half1/pallas_call | solution.py:181
  66.8 3.8 %collective-permute-start.23 = (bf16[4,8,32,128]{3,2,1,0:T(8,128)(2,1)S(1)}, bf16[4,8,32,128]{3,2,1,0:T(8,128)(2,1)S(1)}, u32[]{:S(2)}, u32[]{:S(2)}) collective-permute-start(bf16[4,8,32,128]{3,2,1,0:T(8,128)(2,1)S(1)} %edge_half1.5.refs_2_.second_ref), channel_id=1, source_target_pairs={{1,0},{2,1},{3,2},{0,3},{5,4},{6,5},{7,6},{4,7},{9,8},{10,9},{11,1... | collective-permute-start | bytes 786440 | tf_op jit(solution)/shard_map/ppermute | solution.py:202
  70.7 1.0 collective-permute-start.19
  71.7 0.1 collective-permute-start.18
  71.8 1.5 %inner_half0.6.refs_7_.refs_8_ = bf16[2,8,32,128]{3,2,1,0:T(8,128)(2,1)S(1)} custom-call(s32[8,12]{1,0:T(8,128)S(1)} %fusion.4.refs_0_, bf16[4,8,64,768]{3,2,1,0:T(8,128)(2,1)S(1)} %halves_of_rows.1.refs_1_, bf16[4,8,32,128]{3,2,1,0:T(8,128)(2,1)S(1)} %edge_half0.5.refs_2_.first_ref, bf16[4,8,32,128]{3,2,1,0:T(8,128)(2,1)S(1)} %collective-permute-done.12.refs_3_, ...), custom_call_target="tpu_custom_call" | custom-call | flops 20132659200 | bytes 157286400 | tf_op jit(solution)/shard_map/inner_half0/pallas_call | solution.py:181
  73.3 3.0 %collective-permute-done.19.refs_6_ = bf16[3,8,32,128]{3,2,1,0:T(8,128)(2,1)S(1)} collective-permute-done((bf16[3,8,32,128]{3,2,1,0:T(8,128)(2,1)S(1)}, bf16[3,8,32,128]{3,2,1,0:T(8,128)(2,1)S(1)}, u32[]{:S(2)}, u32[]{:S(2)}) %collective-permute-start.19) | collective-permute-done | bytes 196640 | tf_op jit(solution)/shard_map/ppermute | solution.py:202
  76.3 1.5 %collective-permute-done.18.refs_5_ = bf16[3,8,32,128]{3,2,1,0:T(8,128)(2,1)S(1)} collective-permute-done((bf16[3,8,32,128]{3,2,1,0:T(8,128)(2,1)S(1)}, bf16[3,8,32,128]{3,2,1,0:T(8,128)(2,1)S(1)}, u32[]{:S(2)}, u32[]{:S(2)}) %collective-permute-start.18) | collective-permute-done | bytes 196640 | tf_op jit(solution)/shard_map/ppermute | solution.py:202
  77.8 1.6 %edge_half0.6.refs_2_.first_ref = bf16[4,8,32,128]{3,2,1,0:T(8,128)(2,1)S(1)} custom-call(s32[8,12]{1,0:T(8,128)S(1)} %fusion.4.refs_0_, bf16[4,8,64,768]{3,2,1,0:T(8,128)(2,1)S(1)} %halves_of_rows.1.refs_1_, bf16[4,8,32,128]{3,2,1,0:T(8,128)(2,1)S(1)} %edge_half0.5.refs_2_.first_ref, bf16[4,8,32,128]{3,2,1,0:T(8,128)(2,1)S(1)} %collective-permute-done.12.refs_3_, ...), custom_call_target="tpu_custom_call" | custom-call | flops 20132659200 | bytes 157286400 | tf_op jit(solution)/shard_map/edge_half0/pallas_call | solution.py:181
  79.4 3.8 %collective-permute-start.21 = (bf16[4,8,32,128]{3,2,1,0:T(8,128)(2,1)S(1)}, bf16[4,8,32,128]{3,2,1,0:T(8,128)(2,1)S(1)}, u32[]{:S(2)}, u32[]{:S(2)}) collective-permute-start(bf16[4,8,32,128]{3,2,1,0:T(8,128)(2,1)S(1)} %edge_half0.6.refs_2_.first_ref), channel_id=1, source_target_pairs={{1,0},{2,1},{3,2},{0,3},{5,4},{6,5},{7,6},{4,7},{9,8},{10,9},{11,1... | collective-permute-start | bytes 786440 | tf_op jit(solution)/shard_map/ppermute | solution.py:202
  83.3 0.8 collective-permute-start.25
  84.3 1.5 %inner_half1.6.refs_1_.refs_7_ = bf16[2,8,32,128]{3,2,1,0:T(8,128)(2,1)S(1)} custom-call(s32[8,12]{1,0:T(8,128)S(1)} %fusion.4.refs_0_, bf16[4,8,64,768]{3,2,1,0:T(8,128)(2,1)S(1)} %halves_of_rows.1.refs_1_, bf16[4,8,32,128]{3,2,1,0:T(8,128)(2,1)S(1)} %edge_half1.5.refs_2_.second_ref, bf16[4,8,32,128]{3,2,1,0:T(8,128)(2,1)S(1)} %collective-permute-done.22.refs_3_, ...), custom_call_target="tpu_custom_call" | custom-call | flops 20132659200 | bytes 157286400 | tf_op jit(solution)/shard_map/inner_half1/pallas_call | solution.py:181
  85.8 0.9 unpack.5
  86.7 1.9 %collective-permute-done.25.refs_6_ = bf16[3,8,32,128]{3,2,1,0:T(8,128)(2,1)S(1)} collective-permute-done((bf16[3,8,32,128]{3,2,1,0:T(8,128)(2,1)S(1)}, bf16[3,8,32,128]{3,2,1,0:T(8,128)(2,1)S(1)}, u32[]{:S(2)}, u32[]{:S(2)}) %collective-permute-start.25) | collective-permute-done | bytes 196640 | tf_op jit(solution)/shard_map/ppermute | solution.py:202
  88.6 1.7 %collective-permute-done.24.refs_5_ = bf16[3,8,32,128]{3,2,1,0:T(8,128)(2,1)S(1)} collective-permute-done((bf16[3,8,32,128]{3,2,1,0:T(8,128)(2,1)S(1)}, bf16[3,8,32,128]{3,2,1,0:T(8,128)(2,1)S(1)}, u32[]{:S(2)}, u32[]{:S(2)}) %collective-permute-start.24) | collective-permute-done | bytes 196640 | tf_op jit(solution)/shard_map/ppermute | solution.py:202
  90.3 1.6 %edge_half1.6.refs_2_.second_ref = bf16[4,8,32,128]{3,2,1,0:T(8,128)(2,1)S(1)} custom-call(s32[8,12]{1,0:T(8,128)S(1)} %fusion.4.refs_0_, bf16[4,8,64,768]{3,2,1,0:T(8,128)(2,1)S(1)} %halves_of_rows.1.refs_1_, bf16[4,8,32,128]{3,2,1,0:T(8,128)(2,1)S(1)} %edge_half1.5.refs_2_.second_ref, bf16[4,8,32,128]{3,2,1,0:T(8,128)(2,1)S(1)} %collective-permute-done.22.refs_3_, ...), custom_call_target="tpu_custom_call" | custom-call | flops 20132659200 | bytes 157286400 | tf_op jit(solution)/shard_map/edge_half1/pallas_call | solution.py:181
  92.0 0.1 collective-permute-start.28
  92.0 3.8 %collective-permute-start.29 = (bf16[2,8,32,128]{3,2,1,0:T(8,128)(2,1)S(1)}, bf16[2,8,32,128]{3,2,1,0:T(8,128)(2,1)S(1)}, u32[]{:S(2)}, u32[]{:S(2)}) collective-permute-start(bf16[2,8,32,128]{3,2,1,0:T(8,128)(2,1)S(1)} %pad_maximum_fusion.18), channel_id=1, source_target_pairs={{1,0},{2,1},{3,2},{0,3},{5,4},{6,5},{7,6},{4,7},{9,8},{10,9},{11,1... | collective-permute-start | bytes 393224 | tf_op jit(solution)/shard_map/ppermute | solution.py:202
  95.8 0.1 collective-permute-start.30
  95.9 3.8 %collective-permute-start.31 = (bf16[2,8,32,128]{3,2,1,0:T(8,128)(2,1)S(1)}, bf16[2,8,32,128]{3,2,1,0:T(8,128)(2,1)S(1)}, u32[]{:S(2)}, u32[]{:S(2)}) collective-permute-start(bf16[2,8,32,128]{3,2,1,0:T(8,128)(2,1)S(1)} %slice.222), channel_id=1, source_target_pairs={{1,0},{2,1},{3,2},{0,3},{5,4},{6,5},{7,6},{4,7},{9,8},{10,9},{11,1... | collective-permute-start | bytes 393224 | tf_op jit(solution)/shard_map/ppermute | solution.py:202
  99.9 1.5 %inner_half0.7.refs_7_.refs_8_ = bf16[2,8,32,128]{3,2,1,0:T(8,128)(2,1)S(1)} custom-call(s32[8,12]{1,0:T(8,128)S(1)} %fusion.4.refs_0_, bf16[4,8,64,768]{3,2,1,0:T(8,128)(2,1)S(1)} %halves_of_rows.1.refs_1_, bf16[4,8,32,128]{3,2,1,0:T(8,128)(2,1)S(1)} %edge_half0.6.refs_2_.first_ref, bf16[4,8,32,128]{3,2,1,0:T(8,128)(2,1)S(1)} %collective-permute-done.20.refs_3_, ...), custom_call_target="tpu_custom_call" | custom-call | flops 20132659200 | bytes 157286400 | tf_op jit(solution)/shard_map/inner_half0/pallas_call | solution.py:181
  101.4 0.5 collective-permute-start.26
  102.1 2.2 %collective-permute-start.33 = (bf16[3,8,32,128]{3,2,1,0:T(8,128)(2,1)S(1)}, bf16[3,8,32,128]{3,2,1,0:T(8,128)(2,1)S(1)}, u32[]{:S(2)}, u32[]{:S(2)}) collective-permute-start(bf16[3,8,32,128]{3,2,1,0:T(8,128)(2,1)S(1)} %pad_maximum_fusion.17.refs_5_), channel_id=1, source_target_pairs={{4,0},{8,4},{12,8},{16,12},{20,16},{24,20},{28,24},{0,28},{5,1},{9... | collective-permute-start | bytes 589832 | tf_op jit(solution)/shard_map/ppermute | solution.py:202
  104.4 4.7 %collective-permute-done.26.refs_5_ = bf16[3,8,32,128]{3,2,1,0:T(8,128)(2,1)S(1)} collective-permute-done((bf16[3,8,32,128]{3,2,1,0:T(8,128)(2,1)S(1)}, bf16[3,8,32,128]{3,2,1,0:T(8,128)(2,1)S(1)}, u32[]{:S(2)}, u32[]{:S(2)}) %collective-permute-start.26) | collective-permute-done | bytes 196640 | tf_op jit(solution)/shard_map/ppermute | solution.py:202
  109.1 1.6 %edge_half0.7.first_ref = bf16[4,8,32,128]{3,2,1,0:T(8,128)(2,1)S(1)} custom-call(s32[8,12]{1,0:T(8,128)S(1)} %fusion.4.refs_0_, bf16[4,8,64,768]{3,2,1,0:T(8,128)(2,1)S(1)} %halves_of_rows.1.refs_1_, bf16[4,8,32,128]{3,2,1,0:T(8,128)(2,1)S(1)} %edge_half0.6.refs_2_.first_ref, bf16[4,8,32,128]{3,2,1,0:T(8,128)(2,1)S(1)} %collective-permute-done.20.refs_3_, ...), custom_call_target="tpu_custom_call" | custom-call | flops 20132659200 | bytes 157286400 | tf_op jit(solution)/shard_map/edge_half0/pallas_call | solution.py:181
  110.8 1.5 %inner_half1.7.refs_1_.refs_7_ = bf16[2,8,32,128]{3,2,1,0:T(8,128)(2,1)S(1)} custom-call(s32[8,12]{1,0:T(8,128)S(1)} %fusion.4.refs_0_, bf16[4,8,64,768]{3,2,1,0:T(8,128)(2,1)S(1)} %halves_of_rows.1.refs_1_, bf16[4,8,32,128]{3,2,1,0:T(8,128)(2,1)S(1)} %edge_half1.6.refs_2_.second_ref, bf16[4,8,32,128]{3,2,1,0:T(8,128)(2,1)S(1)} %pad_maximum_fusion.refs_3_, ...), custom_call_target="tpu_custom_call" | custom-call | flops 20132659200 | bytes 157286400 | tf_op jit(solution)/shard_map/inner_half1/pallas_call | solution.py:181
  112.3 0.9 unpack.6
  113.3 1.6 %edge_half1.7.second_ref = bf16[4,8,32,128]{3,2,1,0:T(8,128)(2,1)S(1)} custom-call(s32[8,12]{1,0:T(8,128)S(1)} %fusion.4.refs_0_, bf16[4,8,64,768]{3,2,1,0:T(8,128)(2,1)S(1)} %halves_of_rows.1.refs_1_, bf16[4,8,32,128]{3,2,1,0:T(8,128)(2,1)S(1)} %edge_half1.6.refs_2_.second_ref, bf16[4,8,32,128]{3,2,1,0:T(8,128)(2,1)S(1)} %pad_maximum_fusion.refs_3_, ...), custom_call_target="tpu_custom_call" | custom-call | flops 20132659200 | bytes 157286400 | tf_op jit(solution)/shard_map/edge_half1/pallas_call | solution.py:181
  114.9 1.5 %unpack.7 = (bf16[4,4,8,64,128]{4,3,2,1,0:T(8,128)(2,1)}, f32[8,128]{1,0:T(8,128)}) custom-call(bf16[4,8,32,128]{3,2,1,0:T(8,128)(2,1)S(1)} %edge_half0.7.first_ref, bf16[4,8,32,128]{3,2,1,0:T(8,128)(2,1)S(1)} %edge_half1.7.second_ref, bf16[4,4,8,64,128]{4,3,2,1,0:T(8,128)(2,1)} %get-tuple-element.77.refs_0_), custom_call_target="tpu_custom_call", output_to_operand_aliasing={{0}: (2, {})} | custom-call | tf_op jit(solution)/shard_map/unpack/pallas_call | solution.py:79
  (79 shorter events, 1.2 us)
Async XLA Ops:
  0.0 1.0 copy-start.1
  1.2 13.7 %collective-permute-start = (bf16[4,8,32,128]{3,2,1,0:T(8,128)(2,1)S(1)}, bf16[4,8,32,128]{3,2,1,0:T(8,128)(2,1)S(1)}, u32[]{:S(2)}, u32[]{:S(2)}) collective-permute-start(bf16[4,8,32,128]{3,2,1,0:T(8,128)(2,1)S(1)} %get-tuple-element.44.refs_2_), channel_id=1, source_target_pairs={{0,1},{1,2},{2,3},{3,0},{4,5},{5,6},{6,7},{7,4},{8,9},{9,10},{10,1... | collective-permute-start | bytes 786440 | tf_op jit(solution)/shard_map/ppermute | solution.py:202
  4.3 15.0 %collective-permute-start.1 = (bf16[4,8,32,128]{3,2,1,0:T(8,128)(2,1)S(1)}, bf16[4,8,32,128]{3,2,1,0:T(8,128)(2,1)S(1)}, u32[]{:S(2)}, u32[]{:S(2)}) collective-permute-start(bf16[4,8,32,128]{3,2,1,0:T(8,128)(2,1)S(1)} %get-tuple-element.44.refs_2_), channel_id=1, source_target_pairs={{1,0},{2,1},{3,2},{0,3},{5,4},{6,5},{7,6},{4,7},{9,8},{10,9},{11,1... | collective-permute-start | bytes 786440 | tf_op jit(solution)/shard_map/ppermute | solution.py:202
  6.4 26.7 %collective-permute-start.6 = (bf16[4,8,32,128]{3,2,1,0:T(8,128)(2,1)S(1)}, bf16[4,8,32,128]{3,2,1,0:T(8,128)(2,1)S(1)}, u32[]{:S(2)}, u32[]{:S(2)}) collective-permute-start(bf16[4,8,32,128]{3,2,1,0:T(8,128)(2,1)S(1)} %get-tuple-element.48.refs_2_), channel_id=1, source_target_pairs={{0,1},{1,2},{2,3},{3,0},{4,5},{5,6},{6,7},{7,4},{8,9},{9,10},{10,1... | collective-permute-start | bytes 786440 | tf_op jit(solution)/shard_map/ppermute | solution.py:202
  6.4 26.7 %collective-permute-start.7 = (bf16[4,8,32,128]{3,2,1,0:T(8,128)(2,1)S(1)}, bf16[4,8,32,128]{3,2,1,0:T(8,128)(2,1)S(1)}, u32[]{:S(2)}, u32[]{:S(2)}) collective-permute-start(bf16[4,8,32,128]{3,2,1,0:T(8,128)(2,1)S(1)} %get-tuple-element.48.refs_2_), channel_id=1, source_target_pairs={{1,0},{2,1},{3,2},{0,3},{5,4},{6,5},{7,6},{4,7},{9,8},{10,9},{11,1... | collective-permute-start | bytes 786440 | tf_op jit(solution)/shard_map/ppermute | solution.py:202
  10.2 1.9 %copy-start = (bf16[4,1,8,64,768]{4,3,2,1,0:T(8,128)(2,1)S(1)}, bf16[4,1,8,64,768]{4,3,2,1,0:T(8,128)(2,1)}, u32[]{:S(2)}) copy-start(bf16[4,1,8,64,768]{4,3,2,1,0:T(8,128)(2,1)} %param.4) | copy-start | bytes 9437188
  12.1 2.7 %copy-start.2 = (s32[1,8,12]{2,1,0:T(8,128)S(1)}, s32[1,8,12]{2,1,0:T(8,128)}, u32[]{:S(2)}) copy-start(s32[1,8,12]{2,1,0:T(8,128)} %param.5) | copy-start | bytes 1156
  19.4 4.1 %collective-permute-start.3 = (bf16[3,8,32,128]{3,2,1,0:T(8,128)(2,1)S(1)}, bf16[3,8,32,128]{3,2,1,0:T(8,128)(2,1)S(1)}, u32[]{:S(2)}, u32[]{:S(2)}) collective-permute-start(bf16[3,8,32,128]{3,2,1,0:T(8,128)(2,1)S(1)} %pad_maximum_fusion.3.refs_5_), channel_id=1, source_target_pairs={{4,0},{8,4},{12,8},{16,12},{20,16},{24,20},{28,24},{0,28},{5,1},{9... | collective-permute-start | bytes 589832 | tf_op jit(solution)/shard_map/ppermute | solution.py:202
  19.5 8.2 %collective-permute-start.2 = (bf16[3,8,32,128]{3,2,1,0:T(8,128)(2,1)S(1)}, bf16[3,8,32,128]{3,2,1,0:T(8,128)(2,1)S(1)}, u32[]{:S(2)}, u32[]{:S(2)}) collective-permute-start(bf16[3,8,32,128]{3,2,1,0:T(8,128)(2,1)S(1)} %pad_maximum_fusion.2.refs_6_), channel_id=1, source_target_pairs={{0,4},{4,8},{8,12},{12,16},{16,20},{20,24},{24,28},{28,0},{1,5},{5... | collective-permute-start | bytes 589832 | tf_op jit(solution)/shard_map/ppermute | solution.py:202
  29.2 16.5 %collective-permute-start.4 = (bf16[4,8,32,128]{3,2,1,0:T(8,128)(2,1)S(1)}, bf16[4,8,32,128]{3,2,1,0:T(8,128)(2,1)S(1)}, u32[]{:S(2)}, u32[]{:S(2)}) collective-permute-start(bf16[4,8,32,128]{3,2,1,0:T(8,128)(2,1)S(1)} %edge_half0.4.refs_2_.first_ref), channel_id=1, source_target_pairs={{0,1},{1,2},{2,3},{3,0},{4,5},{5,6},{6,7},{7,4},{8,9},{9,10},{10,1... | collective-permute-start | bytes 786440 | tf_op jit(solution)/shard_map/ppermute | solution.py:202
  29.9 15.8 %collective-permute-start.5 = (bf16[4,8,32,128]{3,2,1,0:T(8,128)(2,1)S(1)}, bf16[4,8,32,128]{3,2,1,0:T(8,128)(2,1)S(1)}, u32[]{:S(2)}, u32[]{:S(2)}) collective-permute-start(bf16[4,8,32,128]{3,2,1,0:T(8,128)(2,1)S(1)} %edge_half0.4.refs_2_.first_ref), channel_id=1, source_target_pairs={{1,0},{2,1},{3,2},{0,3},{5,4},{6,5},{7,6},{4,7},{9,8},{10,9},{11,1... | collective-permute-start | bytes 786440 | tf_op jit(solution)/shard_map/ppermute | solution.py:202
  33.2 5.3 %collective-permute-start.9 = (bf16[3,8,32,128]{3,2,1,0:T(8,128)(2,1)S(1)}, bf16[3,8,32,128]{3,2,1,0:T(8,128)(2,1)S(1)}, u32[]{:S(2)}, u32[]{:S(2)}) collective-permute-start(bf16[3,8,32,128]{3,2,1,0:T(8,128)(2,1)S(1)} %pad_maximum_fusion.5.refs_5_), channel_id=1, source_target_pairs={{4,0},{8,4},{12,8},{16,12},{20,16},{24,20},{28,24},{0,28},{5,1},{9... | collective-permute-start | bytes 589832 | tf_op jit(solution)/shard_map/ppermute | solution.py:202
  33.3 7.0 %collective-permute-start.8 = (bf16[3,8,32,128]{3,2,1,0:T(8,128)(2,1)S(1)}, bf16[3,8,32,128]{3,2,1,0:T(8,128)(2,1)S(1)}, u32[]{:S(2)}, u32[]{:S(2)}) collective-permute-start(bf16[3,8,32,128]{3,2,1,0:T(8,128)(2,1)S(1)} %pad_maximum_fusion.4.refs_6_), channel_id=1, source_target_pairs={{0,4},{4,8},{8,12},{12,16},{16,20},{20,24},{24,28},{28,0},{1,5},{5... | collective-permute-start | bytes 589832 | tf_op jit(solution)/shard_map/ppermute | solution.py:202
  41.9 16.1 %collective-permute-start.14 = (bf16[4,8,32,128]{3,2,1,0:T(8,128)(2,1)S(1)}, bf16[4,8,32,128]{3,2,1,0:T(8,128)(2,1)S(1)}, u32[]{:S(2)}, u32[]{:S(2)}) collective-permute-start(bf16[4,8,32,128]{3,2,1,0:T(8,128)(2,1)S(1)} %edge_half1.4.refs_2_.second_ref), channel_id=1, source_target_pairs={{0,1},{1,2},{2,3},{3,0},{4,5},{5,6},{6,7},{7,4},{8,9},{9,10},{10,1... | collective-permute-start | bytes 786440 | tf_op jit(solution)/shard_map/ppermute | solution.py:202
  41.9 16.1 %collective-permute-start.15 = (bf16[4,8,32,128]{3,2,1,0:T(8,128)(2,1)S(1)}, bf16[4,8,32,128]{3,2,1,0:T(8,128)(2,1)S(1)}, u32[]{:S(2)}, u32[]{:S(2)}) collective-permute-start(bf16[4,8,32,128]{3,2,1,0:T(8,128)(2,1)S(1)} %edge_half1.4.refs_2_.second_ref), channel_id=1, source_target_pairs={{1,0},{2,1},{3,2},{0,3},{5,4},{6,5},{7,6},{4,7},{9,8},{10,9},{11,1... | collective-permute-start | bytes 786440 | tf_op jit(solution)/shard_map/ppermute | solution.py:202
  45.8 5.4 %collective-permute-start.11 = (bf16[3,8,32,128]{3,2,1,0:T(8,128)(2,1)S(1)}, bf16[3,8,32,128]{3,2,1,0:T(8,128)(2,1)S(1)}, u32[]{:S(2)}, u32[]{:S(2)}) collective-permute-start(bf16[3,8,32,128]{3,2,1,0:T(8,128)(2,1)S(1)} %pad_maximum_fusion.7.refs_5_), channel_id=1, source_target_pairs={{4,0},{8,4},{12,8},{16,12},{20,16},{24,20},{28,24},{0,28},{5,1},{9... | collective-permute-start | bytes 589832 | tf_op jit(solution)/shard_map/ppermute | solution.py:202
  46.3 6.2 %collective-permute-start.10 = (bf16[3,8,32,128]{3,2,1,0:T(8,128)(2,1)S(1)}, bf16[3,8,32,128]{3,2,1,0:T(8,128)(2,1)S(1)}, u32[]{:S(2)}, u32[]{:S(2)}) collective-permute-start(bf16[3,8,32,128]{3,2,1,0:T(8,128)(2,1)S(1)} %pad_maximum_fusion.6.refs_6_), channel_id=1, source_target_pairs={{0,4},{4,8},{8,12},{12,16},{16,20},{20,24},{24,28},{28,0},{1,5},{5... | collective-permute-start | bytes 589832 | tf_op jit(solution)/shard_map/ppermute | solution.py:202
  54.1 16.5 %collective-permute-start.12 = (bf16[4,8,32,128]{3,2,1,0:T(8,128)(2,1)S(1)}, bf16[4,8,32,128]{3,2,1,0:T(8,128)(2,1)S(1)}, u32[]{:S(2)}, u32[]{:S(2)}) collective-permute-start(bf16[4,8,32,128]{3,2,1,0:T(8,128)(2,1)S(1)} %edge_half0.5.refs_2_.first_ref), channel_id=1, source_target_pairs={{0,1},{1,2},{2,3},{3,0},{4,5},{5,6},{6,7},{7,4},{8,9},{9,10},{10,1... | collective-permute-start | bytes 786440 | tf_op jit(solution)/shard_map/ppermute | solution.py:202
  54.2 16.5 %collective-permute-start.13 = (bf16[4,8,32,128]{3,2,1,0:T(8,128)(2,1)S(1)}, bf16[4,8,32,128]{3,2,1,0:T(8,128)(2,1)S(1)}, u32[]{:S(2)}, u32[]{:S(2)}) collective-permute-start(bf16[4,8,32,128]{3,2,1,0:T(8,128)(2,1)S(1)} %edge_half0.5.refs_2_.first_ref), channel_id=1, source_target_pairs={{1,0},{2,1},{3,2},{0,3},{5,4},{6,5},{7,6},{4,7},{9,8},{10,9},{11,1... | collective-permute-start | bytes 786440 | tf_op jit(solution)/shard_map/ppermute | solution.py:202
  58.1 5.8 %collective-permute-start.17 = (bf16[3,8,32,128]{3,2,1,0:T(8,128)(2,1)S(1)}, bf16[3,8,32,128]{3,2,1,0:T(8,128)(2,1)S(1)}, u32[]{:S(2)}, u32[]{:S(2)}) collective-permute-start(bf16[3,8,32,128]{3,2,1,0:T(8,128)(2,1)S(1)} %pad_maximum_fusion.9.refs_5_), channel_id=1, source_target_pairs={{4,0},{8,4},{12,8},{16,12},{20,16},{24,20},{28,24},{0,28},{5,1},{9... | collective-permute-start | bytes 589832 | tf_op jit(solution)/shard_map/ppermute | solution.py:202
  59.1 6.0 %collective-permute-start.16 = (bf16[3,8,32,128]{3,2,1,0:T(8,128)(2,1)S(1)}, bf16[3,8,32,128]{3,2,1,0:T(8,128)(2,1)S(1)}, u32[]{:S(2)}, u32[]{:S(2)}) collective-permute-start(bf16[3,8,32,128]{3,2,1,0:T(8,128)(2,1)S(1)} %pad_maximum_fusion.8.refs_6_), channel_id=1, source_target_pairs={{0,4},{4,8},{8,12},{12,16},{16,20},{20,24},{24,28},{28,0},{1,5},{5... | collective-permute-start | bytes 589832 | tf_op jit(solution)/shard_map/ppermute | solution.py:202
  66.7 16.5 %collective-permute-start.22 = (bf16[4,8,32,128]{3,2,1,0:T(8,128)(2,1)S(1)}, bf16[4,8,32,128]{3,2,1,0:T(8,128)(2,1)S(1)}, u32[]{:S(2)}, u32[]{:S(2)}) collective-permute-start(bf16[4,8,32,128]{3,2,1,0:T(8,128)(2,1)S(1)} %edge_half1.5.refs_2_.second_ref), channel_id=1, source_target_pairs={{0,1},{1,2},{2,3},{3,0},{4,5},{5,6},{6,7},{7,4},{8,9},{9,10},{10,1... | collective-permute-start | bytes 786440 | tf_op jit(solution)/shard_map/ppermute | solution.py:202
  66.8 16.4 %collective-permute-start.23 = (bf16[4,8,32,128]{3,2,1,0:T(8,128)(2,1)S(1)}, bf16[4,8,32,128]{3,2,1,0:T(8,128)(2,1)S(1)}, u32[]{:S(2)}, u32[]{:S(2)}) collective-permute-start(bf16[4,8,32,128]{3,2,1,0:T(8,128)(2,1)S(1)} %edge_half1.5.refs_2_.second_ref), channel_id=1, source_target_pairs={{1,0},{2,1},{3,2},{0,3},{5,4},{6,5},{7,6},{4,7},{9,8},{10,9},{11,1... | collective-permute-start | bytes 786440 | tf_op jit(solution)/shard_map/ppermute | solution.py:202
  70.7 5.6 %collective-permute-start.19 = (bf16[3,8,32,128]{3,2,1,0:T(8,128)(2,1)S(1)}, bf16[3,8,32,128]{3,2,1,0:T(8,128)(2,1)S(1)}, u32[]{:S(2)}, u32[]{:S(2)}) collective-permute-start(bf16[3,8,32,128]{3,2,1,0:T(8,128)(2,1)S(1)} %pad_maximum_fusion.11.refs_5_), channel_id=1, source_target_pairs={{4,0},{8,4},{12,8},{16,12},{20,16},{24,20},{28,24},{0,28},{5,1},{9... | collective-permute-start | bytes 589832 | tf_op jit(solution)/shard_map/ppermute | solution.py:202
  71.7 6.0 %collective-permute-start.18 = (bf16[3,8,32,128]{3,2,1,0:T(8,128)(2,1)S(1)}, bf16[3,8,32,128]{3,2,1,0:T(8,128)(2,1)S(1)}, u32[]{:S(2)}, u32[]{:S(2)}) collective-permute-start(bf16[3,8,32,128]{3,2,1,0:T(8,128)(2,1)S(1)} %pad_maximum_fusion.10.refs_6_), channel_id=1, source_target_pairs={{0,4},{4,8},{8,12},{12,16},{16,20},{20,24},{24,28},{28,0},{1,5},{5... | collective-permute-start | bytes 589832 | tf_op jit(solution)/shard_map/ppermute | solution.py:202
  79.4 16.5 %collective-permute-start.20 = (bf16[4,8,32,128]{3,2,1,0:T(8,128)(2,1)S(1)}, bf16[4,8,32,128]{3,2,1,0:T(8,128)(2,1)S(1)}, u32[]{:S(2)}, u32[]{:S(2)}) collective-permute-start(bf16[4,8,32,128]{3,2,1,0:T(8,128)(2,1)S(1)} %edge_half0.6.refs_2_.first_ref), channel_id=1, source_target_pairs={{0,1},{1,2},{2,3},{3,0},{4,5},{5,6},{6,7},{7,4},{8,9},{9,10},{10,1... | collective-permute-start | bytes 786440 | tf_op jit(solution)/shard_map/ppermute | solution.py:202
  79.4 20.3 %collective-permute-start.21 = (bf16[4,8,32,128]{3,2,1,0:T(8,128)(2,1)S(1)}, bf16[4,8,32,128]{3,2,1,0:T(8,128)(2,1)S(1)}, u32[]{:S(2)}, u32[]{:S(2)}) collective-permute-start(bf16[4,8,32,128]{3,2,1,0:T(8,128)(2,1)S(1)} %edge_half0.6.refs_2_.first_ref), channel_id=1, source_target_pairs={{1,0},{2,1},{3,2},{0,3},{5,4},{6,5},{7,6},{4,7},{9,8},{10,9},{11,1... | collective-permute-start | bytes 786440 | tf_op jit(solution)/shard_map/ppermute | solution.py:202
  83.3 5.3 %collective-permute-start.25 = (bf16[3,8,32,128]{3,2,1,0:T(8,128)(2,1)S(1)}, bf16[3,8,32,128]{3,2,1,0:T(8,128)(2,1)S(1)}, u32[]{:S(2)}, u32[]{:S(2)}) collective-permute-start(bf16[3,8,32,128]{3,2,1,0:T(8,128)(2,1)S(1)} %pad_maximum_fusion.13.refs_5_), channel_id=1, source_target_pairs={{4,0},{8,4},{12,8},{16,12},{20,16},{24,20},{28,24},{0,28},{5,1},{9... | collective-permute-start | bytes 589832 | tf_op jit(solution)/shard_map/ppermute | solution.py:202
  84.2 6.1 %collective-permute-start.24 = (bf16[3,8,32,128]{3,2,1,0:T(8,128)(2,1)S(1)}, bf16[3,8,32,128]{3,2,1,0:T(8,128)(2,1)S(1)}, u32[]{:S(2)}, u32[]{:S(2)}) collective-permute-start(bf16[3,8,32,128]{3,2,1,0:T(8,128)(2,1)S(1)} %pad_maximum_fusion.12.refs_6_), channel_id=1, source_target_pairs={{0,4},{4,8},{8,12},{12,16},{16,20},{20,24},{24,28},{28,0},{1,5},{5... | collective-permute-start | bytes 589832 | tf_op jit(solution)/shard_map/ppermute | solution.py:202
  92.0 9.5 %collective-permute-start.28 = (bf16[2,8,32,128]{3,2,1,0:T(8,128)(2,1)S(1)}, bf16[2,8,32,128]{3,2,1,0:T(8,128)(2,1)S(1)}, u32[]{:S(2)}, u32[]{:S(2)}) collective-permute-start(bf16[2,8,32,128]{3,2,1,0:T(8,128)(2,1)S(1)} %pad_maximum_fusion.18), channel_id=1, source_target_pairs={{0,1},{1,2},{2,3},{3,0},{4,5},{5,6},{6,7},{7,4},{8,9},{9,10},{10,1... | collective-permute-start | bytes 393224 | tf_op jit(solution)/shard_map/ppermute | solution.py:202
  92.0 10.0 %collective-permute-start.29 = (bf16[2,8,32,128]{3,2,1,0:T(8,128)(2,1)S(1)}, bf16[2,8,32,128]{3,2,1,0:T(8,128)(2,1)S(1)}, u32[]{:S(2)}, u32[]{:S(2)}) collective-permute-start(bf16[2,8,32,128]{3,2,1,0:T(8,128)(2,1)S(1)} %pad_maximum_fusion.18), channel_id=1, source_target_pairs={{1,0},{2,1},{3,2},{0,3},{5,4},{6,5},{7,6},{4,7},{9,8},{10,9},{11,1... | collective-permute-start | bytes 393224 | tf_op jit(solution)/shard_map/ppermute | solution.py:202
  95.8 14.8 %collective-permute-start.30 = (bf16[2,8,32,128]{3,2,1,0:T(8,128)(2,1)S(1)}, bf16[2,8,32,128]{3,2,1,0:T(8,128)(2,1)S(1)}, u32[]{:S(2)}, u32[]{:S(2)}) collective-permute-start(bf16[2,8,32,128]{3,2,1,0:T(8,128)(2,1)S(1)} %slice.222), channel_id=1, source_target_pairs={{0,1},{1,2},{2,3},{3,0},{4,5},{5,6},{6,7},{7,4},{8,9},{9,10},{10,1... | collective-permute-start | bytes 393224 | tf_op jit(solution)/shard_map/ppermute | solution.py:202
  95.9 14.8 %collective-permute-start.31 = (bf16[2,8,32,128]{3,2,1,0:T(8,128)(2,1)S(1)}, bf16[2,8,32,128]{3,2,1,0:T(8,128)(2,1)S(1)}, u32[]{:S(2)}, u32[]{:S(2)}) collective-permute-start(bf16[2,8,32,128]{3,2,1,0:T(8,128)(2,1)S(1)} %slice.222), channel_id=1, source_target_pairs={{1,0},{2,1},{3,2},{0,3},{5,4},{6,5},{7,6},{4,7},{9,8},{10,9},{11,1... | collective-permute-start | bytes 393224 | tf_op jit(solution)/shard_map/ppermute | solution.py:202
  99.8 4.5 %collective-permute-start.27 = (bf16[3,8,32,128]{3,2,1,0:T(8,128)(2,1)S(1)}, bf16[3,8,32,128]{3,2,1,0:T(8,128)(2,1)S(1)}, u32[]{:S(2)}, u32[]{:S(2)}) collective-permute-start(bf16[3,8,32,128]{3,2,1,0:T(8,128)(2,1)S(1)} %pad_maximum_fusion.15.refs_5_), channel_id=1, source_target_pairs={{4,0},{8,4},{12,8},{16,12},{20,16},{24,20},{28,24},{0,28},{5,1},{9... | collective-permute-start | bytes 589832 | tf_op jit(solution)/shard_map/ppermute | solution.py:202
  101.4 7.7 %collective-permute-start.26 = (bf16[3,8,32,128]{3,2,1,0:T(8,128)(2,1)S(1)}, bf16[3,8,32,128]{3,2,1,0:T(8,128)(2,1)S(1)}, u32[]{:S(2)}, u32[]{:S(2)}) collective-permute-start(bf16[3,8,32,128]{3,2,1,0:T(8,128)(2,1)S(1)} %pad_maximum_fusion.14.refs_6_), channel_id=1, source_target_pairs={{0,4},{4,8},{8,12},{12,16},{16,20},{20,24},{24,28},{28,0},{1,5},{5... | collective-permute-start | bytes 589832 | tf_op jit(solution)/shard_map/ppermute | solution.py:202
  102.1 11.2 %collective-permute-start.33 = (bf16[3,8,32,128]{3,2,1,0:T(8,128)(2,1)S(1)}, bf16[3,8,32,128]{3,2,1,0:T(8,128)(2,1)S(1)}, u32[]{:S(2)}, u32[]{:S(2)}) collective-permute-start(bf16[3,8,32,128]{3,2,1,0:T(8,128)(2,1)S(1)} %pad_maximum_fusion.17.refs_5_), channel_id=1, source_target_pairs={{4,0},{8,4},{12,8},{16,12},{20,16},{24,20},{28,24},{0,28},{5,1},{9... | collective-permute-start | bytes 589832 | tf_op jit(solution)/shard_map/ppermute | solution.py:202
  104.3 9.0 %collective-permute-start.32 = (bf16[3,8,32,128]{3,2,1,0:T(8,128)(2,1)S(1)}, bf16[3,8,32,128]{3,2,1,0:T(8,128)(2,1)S(1)}, u32[]{:S(2)}, u32[]{:S(2)}) collective-permute-start(bf16[3,8,32,128]{3,2,1,0:T(8,128)(2,1)S(1)} %pad_maximum_fusion.16.refs_6_), channel_id=1, source_target_pairs={{0,4},{4,8},{8,12},{12,16},{16,20},{20,24},{24,28},{28,0},{1,5},{5... | collective-permute-start | bytes 589832 | tf_op jit(solution)/shard_map/ppermute | solution.py:202

commit v10 on v7

--- a/solution.py
+++ b/solution.py
@@ -9,6 +9,7 @@
 
 STEPS = 4
 HALVES = 2
+WEIGHT = 100
 VMEM_LIMIT = 4 * 1024 * 1024
 VMEM = pl.BlockSpec(memory_space=pltpu.VMEM)
 ANY = pl.BlockSpec(memory_space=pl.ANY)
@@ -91,21 +92,26 @@
     )(first, second, *extra)
 
 
-def edges(own, low_az, high_az, after):
-    *trio, _ = lax.optimization_barrier((low_az, own, high_az, after))
-    columns = own.shape[0]
-    return jnp.stack([part[0] for part in trio]), jnp.stack([part[columns - 1] for part in trio])
+def held(values, *after):
+    return lax.optimization_barrier((tuple(values), after))[0]
+
+
+def edges(values, *after):
+    values = held(values, *after)
+    return jnp.stack([value[0] for value in values]), jnp.stack([value[-1] for value in values])
 
 
 def part_kernel(half, *refs):
-    table, blocks, own, low_az, high_az = refs[:5]
-    following, window = refs[-2:]
-    edge = len(refs) > 9
+    table_ref, blocks, own, low_az, high_az = refs[:5]
+    following, window, index, sem = refs[-4:]
+    edge = len(refs) > 13
     faces, width, depth = blocks.shape[1:]
     columns = own.shape[0]
     span = columns + 2
     rows, lanes = window.shape[1:]
     view = window.reshape(3, span, faces, rows, lanes)
+    indexing = pltpu.make_async_copy(table_ref, index, sem)
+    indexing.start()
 
     def enter(column, carry):
         for azim, source in enumerate((low_az, own, high_az)):
@@ -115,18 +121,21 @@
 
     lax.fori_loop(0, columns, enter, 0)
     if edge:
-        low_st, high_st, before = refs[5:8]
+        low_st, high_st, low_rest, high_rest, before = refs[5:10]
 
         def enter_stream(face, carry):
-            for azim in range(3):
+            for azim in range(2):
                 view[azim, 0, face] = low_st[azim, face]
                 view[azim, span - 1, face] = high_st[azim, face]
+            view[2, 0, face] = low_rest[0, face]
+            view[2, span - 1, face] = high_rest[0, face]
             for column in range(columns - 2):
                 following[column + 1, face] = before[column, face]
             return carry
 
         lax.fori_loop(0, faces, enter_stream, 0)
-    neighbours = table.shape[1]
+    indexing.wait()
+    neighbours = index.shape[1]
     low = low_lanes((rows, lanes))
 
     def turn(n, carry):
@@ -134,7 +143,7 @@
         slot = column if edge else n
         for face in range(faces):
             gathered = jnp.concatenate(
-                [window[table[face, k] + column * faces] for k in range(neighbours)], axis=0
+                [window[index[face, k] + column * faces] for k in range(neighbours)], axis=0
             )
             block = blocks[column, face]
             stacked = jnp.concatenate([block[:, : depth // 2], block[:, depth // 2 :]], axis=0)
@@ -155,20 +164,23 @@
 def part(half, table, blocks, pieces, rest):
     columns, faces, width, depth = blocks.shape
     rows, lanes = pieces[0].shape[2:]
-    edge = len(rest) > 2
+    edge = len(rest) > 4
     name = "edge" if edge else "inner"
     done, kept = (2, columns) if edge else (columns - 2, columns - 2)
-    in_specs = [pl.BlockSpec(memory_space=pltpu.SMEM)] + [VMEM] * 4
-    in_specs += [VMEM] * 3 + [ANY] if edge else [ANY] * 2
+    in_specs = [ANY] + [VMEM] * 4 + ([VMEM] * 5 + [ANY] if edge else [ANY] * 4)
     return pl.pallas_call(
         functools.partial(part_kernel, half),
         in_specs=in_specs,
         out_specs=VMEM,
         out_shape=jax.ShapeDtypeStruct((kept, faces, rows, lanes), jnp.bfloat16),
-        scratch_shapes=[pltpu.VMEM((3 * (columns + 2) * faces, rows, lanes), jnp.bfloat16)],
+        scratch_shapes=[
+            pltpu.VMEM((3 * (columns + 2) * faces, rows, lanes), jnp.bfloat16),
+            pltpu.SMEM(table.shape, jnp.int32),
+            pltpu.SemaphoreType.DMA,
+        ],
         cost_estimate=pl.CostEstimate(
-            flops=2 * done * faces * width * depth * lanes,
-            bytes_accessed=2 * done * faces * width * depth,
+            flops=WEIGHT * 2 * done * faces * width * depth * lanes,
+            bytes_accessed=WEIGHT * 2 * done * faces * width * depth,
             transcendentals=0,
         ),
         compiler_params=pltpu.CompilerParams(vmem_limit_bytes=VMEM_LIMIT),
@@ -238,11 +250,19 @@
         previous = tuple(current)
         for h in range(HALVES):
             pieces = (current[h], lows[h], highs[h])
-            to_low, to_high = edges(*pieces, latest)
-            stream = (shift(to_high, "stream", True), shift(to_low, "stream", False))
-            middle = part(h, table, blocks, pieces, (to_low, to_high))
-            after = middle
-            if h == 1 and index > 0:
+            to_low, to_high = edges((lows[h], current[h]), latest)
+            low_st = shift(to_high, "stream", True)
+            high_st = shift(to_low, "stream", False)
+            rest_low, rest_high = edges((highs[h],), low_st, high_st)
+            stream = (
+                low_st,
+                high_st,
+                shift(rest_high, "stream", True),
+                shift(rest_low, "stream", False),
+            )
+            sent = (to_low, to_high, rest_low, rest_high)
+            after = middle = part(h, table, blocks, pieces, sent)
+            if h == 0 and index > 0:
                 basis, after = unpack(index - 1, every, *previous, basis, middle)
             current[h] = latest = part(h, table, blocks, pieces, (*stream, middle, after))
             if index < STEPS - 1:

time: 116 us -> 135 us (1.16); the launches traced: 116 us -> 133 us
  starting transfers between devices: 40 us -> 80 us
  waiting for transfers between devices: 40.4 us -> 18.4 us
    ppermute x32 -> x48, starting transfers between devices: 40 us -> 80 us  [shift(): return lax.ppermute(value, axis, pairs)]
    ppermute x32 -> x48, waiting for transfers between devices: 40.4 us -> 18.4 us  [shift(): return lax.ppermute(value, axis, pairs)]
  transfers between devices with their start and end apart: 32 -> 48, of which waited for: 17 -> 16; matrix products, arithmetic and copies ran while one was open for 1% -> 0% of each run, Pallas kernels for 25% -> 21%
where the time goes in v10:
time: 135 us; the launch traced here: 133 us
  starting transfers between devices  80 us (59%)
  Pallas kernels  30.7 us (23%)
  waiting for transfers between devices  18.4 us (14%)
  local copies, waits for them, and re-layouts  3.18 us (2%)
    ppermute x48, starting transfers between devices, shift(): return lax.ppermute(value, axis, pairs)  80 us
    pallas_call x16, Pallas kernels, part(): pl.pallas_call(functools.partial(part_kernel, half), in_specs=in_specs, o...  23.6 us
    ppermute x48, waiting for transfers between devices, shift(): return lax.ppermute(value, axis, pairs)  18.4 us
    pallas_call x4, Pallas kernels, unpack(): pl.pallas_call(functools.partial(unpack_kernel, index, chosen, skipped),...  4.25 us
    unnamed x6, local copies, waits for them, and re-layouts  2.93 us
    pallas_call x1, Pallas kernels, halves_of_rows(): pl.pallas_call(halves_kernel, in_specs=[VMEM], out_specs=VMEM, out_shape=...  2.72 us
  transfers between devices with their start and end apart: 48, of which 16 were waited for; matrix products, arithmetic and copies ran while one was open for 0% of the time, Pallas kernels for 21%

profile of v10, /device:TPU:0, one launch (start us, length us, event | category | flops | bytes accessed | tf_op | source)
XLA Modules:
  0.0 133.4 jit_solution(8693953083971684981)
XLA Ops:
  0.0 1.0 copy-done.1
  1.2 3.1 %collective-permute-start = (bf16[4,8,32,128]{3,2,1,0:T(8,128)(2,1)S(1)}, bf16[4,8,32,128]{3,2,1,0:T(8,128)(2,1)S(1)}, u32[]{:S(2)}, u32[]{:S(2)}) collective-permute-start(bf16[4,8,32,128]{3,2,1,0:T(8,128)(2,1)S(1)} %get-tuple-element.40.refs_2_), channel_id=1, source_target_pairs={{0,1},{1,2},{2,3},{3,0},{4,5},{5,6},{6,7},{7,4},{8,9},{9,10},{10,1... | collective-permute-start | bytes 786440 | tf_op jit(solution)/shard_map/ppermute | solution.py:196
  4.3 2.1 %collective-permute-start.1 = (bf16[4,8,32,128]{3,2,1,0:T(8,128)(2,1)S(1)}, bf16[4,8,32,128]{3,2,1,0:T(8,128)(2,1)S(1)}, u32[]{:S(2)}, u32[]{:S(2)}) collective-permute-start(bf16[4,8,32,128]{3,2,1,0:T(8,128)(2,1)S(1)} %get-tuple-element.40.refs_2_), channel_id=1, source_target_pairs={{1,0},{2,1},{3,2},{0,3},{5,4},{6,5},{7,6},{4,7},{9,8},{10,9},{11,1... | collective-permute-start | bytes 786440 | tf_op jit(solution)/shard_map/ppermute | solution.py:196
  6.4 3.8 %collective-permute-start.9 = (bf16[4,8,32,128]{3,2,1,0:T(8,128)(2,1)S(1)}, bf16[4,8,32,128]{3,2,1,0:T(8,128)(2,1)S(1)}, u32[]{:S(2)}, u32[]{:S(2)}) collective-permute-start(bf16[4,8,32,128]{3,2,1,0:T(8,128)(2,1)S(1)} %get-tuple-element.44.refs_2_), channel_id=1, source_target_pairs={{1,0},{2,1},{3,2},{0,3},{5,4},{6,5},{7,6},{4,7},{9,8},{10,9},{11,1... | collective-permute-start | bytes 786440 | tf_op jit(solution)/shard_map/ppermute | solution.py:196
  10.2 1.9 %copy-done = bf16[4,1,8,64,768]{4,3,2,1,0:T(8,128)(2,1)S(1)} copy-done((bf16[4,1,8,64,768]{4,3,2,1,0:T(8,128)(2,1)S(1)}, bf16[4,1,8,64,768]{4,3,2,1,0:T(8,128)(2,1)}, u32[]{:S(2)}) %copy-start) | copy-done | bytes 3145752
  12.1 2.7 %halves_of_rows.1.refs_1_ = bf16[4,8,64,768]{3,2,1,0:T(8,128)(2,1)S(1)} custom-call(bf16[4,8,64,768]{3,2,1,0:T(8,128)(2,1)S(1)} %bitcast.29), custom_call_target="tpu_custom_call" | custom-call | tf_op jit(solution)/shard_map/halves_of_rows/pallas_call | solution.py:227
  14.9 1.1 collective-permute-start.3
  16.1 3.2 %collective-permute-done.1.refs_4_ = bf16[4,8,32,128]{3,2,1,0:T(8,128)(2,1)S(1)} collective-permute-done((bf16[4,8,32,128]{3,2,1,0:T(8,128)(2,1)S(1)}, bf16[4,8,32,128]{3,2,1,0:T(8,128)(2,1)S(1)}, u32[]{:S(2)}, u32[]{:S(2)}) %collective-permute-start.1) | collective-permute-done | bytes 262176 | tf_op jit(solution)/shard_map/ppermute | solution.py:196
  19.8 2.1 %collective-permute-done.2.refs_5_ = bf16[2,8,32,128]{3,2,1,0:T(8,128)(2,1)S(1)} collective-permute-done((bf16[2,8,32,128]{3,2,1,0:T(8,128)(2,1)S(1)}, bf16[2,8,32,128]{3,2,1,0:T(8,128)(2,1)S(1)}, u32[]{:S(2)}, u32[]{:S(2)}) %collective-permute-start.2) | collective-permute-done | bytes 131104 | tf_op jit(solution)/shard_map/ppermute | solution.py:196
  22.0 2.6 %collective-permute-start.5 = (bf16[1,8,32,128]{3,2,1,0:T(8,128)(2,1)S(1)}, bf16[1,8,32,128]{3,2,1,0:T(8,128)(2,1)S(1)}, u32[]{:S(2)}, u32[]{:S(2)}) collective-permute-start(bf16[1,8,32,128]{3,2,1,0:T(8,128)(2,1)S(1)} %get-tuple-element.113.refs_7_), channel_id=1, source_target_pairs={{4,0},{8,4},{12,8},{16,12},{20,16},{24,20},{28,24},{0,28},{5,1},{9... | collective-permute-start | bytes 196616 | tf_op jit(solution)/shard_map/ppermute | solution.py:196
  24.6 1.5 %inner_half0.4.refs_9_.refs_10_ = bf16[2,8,32,128]{3,2,1,0:T(8,128)(2,1)S(1)} custom-call(s32[8,12]{1,0:T(8,128)S(1)} %fusion.4.refs_0_, bf16[4,8,64,768]{3,2,1,0:T(8,128)(2,1)S(1)} %halves_of_rows.1.refs_1_, bf16[4,8,32,128]{3,2,1,0:T(8,128)(2,1)S(1)} %get-tuple-element.40.refs_2_, bf16[4,8,32,128]{3,2,1,0:T(8,128)(2,1)S(1)} %collective-permute-done.refs_3_, ...), custom_call_target="tpu_custom_call" | custom-call | flops 20132659200 | bytes 157286400 | tf_op jit(solution)/shard_map/inner_half0/pallas_call | solution.py:171
  26.1 1.1 collective-permute-done.4.refs_7_
  27.2 1.5 %edge_half0.4.refs_2_.first_ref = bf16[4,8,32,128]{3,2,1,0:T(8,128)(2,1)S(1)} custom-call(s32[8,12]{1,0:T(8,128)S(1)} %fusion.4.refs_0_, bf16[4,8,64,768]{3,2,1,0:T(8,128)(2,1)S(1)} %halves_of_rows.1.refs_1_, bf16[4,8,32,128]{3,2,1,0:T(8,128)(2,1)S(1)} %get-tuple-element.40.refs_2_, bf16[4,8,32,128]{3,2,1,0:T(8,128)(2,1)S(1)} %collective-permute-done.refs_3_, ...), custom_call_target="tpu_custom_call" | custom-call | flops 20132659200 | bytes 157286400 | tf_op jit(solution)/shard_map/edge_half0/pallas_call | solution.py:171
  28.7 2.1 %collective-permute-start.11 = (bf16[2,8,32,128]{3,2,1,0:T(8,128)(2,1)S(1)}, bf16[2,8,32,128]{3,2,1,0:T(8,128)(2,1)S(1)}, u32[]{:S(2)}, u32[]{:S(2)}) collective-permute-start(bf16[2,8,32,128]{3,2,1,0:T(8,128)(2,1)S(1)} %pad_maximum_fusion.3.refs_5_), channel_id=1, source_target_pairs={{4,0},{8,4},{12,8},{16,12},{20,16},{24,20},{28,24},{0,28},{5,1},{9... | collective-permute-start | bytes 393224 | tf_op jit(solution)/shard_map/ppermute | solution.py:196
  30.9 2.8 %collective-permute-start.6 = (bf16[4,8,32,128]{3,2,1,0:T(8,128)(2,1)S(1)}, bf16[4,8,32,128]{3,2,1,0:T(8,128)(2,1)S(1)}, u32[]{:S(2)}, u32[]{:S(2)}) collective-permute-start(bf16[4,8,32,128]{3,2,1,0:T(8,128)(2,1)S(1)} %edge_half0.4.refs_2_.first_ref), channel_id=1, source_target_pairs={{0,1},{1,2},{2,3},{3,0},{4,5},{5,6},{6,7},{7,4},{8,9},{9,10},{10,1... | collective-permute-start | bytes 786440 | tf_op jit(solution)/shard_map/ppermute | solution.py:196
  33.7 3.4 %collective-permute-start.7 = (bf16[4,8,32,128]{3,2,1,0:T(8,128)(2,1)S(1)}, bf16[4,8,32,128]{3,2,1,0:T(8,128)(2,1)S(1)}, u32[]{:S(2)}, u32[]{:S(2)}) collective-permute-start(bf16[4,8,32,128]{3,2,1,0:T(8,128)(2,1)S(1)} %edge_half0.4.refs_2_.first_ref), channel_id=1, source_target_pairs={{1,0},{2,1},{3,2},{0,3},{5,4},{6,5},{7,6},{4,7},{9,8},{10,9},{11,1... | collective-permute-start | bytes 786440 | tf_op jit(solution)/shard_map/ppermute | solution.py:196
  37.2 2.6 %collective-permute-start.13 = (bf16[1,8,32,128]{3,2,1,0:T(8,128)(2,1)S(1)}, bf16[1,8,32,128]{3,2,1,0:T(8,128)(2,1)S(1)}, u32[]{:S(2)}, u32[]{:S(2)}) collective-permute-start(bf16[1,8,32,128]{3,2,1,0:T(8,128)(2,1)S(1)} %get-tuple-element.107.refs_7_), channel_id=1, source_target_pairs={{4,0},{8,4},{12,8},{16,12},{20,16},{24,20},{28,24},{0,28},{5,1},{9... | collective-permute-start | bytes 196616 | tf_op jit(solution)/shard_map/ppermute | solution.py:196
  39.8 1.5 %inner_half1.4.refs_9_.refs_10_ = bf16[2,8,32,128]{3,2,1,0:T(8,128)(2,1)S(1)} custom-call(s32[8,12]{1,0:T(8,128)S(1)} %fusion.4.refs_0_, bf16[4,8,64,768]{3,2,1,0:T(8,128)(2,1)S(1)} %halves_of_rows.1.refs_1_, bf16[4,8,32,128]{3,2,1,0:T(8,128)(2,1)S(1)} %get-tuple-element.44.refs_2_, bf16[4,8,32,128]{3,2,1,0:T(8,128)(2,1)S(1)} %collective-permute-done.8.refs_3_, ...), custom_call_target="tpu_custom_call" | custom-call | flops 20132659200 | bytes 157286400 | tf_op jit(solution)/shard_map/inner_half1/pallas_call | solution.py:171
  41.3 0.9 collective-permute-done.12.refs_7_
  42.2 1.5 %edge_half1.4.second_ref.refs_2_ = bf16[4,8,32,128]{3,2,1,0:T(8,128)(2,1)S(1)} custom-call(s32[8,12]{1,0:T(8,128)S(1)} %fusion.4.refs_0_, bf16[4,8,64,768]{3,2,1,0:T(8,128)(2,1)S(1)} %halves_of_rows.1.refs_1_, bf16[4,8,32,128]{3,2,1,0:T(8,128)(2,1)S(1)} %get-tuple-element.44.refs_2_, bf16[4,8,32,128]{3,2,1,0:T(8,128)(2,1)S(1)} %collective-permute-done.8.refs_3_, ...), custom_call_target="tpu_custom_call" | custom-call | flops 20132659200 | bytes 157286400 | tf_op jit(solution)/shard_map/edge_half1/pallas_call | solution.py:171
  43.7 0.6 collective-permute-done.6.refs_3_
  44.4 1.8 %collective-permute-start.15 = (bf16[2,8,32,128]{3,2,1,0:T(8,128)(2,1)S(1)}, bf16[2,8,32,128]{3,2,1,0:T(8,128)(2,1)S(1)}, u32[]{:S(2)}, u32[]{:S(2)}) collective-permute-start(bf16[2,8,32,128]{3,2,1,0:T(8,128)(2,1)S(1)} %pad_maximum_fusion.5.refs_5_), channel_id=1, source_target_pairs={{4,0},{8,4},{12,8},{16,12},{20,16},{24,20},{28,24},{0,28},{5,1},{9... | collective-permute-start | bytes 393224 | tf_op jit(solution)/shard_map/ppermute | solution.py:196
  46.3 3.0 %collective-permute-start.20 = (bf16[4,8,32,128]{3,2,1,0:T(8,128)(2,1)S(1)}, bf16[4,8,32,128]{3,2,1,0:T(8,128)(2,1)S(1)}, u32[]{:S(2)}, u32[]{:S(2)}) collective-permute-start(bf16[4,8,32,128]{3,2,1,0:T(8,128)(2,1)S(1)} %edge_half1.4.second_ref.refs_2_), channel_id=1, source_target_pairs={{0,1},{1,2},{2,3},{3,0},{4,5},{5,6},{6,7},{7,4},{8,9},{9,10},{10,1... | collective-permute-start | bytes 786440 | tf_op jit(solution)/shard_map/ppermute | solution.py:196
  49.2 2.7 %collective-permute-start.21 = (bf16[4,8,32,128]{3,2,1,0:T(8,128)(2,1)S(1)}, bf16[4,8,32,128]{3,2,1,0:T(8,128)(2,1)S(1)}, u32[]{:S(2)}, u32[]{:S(2)}) collective-permute-start(bf16[4,8,32,128]{3,2,1,0:T(8,128)(2,1)S(1)} %edge_half1.4.second_ref.refs_2_), channel_id=1, source_target_pairs={{1,0},{2,1},{3,2},{0,3},{5,4},{6,5},{7,6},{4,7},{9,8},{10,9},{11,1... | collective-permute-start | bytes 786440 | tf_op jit(solution)/shard_map/ppermute | solution.py:196
  52.0 2.6 %collective-permute-start.17 = (bf16[1,8,32,128]{3,2,1,0:T(8,128)(2,1)S(1)}, bf16[1,8,32,128]{3,2,1,0:T(8,128)(2,1)S(1)}, u32[]{:S(2)}, u32[]{:S(2)}) collective-permute-start(bf16[1,8,32,128]{3,2,1,0:T(8,128)(2,1)S(1)} %get-tuple-element.101.refs_7_), channel_id=1, source_target_pairs={{4,0},{8,4},{12,8},{16,12},{20,16},{24,20},{28,24},{0,28},{5,1},{9... | collective-permute-start | bytes 196616 | tf_op jit(solution)/shard_map/ppermute | solution.py:196
  54.7 1.5 %inner_half0.5.refs_0_.refs_9_ = bf16[2,8,32,128]{3,2,1,0:T(8,128)(2,1)S(1)} custom-call(s32[8,12]{1,0:T(8,128)S(1)} %fusion.4.refs_0_, bf16[4,8,64,768]{3,2,1,0:T(8,128)(2,1)S(1)} %halves_of_rows.1.refs_1_, bf16[4,8,32,128]{3,2,1,0:T(8,128)(2,1)S(1)} %edge_half0.4.refs_2_.first_ref, bf16[4,8,32,128]{3,2,1,0:T(8,128)(2,1)S(1)} %collective-permute-done.6.refs_3_, ...), custom_call_target="tpu_custom_call" | custom-call | flops 20132659200 | bytes 157286400 | tf_op jit(solution)/shard_map/inner_half0/pallas_call | solution.py:171
  56.1 0.9 unpack.4
  57.1 1.5 %edge_half0.5.refs_2_.first_ref = bf16[4,8,32,128]{3,2,1,0:T(8,128)(2,1)S(1)} custom-call(s32[8,12]{1,0:T(8,128)S(1)} %fusion.4.refs_0_, bf16[4,8,64,768]{3,2,1,0:T(8,128)(2,1)S(1)} %halves_of_rows.1.refs_1_, bf16[4,8,32,128]{3,2,1,0:T(8,128)(2,1)S(1)} %edge_half0.4.refs_2_.first_ref, bf16[4,8,32,128]{3,2,1,0:T(8,128)(2,1)S(1)} %collective-permute-done.6.refs_3_, ...), custom_call_target="tpu_custom_call" | custom-call | flops 20132659200 | bytes 157286400 | tf_op jit(solution)/shard_map/edge_half0/pallas_call | solution.py:171
  59.2 1.8 %collective-permute-start.23 = (bf16[2,8,32,128]{3,2,1,0:T(8,128)(2,1)S(1)}, bf16[2,8,32,128]{3,2,1,0:T(8,128)(2,1)S(1)}, u32[]{:S(2)}, u32[]{:S(2)}) collective-permute-start(bf16[2,8,32,128]{3,2,1,0:T(8,128)(2,1)S(1)} %pad_maximum_fusion.7.refs_5_), channel_id=1, source_target_pairs={{4,0},{8,4},{12,8},{16,12},{20,16},{24,20},{28,24},{0,28},{5,1},{9... | collective-permute-start | bytes 393224 | tf_op jit(solution)/shard_map/ppermute | solution.py:196
  61.1 3.0 %collective-permute-start.18 = (bf16[4,8,32,128]{3,2,1,0:T(8,128)(2,1)S(1)}, bf16[4,8,32,128]{3,2,1,0:T(8,128)(2,1)S(1)}, u32[]{:S(2)}, u32[]{:S(2)}) collective-permute-start(bf16[4,8,32,128]{3,2,1,0:T(8,128)(2,1)S(1)} %edge_half0.5.refs_2_.first_ref), channel_id=1, source_target_pairs={{0,1},{1,2},{2,3},{3,0},{4,5},{5,6},{6,7},{7,4},{8,9},{9,10},{10,1... | collective-permute-start | bytes 786440 | tf_op jit(solution)/shard_map/ppermute | solution.py:196
  64.0 2.7 %collective-permute-start.19 = (bf16[4,8,32,128]{3,2,1,0:T(8,128)(2,1)S(1)}, bf16[4,8,32,128]{3,2,1,0:T(8,128)(2,1)S(1)}, u32[]{:S(2)}, u32[]{:S(2)}) collective-permute-start(bf16[4,8,32,128]{3,2,1,0:T(8,128)(2,1)S(1)} %edge_half0.5.refs_2_.first_ref), channel_id=1, source_target_pairs={{1,0},{2,1},{3,2},{0,3},{5,4},{6,5},{7,6},{4,7},{9,8},{10,9},{11,1... | collective-permute-start | bytes 786440 | tf_op jit(solution)/shard_map/ppermute | solution.py:196
  66.8 2.6 %collective-permute-start.25 = (bf16[1,8,32,128]{3,2,1,0:T(8,128)(2,1)S(1)}, bf16[1,8,32,128]{3,2,1,0:T(8,128)(2,1)S(1)}, u32[]{:S(2)}, u32[]{:S(2)}) collective-permute-start(bf16[1,8,32,128]{3,2,1,0:T(8,128)(2,1)S(1)} %get-tuple-element.95.refs_7_), channel_id=1, source_target_pairs={{4,0},{8,4},{12,8},{16,12},{20,16},{24,20},{28,24},{0,28},{5,1},{9... | collective-permute-start | bytes 196616 | tf_op jit(solution)/shard_map/ppermute | solution.py:196
  69.5 1.5 %inner_half1.5.refs_9_.refs_10_ = bf16[2,8,32,128]{3,2,1,0:T(8,128)(2,1)S(1)} custom-call(s32[8,12]{1,0:T(8,128)S(1)} %fusion.4.refs_0_, bf16[4,8,64,768]{3,2,1,0:T(8,128)(2,1)S(1)} %halves_of_rows.1.refs_1_, bf16[4,8,32,128]{3,2,1,0:T(8,128)(2,1)S(1)} %edge_half1.4.second_ref.refs_2_, bf16[4,8,32,128]{3,2,1,0:T(8,128)(2,1)S(1)} %collective-permute-done.20.refs_3_, ...), custom_call_target="tpu_custom_call" | custom-call | flops 20132659200 | bytes 157286400 | tf_op jit(solution)/shard_map/inner_half1/pallas_call | solution.py:171
  71.0 0.9 collective-permute-done.24.refs_7_
  71.8 1.5 %edge_half1.5.second_ref.refs_2_ = bf16[4,8,32,128]{3,2,1,0:T(8,128)(2,1)S(1)} custom-call(s32[8,12]{1,0:T(8,128)S(1)} %fusion.4.refs_0_, bf16[4,8,64,768]{3,2,1,0:T(8,128)(2,1)S(1)} %halves_of_rows.1.refs_1_, bf16[4,8,32,128]{3,2,1,0:T(8,128)(2,1)S(1)} %edge_half1.4.second_ref.refs_2_, bf16[4,8,32,128]{3,2,1,0:T(8,128)(2,1)S(1)} %collective-permute-done.20.refs_3_, ...), custom_call_target="tpu_custom_call" | custom-call | flops 20132659200 | bytes 157286400 | tf_op jit(solution)/shard_map/edge_half1/pallas_call | solution.py:171
  73.3 0.6 collective-permute-done.18.refs_3_
  74.0 1.8 %collective-permute-start.27 = (bf16[2,8,32,128]{3,2,1,0:T(8,128)(2,1)S(1)}, bf16[2,8,32,128]{3,2,1,0:T(8,128)(2,1)S(1)}, u32[]{:S(2)}, u32[]{:S(2)}) collective-permute-start(bf16[2,8,32,128]{3,2,1,0:T(8,128)(2,1)S(1)} %pad_maximum_fusion.9.refs_5_), channel_id=1, source_target_pairs={{4,0},{8,4},{12,8},{16,12},{20,16},{24,20},{28,24},{0,28},{5,1},{9... | collective-permute-start | bytes 393224 | tf_op jit(solution)/shard_map/ppermute | solution.py:196
  75.9 3.0 %collective-permute-start.32 = (bf16[4,8,32,128]{3,2,1,0:T(8,128)(2,1)S(1)}, bf16[4,8,32,128]{3,2,1,0:T(8,128)(2,1)S(1)}, u32[]{:S(2)}, u32[]{:S(2)}) collective-permute-start(bf16[4,8,32,128]{3,2,1,0:T(8,128)(2,1)S(1)} %edge_half1.5.second_ref.refs_2_), channel_id=1, source_target_pairs={{0,1},{1,2},{2,3},{3,0},{4,5},{5,6},{6,7},{7,4},{8,9},{9,10},{10,1... | collective-permute-start | bytes 786440 | tf_op jit(solution)/shard_map/ppermute | solution.py:196
  78.9 2.7 %collective-permute-start.33 = (bf16[4,8,32,128]{3,2,1,0:T(8,128)(2,1)S(1)}, bf16[4,8,32,128]{3,2,1,0:T(8,128)(2,1)S(1)}, u32[]{:S(2)}, u32[]{:S(2)}) collective-permute-start(bf16[4,8,32,128]{3,2,1,0:T(8,128)(2,1)S(1)} %edge_half1.5.second_ref.refs_2_), channel_id=1, source_target_pairs={{1,0},{2,1},{3,2},{0,3},{5,4},{6,5},{7,6},{4,7},{9,8},{10,9},{11,1... | collective-permute-start | bytes 786440 | tf_op jit(solution)/shard_map/ppermute | solution.py:196
  81.7 2.6 %collective-permute-start.29 = (bf16[1,8,32,128]{3,2,1,0:T(8,128)(2,1)S(1)}, bf16[1,8,32,128]{3,2,1,0:T(8,128)(2,1)S(1)}, u32[]{:S(2)}, u32[]{:S(2)}) collective-permute-start(bf16[1,8,32,128]{3,2,1,0:T(8,128)(2,1)S(1)} %get-tuple-element.89.refs_7_), channel_id=1, source_target_pairs={{4,0},{8,4},{12,8},{16,12},{20,16},{24,20},{28,24},{0,28},{5,1},{9... | collective-permute-start | bytes 196616 | tf_op jit(solution)/shard_map/ppermute | solution.py:196
  84.3 1.5 %inner_half0.6.refs_1_.refs_9_ = bf16[2,8,32,128]{3,2,1,0:T(8,128)(2,1)S(1)} custom-call(s32[8,12]{1,0:T(8,128)S(1)} %fusion.4.refs_0_, bf16[4,8,64,768]{3,2,1,0:T(8,128)(2,1)S(1)} %halves_of_rows.1.refs_1_, bf16[4,8,32,128]{3,2,1,0:T(8,128)(2,1)S(1)} %edge_half0.5.refs_2_.first_ref, bf16[4,8,32,128]{3,2,1,0:T(8,128)(2,1)S(1)} %collective-permute-done.18.refs_3_, ...), custom_call_target="tpu_custom_call" | custom-call | flops 20132659200 | bytes 157286400 | tf_op jit(solution)/shard_map/inner_half0/pallas_call | solution.py:171
  85.8 0.9 unpack.5
  86.7 1.5 %edge_half0.6.refs_2_.first_ref = bf16[4,8,32,128]{3,2,1,0:T(8,128)(2,1)S(1)} custom-call(s32[8,12]{1,0:T(8,128)S(1)} %fusion.4.refs_0_, bf16[4,8,64,768]{3,2,1,0:T(8,128)(2,1)S(1)} %halves_of_rows.1.refs_1_, bf16[4,8,32,128]{3,2,1,0:T(8,128)(2,1)S(1)} %edge_half0.5.refs_2_.first_ref, bf16[4,8,32,128]{3,2,1,0:T(8,128)(2,1)S(1)} %collective-permute-done.18.refs_3_, ...), custom_call_target="tpu_custom_call" | custom-call | flops 20132659200 | bytes 157286400 | tf_op jit(solution)/shard_map/edge_half0/pallas_call | solution.py:171
  88.8 1.8 %collective-permute-start.35 = (bf16[2,8,32,128]{3,2,1,0:T(8,128)(2,1)S(1)}, bf16[2,8,32,128]{3,2,1,0:T(8,128)(2,1)S(1)}, u32[]{:S(2)}, u32[]{:S(2)}) collective-permute-start(bf16[2,8,32,128]{3,2,1,0:T(8,128)(2,1)S(1)} %pad_maximum_fusion.11.refs_5_), channel_id=1, source_target_pairs={{4,0},{8,4},{12,8},{16,12},{20,16},{24,20},{28,24},{0,28},{5,1},{9... | collective-permute-start | bytes 393224 | tf_op jit(solution)/shard_map/ppermute | solution.py:196
  90.7 3.0 %collective-permute-start.30 = (bf16[4,8,32,128]{3,2,1,0:T(8,128)(2,1)S(1)}, bf16[4,8,32,128]{3,2,1,0:T(8,128)(2,1)S(1)}, u32[]{:S(2)}, u32[]{:S(2)}) collective-permute-start(bf16[4,8,32,128]{3,2,1,0:T(8,128)(2,1)S(1)} %edge_half0.6.refs_2_.first_ref), channel_id=1, source_target_pairs={{0,1},{1,2},{2,3},{3,0},{4,5},{5,6},{6,7},{7,4},{8,9},{9,10},{10,1... | collective-permute-start | bytes 786440 | tf_op jit(solution)/shard_map/ppermute | solution.py:196
  93.7 2.7 %collective-permute-start.31 = (bf16[4,8,32,128]{3,2,1,0:T(8,128)(2,1)S(1)}, bf16[4,8,32,128]{3,2,1,0:T(8,128)(2,1)S(1)}, u32[]{:S(2)}, u32[]{:S(2)}) collective-permute-start(bf16[4,8,32,128]{3,2,1,0:T(8,128)(2,1)S(1)} %edge_half0.6.refs_2_.first_ref), channel_id=1, source_target_pairs={{1,0},{2,1},{3,2},{0,3},{5,4},{6,5},{7,6},{4,7},{9,8},{10,9},{11,1... | collective-permute-start | bytes 786440 | tf_op jit(solution)/shard_map/ppermute | solution.py:196
  96.5 2.6 %collective-permute-start.37 = (bf16[1,8,32,128]{3,2,1,0:T(8,128)(2,1)S(1)}, bf16[1,8,32,128]{3,2,1,0:T(8,128)(2,1)S(1)}, u32[]{:S(2)}, u32[]{:S(2)}) collective-permute-start(bf16[1,8,32,128]{3,2,1,0:T(8,128)(2,1)S(1)} %get-tuple-element.83.refs_7_), channel_id=1, source_target_pairs={{4,0},{8,4},{12,8},{16,12},{20,16},{24,20},{28,24},{0,28},{5,1},{9... | collective-permute-start | bytes 196616 | tf_op jit(solution)/shard_map/ppermute | solution.py:196
  99.1 1.5 %inner_half1.6.refs_9_.refs_10_ = bf16[2,8,32,128]{3,2,1,0:T(8,128)(2,1)S(1)} custom-call(s32[8,12]{1,0:T(8,128)S(1)} %fusion.4.refs_0_, bf16[4,8,64,768]{3,2,1,0:T(8,128)(2,1)S(1)} %halves_of_rows.1.refs_1_, bf16[4,8,32,128]{3,2,1,0:T(8,128)(2,1)S(1)} %edge_half1.5.second_ref.refs_2_, bf16[4,8,32,128]{3,2,1,0:T(8,128)(2,1)S(1)} %collective-permute-done.32.refs_3_, ...), custom_call_target="tpu_custom_call" | custom-call | flops 20132659200 | bytes 157286400 | tf_op jit(solution)/shard_map/inner_half1/pallas_call | solution.py:171
  100.6 0.9 collective-permute-done.36.refs_7_
  101.5 1.5 %edge_half1.6.second_ref.refs_2_ = bf16[4,8,32,128]{3,2,1,0:T(8,128)(2,1)S(1)} custom-call(s32[8,12]{1,0:T(8,128)S(1)} %fusion.4.refs_0_, bf16[4,8,64,768]{3,2,1,0:T(8,128)(2,1)S(1)} %halves_of_rows.1.refs_1_, bf16[4,8,32,128]{3,2,1,0:T(8,128)(2,1)S(1)} %edge_half1.5.second_ref.refs_2_, bf16[4,8,32,128]{3,2,1,0:T(8,128)(2,1)S(1)} %collective-permute-done.32.refs_3_, ...), custom_call_target="tpu_custom_call" | custom-call | flops 20132659200 | bytes 157286400 | tf_op jit(solution)/shard_map/edge_half1/pallas_call | solution.py:171
  103.6 1.9 %collective-permute-start.39 = (bf16[2,8,32,128]{3,2,1,0:T(8,128)(2,1)S(1)}, bf16[2,8,32,128]{3,2,1,0:T(8,128)(2,1)S(1)}, u32[]{:S(2)}, u32[]{:S(2)}) collective-permute-start(bf16[2,8,32,128]{3,2,1,0:T(8,128)(2,1)S(1)} %pad_maximum_fusion.13.refs_5_), channel_id=1, source_target_pairs={{4,0},{8,4},{12,8},{16,12},{20,16},{24,20},{28,24},{0,28},{5,1},{9... | collective-permute-start | bytes 393224 | tf_op jit(solution)/shard_map/ppermute | solution.py:196
  105.5 3.0 %collective-permute-start.42 = (bf16[4,8,32,128]{3,2,1,0:T(8,128)(2,1)S(1)}, bf16[4,8,32,128]{3,2,1,0:T(8,128)(2,1)S(1)}, u32[]{:S(2)}, u32[]{:S(2)}) collective-permute-start(bf16[4,8,32,128]{3,2,1,0:T(8,128)(2,1)S(1)} %edge_half1.6.second_ref.refs_2_), channel_id=1, source_target_pairs={{0,1},{1,2},{2,3},{3,0},{4,5},{5,6},{6,7},{7,4},{8,9},{9,10},{10,1... | collective-permute-start | bytes 786440 | tf_op jit(solution)/shard_map/ppermute | solution.py:196
  108.5 2.7 %collective-permute-start.43 = (bf16[4,8,32,128]{3,2,1,0:T(8,128)(2,1)S(1)}, bf16[4,8,32,128]{3,2,1,0:T(8,128)(2,1)S(1)}, u32[]{:S(2)}, u32[]{:S(2)}) collective-permute-start(bf16[4,8,32,128]{3,2,1,0:T(8,128)(2,1)S(1)} %edge_half1.6.second_ref.refs_2_), channel_id=1, source_target_pairs={{1,0},{2,1},{3,2},{0,3},{5,4},{6,5},{7,6},{4,7},{9,8},{10,9},{11,1... | collective-permute-start | bytes 786440 | tf_op jit(solution)/shard_map/ppermute | solution.py:196
  111.3 2.6 %collective-permute-start.41 = (bf16[1,8,32,128]{3,2,1,0:T(8,128)(2,1)S(1)}, bf16[1,8,32,128]{3,2,1,0:T(8,128)(2,1)S(1)}, u32[]{:S(2)}, u32[]{:S(2)}) collective-permute-start(bf16[1,8,32,128]{3,2,1,0:T(8,128)(2,1)S(1)} %get-tuple-element.77.refs_7_), channel_id=1, source_target_pairs={{4,0},{8,4},{12,8},{16,12},{20,16},{24,20},{28,24},{0,28},{5,1},{9... | collective-permute-start | bytes 196616 | tf_op jit(solution)/shard_map/ppermute | solution.py:196
  113.9 1.5 %inner_half0.7.refs_1_.refs_9_ = bf16[2,8,32,128]{3,2,1,0:T(8,128)(2,1)S(1)} custom-call(s32[8,12]{1,0:T(8,128)S(1)} %fusion.4.refs_0_, bf16[4,8,64,768]{3,2,1,0:T(8,128)(2,1)S(1)} %halves_of_rows.1.refs_1_, bf16[4,8,32,128]{3,2,1,0:T(8,128)(2,1)S(1)} %edge_half0.6.refs_2_.first_ref, bf16[4,8,32,128]{3,2,1,0:T(8,128)(2,1)S(1)} %collective-permute-done.30.refs_3_, ...), custom_call_target="tpu_custom_call" | custom-call | flops 20132659200 | bytes 157286400 | tf_op jit(solution)/shard_map/inner_half0/pallas_call | solution.py:171
  115.4 0.9 unpack.6
  116.3 1.5 %edge_half0.7.first_ref = bf16[4,8,32,128]{3,2,1,0:T(8,128)(2,1)S(1)} custom-call(s32[8,12]{1,0:T(8,128)S(1)} %fusion.4.refs_0_, bf16[4,8,64,768]{3,2,1,0:T(8,128)(2,1)S(1)} %halves_of_rows.1.refs_1_, bf16[4,8,32,128]{3,2,1,0:T(8,128)(2,1)S(1)} %edge_half0.6.refs_2_.first_ref, bf16[4,8,32,128]{3,2,1,0:T(8,128)(2,1)S(1)} %collective-permute-done.30.refs_3_, ...), custom_call_target="tpu_custom_call" | custom-call | flops 20132659200 | bytes 157286400 | tf_op jit(solution)/shard_map/edge_half0/pallas_call | solution.py:171
  118.2 2.1 %collective-permute-start.45 = (bf16[2,8,32,128]{3,2,1,0:T(8,128)(2,1)S(1)}, bf16[2,8,32,128]{3,2,1,0:T(8,128)(2,1)S(1)}, u32[]{:S(2)}, u32[]{:S(2)}) collective-permute-start(bf16[2,8,32,128]{3,2,1,0:T(8,128)(2,1)S(1)} %pad_maximum_fusion.15.refs_5_), channel_id=1, source_target_pairs={{4,0},{8,4},{12,8},{16,12},{20,16},{24,20},{28,24},{0,28},{5,1},{9... | collective-permute-start | bytes 393224 | tf_op jit(solution)/shard_map/ppermute | solution.py:196
  120.4 2.4 %collective-permute-done.45.refs_6_ = bf16[2,8,32,128]{3,2,1,0:T(8,128)(2,1)S(1)} collective-permute-done((bf16[2,8,32,128]{3,2,1,0:T(8,128)(2,1)S(1)}, bf16[2,8,32,128]{3,2,1,0:T(8,128)(2,1)S(1)}, u32[]{:S(2)}, u32[]{:S(2)}) %collective-permute-start.45) | collective-permute-done | bytes 131104 | tf_op jit(solution)/shard_map/ppermute | solution.py:196
  122.8 2.8 %collective-permute-done.44.refs_5_ = bf16[2,8,32,128]{3,2,1,0:T(8,128)(2,1)S(1)} collective-permute-done((bf16[2,8,32,128]{3,2,1,0:T(8,128)(2,1)S(1)}, bf16[2,8,32,128]{3,2,1,0:T(8,128)(2,1)S(1)}, u32[]{:S(2)}, u32[]{:S(2)}) %collective-permute-start.44) | collective-permute-done | bytes 131104 | tf_op jit(solution)/shard_map/ppermute | solution.py:196
  125.7 2.6 %collective-permute-start.47 = (bf16[1,8,32,128]{3,2,1,0:T(8,128)(2,1)S(1)}, bf16[1,8,32,128]{3,2,1,0:T(8,128)(2,1)S(1)}, u32[]{:S(2)}, u32[]{:S(2)}) collective-permute-start(bf16[1,8,32,128]{3,2,1,0:T(8,128)(2,1)S(1)} %get-tuple-element.71.refs_7_), channel_id=1, source_target_pairs={{4,0},{8,4},{12,8},{16,12},{20,16},{24,20},{28,24},{0,28},{5,1},{9... | collective-permute-start | bytes 196616 | tf_op jit(solution)/shard_map/ppermute | solution.py:196
  128.3 1.5 %inner_half1.7.refs_9_.refs_10_ = bf16[2,8,32,128]{3,2,1,0:T(8,128)(2,1)S(1)} custom-call(s32[8,12]{1,0:T(8,128)S(1)} %fusion.4.refs_0_, bf16[4,8,64,768]{3,2,1,0:T(8,128)(2,1)S(1)} %halves_of_rows.1.refs_1_, bf16[4,8,32,128]{3,2,1,0:T(8,128)(2,1)S(1)} %edge_half1.6.second_ref.refs_2_, bf16[4,8,32,128]{3,2,1,0:T(8,128)(2,1)S(1)} %collective-permute-done.42.refs_3_, ...), custom_call_target="tpu_custom_call" | custom-call | flops 20132659200 | bytes 157286400 | tf_op jit(solution)/shard_map/inner_half1/pallas_call | solution.py:171
  130.3 1.5 %edge_half1.7.second_ref = bf16[4,8,32,128]{3,2,1,0:T(8,128)(2,1)S(1)} custom-call(s32[8,12]{1,0:T(8,128)S(1)} %fusion.4.refs_0_, bf16[4,8,64,768]{3,2,1,0:T(8,128)(2,1)S(1)} %halves_of_rows.1.refs_1_, bf16[4,8,32,128]{3,2,1,0:T(8,128)(2,1)S(1)} %edge_half1.6.second_ref.refs_2_, bf16[4,8,32,128]{3,2,1,0:T(8,128)(2,1)S(1)} %collective-permute-done.42.refs_3_, ...), custom_call_target="tpu_custom_call" | custom-call | flops 20132659200 | bytes 157286400 | tf_op jit(solution)/shard_map/edge_half1/pallas_call | solution.py:171
  131.8 1.5 %unpack.7 = (bf16[4,4,8,64,128]{4,3,2,1,0:T(8,128)(2,1)}, f32[8,128]{1,0:T(8,128)}) custom-call(bf16[4,8,32,128]{3,2,1,0:T(8,128)(2,1)S(1)} %edge_half0.7.first_ref, bf16[4,8,32,128]{3,2,1,0:T(8,128)(2,1)S(1)} %edge_half1.7.second_ref, bf16[4,4,8,64,128]{4,3,2,1,0:T(8,128)(2,1)} %get-tuple-element.69.refs_0_), custom_call_target="tpu_custom_call", output_to_operand_aliasing={{0}: (2, {})} | custom-call | tf_op jit(solution)/shard_map/unpack/pallas_call | solution.py:77
  (100 shorter events, 4.5 us)
Async XLA Ops:
  0.0 1.0 copy-start.1
  1.2 13.6 %collective-permute-start = (bf16[4,8,32,128]{3,2,1,0:T(8,128)(2,1)S(1)}, bf16[4,8,32,128]{3,2,1,0:T(8,128)(2,1)S(1)}, u32[]{:S(2)}, u32[]{:S(2)}) collective-permute-start(bf16[4,8,32,128]{3,2,1,0:T(8,128)(2,1)S(1)} %get-tuple-element.40.refs_2_), channel_id=1, source_target_pairs={{0,1},{1,2},{2,3},{3,0},{4,5},{5,6},{6,7},{7,4},{8,9},{9,10},{10,1... | collective-permute-start | bytes 786440 | tf_op jit(solution)/shard_map/ppermute | solution.py:196
  4.3 15.0 %collective-permute-start.1 = (bf16[4,8,32,128]{3,2,1,0:T(8,128)(2,1)S(1)}, bf16[4,8,32,128]{3,2,1,0:T(8,128)(2,1)S(1)}, u32[]{:S(2)}, u32[]{:S(2)}) collective-permute-start(bf16[4,8,32,128]{3,2,1,0:T(8,128)(2,1)S(1)} %get-tuple-element.40.refs_2_), channel_id=1, source_target_pairs={{1,0},{2,1},{3,2},{0,3},{5,4},{6,5},{7,6},{4,7},{9,8},{10,9},{11,1... | collective-permute-start | bytes 786440 | tf_op jit(solution)/shard_map/ppermute | solution.py:196
  6.4 22.3 %collective-permute-start.8 = (bf16[4,8,32,128]{3,2,1,0:T(8,128)(2,1)S(1)}, bf16[4,8,32,128]{3,2,1,0:T(8,128)(2,1)S(1)}, u32[]{:S(2)}, u32[]{:S(2)}) collective-permute-start(bf16[4,8,32,128]{3,2,1,0:T(8,128)(2,1)S(1)} %get-tuple-element.44.refs_2_), channel_id=1, source_target_pairs={{0,1},{1,2},{2,3},{3,0},{4,5},{5,6},{6,7},{7,4},{8,9},{9,10},{10,1... | collective-permute-start | bytes 786440 | tf_op jit(solution)/shard_map/ppermute | solution.py:196
  6.4 30.7 %collective-permute-start.9 = (bf16[4,8,32,128]{3,2,1,0:T(8,128)(2,1)S(1)}, bf16[4,8,32,128]{3,2,1,0:T(8,128)(2,1)S(1)}, u32[]{:S(2)}, u32[]{:S(2)}) collective-permute-start(bf16[4,8,32,128]{3,2,1,0:T(8,128)(2,1)S(1)} %get-tuple-element.44.refs_2_), channel_id=1, source_target_pairs={{1,0},{2,1},{3,2},{0,3},{5,4},{6,5},{7,6},{4,7},{9,8},{10,9},{11,1... | collective-permute-start | bytes 786440 | tf_op jit(solution)/shard_map/ppermute | solution.py:196
  10.2 1.9 %copy-start = (bf16[4,1,8,64,768]{4,3,2,1,0:T(8,128)(2,1)S(1)}, bf16[4,1,8,64,768]{4,3,2,1,0:T(8,128)(2,1)}, u32[]{:S(2)}) copy-start(bf16[4,1,8,64,768]{4,3,2,1,0:T(8,128)(2,1)} %param.4) | copy-start | bytes 9437188
  12.1 4.0 %copy-start.2 = (s32[1,8,12]{2,1,0:T(8,128)S(1)}, s32[1,8,12]{2,1,0:T(8,128)}, u32[]{:S(2)}) copy-start(s32[1,8,12]{2,1,0:T(8,128)} %param.5) | copy-start | bytes 1156
  14.9 4.9 %collective-permute-start.3 = (bf16[2,8,32,128]{3,2,1,0:T(8,128)(2,1)S(1)}, bf16[2,8,32,128]{3,2,1,0:T(8,128)(2,1)S(1)}, u32[]{:S(2)}, u32[]{:S(2)}) collective-permute-start(bf16[2,8,32,128]{3,2,1,0:T(8,128)(2,1)S(1)} %pad_maximum_fusion.1.refs_5_), channel_id=1, source_target_pairs={{4,0},{8,4},{12,8},{16,12},{20,16},{24,20},{28,24},{0,28},{5,1},{9... | collective-permute-start | bytes 393224 | tf_op jit(solution)/shard_map/ppermute | solution.py:196
  16.0 5.9 %collective-permute-start.2 = (bf16[2,8,32,128]{3,2,1,0:T(8,128)(2,1)S(1)}, bf16[2,8,32,128]{3,2,1,0:T(8,128)(2,1)S(1)}, u32[]{:S(2)}, u32[]{:S(2)}) collective-permute-start(bf16[2,8,32,128]{3,2,1,0:T(8,128)(2,1)S(1)} %pad_maximum_fusion.refs_6_), channel_id=1, source_target_pairs={{0,4},{4,8},{8,12},{12,16},{16,20},{20,24},{24,28},{28,0},{1,5},{5... | collective-permute-start | bytes 393224 | tf_op jit(solution)/shard_map/ppermute | solution.py:196
  21.9 5.3 %collective-permute-start.4 = (bf16[1,8,32,128]{3,2,1,0:T(8,128)(2,1)S(1)}, bf16[1,8,32,128]{3,2,1,0:T(8,128)(2,1)S(1)}, u32[]{:S(2)}, u32[]{:S(2)}) collective-permute-start(bf16[1,8,32,128]{3,2,1,0:T(8,128)(2,1)S(1)} %get-tuple-element.114.refs_8_), channel_id=1, source_target_pairs={{0,4},{4,8},{8,12},{12,16},{16,20},{20,24},{24,28},{28,0},{1,5},{5... | collective-permute-start | bytes 196616 | tf_op jit(solution)/shard_map/ppermute | solution.py:196
  22.0 5.2 %collective-permute-start.5 = (bf16[1,8,32,128]{3,2,1,0:T(8,128)(2,1)S(1)}, bf16[1,8,32,128]{3,2,1,0:T(8,128)(2,1)S(1)}, u32[]{:S(2)}, u32[]{:S(2)}) collective-permute-start(bf16[1,8,32,128]{3,2,1,0:T(8,128)(2,1)S(1)} %get-tuple-element.113.refs_7_), channel_id=1, source_target_pairs={{4,0},{8,4},{12,8},{16,12},{20,16},{24,20},{28,24},{0,28},{5,1},{9... | collective-permute-start | bytes 196616 | tf_op jit(solution)/shard_map/ppermute | solution.py:196
  28.7 8.4 %collective-permute-start.11 = (bf16[2,8,32,128]{3,2,1,0:T(8,128)(2,1)S(1)}, bf16[2,8,32,128]{3,2,1,0:T(8,128)(2,1)S(1)}, u32[]{:S(2)}, u32[]{:S(2)}) collective-permute-start(bf16[2,8,32,128]{3,2,1,0:T(8,128)(2,1)S(1)} %pad_maximum_fusion.3.refs_5_), channel_id=1, source_target_pairs={{4,0},{8,4},{12,8},{16,12},{20,16},{24,20},{28,24},{0,28},{5,1},{9... | collective-permute-start | bytes 393224 | tf_op jit(solution)/shard_map/ppermute | solution.py:196
  30.8 6.3 %collective-permute-start.10 = (bf16[2,8,32,128]{3,2,1,0:T(8,128)(2,1)S(1)}, bf16[2,8,32,128]{3,2,1,0:T(8,128)(2,1)S(1)}, u32[]{:S(2)}, u32[]{:S(2)}) collective-permute-start(bf16[2,8,32,128]{3,2,1,0:T(8,128)(2,1)S(1)} %pad_maximum_fusion.2.refs_6_), channel_id=1, source_target_pairs={{0,4},{4,8},{8,12},{12,16},{16,20},{20,24},{24,28},{28,0},{1,5},{5... | collective-permute-start | bytes 393224 | tf_op jit(solution)/shard_map/ppermute | solution.py:196
  30.9 13.4 %collective-permute-start.6 = (bf16[4,8,32,128]{3,2,1,0:T(8,128)(2,1)S(1)}, bf16[4,8,32,128]{3,2,1,0:T(8,128)(2,1)S(1)}, u32[]{:S(2)}, u32[]{:S(2)}) collective-permute-start(bf16[4,8,32,128]{3,2,1,0:T(8,128)(2,1)S(1)} %edge_half0.4.refs_2_.first_ref), channel_id=1, source_target_pairs={{0,1},{1,2},{2,3},{3,0},{4,5},{5,6},{6,7},{7,4},{8,9},{9,10},{10,1... | collective-permute-start | bytes 786440 | tf_op jit(solution)/shard_map/ppermute | solution.py:196
  33.7 18.3 %collective-permute-start.7 = (bf16[4,8,32,128]{3,2,1,0:T(8,128)(2,1)S(1)}, bf16[4,8,32,128]{3,2,1,0:T(8,128)(2,1)S(1)}, u32[]{:S(2)}, u32[]{:S(2)}) collective-permute-start(bf16[4,8,32,128]{3,2,1,0:T(8,128)(2,1)S(1)} %edge_half0.4.refs_2_.first_ref), channel_id=1, source_target_pairs={{1,0},{2,1},{3,2},{0,3},{5,4},{6,5},{7,6},{4,7},{9,8},{10,9},{11,1... | collective-permute-start | bytes 786440 | tf_op jit(solution)/shard_map/ppermute | solution.py:196
  37.1 5.1 %collective-permute-start.12 = (bf16[1,8,32,128]{3,2,1,0:T(8,128)(2,1)S(1)}, bf16[1,8,32,128]{3,2,1,0:T(8,128)(2,1)S(1)}, u32[]{:S(2)}, u32[]{:S(2)}) collective-permute-start(bf16[1,8,32,128]{3,2,1,0:T(8,128)(2,1)S(1)} %get-tuple-element.108.refs_8_), channel_id=1, source_target_pairs={{0,4},{4,8},{8,12},{12,16},{16,20},{20,24},{24,28},{28,0},{1,5},{5... | collective-permute-start | bytes 196616 | tf_op jit(solution)/shard_map/ppermute | solution.py:196
  37.2 5.0 %collective-permute-start.13 = (bf16[1,8,32,128]{3,2,1,0:T(8,128)(2,1)S(1)}, bf16[1,8,32,128]{3,2,1,0:T(8,128)(2,1)S(1)}, u32[]{:S(2)}, u32[]{:S(2)}) collective-permute-start(bf16[1,8,32,128]{3,2,1,0:T(8,128)(2,1)S(1)} %get-tuple-element.107.refs_7_), channel_id=1, source_target_pairs={{4,0},{8,4},{12,8},{16,12},{20,16},{24,20},{28,24},{0,28},{5,1},{9... | collective-permute-start | bytes 196616 | tf_op jit(solution)/shard_map/ppermute | solution.py:196
  44.4 7.6 %collective-permute-start.15 = (bf16[2,8,32,128]{3,2,1,0:T(8,128)(2,1)S(1)}, bf16[2,8,32,128]{3,2,1,0:T(8,128)(2,1)S(1)}, u32[]{:S(2)}, u32[]{:S(2)}) collective-permute-start(bf16[2,8,32,128]{3,2,1,0:T(8,128)(2,1)S(1)} %pad_maximum_fusion.5.refs_5_), channel_id=1, source_target_pairs={{4,0},{8,4},{12,8},{16,12},{20,16},{24,20},{28,24},{0,28},{5,1},{9... | collective-permute-start | bytes 393224 | tf_op jit(solution)/shard_map/ppermute | solution.py:196
  46.2 5.7 %collective-permute-start.14 = (bf16[2,8,32,128]{3,2,1,0:T(8,128)(2,1)S(1)}, bf16[2,8,32,128]{3,2,1,0:T(8,128)(2,1)S(1)}, u32[]{:S(2)}, u32[]{:S(2)}) collective-permute-start(bf16[2,8,32,128]{3,2,1,0:T(8,128)(2,1)S(1)} %pad_maximum_fusion.4.refs_6_), channel_id=1, source_target_pairs={{0,4},{4,8},{8,12},{12,16},{16,20},{20,24},{24,28},{28,0},{1,5},{5... | collective-permute-start | bytes 393224 | tf_op jit(solution)/shard_map/ppermute | solution.py:196
  46.3 12.9 %collective-permute-start.20 = (bf16[4,8,32,128]{3,2,1,0:T(8,128)(2,1)S(1)}, bf16[4,8,32,128]{3,2,1,0:T(8,128)(2,1)S(1)}, u32[]{:S(2)}, u32[]{:S(2)}) collective-permute-start(bf16[4,8,32,128]{3,2,1,0:T(8,128)(2,1)S(1)} %edge_half1.4.second_ref.refs_2_), channel_id=1, source_target_pairs={{0,1},{1,2},{2,3},{3,0},{4,5},{5,6},{6,7},{7,4},{8,9},{9,10},{10,1... | collective-permute-start | bytes 786440 | tf_op jit(solution)/shard_map/ppermute | solution.py:196
  49.2 17.5 %collective-permute-start.21 = (bf16[4,8,32,128]{3,2,1,0:T(8,128)(2,1)S(1)}, bf16[4,8,32,128]{3,2,1,0:T(8,128)(2,1)S(1)}, u32[]{:S(2)}, u32[]{:S(2)}) collective-permute-start(bf16[4,8,32,128]{3,2,1,0:T(8,128)(2,1)S(1)} %edge_half1.4.second_ref.refs_2_), channel_id=1, source_target_pairs={{1,0},{2,1},{3,2},{0,3},{5,4},{6,5},{7,6},{4,7},{9,8},{10,9},{11,1... | collective-permute-start | bytes 786440 | tf_op jit(solution)/shard_map/ppermute | solution.py:196
  52.0 5.1 %collective-permute-start.16 = (bf16[1,8,32,128]{3,2,1,0:T(8,128)(2,1)S(1)}, bf16[1,8,32,128]{3,2,1,0:T(8,128)(2,1)S(1)}, u32[]{:S(2)}, u32[]{:S(2)}) collective-permute-start(bf16[1,8,32,128]{3,2,1,0:T(8,128)(2,1)S(1)} %get-tuple-element.102.refs_8_), channel_id=1, source_target_pairs={{0,4},{4,8},{8,12},{12,16},{16,20},{20,24},{24,28},{28,0},{1,5},{5... | collective-permute-start | bytes 196616 | tf_op jit(solution)/shard_map/ppermute | solution.py:196
  52.0 5.0 %collective-permute-start.17 = (bf16[1,8,32,128]{3,2,1,0:T(8,128)(2,1)S(1)}, bf16[1,8,32,128]{3,2,1,0:T(8,128)(2,1)S(1)}, u32[]{:S(2)}, u32[]{:S(2)}) collective-permute-start(bf16[1,8,32,128]{3,2,1,0:T(8,128)(2,1)S(1)} %get-tuple-element.101.refs_7_), channel_id=1, source_target_pairs={{4,0},{8,4},{12,8},{16,12},{20,16},{24,20},{28,24},{0,28},{5,1},{9... | collective-permute-start | bytes 196616 | tf_op jit(solution)/shard_map/ppermute | solution.py:196
  59.2 7.6 %collective-permute-start.23 = (bf16[2,8,32,128]{3,2,1,0:T(8,128)(2,1)S(1)}, bf16[2,8,32,128]{3,2,1,0:T(8,128)(2,1)S(1)}, u32[]{:S(2)}, u32[]{:S(2)}) collective-permute-start(bf16[2,8,32,128]{3,2,1,0:T(8,128)(2,1)S(1)} %pad_maximum_fusion.7.refs_5_), channel_id=1, source_target_pairs={{4,0},{8,4},{12,8},{16,12},{20,16},{24,20},{28,24},{0,28},{5,1},{9... | collective-permute-start | bytes 393224 | tf_op jit(solution)/shard_map/ppermute | solution.py:196
  61.0 5.7 %collective-permute-start.22 = (bf16[2,8,32,128]{3,2,1,0:T(8,128)(2,1)S(1)}, bf16[2,8,32,128]{3,2,1,0:T(8,128)(2,1)S(1)}, u32[]{:S(2)}, u32[]{:S(2)}) collective-permute-start(bf16[2,8,32,128]{3,2,1,0:T(8,128)(2,1)S(1)} %pad_maximum_fusion.6.refs_6_), channel_id=1, source_target_pairs={{0,4},{4,8},{8,12},{12,16},{16,20},{20,24},{24,28},{28,0},{1,5},{5... | collective-permute-start | bytes 393224 | tf_op jit(solution)/shard_map/ppermute | solution.py:196
  61.1 12.8 %collective-permute-start.18 = (bf16[4,8,32,128]{3,2,1,0:T(8,128)(2,1)S(1)}, bf16[4,8,32,128]{3,2,1,0:T(8,128)(2,1)S(1)}, u32[]{:S(2)}, u32[]{:S(2)}) collective-permute-start(bf16[4,8,32,128]{3,2,1,0:T(8,128)(2,1)S(1)} %edge_half0.5.refs_2_.first_ref), channel_id=1, source_target_pairs={{0,1},{1,2},{2,3},{3,0},{4,5},{5,6},{6,7},{7,4},{8,9},{9,10},{10,1... | collective-permute-start | bytes 786440 | tf_op jit(solution)/shard_map/ppermute | solution.py:196
  64.0 17.5 %collective-permute-start.19 = (bf16[4,8,32,128]{3,2,1,0:T(8,128)(2,1)S(1)}, bf16[4,8,32,128]{3,2,1,0:T(8,128)(2,1)S(1)}, u32[]{:S(2)}, u32[]{:S(2)}) collective-permute-start(bf16[4,8,32,128]{3,2,1,0:T(8,128)(2,1)S(1)} %edge_half0.5.refs_2_.first_ref), channel_id=1, source_target_pairs={{1,0},{2,1},{3,2},{0,3},{5,4},{6,5},{7,6},{4,7},{9,8},{10,9},{11,1... | collective-permute-start | bytes 786440 | tf_op jit(solution)/shard_map/ppermute | solution.py:196
  66.8 5.1 %collective-permute-start.24 = (bf16[1,8,32,128]{3,2,1,0:T(8,128)(2,1)S(1)}, bf16[1,8,32,128]{3,2,1,0:T(8,128)(2,1)S(1)}, u32[]{:S(2)}, u32[]{:S(2)}) collective-permute-start(bf16[1,8,32,128]{3,2,1,0:T(8,128)(2,1)S(1)} %get-tuple-element.96.refs_8_), channel_id=1, source_target_pairs={{0,4},{4,8},{8,12},{12,16},{16,20},{20,24},{24,28},{28,0},{1,5},{5... | collective-permute-start | bytes 196616 | tf_op jit(solution)/shard_map/ppermute | solution.py:196
  66.8 5.0 %collective-permute-start.25 = (bf16[1,8,32,128]{3,2,1,0:T(8,128)(2,1)S(1)}, bf16[1,8,32,128]{3,2,1,0:T(8,128)(2,1)S(1)}, u32[]{:S(2)}, u32[]{:S(2)}) collective-permute-start(bf16[1,8,32,128]{3,2,1,0:T(8,128)(2,1)S(1)} %get-tuple-element.95.refs_7_), channel_id=1, source_target_pairs={{4,0},{8,4},{12,8},{16,12},{20,16},{24,20},{28,24},{0,28},{5,1},{9... | collective-permute-start | bytes 196616 | tf_op jit(solution)/shard_map/ppermute | solution.py:196
  74.0 7.6 %collective-permute-start.27 = (bf16[2,8,32,128]{3,2,1,0:T(8,128)(2,1)S(1)}, bf16[2,8,32,128]{3,2,1,0:T(8,128)(2,1)S(1)}, u32[]{:S(2)}, u32[]{:S(2)}) collective-permute-start(bf16[2,8,32,128]{3,2,1,0:T(8,128)(2,1)S(1)} %pad_maximum_fusion.9.refs_5_), channel_id=1, source_target_pairs={{4,0},{8,4},{12,8},{16,12},{20,16},{24,20},{28,24},{0,28},{5,1},{9... | collective-permute-start | bytes 393224 | tf_op jit(solution)/shard_map/ppermute | solution.py:196
  75.8 5.7 %collective-permute-start.26 = (bf16[2,8,32,128]{3,2,1,0:T(8,128)(2,1)S(1)}, bf16[2,8,32,128]{3,2,1,0:T(8,128)(2,1)S(1)}, u32[]{:S(2)}, u32[]{:S(2)}) collective-permute-start(bf16[2,8,32,128]{3,2,1,0:T(8,128)(2,1)S(1)} %pad_maximum_fusion.8.refs_6_), channel_id=1, source_target_pairs={{0,4},{4,8},{8,12},{12,16},{16,20},{20,24},{24,28},{28,0},{1,5},{5... | collective-permute-start | bytes 393224 | tf_op jit(solution)/shard_map/ppermute | solution.py:196
  75.9 12.8 %collective-permute-start.32 = (bf16[4,8,32,128]{3,2,1,0:T(8,128)(2,1)S(1)}, bf16[4,8,32,128]{3,2,1,0:T(8,128)(2,1)S(1)}, u32[]{:S(2)}, u32[]{:S(2)}) collective-permute-start(bf16[4,8,32,128]{3,2,1,0:T(8,128)(2,1)S(1)} %edge_half1.5.second_ref.refs_2_), channel_id=1, source_target_pairs={{0,1},{1,2},{2,3},{3,0},{4,5},{5,6},{6,7},{7,4},{8,9},{9,10},{10,1... | collective-permute-start | bytes 786440 | tf_op jit(solution)/shard_map/ppermute | solution.py:196
  78.9 17.5 %collective-permute-start.33 = (bf16[4,8,32,128]{3,2,1,0:T(8,128)(2,1)S(1)}, bf16[4,8,32,128]{3,2,1,0:T(8,128)(2,1)S(1)}, u32[]{:S(2)}, u32[]{:S(2)}) collective-permute-start(bf16[4,8,32,128]{3,2,1,0:T(8,128)(2,1)S(1)} %edge_half1.5.second_ref.refs_2_), channel_id=1, source_target_pairs={{1,0},{2,1},{3,2},{0,3},{5,4},{6,5},{7,6},{4,7},{9,8},{10,9},{11,1... | collective-permute-start | bytes 786440 | tf_op jit(solution)/shard_map/ppermute | solution.py:196
  81.6 5.1 %collective-permute-start.28 = (bf16[1,8,32,128]{3,2,1,0:T(8,128)(2,1)S(1)}, bf16[1,8,32,128]{3,2,1,0:T(8,128)(2,1)S(1)}, u32[]{:S(2)}, u32[]{:S(2)}) collective-permute-start(bf16[1,8,32,128]{3,2,1,0:T(8,128)(2,1)S(1)} %get-tuple-element.90.refs_8_), channel_id=1, source_target_pairs={{0,4},{4,8},{8,12},{12,16},{16,20},{20,24},{24,28},{28,0},{1,5},{5... | collective-permute-start | bytes 196616 | tf_op jit(solution)/shard_map/ppermute | solution.py:196
  81.7 5.0 %collective-permute-start.29 = (bf16[1,8,32,128]{3,2,1,0:T(8,128)(2,1)S(1)}, bf16[1,8,32,128]{3,2,1,0:T(8,128)(2,1)S(1)}, u32[]{:S(2)}, u32[]{:S(2)}) collective-permute-start(bf16[1,8,32,128]{3,2,1,0:T(8,128)(2,1)S(1)} %get-tuple-element.89.refs_7_), channel_id=1, source_target_pairs={{4,0},{8,4},{12,8},{16,12},{20,16},{24,20},{28,24},{0,28},{5,1},{9... | collective-permute-start | bytes 196616 | tf_op jit(solution)/shard_map/ppermute | solution.py:196
  88.8 7.6 %collective-permute-start.35 = (bf16[2,8,32,128]{3,2,1,0:T(8,128)(2,1)S(1)}, bf16[2,8,32,128]{3,2,1,0:T(8,128)(2,1)S(1)}, u32[]{:S(2)}, u32[]{:S(2)}) collective-permute-start(bf16[2,8,32,128]{3,2,1,0:T(8,128)(2,1)S(1)} %pad_maximum_fusion.11.refs_5_), channel_id=1, source_target_pairs={{4,0},{8,4},{12,8},{16,12},{20,16},{24,20},{28,24},{0,28},{5,1},{9... | collective-permute-start | bytes 393224 | tf_op jit(solution)/shard_map/ppermute | solution.py:196
  90.6 5.7 %collective-permute-start.34 = (bf16[2,8,32,128]{3,2,1,0:T(8,128)(2,1)S(1)}, bf16[2,8,32,128]{3,2,1,0:T(8,128)(2,1)S(1)}, u32[]{:S(2)}, u32[]{:S(2)}) collective-permute-start(bf16[2,8,32,128]{3,2,1,0:T(8,128)(2,1)S(1)} %pad_maximum_fusion.10.refs_6_), channel_id=1, source_target_pairs={{0,4},{4,8},{8,12},{12,16},{16,20},{20,24},{24,28},{28,0},{1,5},{5... | collective-permute-start | bytes 393224 | tf_op jit(solution)/shard_map/ppermute | solution.py:196
  90.7 12.8 %collective-permute-start.30 = (bf16[4,8,32,128]{3,2,1,0:T(8,128)(2,1)S(1)}, bf16[4,8,32,128]{3,2,1,0:T(8,128)(2,1)S(1)}, u32[]{:S(2)}, u32[]{:S(2)}) collective-permute-start(bf16[4,8,32,128]{3,2,1,0:T(8,128)(2,1)S(1)} %edge_half0.6.refs_2_.first_ref), channel_id=1, source_target_pairs={{0,1},{1,2},{2,3},{3,0},{4,5},{5,6},{6,7},{7,4},{8,9},{9,10},{10,1... | collective-permute-start | bytes 786440 | tf_op jit(solution)/shard_map/ppermute | solution.py:196
  93.7 17.5 %collective-permute-start.31 = (bf16[4,8,32,128]{3,2,1,0:T(8,128)(2,1)S(1)}, bf16[4,8,32,128]{3,2,1,0:T(8,128)(2,1)S(1)}, u32[]{:S(2)}, u32[]{:S(2)}) collective-permute-start(bf16[4,8,32,128]{3,2,1,0:T(8,128)(2,1)S(1)} %edge_half0.6.refs_2_.first_ref), channel_id=1, source_target_pairs={{1,0},{2,1},{3,2},{0,3},{5,4},{6,5},{7,6},{4,7},{9,8},{10,9},{11,1... | collective-permute-start | bytes 786440 | tf_op jit(solution)/shard_map/ppermute | solution.py:196
  96.4 5.1 %collective-permute-start.36 = (bf16[1,8,32,128]{3,2,1,0:T(8,128)(2,1)S(1)}, bf16[1,8,32,128]{3,2,1,0:T(8,128)(2,1)S(1)}, u32[]{:S(2)}, u32[]{:S(2)}) collective-permute-start(bf16[1,8,32,128]{3,2,1,0:T(8,128)(2,1)S(1)} %get-tuple-element.84.refs_8_), channel_id=1, source_target_pairs={{0,4},{4,8},{8,12},{12,16},{16,20},{20,24},{24,28},{28,0},{1,5},{5... | collective-permute-start | bytes 196616 | tf_op jit(solution)/shard_map/ppermute | solution.py:196
  96.5 5.0 %collective-permute-start.37 = (bf16[1,8,32,128]{3,2,1,0:T(8,128)(2,1)S(1)}, bf16[1,8,32,128]{3,2,1,0:T(8,128)(2,1)S(1)}, u32[]{:S(2)}, u32[]{:S(2)}) collective-permute-start(bf16[1,8,32,128]{3,2,1,0:T(8,128)(2,1)S(1)} %get-tuple-element.83.refs_7_), channel_id=1, source_target_pairs={{4,0},{8,4},{12,8},{16,12},{20,16},{24,20},{28,24},{0,28},{5,1},{9... | collective-permute-start | bytes 196616 | tf_op jit(solution)/shard_map/ppermute | solution.py:196
  103.6 7.7 %collective-permute-start.39 = (bf16[2,8,32,128]{3,2,1,0:T(8,128)(2,1)S(1)}, bf16[2,8,32,128]{3,2,1,0:T(8,128)(2,1)S(1)}, u32[]{:S(2)}, u32[]{:S(2)}) collective-permute-start(bf16[2,8,32,128]{3,2,1,0:T(8,128)(2,1)S(1)} %pad_maximum_fusion.13.refs_5_), channel_id=1, source_target_pairs={{4,0},{8,4},{12,8},{16,12},{20,16},{24,20},{28,24},{0,28},{5,1},{9... | collective-permute-start | bytes 393224 | tf_op jit(solution)/shard_map/ppermute | solution.py:196
  105.5 5.7 %collective-permute-start.38 = (bf16[2,8,32,128]{3,2,1,0:T(8,128)(2,1)S(1)}, bf16[2,8,32,128]{3,2,1,0:T(8,128)(2,1)S(1)}, u32[]{:S(2)}, u32[]{:S(2)}) collective-permute-start(bf16[2,8,32,128]{3,2,1,0:T(8,128)(2,1)S(1)} %pad_maximum_fusion.12.refs_6_), channel_id=1, source_target_pairs={{0,4},{4,8},{8,12},{12,16},{16,20},{20,24},{24,28},{28,0},{1,5},{5... | collective-permute-start | bytes 393224 | tf_op jit(solution)/shard_map/ppermute | solution.py:196
  105.5 12.6 %collective-permute-start.42 = (bf16[4,8,32,128]{3,2,1,0:T(8,128)(2,1)S(1)}, bf16[4,8,32,128]{3,2,1,0:T(8,128)(2,1)S(1)}, u32[]{:S(2)}, u32[]{:S(2)}) collective-permute-start(bf16[4,8,32,128]{3,2,1,0:T(8,128)(2,1)S(1)} %edge_half1.6.second_ref.refs_2_), channel_id=1, source_target_pairs={{0,1},{1,2},{2,3},{3,0},{4,5},{5,6},{6,7},{7,4},{8,9},{9,10},{10,1... | collective-permute-start | bytes 786440 | tf_op jit(solution)/shard_map/ppermute | solution.py:196
  108.5 11.8 %collective-permute-start.43 = (bf16[4,8,32,128]{3,2,1,0:T(8,128)(2,1)S(1)}, bf16[4,8,32,128]{3,2,1,0:T(8,128)(2,1)S(1)}, u32[]{:S(2)}, u32[]{:S(2)}) collective-permute-start(bf16[4,8,32,128]{3,2,1,0:T(8,128)(2,1)S(1)} %edge_half1.6.second_ref.refs_2_), channel_id=1, source_target_pairs={{1,0},{2,1},{3,2},{0,3},{5,4},{6,5},{7,6},{4,7},{9,8},{10,9},{11,1... | collective-permute-start | bytes 786440 | tf_op jit(solution)/shard_map/ppermute | solution.py:196
  111.2 5.1 %collective-permute-start.40 = (bf16[1,8,32,128]{3,2,1,0:T(8,128)(2,1)S(1)}, bf16[1,8,32,128]{3,2,1,0:T(8,128)(2,1)S(1)}, u32[]{:S(2)}, u32[]{:S(2)}) collective-permute-start(bf16[1,8,32,128]{3,2,1,0:T(8,128)(2,1)S(1)} %get-tuple-element.78.refs_8_), channel_id=1, source_target_pairs={{0,4},{4,8},{8,12},{12,16},{16,20},{20,24},{24,28},{28,0},{1,5},{5... | collective-permute-start | bytes 196616 | tf_op jit(solution)/shard_map/ppermute | solution.py:196
  111.3 5.0 %collective-permute-start.41 = (bf16[1,8,32,128]{3,2,1,0:T(8,128)(2,1)S(1)}, bf16[1,8,32,128]{3,2,1,0:T(8,128)(2,1)S(1)}, u32[]{:S(2)}, u32[]{:S(2)}) collective-permute-start(bf16[1,8,32,128]{3,2,1,0:T(8,128)(2,1)S(1)} %get-tuple-element.77.refs_7_), channel_id=1, source_target_pairs={{4,0},{8,4},{12,8},{16,12},{20,16},{24,20},{28,24},{0,28},{5,1},{9... | collective-permute-start | bytes 196616 | tf_op jit(solution)/shard_map/ppermute | solution.py:196
  118.2 4.6 %collective-permute-start.45 = (bf16[2,8,32,128]{3,2,1,0:T(8,128)(2,1)S(1)}, bf16[2,8,32,128]{3,2,1,0:T(8,128)(2,1)S(1)}, u32[]{:S(2)}, u32[]{:S(2)}) collective-permute-start(bf16[2,8,32,128]{3,2,1,0:T(8,128)(2,1)S(1)} %pad_maximum_fusion.15.refs_5_), channel_id=1, source_target_pairs={{4,0},{8,4},{12,8},{16,12},{20,16},{24,20},{28,24},{0,28},{5,1},{9... | collective-permute-start | bytes 393224 | tf_op jit(solution)/shard_map/ppermute | solution.py:196
  120.3 5.3 %collective-permute-start.44 = (bf16[2,8,32,128]{3,2,1,0:T(8,128)(2,1)S(1)}, bf16[2,8,32,128]{3,2,1,0:T(8,128)(2,1)S(1)}, u32[]{:S(2)}, u32[]{:S(2)}) collective-permute-start(bf16[2,8,32,128]{3,2,1,0:T(8,128)(2,1)S(1)} %pad_maximum_fusion.14.refs_6_), channel_id=1, source_target_pairs={{0,4},{4,8},{8,12},{12,16},{16,20},{20,24},{24,28},{28,0},{1,5},{5... | collective-permute-start | bytes 393224 | tf_op jit(solution)/shard_map/ppermute | solution.py:196
  125.6 4.6 %collective-permute-start.46 = (bf16[1,8,32,128]{3,2,1,0:T(8,128)(2,1)S(1)}, bf16[1,8,32,128]{3,2,1,0:T(8,128)(2,1)S(1)}, u32[]{:S(2)}, u32[]{:S(2)}) collective-permute-start(bf16[1,8,32,128]{3,2,1,0:T(8,128)(2,1)S(1)} %get-tuple-element.72.refs_8_), channel_id=1, source_target_pairs={{0,4},{4,8},{8,12},{12,16},{16,20},{20,24},{24,28},{28,0},{1,5},{5... | collective-permute-start | bytes 196616 | tf_op jit(solution)/shard_map/ppermute | solution.py:196
  125.7 4.6 %collective-permute-start.47 = (bf16[1,8,32,128]{3,2,1,0:T(8,128)(2,1)S(1)}, bf16[1,8,32,128]{3,2,1,0:T(8,128)(2,1)S(1)}, u32[]{:S(2)}, u32[]{:S(2)}) collective-permute-start(bf16[1,8,32,128]{3,2,1,0:T(8,128)(2,1)S(1)} %get-tuple-element.71.refs_7_), channel_id=1, source_target_pairs={{4,0},{8,4},{12,8},{16,12},{20,16},{24,20},{28,24},{0,28},{5,1},{9... | collective-permute-start | bytes 196616 | tf_op jit(solution)/shard_map/ppermute | solution.py:196

commit v11 on v9

--- a/solution.py
+++ b/solution.py
@@ -9,8 +9,6 @@
 
 STEPS = 4
 HALVES = 2
-APART_FIRST = (False, False)
-APART_LAST = (False, True)
 WEIGHT = 100
 VMEM_LIMIT = 4 * 1024 * 1024
 VMEM = pl.BlockSpec(memory_space=pltpu.VMEM)
@@ -99,12 +97,8 @@
     return jnp.stack([part[0] for part in trio]), jnp.stack([part[-1] for part in trio])
 
 
-def neighbours_of(value, apart):
-    if apart:
-        parts = (jnp.stack([value[0], value[-1]]), value[1:-1])
-    else:
-        parts = (value,)
-    return [(part, shift(part, "azim", True), shift(part, "azim", False)) for part in parts]
+def from_neighbours(value):
+    return value, shift(value, "azim", True), shift(value, "azim", False)
 
 
 def joined(value, outer, inner, after):
@@ -116,14 +110,16 @@
 
 
 def part_kernel(half, *refs):
-    table, blocks, own, low_az, high_az = refs[:5]
-    following, window = refs[-2:]
-    edge = len(refs) > 9
+    table_ref, blocks, own, low_az, high_az = refs[:5]
+    following, window, index, sem = refs[-4:]
+    edge = len(refs) > 11
     faces, width, depth = blocks.shape[1:]
     columns = own.shape[0]
     span = columns + 2
     rows, lanes = window.shape[1:]
     view = window.reshape(3, span, faces, rows, lanes)
+    indexing = pltpu.make_async_copy(table_ref, index, sem)
+    indexing.start()
 
     def enter(column, carry):
         for azim, source in enumerate((low_az, own, high_az)):
@@ -144,7 +140,8 @@
             return carry
 
         lax.fori_loop(0, faces, enter_stream, 0)
-    neighbours = table.shape[1]
+    indexing.wait()
+    neighbours = index.shape[1]
     low = low_lanes((rows, lanes))
 
     def turn(n, carry):
@@ -152,7 +149,7 @@
         slot = column if edge else n
         for face in range(faces):
             gathered = jnp.concatenate(
-                [window[table[face, k] + column * faces] for k in range(neighbours)], axis=0
+                [window[index[face, k] + column * faces] for k in range(neighbours)], axis=0
             )
             block = blocks[column, face]
             stacked = jnp.concatenate([block[:, : depth // 2], block[:, depth // 2 :]], axis=0)
@@ -176,14 +173,18 @@
     edge = len(rest) > 2
     name = "edge" if edge else "inner"
     done, kept = (2, columns) if edge else (columns - 2, columns - 2)
-    in_specs = [pl.BlockSpec(memory_space=pltpu.SMEM)] + [VMEM] * 4
+    in_specs = [ANY] + [VMEM] * 4
     in_specs += [VMEM] * 3 + [ANY] if edge else [ANY] * 2
     return pl.pallas_call(
         functools.partial(part_kernel, half),
         in_specs=in_specs,
         out_specs=VMEM,
         out_shape=jax.ShapeDtypeStruct((kept, faces, rows, lanes), jnp.bfloat16),
-        scratch_shapes=[pltpu.VMEM((3 * (columns + 2) * faces, rows, lanes), jnp.bfloat16)],
+        scratch_shapes=[
+            pltpu.VMEM((3 * (columns + 2) * faces, rows, lanes), jnp.bfloat16),
+            pltpu.SMEM(table.shape, jnp.int32),
+            pltpu.SemaphoreType.DMA,
+        ],
         cost_estimate=pl.CostEstimate(
             flops=WEIGHT * 2 * done * faces * width * depth * lanes,
             bytes_accessed=WEIGHT * 2 * done * faces * width * depth,
@@ -246,27 +247,32 @@
     blocks = halves_of_rows(trace_blocks.reshape(columns, faces, width, -1))
     codes = neighbour.reshape(faces, -1)
     table = (((codes // faces) % 3) * (columns + 2) + codes // (3 * faces)) * faces + codes % faces
-    table = pltpu.with_memory_space_constraint(table, pltpu.SMEM)
     every = tuple(range(columns))
     current = list(pack(start))
     basis = None
     latest = current[0]
-    around_z = [neighbours_of(current[h], APART_FIRST[h]) for h in range(HALVES)]
+    pieces = [from_neighbours(value) for value in current]
+    outer = None
     for index in range(STEPS):
         previous = tuple(current)
         for h in range(HALVES):
-            parts = around_z[h]
-            apart = len(parts) > 1
-            to_low, to_high = edges(*parts[0], middle if apart and h else latest)
-            pieces = joined(current[h], *parts, latest if h else to_high) if apart else parts[0]
+            if outer is None or h < HALVES - 1:
+                to_low, to_high = edges(*pieces[h], latest)
+            else:
+                own_inner, _ = lax.optimization_barrier((current[h][1:-1], middle))
+                inner = from_neighbours(own_inner)
+                to_low, to_high = edges(*outer, middle)
+                pieces[h] = joined(current[h], outer, inner, latest)
             stream = (shift(to_high, "stream", True), shift(to_low, "stream", False))
-            middle = part(h, table, blocks, pieces, (to_low, to_high))
+            middle = part(h, table, blocks, pieces[h], (to_low, to_high))
             after = middle
-            if h == 1 and index > 0:
+            if h == 0 and index > 0:
                 basis, after = unpack(index - 1, every, *previous, basis, middle)
-            current[h] = latest = part(h, table, blocks, pieces, (*stream, middle, after))
-            if index < STEPS - 1:
-                around_z[h] = neighbours_of(current[h], index == STEPS - 2 and APART_LAST[h])
+            current[h] = latest = part(h, table, blocks, pieces[h], (*stream, middle, after))
+            if index == STEPS - 2 and h == HALVES - 1:
+                outer = from_neighbours(jnp.stack([current[h][0], current[h][-1]]))
+            elif index < STEPS - 1:
+                pieces[h] = from_neighbours(current[h])
     basis, _ = unpack(STEPS - 1, every, *current, basis, None)
     return basis.reshape(STEPS, columns, around, faces, width, lanes)
 

time: 117 us -> 116 us (level)
  waiting for transfers between devices: 36.4 us -> 21.6 us
  starting transfers between devices: 43.8 us -> 58 us
  Pallas kernels: 31.9 us -> 30.7 us
    ppermute x34, waiting for transfers between devices: 36.4 us -> 21.6 us  [shift(): return lax.ppermute(value, axis, pairs)]
    ppermute x34, starting transfers between devices: 43.8 us -> 58 us  [shift(): return lax.ppermute(value, axis, pairs)]
    pallas_call x16, Pallas kernels: 24.8 us -> 23.5 us  [part(): pl.pallas_call(functools.partial(part_kernel, half), in_specs=in_specs, o...]
  transfers between devices with their start and end apart: 34 -> 34, of which waited for: 14 -> 9; matrix products, arithmetic and copies ran while one was open for 1% -> 1% of each run, Pallas kernels for 25% -> 24%
where the time goes in v11:
time: 116 us; the launch traced here: 115 us
  starting transfers between devices  58 us (50%)
  Pallas kernels  30.7 us (26%)
  waiting for transfers between devices  21.6 us (19%)
  local copies, waits for them, and re-layouts  3.23 us (3%)
    ppermute x34, starting transfers between devices, shift(): return lax.ppermute(value, axis, pairs)  58 us
    pallas_call x16, Pallas kernels, part(): pl.pallas_call(functools.partial(part_kernel, half), in_specs=in_specs, o...  23.5 us
    ppermute x34, waiting for transfers between devices, shift(): return lax.ppermute(value, axis, pairs)  21.6 us
    pallas_call x4, Pallas kernels, unpack(): pl.pallas_call(functools.partial(unpack_kernel, index, chosen, skipped),...  4.25 us
    unnamed x6, local copies, waits for them, and re-layouts  2.93 us
    pallas_call x1, Pallas kernels, halves_of_rows(): pl.pallas_call(halves_kernel, in_specs=[VMEM], out_specs=VMEM, out_shape=...  2.72 us
  transfers between devices with their start and end apart: 34, of which 9 were waited for; matrix products, arithmetic and copies ran while one was open for 1% of the time, Pallas kernels for 24%

profile of v11, /device:TPU:0, one launch (start us, length us, event | category | flops | bytes accessed | tf_op | source)
XLA Modules:
  0.0 114.7 jit_solution(12088943850051923000)
XLA Ops:
  0.0 1.0 copy-done.1
  1.0 0.2 pack.1
  1.2 3.1 %collective-permute-start = (bf16[4,8,32,128]{3,2,1,0:T(8,128)(2,1)S(1)}, bf16[4,8,32,128]{3,2,1,0:T(8,128)(2,1)S(1)}, u32[]{:S(2)}, u32[]{:S(2)}) collective-permute-start(bf16[4,8,32,128]{3,2,1,0:T(8,128)(2,1)S(1)} %get-tuple-element.45.refs_2_), channel_id=1, source_target_pairs={{0,1},{1,2},{2,3},{3,0},{4,5},{5,6},{6,7},{7,4},{8,9},{9,10},{10,1... | collective-permute-start | bytes 786440 | tf_op jit(solution)/shard_map/ppermute | solution.py:203
  4.3 2.1 %collective-permute-start.1 = (bf16[4,8,32,128]{3,2,1,0:T(8,128)(2,1)S(1)}, bf16[4,8,32,128]{3,2,1,0:T(8,128)(2,1)S(1)}, u32[]{:S(2)}, u32[]{:S(2)}) collective-permute-start(bf16[4,8,32,128]{3,2,1,0:T(8,128)(2,1)S(1)} %get-tuple-element.45.refs_2_), channel_id=1, source_target_pairs={{1,0},{2,1},{3,2},{0,3},{5,4},{6,5},{7,6},{4,7},{9,8},{10,9},{11,1... | collective-permute-start | bytes 786440 | tf_op jit(solution)/shard_map/ppermute | solution.py:203
  6.4 3.8 %collective-permute-start.7 = (bf16[4,8,32,128]{3,2,1,0:T(8,128)(2,1)S(1)}, bf16[4,8,32,128]{3,2,1,0:T(8,128)(2,1)S(1)}, u32[]{:S(2)}, u32[]{:S(2)}) collective-permute-start(bf16[4,8,32,128]{3,2,1,0:T(8,128)(2,1)S(1)} %get-tuple-element.49.refs_2_), channel_id=1, source_target_pairs={{1,0},{2,1},{3,2},{0,3},{5,4},{6,5},{7,6},{4,7},{9,8},{10,9},{11,1... | collective-permute-start | bytes 786440 | tf_op jit(solution)/shard_map/ppermute | solution.py:203
  10.2 1.9 %copy-done = bf16[4,1,8,64,768]{4,3,2,1,0:T(8,128)(2,1)S(1)} copy-done((bf16[4,1,8,64,768]{4,3,2,1,0:T(8,128)(2,1)S(1)}, bf16[4,1,8,64,768]{4,3,2,1,0:T(8,128)(2,1)}, u32[]{:S(2)}) %copy-start) | copy-done | bytes 3145752
  12.1 2.7 %halves_of_rows.1.refs_1_ = bf16[4,8,64,768]{3,2,1,0:T(8,128)(2,1)S(1)} custom-call(bf16[4,8,64,768]{3,2,1,0:T(8,128)(2,1)S(1)} %bitcast.29), custom_call_target="tpu_custom_call" | custom-call | tf_op jit(solution)/shard_map/halves_of_rows/pallas_call | solution.py:234
  14.9 4.4 %collective-permute-done.1.refs_4_ = bf16[4,8,32,128]{3,2,1,0:T(8,128)(2,1)S(1)} collective-permute-done((bf16[4,8,32,128]{3,2,1,0:T(8,128)(2,1)S(1)}, bf16[4,8,32,128]{3,2,1,0:T(8,128)(2,1)S(1)}, u32[]{:S(2)}, u32[]{:S(2)}) %collective-permute-start.1) | collective-permute-done | bytes 262176 | tf_op jit(solution)/shard_map/ppermute | solution.py:203
  19.4 0.1 collective-permute-start.2
  19.5 2.7 %collective-permute-start.3 = (bf16[3,8,32,128]{3,2,1,0:T(8,128)(2,1)S(1)}, bf16[3,8,32,128]{3,2,1,0:T(8,128)(2,1)S(1)}, u32[]{:S(2)}, u32[]{:S(2)}) collective-permute-start(bf16[3,8,32,128]{3,2,1,0:T(8,128)(2,1)S(1)} %pad_maximum_fusion.3.refs_5_), channel_id=1, source_target_pairs={{4,0},{8,4},{12,8},{16,12},{20,16},{24,20},{28,24},{0,28},{5,1},{9... | collective-permute-start | bytes 589832 | tf_op jit(solution)/shard_map/ppermute | solution.py:203
  22.1 1.5 %inner_half0.4.refs_7_.refs_8_ = bf16[2,8,32,128]{3,2,1,0:T(8,128)(2,1)S(1)} custom-call(s32[8,12]{1,0:T(8,128)S(1)} %fusion.4.refs_0_, bf16[4,8,64,768]{3,2,1,0:T(8,128)(2,1)S(1)} %halves_of_rows.1.refs_1_, bf16[4,8,32,128]{3,2,1,0:T(8,128)(2,1)S(1)} %get-tuple-element.45.refs_2_, bf16[4,8,32,128]{3,2,1,0:T(8,128)(2,1)S(1)} %collective-permute-done.refs_3_, ...), custom_call_target="tpu_custom_call" | custom-call | flops 20132659200 | bytes 157286400 | tf_op jit(solution)/shard_map/inner_half0/pallas_call | solution.py:178
  23.6 1.8 %collective-permute-done.2.refs_5_ = bf16[3,8,32,128]{3,2,1,0:T(8,128)(2,1)S(1)} collective-permute-done((bf16[3,8,32,128]{3,2,1,0:T(8,128)(2,1)S(1)}, bf16[3,8,32,128]{3,2,1,0:T(8,128)(2,1)S(1)}, u32[]{:S(2)}, u32[]{:S(2)}) %collective-permute-start.2) | collective-permute-done | bytes 196640 | tf_op jit(solution)/shard_map/ppermute | solution.py:203
  25.4 0.5 collective-permute-done.3.refs_6_
  25.9 1.5 %edge_half0.4.refs_2_.first_ref = bf16[4,8,32,128]{3,2,1,0:T(8,128)(2,1)S(1)} custom-call(s32[8,12]{1,0:T(8,128)S(1)} %fusion.4.refs_0_, bf16[4,8,64,768]{3,2,1,0:T(8,128)(2,1)S(1)} %halves_of_rows.1.refs_1_, bf16[4,8,32,128]{3,2,1,0:T(8,128)(2,1)S(1)} %get-tuple-element.45.refs_2_, bf16[4,8,32,128]{3,2,1,0:T(8,128)(2,1)S(1)} %collective-permute-done.refs_3_, ...), custom_call_target="tpu_custom_call" | custom-call | flops 20132659200 | bytes 157286400 | tf_op jit(solution)/shard_map/edge_half0/pallas_call | solution.py:178
  27.3 0.5 collective-permute-start.4
  27.9 3.4 %collective-permute-start.5 = (bf16[4,8,32,128]{3,2,1,0:T(8,128)(2,1)S(1)}, bf16[4,8,32,128]{3,2,1,0:T(8,128)(2,1)S(1)}, u32[]{:S(2)}, u32[]{:S(2)}) collective-permute-start(bf16[4,8,32,128]{3,2,1,0:T(8,128)(2,1)S(1)} %edge_half0.4.refs_2_.first_ref), channel_id=1, source_target_pairs={{1,0},{2,1},{3,2},{0,3},{5,4},{6,5},{7,6},{4,7},{9,8},{10,9},{11,1... | collective-permute-start | bytes 786440 | tf_op jit(solution)/shard_map/ppermute | solution.py:203
  31.3 1.5 %collective-permute-start.8 = (bf16[3,8,32,128]{3,2,1,0:T(8,128)(2,1)S(1)}, bf16[3,8,32,128]{3,2,1,0:T(8,128)(2,1)S(1)}, u32[]{:S(2)}, u32[]{:S(2)}) collective-permute-start(bf16[3,8,32,128]{3,2,1,0:T(8,128)(2,1)S(1)} %pad_maximum_fusion.4.refs_6_), channel_id=1, source_target_pairs={{0,4},{4,8},{8,12},{12,16},{16,20},{20,24},{24,28},{28,0},{1,5},{5... | collective-permute-start | bytes 589832 | tf_op jit(solution)/shard_map/ppermute | solution.py:203
  32.9 1.2 %collective-permute-start.9 = (bf16[3,8,32,128]{3,2,1,0:T(8,128)(2,1)S(1)}, bf16[3,8,32,128]{3,2,1,0:T(8,128)(2,1)S(1)}, u32[]{:S(2)}, u32[]{:S(2)}) collective-permute-start(bf16[3,8,32,128]{3,2,1,0:T(8,128)(2,1)S(1)} %pad_maximum_fusion.5.refs_5_), channel_id=1, source_target_pairs={{4,0},{8,4},{12,8},{16,12},{20,16},{24,20},{28,24},{0,28},{5,1},{9... | collective-permute-start | bytes 589832 | tf_op jit(solution)/shard_map/ppermute | solution.py:203
  34.1 1.5 %inner_half1.4.refs_7_.refs_8_ = bf16[2,8,32,128]{3,2,1,0:T(8,128)(2,1)S(1)} custom-call(s32[8,12]{1,0:T(8,128)S(1)} %fusion.4.refs_0_, bf16[4,8,64,768]{3,2,1,0:T(8,128)(2,1)S(1)} %halves_of_rows.1.refs_1_, bf16[4,8,32,128]{3,2,1,0:T(8,128)(2,1)S(1)} %get-tuple-element.49.refs_2_, bf16[4,8,32,128]{3,2,1,0:T(8,128)(2,1)S(1)} %collective-permute-done.6.refs_3_, ...), custom_call_target="tpu_custom_call" | custom-call | flops 20132659200 | bytes 157286400 | tf_op jit(solution)/shard_map/inner_half1/pallas_call | solution.py:178
  35.6 2.8 %collective-permute-done.8.refs_5_ = bf16[3,8,32,128]{3,2,1,0:T(8,128)(2,1)S(1)} collective-permute-done((bf16[3,8,32,128]{3,2,1,0:T(8,128)(2,1)S(1)}, bf16[3,8,32,128]{3,2,1,0:T(8,128)(2,1)S(1)}, u32[]{:S(2)}, u32[]{:S(2)}) %collective-permute-start.8) | collective-permute-done | bytes 196640 | tf_op jit(solution)/shard_map/ppermute | solution.py:203
  38.4 1.5 %edge_half1.4.second_ref.refs_2_ = bf16[4,8,32,128]{3,2,1,0:T(8,128)(2,1)S(1)} custom-call(s32[8,12]{1,0:T(8,128)S(1)} %fusion.4.refs_0_, bf16[4,8,64,768]{3,2,1,0:T(8,128)(2,1)S(1)} %halves_of_rows.1.refs_1_, bf16[4,8,32,128]{3,2,1,0:T(8,128)(2,1)S(1)} %get-tuple-element.49.refs_2_, bf16[4,8,32,128]{3,2,1,0:T(8,128)(2,1)S(1)} %collective-permute-done.6.refs_3_, ...), custom_call_target="tpu_custom_call" | custom-call | flops 20132659200 | bytes 157286400 | tf_op jit(solution)/shard_map/edge_half1/pallas_call | solution.py:178
  39.9 0.1 collective-permute-start.14
  40.0 3.8 %collective-permute-start.15 = (bf16[4,8,32,128]{3,2,1,0:T(8,128)(2,1)S(1)}, bf16[4,8,32,128]{3,2,1,0:T(8,128)(2,1)S(1)}, u32[]{:S(2)}, u32[]{:S(2)}) collective-permute-start(bf16[4,8,32,128]{3,2,1,0:T(8,128)(2,1)S(1)} %edge_half1.4.second_ref.refs_2_), channel_id=1, source_target_pairs={{1,0},{2,1},{3,2},{0,3},{5,4},{6,5},{7,6},{4,7},{9,8},{10,9},{11,1... | collective-permute-start | bytes 786440 | tf_op jit(solution)/shard_map/ppermute | solution.py:203
  43.9 1.5 %collective-permute-start.10 = (bf16[3,8,32,128]{3,2,1,0:T(8,128)(2,1)S(1)}, bf16[3,8,32,128]{3,2,1,0:T(8,128)(2,1)S(1)}, u32[]{:S(2)}, u32[]{:S(2)}) collective-permute-start(bf16[3,8,32,128]{3,2,1,0:T(8,128)(2,1)S(1)} %pad_maximum_fusion.6.refs_6_), channel_id=1, source_target_pairs={{0,4},{4,8},{8,12},{12,16},{16,20},{20,24},{24,28},{28,0},{1,5},{5... | collective-permute-start | bytes 589832 | tf_op jit(solution)/shard_map/ppermute | solution.py:203
  45.4 1.2 %collective-permute-start.11 = (bf16[3,8,32,128]{3,2,1,0:T(8,128)(2,1)S(1)}, bf16[3,8,32,128]{3,2,1,0:T(8,128)(2,1)S(1)}, u32[]{:S(2)}, u32[]{:S(2)}) collective-permute-start(bf16[3,8,32,128]{3,2,1,0:T(8,128)(2,1)S(1)} %pad_maximum_fusion.7.refs_5_), channel_id=1, source_target_pairs={{4,0},{8,4},{12,8},{16,12},{20,16},{24,20},{28,24},{0,28},{5,1},{9... | collective-permute-start | bytes 589832 | tf_op jit(solution)/shard_map/ppermute | solution.py:203
  46.7 1.5 %inner_half0.5.refs_0_.refs_7_ = bf16[2,8,32,128]{3,2,1,0:T(8,128)(2,1)S(1)} custom-call(s32[8,12]{1,0:T(8,128)S(1)} %fusion.4.refs_0_, bf16[4,8,64,768]{3,2,1,0:T(8,128)(2,1)S(1)} %halves_of_rows.1.refs_1_, bf16[4,8,32,128]{3,2,1,0:T(8,128)(2,1)S(1)} %edge_half0.4.refs_2_.first_ref, bf16[4,8,32,128]{3,2,1,0:T(8,128)(2,1)S(1)} %collective-permute-done.4.refs_3_, ...), custom_call_target="tpu_custom_call" | custom-call | flops 20132659200 | bytes 157286400 | tf_op jit(solution)/shard_map/inner_half0/pallas_call | solution.py:178
  48.1 0.9 unpack.4
  49.1 2.9 %collective-permute-done.10.refs_5_ = bf16[3,8,32,128]{3,2,1,0:T(8,128)(2,1)S(1)} collective-permute-done((bf16[3,8,32,128]{3,2,1,0:T(8,128)(2,1)S(1)}, bf16[3,8,32,128]{3,2,1,0:T(8,128)(2,1)S(1)}, u32[]{:S(2)}, u32[]{:S(2)}) %collective-permute-start.10) | collective-permute-done | bytes 196640 | tf_op jit(solution)/shard_map/ppermute | solution.py:203
  52.0 1.5 %edge_half0.5.refs_2_.first_ref = bf16[4,8,32,128]{3,2,1,0:T(8,128)(2,1)S(1)} custom-call(s32[8,12]{1,0:T(8,128)S(1)} %fusion.4.refs_0_, bf16[4,8,64,768]{3,2,1,0:T(8,128)(2,1)S(1)} %halves_of_rows.1.refs_1_, bf16[4,8,32,128]{3,2,1,0:T(8,128)(2,1)S(1)} %edge_half0.4.refs_2_.first_ref, bf16[4,8,32,128]{3,2,1,0:T(8,128)(2,1)S(1)} %collective-permute-done.4.refs_3_, ...), custom_call_target="tpu_custom_call" | custom-call | flops 20132659200 | bytes 157286400 | tf_op jit(solution)/shard_map/edge_half0/pallas_call | solution.py:178
  53.4 0.1 collective-permute-start.12
  53.5 3.8 %collective-permute-start.13 = (bf16[4,8,32,128]{3,2,1,0:T(8,128)(2,1)S(1)}, bf16[4,8,32,128]{3,2,1,0:T(8,128)(2,1)S(1)}, u32[]{:S(2)}, u32[]{:S(2)}) collective-permute-start(bf16[4,8,32,128]{3,2,1,0:T(8,128)(2,1)S(1)} %edge_half0.5.refs_2_.first_ref), channel_id=1, source_target_pairs={{1,0},{2,1},{3,2},{0,3},{5,4},{6,5},{7,6},{4,7},{9,8},{10,9},{11,1... | collective-permute-start | bytes 786440 | tf_op jit(solution)/shard_map/ppermute | solution.py:203
  57.5 2.7 %collective-permute-start.17 = (bf16[3,8,32,128]{3,2,1,0:T(8,128)(2,1)S(1)}, bf16[3,8,32,128]{3,2,1,0:T(8,128)(2,1)S(1)}, u32[]{:S(2)}, u32[]{:S(2)}) collective-permute-start(bf16[3,8,32,128]{3,2,1,0:T(8,128)(2,1)S(1)} %pad_maximum_fusion.9.refs_5_), channel_id=1, source_target_pairs={{4,0},{8,4},{12,8},{16,12},{20,16},{24,20},{28,24},{0,28},{5,1},{9... | collective-permute-start | bytes 589832 | tf_op jit(solution)/shard_map/ppermute | solution.py:203
  60.2 1.5 %inner_half1.5.refs_7_.refs_8_ = bf16[2,8,32,128]{3,2,1,0:T(8,128)(2,1)S(1)} custom-call(s32[8,12]{1,0:T(8,128)S(1)} %fusion.4.refs_0_, bf16[4,8,64,768]{3,2,1,0:T(8,128)(2,1)S(1)} %halves_of_rows.1.refs_1_, bf16[4,8,32,128]{3,2,1,0:T(8,128)(2,1)S(1)} %edge_half1.4.second_ref.refs_2_, bf16[4,8,32,128]{3,2,1,0:T(8,128)(2,1)S(1)} %collective-permute-done.14.refs_3_, ...), custom_call_target="tpu_custom_call" | custom-call | flops 20132659200 | bytes 157286400 | tf_op jit(solution)/shard_map/inner_half1/pallas_call | solution.py:178
  61.7 3.0 %collective-permute-done.16.refs_5_ = bf16[3,8,32,128]{3,2,1,0:T(8,128)(2,1)S(1)} collective-permute-done((bf16[3,8,32,128]{3,2,1,0:T(8,128)(2,1)S(1)}, bf16[3,8,32,128]{3,2,1,0:T(8,128)(2,1)S(1)}, u32[]{:S(2)}, u32[]{:S(2)}) %collective-permute-start.16) | collective-permute-done | bytes 196640 | tf_op jit(solution)/shard_map/ppermute | solution.py:203
  64.7 1.5 %edge_half1.5.second_ref.refs_2_ = bf16[4,8,32,128]{3,2,1,0:T(8,128)(2,1)S(1)} custom-call(s32[8,12]{1,0:T(8,128)S(1)} %fusion.4.refs_0_, bf16[4,8,64,768]{3,2,1,0:T(8,128)(2,1)S(1)} %halves_of_rows.1.refs_1_, bf16[4,8,32,128]{3,2,1,0:T(8,128)(2,1)S(1)} %edge_half1.4.second_ref.refs_2_, bf16[4,8,32,128]{3,2,1,0:T(8,128)(2,1)S(1)} %collective-permute-done.14.refs_3_, ...), custom_call_target="tpu_custom_call" | custom-call | flops 20132659200 | bytes 157286400 | tf_op jit(solution)/shard_map/edge_half1/pallas_call | solution.py:178
  66.1 0.1 collective-permute-start.22
  66.2 3.8 %collective-permute-start.23 = (bf16[4,8,32,128]{3,2,1,0:T(8,128)(2,1)S(1)}, bf16[4,8,32,128]{3,2,1,0:T(8,128)(2,1)S(1)}, u32[]{:S(2)}, u32[]{:S(2)}) collective-permute-start(bf16[4,8,32,128]{3,2,1,0:T(8,128)(2,1)S(1)} %edge_half1.5.second_ref.refs_2_), channel_id=1, source_target_pairs={{1,0},{2,1},{3,2},{0,3},{5,4},{6,5},{7,6},{4,7},{9,8},{10,9},{11,1... | collective-permute-start | bytes 786440 | tf_op jit(solution)/shard_map/ppermute | solution.py:203
  70.1 0.1 collective-permute-start.18
  70.2 2.6 %collective-permute-start.19 = (bf16[3,8,32,128]{3,2,1,0:T(8,128)(2,1)S(1)}, bf16[3,8,32,128]{3,2,1,0:T(8,128)(2,1)S(1)}, u32[]{:S(2)}, u32[]{:S(2)}) collective-permute-start(bf16[3,8,32,128]{3,2,1,0:T(8,128)(2,1)S(1)} %pad_maximum_fusion.11.refs_5_), channel_id=1, source_target_pairs={{4,0},{8,4},{12,8},{16,12},{20,16},{24,20},{28,24},{0,28},{5,1},{9... | collective-permute-start | bytes 589832 | tf_op jit(solution)/shard_map/ppermute | solution.py:203
  72.9 1.5 %inner_half0.6.refs_1_.refs_7_ = bf16[2,8,32,128]{3,2,1,0:T(8,128)(2,1)S(1)} custom-call(s32[8,12]{1,0:T(8,128)S(1)} %fusion.4.refs_0_, bf16[4,8,64,768]{3,2,1,0:T(8,128)(2,1)S(1)} %halves_of_rows.1.refs_1_, bf16[4,8,32,128]{3,2,1,0:T(8,128)(2,1)S(1)} %edge_half0.5.refs_2_.first_ref, bf16[4,8,32,128]{3,2,1,0:T(8,128)(2,1)S(1)} %collective-permute-done.12.refs_3_, ...), custom_call_target="tpu_custom_call" | custom-call | flops 20132659200 | bytes 157286400 | tf_op jit(solution)/shard_map/inner_half0/pallas_call | solution.py:178
  74.4 0.9 unpack.5
  75.3 2.1 %collective-permute-done.18.refs_5_ = bf16[3,8,32,128]{3,2,1,0:T(8,128)(2,1)S(1)} collective-permute-done((bf16[3,8,32,128]{3,2,1,0:T(8,128)(2,1)S(1)}, bf16[3,8,32,128]{3,2,1,0:T(8,128)(2,1)S(1)}, u32[]{:S(2)}, u32[]{:S(2)}) %collective-permute-start.18) | collective-permute-done | bytes 196640 | tf_op jit(solution)/shard_map/ppermute | solution.py:203
  77.4 1.5 %edge_half0.6.refs_2_.first_ref = bf16[4,8,32,128]{3,2,1,0:T(8,128)(2,1)S(1)} custom-call(s32[8,12]{1,0:T(8,128)S(1)} %fusion.4.refs_0_, bf16[4,8,64,768]{3,2,1,0:T(8,128)(2,1)S(1)} %halves_of_rows.1.refs_1_, bf16[4,8,32,128]{3,2,1,0:T(8,128)(2,1)S(1)} %edge_half0.5.refs_2_.first_ref, bf16[4,8,32,128]{3,2,1,0:T(8,128)(2,1)S(1)} %collective-permute-done.12.refs_3_, ...), custom_call_target="tpu_custom_call" | custom-call | flops 20132659200 | bytes 157286400 | tf_op jit(solution)/shard_map/edge_half0/pallas_call | solution.py:178
  78.8 0.1 collective-permute-start.20
  78.9 3.8 %collective-permute-start.21 = (bf16[4,8,32,128]{3,2,1,0:T(8,128)(2,1)S(1)}, bf16[4,8,32,128]{3,2,1,0:T(8,128)(2,1)S(1)}, u32[]{:S(2)}, u32[]{:S(2)}) collective-permute-start(bf16[4,8,32,128]{3,2,1,0:T(8,128)(2,1)S(1)} %edge_half0.6.refs_2_.first_ref), channel_id=1, source_target_pairs={{1,0},{2,1},{3,2},{0,3},{5,4},{6,5},{7,6},{4,7},{9,8},{10,9},{11,1... | collective-permute-start | bytes 786440 | tf_op jit(solution)/shard_map/ppermute | solution.py:203
  82.8 0.1 collective-permute-start.24
  82.9 2.7 %collective-permute-start.25 = (bf16[3,8,32,128]{3,2,1,0:T(8,128)(2,1)S(1)}, bf16[3,8,32,128]{3,2,1,0:T(8,128)(2,1)S(1)}, u32[]{:S(2)}, u32[]{:S(2)}) collective-permute-start(bf16[3,8,32,128]{3,2,1,0:T(8,128)(2,1)S(1)} %pad_maximum_fusion.13.refs_5_), channel_id=1, source_target_pairs={{4,0},{8,4},{12,8},{16,12},{20,16},{24,20},{28,24},{0,28},{5,1},{9... | collective-permute-start | bytes 589832 | tf_op jit(solution)/shard_map/ppermute | solution.py:203
  85.6 1.5 %inner_half1.6.refs_7_.refs_8_ = bf16[2,8,32,128]{3,2,1,0:T(8,128)(2,1)S(1)} custom-call(s32[8,12]{1,0:T(8,128)S(1)} %fusion.4.refs_0_, bf16[4,8,64,768]{3,2,1,0:T(8,128)(2,1)S(1)} %halves_of_rows.1.refs_1_, bf16[4,8,32,128]{3,2,1,0:T(8,128)(2,1)S(1)} %edge_half1.5.second_ref.refs_2_, bf16[4,8,32,128]{3,2,1,0:T(8,128)(2,1)S(1)} %collective-permute-done.22.refs_3_, ...), custom_call_target="tpu_custom_call" | custom-call | flops 20132659200 | bytes 157286400 | tf_op jit(solution)/shard_map/inner_half1/pallas_call | solution.py:178
  87.1 3.0 %collective-permute-done.24.refs_5_ = bf16[3,8,32,128]{3,2,1,0:T(8,128)(2,1)S(1)} collective-permute-done((bf16[3,8,32,128]{3,2,1,0:T(8,128)(2,1)S(1)}, bf16[3,8,32,128]{3,2,1,0:T(8,128)(2,1)S(1)}, u32[]{:S(2)}, u32[]{:S(2)}) %collective-permute-start.24) | collective-permute-done | bytes 196640 | tf_op jit(solution)/shard_map/ppermute | solution.py:203
  90.1 1.5 %edge_half1.6.second_ref.refs_2_ = bf16[4,8,32,128]{3,2,1,0:T(8,128)(2,1)S(1)} custom-call(s32[8,12]{1,0:T(8,128)S(1)} %fusion.4.refs_0_, bf16[4,8,64,768]{3,2,1,0:T(8,128)(2,1)S(1)} %halves_of_rows.1.refs_1_, bf16[4,8,32,128]{3,2,1,0:T(8,128)(2,1)S(1)} %edge_half1.5.second_ref.refs_2_, bf16[4,8,32,128]{3,2,1,0:T(8,128)(2,1)S(1)} %collective-permute-done.22.refs_3_, ...), custom_call_target="tpu_custom_call" | custom-call | flops 20132659200 | bytes 157286400 | tf_op jit(solution)/shard_map/edge_half1/pallas_call | solution.py:178
  91.6 0.1 collective-permute-start.28
  91.7 3.8 %collective-permute-start.29 = (bf16[2,8,32,128]{3,2,1,0:T(8,128)(2,1)S(1)}, bf16[2,8,32,128]{3,2,1,0:T(8,128)(2,1)S(1)}, u32[]{:S(2)}, u32[]{:S(2)}) collective-permute-start(bf16[2,8,32,128]{3,2,1,0:T(8,128)(2,1)S(1)} %pad_maximum_fusion.18), channel_id=1, source_target_pairs={{1,0},{2,1},{3,2},{0,3},{5,4},{6,5},{7,6},{4,7},{9,8},{10,9},{11,1... | collective-permute-start | bytes 393224 | tf_op jit(solution)/shard_map/ppermute | solution.py:203
  95.6 0.1 collective-permute-start.26
  95.7 2.6 %collective-permute-start.27 = (bf16[3,8,32,128]{3,2,1,0:T(8,128)(2,1)S(1)}, bf16[3,8,32,128]{3,2,1,0:T(8,128)(2,1)S(1)}, u32[]{:S(2)}, u32[]{:S(2)}) collective-permute-start(bf16[3,8,32,128]{3,2,1,0:T(8,128)(2,1)S(1)} %pad_maximum_fusion.15.refs_5_), channel_id=1, source_target_pairs={{4,0},{8,4},{12,8},{16,12},{20,16},{24,20},{28,24},{0,28},{5,1},{9... | collective-permute-start | bytes 589832 | tf_op jit(solution)/shard_map/ppermute | solution.py:203
  98.4 1.5 %inner_half0.7.refs_1_.refs_7_ = bf16[2,8,32,128]{3,2,1,0:T(8,128)(2,1)S(1)} custom-call(s32[8,12]{1,0:T(8,128)S(1)} %fusion.4.refs_0_, bf16[4,8,64,768]{3,2,1,0:T(8,128)(2,1)S(1)} %halves_of_rows.1.refs_1_, bf16[4,8,32,128]{3,2,1,0:T(8,128)(2,1)S(1)} %edge_half0.6.refs_2_.first_ref, bf16[4,8,32,128]{3,2,1,0:T(8,128)(2,1)S(1)} %collective-permute-done.20.refs_3_, ...), custom_call_target="tpu_custom_call" | custom-call | flops 20132659200 | bytes 157286400 | tf_op jit(solution)/shard_map/inner_half0/pallas_call | solution.py:178
  99.8 0.9 unpack.6
  100.8 0.1 collective-permute-start.30
  100.8 3.8 %collective-permute-start.31 = (bf16[2,8,32,128]{3,2,1,0:T(8,128)(2,1)S(1)}, bf16[2,8,32,128]{3,2,1,0:T(8,128)(2,1)S(1)}, u32[]{:S(2)}, u32[]{:S(2)}) collective-permute-start(bf16[2,8,32,128]{3,2,1,0:T(8,128)(2,1)S(1)} %slice.222), channel_id=1, source_target_pairs={{1,0},{2,1},{3,2},{0,3},{5,4},{6,5},{7,6},{4,7},{9,8},{10,9},{11,1... | collective-permute-start | bytes 393224 | tf_op jit(solution)/shard_map/ppermute | solution.py:203
  104.8 2.7 %collective-permute-start.33 = (bf16[3,8,32,128]{3,2,1,0:T(8,128)(2,1)S(1)}, bf16[3,8,32,128]{3,2,1,0:T(8,128)(2,1)S(1)}, u32[]{:S(2)}, u32[]{:S(2)}) collective-permute-start(bf16[3,8,32,128]{3,2,1,0:T(8,128)(2,1)S(1)} %pad_maximum_fusion.17.refs_5_), channel_id=1, source_target_pairs={{4,0},{8,4},{12,8},{16,12},{20,16},{24,20},{28,24},{0,28},{5,1},{9... | collective-permute-start | bytes 589832 | tf_op jit(solution)/shard_map/ppermute | solution.py:203
  107.5 1.5 %edge_half0.7.first_ref = bf16[4,8,32,128]{3,2,1,0:T(8,128)(2,1)S(1)} custom-call(s32[8,12]{1,0:T(8,128)S(1)} %fusion.4.refs_0_, bf16[4,8,64,768]{3,2,1,0:T(8,128)(2,1)S(1)} %halves_of_rows.1.refs_1_, bf16[4,8,32,128]{3,2,1,0:T(8,128)(2,1)S(1)} %edge_half0.6.refs_2_.first_ref, bf16[4,8,32,128]{3,2,1,0:T(8,128)(2,1)S(1)} %collective-permute-done.20.refs_3_, ...), custom_call_target="tpu_custom_call" | custom-call | flops 20132659200 | bytes 157286400 | tf_op jit(solution)/shard_map/edge_half0/pallas_call | solution.py:178
  109.2 1.5 %inner_half1.7.refs_7_.refs_8_ = bf16[2,8,32,128]{3,2,1,0:T(8,128)(2,1)S(1)} custom-call(s32[8,12]{1,0:T(8,128)S(1)} %fusion.4.refs_0_, bf16[4,8,64,768]{3,2,1,0:T(8,128)(2,1)S(1)} %halves_of_rows.1.refs_1_, bf16[4,8,32,128]{3,2,1,0:T(8,128)(2,1)S(1)} %edge_half1.6.second_ref.refs_2_, bf16[4,8,32,128]{3,2,1,0:T(8,128)(2,1)S(1)} %pad_maximum_fusion.refs_3_, ...), custom_call_target="tpu_custom_call" | custom-call | flops 20132659200 | bytes 157286400 | tf_op jit(solution)/shard_map/inner_half1/pallas_call | solution.py:178
  110.6 1.1 collective-permute-done.32.refs_5_
  111.7 1.5 %edge_half1.7.second_ref = bf16[4,8,32,128]{3,2,1,0:T(8,128)(2,1)S(1)} custom-call(s32[8,12]{1,0:T(8,128)S(1)} %fusion.4.refs_0_, bf16[4,8,64,768]{3,2,1,0:T(8,128)(2,1)S(1)} %halves_of_rows.1.refs_1_, bf16[4,8,32,128]{3,2,1,0:T(8,128)(2,1)S(1)} %edge_half1.6.second_ref.refs_2_, bf16[4,8,32,128]{3,2,1,0:T(8,128)(2,1)S(1)} %pad_maximum_fusion.refs_3_, ...), custom_call_target="tpu_custom_call" | custom-call | flops 20132659200 | bytes 157286400 | tf_op jit(solution)/shard_map/edge_half1/pallas_call | solution.py:178
  113.2 1.5 %unpack.7 = (bf16[4,4,8,64,128]{4,3,2,1,0:T(8,128)(2,1)}, f32[8,128]{1,0:T(8,128)}) custom-call(bf16[4,8,32,128]{3,2,1,0:T(8,128)(2,1)S(1)} %edge_half0.7.first_ref, bf16[4,8,32,128]{3,2,1,0:T(8,128)(2,1)S(1)} %edge_half1.7.second_ref, bf16[4,4,8,64,128]{4,3,2,1,0:T(8,128)(2,1)} %get-tuple-element.79.refs_0_), custom_call_target="tpu_custom_call", output_to_operand_aliasing={{0}: (2, {})} | custom-call | tf_op jit(solution)/shard_map/unpack/pallas_call | solution.py:77
  (79 shorter events, 1.0 us)
Async XLA Ops:
  0.0 1.0 copy-start.1
  1.2 13.7 %collective-permute-start = (bf16[4,8,32,128]{3,2,1,0:T(8,128)(2,1)S(1)}, bf16[4,8,32,128]{3,2,1,0:T(8,128)(2,1)S(1)}, u32[]{:S(2)}, u32[]{:S(2)}) collective-permute-start(bf16[4,8,32,128]{3,2,1,0:T(8,128)(2,1)S(1)} %get-tuple-element.45.refs_2_), channel_id=1, source_target_pairs={{0,1},{1,2},{2,3},{3,0},{4,5},{5,6},{6,7},{7,4},{8,9},{9,10},{10,1... | collective-permute-start | bytes 786440 | tf_op jit(solution)/shard_map/ppermute | solution.py:203
  4.3 15.0 %collective-permute-start.1 = (bf16[4,8,32,128]{3,2,1,0:T(8,128)(2,1)S(1)}, bf16[4,8,32,128]{3,2,1,0:T(8,128)(2,1)S(1)}, u32[]{:S(2)}, u32[]{:S(2)}) collective-permute-start(bf16[4,8,32,128]{3,2,1,0:T(8,128)(2,1)S(1)} %get-tuple-element.45.refs_2_), channel_id=1, source_target_pairs={{1,0},{2,1},{3,2},{0,3},{5,4},{6,5},{7,6},{4,7},{9,8},{10,9},{11,1... | collective-permute-start | bytes 786440 | tf_op jit(solution)/shard_map/ppermute | solution.py:203
  6.4 24.8 %collective-permute-start.6 = (bf16[4,8,32,128]{3,2,1,0:T(8,128)(2,1)S(1)}, bf16[4,8,32,128]{3,2,1,0:T(8,128)(2,1)S(1)}, u32[]{:S(2)}, u32[]{:S(2)}) collective-permute-start(bf16[4,8,32,128]{3,2,1,0:T(8,128)(2,1)S(1)} %get-tuple-element.49.refs_2_), channel_id=1, source_target_pairs={{0,1},{1,2},{2,3},{3,0},{4,5},{5,6},{6,7},{7,4},{8,9},{9,10},{10,1... | collective-permute-start | bytes 786440 | tf_op jit(solution)/shard_map/ppermute | solution.py:203
  6.4 24.8 %collective-permute-start.7 = (bf16[4,8,32,128]{3,2,1,0:T(8,128)(2,1)S(1)}, bf16[4,8,32,128]{3,2,1,0:T(8,128)(2,1)S(1)}, u32[]{:S(2)}, u32[]{:S(2)}) collective-permute-start(bf16[4,8,32,128]{3,2,1,0:T(8,128)(2,1)S(1)} %get-tuple-element.49.refs_2_), channel_id=1, source_target_pairs={{1,0},{2,1},{3,2},{0,3},{5,4},{6,5},{7,6},{4,7},{9,8},{10,9},{11,1... | collective-permute-start | bytes 786440 | tf_op jit(solution)/shard_map/ppermute | solution.py:203
  10.2 1.9 %copy-start = (bf16[4,1,8,64,768]{4,3,2,1,0:T(8,128)(2,1)S(1)}, bf16[4,1,8,64,768]{4,3,2,1,0:T(8,128)(2,1)}, u32[]{:S(2)}) copy-start(bf16[4,1,8,64,768]{4,3,2,1,0:T(8,128)(2,1)} %param.4) | copy-start | bytes 9437188
  12.1 2.7 %copy-start.2 = (s32[1,8,12]{2,1,0:T(8,128)S(1)}, s32[1,8,12]{2,1,0:T(8,128)}, u32[]{:S(2)}) copy-start(s32[1,8,12]{2,1,0:T(8,128)} %param.5) | copy-start | bytes 1156
  19.4 6.0 %collective-permute-start.2 = (bf16[3,8,32,128]{3,2,1,0:T(8,128)(2,1)S(1)}, bf16[3,8,32,128]{3,2,1,0:T(8,128)(2,1)S(1)}, u32[]{:S(2)}, u32[]{:S(2)}) collective-permute-start(bf16[3,8,32,128]{3,2,1,0:T(8,128)(2,1)S(1)} %pad_maximum_fusion.2.refs_6_), channel_id=1, source_target_pairs={{0,4},{4,8},{8,12},{12,16},{16,20},{20,24},{24,28},{28,0},{1,5},{5... | collective-permute-start | bytes 589832 | tf_op jit(solution)/shard_map/ppermute | solution.py:203
  19.5 6.4 %collective-permute-start.3 = (bf16[3,8,32,128]{3,2,1,0:T(8,128)(2,1)S(1)}, bf16[3,8,32,128]{3,2,1,0:T(8,128)(2,1)S(1)}, u32[]{:S(2)}, u32[]{:S(2)}) collective-permute-start(bf16[3,8,32,128]{3,2,1,0:T(8,128)(2,1)S(1)} %pad_maximum_fusion.3.refs_5_), channel_id=1, source_target_pairs={{4,0},{8,4},{12,8},{16,12},{20,16},{24,20},{28,24},{0,28},{5,1},{9... | collective-permute-start | bytes 589832 | tf_op jit(solution)/shard_map/ppermute | solution.py:203
  27.3 16.4 %collective-permute-start.4 = (bf16[4,8,32,128]{3,2,1,0:T(8,128)(2,1)S(1)}, bf16[4,8,32,128]{3,2,1,0:T(8,128)(2,1)S(1)}, u32[]{:S(2)}, u32[]{:S(2)}) collective-permute-start(bf16[4,8,32,128]{3,2,1,0:T(8,128)(2,1)S(1)} %edge_half0.4.refs_2_.first_ref), channel_id=1, source_target_pairs={{0,1},{1,2},{2,3},{3,0},{4,5},{5,6},{6,7},{7,4},{8,9},{9,10},{10,1... | collective-permute-start | bytes 786440 | tf_op jit(solution)/shard_map/ppermute | solution.py:203
  27.9 15.9 %collective-permute-start.5 = (bf16[4,8,32,128]{3,2,1,0:T(8,128)(2,1)S(1)}, bf16[4,8,32,128]{3,2,1,0:T(8,128)(2,1)S(1)}, u32[]{:S(2)}, u32[]{:S(2)}) collective-permute-start(bf16[4,8,32,128]{3,2,1,0:T(8,128)(2,1)S(1)} %edge_half0.4.refs_2_.first_ref), channel_id=1, source_target_pairs={{1,0},{2,1},{3,2},{0,3},{5,4},{6,5},{7,6},{4,7},{9,8},{10,9},{11,1... | collective-permute-start | bytes 786440 | tf_op jit(solution)/shard_map/ppermute | solution.py:203
  31.3 7.1 %collective-permute-start.8 = (bf16[3,8,32,128]{3,2,1,0:T(8,128)(2,1)S(1)}, bf16[3,8,32,128]{3,2,1,0:T(8,128)(2,1)S(1)}, u32[]{:S(2)}, u32[]{:S(2)}) collective-permute-start(bf16[3,8,32,128]{3,2,1,0:T(8,128)(2,1)S(1)} %pad_maximum_fusion.4.refs_6_), channel_id=1, source_target_pairs={{0,4},{4,8},{8,12},{12,16},{16,20},{20,24},{24,28},{28,0},{1,5},{5... | collective-permute-start | bytes 589832 | tf_op jit(solution)/shard_map/ppermute | solution.py:203
  32.9 5.5 %collective-permute-start.9 = (bf16[3,8,32,128]{3,2,1,0:T(8,128)(2,1)S(1)}, bf16[3,8,32,128]{3,2,1,0:T(8,128)(2,1)S(1)}, u32[]{:S(2)}, u32[]{:S(2)}) collective-permute-start(bf16[3,8,32,128]{3,2,1,0:T(8,128)(2,1)S(1)} %pad_maximum_fusion.5.refs_5_), channel_id=1, source_target_pairs={{4,0},{8,4},{12,8},{16,12},{20,16},{24,20},{28,24},{0,28},{5,1},{9... | collective-permute-start | bytes 589832 | tf_op jit(solution)/shard_map/ppermute | solution.py:203
  39.9 17.4 %collective-permute-start.14 = (bf16[4,8,32,128]{3,2,1,0:T(8,128)(2,1)S(1)}, bf16[4,8,32,128]{3,2,1,0:T(8,128)(2,1)S(1)}, u32[]{:S(2)}, u32[]{:S(2)}) collective-permute-start(bf16[4,8,32,128]{3,2,1,0:T(8,128)(2,1)S(1)} %edge_half1.4.second_ref.refs_2_), channel_id=1, source_target_pairs={{0,1},{1,2},{2,3},{3,0},{4,5},{5,6},{6,7},{7,4},{8,9},{9,10},{10,1... | collective-permute-start | bytes 786440 | tf_op jit(solution)/shard_map/ppermute | solution.py:203
  40.0 17.4 %collective-permute-start.15 = (bf16[4,8,32,128]{3,2,1,0:T(8,128)(2,1)S(1)}, bf16[4,8,32,128]{3,2,1,0:T(8,128)(2,1)S(1)}, u32[]{:S(2)}, u32[]{:S(2)}) collective-permute-start(bf16[4,8,32,128]{3,2,1,0:T(8,128)(2,1)S(1)} %edge_half1.4.second_ref.refs_2_), channel_id=1, source_target_pairs={{1,0},{2,1},{3,2},{0,3},{5,4},{6,5},{7,6},{4,7},{9,8},{10,9},{11,1... | collective-permute-start | bytes 786440 | tf_op jit(solution)/shard_map/ppermute | solution.py:203
  43.9 8.1 %collective-permute-start.10 = (bf16[3,8,32,128]{3,2,1,0:T(8,128)(2,1)S(1)}, bf16[3,8,32,128]{3,2,1,0:T(8,128)(2,1)S(1)}, u32[]{:S(2)}, u32[]{:S(2)}) collective-permute-start(bf16[3,8,32,128]{3,2,1,0:T(8,128)(2,1)S(1)} %pad_maximum_fusion.6.refs_6_), channel_id=1, source_target_pairs={{0,4},{4,8},{8,12},{12,16},{16,20},{20,24},{24,28},{28,0},{1,5},{5... | collective-permute-start | bytes 589832 | tf_op jit(solution)/shard_map/ppermute | solution.py:203
  45.4 6.5 %collective-permute-start.11 = (bf16[3,8,32,128]{3,2,1,0:T(8,128)(2,1)S(1)}, bf16[3,8,32,128]{3,2,1,0:T(8,128)(2,1)S(1)}, u32[]{:S(2)}, u32[]{:S(2)}) collective-permute-start(bf16[3,8,32,128]{3,2,1,0:T(8,128)(2,1)S(1)} %pad_maximum_fusion.7.refs_5_), channel_id=1, source_target_pairs={{4,0},{8,4},{12,8},{16,12},{20,16},{24,20},{28,24},{0,28},{5,1},{9... | collective-permute-start | bytes 589832 | tf_op jit(solution)/shard_map/ppermute | solution.py:203
  53.4 16.6 %collective-permute-start.12 = (bf16[4,8,32,128]{3,2,1,0:T(8,128)(2,1)S(1)}, bf16[4,8,32,128]{3,2,1,0:T(8,128)(2,1)S(1)}, u32[]{:S(2)}, u32[]{:S(2)}) collective-permute-start(bf16[4,8,32,128]{3,2,1,0:T(8,128)(2,1)S(1)} %edge_half0.5.refs_2_.first_ref), channel_id=1, source_target_pairs={{0,1},{1,2},{2,3},{3,0},{4,5},{5,6},{6,7},{7,4},{8,9},{9,10},{10,1... | collective-permute-start | bytes 786440 | tf_op jit(solution)/shard_map/ppermute | solution.py:203
  53.5 16.5 %collective-permute-start.13 = (bf16[4,8,32,128]{3,2,1,0:T(8,128)(2,1)S(1)}, bf16[4,8,32,128]{3,2,1,0:T(8,128)(2,1)S(1)}, u32[]{:S(2)}, u32[]{:S(2)}) collective-permute-start(bf16[4,8,32,128]{3,2,1,0:T(8,128)(2,1)S(1)} %edge_half0.5.refs_2_.first_ref), channel_id=1, source_target_pairs={{1,0},{2,1},{3,2},{0,3},{5,4},{6,5},{7,6},{4,7},{9,8},{10,9},{11,1... | collective-permute-start | bytes 786440 | tf_op jit(solution)/shard_map/ppermute | solution.py:203
  57.4 7.2 %collective-permute-start.16 = (bf16[3,8,32,128]{3,2,1,0:T(8,128)(2,1)S(1)}, bf16[3,8,32,128]{3,2,1,0:T(8,128)(2,1)S(1)}, u32[]{:S(2)}, u32[]{:S(2)}) collective-permute-start(bf16[3,8,32,128]{3,2,1,0:T(8,128)(2,1)S(1)} %pad_maximum_fusion.8.refs_6_), channel_id=1, source_target_pairs={{0,4},{4,8},{8,12},{12,16},{16,20},{20,24},{24,28},{28,0},{1,5},{5... | collective-permute-start | bytes 589832 | tf_op jit(solution)/shard_map/ppermute | solution.py:203
  57.5 7.2 %collective-permute-start.17 = (bf16[3,8,32,128]{3,2,1,0:T(8,128)(2,1)S(1)}, bf16[3,8,32,128]{3,2,1,0:T(8,128)(2,1)S(1)}, u32[]{:S(2)}, u32[]{:S(2)}) collective-permute-start(bf16[3,8,32,128]{3,2,1,0:T(8,128)(2,1)S(1)} %pad_maximum_fusion.9.refs_5_), channel_id=1, source_target_pairs={{4,0},{8,4},{12,8},{16,12},{20,16},{24,20},{28,24},{0,28},{5,1},{9... | collective-permute-start | bytes 589832 | tf_op jit(solution)/shard_map/ppermute | solution.py:203
  66.1 16.6 %collective-permute-start.22 = (bf16[4,8,32,128]{3,2,1,0:T(8,128)(2,1)S(1)}, bf16[4,8,32,128]{3,2,1,0:T(8,128)(2,1)S(1)}, u32[]{:S(2)}, u32[]{:S(2)}) collective-permute-start(bf16[4,8,32,128]{3,2,1,0:T(8,128)(2,1)S(1)} %edge_half1.5.second_ref.refs_2_), channel_id=1, source_target_pairs={{0,1},{1,2},{2,3},{3,0},{4,5},{5,6},{6,7},{7,4},{8,9},{9,10},{10,1... | collective-permute-start | bytes 786440 | tf_op jit(solution)/shard_map/ppermute | solution.py:203
  66.2 16.5 %collective-permute-start.23 = (bf16[4,8,32,128]{3,2,1,0:T(8,128)(2,1)S(1)}, bf16[4,8,32,128]{3,2,1,0:T(8,128)(2,1)S(1)}, u32[]{:S(2)}, u32[]{:S(2)}) collective-permute-start(bf16[4,8,32,128]{3,2,1,0:T(8,128)(2,1)S(1)} %edge_half1.5.second_ref.refs_2_), channel_id=1, source_target_pairs={{1,0},{2,1},{3,2},{0,3},{5,4},{6,5},{7,6},{4,7},{9,8},{10,9},{11,1... | collective-permute-start | bytes 786440 | tf_op jit(solution)/shard_map/ppermute | solution.py:203
  70.1 7.2 %collective-permute-start.18 = (bf16[3,8,32,128]{3,2,1,0:T(8,128)(2,1)S(1)}, bf16[3,8,32,128]{3,2,1,0:T(8,128)(2,1)S(1)}, u32[]{:S(2)}, u32[]{:S(2)}) collective-permute-start(bf16[3,8,32,128]{3,2,1,0:T(8,128)(2,1)S(1)} %pad_maximum_fusion.10.refs_6_), channel_id=1, source_target_pairs={{0,4},{4,8},{8,12},{12,16},{16,20},{20,24},{24,28},{28,0},{1,5},{5... | collective-permute-start | bytes 589832 | tf_op jit(solution)/shard_map/ppermute | solution.py:203
  70.2 7.1 %collective-permute-start.19 = (bf16[3,8,32,128]{3,2,1,0:T(8,128)(2,1)S(1)}, bf16[3,8,32,128]{3,2,1,0:T(8,128)(2,1)S(1)}, u32[]{:S(2)}, u32[]{:S(2)}) collective-permute-start(bf16[3,8,32,128]{3,2,1,0:T(8,128)(2,1)S(1)} %pad_maximum_fusion.11.refs_5_), channel_id=1, source_target_pairs={{4,0},{8,4},{12,8},{16,12},{20,16},{24,20},{28,24},{0,28},{5,1},{9... | collective-permute-start | bytes 589832 | tf_op jit(solution)/shard_map/ppermute | solution.py:203
  78.8 16.6 %collective-permute-start.20 = (bf16[4,8,32,128]{3,2,1,0:T(8,128)(2,1)S(1)}, bf16[4,8,32,128]{3,2,1,0:T(8,128)(2,1)S(1)}, u32[]{:S(2)}, u32[]{:S(2)}) collective-permute-start(bf16[4,8,32,128]{3,2,1,0:T(8,128)(2,1)S(1)} %edge_half0.6.refs_2_.first_ref), channel_id=1, source_target_pairs={{0,1},{1,2},{2,3},{3,0},{4,5},{5,6},{6,7},{7,4},{8,9},{9,10},{10,1... | collective-permute-start | bytes 786440 | tf_op jit(solution)/shard_map/ppermute | solution.py:203
  78.9 16.6 %collective-permute-start.21 = (bf16[4,8,32,128]{3,2,1,0:T(8,128)(2,1)S(1)}, bf16[4,8,32,128]{3,2,1,0:T(8,128)(2,1)S(1)}, u32[]{:S(2)}, u32[]{:S(2)}) collective-permute-start(bf16[4,8,32,128]{3,2,1,0:T(8,128)(2,1)S(1)} %edge_half0.6.refs_2_.first_ref), channel_id=1, source_target_pairs={{1,0},{2,1},{3,2},{0,3},{5,4},{6,5},{7,6},{4,7},{9,8},{10,9},{11,1... | collective-permute-start | bytes 786440 | tf_op jit(solution)/shard_map/ppermute | solution.py:203
  82.8 7.2 %collective-permute-start.24 = (bf16[3,8,32,128]{3,2,1,0:T(8,128)(2,1)S(1)}, bf16[3,8,32,128]{3,2,1,0:T(8,128)(2,1)S(1)}, u32[]{:S(2)}, u32[]{:S(2)}) collective-permute-start(bf16[3,8,32,128]{3,2,1,0:T(8,128)(2,1)S(1)} %pad_maximum_fusion.12.refs_6_), channel_id=1, source_target_pairs={{0,4},{4,8},{8,12},{12,16},{16,20},{20,24},{24,28},{28,0},{1,5},{5... | collective-permute-start | bytes 589832 | tf_op jit(solution)/shard_map/ppermute | solution.py:203
  82.9 7.1 %collective-permute-start.25 = (bf16[3,8,32,128]{3,2,1,0:T(8,128)(2,1)S(1)}, bf16[3,8,32,128]{3,2,1,0:T(8,128)(2,1)S(1)}, u32[]{:S(2)}, u32[]{:S(2)}) collective-permute-start(bf16[3,8,32,128]{3,2,1,0:T(8,128)(2,1)S(1)} %pad_maximum_fusion.13.refs_5_), channel_id=1, source_target_pairs={{4,0},{8,4},{12,8},{16,12},{20,16},{24,20},{28,24},{0,28},{5,1},{9... | collective-permute-start | bytes 589832 | tf_op jit(solution)/shard_map/ppermute | solution.py:203
  91.6 9.2 %collective-permute-start.28 = (bf16[2,8,32,128]{3,2,1,0:T(8,128)(2,1)S(1)}, bf16[2,8,32,128]{3,2,1,0:T(8,128)(2,1)S(1)}, u32[]{:S(2)}, u32[]{:S(2)}) collective-permute-start(bf16[2,8,32,128]{3,2,1,0:T(8,128)(2,1)S(1)} %pad_maximum_fusion.18), channel_id=1, source_target_pairs={{0,1},{1,2},{2,3},{3,0},{4,5},{5,6},{6,7},{7,4},{8,9},{9,10},{10,1... | collective-permute-start | bytes 393224 | tf_op jit(solution)/shard_map/ppermute | solution.py:203
  91.7 13.0 %collective-permute-start.29 = (bf16[2,8,32,128]{3,2,1,0:T(8,128)(2,1)S(1)}, bf16[2,8,32,128]{3,2,1,0:T(8,128)(2,1)S(1)}, u32[]{:S(2)}, u32[]{:S(2)}) collective-permute-start(bf16[2,8,32,128]{3,2,1,0:T(8,128)(2,1)S(1)} %pad_maximum_fusion.18), channel_id=1, source_target_pairs={{1,0},{2,1},{3,2},{0,3},{5,4},{6,5},{7,6},{4,7},{9,8},{10,9},{11,1... | collective-permute-start | bytes 393224 | tf_op jit(solution)/shard_map/ppermute | solution.py:203
  95.6 9.2 %collective-permute-start.26 = (bf16[3,8,32,128]{3,2,1,0:T(8,128)(2,1)S(1)}, bf16[3,8,32,128]{3,2,1,0:T(8,128)(2,1)S(1)}, u32[]{:S(2)}, u32[]{:S(2)}) collective-permute-start(bf16[3,8,32,128]{3,2,1,0:T(8,128)(2,1)S(1)} %pad_maximum_fusion.14.refs_6_), channel_id=1, source_target_pairs={{0,4},{4,8},{8,12},{12,16},{16,20},{20,24},{24,28},{28,0},{1,5},{5... | collective-permute-start | bytes 589832 | tf_op jit(solution)/shard_map/ppermute | solution.py:203
  95.7 11.8 %collective-permute-start.27 = (bf16[3,8,32,128]{3,2,1,0:T(8,128)(2,1)S(1)}, bf16[3,8,32,128]{3,2,1,0:T(8,128)(2,1)S(1)}, u32[]{:S(2)}, u32[]{:S(2)}) collective-permute-start(bf16[3,8,32,128]{3,2,1,0:T(8,128)(2,1)S(1)} %pad_maximum_fusion.15.refs_5_), channel_id=1, source_target_pairs={{4,0},{8,4},{12,8},{16,12},{20,16},{24,20},{28,24},{0,28},{5,1},{9... | collective-permute-start | bytes 589832 | tf_op jit(solution)/shard_map/ppermute | solution.py:203
  100.8 8.2 %collective-permute-start.30 = (bf16[2,8,32,128]{3,2,1,0:T(8,128)(2,1)S(1)}, bf16[2,8,32,128]{3,2,1,0:T(8,128)(2,1)S(1)}, u32[]{:S(2)}, u32[]{:S(2)}) collective-permute-start(bf16[2,8,32,128]{3,2,1,0:T(8,128)(2,1)S(1)} %slice.222), channel_id=1, source_target_pairs={{0,1},{1,2},{2,3},{3,0},{4,5},{5,6},{6,7},{7,4},{8,9},{9,10},{10,1... | collective-permute-start | bytes 393224 | tf_op jit(solution)/shard_map/ppermute | solution.py:203
  100.8 8.2 %collective-permute-start.31 = (bf16[2,8,32,128]{3,2,1,0:T(8,128)(2,1)S(1)}, bf16[2,8,32,128]{3,2,1,0:T(8,128)(2,1)S(1)}, u32[]{:S(2)}, u32[]{:S(2)}) collective-permute-start(bf16[2,8,32,128]{3,2,1,0:T(8,128)(2,1)S(1)} %slice.222), channel_id=1, source_target_pairs={{1,0},{2,1},{3,2},{0,3},{5,4},{6,5},{7,6},{4,7},{9,8},{10,9},{11,1... | collective-permute-start | bytes 393224 | tf_op jit(solution)/shard_map/ppermute | solution.py:203
  104.7 6.9 %collective-permute-start.32 = (bf16[3,8,32,128]{3,2,1,0:T(8,128)(2,1)S(1)}, bf16[3,8,32,128]{3,2,1,0:T(8,128)(2,1)S(1)}, u32[]{:S(2)}, u32[]{:S(2)}) collective-permute-start(bf16[3,8,32,128]{3,2,1,0:T(8,128)(2,1)S(1)} %pad_maximum_fusion.16.refs_6_), channel_id=1, source_target_pairs={{0,4},{4,8},{8,12},{12,16},{16,20},{20,24},{24,28},{28,0},{1,5},{5... | collective-permute-start | bytes 589832 | tf_op jit(solution)/shard_map/ppermute | solution.py:203
  104.8 6.8 %collective-permute-start.33 = (bf16[3,8,32,128]{3,2,1,0:T(8,128)(2,1)S(1)}, bf16[3,8,32,128]{3,2,1,0:T(8,128)(2,1)S(1)}, u32[]{:S(2)}, u32[]{:S(2)}) collective-permute-start(bf16[3,8,32,128]{3,2,1,0:T(8,128)(2,1)S(1)} %pad_maximum_fusion.17.refs_5_), channel_id=1, source_target_pairs={{4,0},{8,4},{12,8},{16,12},{20,16},{24,20},{28,24},{0,28},{5,1},{9... | collective-permute-start | bytes 589832 | tf_op jit(solution)/shard_map/ppermute | solution.py:203

commit v12 on v11

--- a/solution.py
+++ b/solution.py
@@ -129,7 +129,7 @@
 
     lax.fori_loop(0, columns, enter, 0)
     if edge:
-        low_st, high_st, before = refs[5:8]
+        high_st, low_st, before = refs[5:8]
 
         def enter_stream(face, carry):
             for azim in range(3):
@@ -263,8 +263,8 @@
                 inner = from_neighbours(own_inner)
                 to_low, to_high = edges(*outer, middle)
                 pieces[h] = joined(current[h], outer, inner, latest)
-            stream = (shift(to_high, "stream", True), shift(to_low, "stream", False))
-            middle = part(h, table, blocks, pieces[h], (to_low, to_high))
+            stream = (shift(to_low, "stream", False), shift(to_high, "stream", True))
+            middle = part(h, table, blocks, pieces[h], (to_high, to_low))
             after = middle
             if h == 0 and index > 0:
                 basis, after = unpack(index - 1, every, *previous, basis, middle)

time: 116 us -> 114 us (0.983)
  starting transfers between devices: 58 us -> 43.8 us
  waiting for transfers between devices: 21.6 us -> 34.7 us
    ppermute x34, starting transfers between devices: 58 us -> 43.8 us  [shift(): return lax.ppermute(value, axis, pairs)]
    ppermute x34, waiting for transfers between devices: 21.6 us -> 34.7 us  [shift(): return lax.ppermute(value, axis, pairs)]
  transfers between devices with their start and end apart: 34 -> 34, of which waited for: 9 -> 15; matrix products, arithmetic and copies ran while one was open for 1% -> 1% of each run, Pallas kernels for 24% -> 24%
where the time goes in v12:
time: 114 us
  starting transfers between devices  43.8 us (38%)
  waiting for transfers between devices  34.7 us (30%)
  Pallas kernels  30.7 us (27%)
  local copies, waits for them, and re-layouts  3.23 us (3%)
    ppermute x34, starting transfers between devices, shift(): return lax.ppermute(value, axis, pairs)  43.8 us
    ppermute x34, waiting for transfers between devices, shift(): return lax.ppermute(value, axis, pairs)  34.7 us
    pallas_call x16, Pallas kernels, part(): pl.pallas_call(functools.partial(part_kernel, half), in_specs=in_specs, o...  23.6 us
    pallas_call x4, Pallas kernels, unpack(): pl.pallas_call(functools.partial(unpack_kernel, index, chosen, skipped),...  4.25 us
    unnamed x6, local copies, waits for them, and re-layouts  2.93 us
    pallas_call x1, Pallas kernels, halves_of_rows(): pl.pallas_call(halves_kernel, in_specs=[VMEM], out_specs=VMEM, out_shape=...  2.72 us
  transfers between devices with their start and end apart: 34, of which 15 were waited for; matrix products, arithmetic and copies ran while one was open for 1% of the time, Pallas kernels for 24%

profile of v12, /device:TPU:0, one launch (start us, length us, event | category | flops | bytes accessed | tf_op | source)
XLA Modules:
  0.0 113.6 jit_solution(918973524927297988)
XLA Ops:
  0.0 1.0 copy-done.1
  1.0 0.2 pack.1
  1.2 3.1 %collective-permute-start = (bf16[4,8,32,128]{3,2,1,0:T(8,128)(2,1)S(1)}, bf16[4,8,32,128]{3,2,1,0:T(8,128)(2,1)S(1)}, u32[]{:S(2)}, u32[]{:S(2)}) collective-permute-start(bf16[4,8,32,128]{3,2,1,0:T(8,128)(2,1)S(1)} %get-tuple-element.45.refs_2_), channel_id=1, source_target_pairs={{0,1},{1,2},{2,3},{3,0},{4,5},{5,6},{6,7},{7,4},{8,9},{9,10},{10,1... | collective-permute-start | bytes 786440 | tf_op jit(solution)/shard_map/ppermute | solution.py:203
  4.3 2.1 %collective-permute-start.1 = (bf16[4,8,32,128]{3,2,1,0:T(8,128)(2,1)S(1)}, bf16[4,8,32,128]{3,2,1,0:T(8,128)(2,1)S(1)}, u32[]{:S(2)}, u32[]{:S(2)}) collective-permute-start(bf16[4,8,32,128]{3,2,1,0:T(8,128)(2,1)S(1)} %get-tuple-element.45.refs_2_), channel_id=1, source_target_pairs={{1,0},{2,1},{3,2},{0,3},{5,4},{6,5},{7,6},{4,7},{9,8},{10,9},{11,1... | collective-permute-start | bytes 786440 | tf_op jit(solution)/shard_map/ppermute | solution.py:203
  6.4 3.8 %collective-permute-start.7 = (bf16[4,8,32,128]{3,2,1,0:T(8,128)(2,1)S(1)}, bf16[4,8,32,128]{3,2,1,0:T(8,128)(2,1)S(1)}, u32[]{:S(2)}, u32[]{:S(2)}) collective-permute-start(bf16[4,8,32,128]{3,2,1,0:T(8,128)(2,1)S(1)} %get-tuple-element.49.refs_2_), channel_id=1, source_target_pairs={{1,0},{2,1},{3,2},{0,3},{5,4},{6,5},{7,6},{4,7},{9,8},{10,9},{11,1... | collective-permute-start | bytes 786440 | tf_op jit(solution)/shard_map/ppermute | solution.py:203
  10.2 1.9 %copy-done = bf16[4,1,8,64,768]{4,3,2,1,0:T(8,128)(2,1)S(1)} copy-done((bf16[4,1,8,64,768]{4,3,2,1,0:T(8,128)(2,1)S(1)}, bf16[4,1,8,64,768]{4,3,2,1,0:T(8,128)(2,1)}, u32[]{:S(2)}) %copy-start) | copy-done | bytes 3145752
  12.1 2.7 %halves_of_rows.1.refs_1_ = bf16[4,8,64,768]{3,2,1,0:T(8,128)(2,1)S(1)} custom-call(bf16[4,8,64,768]{3,2,1,0:T(8,128)(2,1)S(1)} %bitcast.29), custom_call_target="tpu_custom_call" | custom-call | tf_op jit(solution)/shard_map/halves_of_rows/pallas_call | solution.py:234
  14.9 4.4 %collective-permute-done.1.refs_4_ = bf16[4,8,32,128]{3,2,1,0:T(8,128)(2,1)S(1)} collective-permute-done((bf16[4,8,32,128]{3,2,1,0:T(8,128)(2,1)S(1)}, bf16[4,8,32,128]{3,2,1,0:T(8,128)(2,1)S(1)}, u32[]{:S(2)}, u32[]{:S(2)}) %collective-permute-start.1) | collective-permute-done | bytes 262176 | tf_op jit(solution)/shard_map/ppermute | solution.py:203
  19.5 0.5 collective-permute-start.3
  20.0 1.5 %inner_half0.4.refs_7_.refs_8_ = bf16[2,8,32,128]{3,2,1,0:T(8,128)(2,1)S(1)} custom-call(s32[8,12]{1,0:T(8,128)S(1)} %fusion.4.refs_0_, bf16[4,8,64,768]{3,2,1,0:T(8,128)(2,1)S(1)} %halves_of_rows.1.refs_1_, bf16[4,8,32,128]{3,2,1,0:T(8,128)(2,1)S(1)} %get-tuple-element.45.refs_2_, bf16[4,8,32,128]{3,2,1,0:T(8,128)(2,1)S(1)} %collective-permute-done.refs_3_, ...), custom_call_target="tpu_custom_call" | custom-call | flops 20132659200 | bytes 157286400 | tf_op jit(solution)/shard_map/inner_half0/pallas_call | solution.py:178
  21.5 1.9 %collective-permute-done.2.refs_5_ = bf16[3,8,32,128]{3,2,1,0:T(8,128)(2,1)S(1)} collective-permute-done((bf16[3,8,32,128]{3,2,1,0:T(8,128)(2,1)S(1)}, bf16[3,8,32,128]{3,2,1,0:T(8,128)(2,1)S(1)}, u32[]{:S(2)}, u32[]{:S(2)}) %collective-permute-start.2) | collective-permute-done | bytes 196640 | tf_op jit(solution)/shard_map/ppermute | solution.py:203
  23.4 4.2 %collective-permute-done.3.refs_6_ = bf16[3,8,32,128]{3,2,1,0:T(8,128)(2,1)S(1)} collective-permute-done((bf16[3,8,32,128]{3,2,1,0:T(8,128)(2,1)S(1)}, bf16[3,8,32,128]{3,2,1,0:T(8,128)(2,1)S(1)}, u32[]{:S(2)}, u32[]{:S(2)}) %collective-permute-start.3) | collective-permute-done | bytes 196640 | tf_op jit(solution)/shard_map/ppermute | solution.py:203
  27.7 1.5 %edge_half0.4.refs_2_.first_ref = bf16[4,8,32,128]{3,2,1,0:T(8,128)(2,1)S(1)} custom-call(s32[8,12]{1,0:T(8,128)S(1)} %fusion.4.refs_0_, bf16[4,8,64,768]{3,2,1,0:T(8,128)(2,1)S(1)} %halves_of_rows.1.refs_1_, bf16[4,8,32,128]{3,2,1,0:T(8,128)(2,1)S(1)} %get-tuple-element.45.refs_2_, bf16[4,8,32,128]{3,2,1,0:T(8,128)(2,1)S(1)} %collective-permute-done.refs_3_, ...), custom_call_target="tpu_custom_call" | custom-call | flops 20132659200 | bytes 157286400 | tf_op jit(solution)/shard_map/edge_half0/pallas_call | solution.py:178
  29.1 0.7 collective-permute-start.4
  29.9 3.2 %collective-permute-start.5 = (bf16[4,8,32,128]{3,2,1,0:T(8,128)(2,1)S(1)}, bf16[4,8,32,128]{3,2,1,0:T(8,128)(2,1)S(1)}, u32[]{:S(2)}, u32[]{:S(2)}) collective-permute-start(bf16[4,8,32,128]{3,2,1,0:T(8,128)(2,1)S(1)} %edge_half0.4.refs_2_.first_ref), channel_id=1, source_target_pairs={{1,0},{2,1},{3,2},{0,3},{5,4},{6,5},{7,6},{4,7},{9,8},{10,9},{11,1... | collective-permute-start | bytes 786440 | tf_op jit(solution)/shard_map/ppermute | solution.py:203
  33.2 0.5 collective-permute-start.9
  33.7 1.5 %inner_half1.4.refs_7_.refs_8_ = bf16[2,8,32,128]{3,2,1,0:T(8,128)(2,1)S(1)} custom-call(s32[8,12]{1,0:T(8,128)S(1)} %fusion.4.refs_0_, bf16[4,8,64,768]{3,2,1,0:T(8,128)(2,1)S(1)} %halves_of_rows.1.refs_1_, bf16[4,8,32,128]{3,2,1,0:T(8,128)(2,1)S(1)} %get-tuple-element.49.refs_2_, bf16[4,8,32,128]{3,2,1,0:T(8,128)(2,1)S(1)} %collective-permute-done.6.refs_3_, ...), custom_call_target="tpu_custom_call" | custom-call | flops 20132659200 | bytes 157286400 | tf_op jit(solution)/shard_map/inner_half1/pallas_call | solution.py:178
  35.2 3.1 %collective-permute-done.8.refs_5_ = bf16[3,8,32,128]{3,2,1,0:T(8,128)(2,1)S(1)} collective-permute-done((bf16[3,8,32,128]{3,2,1,0:T(8,128)(2,1)S(1)}, bf16[3,8,32,128]{3,2,1,0:T(8,128)(2,1)S(1)}, u32[]{:S(2)}, u32[]{:S(2)}) %collective-permute-start.8) | collective-permute-done | bytes 196640 | tf_op jit(solution)/shard_map/ppermute | solution.py:203
  38.4 1.8 %collective-permute-done.9.refs_6_ = bf16[3,8,32,128]{3,2,1,0:T(8,128)(2,1)S(1)} collective-permute-done((bf16[3,8,32,128]{3,2,1,0:T(8,128)(2,1)S(1)}, bf16[3,8,32,128]{3,2,1,0:T(8,128)(2,1)S(1)}, u32[]{:S(2)}, u32[]{:S(2)}) %collective-permute-start.9) | collective-permute-done | bytes 196640 | tf_op jit(solution)/shard_map/ppermute | solution.py:203
  40.2 1.5 %edge_half1.4.second_ref.refs_2_ = bf16[4,8,32,128]{3,2,1,0:T(8,128)(2,1)S(1)} custom-call(s32[8,12]{1,0:T(8,128)S(1)} %fusion.4.refs_0_, bf16[4,8,64,768]{3,2,1,0:T(8,128)(2,1)S(1)} %halves_of_rows.1.refs_1_, bf16[4,8,32,128]{3,2,1,0:T(8,128)(2,1)S(1)} %get-tuple-element.49.refs_2_, bf16[4,8,32,128]{3,2,1,0:T(8,128)(2,1)S(1)} %collective-permute-done.6.refs_3_, ...), custom_call_target="tpu_custom_call" | custom-call | flops 20132659200 | bytes 157286400 | tf_op jit(solution)/shard_map/edge_half1/pallas_call | solution.py:178
  41.7 0.1 collective-permute-start.14
  41.8 3.8 %collective-permute-start.15 = (bf16[4,8,32,128]{3,2,1,0:T(8,128)(2,1)S(1)}, bf16[4,8,32,128]{3,2,1,0:T(8,128)(2,1)S(1)}, u32[]{:S(2)}, u32[]{:S(2)}) collective-permute-start(bf16[4,8,32,128]{3,2,1,0:T(8,128)(2,1)S(1)} %edge_half1.4.second_ref.refs_2_), channel_id=1, source_target_pairs={{1,0},{2,1},{3,2},{0,3},{5,4},{6,5},{7,6},{4,7},{9,8},{10,9},{11,1... | collective-permute-start | bytes 786440 | tf_op jit(solution)/shard_map/ppermute | solution.py:203
  45.7 0.5 collective-permute-start.10
  46.1 0.2 collective-permute-start.11
  46.3 1.5 %inner_half0.5.refs_0_.refs_7_ = bf16[2,8,32,128]{3,2,1,0:T(8,128)(2,1)S(1)} custom-call(s32[8,12]{1,0:T(8,128)S(1)} %fusion.4.refs_0_, bf16[4,8,64,768]{3,2,1,0:T(8,128)(2,1)S(1)} %halves_of_rows.1.refs_1_, bf16[4,8,32,128]{3,2,1,0:T(8,128)(2,1)S(1)} %edge_half0.4.refs_2_.first_ref, bf16[4,8,32,128]{3,2,1,0:T(8,128)(2,1)S(1)} %collective-permute-done.4.refs_3_, ...), custom_call_target="tpu_custom_call" | custom-call | flops 20132659200 | bytes 157286400 | tf_op jit(solution)/shard_map/inner_half0/pallas_call | solution.py:178
  47.8 0.9 unpack.4
  48.7 2.4 %collective-permute-done.10.refs_5_ = bf16[3,8,32,128]{3,2,1,0:T(8,128)(2,1)S(1)} collective-permute-done((bf16[3,8,32,128]{3,2,1,0:T(8,128)(2,1)S(1)}, bf16[3,8,32,128]{3,2,1,0:T(8,128)(2,1)S(1)}, u32[]{:S(2)}, u32[]{:S(2)}) %collective-permute-start.10) | collective-permute-done | bytes 196640 | tf_op jit(solution)/shard_map/ppermute | solution.py:203
  51.1 1.3 %collective-permute-done.11.refs_6_ = bf16[3,8,32,128]{3,2,1,0:T(8,128)(2,1)S(1)} collective-permute-done((bf16[3,8,32,128]{3,2,1,0:T(8,128)(2,1)S(1)}, bf16[3,8,32,128]{3,2,1,0:T(8,128)(2,1)S(1)}, u32[]{:S(2)}, u32[]{:S(2)}) %collective-permute-start.11) | collective-permute-done | bytes 196640 | tf_op jit(solution)/shard_map/ppermute | solution.py:203
  52.3 1.5 %edge_half0.5.refs_2_.first_ref = bf16[4,8,32,128]{3,2,1,0:T(8,128)(2,1)S(1)} custom-call(s32[8,12]{1,0:T(8,128)S(1)} %fusion.4.refs_0_, bf16[4,8,64,768]{3,2,1,0:T(8,128)(2,1)S(1)} %halves_of_rows.1.refs_1_, bf16[4,8,32,128]{3,2,1,0:T(8,128)(2,1)S(1)} %edge_half0.4.refs_2_.first_ref, bf16[4,8,32,128]{3,2,1,0:T(8,128)(2,1)S(1)} %collective-permute-done.4.refs_3_, ...), custom_call_target="tpu_custom_call" | custom-call | flops 20132659200 | bytes 157286400 | tf_op jit(solution)/shard_map/edge_half0/pallas_call | solution.py:178
  53.8 0.1 collective-permute-start.12
  53.9 3.8 %collective-permute-start.13 = (bf16[4,8,32,128]{3,2,1,0:T(8,128)(2,1)S(1)}, bf16[4,8,32,128]{3,2,1,0:T(8,128)(2,1)S(1)}, u32[]{:S(2)}, u32[]{:S(2)}) collective-permute-start(bf16[4,8,32,128]{3,2,1,0:T(8,128)(2,1)S(1)} %edge_half0.5.refs_2_.first_ref), channel_id=1, source_target_pairs={{1,0},{2,1},{3,2},{0,3},{5,4},{6,5},{7,6},{4,7},{9,8},{10,9},{11,1... | collective-permute-start | bytes 786440 | tf_op jit(solution)/shard_map/ppermute | solution.py:203
  57.8 1.0 collective-permute-start.16
  58.9 1.5 %inner_half1.5.refs_7_.refs_8_ = bf16[2,8,32,128]{3,2,1,0:T(8,128)(2,1)S(1)} custom-call(s32[8,12]{1,0:T(8,128)S(1)} %fusion.4.refs_0_, bf16[4,8,64,768]{3,2,1,0:T(8,128)(2,1)S(1)} %halves_of_rows.1.refs_1_, bf16[4,8,32,128]{3,2,1,0:T(8,128)(2,1)S(1)} %edge_half1.4.second_ref.refs_2_, bf16[4,8,32,128]{3,2,1,0:T(8,128)(2,1)S(1)} %collective-permute-done.14.refs_3_, ...), custom_call_target="tpu_custom_call" | custom-call | flops 20132659200 | bytes 157286400 | tf_op jit(solution)/shard_map/inner_half1/pallas_call | solution.py:178
  60.4 3.2 %collective-permute-done.16.refs_5_ = bf16[3,8,32,128]{3,2,1,0:T(8,128)(2,1)S(1)} collective-permute-done((bf16[3,8,32,128]{3,2,1,0:T(8,128)(2,1)S(1)}, bf16[3,8,32,128]{3,2,1,0:T(8,128)(2,1)S(1)}, u32[]{:S(2)}, u32[]{:S(2)}) %collective-permute-start.16) | collective-permute-done | bytes 196640 | tf_op jit(solution)/shard_map/ppermute | solution.py:203
  63.6 1.3 %collective-permute-done.17.refs_6_ = bf16[3,8,32,128]{3,2,1,0:T(8,128)(2,1)S(1)} collective-permute-done((bf16[3,8,32,128]{3,2,1,0:T(8,128)(2,1)S(1)}, bf16[3,8,32,128]{3,2,1,0:T(8,128)(2,1)S(1)}, u32[]{:S(2)}, u32[]{:S(2)}) %collective-permute-start.17) | collective-permute-done | bytes 196640 | tf_op jit(solution)/shard_map/ppermute | solution.py:203
  64.9 1.5 %edge_half1.5.second_ref.refs_2_ = bf16[4,8,32,128]{3,2,1,0:T(8,128)(2,1)S(1)} custom-call(s32[8,12]{1,0:T(8,128)S(1)} %fusion.4.refs_0_, bf16[4,8,64,768]{3,2,1,0:T(8,128)(2,1)S(1)} %halves_of_rows.1.refs_1_, bf16[4,8,32,128]{3,2,1,0:T(8,128)(2,1)S(1)} %edge_half1.4.second_ref.refs_2_, bf16[4,8,32,128]{3,2,1,0:T(8,128)(2,1)S(1)} %collective-permute-done.14.refs_3_, ...), custom_call_target="tpu_custom_call" | custom-call | flops 20132659200 | bytes 157286400 | tf_op jit(solution)/shard_map/edge_half1/pallas_call | solution.py:178
  66.4 0.1 collective-permute-start.22
  66.4 3.8 %collective-permute-start.23 = (bf16[4,8,32,128]{3,2,1,0:T(8,128)(2,1)S(1)}, bf16[4,8,32,128]{3,2,1,0:T(8,128)(2,1)S(1)}, u32[]{:S(2)}, u32[]{:S(2)}) collective-permute-start(bf16[4,8,32,128]{3,2,1,0:T(8,128)(2,1)S(1)} %edge_half1.5.second_ref.refs_2_), channel_id=1, source_target_pairs={{1,0},{2,1},{3,2},{0,3},{5,4},{6,5},{7,6},{4,7},{9,8},{10,9},{11,1... | collective-permute-start | bytes 786440 | tf_op jit(solution)/shard_map/ppermute | solution.py:203
  70.3 1.0 collective-permute-start.18
  71.5 1.5 %inner_half0.6.refs_1_.refs_7_ = bf16[2,8,32,128]{3,2,1,0:T(8,128)(2,1)S(1)} custom-call(s32[8,12]{1,0:T(8,128)S(1)} %fusion.4.refs_0_, bf16[4,8,64,768]{3,2,1,0:T(8,128)(2,1)S(1)} %halves_of_rows.1.refs_1_, bf16[4,8,32,128]{3,2,1,0:T(8,128)(2,1)S(1)} %edge_half0.5.refs_2_.first_ref, bf16[4,8,32,128]{3,2,1,0:T(8,128)(2,1)S(1)} %collective-permute-done.12.refs_3_, ...), custom_call_target="tpu_custom_call" | custom-call | flops 20132659200 | bytes 157286400 | tf_op jit(solution)/shard_map/inner_half0/pallas_call | solution.py:178
  72.9 0.9 unpack.5
  73.9 2.1 %collective-permute-done.18.refs_5_ = bf16[3,8,32,128]{3,2,1,0:T(8,128)(2,1)S(1)} collective-permute-done((bf16[3,8,32,128]{3,2,1,0:T(8,128)(2,1)S(1)}, bf16[3,8,32,128]{3,2,1,0:T(8,128)(2,1)S(1)}, u32[]{:S(2)}, u32[]{:S(2)}) %collective-permute-start.18) | collective-permute-done | bytes 196640 | tf_op jit(solution)/shard_map/ppermute | solution.py:203
  76.0 1.5 %collective-permute-done.19.refs_6_ = bf16[3,8,32,128]{3,2,1,0:T(8,128)(2,1)S(1)} collective-permute-done((bf16[3,8,32,128]{3,2,1,0:T(8,128)(2,1)S(1)}, bf16[3,8,32,128]{3,2,1,0:T(8,128)(2,1)S(1)}, u32[]{:S(2)}, u32[]{:S(2)}) %collective-permute-start.19) | collective-permute-done | bytes 196640 | tf_op jit(solution)/shard_map/ppermute | solution.py:203
  77.4 1.5 %edge_half0.6.refs_2_.first_ref = bf16[4,8,32,128]{3,2,1,0:T(8,128)(2,1)S(1)} custom-call(s32[8,12]{1,0:T(8,128)S(1)} %fusion.4.refs_0_, bf16[4,8,64,768]{3,2,1,0:T(8,128)(2,1)S(1)} %halves_of_rows.1.refs_1_, bf16[4,8,32,128]{3,2,1,0:T(8,128)(2,1)S(1)} %edge_half0.5.refs_2_.first_ref, bf16[4,8,32,128]{3,2,1,0:T(8,128)(2,1)S(1)} %collective-permute-done.12.refs_3_, ...), custom_call_target="tpu_custom_call" | custom-call | flops 20132659200 | bytes 157286400 | tf_op jit(solution)/shard_map/edge_half0/pallas_call | solution.py:178
  78.9 0.1 collective-permute-start.20
  79.0 3.8 %collective-permute-start.21 = (bf16[4,8,32,128]{3,2,1,0:T(8,128)(2,1)S(1)}, bf16[4,8,32,128]{3,2,1,0:T(8,128)(2,1)S(1)}, u32[]{:S(2)}, u32[]{:S(2)}) collective-permute-start(bf16[4,8,32,128]{3,2,1,0:T(8,128)(2,1)S(1)} %edge_half0.6.refs_2_.first_ref), channel_id=1, source_target_pairs={{1,0},{2,1},{3,2},{0,3},{5,4},{6,5},{7,6},{4,7},{9,8},{10,9},{11,1... | collective-permute-start | bytes 786440 | tf_op jit(solution)/shard_map/ppermute | solution.py:203
  82.9 0.8 collective-permute-start.24
  83.8 1.5 %inner_half1.6.refs_7_.refs_8_ = bf16[2,8,32,128]{3,2,1,0:T(8,128)(2,1)S(1)} custom-call(s32[8,12]{1,0:T(8,128)S(1)} %fusion.4.refs_0_, bf16[4,8,64,768]{3,2,1,0:T(8,128)(2,1)S(1)} %halves_of_rows.1.refs_1_, bf16[4,8,32,128]{3,2,1,0:T(8,128)(2,1)S(1)} %edge_half1.5.second_ref.refs_2_, bf16[4,8,32,128]{3,2,1,0:T(8,128)(2,1)S(1)} %collective-permute-done.22.refs_3_, ...), custom_call_target="tpu_custom_call" | custom-call | flops 20132659200 | bytes 157286400 | tf_op jit(solution)/shard_map/inner_half1/pallas_call | solution.py:178
  85.3 2.8 %collective-permute-done.24.refs_5_ = bf16[3,8,32,128]{3,2,1,0:T(8,128)(2,1)S(1)} collective-permute-done((bf16[3,8,32,128]{3,2,1,0:T(8,128)(2,1)S(1)}, bf16[3,8,32,128]{3,2,1,0:T(8,128)(2,1)S(1)}, u32[]{:S(2)}, u32[]{:S(2)}) %collective-permute-start.24) | collective-permute-done | bytes 196640 | tf_op jit(solution)/shard_map/ppermute | solution.py:203
  88.1 1.7 %collective-permute-done.25.refs_6_ = bf16[3,8,32,128]{3,2,1,0:T(8,128)(2,1)S(1)} collective-permute-done((bf16[3,8,32,128]{3,2,1,0:T(8,128)(2,1)S(1)}, bf16[3,8,32,128]{3,2,1,0:T(8,128)(2,1)S(1)}, u32[]{:S(2)}, u32[]{:S(2)}) %collective-permute-start.25) | collective-permute-done | bytes 196640 | tf_op jit(solution)/shard_map/ppermute | solution.py:203
  89.8 1.5 %edge_half1.6.second_ref.refs_2_ = bf16[4,8,32,128]{3,2,1,0:T(8,128)(2,1)S(1)} custom-call(s32[8,12]{1,0:T(8,128)S(1)} %fusion.4.refs_0_, bf16[4,8,64,768]{3,2,1,0:T(8,128)(2,1)S(1)} %halves_of_rows.1.refs_1_, bf16[4,8,32,128]{3,2,1,0:T(8,128)(2,1)S(1)} %edge_half1.5.second_ref.refs_2_, bf16[4,8,32,128]{3,2,1,0:T(8,128)(2,1)S(1)} %collective-permute-done.22.refs_3_, ...), custom_call_target="tpu_custom_call" | custom-call | flops 20132659200 | bytes 157286400 | tf_op jit(solution)/shard_map/edge_half1/pallas_call | solution.py:178
  91.3 0.1 collective-permute-start.28
  91.4 3.8 %collective-permute-start.29 = (bf16[2,8,32,128]{3,2,1,0:T(8,128)(2,1)S(1)}, bf16[2,8,32,128]{3,2,1,0:T(8,128)(2,1)S(1)}, u32[]{:S(2)}, u32[]{:S(2)}) collective-permute-start(bf16[2,8,32,128]{3,2,1,0:T(8,128)(2,1)S(1)} %pad_maximum_fusion.18), channel_id=1, source_target_pairs={{1,0},{2,1},{3,2},{0,3},{5,4},{6,5},{7,6},{4,7},{9,8},{10,9},{11,1... | collective-permute-start | bytes 393224 | tf_op jit(solution)/shard_map/ppermute | solution.py:203
  95.3 0.6 collective-permute-start.26
  96.1 1.5 %inner_half0.7.refs_1_.refs_7_ = bf16[2,8,32,128]{3,2,1,0:T(8,128)(2,1)S(1)} custom-call(s32[8,12]{1,0:T(8,128)S(1)} %fusion.4.refs_0_, bf16[4,8,64,768]{3,2,1,0:T(8,128)(2,1)S(1)} %halves_of_rows.1.refs_1_, bf16[4,8,32,128]{3,2,1,0:T(8,128)(2,1)S(1)} %edge_half0.6.refs_2_.first_ref, bf16[4,8,32,128]{3,2,1,0:T(8,128)(2,1)S(1)} %collective-permute-done.20.refs_3_, ...), custom_call_target="tpu_custom_call" | custom-call | flops 20132659200 | bytes 157286400 | tf_op jit(solution)/shard_map/inner_half0/pallas_call | solution.py:178
  97.5 0.9 unpack.6
  98.5 3.8 %collective-permute-start.31 = (bf16[2,8,32,128]{3,2,1,0:T(8,128)(2,1)S(1)}, bf16[2,8,32,128]{3,2,1,0:T(8,128)(2,1)S(1)}, u32[]{:S(2)}, u32[]{:S(2)}) collective-permute-start(bf16[2,8,32,128]{3,2,1,0:T(8,128)(2,1)S(1)} %slice.222), channel_id=1, source_target_pairs={{1,0},{2,1},{3,2},{0,3},{5,4},{6,5},{7,6},{4,7},{9,8},{10,9},{11,1... | collective-permute-start | bytes 393224 | tf_op jit(solution)/shard_map/ppermute | solution.py:203
  102.4 2.1 %collective-permute-start.32 = (bf16[3,8,32,128]{3,2,1,0:T(8,128)(2,1)S(1)}, bf16[3,8,32,128]{3,2,1,0:T(8,128)(2,1)S(1)}, u32[]{:S(2)}, u32[]{:S(2)}) collective-permute-start(bf16[3,8,32,128]{3,2,1,0:T(8,128)(2,1)S(1)} %pad_maximum_fusion.16.refs_6_), channel_id=1, source_target_pairs={{4,0},{8,4},{12,8},{16,12},{20,16},{24,20},{28,24},{0,28},{5,1},{9... | collective-permute-start | bytes 589832 | tf_op jit(solution)/shard_map/ppermute | solution.py:203
  104.7 1.5 %edge_half0.7.first_ref = bf16[4,8,32,128]{3,2,1,0:T(8,128)(2,1)S(1)} custom-call(s32[8,12]{1,0:T(8,128)S(1)} %fusion.4.refs_0_, bf16[4,8,64,768]{3,2,1,0:T(8,128)(2,1)S(1)} %halves_of_rows.1.refs_1_, bf16[4,8,32,128]{3,2,1,0:T(8,128)(2,1)S(1)} %edge_half0.6.refs_2_.first_ref, bf16[4,8,32,128]{3,2,1,0:T(8,128)(2,1)S(1)} %collective-permute-done.20.refs_3_, ...), custom_call_target="tpu_custom_call" | custom-call | flops 20132659200 | bytes 157286400 | tf_op jit(solution)/shard_map/edge_half0/pallas_call | solution.py:178
  106.2 0.5 collective-permute-done.30
  106.9 1.5 %inner_half1.7.refs_7_.refs_8_ = bf16[2,8,32,128]{3,2,1,0:T(8,128)(2,1)S(1)} custom-call(s32[8,12]{1,0:T(8,128)S(1)} %fusion.4.refs_0_, bf16[4,8,64,768]{3,2,1,0:T(8,128)(2,1)S(1)} %halves_of_rows.1.refs_1_, bf16[4,8,32,128]{3,2,1,0:T(8,128)(2,1)S(1)} %edge_half1.6.second_ref.refs_2_, bf16[4,8,32,128]{3,2,1,0:T(8,128)(2,1)S(1)} %pad_maximum_fusion.refs_3_, ...), custom_call_target="tpu_custom_call" | custom-call | flops 20132659200 | bytes 157286400 | tf_op jit(solution)/shard_map/inner_half1/pallas_call | solution.py:178
  108.3 2.3 %collective-permute-done.33.refs_6_ = bf16[3,8,32,128]{3,2,1,0:T(8,128)(2,1)S(1)} collective-permute-done((bf16[3,8,32,128]{3,2,1,0:T(8,128)(2,1)S(1)}, bf16[3,8,32,128]{3,2,1,0:T(8,128)(2,1)S(1)}, u32[]{:S(2)}, u32[]{:S(2)}) %collective-permute-start.33) | collective-permute-done | bytes 196640 | tf_op jit(solution)/shard_map/ppermute | solution.py:203
  110.6 1.5 %edge_half1.7.second_ref = bf16[4,8,32,128]{3,2,1,0:T(8,128)(2,1)S(1)} custom-call(s32[8,12]{1,0:T(8,128)S(1)} %fusion.4.refs_0_, bf16[4,8,64,768]{3,2,1,0:T(8,128)(2,1)S(1)} %halves_of_rows.1.refs_1_, bf16[4,8,32,128]{3,2,1,0:T(8,128)(2,1)S(1)} %edge_half1.6.second_ref.refs_2_, bf16[4,8,32,128]{3,2,1,0:T(8,128)(2,1)S(1)} %pad_maximum_fusion.refs_3_, ...), custom_call_target="tpu_custom_call" | custom-call | flops 20132659200 | bytes 157286400 | tf_op jit(solution)/shard_map/edge_half1/pallas_call | solution.py:178
  112.1 1.5 %unpack.7 = (bf16[4,4,8,64,128]{4,3,2,1,0:T(8,128)(2,1)}, f32[8,128]{1,0:T(8,128)}) custom-call(bf16[4,8,32,128]{3,2,1,0:T(8,128)(2,1)S(1)} %edge_half0.7.first_ref, bf16[4,8,32,128]{3,2,1,0:T(8,128)(2,1)S(1)} %edge_half1.7.second_ref, bf16[4,4,8,64,128]{4,3,2,1,0:T(8,128)(2,1)} %get-tuple-element.79.refs_0_), custom_call_target="tpu_custom_call", output_to_operand_aliasing={{0}: (2, {})} | custom-call | tf_op jit(solution)/shard_map/unpack/pallas_call | solution.py:77
  (79 shorter events, 1.4 us)
Async XLA Ops:
  0.0 1.0 copy-start.1
  1.2 13.7 %collective-permute-start = (bf16[4,8,32,128]{3,2,1,0:T(8,128)(2,1)S(1)}, bf16[4,8,32,128]{3,2,1,0:T(8,128)(2,1)S(1)}, u32[]{:S(2)}, u32[]{:S(2)}) collective-permute-start(bf16[4,8,32,128]{3,2,1,0:T(8,128)(2,1)S(1)} %get-tuple-element.45.refs_2_), channel_id=1, source_target_pairs={{0,1},{1,2},{2,3},{3,0},{4,5},{5,6},{6,7},{7,4},{8,9},{9,10},{10,1... | collective-permute-start | bytes 786440 | tf_op jit(solution)/shard_map/ppermute | solution.py:203
  4.3 15.0 %collective-permute-start.1 = (bf16[4,8,32,128]{3,2,1,0:T(8,128)(2,1)S(1)}, bf16[4,8,32,128]{3,2,1,0:T(8,128)(2,1)S(1)}, u32[]{:S(2)}, u32[]{:S(2)}) collective-permute-start(bf16[4,8,32,128]{3,2,1,0:T(8,128)(2,1)S(1)} %get-tuple-element.45.refs_2_), channel_id=1, source_target_pairs={{1,0},{2,1},{3,2},{0,3},{5,4},{6,5},{7,6},{4,7},{9,8},{10,9},{11,1... | collective-permute-start | bytes 786440 | tf_op jit(solution)/shard_map/ppermute | solution.py:203
  6.4 26.6 %collective-permute-start.6 = (bf16[4,8,32,128]{3,2,1,0:T(8,128)(2,1)S(1)}, bf16[4,8,32,128]{3,2,1,0:T(8,128)(2,1)S(1)}, u32[]{:S(2)}, u32[]{:S(2)}) collective-permute-start(bf16[4,8,32,128]{3,2,1,0:T(8,128)(2,1)S(1)} %get-tuple-element.49.refs_2_), channel_id=1, source_target_pairs={{0,1},{1,2},{2,3},{3,0},{4,5},{5,6},{6,7},{7,4},{8,9},{9,10},{10,1... | collective-permute-start | bytes 786440 | tf_op jit(solution)/shard_map/ppermute | solution.py:203
  6.4 26.6 %collective-permute-start.7 = (bf16[4,8,32,128]{3,2,1,0:T(8,128)(2,1)S(1)}, bf16[4,8,32,128]{3,2,1,0:T(8,128)(2,1)S(1)}, u32[]{:S(2)}, u32[]{:S(2)}) collective-permute-start(bf16[4,8,32,128]{3,2,1,0:T(8,128)(2,1)S(1)} %get-tuple-element.49.refs_2_), channel_id=1, source_target_pairs={{1,0},{2,1},{3,2},{0,3},{5,4},{6,5},{7,6},{4,7},{9,8},{10,9},{11,1... | collective-permute-start | bytes 786440 | tf_op jit(solution)/shard_map/ppermute | solution.py:203
  10.2 1.9 %copy-start = (bf16[4,1,8,64,768]{4,3,2,1,0:T(8,128)(2,1)S(1)}, bf16[4,1,8,64,768]{4,3,2,1,0:T(8,128)(2,1)}, u32[]{:S(2)}) copy-start(bf16[4,1,8,64,768]{4,3,2,1,0:T(8,128)(2,1)} %param.4) | copy-start | bytes 9437188
  12.1 2.7 %copy-start.2 = (s32[1,8,12]{2,1,0:T(8,128)S(1)}, s32[1,8,12]{2,1,0:T(8,128)}, u32[]{:S(2)}) copy-start(s32[1,8,12]{2,1,0:T(8,128)} %param.5) | copy-start | bytes 1156
  19.4 4.1 %collective-permute-start.2 = (bf16[3,8,32,128]{3,2,1,0:T(8,128)(2,1)S(1)}, bf16[3,8,32,128]{3,2,1,0:T(8,128)(2,1)S(1)}, u32[]{:S(2)}, u32[]{:S(2)}) collective-permute-start(bf16[3,8,32,128]{3,2,1,0:T(8,128)(2,1)S(1)} %pad_maximum_fusion.2.refs_6_), channel_id=1, source_target_pairs={{4,0},{8,4},{12,8},{16,12},{20,16},{24,20},{28,24},{0,28},{5,1},{9... | collective-permute-start | bytes 589832 | tf_op jit(solution)/shard_map/ppermute | solution.py:203
  19.5 8.2 %collective-permute-start.3 = (bf16[3,8,32,128]{3,2,1,0:T(8,128)(2,1)S(1)}, bf16[3,8,32,128]{3,2,1,0:T(8,128)(2,1)S(1)}, u32[]{:S(2)}, u32[]{:S(2)}) collective-permute-start(bf16[3,8,32,128]{3,2,1,0:T(8,128)(2,1)S(1)} %pad_maximum_fusion.3.refs_5_), channel_id=1, source_target_pairs={{0,4},{4,8},{8,12},{12,16},{16,20},{20,24},{24,28},{28,0},{1,5},{5... | collective-permute-start | bytes 589832 | tf_op jit(solution)/shard_map/ppermute | solution.py:203
  29.1 16.4 %collective-permute-start.4 = (bf16[4,8,32,128]{3,2,1,0:T(8,128)(2,1)S(1)}, bf16[4,8,32,128]{3,2,1,0:T(8,128)(2,1)S(1)}, u32[]{:S(2)}, u32[]{:S(2)}) collective-permute-start(bf16[4,8,32,128]{3,2,1,0:T(8,128)(2,1)S(1)} %edge_half0.4.refs_2_.first_ref), channel_id=1, source_target_pairs={{0,1},{1,2},{2,3},{3,0},{4,5},{5,6},{6,7},{7,4},{8,9},{9,10},{10,1... | collective-permute-start | bytes 786440 | tf_op jit(solution)/shard_map/ppermute | solution.py:203
  29.9 15.7 %collective-permute-start.5 = (bf16[4,8,32,128]{3,2,1,0:T(8,128)(2,1)S(1)}, bf16[4,8,32,128]{3,2,1,0:T(8,128)(2,1)S(1)}, u32[]{:S(2)}, u32[]{:S(2)}) collective-permute-start(bf16[4,8,32,128]{3,2,1,0:T(8,128)(2,1)S(1)} %edge_half0.4.refs_2_.first_ref), channel_id=1, source_target_pairs={{1,0},{2,1},{3,2},{0,3},{5,4},{6,5},{7,6},{4,7},{9,8},{10,9},{11,1... | collective-permute-start | bytes 786440 | tf_op jit(solution)/shard_map/ppermute | solution.py:203
  33.1 5.3 %collective-permute-start.8 = (bf16[3,8,32,128]{3,2,1,0:T(8,128)(2,1)S(1)}, bf16[3,8,32,128]{3,2,1,0:T(8,128)(2,1)S(1)}, u32[]{:S(2)}, u32[]{:S(2)}) collective-permute-start(bf16[3,8,32,128]{3,2,1,0:T(8,128)(2,1)S(1)} %pad_maximum_fusion.4.refs_6_), channel_id=1, source_target_pairs={{4,0},{8,4},{12,8},{16,12},{20,16},{24,20},{28,24},{0,28},{5,1},{9... | collective-permute-start | bytes 589832 | tf_op jit(solution)/shard_map/ppermute | solution.py:203
  33.2 7.0 %collective-permute-start.9 = (bf16[3,8,32,128]{3,2,1,0:T(8,128)(2,1)S(1)}, bf16[3,8,32,128]{3,2,1,0:T(8,128)(2,1)S(1)}, u32[]{:S(2)}, u32[]{:S(2)}) collective-permute-start(bf16[3,8,32,128]{3,2,1,0:T(8,128)(2,1)S(1)} %pad_maximum_fusion.5.refs_5_), channel_id=1, source_target_pairs={{0,4},{4,8},{8,12},{12,16},{16,20},{20,24},{24,28},{28,0},{1,5},{5... | collective-permute-start | bytes 589832 | tf_op jit(solution)/shard_map/ppermute | solution.py:203
  41.7 16.0 %collective-permute-start.14 = (bf16[4,8,32,128]{3,2,1,0:T(8,128)(2,1)S(1)}, bf16[4,8,32,128]{3,2,1,0:T(8,128)(2,1)S(1)}, u32[]{:S(2)}, u32[]{:S(2)}) collective-permute-start(bf16[4,8,32,128]{3,2,1,0:T(8,128)(2,1)S(1)} %edge_half1.4.second_ref.refs_2_), channel_id=1, source_target_pairs={{0,1},{1,2},{2,3},{3,0},{4,5},{5,6},{6,7},{7,4},{8,9},{9,10},{10,1... | collective-permute-start | bytes 786440 | tf_op jit(solution)/shard_map/ppermute | solution.py:203
  41.8 16.0 %collective-permute-start.15 = (bf16[4,8,32,128]{3,2,1,0:T(8,128)(2,1)S(1)}, bf16[4,8,32,128]{3,2,1,0:T(8,128)(2,1)S(1)}, u32[]{:S(2)}, u32[]{:S(2)}) collective-permute-start(bf16[4,8,32,128]{3,2,1,0:T(8,128)(2,1)S(1)} %edge_half1.4.second_ref.refs_2_), channel_id=1, source_target_pairs={{1,0},{2,1},{3,2},{0,3},{5,4},{6,5},{7,6},{4,7},{9,8},{10,9},{11,1... | collective-permute-start | bytes 786440 | tf_op jit(solution)/shard_map/ppermute | solution.py:203
  45.7 5.4 %collective-permute-start.10 = (bf16[3,8,32,128]{3,2,1,0:T(8,128)(2,1)S(1)}, bf16[3,8,32,128]{3,2,1,0:T(8,128)(2,1)S(1)}, u32[]{:S(2)}, u32[]{:S(2)}) collective-permute-start(bf16[3,8,32,128]{3,2,1,0:T(8,128)(2,1)S(1)} %pad_maximum_fusion.6.refs_6_), channel_id=1, source_target_pairs={{4,0},{8,4},{12,8},{16,12},{20,16},{24,20},{28,24},{0,28},{5,1},{9... | collective-permute-start | bytes 589832 | tf_op jit(solution)/shard_map/ppermute | solution.py:203
  46.1 6.2 %collective-permute-start.11 = (bf16[3,8,32,128]{3,2,1,0:T(8,128)(2,1)S(1)}, bf16[3,8,32,128]{3,2,1,0:T(8,128)(2,1)S(1)}, u32[]{:S(2)}, u32[]{:S(2)}) collective-permute-start(bf16[3,8,32,128]{3,2,1,0:T(8,128)(2,1)S(1)} %pad_maximum_fusion.7.refs_5_), channel_id=1, source_target_pairs={{0,4},{4,8},{8,12},{12,16},{16,20},{20,24},{24,28},{28,0},{1,5},{5... | collective-permute-start | bytes 589832 | tf_op jit(solution)/shard_map/ppermute | solution.py:203
  53.8 16.4 %collective-permute-start.12 = (bf16[4,8,32,128]{3,2,1,0:T(8,128)(2,1)S(1)}, bf16[4,8,32,128]{3,2,1,0:T(8,128)(2,1)S(1)}, u32[]{:S(2)}, u32[]{:S(2)}) collective-permute-start(bf16[4,8,32,128]{3,2,1,0:T(8,128)(2,1)S(1)} %edge_half0.5.refs_2_.first_ref), channel_id=1, source_target_pairs={{0,1},{1,2},{2,3},{3,0},{4,5},{5,6},{6,7},{7,4},{8,9},{9,10},{10,1... | collective-permute-start | bytes 786440 | tf_op jit(solution)/shard_map/ppermute | solution.py:203
  53.9 16.4 %collective-permute-start.13 = (bf16[4,8,32,128]{3,2,1,0:T(8,128)(2,1)S(1)}, bf16[4,8,32,128]{3,2,1,0:T(8,128)(2,1)S(1)}, u32[]{:S(2)}, u32[]{:S(2)}) collective-permute-start(bf16[4,8,32,128]{3,2,1,0:T(8,128)(2,1)S(1)} %edge_half0.5.refs_2_.first_ref), channel_id=1, source_target_pairs={{1,0},{2,1},{3,2},{0,3},{5,4},{6,5},{7,6},{4,7},{9,8},{10,9},{11,1... | collective-permute-start | bytes 786440 | tf_op jit(solution)/shard_map/ppermute | solution.py:203
  57.8 5.8 %collective-permute-start.16 = (bf16[3,8,32,128]{3,2,1,0:T(8,128)(2,1)S(1)}, bf16[3,8,32,128]{3,2,1,0:T(8,128)(2,1)S(1)}, u32[]{:S(2)}, u32[]{:S(2)}) collective-permute-start(bf16[3,8,32,128]{3,2,1,0:T(8,128)(2,1)S(1)} %pad_maximum_fusion.8.refs_6_), channel_id=1, source_target_pairs={{4,0},{8,4},{12,8},{16,12},{20,16},{24,20},{28,24},{0,28},{5,1},{9... | collective-permute-start | bytes 589832 | tf_op jit(solution)/shard_map/ppermute | solution.py:203
  58.8 6.0 %collective-permute-start.17 = (bf16[3,8,32,128]{3,2,1,0:T(8,128)(2,1)S(1)}, bf16[3,8,32,128]{3,2,1,0:T(8,128)(2,1)S(1)}, u32[]{:S(2)}, u32[]{:S(2)}) collective-permute-start(bf16[3,8,32,128]{3,2,1,0:T(8,128)(2,1)S(1)} %pad_maximum_fusion.9.refs_5_), channel_id=1, source_target_pairs={{0,4},{4,8},{8,12},{12,16},{16,20},{20,24},{24,28},{28,0},{1,5},{5... | collective-permute-start | bytes 589832 | tf_op jit(solution)/shard_map/ppermute | solution.py:203
  66.4 16.4 %collective-permute-start.22 = (bf16[4,8,32,128]{3,2,1,0:T(8,128)(2,1)S(1)}, bf16[4,8,32,128]{3,2,1,0:T(8,128)(2,1)S(1)}, u32[]{:S(2)}, u32[]{:S(2)}) collective-permute-start(bf16[4,8,32,128]{3,2,1,0:T(8,128)(2,1)S(1)} %edge_half1.5.second_ref.refs_2_), channel_id=1, source_target_pairs={{0,1},{1,2},{2,3},{3,0},{4,5},{5,6},{6,7},{7,4},{8,9},{9,10},{10,1... | collective-permute-start | bytes 786440 | tf_op jit(solution)/shard_map/ppermute | solution.py:203
  66.4 16.4 %collective-permute-start.23 = (bf16[4,8,32,128]{3,2,1,0:T(8,128)(2,1)S(1)}, bf16[4,8,32,128]{3,2,1,0:T(8,128)(2,1)S(1)}, u32[]{:S(2)}, u32[]{:S(2)}) collective-permute-start(bf16[4,8,32,128]{3,2,1,0:T(8,128)(2,1)S(1)} %edge_half1.5.second_ref.refs_2_), channel_id=1, source_target_pairs={{1,0},{2,1},{3,2},{0,3},{5,4},{6,5},{7,6},{4,7},{9,8},{10,9},{11,1... | collective-permute-start | bytes 786440 | tf_op jit(solution)/shard_map/ppermute | solution.py:203
  70.3 5.6 %collective-permute-start.18 = (bf16[3,8,32,128]{3,2,1,0:T(8,128)(2,1)S(1)}, bf16[3,8,32,128]{3,2,1,0:T(8,128)(2,1)S(1)}, u32[]{:S(2)}, u32[]{:S(2)}) collective-permute-start(bf16[3,8,32,128]{3,2,1,0:T(8,128)(2,1)S(1)} %pad_maximum_fusion.10.refs_6_), channel_id=1, source_target_pairs={{4,0},{8,4},{12,8},{16,12},{20,16},{24,20},{28,24},{0,28},{5,1},{9... | collective-permute-start | bytes 589832 | tf_op jit(solution)/shard_map/ppermute | solution.py:203
  71.4 6.0 %collective-permute-start.19 = (bf16[3,8,32,128]{3,2,1,0:T(8,128)(2,1)S(1)}, bf16[3,8,32,128]{3,2,1,0:T(8,128)(2,1)S(1)}, u32[]{:S(2)}, u32[]{:S(2)}) collective-permute-start(bf16[3,8,32,128]{3,2,1,0:T(8,128)(2,1)S(1)} %pad_maximum_fusion.11.refs_5_), channel_id=1, source_target_pairs={{0,4},{4,8},{8,12},{12,16},{16,20},{20,24},{24,28},{28,0},{1,5},{5... | collective-permute-start | bytes 589832 | tf_op jit(solution)/shard_map/ppermute | solution.py:203
  78.9 16.3 %collective-permute-start.20 = (bf16[4,8,32,128]{3,2,1,0:T(8,128)(2,1)S(1)}, bf16[4,8,32,128]{3,2,1,0:T(8,128)(2,1)S(1)}, u32[]{:S(2)}, u32[]{:S(2)}) collective-permute-start(bf16[4,8,32,128]{3,2,1,0:T(8,128)(2,1)S(1)} %edge_half0.6.refs_2_.first_ref), channel_id=1, source_target_pairs={{0,1},{1,2},{2,3},{3,0},{4,5},{5,6},{6,7},{7,4},{8,9},{9,10},{10,1... | collective-permute-start | bytes 786440 | tf_op jit(solution)/shard_map/ppermute | solution.py:203
  79.0 16.3 %collective-permute-start.21 = (bf16[4,8,32,128]{3,2,1,0:T(8,128)(2,1)S(1)}, bf16[4,8,32,128]{3,2,1,0:T(8,128)(2,1)S(1)}, u32[]{:S(2)}, u32[]{:S(2)}) collective-permute-start(bf16[4,8,32,128]{3,2,1,0:T(8,128)(2,1)S(1)} %edge_half0.6.refs_2_.first_ref), channel_id=1, source_target_pairs={{1,0},{2,1},{3,2},{0,3},{5,4},{6,5},{7,6},{4,7},{9,8},{10,9},{11,1... | collective-permute-start | bytes 786440 | tf_op jit(solution)/shard_map/ppermute | solution.py:203
  82.9 5.3 %collective-permute-start.24 = (bf16[3,8,32,128]{3,2,1,0:T(8,128)(2,1)S(1)}, bf16[3,8,32,128]{3,2,1,0:T(8,128)(2,1)S(1)}, u32[]{:S(2)}, u32[]{:S(2)}) collective-permute-start(bf16[3,8,32,128]{3,2,1,0:T(8,128)(2,1)S(1)} %pad_maximum_fusion.12.refs_6_), channel_id=1, source_target_pairs={{4,0},{8,4},{12,8},{16,12},{20,16},{24,20},{28,24},{0,28},{5,1},{9... | collective-permute-start | bytes 589832 | tf_op jit(solution)/shard_map/ppermute | solution.py:203
  83.8 6.0 %collective-permute-start.25 = (bf16[3,8,32,128]{3,2,1,0:T(8,128)(2,1)S(1)}, bf16[3,8,32,128]{3,2,1,0:T(8,128)(2,1)S(1)}, u32[]{:S(2)}, u32[]{:S(2)}) collective-permute-start(bf16[3,8,32,128]{3,2,1,0:T(8,128)(2,1)S(1)} %pad_maximum_fusion.13.refs_5_), channel_id=1, source_target_pairs={{0,4},{4,8},{8,12},{12,16},{16,20},{20,24},{24,28},{28,0},{1,5},{5... | collective-permute-start | bytes 589832 | tf_op jit(solution)/shard_map/ppermute | solution.py:203
  91.3 7.2 %collective-permute-start.28 = (bf16[2,8,32,128]{3,2,1,0:T(8,128)(2,1)S(1)}, bf16[2,8,32,128]{3,2,1,0:T(8,128)(2,1)S(1)}, u32[]{:S(2)}, u32[]{:S(2)}) collective-permute-start(bf16[2,8,32,128]{3,2,1,0:T(8,128)(2,1)S(1)} %pad_maximum_fusion.18), channel_id=1, source_target_pairs={{0,1},{1,2},{2,3},{3,0},{4,5},{5,6},{6,7},{7,4},{8,9},{9,10},{10,1... | collective-permute-start | bytes 393224 | tf_op jit(solution)/shard_map/ppermute | solution.py:203
  91.4 11.0 %collective-permute-start.29 = (bf16[2,8,32,128]{3,2,1,0:T(8,128)(2,1)S(1)}, bf16[2,8,32,128]{3,2,1,0:T(8,128)(2,1)S(1)}, u32[]{:S(2)}, u32[]{:S(2)}) collective-permute-start(bf16[2,8,32,128]{3,2,1,0:T(8,128)(2,1)S(1)} %pad_maximum_fusion.18), channel_id=1, source_target_pairs={{1,0},{2,1},{3,2},{0,3},{5,4},{6,5},{7,6},{4,7},{9,8},{10,9},{11,1... | collective-permute-start | bytes 393224 | tf_op jit(solution)/shard_map/ppermute | solution.py:203
  95.3 9.3 %collective-permute-start.26 = (bf16[3,8,32,128]{3,2,1,0:T(8,128)(2,1)S(1)}, bf16[3,8,32,128]{3,2,1,0:T(8,128)(2,1)S(1)}, u32[]{:S(2)}, u32[]{:S(2)}) collective-permute-start(bf16[3,8,32,128]{3,2,1,0:T(8,128)(2,1)S(1)} %pad_maximum_fusion.14.refs_6_), channel_id=1, source_target_pairs={{4,0},{8,4},{12,8},{16,12},{20,16},{24,20},{28,24},{0,28},{5,1},{9... | collective-permute-start | bytes 589832 | tf_op jit(solution)/shard_map/ppermute | solution.py:203
  96.0 8.7 %collective-permute-start.27 = (bf16[3,8,32,128]{3,2,1,0:T(8,128)(2,1)S(1)}, bf16[3,8,32,128]{3,2,1,0:T(8,128)(2,1)S(1)}, u32[]{:S(2)}, u32[]{:S(2)}) collective-permute-start(bf16[3,8,32,128]{3,2,1,0:T(8,128)(2,1)S(1)} %pad_maximum_fusion.15.refs_5_), channel_id=1, source_target_pairs={{0,4},{4,8},{8,12},{12,16},{16,20},{20,24},{24,28},{28,0},{1,5},{5... | collective-permute-start | bytes 589832 | tf_op jit(solution)/shard_map/ppermute | solution.py:203
  98.5 8.2 %collective-permute-start.30 = (bf16[2,8,32,128]{3,2,1,0:T(8,128)(2,1)S(1)}, bf16[2,8,32,128]{3,2,1,0:T(8,128)(2,1)S(1)}, u32[]{:S(2)}, u32[]{:S(2)}) collective-permute-start(bf16[2,8,32,128]{3,2,1,0:T(8,128)(2,1)S(1)} %slice.222), channel_id=1, source_target_pairs={{0,1},{1,2},{2,3},{3,0},{4,5},{5,6},{6,7},{7,4},{8,9},{9,10},{10,1... | collective-permute-start | bytes 393224 | tf_op jit(solution)/shard_map/ppermute | solution.py:203
  98.5 8.2 %collective-permute-start.31 = (bf16[2,8,32,128]{3,2,1,0:T(8,128)(2,1)S(1)}, bf16[2,8,32,128]{3,2,1,0:T(8,128)(2,1)S(1)}, u32[]{:S(2)}, u32[]{:S(2)}) collective-permute-start(bf16[2,8,32,128]{3,2,1,0:T(8,128)(2,1)S(1)} %slice.222), channel_id=1, source_target_pairs={{1,0},{2,1},{3,2},{0,3},{5,4},{6,5},{7,6},{4,7},{9,8},{10,9},{11,1... | collective-permute-start | bytes 393224 | tf_op jit(solution)/shard_map/ppermute | solution.py:203
  102.4 5.9 %collective-permute-start.32 = (bf16[3,8,32,128]{3,2,1,0:T(8,128)(2,1)S(1)}, bf16[3,8,32,128]{3,2,1,0:T(8,128)(2,1)S(1)}, u32[]{:S(2)}, u32[]{:S(2)}) collective-permute-start(bf16[3,8,32,128]{3,2,1,0:T(8,128)(2,1)S(1)} %pad_maximum_fusion.16.refs_6_), channel_id=1, source_target_pairs={{4,0},{8,4},{12,8},{16,12},{20,16},{24,20},{28,24},{0,28},{5,1},{9... | collective-permute-start | bytes 589832 | tf_op jit(solution)/shard_map/ppermute | solution.py:203
  104.6 6.0 %collective-permute-start.33 = (bf16[3,8,32,128]{3,2,1,0:T(8,128)(2,1)S(1)}, bf16[3,8,32,128]{3,2,1,0:T(8,128)(2,1)S(1)}, u32[]{:S(2)}, u32[]{:S(2)}) collective-permute-start(bf16[3,8,32,128]{3,2,1,0:T(8,128)(2,1)S(1)} %pad_maximum_fusion.17.refs_5_), channel_id=1, source_target_pairs={{0,4},{4,8},{8,12},{12,16},{16,20},{20,24},{24,28},{28,0},{1,5},{5... | collective-permute-start | bytes 589832 | tf_op jit(solution)/shard_map/ppermute | solution.py:203

commit v13 on v12

--- a/solution.py
+++ b/solution.py
@@ -97,8 +97,8 @@
     return jnp.stack([part[0] for part in trio]), jnp.stack([part[-1] for part in trio])
 
 
-def from_neighbours(value):
-    return value, shift(value, "azim", True), shift(value, "azim", False)
+def from_neighbours(value, half):
+    return value, *(shift(value, "azim", up) for up in (half == 0, half > 0))
 
 
 def joined(value, outer, inner, after):
@@ -246,12 +246,16 @@
     start = start_vector.reshape(columns, faces, width, lanes)
     blocks = halves_of_rows(trace_blocks.reshape(columns, faces, width, -1))
     codes = neighbour.reshape(faces, -1)
-    table = (((codes // faces) % 3) * (columns + 2) + codes // (3 * faces)) * faces + codes % faces
+    around_shift = (codes // faces) % 3
+    tables = [
+        (place * (columns + 2) + codes // (3 * faces)) * faces + codes % faces
+        for place in (around_shift, 2 - around_shift)
+    ]
     every = tuple(range(columns))
     current = list(pack(start))
     basis = None
     latest = current[0]
-    pieces = [from_neighbours(value) for value in current]
+    pieces = [from_neighbours(value, h) for h, value in enumerate(current)]
     outer = None
     for index in range(STEPS):
         previous = tuple(current)
@@ -260,19 +264,19 @@
                 to_low, to_high = edges(*pieces[h], latest)
             else:
                 own_inner, _ = lax.optimization_barrier((current[h][1:-1], middle))
-                inner = from_neighbours(own_inner)
+                inner = from_neighbours(own_inner, h)
                 to_low, to_high = edges(*outer, middle)
                 pieces[h] = joined(current[h], outer, inner, latest)
             stream = (shift(to_low, "stream", False), shift(to_high, "stream", True))
-            middle = part(h, table, blocks, pieces[h], (to_high, to_low))
+            middle = part(h, tables[h], blocks, pieces[h], (to_high, to_low))
             after = middle
             if h == 0 and index > 0:
                 basis, after = unpack(index - 1, every, *previous, basis, middle)
-            current[h] = latest = part(h, table, blocks, pieces[h], (*stream, middle, after))
+            current[h] = latest = part(h, tables[h], blocks, pieces[h], (*stream, middle, after))
             if index == STEPS - 2 and h == HALVES - 1:
-                outer = from_neighbours(jnp.stack([current[h][0], current[h][-1]]))
+                outer = from_neighbours(jnp.stack([current[h][0], current[h][-1]]), h)
             elif index < STEPS - 1:
-                pieces[h] = from_neighbours(current[h])
+                pieces[h] = from_neighbours(current[h], h)
     basis, _ = unpack(STEPS - 1, every, *current, basis, None)
     return basis.reshape(STEPS, columns, around, faces, width, lanes)
 

time: 114 us -> 117 us (1.026)
  waiting for transfers between devices: 34.7 us -> 40.7 us
  starting transfers between devices: 43.8 us -> 41.5 us
    ppermute x34, waiting for transfers between devices: 34.7 us -> 40.7 us  [shift(): return lax.ppermute(value, axis, pairs)]
    ppermute x34, starting transfers between devices: 43.8 us -> 41.5 us  [shift(): return lax.ppermute(value, axis, pairs)]
  transfers between devices with their start and end apart: 34 -> 34, of which waited for: 15 -> 16; matrix products, arithmetic and copies ran while one was open for 1% -> 1% of each run, Pallas kernels for 24% -> 24%
where the time goes in v13:
time: 117 us
  starting transfers between devices  41.5 us (35%)
  waiting for transfers between devices  40.7 us (35%)
  Pallas kernels  30.7 us (26%)
  local copies, waits for them, and re-layouts  3.23 us (3%)
    ppermute x34, starting transfers between devices, shift(): return lax.ppermute(value, axis, pairs)  41.5 us
    ppermute x34, waiting for transfers between devices, shift(): return lax.ppermute(value, axis, pairs)  40.7 us
    pallas_call x16, Pallas kernels, part(): pl.pallas_call(functools.partial(part_kernel, half), in_specs=in_specs, o...  23.6 us
    pallas_call x4, Pallas kernels, unpack(): pl.pallas_call(functools.partial(unpack_kernel, index, chosen, skipped),...  4.26 us
    unnamed x6, local copies, waits for them, and re-layouts  2.93 us
    pallas_call x1, Pallas kernels, halves_of_rows(): pl.pallas_call(halves_kernel, in_specs=[VMEM], out_specs=VMEM, out_shape=...  2.72 us
  transfers between devices with their start and end apart: 34, of which 16 were waited for; matrix products, arithmetic and copies ran while one was open for 1% of the time, Pallas kernels for 24%

profile of v13, /device:TPU:0, one launch (start us, length us, event | category | flops | bytes accessed | tf_op | source)
XLA Modules:
  0.0 117.2 jit_solution(1328691233803780433)
XLA Ops:
  0.0 1.0 copy-done.1
  1.0 0.2 pack.1
  1.2 3.1 %collective-permute-start = (bf16[4,8,32,128]{3,2,1,0:T(8,128)(2,1)S(1)}, bf16[4,8,32,128]{3,2,1,0:T(8,128)(2,1)S(1)}, u32[]{:S(2)}, u32[]{:S(2)}) collective-permute-start(bf16[4,8,32,128]{3,2,1,0:T(8,128)(2,1)S(1)} %get-tuple-element.45.refs_2_), channel_id=1, source_target_pairs={{0,1},{1,2},{2,3},{3,0},{4,5},{5,6},{6,7},{7,4},{8,9},{9,10},{10,1... | collective-permute-start | bytes 786440 | tf_op jit(solution)/shard_map/ppermute | solution.py:203
  4.3 2.1 %collective-permute-start.1 = (bf16[4,8,32,128]{3,2,1,0:T(8,128)(2,1)S(1)}, bf16[4,8,32,128]{3,2,1,0:T(8,128)(2,1)S(1)}, u32[]{:S(2)}, u32[]{:S(2)}) collective-permute-start(bf16[4,8,32,128]{3,2,1,0:T(8,128)(2,1)S(1)} %get-tuple-element.45.refs_2_), channel_id=1, source_target_pairs={{1,0},{2,1},{3,2},{0,3},{5,4},{6,5},{7,6},{4,7},{9,8},{10,9},{11,1... | collective-permute-start | bytes 786440 | tf_op jit(solution)/shard_map/ppermute | solution.py:203
  6.4 2.0 %collective-permute-start.6 = (bf16[4,8,32,128]{3,2,1,0:T(8,128)(2,1)S(1)}, bf16[4,8,32,128]{3,2,1,0:T(8,128)(2,1)S(1)}, u32[]{:S(2)}, u32[]{:S(2)}) collective-permute-start(bf16[4,8,32,128]{3,2,1,0:T(8,128)(2,1)S(1)} %get-tuple-element.49.refs_2_), channel_id=1, source_target_pairs={{1,0},{2,1},{3,2},{0,3},{5,4},{6,5},{7,6},{4,7},{9,8},{10,9},{11,1... | collective-permute-start | bytes 786440 | tf_op jit(solution)/shard_map/ppermute | solution.py:203
  8.3 0.1 collective-permute-start.7
  8.4 1.9 %copy-done = bf16[4,1,8,64,768]{4,3,2,1,0:T(8,128)(2,1)S(1)} copy-done((bf16[4,1,8,64,768]{4,3,2,1,0:T(8,128)(2,1)S(1)}, bf16[4,1,8,64,768]{4,3,2,1,0:T(8,128)(2,1)}, u32[]{:S(2)}) %copy-start) | copy-done | bytes 3145752
  10.3 2.7 %halves_of_rows.1.refs_1_ = bf16[4,8,64,768]{3,2,1,0:T(8,128)(2,1)S(1)} custom-call(bf16[4,8,64,768]{3,2,1,0:T(8,128)(2,1)S(1)} %bitcast.53), custom_call_target="tpu_custom_call" | custom-call | tf_op jit(solution)/shard_map/halves_of_rows/pallas_call | solution.py:234
  13.1 0.4 collective-permute-done.refs_3_
  13.5 4.9 %collective-permute-done.1.refs_4_ = bf16[4,8,32,128]{3,2,1,0:T(8,128)(2,1)S(1)} collective-permute-done((bf16[4,8,32,128]{3,2,1,0:T(8,128)(2,1)S(1)}, bf16[4,8,32,128]{3,2,1,0:T(8,128)(2,1)S(1)}, u32[]{:S(2)}, u32[]{:S(2)}) %collective-permute-start.1) | collective-permute-done | bytes 262176 | tf_op jit(solution)/shard_map/ppermute | solution.py:203
  18.5 0.8 collective-permute-start.2
  19.3 1.5 %inner_half0.4.refs_7_.refs_8_ = bf16[2,8,32,128]{3,2,1,0:T(8,128)(2,1)S(1)} custom-call(s32[8,12]{1,0:T(8,128)S(1)} %get-tuple-element.136.refs_0_, bf16[4,8,64,768]{3,2,1,0:T(8,128)(2,1)S(1)} %halves_of_rows.1.refs_1_, bf16[4,8,32,128]{3,2,1,0:T(8,128)(2,1)S(1)} %get-tuple-element.45.refs_2_, bf16[4,8,32,128]{3,2,1,0:T(8,128)(2,1)S(1)} %collective-permute-done.refs_3_, ...), custom_call_target="tpu_custom_call" | custom-call | flops 20132659200 | bytes 157286400 | tf_op jit(solution)/shard_map/inner_half0/pallas_call | solution.py:178
  20.8 3.4 %collective-permute-done.2.refs_5_ = bf16[3,8,32,128]{3,2,1,0:T(8,128)(2,1)S(1)} collective-permute-done((bf16[3,8,32,128]{3,2,1,0:T(8,128)(2,1)S(1)}, bf16[3,8,32,128]{3,2,1,0:T(8,128)(2,1)S(1)}, u32[]{:S(2)}, u32[]{:S(2)}) %collective-permute-start.2) | collective-permute-done | bytes 196640 | tf_op jit(solution)/shard_map/ppermute | solution.py:203
  24.3 2.5 %collective-permute-done.3.refs_6_ = bf16[3,8,32,128]{3,2,1,0:T(8,128)(2,1)S(1)} collective-permute-done((bf16[3,8,32,128]{3,2,1,0:T(8,128)(2,1)S(1)}, bf16[3,8,32,128]{3,2,1,0:T(8,128)(2,1)S(1)}, u32[]{:S(2)}, u32[]{:S(2)}) %collective-permute-start.3) | collective-permute-done | bytes 196640 | tf_op jit(solution)/shard_map/ppermute | solution.py:203
  26.7 1.5 %edge_half0.4.refs_2_.first_ref = bf16[4,8,32,128]{3,2,1,0:T(8,128)(2,1)S(1)} custom-call(s32[8,12]{1,0:T(8,128)S(1)} %get-tuple-element.136.refs_0_, bf16[4,8,64,768]{3,2,1,0:T(8,128)(2,1)S(1)} %halves_of_rows.1.refs_1_, bf16[4,8,32,128]{3,2,1,0:T(8,128)(2,1)S(1)} %get-tuple-element.45.refs_2_, bf16[4,8,32,128]{3,2,1,0:T(8,128)(2,1)S(1)} %collective-permute-done.refs_3_, ...), custom_call_target="tpu_custom_call" | custom-call | flops 20132659200 | bytes 157286400 | tf_op jit(solution)/shard_map/edge_half0/pallas_call | solution.py:178
  28.2 5.0 %collective-permute-start.4 = (bf16[4,8,32,128]{3,2,1,0:T(8,128)(2,1)S(1)}, bf16[4,8,32,128]{3,2,1,0:T(8,128)(2,1)S(1)}, u32[]{:S(2)}, u32[]{:S(2)}) collective-permute-start(bf16[4,8,32,128]{3,2,1,0:T(8,128)(2,1)S(1)} %edge_half0.4.refs_2_.first_ref), channel_id=1, source_target_pairs={{0,1},{1,2},{2,3},{3,0},{4,5},{5,6},{6,7},{7,4},{8,9},{9,10},{10,1... | collective-permute-start | bytes 786440 | tf_op jit(solution)/shard_map/ppermute | solution.py:203
  33.2 3.4 %collective-permute-start.5 = (bf16[4,8,32,128]{3,2,1,0:T(8,128)(2,1)S(1)}, bf16[4,8,32,128]{3,2,1,0:T(8,128)(2,1)S(1)}, u32[]{:S(2)}, u32[]{:S(2)}) collective-permute-start(bf16[4,8,32,128]{3,2,1,0:T(8,128)(2,1)S(1)} %edge_half0.4.refs_2_.first_ref), channel_id=1, source_target_pairs={{1,0},{2,1},{3,2},{0,3},{5,4},{6,5},{7,6},{4,7},{9,8},{10,9},{11,1... | collective-permute-start | bytes 786440 | tf_op jit(solution)/shard_map/ppermute | solution.py:203
  36.9 0.5 collective-permute-start.9
  37.4 1.5 %inner_half1.4.refs_7_.refs_8_ = bf16[2,8,32,128]{3,2,1,0:T(8,128)(2,1)S(1)} custom-call(s32[8,12]{1,0:T(8,128)S(1)} %get-tuple-element.135.refs_0_, bf16[4,8,64,768]{3,2,1,0:T(8,128)(2,1)S(1)} %halves_of_rows.1.refs_1_, bf16[4,8,32,128]{3,2,1,0:T(8,128)(2,1)S(1)} %get-tuple-element.49.refs_2_, bf16[4,8,32,128]{3,2,1,0:T(8,128)(2,1)S(1)} %collective-permute-done.6.refs_3_, ...), custom_call_target="tpu_custom_call" | custom-call | flops 20132659200 | bytes 157286400 | tf_op jit(solution)/shard_map/inner_half1/pallas_call | solution.py:178
  38.9 3.1 %collective-permute-done.8.refs_5_ = bf16[3,8,32,128]{3,2,1,0:T(8,128)(2,1)S(1)} collective-permute-done((bf16[3,8,32,128]{3,2,1,0:T(8,128)(2,1)S(1)}, bf16[3,8,32,128]{3,2,1,0:T(8,128)(2,1)S(1)}, u32[]{:S(2)}, u32[]{:S(2)}) %collective-permute-start.8) | collective-permute-done | bytes 196640 | tf_op jit(solution)/shard_map/ppermute | solution.py:203
  42.0 2.0 %collective-permute-done.9.refs_6_ = bf16[3,8,32,128]{3,2,1,0:T(8,128)(2,1)S(1)} collective-permute-done((bf16[3,8,32,128]{3,2,1,0:T(8,128)(2,1)S(1)}, bf16[3,8,32,128]{3,2,1,0:T(8,128)(2,1)S(1)}, u32[]{:S(2)}, u32[]{:S(2)}) %collective-permute-start.9) | collective-permute-done | bytes 196640 | tf_op jit(solution)/shard_map/ppermute | solution.py:203
  44.0 1.5 %edge_half1.4.second_ref.refs_2_ = bf16[4,8,32,128]{3,2,1,0:T(8,128)(2,1)S(1)} custom-call(s32[8,12]{1,0:T(8,128)S(1)} %get-tuple-element.135.refs_0_, bf16[4,8,64,768]{3,2,1,0:T(8,128)(2,1)S(1)} %halves_of_rows.1.refs_1_, bf16[4,8,32,128]{3,2,1,0:T(8,128)(2,1)S(1)} %get-tuple-element.49.refs_2_, bf16[4,8,32,128]{3,2,1,0:T(8,128)(2,1)S(1)} %collective-permute-done.6.refs_3_, ...), custom_call_target="tpu_custom_call" | custom-call | flops 20132659200 | bytes 157286400 | tf_op jit(solution)/shard_map/edge_half1/pallas_call | solution.py:178
  45.5 1.7 %collective-permute-start.14 = (bf16[4,8,32,128]{3,2,1,0:T(8,128)(2,1)S(1)}, bf16[4,8,32,128]{3,2,1,0:T(8,128)(2,1)S(1)}, u32[]{:S(2)}, u32[]{:S(2)}) collective-permute-start(bf16[4,8,32,128]{3,2,1,0:T(8,128)(2,1)S(1)} %edge_half1.4.second_ref.refs_2_), channel_id=1, source_target_pairs={{1,0},{2,1},{3,2},{0,3},{5,4},{6,5},{7,6},{4,7},{9,8},{10,9},{11,1... | collective-permute-start | bytes 786440 | tf_op jit(solution)/shard_map/ppermute | solution.py:203
  47.2 0.3 collective-permute-start.15
  47.7 0.9 collective-permute-start.10
  48.6 1.5 %inner_half0.5.refs_0_.refs_7_ = bf16[2,8,32,128]{3,2,1,0:T(8,128)(2,1)S(1)} custom-call(s32[8,12]{1,0:T(8,128)S(1)} %get-tuple-element.136.refs_0_, bf16[4,8,64,768]{3,2,1,0:T(8,128)(2,1)S(1)} %halves_of_rows.1.refs_1_, bf16[4,8,32,128]{3,2,1,0:T(8,128)(2,1)S(1)} %edge_half0.4.refs_2_.first_ref, bf16[4,8,32,128]{3,2,1,0:T(8,128)(2,1)S(1)} %collective-permute-done.4.refs_3_, ...), custom_call_target="tpu_custom_call" | custom-call | flops 20132659200 | bytes 157286400 | tf_op jit(solution)/shard_map/inner_half0/pallas_call | solution.py:178
  50.1 0.9 unpack.4
  51.0 1.9 %collective-permute-done.10.refs_5_ = bf16[3,8,32,128]{3,2,1,0:T(8,128)(2,1)S(1)} collective-permute-done((bf16[3,8,32,128]{3,2,1,0:T(8,128)(2,1)S(1)}, bf16[3,8,32,128]{3,2,1,0:T(8,128)(2,1)S(1)}, u32[]{:S(2)}, u32[]{:S(2)}) %collective-permute-start.10) | collective-permute-done | bytes 196640 | tf_op jit(solution)/shard_map/ppermute | solution.py:203
  52.9 1.9 %collective-permute-done.11.refs_6_ = bf16[3,8,32,128]{3,2,1,0:T(8,128)(2,1)S(1)} collective-permute-done((bf16[3,8,32,128]{3,2,1,0:T(8,128)(2,1)S(1)}, bf16[3,8,32,128]{3,2,1,0:T(8,128)(2,1)S(1)}, u32[]{:S(2)}, u32[]{:S(2)}) %collective-permute-start.11) | collective-permute-done | bytes 196640 | tf_op jit(solution)/shard_map/ppermute | solution.py:203
  54.9 1.5 %edge_half0.5.refs_2_.first_ref = bf16[4,8,32,128]{3,2,1,0:T(8,128)(2,1)S(1)} custom-call(s32[8,12]{1,0:T(8,128)S(1)} %get-tuple-element.136.refs_0_, bf16[4,8,64,768]{3,2,1,0:T(8,128)(2,1)S(1)} %halves_of_rows.1.refs_1_, bf16[4,8,32,128]{3,2,1,0:T(8,128)(2,1)S(1)} %edge_half0.4.refs_2_.first_ref, ...), custom_call_target="tpu_custom_call" | custom-call | flops 20132659200 | bytes 157286400 | tf_op jit(solution)/shard_map/edge_half0/pallas_call | solution.py:178
  56.4 2.0 %collective-permute-start.12 = (bf16[4,8,32,128]{3,2,1,0:T(8,128)(2,1)S(1)}, bf16[4,8,32,128]{3,2,1,0:T(8,128)(2,1)S(1)}, u32[]{:S(2)}, u32[]{:S(2)}) collective-permute-start(bf16[4,8,32,128]{3,2,1,0:T(8,128)(2,1)S(1)} %edge_half0.5.refs_2_.first_ref), channel_id=1, source_target_pairs={{0,1},{1,2},{2,3},{3,0},{4,5},{5,6},{6,7},{7,4},{8,9},{9,10},{10,1... | collective-permute-start | bytes 786440 | tf_op jit(solution)/shard_map/ppermute | solution.py:203
  58.4 1.8 %collective-permute-start.13 = (bf16[4,8,32,128]{3,2,1,0:T(8,128)(2,1)S(1)}, bf16[4,8,32,128]{3,2,1,0:T(8,128)(2,1)S(1)}, u32[]{:S(2)}, u32[]{:S(2)}) collective-permute-start(bf16[4,8,32,128]{3,2,1,0:T(8,128)(2,1)S(1)} %edge_half0.5.refs_2_.first_ref), channel_id=1, source_target_pairs={{1,0},{2,1},{3,2},{0,3},{5,4},{6,5},{7,6},{4,7},{9,8},{10,9},{11,1... | collective-permute-start | bytes 786440 | tf_op jit(solution)/shard_map/ppermute | solution.py:203
  60.3 0.7 collective-permute-start.16
  61.1 1.5 %inner_half1.5.refs_7_.refs_8_ = bf16[2,8,32,128]{3,2,1,0:T(8,128)(2,1)S(1)} custom-call(s32[8,12]{1,0:T(8,128)S(1)} %get-tuple-element.135.refs_0_, bf16[4,8,64,768]{3,2,1,0:T(8,128)(2,1)S(1)} %halves_of_rows.1.refs_1_, bf16[4,8,32,128]{3,2,1,0:T(8,128)(2,1)S(1)} %edge_half1.4.second_ref.refs_2_, ...), custom_call_target="tpu_custom_call" | custom-call | flops 20132659200 | bytes 157286400 | tf_op jit(solution)/shard_map/inner_half1/pallas_call | solution.py:178
  62.6 3.0 %collective-permute-done.16.refs_5_ = bf16[3,8,32,128]{3,2,1,0:T(8,128)(2,1)S(1)} collective-permute-done((bf16[3,8,32,128]{3,2,1,0:T(8,128)(2,1)S(1)}, bf16[3,8,32,128]{3,2,1,0:T(8,128)(2,1)S(1)}, u32[]{:S(2)}, u32[]{:S(2)}) %collective-permute-start.16) | collective-permute-done | bytes 196640 | tf_op jit(solution)/shard_map/ppermute | solution.py:203
  65.6 5.7 %collective-permute-done.17.refs_6_ = bf16[3,8,32,128]{3,2,1,0:T(8,128)(2,1)S(1)} collective-permute-done((bf16[3,8,32,128]{3,2,1,0:T(8,128)(2,1)S(1)}, bf16[3,8,32,128]{3,2,1,0:T(8,128)(2,1)S(1)}, u32[]{:S(2)}, u32[]{:S(2)}) %collective-permute-start.17) | collective-permute-done | bytes 196640 | tf_op jit(solution)/shard_map/ppermute | solution.py:203
  71.3 1.5 %edge_half1.5.second_ref.refs_2_ = bf16[4,8,32,128]{3,2,1,0:T(8,128)(2,1)S(1)} custom-call(s32[8,12]{1,0:T(8,128)S(1)} %get-tuple-element.135.refs_0_, bf16[4,8,64,768]{3,2,1,0:T(8,128)(2,1)S(1)} %halves_of_rows.1.refs_1_, bf16[4,8,32,128]{3,2,1,0:T(8,128)(2,1)S(1)} %edge_half1.4.second_ref.refs_2_, ...), custom_call_target="tpu_custom_call" | custom-call | flops 20132659200 | bytes 157286400 | tf_op jit(solution)/shard_map/edge_half1/pallas_call | solution.py:178
  72.8 2.0 %collective-permute-start.22 = (bf16[4,8,32,128]{3,2,1,0:T(8,128)(2,1)S(1)}, bf16[4,8,32,128]{3,2,1,0:T(8,128)(2,1)S(1)}, u32[]{:S(2)}, u32[]{:S(2)}) collective-permute-start(bf16[4,8,32,128]{3,2,1,0:T(8,128)(2,1)S(1)} %edge_half1.5.second_ref.refs_2_), channel_id=1, source_target_pairs={{1,0},{2,1},{3,2},{0,3},{5,4},{6,5},{7,6},{4,7},{9,8},{10,9},{11,1... | collective-permute-start | bytes 786440 | tf_op jit(solution)/shard_map/ppermute | solution.py:203
  75.1 0.5 collective-permute-start.19
  75.6 1.5 %inner_half0.6.refs_1_.refs_7_ = bf16[2,8,32,128]{3,2,1,0:T(8,128)(2,1)S(1)} custom-call(s32[8,12]{1,0:T(8,128)S(1)} %get-tuple-element.136.refs_0_, bf16[4,8,64,768]{3,2,1,0:T(8,128)(2,1)S(1)} %halves_of_rows.1.refs_1_, bf16[4,8,32,128]{3,2,1,0:T(8,128)(2,1)S(1)} %edge_half0.5.refs_2_.first_ref, ...), custom_call_target="tpu_custom_call" | custom-call | flops 20132659200 | bytes 157286400 | tf_op jit(solution)/shard_map/inner_half0/pallas_call | solution.py:178
  77.1 0.9 unpack.5
  78.0 2.2 %collective-permute-done.18.refs_5_ = bf16[3,8,32,128]{3,2,1,0:T(8,128)(2,1)S(1)} collective-permute-done((bf16[3,8,32,128]{3,2,1,0:T(8,128)(2,1)S(1)}, bf16[3,8,32,128]{3,2,1,0:T(8,128)(2,1)S(1)}, u32[]{:S(2)}, u32[]{:S(2)}) %collective-permute-start.18) | collective-permute-done | bytes 196640 | tf_op jit(solution)/shard_map/ppermute | solution.py:203
  80.2 2.1 %collective-permute-done.19.refs_6_ = bf16[3,8,32,128]{3,2,1,0:T(8,128)(2,1)S(1)} collective-permute-done((bf16[3,8,32,128]{3,2,1,0:T(8,128)(2,1)S(1)}, bf16[3,8,32,128]{3,2,1,0:T(8,128)(2,1)S(1)}, u32[]{:S(2)}, u32[]{:S(2)}) %collective-permute-start.19) | collective-permute-done | bytes 196640 | tf_op jit(solution)/shard_map/ppermute | solution.py:203
  82.3 1.5 %edge_half0.6.refs_2_.first_ref = bf16[4,8,32,128]{3,2,1,0:T(8,128)(2,1)S(1)} custom-call(s32[8,12]{1,0:T(8,128)S(1)} %get-tuple-element.136.refs_0_, bf16[4,8,64,768]{3,2,1,0:T(8,128)(2,1)S(1)} %halves_of_rows.1.refs_1_, bf16[4,8,32,128]{3,2,1,0:T(8,128)(2,1)S(1)} %edge_half0.5.refs_2_.first_ref, ...), custom_call_target="tpu_custom_call" | custom-call | flops 20132659200 | bytes 157286400 | tf_op jit(solution)/shard_map/edge_half0/pallas_call | solution.py:178
  83.8 0.8 collective-permute-start.20
  84.6 3.1 %collective-permute-start.21 = (bf16[4,8,32,128]{3,2,1,0:T(8,128)(2,1)S(1)}, bf16[4,8,32,128]{3,2,1,0:T(8,128)(2,1)S(1)}, u32[]{:S(2)}, u32[]{:S(2)}) collective-permute-start(bf16[4,8,32,128]{3,2,1,0:T(8,128)(2,1)S(1)} %edge_half0.6.refs_2_.first_ref), channel_id=1, source_target_pairs={{1,0},{2,1},{3,2},{0,3},{5,4},{6,5},{7,6},{4,7},{9,8},{10,9},{11,1... | collective-permute-start | bytes 786440 | tf_op jit(solution)/shard_map/ppermute | solution.py:203
  87.8 0.8 collective-permute-start.24
  88.6 1.5 %inner_half1.6.refs_7_.refs_8_ = bf16[2,8,32,128]{3,2,1,0:T(8,128)(2,1)S(1)} custom-call(s32[8,12]{1,0:T(8,128)S(1)} %get-tuple-element.135.refs_0_, bf16[4,8,64,768]{3,2,1,0:T(8,128)(2,1)S(1)} %halves_of_rows.1.refs_1_, bf16[4,8,32,128]{3,2,1,0:T(8,128)(2,1)S(1)} %edge_half1.5.second_ref.refs_2_, ...), custom_call_target="tpu_custom_call" | custom-call | flops 20132659200 | bytes 157286400 | tf_op jit(solution)/shard_map/inner_half1/pallas_call | solution.py:178
  90.1 2.9 %collective-permute-done.24.refs_5_ = bf16[3,8,32,128]{3,2,1,0:T(8,128)(2,1)S(1)} collective-permute-done((bf16[3,8,32,128]{3,2,1,0:T(8,128)(2,1)S(1)}, bf16[3,8,32,128]{3,2,1,0:T(8,128)(2,1)S(1)}, u32[]{:S(2)}, u32[]{:S(2)}) %collective-permute-start.24) | collective-permute-done | bytes 196640 | tf_op jit(solution)/shard_map/ppermute | solution.py:203
  93.0 1.6 %collective-permute-done.25.refs_6_ = bf16[3,8,32,128]{3,2,1,0:T(8,128)(2,1)S(1)} collective-permute-done((bf16[3,8,32,128]{3,2,1,0:T(8,128)(2,1)S(1)}, bf16[3,8,32,128]{3,2,1,0:T(8,128)(2,1)S(1)}, u32[]{:S(2)}, u32[]{:S(2)}) %collective-permute-start.25) | collective-permute-done | bytes 196640 | tf_op jit(solution)/shard_map/ppermute | solution.py:203
  94.7 1.5 %edge_half1.6.second_ref.refs_2_ = bf16[4,8,32,128]{3,2,1,0:T(8,128)(2,1)S(1)} custom-call(s32[8,12]{1,0:T(8,128)S(1)} %get-tuple-element.135.refs_0_, bf16[4,8,64,768]{3,2,1,0:T(8,128)(2,1)S(1)} %halves_of_rows.1.refs_1_, bf16[4,8,32,128]{3,2,1,0:T(8,128)(2,1)S(1)} %edge_half1.5.second_ref.refs_2_, ...), custom_call_target="tpu_custom_call" | custom-call | flops 20132659200 | bytes 157286400 | tf_op jit(solution)/shard_map/edge_half1/pallas_call | solution.py:178
  96.2 2.0 %collective-permute-start.28 = (bf16[2,8,32,128]{3,2,1,0:T(8,128)(2,1)S(1)}, bf16[2,8,32,128]{3,2,1,0:T(8,128)(2,1)S(1)}, u32[]{:S(2)}, u32[]{:S(2)}) collective-permute-start(bf16[2,8,32,128]{3,2,1,0:T(8,128)(2,1)S(1)} %pad_maximum_fusion.18), channel_id=1, source_target_pairs={{1,0},{2,1},{3,2},{0,3},{5,4},{6,5},{7,6},{4,7},{9,8},{10,9},{11,1... | collective-permute-start | bytes 393224 | tf_op jit(solution)/shard_map/ppermute | solution.py:203
  98.2 0.1 collective-permute-start.29
  98.4 1.2 collective-permute-start.26
  99.6 1.5 %inner_half0.7.refs_1_.refs_7_ = bf16[2,8,32,128]{3,2,1,0:T(8,128)(2,1)S(1)} custom-call(s32[8,12]{1,0:T(8,128)S(1)} %get-tuple-element.136.refs_0_, bf16[4,8,64,768]{3,2,1,0:T(8,128)(2,1)S(1)} %halves_of_rows.1.refs_1_, bf16[4,8,32,128]{3,2,1,0:T(8,128)(2,1)S(1)} %edge_half0.6.refs_2_.first_ref, ...), custom_call_target="tpu_custom_call" | custom-call | flops 20132659200 | bytes 157286400 | tf_op jit(solution)/shard_map/inner_half0/pallas_call | solution.py:178
  101.1 0.9 unpack.6
  102.0 3.6 %collective-permute-start.30 = (bf16[2,8,32,128]{3,2,1,0:T(8,128)(2,1)S(1)}, bf16[2,8,32,128]{3,2,1,0:T(8,128)(2,1)S(1)}, u32[]{:S(2)}, u32[]{:S(2)}) collective-permute-start(bf16[2,8,32,128]{3,2,1,0:T(8,128)(2,1)S(1)} %slice.222), channel_id=1, source_target_pairs={{1,0},{2,1},{3,2},{0,3},{5,4},{6,5},{7,6},{4,7},{9,8},{10,9},{11,1... | collective-permute-start | bytes 393224 | tf_op jit(solution)/shard_map/ppermute | solution.py:203
  105.7 2.4 %collective-permute-start.32 = (bf16[3,8,32,128]{3,2,1,0:T(8,128)(2,1)S(1)}, bf16[3,8,32,128]{3,2,1,0:T(8,128)(2,1)S(1)}, u32[]{:S(2)}, u32[]{:S(2)}) collective-permute-start(bf16[3,8,32,128]{3,2,1,0:T(8,128)(2,1)S(1)} %pad_maximum_fusion.16.refs_6_), channel_id=1, source_target_pairs={{4,0},{8,4},{12,8},{16,12},{20,16},{24,20},{28,24},{0,28},{5,1},{9... | collective-permute-start | bytes 589832 | tf_op jit(solution)/shard_map/ppermute | solution.py:203
  108.3 1.5 %edge_half0.7.first_ref = bf16[4,8,32,128]{3,2,1,0:T(8,128)(2,1)S(1)} custom-call(s32[8,12]{1,0:T(8,128)S(1)} %get-tuple-element.136.refs_0_, bf16[4,8,64,768]{3,2,1,0:T(8,128)(2,1)S(1)} %halves_of_rows.1.refs_1_, bf16[4,8,32,128]{3,2,1,0:T(8,128)(2,1)S(1)} %edge_half0.6.refs_2_.first_ref, bf16[4,8,32,128]{3,2,1,0:T(8,128)(2,1)S(1)} %collective-permute-done.20.refs_3_, ...), custom_call_target="tpu_custom_call" | custom-call | flops 20132659200 | bytes 157286400 | tf_op jit(solution)/shard_map/edge_half0/pallas_call | solution.py:178
  109.8 2.7 %collective-permute-done.31 = bf16[2,8,32,128]{3,2,1,0:T(8,128)(2,1)S(1)} collective-permute-done((bf16[2,8,32,128]{3,2,1,0:T(8,128)(2,1)S(1)}, bf16[2,8,32,128]{3,2,1,0:T(8,128)(2,1)S(1)}, u32[]{:S(2)}, u32[]{:S(2)}) %collective-permute-start.31) | collective-permute-done | bytes 131104 | tf_op jit(solution)/shard_map/ppermute | solution.py:203
  112.5 1.5 %inner_half1.7.refs_7_.refs_8_ = bf16[2,8,32,128]{3,2,1,0:T(8,128)(2,1)S(1)} custom-call(s32[8,12]{1,0:T(8,128)S(1)} %get-tuple-element.135.refs_0_, bf16[4,8,64,768]{3,2,1,0:T(8,128)(2,1)S(1)} %halves_of_rows.1.refs_1_, bf16[4,8,32,128]{3,2,1,0:T(8,128)(2,1)S(1)} %edge_half1.6.second_ref.refs_2_, bf16[4,8,32,128]{3,2,1,0:T(8,128)(2,1)S(1)} %pad_maximum_fusion.refs_3_, ...), custom_call_target="tpu_custom_call" | custom-call | flops 20132659200 | bytes 157286400 | tf_op jit(solution)/shard_map/inner_half1/pallas_call | solution.py:178
  114.0 0.2 collective-permute-done.33.refs_6_
  114.2 1.5 %edge_half1.7.second_ref = bf16[4,8,32,128]{3,2,1,0:T(8,128)(2,1)S(1)} custom-call(s32[8,12]{1,0:T(8,128)S(1)} %get-tuple-element.135.refs_0_, bf16[4,8,64,768]{3,2,1,0:T(8,128)(2,1)S(1)} %halves_of_rows.1.refs_1_, bf16[4,8,32,128]{3,2,1,0:T(8,128)(2,1)S(1)} %edge_half1.6.second_ref.refs_2_, bf16[4,8,32,128]{3,2,1,0:T(8,128)(2,1)S(1)} %pad_maximum_fusion.refs_3_, ...), custom_call_target="tpu_custom_call" | custom-call | flops 20132659200 | bytes 157286400 | tf_op jit(solution)/shard_map/edge_half1/pallas_call | solution.py:178
  115.7 1.5 %unpack.7 = (bf16[4,4,8,64,128]{4,3,2,1,0:T(8,128)(2,1)}, f32[8,128]{1,0:T(8,128)}) custom-call(bf16[4,8,32,128]{3,2,1,0:T(8,128)(2,1)S(1)} %edge_half0.7.first_ref, bf16[4,8,32,128]{3,2,1,0:T(8,128)(2,1)S(1)} %edge_half1.7.second_ref, bf16[4,4,8,64,128]{4,3,2,1,0:T(8,128)(2,1)} %get-tuple-element.79.refs_0_), custom_call_target="tpu_custom_call", output_to_operand_aliasing={{0}: (2, {})} | custom-call | tf_op jit(solution)/shard_map/unpack/pallas_call | solution.py:77
  (79 shorter events, 1.4 us)
Async XLA Ops:
  0.0 1.0 copy-start.1
  1.2 12.3 %collective-permute-start = (bf16[4,8,32,128]{3,2,1,0:T(8,128)(2,1)S(1)}, bf16[4,8,32,128]{3,2,1,0:T(8,128)(2,1)S(1)}, u32[]{:S(2)}, u32[]{:S(2)}) collective-permute-start(bf16[4,8,32,128]{3,2,1,0:T(8,128)(2,1)S(1)} %get-tuple-element.45.refs_2_), channel_id=1, source_target_pairs={{0,1},{1,2},{2,3},{3,0},{4,5},{5,6},{6,7},{7,4},{8,9},{9,10},{10,1... | collective-permute-start | bytes 786440 | tf_op jit(solution)/shard_map/ppermute | solution.py:203
  4.3 14.1 %collective-permute-start.1 = (bf16[4,8,32,128]{3,2,1,0:T(8,128)(2,1)S(1)}, bf16[4,8,32,128]{3,2,1,0:T(8,128)(2,1)S(1)}, u32[]{:S(2)}, u32[]{:S(2)}) collective-permute-start(bf16[4,8,32,128]{3,2,1,0:T(8,128)(2,1)S(1)} %get-tuple-element.45.refs_2_), channel_id=1, source_target_pairs={{1,0},{2,1},{3,2},{0,3},{5,4},{6,5},{7,6},{4,7},{9,8},{10,9},{11,1... | collective-permute-start | bytes 786440 | tf_op jit(solution)/shard_map/ppermute | solution.py:203
  6.4 30.3 %collective-permute-start.6 = (bf16[4,8,32,128]{3,2,1,0:T(8,128)(2,1)S(1)}, bf16[4,8,32,128]{3,2,1,0:T(8,128)(2,1)S(1)}, u32[]{:S(2)}, u32[]{:S(2)}) collective-permute-start(bf16[4,8,32,128]{3,2,1,0:T(8,128)(2,1)S(1)} %get-tuple-element.49.refs_2_), channel_id=1, source_target_pairs={{1,0},{2,1},{3,2},{0,3},{5,4},{6,5},{7,6},{4,7},{9,8},{10,9},{11,1... | collective-permute-start | bytes 786440 | tf_op jit(solution)/shard_map/ppermute | solution.py:203
  8.3 28.3 %collective-permute-start.7 = (bf16[4,8,32,128]{3,2,1,0:T(8,128)(2,1)S(1)}, bf16[4,8,32,128]{3,2,1,0:T(8,128)(2,1)S(1)}, u32[]{:S(2)}, u32[]{:S(2)}) collective-permute-start(bf16[4,8,32,128]{3,2,1,0:T(8,128)(2,1)S(1)} %get-tuple-element.49.refs_2_), channel_id=1, source_target_pairs={{0,1},{1,2},{2,3},{3,0},{4,5},{5,6},{6,7},{7,4},{8,9},{9,10},{10,1... | collective-permute-start | bytes 786440 | tf_op jit(solution)/shard_map/ppermute | solution.py:203
  8.4 1.9 %copy-start = (bf16[4,1,8,64,768]{4,3,2,1,0:T(8,128)(2,1)S(1)}, bf16[4,1,8,64,768]{4,3,2,1,0:T(8,128)(2,1)}, u32[]{:S(2)}) copy-start(bf16[4,1,8,64,768]{4,3,2,1,0:T(8,128)(2,1)} %param.4) | copy-start | bytes 9437188
  10.3 2.7 %copy-start.2 = (s32[1,8,12]{2,1,0:T(8,128)S(1)}, s32[1,8,12]{2,1,0:T(8,128)}, u32[]{:S(2)}) copy-start(s32[1,8,12]{2,1,0:T(8,128)} %param.5) | copy-start | bytes 1156
  18.5 5.8 %collective-permute-start.2 = (bf16[3,8,32,128]{3,2,1,0:T(8,128)(2,1)S(1)}, bf16[3,8,32,128]{3,2,1,0:T(8,128)(2,1)S(1)}, u32[]{:S(2)}, u32[]{:S(2)}) collective-permute-start(bf16[3,8,32,128]{3,2,1,0:T(8,128)(2,1)S(1)} %pad_maximum_fusion.2.refs_6_), channel_id=1, source_target_pairs={{4,0},{8,4},{12,8},{16,12},{20,16},{24,20},{28,24},{0,28},{5,1},{9... | collective-permute-start | bytes 589832 | tf_op jit(solution)/shard_map/ppermute | solution.py:203
  19.3 7.4 %collective-permute-start.3 = (bf16[3,8,32,128]{3,2,1,0:T(8,128)(2,1)S(1)}, bf16[3,8,32,128]{3,2,1,0:T(8,128)(2,1)S(1)}, u32[]{:S(2)}, u32[]{:S(2)}) collective-permute-start(bf16[3,8,32,128]{3,2,1,0:T(8,128)(2,1)S(1)} %pad_maximum_fusion.3.refs_5_), channel_id=1, source_target_pairs={{0,4},{4,8},{8,12},{12,16},{16,20},{20,24},{24,28},{28,0},{1,5},{5... | collective-permute-start | bytes 589832 | tf_op jit(solution)/shard_map/ppermute | solution.py:203
  28.2 19.4 %collective-permute-start.4 = (bf16[4,8,32,128]{3,2,1,0:T(8,128)(2,1)S(1)}, bf16[4,8,32,128]{3,2,1,0:T(8,128)(2,1)S(1)}, u32[]{:S(2)}, u32[]{:S(2)}) collective-permute-start(bf16[4,8,32,128]{3,2,1,0:T(8,128)(2,1)S(1)} %edge_half0.4.refs_2_.first_ref), channel_id=1, source_target_pairs={{0,1},{1,2},{2,3},{3,0},{4,5},{5,6},{6,7},{7,4},{8,9},{9,10},{10,1... | collective-permute-start | bytes 786440 | tf_op jit(solution)/shard_map/ppermute | solution.py:203
  33.2 14.3 %collective-permute-start.5 = (bf16[4,8,32,128]{3,2,1,0:T(8,128)(2,1)S(1)}, bf16[4,8,32,128]{3,2,1,0:T(8,128)(2,1)S(1)}, u32[]{:S(2)}, u32[]{:S(2)}) collective-permute-start(bf16[4,8,32,128]{3,2,1,0:T(8,128)(2,1)S(1)} %edge_half0.4.refs_2_.first_ref), channel_id=1, source_target_pairs={{1,0},{2,1},{3,2},{0,3},{5,4},{6,5},{7,6},{4,7},{9,8},{10,9},{11,1... | collective-permute-start | bytes 786440 | tf_op jit(solution)/shard_map/ppermute | solution.py:203
  36.8 5.3 %collective-permute-start.8 = (bf16[3,8,32,128]{3,2,1,0:T(8,128)(2,1)S(1)}, bf16[3,8,32,128]{3,2,1,0:T(8,128)(2,1)S(1)}, u32[]{:S(2)}, u32[]{:S(2)}) collective-permute-start(bf16[3,8,32,128]{3,2,1,0:T(8,128)(2,1)S(1)} %pad_maximum_fusion.4.refs_6_), channel_id=1, source_target_pairs={{4,0},{8,4},{12,8},{16,12},{20,16},{24,20},{28,24},{0,28},{5,1},{9... | collective-permute-start | bytes 589832 | tf_op jit(solution)/shard_map/ppermute | solution.py:203
  36.9 7.1 %collective-permute-start.9 = (bf16[3,8,32,128]{3,2,1,0:T(8,128)(2,1)S(1)}, bf16[3,8,32,128]{3,2,1,0:T(8,128)(2,1)S(1)}, u32[]{:S(2)}, u32[]{:S(2)}) collective-permute-start(bf16[3,8,32,128]{3,2,1,0:T(8,128)(2,1)S(1)} %pad_maximum_fusion.5.refs_5_), channel_id=1, source_target_pairs={{0,4},{4,8},{8,12},{12,16},{16,20},{20,24},{24,28},{28,0},{1,5},{5... | collective-permute-start | bytes 589832 | tf_op jit(solution)/shard_map/ppermute | solution.py:203
  45.5 14.8 %collective-permute-start.14 = (bf16[4,8,32,128]{3,2,1,0:T(8,128)(2,1)S(1)}, bf16[4,8,32,128]{3,2,1,0:T(8,128)(2,1)S(1)}, u32[]{:S(2)}, u32[]{:S(2)}) collective-permute-start(bf16[4,8,32,128]{3,2,1,0:T(8,128)(2,1)S(1)} %edge_half1.4.second_ref.refs_2_), channel_id=1, source_target_pairs={{1,0},{2,1},{3,2},{0,3},{5,4},{6,5},{7,6},{4,7},{9,8},{10,9},{11,1... | collective-permute-start | bytes 786440 | tf_op jit(solution)/shard_map/ppermute | solution.py:203
  47.2 13.0 %collective-permute-start.15 = (bf16[4,8,32,128]{3,2,1,0:T(8,128)(2,1)S(1)}, bf16[4,8,32,128]{3,2,1,0:T(8,128)(2,1)S(1)}, u32[]{:S(2)}, u32[]{:S(2)}) collective-permute-start(bf16[4,8,32,128]{3,2,1,0:T(8,128)(2,1)S(1)} %edge_half1.4.second_ref.refs_2_), channel_id=1, source_target_pairs={{0,1},{1,2},{2,3},{3,0},{4,5},{5,6},{6,7},{7,4},{8,9},{9,10},{10,1... | collective-permute-start | bytes 786440 | tf_op jit(solution)/shard_map/ppermute | solution.py:203
  47.7 5.3 %collective-permute-start.10 = (bf16[3,8,32,128]{3,2,1,0:T(8,128)(2,1)S(1)}, bf16[3,8,32,128]{3,2,1,0:T(8,128)(2,1)S(1)}, u32[]{:S(2)}, u32[]{:S(2)}) collective-permute-start(bf16[3,8,32,128]{3,2,1,0:T(8,128)(2,1)S(1)} %pad_maximum_fusion.6.refs_6_), channel_id=1, source_target_pairs={{4,0},{8,4},{12,8},{16,12},{20,16},{24,20},{28,24},{0,28},{5,1},{9... | collective-permute-start | bytes 589832 | tf_op jit(solution)/shard_map/ppermute | solution.py:203
  48.5 6.3 %collective-permute-start.11 = (bf16[3,8,32,128]{3,2,1,0:T(8,128)(2,1)S(1)}, bf16[3,8,32,128]{3,2,1,0:T(8,128)(2,1)S(1)}, u32[]{:S(2)}, u32[]{:S(2)}) collective-permute-start(bf16[3,8,32,128]{3,2,1,0:T(8,128)(2,1)S(1)} %pad_maximum_fusion.7.refs_5_), channel_id=1, source_target_pairs={{0,4},{4,8},{8,12},{12,16},{16,20},{20,24},{24,28},{28,0},{1,5},{5... | collective-permute-start | bytes 589832 | tf_op jit(solution)/shard_map/ppermute | solution.py:203
  56.4 18.5 %collective-permute-start.12 = (bf16[4,8,32,128]{3,2,1,0:T(8,128)(2,1)S(1)}, bf16[4,8,32,128]{3,2,1,0:T(8,128)(2,1)S(1)}, u32[]{:S(2)}, u32[]{:S(2)}) collective-permute-start(bf16[4,8,32,128]{3,2,1,0:T(8,128)(2,1)S(1)} %edge_half0.5.refs_2_.first_ref), channel_id=1, source_target_pairs={{0,1},{1,2},{2,3},{3,0},{4,5},{5,6},{6,7},{7,4},{8,9},{9,10},{10,1... | collective-permute-start | bytes 786440 | tf_op jit(solution)/shard_map/ppermute | solution.py:203
  58.4 16.5 %collective-permute-start.13 = (bf16[4,8,32,128]{3,2,1,0:T(8,128)(2,1)S(1)}, bf16[4,8,32,128]{3,2,1,0:T(8,128)(2,1)S(1)}, u32[]{:S(2)}, u32[]{:S(2)}) collective-permute-start(bf16[4,8,32,128]{3,2,1,0:T(8,128)(2,1)S(1)} %edge_half0.5.refs_2_.first_ref), channel_id=1, source_target_pairs={{1,0},{2,1},{3,2},{0,3},{5,4},{6,5},{7,6},{4,7},{9,8},{10,9},{11,1... | collective-permute-start | bytes 786440 | tf_op jit(solution)/shard_map/ppermute | solution.py:203
  60.3 5.3 %collective-permute-start.16 = (bf16[3,8,32,128]{3,2,1,0:T(8,128)(2,1)S(1)}, bf16[3,8,32,128]{3,2,1,0:T(8,128)(2,1)S(1)}, u32[]{:S(2)}, u32[]{:S(2)}) collective-permute-start(bf16[3,8,32,128]{3,2,1,0:T(8,128)(2,1)S(1)} %pad_maximum_fusion.8.refs_6_), channel_id=1, source_target_pairs={{4,0},{8,4},{12,8},{16,12},{20,16},{24,20},{28,24},{0,28},{5,1},{9... | collective-permute-start | bytes 589832 | tf_op jit(solution)/shard_map/ppermute | solution.py:203
  61.0 10.3 %collective-permute-start.17 = (bf16[3,8,32,128]{3,2,1,0:T(8,128)(2,1)S(1)}, bf16[3,8,32,128]{3,2,1,0:T(8,128)(2,1)S(1)}, u32[]{:S(2)}, u32[]{:S(2)}) collective-permute-start(bf16[3,8,32,128]{3,2,1,0:T(8,128)(2,1)S(1)} %pad_maximum_fusion.9.refs_5_), channel_id=1, source_target_pairs={{0,4},{4,8},{8,12},{12,16},{16,20},{20,24},{24,28},{28,0},{1,5},{5... | collective-permute-start | bytes 589832 | tf_op jit(solution)/shard_map/ppermute | solution.py:203
  72.8 14.9 %collective-permute-start.22 = (bf16[4,8,32,128]{3,2,1,0:T(8,128)(2,1)S(1)}, bf16[4,8,32,128]{3,2,1,0:T(8,128)(2,1)S(1)}, u32[]{:S(2)}, u32[]{:S(2)}) collective-permute-start(bf16[4,8,32,128]{3,2,1,0:T(8,128)(2,1)S(1)} %edge_half1.5.second_ref.refs_2_), channel_id=1, source_target_pairs={{1,0},{2,1},{3,2},{0,3},{5,4},{6,5},{7,6},{4,7},{9,8},{10,9},{11,1... | collective-permute-start | bytes 786440 | tf_op jit(solution)/shard_map/ppermute | solution.py:203
  74.8 12.8 %collective-permute-start.23 = (bf16[4,8,32,128]{3,2,1,0:T(8,128)(2,1)S(1)}, bf16[4,8,32,128]{3,2,1,0:T(8,128)(2,1)S(1)}, u32[]{:S(2)}, u32[]{:S(2)}) collective-permute-start(bf16[4,8,32,128]{3,2,1,0:T(8,128)(2,1)S(1)} %edge_half1.5.second_ref.refs_2_), channel_id=1, source_target_pairs={{0,1},{1,2},{2,3},{3,0},{4,5},{5,6},{6,7},{7,4},{8,9},{9,10},{10,1... | collective-permute-start | bytes 786440 | tf_op jit(solution)/shard_map/ppermute | solution.py:203
  75.0 5.3 %collective-permute-start.18 = (bf16[3,8,32,128]{3,2,1,0:T(8,128)(2,1)S(1)}, bf16[3,8,32,128]{3,2,1,0:T(8,128)(2,1)S(1)}, u32[]{:S(2)}, u32[]{:S(2)}) collective-permute-start(bf16[3,8,32,128]{3,2,1,0:T(8,128)(2,1)S(1)} %pad_maximum_fusion.10.refs_6_), channel_id=1, source_target_pairs={{4,0},{8,4},{12,8},{16,12},{20,16},{24,20},{28,24},{0,28},{5,1},{9... | collective-permute-start | bytes 589832 | tf_op jit(solution)/shard_map/ppermute | solution.py:203
  75.1 7.2 %collective-permute-start.19 = (bf16[3,8,32,128]{3,2,1,0:T(8,128)(2,1)S(1)}, bf16[3,8,32,128]{3,2,1,0:T(8,128)(2,1)S(1)}, u32[]{:S(2)}, u32[]{:S(2)}) collective-permute-start(bf16[3,8,32,128]{3,2,1,0:T(8,128)(2,1)S(1)} %pad_maximum_fusion.11.refs_5_), channel_id=1, source_target_pairs={{0,4},{4,8},{8,12},{12,16},{16,20},{20,24},{24,28},{28,0},{1,5},{5... | collective-permute-start | bytes 589832 | tf_op jit(solution)/shard_map/ppermute | solution.py:203
  83.8 14.5 %collective-permute-start.20 = (bf16[4,8,32,128]{3,2,1,0:T(8,128)(2,1)S(1)}, bf16[4,8,32,128]{3,2,1,0:T(8,128)(2,1)S(1)}, u32[]{:S(2)}, u32[]{:S(2)}) collective-permute-start(bf16[4,8,32,128]{3,2,1,0:T(8,128)(2,1)S(1)} %edge_half0.6.refs_2_.first_ref), channel_id=1, source_target_pairs={{0,1},{1,2},{2,3},{3,0},{4,5},{5,6},{6,7},{7,4},{8,9},{9,10},{10,1... | collective-permute-start | bytes 786440 | tf_op jit(solution)/shard_map/ppermute | solution.py:203
  84.6 13.7 %collective-permute-start.21 = (bf16[4,8,32,128]{3,2,1,0:T(8,128)(2,1)S(1)}, bf16[4,8,32,128]{3,2,1,0:T(8,128)(2,1)S(1)}, u32[]{:S(2)}, u32[]{:S(2)}) collective-permute-start(bf16[4,8,32,128]{3,2,1,0:T(8,128)(2,1)S(1)} %edge_half0.6.refs_2_.first_ref), channel_id=1, source_target_pairs={{1,0},{2,1},{3,2},{0,3},{5,4},{6,5},{7,6},{4,7},{9,8},{10,9},{11,1... | collective-permute-start | bytes 786440 | tf_op jit(solution)/shard_map/ppermute | solution.py:203
  87.8 5.3 %collective-permute-start.24 = (bf16[3,8,32,128]{3,2,1,0:T(8,128)(2,1)S(1)}, bf16[3,8,32,128]{3,2,1,0:T(8,128)(2,1)S(1)}, u32[]{:S(2)}, u32[]{:S(2)}) collective-permute-start(bf16[3,8,32,128]{3,2,1,0:T(8,128)(2,1)S(1)} %pad_maximum_fusion.12.refs_6_), channel_id=1, source_target_pairs={{4,0},{8,4},{12,8},{16,12},{20,16},{24,20},{28,24},{0,28},{5,1},{9... | collective-permute-start | bytes 589832 | tf_op jit(solution)/shard_map/ppermute | solution.py:203
  88.6 6.1 %collective-permute-start.25 = (bf16[3,8,32,128]{3,2,1,0:T(8,128)(2,1)S(1)}, bf16[3,8,32,128]{3,2,1,0:T(8,128)(2,1)S(1)}, u32[]{:S(2)}, u32[]{:S(2)}) collective-permute-start(bf16[3,8,32,128]{3,2,1,0:T(8,128)(2,1)S(1)} %pad_maximum_fusion.13.refs_5_), channel_id=1, source_target_pairs={{0,4},{4,8},{8,12},{12,16},{16,20},{20,24},{24,28},{28,0},{1,5},{5... | collective-permute-start | bytes 589832 | tf_op jit(solution)/shard_map/ppermute | solution.py:203
  96.2 9.5 %collective-permute-start.28 = (bf16[2,8,32,128]{3,2,1,0:T(8,128)(2,1)S(1)}, bf16[2,8,32,128]{3,2,1,0:T(8,128)(2,1)S(1)}, u32[]{:S(2)}, u32[]{:S(2)}) collective-permute-start(bf16[2,8,32,128]{3,2,1,0:T(8,128)(2,1)S(1)} %pad_maximum_fusion.18), channel_id=1, source_target_pairs={{1,0},{2,1},{3,2},{0,3},{5,4},{6,5},{7,6},{4,7},{9,8},{10,9},{11,1... | collective-permute-start | bytes 393224 | tf_op jit(solution)/shard_map/ppermute | solution.py:203
  98.2 7.4 %collective-permute-start.29 = (bf16[2,8,32,128]{3,2,1,0:T(8,128)(2,1)S(1)}, bf16[2,8,32,128]{3,2,1,0:T(8,128)(2,1)S(1)}, u32[]{:S(2)}, u32[]{:S(2)}) collective-permute-start(bf16[2,8,32,128]{3,2,1,0:T(8,128)(2,1)S(1)} %pad_maximum_fusion.18), channel_id=1, source_target_pairs={{0,1},{1,2},{2,3},{3,0},{4,5},{5,6},{6,7},{7,4},{8,9},{9,10},{10,1... | collective-permute-start | bytes 393224 | tf_op jit(solution)/shard_map/ppermute | solution.py:203
  98.4 9.8 %collective-permute-start.26 = (bf16[3,8,32,128]{3,2,1,0:T(8,128)(2,1)S(1)}, bf16[3,8,32,128]{3,2,1,0:T(8,128)(2,1)S(1)}, u32[]{:S(2)}, u32[]{:S(2)}) collective-permute-start(bf16[3,8,32,128]{3,2,1,0:T(8,128)(2,1)S(1)} %pad_maximum_fusion.14.refs_6_), channel_id=1, source_target_pairs={{4,0},{8,4},{12,8},{16,12},{20,16},{24,20},{28,24},{0,28},{5,1},{9... | collective-permute-start | bytes 589832 | tf_op jit(solution)/shard_map/ppermute | solution.py:203
  99.6 8.7 %collective-permute-start.27 = (bf16[3,8,32,128]{3,2,1,0:T(8,128)(2,1)S(1)}, bf16[3,8,32,128]{3,2,1,0:T(8,128)(2,1)S(1)}, u32[]{:S(2)}, u32[]{:S(2)}) collective-permute-start(bf16[3,8,32,128]{3,2,1,0:T(8,128)(2,1)S(1)} %pad_maximum_fusion.15.refs_5_), channel_id=1, source_target_pairs={{0,4},{4,8},{8,12},{12,16},{16,20},{20,24},{24,28},{28,0},{1,5},{5... | collective-permute-start | bytes 589832 | tf_op jit(solution)/shard_map/ppermute | solution.py:203
  102.0 7.7 %collective-permute-start.30 = (bf16[2,8,32,128]{3,2,1,0:T(8,128)(2,1)S(1)}, bf16[2,8,32,128]{3,2,1,0:T(8,128)(2,1)S(1)}, u32[]{:S(2)}, u32[]{:S(2)}) collective-permute-start(bf16[2,8,32,128]{3,2,1,0:T(8,128)(2,1)S(1)} %slice.222), channel_id=1, source_target_pairs={{1,0},{2,1},{3,2},{0,3},{5,4},{6,5},{7,6},{4,7},{9,8},{10,9},{11,1... | collective-permute-start | bytes 393224 | tf_op jit(solution)/shard_map/ppermute | solution.py:203
  105.6 6.8 %collective-permute-start.31 = (bf16[2,8,32,128]{3,2,1,0:T(8,128)(2,1)S(1)}, bf16[2,8,32,128]{3,2,1,0:T(8,128)(2,1)S(1)}, u32[]{:S(2)}, u32[]{:S(2)}) collective-permute-start(bf16[2,8,32,128]{3,2,1,0:T(8,128)(2,1)S(1)} %slice.222), channel_id=1, source_target_pairs={{0,1},{1,2},{2,3},{3,0},{4,5},{5,6},{6,7},{7,4},{8,9},{9,10},{10,1... | collective-permute-start | bytes 393224 | tf_op jit(solution)/shard_map/ppermute | solution.py:203
  105.7 8.3 %collective-permute-start.32 = (bf16[3,8,32,128]{3,2,1,0:T(8,128)(2,1)S(1)}, bf16[3,8,32,128]{3,2,1,0:T(8,128)(2,1)S(1)}, u32[]{:S(2)}, u32[]{:S(2)}) collective-permute-start(bf16[3,8,32,128]{3,2,1,0:T(8,128)(2,1)S(1)} %pad_maximum_fusion.16.refs_6_), channel_id=1, source_target_pairs={{4,0},{8,4},{12,8},{16,12},{20,16},{24,20},{28,24},{0,28},{5,1},{9... | collective-permute-start | bytes 589832 | tf_op jit(solution)/shard_map/ppermute | solution.py:203
  108.2 6.0 %collective-permute-start.33 = (bf16[3,8,32,128]{3,2,1,0:T(8,128)(2,1)S(1)}, bf16[3,8,32,128]{3,2,1,0:T(8,128)(2,1)S(1)}, u32[]{:S(2)}, u32[]{:S(2)}) collective-permute-start(bf16[3,8,32,128]{3,2,1,0:T(8,128)(2,1)S(1)} %pad_maximum_fusion.17.refs_5_), channel_id=1, source_target_pairs={{0,4},{4,8},{8,12},{12,16},{16,20},{20,24},{24,28},{28,0},{1,5},{5... | collective-permute-start | bytes 589832 | tf_op jit(solution)/shard_map/ppermute | solution.py:203

commit v14 on v12

--- a/solution.py
+++ b/solution.py
@@ -92,13 +92,13 @@
     )(first, second, *extra)
 
 
-def edges(own, low_az, high_az, after):
-    *trio, _ = lax.optimization_barrier((low_az, own, high_az, after))
+def edges(own, high_az, low_az, after):
+    *trio, _ = lax.optimization_barrier((high_az, own, low_az, after))
     return jnp.stack([part[0] for part in trio]), jnp.stack([part[-1] for part in trio])
 
 
 def from_neighbours(value):
-    return value, shift(value, "azim", True), shift(value, "azim", False)
+    return value, shift(value, "azim", False), shift(value, "azim", True)
 
 
 def joined(value, outer, inner, after):
@@ -110,7 +110,7 @@
 
 
 def part_kernel(half, *refs):
-    table_ref, blocks, own, low_az, high_az = refs[:5]
+    table_ref, blocks, own, high_az, low_az = refs[:5]
     following, window, index, sem = refs[-4:]
     edge = len(refs) > 11
     faces, width, depth = blocks.shape[1:]
@@ -122,7 +122,7 @@
     indexing.start()
 
     def enter(column, carry):
-        for azim, source in enumerate((low_az, own, high_az)):
+        for azim, source in enumerate((high_az, own, low_az)):
             for face in range(faces):
                 view[azim, column + 1, face] = source[column, face]
         return carry
@@ -246,7 +246,8 @@
     start = start_vector.reshape(columns, faces, width, lanes)
     blocks = halves_of_rows(trace_blocks.reshape(columns, faces, width, -1))
     codes = neighbour.reshape(faces, -1)
-    table = (((codes // faces) % 3) * (columns + 2) + codes // (3 * faces)) * faces + codes % faces
+    around_shift = 2 - (codes // faces) % 3
+    table = (around_shift * (columns + 2) + codes // (3 * faces)) * faces + codes % faces
     every = tuple(range(columns))
     current = list(pack(start))
     basis = None

time: 114 us -> 113 us (level)
  no operation moved by 1% of the time
where the time goes in v14:
time: 113 us
  starting transfers between devices  42.9 us (38%)
  waiting for transfers between devices  35.1 us (31%)
  Pallas kernels  30.8 us (27%)
  local copies, waits for them, and re-layouts  3.24 us (3%)
    ppermute x34, starting transfers between devices, shift(): return lax.ppermute(value, axis, pairs)  42.9 us
    ppermute x34, waiting for transfers between devices, shift(): return lax.ppermute(value, axis, pairs)  35.1 us
    pallas_call x16, Pallas kernels, part(): pl.pallas_call(functools.partial(part_kernel, half), in_specs=in_specs, o...  23.7 us
    pallas_call x4, Pallas kernels, unpack(): pl.pallas_call(functools.partial(unpack_kernel, index, chosen, skipped),...  4.25 us
    unnamed x6, local copies, waits for them, and re-layouts  2.93 us
    pallas_call x1, Pallas kernels, halves_of_rows(): pl.pallas_call(halves_kernel, in_specs=[VMEM], out_specs=VMEM, out_shape=...  2.72 us
  transfers between devices with their start and end apart: 34, of which 15 were waited for; matrix products, arithmetic and copies ran while one was open for 1% of the time, Pallas kernels for 24%

profile of v14, /device:TPU:0, one launch (start us, length us, event | category | flops | bytes accessed | tf_op | source)
XLA Modules:
  0.0 113.2 jit_solution(10032397556957130476)
XLA Ops:
  0.0 1.0 copy-done.1
  1.0 0.2 pack.1
  1.2 5.1 %collective-permute-start = (bf16[4,8,32,128]{3,2,1,0:T(8,128)(2,1)S(1)}, bf16[4,8,32,128]{3,2,1,0:T(8,128)(2,1)S(1)}, u32[]{:S(2)}, u32[]{:S(2)}) collective-permute-start(bf16[4,8,32,128]{3,2,1,0:T(8,128)(2,1)S(1)} %get-tuple-element.45.refs_2_), channel_id=1, source_target_pairs={{1,0},{2,1},{3,2},{0,3},{5,4},{6,5},{7,6},{4,7},{9,8},{10,9},{11,1... | collective-permute-start | bytes 786440 | tf_op jit(solution)/shard_map/ppermute | solution.py:203
  6.3 3.8 %collective-permute-start.6 = (bf16[4,8,32,128]{3,2,1,0:T(8,128)(2,1)S(1)}, bf16[4,8,32,128]{3,2,1,0:T(8,128)(2,1)S(1)}, u32[]{:S(2)}, u32[]{:S(2)}) collective-permute-start(bf16[4,8,32,128]{3,2,1,0:T(8,128)(2,1)S(1)} %get-tuple-element.49.refs_2_), channel_id=1, source_target_pairs={{1,0},{2,1},{3,2},{0,3},{5,4},{6,5},{7,6},{4,7},{9,8},{10,9},{11,1... | collective-permute-start | bytes 786440 | tf_op jit(solution)/shard_map/ppermute | solution.py:203
  10.2 1.9 %copy-done = bf16[4,1,8,64,768]{4,3,2,1,0:T(8,128)(2,1)S(1)} copy-done((bf16[4,1,8,64,768]{4,3,2,1,0:T(8,128)(2,1)S(1)}, bf16[4,1,8,64,768]{4,3,2,1,0:T(8,128)(2,1)}, u32[]{:S(2)}) %copy-start) | copy-done | bytes 3145752
  12.0 2.7 %halves_of_rows.1.refs_1_ = bf16[4,8,64,768]{3,2,1,0:T(8,128)(2,1)S(1)} custom-call(bf16[4,8,64,768]{3,2,1,0:T(8,128)(2,1)S(1)} %bitcast.29), custom_call_target="tpu_custom_call" | custom-call | tf_op jit(solution)/shard_map/halves_of_rows/pallas_call | solution.py:234
  14.8 4.8 %collective-permute-done.1.refs_4_ = bf16[4,8,32,128]{3,2,1,0:T(8,128)(2,1)S(1)} collective-permute-done((bf16[4,8,32,128]{3,2,1,0:T(8,128)(2,1)S(1)}, bf16[4,8,32,128]{3,2,1,0:T(8,128)(2,1)S(1)}, u32[]{:S(2)}, u32[]{:S(2)}) %collective-permute-start.1) | collective-permute-done | bytes 262176 | tf_op jit(solution)/shard_map/ppermute | solution.py:203
  19.7 0.1 collective-permute-start.2
  19.8 0.5 collective-permute-start.3
  20.3 1.5 %inner_half0.4.refs_7_.refs_8_ = bf16[2,8,32,128]{3,2,1,0:T(8,128)(2,1)S(1)} custom-call(s32[8,12]{1,0:T(8,128)S(1)} %fusion.5.refs_0_, bf16[4,8,64,768]{3,2,1,0:T(8,128)(2,1)S(1)} %halves_of_rows.1.refs_1_, bf16[4,8,32,128]{3,2,1,0:T(8,128)(2,1)S(1)} %get-tuple-element.45.refs_2_, bf16[4,8,32,128]{3,2,1,0:T(8,128)(2,1)S(1)} %collective-permute-done.refs_3_, ...), custom_call_target="tpu_custom_call" | custom-call | flops 20132659200 | bytes 157286400 | tf_op jit(solution)/shard_map/inner_half0/pallas_call | solution.py:178
  21.8 2.2 %collective-permute-done.2.refs_5_ = bf16[3,8,32,128]{3,2,1,0:T(8,128)(2,1)S(1)} collective-permute-done((bf16[3,8,32,128]{3,2,1,0:T(8,128)(2,1)S(1)}, bf16[3,8,32,128]{3,2,1,0:T(8,128)(2,1)S(1)}, u32[]{:S(2)}, u32[]{:S(2)}) %collective-permute-start.2) | collective-permute-done | bytes 196640 | tf_op jit(solution)/shard_map/ppermute | solution.py:203
  24.0 3.9 %collective-permute-done.3.refs_6_ = bf16[3,8,32,128]{3,2,1,0:T(8,128)(2,1)S(1)} collective-permute-done((bf16[3,8,32,128]{3,2,1,0:T(8,128)(2,1)S(1)}, bf16[3,8,32,128]{3,2,1,0:T(8,128)(2,1)S(1)}, u32[]{:S(2)}, u32[]{:S(2)}) %collective-permute-start.3) | collective-permute-done | bytes 196640 | tf_op jit(solution)/shard_map/ppermute | solution.py:203
  27.9 1.5 %edge_half0.4.refs_2_.first_ref = bf16[4,8,32,128]{3,2,1,0:T(8,128)(2,1)S(1)} custom-call(s32[8,12]{1,0:T(8,128)S(1)} %fusion.5.refs_0_, bf16[4,8,64,768]{3,2,1,0:T(8,128)(2,1)S(1)} %halves_of_rows.1.refs_1_, bf16[4,8,32,128]{3,2,1,0:T(8,128)(2,1)S(1)} %get-tuple-element.45.refs_2_, bf16[4,8,32,128]{3,2,1,0:T(8,128)(2,1)S(1)} %collective-permute-done.refs_3_, ...), custom_call_target="tpu_custom_call" | custom-call | flops 20132659200 | bytes 157286400 | tf_op jit(solution)/shard_map/edge_half0/pallas_call | solution.py:178
  29.4 2.9 %collective-permute-start.4 = (bf16[4,8,32,128]{3,2,1,0:T(8,128)(2,1)S(1)}, bf16[4,8,32,128]{3,2,1,0:T(8,128)(2,1)S(1)}, u32[]{:S(2)}, u32[]{:S(2)}) collective-permute-start(bf16[4,8,32,128]{3,2,1,0:T(8,128)(2,1)S(1)} %edge_half0.4.refs_2_.first_ref), channel_id=1, source_target_pairs={{1,0},{2,1},{3,2},{0,3},{5,4},{6,5},{7,6},{4,7},{9,8},{10,9},{11,1... | collective-permute-start | bytes 786440 | tf_op jit(solution)/shard_map/ppermute | solution.py:203
  32.5 0.1 collective-permute-start.8
  32.6 0.5 collective-permute-start.9
  33.1 1.5 %inner_half1.4.refs_7_.refs_8_ = bf16[2,8,32,128]{3,2,1,0:T(8,128)(2,1)S(1)} custom-call(s32[8,12]{1,0:T(8,128)S(1)} %fusion.5.refs_0_, bf16[4,8,64,768]{3,2,1,0:T(8,128)(2,1)S(1)} %halves_of_rows.1.refs_1_, bf16[4,8,32,128]{3,2,1,0:T(8,128)(2,1)S(1)} %get-tuple-element.49.refs_2_, bf16[4,8,32,128]{3,2,1,0:T(8,128)(2,1)S(1)} %collective-permute-done.6.refs_3_, ...), custom_call_target="tpu_custom_call" | custom-call | flops 20132659200 | bytes 157286400 | tf_op jit(solution)/shard_map/inner_half1/pallas_call | solution.py:178
  34.6 3.1 %collective-permute-done.8.refs_5_ = bf16[3,8,32,128]{3,2,1,0:T(8,128)(2,1)S(1)} collective-permute-done((bf16[3,8,32,128]{3,2,1,0:T(8,128)(2,1)S(1)}, bf16[3,8,32,128]{3,2,1,0:T(8,128)(2,1)S(1)}, u32[]{:S(2)}, u32[]{:S(2)}) %collective-permute-start.8) | collective-permute-done | bytes 196640 | tf_op jit(solution)/shard_map/ppermute | solution.py:203
  37.7 2.0 %collective-permute-done.9.refs_6_ = bf16[3,8,32,128]{3,2,1,0:T(8,128)(2,1)S(1)} collective-permute-done((bf16[3,8,32,128]{3,2,1,0:T(8,128)(2,1)S(1)}, bf16[3,8,32,128]{3,2,1,0:T(8,128)(2,1)S(1)}, u32[]{:S(2)}, u32[]{:S(2)}) %collective-permute-start.9) | collective-permute-done | bytes 196640 | tf_op jit(solution)/shard_map/ppermute | solution.py:203
  39.7 1.5 %edge_half1.4.second_ref.refs_2_ = bf16[4,8,32,128]{3,2,1,0:T(8,128)(2,1)S(1)} custom-call(s32[8,12]{1,0:T(8,128)S(1)} %fusion.5.refs_0_, bf16[4,8,64,768]{3,2,1,0:T(8,128)(2,1)S(1)} %halves_of_rows.1.refs_1_, bf16[4,8,32,128]{3,2,1,0:T(8,128)(2,1)S(1)} %get-tuple-element.49.refs_2_, bf16[4,8,32,128]{3,2,1,0:T(8,128)(2,1)S(1)} %collective-permute-done.6.refs_3_, ...), custom_call_target="tpu_custom_call" | custom-call | flops 20132659200 | bytes 157286400 | tf_op jit(solution)/shard_map/edge_half1/pallas_call | solution.py:178
  41.2 3.6 %collective-permute-start.14 = (bf16[4,8,32,128]{3,2,1,0:T(8,128)(2,1)S(1)}, bf16[4,8,32,128]{3,2,1,0:T(8,128)(2,1)S(1)}, u32[]{:S(2)}, u32[]{:S(2)}) collective-permute-start(bf16[4,8,32,128]{3,2,1,0:T(8,128)(2,1)S(1)} %edge_half1.4.second_ref.refs_2_), channel_id=1, source_target_pairs={{1,0},{2,1},{3,2},{0,3},{5,4},{6,5},{7,6},{4,7},{9,8},{10,9},{11,1... | collective-permute-start | bytes 786440 | tf_op jit(solution)/shard_map/ppermute | solution.py:203
  44.9 0.8 collective-permute-start.10
  45.8 0.1 collective-permute-start.11
  45.9 1.5 %inner_half0.5.refs_0_.refs_7_ = bf16[2,8,32,128]{3,2,1,0:T(8,128)(2,1)S(1)} custom-call(s32[8,12]{1,0:T(8,128)S(1)} %fusion.5.refs_0_, bf16[4,8,64,768]{3,2,1,0:T(8,128)(2,1)S(1)} %halves_of_rows.1.refs_1_, bf16[4,8,32,128]{3,2,1,0:T(8,128)(2,1)S(1)} %edge_half0.4.refs_2_.first_ref, bf16[4,8,32,128]{3,2,1,0:T(8,128)(2,1)S(1)} %collective-permute-done.4.refs_3_, ...), custom_call_target="tpu_custom_call" | custom-call | flops 20132659200 | bytes 157286400 | tf_op jit(solution)/shard_map/inner_half0/pallas_call | solution.py:178
  47.3 0.9 unpack.4
  48.3 2.2 %collective-permute-done.10.refs_5_ = bf16[3,8,32,128]{3,2,1,0:T(8,128)(2,1)S(1)} collective-permute-done((bf16[3,8,32,128]{3,2,1,0:T(8,128)(2,1)S(1)}, bf16[3,8,32,128]{3,2,1,0:T(8,128)(2,1)S(1)}, u32[]{:S(2)}, u32[]{:S(2)}) %collective-permute-start.10) | collective-permute-done | bytes 196640 | tf_op jit(solution)/shard_map/ppermute | solution.py:203
  50.4 1.4 %collective-permute-done.11.refs_6_ = bf16[3,8,32,128]{3,2,1,0:T(8,128)(2,1)S(1)} collective-permute-done((bf16[3,8,32,128]{3,2,1,0:T(8,128)(2,1)S(1)}, bf16[3,8,32,128]{3,2,1,0:T(8,128)(2,1)S(1)}, u32[]{:S(2)}, u32[]{:S(2)}) %collective-permute-start.11) | collective-permute-done | bytes 196640 | tf_op jit(solution)/shard_map/ppermute | solution.py:203
  51.8 1.5 %edge_half0.5.refs_2_.first_ref = bf16[4,8,32,128]{3,2,1,0:T(8,128)(2,1)S(1)} custom-call(s32[8,12]{1,0:T(8,128)S(1)} %fusion.5.refs_0_, bf16[4,8,64,768]{3,2,1,0:T(8,128)(2,1)S(1)} %halves_of_rows.1.refs_1_, bf16[4,8,32,128]{3,2,1,0:T(8,128)(2,1)S(1)} %edge_half0.4.refs_2_.first_ref, bf16[4,8,32,128]{3,2,1,0:T(8,128)(2,1)S(1)} %collective-permute-done.4.refs_3_, ...), custom_call_target="tpu_custom_call" | custom-call | flops 20132659200 | bytes 157286400 | tf_op jit(solution)/shard_map/edge_half0/pallas_call | solution.py:178
  53.3 3.6 %collective-permute-start.12 = (bf16[4,8,32,128]{3,2,1,0:T(8,128)(2,1)S(1)}, bf16[4,8,32,128]{3,2,1,0:T(8,128)(2,1)S(1)}, u32[]{:S(2)}, u32[]{:S(2)}) collective-permute-start(bf16[4,8,32,128]{3,2,1,0:T(8,128)(2,1)S(1)} %edge_half0.5.refs_2_.first_ref), channel_id=1, source_target_pairs={{1,0},{2,1},{3,2},{0,3},{5,4},{6,5},{7,6},{4,7},{9,8},{10,9},{11,1... | collective-permute-start | bytes 786440 | tf_op jit(solution)/shard_map/ppermute | solution.py:203
  57.0 1.4 %collective-permute-start.16 = (bf16[3,8,32,128]{3,2,1,0:T(8,128)(2,1)S(1)}, bf16[3,8,32,128]{3,2,1,0:T(8,128)(2,1)S(1)}, u32[]{:S(2)}, u32[]{:S(2)}) collective-permute-start(bf16[3,8,32,128]{3,2,1,0:T(8,128)(2,1)S(1)} %pad_maximum_fusion.8.refs_6_), channel_id=1, source_target_pairs={{4,0},{8,4},{12,8},{16,12},{20,16},{24,20},{28,24},{0,28},{5,1},{9... | collective-permute-start | bytes 589832 | tf_op jit(solution)/shard_map/ppermute | solution.py:203
  58.5 0.1 collective-permute-start.17
  58.6 1.5 %inner_half1.5.refs_7_.refs_8_ = bf16[2,8,32,128]{3,2,1,0:T(8,128)(2,1)S(1)} custom-call(s32[8,12]{1,0:T(8,128)S(1)} %fusion.5.refs_0_, bf16[4,8,64,768]{3,2,1,0:T(8,128)(2,1)S(1)} %halves_of_rows.1.refs_1_, bf16[4,8,32,128]{3,2,1,0:T(8,128)(2,1)S(1)} %edge_half1.4.second_ref.refs_2_, bf16[4,8,32,128]{3,2,1,0:T(8,128)(2,1)S(1)} %collective-permute-done.14.refs_3_, ...), custom_call_target="tpu_custom_call" | custom-call | flops 20132659200 | bytes 157286400 | tf_op jit(solution)/shard_map/inner_half1/pallas_call | solution.py:178
  60.0 2.9 %collective-permute-done.16.refs_5_ = bf16[3,8,32,128]{3,2,1,0:T(8,128)(2,1)S(1)} collective-permute-done((bf16[3,8,32,128]{3,2,1,0:T(8,128)(2,1)S(1)}, bf16[3,8,32,128]{3,2,1,0:T(8,128)(2,1)S(1)}, u32[]{:S(2)}, u32[]{:S(2)}) %collective-permute-start.16) | collective-permute-done | bytes 196640 | tf_op jit(solution)/shard_map/ppermute | solution.py:203
  62.9 1.6 %collective-permute-done.17.refs_6_ = bf16[3,8,32,128]{3,2,1,0:T(8,128)(2,1)S(1)} collective-permute-done((bf16[3,8,32,128]{3,2,1,0:T(8,128)(2,1)S(1)}, bf16[3,8,32,128]{3,2,1,0:T(8,128)(2,1)S(1)}, u32[]{:S(2)}, u32[]{:S(2)}) %collective-permute-start.17) | collective-permute-done | bytes 196640 | tf_op jit(solution)/shard_map/ppermute | solution.py:203
  64.5 1.5 %edge_half1.5.second_ref.refs_2_ = bf16[4,8,32,128]{3,2,1,0:T(8,128)(2,1)S(1)} custom-call(s32[8,12]{1,0:T(8,128)S(1)} %fusion.5.refs_0_, bf16[4,8,64,768]{3,2,1,0:T(8,128)(2,1)S(1)} %halves_of_rows.1.refs_1_, bf16[4,8,32,128]{3,2,1,0:T(8,128)(2,1)S(1)} %edge_half1.4.second_ref.refs_2_, bf16[4,8,32,128]{3,2,1,0:T(8,128)(2,1)S(1)} %collective-permute-done.14.refs_3_, ...), custom_call_target="tpu_custom_call" | custom-call | flops 20132659200 | bytes 157286400 | tf_op jit(solution)/shard_map/edge_half1/pallas_call | solution.py:178
  66.0 3.6 %collective-permute-start.22 = (bf16[4,8,32,128]{3,2,1,0:T(8,128)(2,1)S(1)}, bf16[4,8,32,128]{3,2,1,0:T(8,128)(2,1)S(1)}, u32[]{:S(2)}, u32[]{:S(2)}) collective-permute-start(bf16[4,8,32,128]{3,2,1,0:T(8,128)(2,1)S(1)} %edge_half1.5.second_ref.refs_2_), channel_id=1, source_target_pairs={{1,0},{2,1},{3,2},{0,3},{5,4},{6,5},{7,6},{4,7},{9,8},{10,9},{11,1... | collective-permute-start | bytes 786440 | tf_op jit(solution)/shard_map/ppermute | solution.py:203
  69.7 1.3 %collective-permute-start.18 = (bf16[3,8,32,128]{3,2,1,0:T(8,128)(2,1)S(1)}, bf16[3,8,32,128]{3,2,1,0:T(8,128)(2,1)S(1)}, u32[]{:S(2)}, u32[]{:S(2)}) collective-permute-start(bf16[3,8,32,128]{3,2,1,0:T(8,128)(2,1)S(1)} %pad_maximum_fusion.10.refs_6_), channel_id=1, source_target_pairs={{4,0},{8,4},{12,8},{16,12},{20,16},{24,20},{28,24},{0,28},{5,1},{9... | collective-permute-start | bytes 589832 | tf_op jit(solution)/shard_map/ppermute | solution.py:203
  71.0 0.1 collective-permute-start.19
  71.1 1.5 %inner_half0.6.refs_1_.refs_7_ = bf16[2,8,32,128]{3,2,1,0:T(8,128)(2,1)S(1)} custom-call(s32[8,12]{1,0:T(8,128)S(1)} %fusion.5.refs_0_, bf16[4,8,64,768]{3,2,1,0:T(8,128)(2,1)S(1)} %halves_of_rows.1.refs_1_, bf16[4,8,32,128]{3,2,1,0:T(8,128)(2,1)S(1)} %edge_half0.5.refs_2_.first_ref, bf16[4,8,32,128]{3,2,1,0:T(8,128)(2,1)S(1)} %collective-permute-done.12.refs_3_, ...), custom_call_target="tpu_custom_call" | custom-call | flops 20132659200 | bytes 157286400 | tf_op jit(solution)/shard_map/inner_half0/pallas_call | solution.py:178
  72.5 0.9 unpack.5
  73.5 1.8 %collective-permute-done.18.refs_5_ = bf16[3,8,32,128]{3,2,1,0:T(8,128)(2,1)S(1)} collective-permute-done((bf16[3,8,32,128]{3,2,1,0:T(8,128)(2,1)S(1)}, bf16[3,8,32,128]{3,2,1,0:T(8,128)(2,1)S(1)}, u32[]{:S(2)}, u32[]{:S(2)}) %collective-permute-start.18) | collective-permute-done | bytes 196640 | tf_op jit(solution)/shard_map/ppermute | solution.py:203
  75.3 1.8 %collective-permute-done.19.refs_6_ = bf16[3,8,32,128]{3,2,1,0:T(8,128)(2,1)S(1)} collective-permute-done((bf16[3,8,32,128]{3,2,1,0:T(8,128)(2,1)S(1)}, bf16[3,8,32,128]{3,2,1,0:T(8,128)(2,1)S(1)}, u32[]{:S(2)}, u32[]{:S(2)}) %collective-permute-start.19) | collective-permute-done | bytes 196640 | tf_op jit(solution)/shard_map/ppermute | solution.py:203
  77.0 1.5 %edge_half0.6.refs_2_.first_ref = bf16[4,8,32,128]{3,2,1,0:T(8,128)(2,1)S(1)} custom-call(s32[8,12]{1,0:T(8,128)S(1)} %fusion.5.refs_0_, bf16[4,8,64,768]{3,2,1,0:T(8,128)(2,1)S(1)} %halves_of_rows.1.refs_1_, bf16[4,8,32,128]{3,2,1,0:T(8,128)(2,1)S(1)} %edge_half0.5.refs_2_.first_ref, bf16[4,8,32,128]{3,2,1,0:T(8,128)(2,1)S(1)} %collective-permute-done.12.refs_3_, ...), custom_call_target="tpu_custom_call" | custom-call | flops 20132659200 | bytes 157286400 | tf_op jit(solution)/shard_map/edge_half0/pallas_call | solution.py:178
  78.5 3.6 %collective-permute-start.20 = (bf16[4,8,32,128]{3,2,1,0:T(8,128)(2,1)S(1)}, bf16[4,8,32,128]{3,2,1,0:T(8,128)(2,1)S(1)}, u32[]{:S(2)}, u32[]{:S(2)}) collective-permute-start(bf16[4,8,32,128]{3,2,1,0:T(8,128)(2,1)S(1)} %edge_half0.6.refs_2_.first_ref), channel_id=1, source_target_pairs={{1,0},{2,1},{3,2},{0,3},{5,4},{6,5},{7,6},{4,7},{9,8},{10,9},{11,1... | collective-permute-start | bytes 786440 | tf_op jit(solution)/shard_map/ppermute | solution.py:203
  82.2 1.1 collective-permute-start.24
  83.3 0.1 collective-permute-start.25
  83.4 1.5 %inner_half1.6.refs_7_.refs_8_ = bf16[2,8,32,128]{3,2,1,0:T(8,128)(2,1)S(1)} custom-call(s32[8,12]{1,0:T(8,128)S(1)} %fusion.5.refs_0_, bf16[4,8,64,768]{3,2,1,0:T(8,128)(2,1)S(1)} %halves_of_rows.1.refs_1_, bf16[4,8,32,128]{3,2,1,0:T(8,128)(2,1)S(1)} %edge_half1.5.second_ref.refs_2_, bf16[4,8,32,128]{3,2,1,0:T(8,128)(2,1)S(1)} %collective-permute-done.22.refs_3_, ...), custom_call_target="tpu_custom_call" | custom-call | flops 20132659200 | bytes 157286400 | tf_op jit(solution)/shard_map/inner_half1/pallas_call | solution.py:178
  84.9 3.0 %collective-permute-done.24.refs_5_ = bf16[3,8,32,128]{3,2,1,0:T(8,128)(2,1)S(1)} collective-permute-done((bf16[3,8,32,128]{3,2,1,0:T(8,128)(2,1)S(1)}, bf16[3,8,32,128]{3,2,1,0:T(8,128)(2,1)S(1)}, u32[]{:S(2)}, u32[]{:S(2)}) %collective-permute-start.24) | collective-permute-done | bytes 196640 | tf_op jit(solution)/shard_map/ppermute | solution.py:203
  87.8 1.5 %collective-permute-done.25.refs_6_ = bf16[3,8,32,128]{3,2,1,0:T(8,128)(2,1)S(1)} collective-permute-done((bf16[3,8,32,128]{3,2,1,0:T(8,128)(2,1)S(1)}, bf16[3,8,32,128]{3,2,1,0:T(8,128)(2,1)S(1)}, u32[]{:S(2)}, u32[]{:S(2)}) %collective-permute-start.25) | collective-permute-done | bytes 196640 | tf_op jit(solution)/shard_map/ppermute | solution.py:203
  89.4 1.5 %edge_half1.6.second_ref.refs_2_ = bf16[4,8,32,128]{3,2,1,0:T(8,128)(2,1)S(1)} custom-call(s32[8,12]{1,0:T(8,128)S(1)} %fusion.5.refs_0_, bf16[4,8,64,768]{3,2,1,0:T(8,128)(2,1)S(1)} %halves_of_rows.1.refs_1_, bf16[4,8,32,128]{3,2,1,0:T(8,128)(2,1)S(1)} %edge_half1.5.second_ref.refs_2_, bf16[4,8,32,128]{3,2,1,0:T(8,128)(2,1)S(1)} %collective-permute-done.22.refs_3_, ...), custom_call_target="tpu_custom_call" | custom-call | flops 20132659200 | bytes 157286400 | tf_op jit(solution)/shard_map/edge_half1/pallas_call | solution.py:178
  90.9 3.6 %collective-permute-start.28 = (bf16[2,8,32,128]{3,2,1,0:T(8,128)(2,1)S(1)}, bf16[2,8,32,128]{3,2,1,0:T(8,128)(2,1)S(1)}, u32[]{:S(2)}, u32[]{:S(2)}) collective-permute-start(bf16[2,8,32,128]{3,2,1,0:T(8,128)(2,1)S(1)} %pad_maximum_fusion.18), channel_id=1, source_target_pairs={{1,0},{2,1},{3,2},{0,3},{5,4},{6,5},{7,6},{4,7},{9,8},{10,9},{11,1... | collective-permute-start | bytes 393224 | tf_op jit(solution)/shard_map/ppermute | solution.py:203
  94.6 1.0 collective-permute-start.26
  95.7 0.1 collective-permute-start.27
  95.8 1.5 %inner_half0.7.refs_1_.refs_7_ = bf16[2,8,32,128]{3,2,1,0:T(8,128)(2,1)S(1)} custom-call(s32[8,12]{1,0:T(8,128)S(1)} %fusion.5.refs_0_, bf16[4,8,64,768]{3,2,1,0:T(8,128)(2,1)S(1)} %halves_of_rows.1.refs_1_, bf16[4,8,32,128]{3,2,1,0:T(8,128)(2,1)S(1)} %edge_half0.6.refs_2_.first_ref, bf16[4,8,32,128]{3,2,1,0:T(8,128)(2,1)S(1)} %collective-permute-done.20.refs_3_, ...), custom_call_target="tpu_custom_call" | custom-call | flops 20132659200 | bytes 157286400 | tf_op jit(solution)/shard_map/inner_half0/pallas_call | solution.py:178
  97.3 0.9 unpack.6
  98.2 3.5 %collective-permute-start.30 = (bf16[2,8,32,128]{3,2,1,0:T(8,128)(2,1)S(1)}, bf16[2,8,32,128]{3,2,1,0:T(8,128)(2,1)S(1)}, u32[]{:S(2)}, u32[]{:S(2)}) collective-permute-start(bf16[2,8,32,128]{3,2,1,0:T(8,128)(2,1)S(1)} %slice.222), channel_id=1, source_target_pairs={{1,0},{2,1},{3,2},{0,3},{5,4},{6,5},{7,6},{4,7},{9,8},{10,9},{11,1... | collective-permute-start | bytes 393224 | tf_op jit(solution)/shard_map/ppermute | solution.py:203
  101.8 2.4 %collective-permute-start.32 = (bf16[3,8,32,128]{3,2,1,0:T(8,128)(2,1)S(1)}, bf16[3,8,32,128]{3,2,1,0:T(8,128)(2,1)S(1)}, u32[]{:S(2)}, u32[]{:S(2)}) collective-permute-start(bf16[3,8,32,128]{3,2,1,0:T(8,128)(2,1)S(1)} %pad_maximum_fusion.16.refs_6_), channel_id=1, source_target_pairs={{4,0},{8,4},{12,8},{16,12},{20,16},{24,20},{28,24},{0,28},{5,1},{9... | collective-permute-start | bytes 589832 | tf_op jit(solution)/shard_map/ppermute | solution.py:203
  104.2 0.1 collective-permute-start.33
  104.3 1.5 %edge_half0.7.first_ref = bf16[4,8,32,128]{3,2,1,0:T(8,128)(2,1)S(1)} custom-call(s32[8,12]{1,0:T(8,128)S(1)} %fusion.5.refs_0_, bf16[4,8,64,768]{3,2,1,0:T(8,128)(2,1)S(1)} %halves_of_rows.1.refs_1_, bf16[4,8,32,128]{3,2,1,0:T(8,128)(2,1)S(1)} %edge_half0.6.refs_2_.first_ref, bf16[4,8,32,128]{3,2,1,0:T(8,128)(2,1)S(1)} %collective-permute-done.20.refs_3_, ...), custom_call_target="tpu_custom_call" | custom-call | flops 20132659200 | bytes 157286400 | tf_op jit(solution)/shard_map/edge_half0/pallas_call | solution.py:178
  105.8 2.7 %collective-permute-done.31 = bf16[2,8,32,128]{3,2,1,0:T(8,128)(2,1)S(1)} collective-permute-done((bf16[2,8,32,128]{3,2,1,0:T(8,128)(2,1)S(1)}, bf16[2,8,32,128]{3,2,1,0:T(8,128)(2,1)S(1)}, u32[]{:S(2)}, u32[]{:S(2)}) %collective-permute-start.31) | collective-permute-done | bytes 131104 | tf_op jit(solution)/shard_map/ppermute | solution.py:203
  108.6 1.5 %inner_half1.7.refs_7_.refs_8_ = bf16[2,8,32,128]{3,2,1,0:T(8,128)(2,1)S(1)} custom-call(s32[8,12]{1,0:T(8,128)S(1)} %fusion.5.refs_0_, bf16[4,8,64,768]{3,2,1,0:T(8,128)(2,1)S(1)} %halves_of_rows.1.refs_1_, bf16[4,8,32,128]{3,2,1,0:T(8,128)(2,1)S(1)} %edge_half1.6.second_ref.refs_2_, bf16[4,8,32,128]{3,2,1,0:T(8,128)(2,1)S(1)} %pad_maximum_fusion.refs_3_, ...), custom_call_target="tpu_custom_call" | custom-call | flops 20132659200 | bytes 157286400 | tf_op jit(solution)/shard_map/inner_half1/pallas_call | solution.py:178
  110.1 0.1 collective-permute-done.33.refs_6_
  110.3 1.5 %edge_half1.7.second_ref = bf16[4,8,32,128]{3,2,1,0:T(8,128)(2,1)S(1)} custom-call(s32[8,12]{1,0:T(8,128)S(1)} %fusion.5.refs_0_, bf16[4,8,64,768]{3,2,1,0:T(8,128)(2,1)S(1)} %halves_of_rows.1.refs_1_, bf16[4,8,32,128]{3,2,1,0:T(8,128)(2,1)S(1)} %edge_half1.6.second_ref.refs_2_, bf16[4,8,32,128]{3,2,1,0:T(8,128)(2,1)S(1)} %pad_maximum_fusion.refs_3_, ...), custom_call_target="tpu_custom_call" | custom-call | flops 20132659200 | bytes 157286400 | tf_op jit(solution)/shard_map/edge_half1/pallas_call | solution.py:178
  111.7 1.5 %unpack.7 = (bf16[4,4,8,64,128]{4,3,2,1,0:T(8,128)(2,1)}, f32[8,128]{1,0:T(8,128)}) custom-call(bf16[4,8,32,128]{3,2,1,0:T(8,128)(2,1)S(1)} %edge_half0.7.first_ref, bf16[4,8,32,128]{3,2,1,0:T(8,128)(2,1)S(1)} %edge_half1.7.second_ref, bf16[4,4,8,64,128]{4,3,2,1,0:T(8,128)(2,1)} %get-tuple-element.79.refs_0_), custom_call_target="tpu_custom_call", output_to_operand_aliasing={{0}: (2, {})} | custom-call | tf_op jit(solution)/shard_map/unpack/pallas_call | solution.py:77
  (79 shorter events, 0.9 us)
Async XLA Ops:
  0.0 1.0 copy-start.1
  1.2 13.6 %collective-permute-start = (bf16[4,8,32,128]{3,2,1,0:T(8,128)(2,1)S(1)}, bf16[4,8,32,128]{3,2,1,0:T(8,128)(2,1)S(1)}, u32[]{:S(2)}, u32[]{:S(2)}) collective-permute-start(bf16[4,8,32,128]{3,2,1,0:T(8,128)(2,1)S(1)} %get-tuple-element.45.refs_2_), channel_id=1, source_target_pairs={{1,0},{2,1},{3,2},{0,3},{5,4},{6,5},{7,6},{4,7},{9,8},{10,9},{11,1... | collective-permute-start | bytes 786440 | tf_op jit(solution)/shard_map/ppermute | solution.py:203
  6.3 13.3 %collective-permute-start.1 = (bf16[4,8,32,128]{3,2,1,0:T(8,128)(2,1)S(1)}, bf16[4,8,32,128]{3,2,1,0:T(8,128)(2,1)S(1)}, u32[]{:S(2)}, u32[]{:S(2)}) collective-permute-start(bf16[4,8,32,128]{3,2,1,0:T(8,128)(2,1)S(1)} %get-tuple-element.45.refs_2_), channel_id=1, source_target_pairs={{0,1},{1,2},{2,3},{3,0},{4,5},{5,6},{6,7},{7,4},{8,9},{9,10},{10,1... | collective-permute-start | bytes 786440 | tf_op jit(solution)/shard_map/ppermute | solution.py:203
  6.3 26.0 %collective-permute-start.6 = (bf16[4,8,32,128]{3,2,1,0:T(8,128)(2,1)S(1)}, bf16[4,8,32,128]{3,2,1,0:T(8,128)(2,1)S(1)}, u32[]{:S(2)}, u32[]{:S(2)}) collective-permute-start(bf16[4,8,32,128]{3,2,1,0:T(8,128)(2,1)S(1)} %get-tuple-element.49.refs_2_), channel_id=1, source_target_pairs={{1,0},{2,1},{3,2},{0,3},{5,4},{6,5},{7,6},{4,7},{9,8},{10,9},{11,1... | collective-permute-start | bytes 786440 | tf_op jit(solution)/shard_map/ppermute | solution.py:203
  10.1 22.2 %collective-permute-start.7 = (bf16[4,8,32,128]{3,2,1,0:T(8,128)(2,1)S(1)}, bf16[4,8,32,128]{3,2,1,0:T(8,128)(2,1)S(1)}, u32[]{:S(2)}, u32[]{:S(2)}) collective-permute-start(bf16[4,8,32,128]{3,2,1,0:T(8,128)(2,1)S(1)} %get-tuple-element.49.refs_2_), channel_id=1, source_target_pairs={{0,1},{1,2},{2,3},{3,0},{4,5},{5,6},{6,7},{7,4},{8,9},{9,10},{10,1... | collective-permute-start | bytes 786440 | tf_op jit(solution)/shard_map/ppermute | solution.py:203
  10.1 1.9 %copy-start = (bf16[4,1,8,64,768]{4,3,2,1,0:T(8,128)(2,1)S(1)}, bf16[4,1,8,64,768]{4,3,2,1,0:T(8,128)(2,1)}, u32[]{:S(2)}) copy-start(bf16[4,1,8,64,768]{4,3,2,1,0:T(8,128)(2,1)} %param.4) | copy-start | bytes 9437188
  12.0 2.7 %copy-start.2 = (s32[1,8,12]{2,1,0:T(8,128)S(1)}, s32[1,8,12]{2,1,0:T(8,128)}, u32[]{:S(2)}) copy-start(s32[1,8,12]{2,1,0:T(8,128)} %param.5) | copy-start | bytes 1156
  19.7 4.3 %collective-permute-start.2 = (bf16[3,8,32,128]{3,2,1,0:T(8,128)(2,1)S(1)}, bf16[3,8,32,128]{3,2,1,0:T(8,128)(2,1)S(1)}, u32[]{:S(2)}, u32[]{:S(2)}) collective-permute-start(bf16[3,8,32,128]{3,2,1,0:T(8,128)(2,1)S(1)} %pad_maximum_fusion.2.refs_6_), channel_id=1, source_target_pairs={{4,0},{8,4},{12,8},{16,12},{20,16},{24,20},{28,24},{0,28},{5,1},{9... | collective-permute-start | bytes 589832 | tf_op jit(solution)/shard_map/ppermute | solution.py:203
  19.8 8.1 %collective-permute-start.3 = (bf16[3,8,32,128]{3,2,1,0:T(8,128)(2,1)S(1)}, bf16[3,8,32,128]{3,2,1,0:T(8,128)(2,1)S(1)}, u32[]{:S(2)}, u32[]{:S(2)}) collective-permute-start(bf16[3,8,32,128]{3,2,1,0:T(8,128)(2,1)S(1)} %pad_maximum_fusion.3.refs_5_), channel_id=1, source_target_pairs={{0,4},{4,8},{8,12},{12,16},{16,20},{20,24},{24,28},{28,0},{1,5},{5... | collective-permute-start | bytes 589832 | tf_op jit(solution)/shard_map/ppermute | solution.py:203
  29.4 15.4 %collective-permute-start.4 = (bf16[4,8,32,128]{3,2,1,0:T(8,128)(2,1)S(1)}, bf16[4,8,32,128]{3,2,1,0:T(8,128)(2,1)S(1)}, u32[]{:S(2)}, u32[]{:S(2)}) collective-permute-start(bf16[4,8,32,128]{3,2,1,0:T(8,128)(2,1)S(1)} %edge_half0.4.refs_2_.first_ref), channel_id=1, source_target_pairs={{1,0},{2,1},{3,2},{0,3},{5,4},{6,5},{7,6},{4,7},{9,8},{10,9},{11,1... | collective-permute-start | bytes 786440 | tf_op jit(solution)/shard_map/ppermute | solution.py:203
  32.4 12.5 %collective-permute-start.5 = (bf16[4,8,32,128]{3,2,1,0:T(8,128)(2,1)S(1)}, bf16[4,8,32,128]{3,2,1,0:T(8,128)(2,1)S(1)}, u32[]{:S(2)}, u32[]{:S(2)}) collective-permute-start(bf16[4,8,32,128]{3,2,1,0:T(8,128)(2,1)S(1)} %edge_half0.4.refs_2_.first_ref), channel_id=1, source_target_pairs={{0,1},{1,2},{2,3},{3,0},{4,5},{5,6},{6,7},{7,4},{8,9},{9,10},{10,1... | collective-permute-start | bytes 786440 | tf_op jit(solution)/shard_map/ppermute | solution.py:203
  32.5 5.3 %collective-permute-start.8 = (bf16[3,8,32,128]{3,2,1,0:T(8,128)(2,1)S(1)}, bf16[3,8,32,128]{3,2,1,0:T(8,128)(2,1)S(1)}, u32[]{:S(2)}, u32[]{:S(2)}) collective-permute-start(bf16[3,8,32,128]{3,2,1,0:T(8,128)(2,1)S(1)} %pad_maximum_fusion.4.refs_6_), channel_id=1, source_target_pairs={{4,0},{8,4},{12,8},{16,12},{20,16},{24,20},{28,24},{0,28},{5,1},{9... | collective-permute-start | bytes 589832 | tf_op jit(solution)/shard_map/ppermute | solution.py:203
  32.6 7.2 %collective-permute-start.9 = (bf16[3,8,32,128]{3,2,1,0:T(8,128)(2,1)S(1)}, bf16[3,8,32,128]{3,2,1,0:T(8,128)(2,1)S(1)}, u32[]{:S(2)}, u32[]{:S(2)}) collective-permute-start(bf16[3,8,32,128]{3,2,1,0:T(8,128)(2,1)S(1)} %pad_maximum_fusion.5.refs_5_), channel_id=1, source_target_pairs={{0,4},{4,8},{8,12},{12,16},{16,20},{20,24},{24,28},{28,0},{1,5},{5... | collective-permute-start | bytes 589832 | tf_op jit(solution)/shard_map/ppermute | solution.py:203
  41.2 15.7 %collective-permute-start.14 = (bf16[4,8,32,128]{3,2,1,0:T(8,128)(2,1)S(1)}, bf16[4,8,32,128]{3,2,1,0:T(8,128)(2,1)S(1)}, u32[]{:S(2)}, u32[]{:S(2)}) collective-permute-start(bf16[4,8,32,128]{3,2,1,0:T(8,128)(2,1)S(1)} %edge_half1.4.second_ref.refs_2_), channel_id=1, source_target_pairs={{1,0},{2,1},{3,2},{0,3},{5,4},{6,5},{7,6},{4,7},{9,8},{10,9},{11,1... | collective-permute-start | bytes 786440 | tf_op jit(solution)/shard_map/ppermute | solution.py:203
  44.8 12.1 %collective-permute-start.15 = (bf16[4,8,32,128]{3,2,1,0:T(8,128)(2,1)S(1)}, bf16[4,8,32,128]{3,2,1,0:T(8,128)(2,1)S(1)}, u32[]{:S(2)}, u32[]{:S(2)}) collective-permute-start(bf16[4,8,32,128]{3,2,1,0:T(8,128)(2,1)S(1)} %edge_half1.4.second_ref.refs_2_), channel_id=1, source_target_pairs={{0,1},{1,2},{2,3},{3,0},{4,5},{5,6},{6,7},{7,4},{8,9},{9,10},{10,1... | collective-permute-start | bytes 786440 | tf_op jit(solution)/shard_map/ppermute | solution.py:203
  44.9 5.5 %collective-permute-start.10 = (bf16[3,8,32,128]{3,2,1,0:T(8,128)(2,1)S(1)}, bf16[3,8,32,128]{3,2,1,0:T(8,128)(2,1)S(1)}, u32[]{:S(2)}, u32[]{:S(2)}) collective-permute-start(bf16[3,8,32,128]{3,2,1,0:T(8,128)(2,1)S(1)} %pad_maximum_fusion.6.refs_6_), channel_id=1, source_target_pairs={{4,0},{8,4},{12,8},{16,12},{20,16},{24,20},{28,24},{0,28},{5,1},{9... | collective-permute-start | bytes 589832 | tf_op jit(solution)/shard_map/ppermute | solution.py:203
  45.8 6.0 %collective-permute-start.11 = (bf16[3,8,32,128]{3,2,1,0:T(8,128)(2,1)S(1)}, bf16[3,8,32,128]{3,2,1,0:T(8,128)(2,1)S(1)}, u32[]{:S(2)}, u32[]{:S(2)}) collective-permute-start(bf16[3,8,32,128]{3,2,1,0:T(8,128)(2,1)S(1)} %pad_maximum_fusion.7.refs_5_), channel_id=1, source_target_pairs={{0,4},{4,8},{8,12},{12,16},{16,20},{20,24},{24,28},{28,0},{1,5},{5... | collective-permute-start | bytes 589832 | tf_op jit(solution)/shard_map/ppermute | solution.py:203
  53.3 16.3 %collective-permute-start.12 = (bf16[4,8,32,128]{3,2,1,0:T(8,128)(2,1)S(1)}, bf16[4,8,32,128]{3,2,1,0:T(8,128)(2,1)S(1)}, u32[]{:S(2)}, u32[]{:S(2)}) collective-permute-start(bf16[4,8,32,128]{3,2,1,0:T(8,128)(2,1)S(1)} %edge_half0.5.refs_2_.first_ref), channel_id=1, source_target_pairs={{1,0},{2,1},{3,2},{0,3},{5,4},{6,5},{7,6},{4,7},{9,8},{10,9},{11,1... | collective-permute-start | bytes 786440 | tf_op jit(solution)/shard_map/ppermute | solution.py:203
  56.9 12.7 %collective-permute-start.13 = (bf16[4,8,32,128]{3,2,1,0:T(8,128)(2,1)S(1)}, bf16[4,8,32,128]{3,2,1,0:T(8,128)(2,1)S(1)}, u32[]{:S(2)}, u32[]{:S(2)}) collective-permute-start(bf16[4,8,32,128]{3,2,1,0:T(8,128)(2,1)S(1)} %edge_half0.5.refs_2_.first_ref), channel_id=1, source_target_pairs={{0,1},{1,2},{2,3},{3,0},{4,5},{5,6},{6,7},{7,4},{8,9},{9,10},{10,1... | collective-permute-start | bytes 786440 | tf_op jit(solution)/shard_map/ppermute | solution.py:203
  57.0 5.9 %collective-permute-start.16 = (bf16[3,8,32,128]{3,2,1,0:T(8,128)(2,1)S(1)}, bf16[3,8,32,128]{3,2,1,0:T(8,128)(2,1)S(1)}, u32[]{:S(2)}, u32[]{:S(2)}) collective-permute-start(bf16[3,8,32,128]{3,2,1,0:T(8,128)(2,1)S(1)} %pad_maximum_fusion.8.refs_6_), channel_id=1, source_target_pairs={{4,0},{8,4},{12,8},{16,12},{20,16},{24,20},{28,24},{0,28},{5,1},{9... | collective-permute-start | bytes 589832 | tf_op jit(solution)/shard_map/ppermute | solution.py:203
  58.5 6.0 %collective-permute-start.17 = (bf16[3,8,32,128]{3,2,1,0:T(8,128)(2,1)S(1)}, bf16[3,8,32,128]{3,2,1,0:T(8,128)(2,1)S(1)}, u32[]{:S(2)}, u32[]{:S(2)}) collective-permute-start(bf16[3,8,32,128]{3,2,1,0:T(8,128)(2,1)S(1)} %pad_maximum_fusion.9.refs_5_), channel_id=1, source_target_pairs={{0,4},{4,8},{8,12},{12,16},{16,20},{20,24},{24,28},{28,0},{1,5},{5... | collective-permute-start | bytes 589832 | tf_op jit(solution)/shard_map/ppermute | solution.py:203
  66.0 16.1 %collective-permute-start.22 = (bf16[4,8,32,128]{3,2,1,0:T(8,128)(2,1)S(1)}, bf16[4,8,32,128]{3,2,1,0:T(8,128)(2,1)S(1)}, u32[]{:S(2)}, u32[]{:S(2)}) collective-permute-start(bf16[4,8,32,128]{3,2,1,0:T(8,128)(2,1)S(1)} %edge_half1.5.second_ref.refs_2_), channel_id=1, source_target_pairs={{1,0},{2,1},{3,2},{0,3},{5,4},{6,5},{7,6},{4,7},{9,8},{10,9},{11,1... | collective-permute-start | bytes 786440 | tf_op jit(solution)/shard_map/ppermute | solution.py:203
  69.6 12.5 %collective-permute-start.23 = (bf16[4,8,32,128]{3,2,1,0:T(8,128)(2,1)S(1)}, bf16[4,8,32,128]{3,2,1,0:T(8,128)(2,1)S(1)}, u32[]{:S(2)}, u32[]{:S(2)}) collective-permute-start(bf16[4,8,32,128]{3,2,1,0:T(8,128)(2,1)S(1)} %edge_half1.5.second_ref.refs_2_), channel_id=1, source_target_pairs={{0,1},{1,2},{2,3},{3,0},{4,5},{5,6},{6,7},{7,4},{8,9},{9,10},{10,1... | collective-permute-start | bytes 786440 | tf_op jit(solution)/shard_map/ppermute | solution.py:203
  69.7 5.5 %collective-permute-start.18 = (bf16[3,8,32,128]{3,2,1,0:T(8,128)(2,1)S(1)}, bf16[3,8,32,128]{3,2,1,0:T(8,128)(2,1)S(1)}, u32[]{:S(2)}, u32[]{:S(2)}) collective-permute-start(bf16[3,8,32,128]{3,2,1,0:T(8,128)(2,1)S(1)} %pad_maximum_fusion.10.refs_6_), channel_id=1, source_target_pairs={{4,0},{8,4},{12,8},{16,12},{20,16},{24,20},{28,24},{0,28},{5,1},{9... | collective-permute-start | bytes 589832 | tf_op jit(solution)/shard_map/ppermute | solution.py:203
  71.0 6.0 %collective-permute-start.19 = (bf16[3,8,32,128]{3,2,1,0:T(8,128)(2,1)S(1)}, bf16[3,8,32,128]{3,2,1,0:T(8,128)(2,1)S(1)}, u32[]{:S(2)}, u32[]{:S(2)}) collective-permute-start(bf16[3,8,32,128]{3,2,1,0:T(8,128)(2,1)S(1)} %pad_maximum_fusion.11.refs_5_), channel_id=1, source_target_pairs={{0,4},{4,8},{8,12},{12,16},{16,20},{20,24},{24,28},{28,0},{1,5},{5... | collective-permute-start | bytes 589832 | tf_op jit(solution)/shard_map/ppermute | solution.py:203
  78.5 16.0 %collective-permute-start.20 = (bf16[4,8,32,128]{3,2,1,0:T(8,128)(2,1)S(1)}, bf16[4,8,32,128]{3,2,1,0:T(8,128)(2,1)S(1)}, u32[]{:S(2)}, u32[]{:S(2)}) collective-permute-start(bf16[4,8,32,128]{3,2,1,0:T(8,128)(2,1)S(1)} %edge_half0.6.refs_2_.first_ref), channel_id=1, source_target_pairs={{1,0},{2,1},{3,2},{0,3},{5,4},{6,5},{7,6},{4,7},{9,8},{10,9},{11,1... | collective-permute-start | bytes 786440 | tf_op jit(solution)/shard_map/ppermute | solution.py:203
  82.1 12.4 %collective-permute-start.21 = (bf16[4,8,32,128]{3,2,1,0:T(8,128)(2,1)S(1)}, bf16[4,8,32,128]{3,2,1,0:T(8,128)(2,1)S(1)}, u32[]{:S(2)}, u32[]{:S(2)}) collective-permute-start(bf16[4,8,32,128]{3,2,1,0:T(8,128)(2,1)S(1)} %edge_half0.6.refs_2_.first_ref), channel_id=1, source_target_pairs={{0,1},{1,2},{2,3},{3,0},{4,5},{5,6},{6,7},{7,4},{8,9},{9,10},{10,1... | collective-permute-start | bytes 786440 | tf_op jit(solution)/shard_map/ppermute | solution.py:203
  82.2 5.6 %collective-permute-start.24 = (bf16[3,8,32,128]{3,2,1,0:T(8,128)(2,1)S(1)}, bf16[3,8,32,128]{3,2,1,0:T(8,128)(2,1)S(1)}, u32[]{:S(2)}, u32[]{:S(2)}) collective-permute-start(bf16[3,8,32,128]{3,2,1,0:T(8,128)(2,1)S(1)} %pad_maximum_fusion.12.refs_6_), channel_id=1, source_target_pairs={{4,0},{8,4},{12,8},{16,12},{20,16},{24,20},{28,24},{0,28},{5,1},{9... | collective-permute-start | bytes 589832 | tf_op jit(solution)/shard_map/ppermute | solution.py:203
  83.3 6.0 %collective-permute-start.25 = (bf16[3,8,32,128]{3,2,1,0:T(8,128)(2,1)S(1)}, bf16[3,8,32,128]{3,2,1,0:T(8,128)(2,1)S(1)}, u32[]{:S(2)}, u32[]{:S(2)}) collective-permute-start(bf16[3,8,32,128]{3,2,1,0:T(8,128)(2,1)S(1)} %pad_maximum_fusion.13.refs_5_), channel_id=1, source_target_pairs={{0,4},{4,8},{8,12},{12,16},{16,20},{20,24},{24,28},{28,0},{1,5},{5... | collective-permute-start | bytes 589832 | tf_op jit(solution)/shard_map/ppermute | solution.py:203
  90.9 10.8 %collective-permute-start.28 = (bf16[2,8,32,128]{3,2,1,0:T(8,128)(2,1)S(1)}, bf16[2,8,32,128]{3,2,1,0:T(8,128)(2,1)S(1)}, u32[]{:S(2)}, u32[]{:S(2)}) collective-permute-start(bf16[2,8,32,128]{3,2,1,0:T(8,128)(2,1)S(1)} %pad_maximum_fusion.18), channel_id=1, source_target_pairs={{1,0},{2,1},{3,2},{0,3},{5,4},{6,5},{7,6},{4,7},{9,8},{10,9},{11,1... | collective-permute-start | bytes 393224 | tf_op jit(solution)/shard_map/ppermute | solution.py:203
  94.5 7.2 %collective-permute-start.29 = (bf16[2,8,32,128]{3,2,1,0:T(8,128)(2,1)S(1)}, bf16[2,8,32,128]{3,2,1,0:T(8,128)(2,1)S(1)}, u32[]{:S(2)}, u32[]{:S(2)}) collective-permute-start(bf16[2,8,32,128]{3,2,1,0:T(8,128)(2,1)S(1)} %pad_maximum_fusion.18), channel_id=1, source_target_pairs={{0,1},{1,2},{2,3},{3,0},{4,5},{5,6},{6,7},{7,4},{8,9},{9,10},{10,1... | collective-permute-start | bytes 393224 | tf_op jit(solution)/shard_map/ppermute | solution.py:203
  94.6 9.6 %collective-permute-start.26 = (bf16[3,8,32,128]{3,2,1,0:T(8,128)(2,1)S(1)}, bf16[3,8,32,128]{3,2,1,0:T(8,128)(2,1)S(1)}, u32[]{:S(2)}, u32[]{:S(2)}) collective-permute-start(bf16[3,8,32,128]{3,2,1,0:T(8,128)(2,1)S(1)} %pad_maximum_fusion.14.refs_6_), channel_id=1, source_target_pairs={{4,0},{8,4},{12,8},{16,12},{20,16},{24,20},{28,24},{0,28},{5,1},{9... | collective-permute-start | bytes 589832 | tf_op jit(solution)/shard_map/ppermute | solution.py:203
  95.7 8.6 %collective-permute-start.27 = (bf16[3,8,32,128]{3,2,1,0:T(8,128)(2,1)S(1)}, bf16[3,8,32,128]{3,2,1,0:T(8,128)(2,1)S(1)}, u32[]{:S(2)}, u32[]{:S(2)}) collective-permute-start(bf16[3,8,32,128]{3,2,1,0:T(8,128)(2,1)S(1)} %pad_maximum_fusion.15.refs_5_), channel_id=1, source_target_pairs={{0,4},{4,8},{8,12},{12,16},{16,20},{20,24},{24,28},{28,0},{1,5},{5... | collective-permute-start | bytes 589832 | tf_op jit(solution)/shard_map/ppermute | solution.py:203
  98.2 7.6 %collective-permute-start.30 = (bf16[2,8,32,128]{3,2,1,0:T(8,128)(2,1)S(1)}, bf16[2,8,32,128]{3,2,1,0:T(8,128)(2,1)S(1)}, u32[]{:S(2)}, u32[]{:S(2)}) collective-permute-start(bf16[2,8,32,128]{3,2,1,0:T(8,128)(2,1)S(1)} %slice.222), channel_id=1, source_target_pairs={{1,0},{2,1},{3,2},{0,3},{5,4},{6,5},{7,6},{4,7},{9,8},{10,9},{11,1... | collective-permute-start | bytes 393224 | tf_op jit(solution)/shard_map/ppermute | solution.py:203
  101.7 6.8 %collective-permute-start.31 = (bf16[2,8,32,128]{3,2,1,0:T(8,128)(2,1)S(1)}, bf16[2,8,32,128]{3,2,1,0:T(8,128)(2,1)S(1)}, u32[]{:S(2)}, u32[]{:S(2)}) collective-permute-start(bf16[2,8,32,128]{3,2,1,0:T(8,128)(2,1)S(1)} %slice.222), channel_id=1, source_target_pairs={{0,1},{1,2},{2,3},{3,0},{4,5},{5,6},{6,7},{7,4},{8,9},{9,10},{10,1... | collective-permute-start | bytes 393224 | tf_op jit(solution)/shard_map/ppermute | solution.py:203
  101.8 8.3 %collective-permute-start.32 = (bf16[3,8,32,128]{3,2,1,0:T(8,128)(2,1)S(1)}, bf16[3,8,32,128]{3,2,1,0:T(8,128)(2,1)S(1)}, u32[]{:S(2)}, u32[]{:S(2)}) collective-permute-start(bf16[3,8,32,128]{3,2,1,0:T(8,128)(2,1)S(1)} %pad_maximum_fusion.16.refs_6_), channel_id=1, source_target_pairs={{4,0},{8,4},{12,8},{16,12},{20,16},{24,20},{28,24},{0,28},{5,1},{9... | collective-permute-start | bytes 589832 | tf_op jit(solution)/shard_map/ppermute | solution.py:203
  104.2 6.0 %collective-permute-start.33 = (bf16[3,8,32,128]{3,2,1,0:T(8,128)(2,1)S(1)}, bf16[3,8,32,128]{3,2,1,0:T(8,128)(2,1)S(1)}, u32[]{:S(2)}, u32[]{:S(2)}) collective-permute-start(bf16[3,8,32,128]{3,2,1,0:T(8,128)(2,1)S(1)} %pad_maximum_fusion.17.refs_5_), channel_id=1, source_target_pairs={{0,4},{4,8},{8,12},{12,16},{16,20},{20,24},{24,28},{28,0},{1,5},{5... | collective-permute-start | bytes 589832 | tf_op jit(solution)/shard_map/ppermute | solution.py:203

commit v15 on v14

--- a/solution.py
+++ b/solution.py
@@ -129,7 +129,7 @@
 
     lax.fori_loop(0, columns, enter, 0)
     if edge:
-        high_st, low_st, before = refs[5:8]
+        low_st, high_st, before = refs[5:8]
 
         def enter_stream(face, carry):
             for azim in range(3):
@@ -260,15 +260,16 @@
             if outer is None or h < HALVES - 1:
                 to_low, to_high = edges(*pieces[h], latest)
             else:
-                own_inner, _ = lax.optimization_barrier((current[h][1:-1], middle))
+                own_inner, _ = lax.optimization_barrier((current[h][1:-1], packed))
                 inner = from_neighbours(own_inner)
                 to_low, to_high = edges(*outer, middle)
                 pieces[h] = joined(current[h], outer, inner, latest)
-            stream = (shift(to_low, "stream", False), shift(to_high, "stream", True))
-            middle = part(h, table, blocks, pieces[h], (to_high, to_low))
+            packed = to_high
+            stream = (shift(to_high, "stream", True), shift(to_low, "stream", False))
+            middle = part(h, table, blocks, pieces[h], (to_low, to_high))
             after = middle
-            if h == 0 and index > 0:
-                basis, after = unpack(index - 1, every, *previous, basis, middle)
+            if index > 0 and h == (index == STEPS - 1):
+                basis, after = unpack(index - 1, every, *previous, basis, latest if h else middle)
             current[h] = latest = part(h, table, blocks, pieces[h], (*stream, middle, after))
             if index == STEPS - 2 and h == HALVES - 1:
                 outer = from_neighbours(jnp.stack([current[h][0], current[h][-1]]))

time: 113 us -> 113 us (level)
  waiting for transfers between devices: 35.1 us -> 36.8 us
  starting transfers between devices: 42.9 us -> 41.3 us
    ppermute x34, waiting for transfers between devices: 35.1 us -> 36.8 us  [shift(): return lax.ppermute(value, axis, pairs)]
    ppermute x34, starting transfers between devices: 42.9 us -> 41.3 us  [shift(): return lax.ppermute(value, axis, pairs)]
where the time goes in v15:
time: 113 us
  starting transfers between devices  41.3 us (37%)
  waiting for transfers between devices  36.8 us (33%)
  Pallas kernels  30.7 us (27%)
  local copies, waits for them, and re-layouts  3.24 us (3%)
    ppermute x34, starting transfers between devices, shift(): return lax.ppermute(value, axis, pairs)  41.3 us
    ppermute x34, waiting for transfers between devices, shift(): return lax.ppermute(value, axis, pairs)  36.8 us
    pallas_call x16, Pallas kernels, part(): pl.pallas_call(functools.partial(part_kernel, half), in_specs=in_specs, o...  23.6 us
    pallas_call x4, Pallas kernels, unpack(): pl.pallas_call(functools.partial(unpack_kernel, index, chosen, skipped),...  4.25 us
    unnamed x6, local copies, waits for them, and re-layouts  2.93 us
    pallas_call x1, Pallas kernels, halves_of_rows(): pl.pallas_call(halves_kernel, in_specs=[VMEM], out_specs=VMEM, out_shape=...  2.72 us
  transfers between devices with their start and end apart: 34, of which 15 were waited for; matrix products, arithmetic and copies ran while one was open for 1% of the time, Pallas kernels for 24%

profile of v15, /device:TPU:0, one launch (start us, length us, event | category | flops | bytes accessed | tf_op | source)
XLA Modules:
  0.0 113.3 jit_solution(4732798958309731090)
XLA Ops:
  0.0 1.0 copy-done.1
  1.0 0.2 pack.1
  1.2 5.1 %collective-permute-start = (bf16[4,8,32,128]{3,2,1,0:T(8,128)(2,1)S(1)}, bf16[4,8,32,128]{3,2,1,0:T(8,128)(2,1)S(1)}, u32[]{:S(2)}, u32[]{:S(2)}) collective-permute-start(bf16[4,8,32,128]{3,2,1,0:T(8,128)(2,1)S(1)} %get-tuple-element.45.refs_2_), channel_id=1, source_target_pairs={{1,0},{2,1},{3,2},{0,3},{5,4},{6,5},{7,6},{4,7},{9,8},{10,9},{11,1... | collective-permute-start | bytes 786440 | tf_op jit(solution)/shard_map/ppermute | solution.py:203
  6.3 3.8 %collective-permute-start.6 = (bf16[4,8,32,128]{3,2,1,0:T(8,128)(2,1)S(1)}, bf16[4,8,32,128]{3,2,1,0:T(8,128)(2,1)S(1)}, u32[]{:S(2)}, u32[]{:S(2)}) collective-permute-start(bf16[4,8,32,128]{3,2,1,0:T(8,128)(2,1)S(1)} %get-tuple-element.49.refs_2_), channel_id=1, source_target_pairs={{1,0},{2,1},{3,2},{0,3},{5,4},{6,5},{7,6},{4,7},{9,8},{10,9},{11,1... | collective-permute-start | bytes 786440 | tf_op jit(solution)/shard_map/ppermute | solution.py:203
  10.2 1.9 %copy-done = bf16[4,1,8,64,768]{4,3,2,1,0:T(8,128)(2,1)S(1)} copy-done((bf16[4,1,8,64,768]{4,3,2,1,0:T(8,128)(2,1)S(1)}, bf16[4,1,8,64,768]{4,3,2,1,0:T(8,128)(2,1)}, u32[]{:S(2)}) %copy-start) | copy-done | bytes 3145752
  12.0 2.7 %halves_of_rows.1.refs_1_ = bf16[4,8,64,768]{3,2,1,0:T(8,128)(2,1)S(1)} custom-call(bf16[4,8,64,768]{3,2,1,0:T(8,128)(2,1)S(1)} %bitcast.29), custom_call_target="tpu_custom_call" | custom-call | tf_op jit(solution)/shard_map/halves_of_rows/pallas_call | solution.py:234
  14.8 4.8 %collective-permute-done.1.refs_4_ = bf16[4,8,32,128]{3,2,1,0:T(8,128)(2,1)S(1)} collective-permute-done((bf16[4,8,32,128]{3,2,1,0:T(8,128)(2,1)S(1)}, bf16[4,8,32,128]{3,2,1,0:T(8,128)(2,1)S(1)}, u32[]{:S(2)}, u32[]{:S(2)}) %collective-permute-start.1) | collective-permute-done | bytes 262176 | tf_op jit(solution)/shard_map/ppermute | solution.py:203
  19.7 0.1 collective-permute-start.3
  19.8 0.5 collective-permute-start.2
  20.3 1.5 %inner_half0.4.refs_7_.refs_8_ = bf16[2,8,32,128]{3,2,1,0:T(8,128)(2,1)S(1)} custom-call(s32[8,12]{1,0:T(8,128)S(1)} %fusion.5.refs_0_, bf16[4,8,64,768]{3,2,1,0:T(8,128)(2,1)S(1)} %halves_of_rows.1.refs_1_, bf16[4,8,32,128]{3,2,1,0:T(8,128)(2,1)S(1)} %get-tuple-element.45.refs_2_, bf16[4,8,32,128]{3,2,1,0:T(8,128)(2,1)S(1)} %collective-permute-done.refs_3_, ...), custom_call_target="tpu_custom_call" | custom-call | flops 20132659200 | bytes 157286400 | tf_op jit(solution)/shard_map/inner_half0/pallas_call | solution.py:178
  21.8 2.2 %collective-permute-done.3.refs_6_ = bf16[3,8,32,128]{3,2,1,0:T(8,128)(2,1)S(1)} collective-permute-done((bf16[3,8,32,128]{3,2,1,0:T(8,128)(2,1)S(1)}, bf16[3,8,32,128]{3,2,1,0:T(8,128)(2,1)S(1)}, u32[]{:S(2)}, u32[]{:S(2)}) %collective-permute-start.3) | collective-permute-done | bytes 196640 | tf_op jit(solution)/shard_map/ppermute | solution.py:203
  24.0 3.9 %collective-permute-done.2.refs_5_ = bf16[3,8,32,128]{3,2,1,0:T(8,128)(2,1)S(1)} collective-permute-done((bf16[3,8,32,128]{3,2,1,0:T(8,128)(2,1)S(1)}, bf16[3,8,32,128]{3,2,1,0:T(8,128)(2,1)S(1)}, u32[]{:S(2)}, u32[]{:S(2)}) %collective-permute-start.2) | collective-permute-done | bytes 196640 | tf_op jit(solution)/shard_map/ppermute | solution.py:203
  27.9 1.5 %edge_half0.4.refs_2_.first_ref = bf16[4,8,32,128]{3,2,1,0:T(8,128)(2,1)S(1)} custom-call(s32[8,12]{1,0:T(8,128)S(1)} %fusion.5.refs_0_, bf16[4,8,64,768]{3,2,1,0:T(8,128)(2,1)S(1)} %halves_of_rows.1.refs_1_, bf16[4,8,32,128]{3,2,1,0:T(8,128)(2,1)S(1)} %get-tuple-element.45.refs_2_, bf16[4,8,32,128]{3,2,1,0:T(8,128)(2,1)S(1)} %collective-permute-done.refs_3_, ...), custom_call_target="tpu_custom_call" | custom-call | flops 20132659200 | bytes 157286400 | tf_op jit(solution)/shard_map/edge_half0/pallas_call | solution.py:178
  29.4 3.0 %collective-permute-start.4 = (bf16[4,8,32,128]{3,2,1,0:T(8,128)(2,1)S(1)}, bf16[4,8,32,128]{3,2,1,0:T(8,128)(2,1)S(1)}, u32[]{:S(2)}, u32[]{:S(2)}) collective-permute-start(bf16[4,8,32,128]{3,2,1,0:T(8,128)(2,1)S(1)} %edge_half0.4.refs_2_.first_ref), channel_id=1, source_target_pairs={{1,0},{2,1},{3,2},{0,3},{5,4},{6,5},{7,6},{4,7},{9,8},{10,9},{11,1... | collective-permute-start | bytes 786440 | tf_op jit(solution)/shard_map/ppermute | solution.py:203
  32.5 0.1 collective-permute-start.9
  32.6 0.5 collective-permute-start.8
  33.1 1.5 %inner_half1.4.refs_7_.refs_8_ = bf16[2,8,32,128]{3,2,1,0:T(8,128)(2,1)S(1)} custom-call(s32[8,12]{1,0:T(8,128)S(1)} %fusion.5.refs_0_, bf16[4,8,64,768]{3,2,1,0:T(8,128)(2,1)S(1)} %halves_of_rows.1.refs_1_, bf16[4,8,32,128]{3,2,1,0:T(8,128)(2,1)S(1)} %get-tuple-element.49.refs_2_, bf16[4,8,32,128]{3,2,1,0:T(8,128)(2,1)S(1)} %collective-permute-done.6.refs_3_, ...), custom_call_target="tpu_custom_call" | custom-call | flops 20132659200 | bytes 157286400 | tf_op jit(solution)/shard_map/inner_half1/pallas_call | solution.py:178
  34.6 3.1 %collective-permute-done.9.refs_6_ = bf16[3,8,32,128]{3,2,1,0:T(8,128)(2,1)S(1)} collective-permute-done((bf16[3,8,32,128]{3,2,1,0:T(8,128)(2,1)S(1)}, bf16[3,8,32,128]{3,2,1,0:T(8,128)(2,1)S(1)}, u32[]{:S(2)}, u32[]{:S(2)}) %collective-permute-start.9) | collective-permute-done | bytes 196640 | tf_op jit(solution)/shard_map/ppermute | solution.py:203
  37.7 2.0 %collective-permute-done.8.refs_5_ = bf16[3,8,32,128]{3,2,1,0:T(8,128)(2,1)S(1)} collective-permute-done((bf16[3,8,32,128]{3,2,1,0:T(8,128)(2,1)S(1)}, bf16[3,8,32,128]{3,2,1,0:T(8,128)(2,1)S(1)}, u32[]{:S(2)}, u32[]{:S(2)}) %collective-permute-start.8) | collective-permute-done | bytes 196640 | tf_op jit(solution)/shard_map/ppermute | solution.py:203
  39.8 1.5 %edge_half1.4.second_ref.refs_2_ = bf16[4,8,32,128]{3,2,1,0:T(8,128)(2,1)S(1)} custom-call(s32[8,12]{1,0:T(8,128)S(1)} %fusion.5.refs_0_, bf16[4,8,64,768]{3,2,1,0:T(8,128)(2,1)S(1)} %halves_of_rows.1.refs_1_, bf16[4,8,32,128]{3,2,1,0:T(8,128)(2,1)S(1)} %get-tuple-element.49.refs_2_, bf16[4,8,32,128]{3,2,1,0:T(8,128)(2,1)S(1)} %collective-permute-done.6.refs_3_, ...), custom_call_target="tpu_custom_call" | custom-call | flops 20132659200 | bytes 157286400 | tf_op jit(solution)/shard_map/edge_half1/pallas_call | solution.py:178
  41.2 3.6 %collective-permute-start.14 = (bf16[4,8,32,128]{3,2,1,0:T(8,128)(2,1)S(1)}, bf16[4,8,32,128]{3,2,1,0:T(8,128)(2,1)S(1)}, u32[]{:S(2)}, u32[]{:S(2)}) collective-permute-start(bf16[4,8,32,128]{3,2,1,0:T(8,128)(2,1)S(1)} %edge_half1.4.second_ref.refs_2_), channel_id=1, source_target_pairs={{1,0},{2,1},{3,2},{0,3},{5,4},{6,5},{7,6},{4,7},{9,8},{10,9},{11,1... | collective-permute-start | bytes 786440 | tf_op jit(solution)/shard_map/ppermute | solution.py:203
  44.9 0.8 collective-permute-start.11
  45.8 0.1 collective-permute-start.10
  45.9 1.5 %inner_half0.5.refs_0_.refs_7_ = bf16[2,8,32,128]{3,2,1,0:T(8,128)(2,1)S(1)} custom-call(s32[8,12]{1,0:T(8,128)S(1)} %fusion.5.refs_0_, bf16[4,8,64,768]{3,2,1,0:T(8,128)(2,1)S(1)} %halves_of_rows.1.refs_1_, bf16[4,8,32,128]{3,2,1,0:T(8,128)(2,1)S(1)} %edge_half0.4.refs_2_.first_ref, bf16[4,8,32,128]{3,2,1,0:T(8,128)(2,1)S(1)} %collective-permute-done.4.refs_3_, ...), custom_call_target="tpu_custom_call" | custom-call | flops 20132659200 | bytes 157286400 | tf_op jit(solution)/shard_map/inner_half0/pallas_call | solution.py:178
  47.4 0.9 unpack.4
  48.3 2.2 %collective-permute-done.11.refs_6_ = bf16[3,8,32,128]{3,2,1,0:T(8,128)(2,1)S(1)} collective-permute-done((bf16[3,8,32,128]{3,2,1,0:T(8,128)(2,1)S(1)}, bf16[3,8,32,128]{3,2,1,0:T(8,128)(2,1)S(1)}, u32[]{:S(2)}, u32[]{:S(2)}) %collective-permute-start.11) | collective-permute-done | bytes 196640 | tf_op jit(solution)/shard_map/ppermute | solution.py:203
  50.4 1.4 %collective-permute-done.10.refs_5_ = bf16[3,8,32,128]{3,2,1,0:T(8,128)(2,1)S(1)} collective-permute-done((bf16[3,8,32,128]{3,2,1,0:T(8,128)(2,1)S(1)}, bf16[3,8,32,128]{3,2,1,0:T(8,128)(2,1)S(1)}, u32[]{:S(2)}, u32[]{:S(2)}) %collective-permute-start.10) | collective-permute-done | bytes 196640 | tf_op jit(solution)/shard_map/ppermute | solution.py:203
  51.9 1.5 %edge_half0.5.refs_2_.first_ref = bf16[4,8,32,128]{3,2,1,0:T(8,128)(2,1)S(1)} custom-call(s32[8,12]{1,0:T(8,128)S(1)} %fusion.5.refs_0_, bf16[4,8,64,768]{3,2,1,0:T(8,128)(2,1)S(1)} %halves_of_rows.1.refs_1_, bf16[4,8,32,128]{3,2,1,0:T(8,128)(2,1)S(1)} %edge_half0.4.refs_2_.first_ref, bf16[4,8,32,128]{3,2,1,0:T(8,128)(2,1)S(1)} %collective-permute-done.4.refs_3_, ...), custom_call_target="tpu_custom_call" | custom-call | flops 20132659200 | bytes 157286400 | tf_op jit(solution)/shard_map/edge_half0/pallas_call | solution.py:178
  53.3 3.6 %collective-permute-start.12 = (bf16[4,8,32,128]{3,2,1,0:T(8,128)(2,1)S(1)}, bf16[4,8,32,128]{3,2,1,0:T(8,128)(2,1)S(1)}, u32[]{:S(2)}, u32[]{:S(2)}) collective-permute-start(bf16[4,8,32,128]{3,2,1,0:T(8,128)(2,1)S(1)} %edge_half0.5.refs_2_.first_ref), channel_id=1, source_target_pairs={{1,0},{2,1},{3,2},{0,3},{5,4},{6,5},{7,6},{4,7},{9,8},{10,9},{11,1... | collective-permute-start | bytes 786440 | tf_op jit(solution)/shard_map/ppermute | solution.py:203
  57.1 1.4 %collective-permute-start.17 = (bf16[3,8,32,128]{3,2,1,0:T(8,128)(2,1)S(1)}, bf16[3,8,32,128]{3,2,1,0:T(8,128)(2,1)S(1)}, u32[]{:S(2)}, u32[]{:S(2)}) collective-permute-start(bf16[3,8,32,128]{3,2,1,0:T(8,128)(2,1)S(1)} %pad_maximum_fusion.9.refs_5_), channel_id=1, source_target_pairs={{4,0},{8,4},{12,8},{16,12},{20,16},{24,20},{28,24},{0,28},{5,1},{9... | collective-permute-start | bytes 589832 | tf_op jit(solution)/shard_map/ppermute | solution.py:203
  58.5 0.1 collective-permute-start.16
  58.6 1.5 %inner_half1.5.refs_7_.refs_8_ = bf16[2,8,32,128]{3,2,1,0:T(8,128)(2,1)S(1)} custom-call(s32[8,12]{1,0:T(8,128)S(1)} %fusion.5.refs_0_, bf16[4,8,64,768]{3,2,1,0:T(8,128)(2,1)S(1)} %halves_of_rows.1.refs_1_, bf16[4,8,32,128]{3,2,1,0:T(8,128)(2,1)S(1)} %edge_half1.4.second_ref.refs_2_, bf16[4,8,32,128]{3,2,1,0:T(8,128)(2,1)S(1)} %collective-permute-done.14.refs_3_, ...), custom_call_target="tpu_custom_call" | custom-call | flops 20132659200 | bytes 157286400 | tf_op jit(solution)/shard_map/inner_half1/pallas_call | solution.py:178
  60.1 2.9 %collective-permute-done.17.refs_6_ = bf16[3,8,32,128]{3,2,1,0:T(8,128)(2,1)S(1)} collective-permute-done((bf16[3,8,32,128]{3,2,1,0:T(8,128)(2,1)S(1)}, bf16[3,8,32,128]{3,2,1,0:T(8,128)(2,1)S(1)}, u32[]{:S(2)}, u32[]{:S(2)}) %collective-permute-start.17) | collective-permute-done | bytes 196640 | tf_op jit(solution)/shard_map/ppermute | solution.py:203
  63.0 1.6 %collective-permute-done.16.refs_5_ = bf16[3,8,32,128]{3,2,1,0:T(8,128)(2,1)S(1)} collective-permute-done((bf16[3,8,32,128]{3,2,1,0:T(8,128)(2,1)S(1)}, bf16[3,8,32,128]{3,2,1,0:T(8,128)(2,1)S(1)}, u32[]{:S(2)}, u32[]{:S(2)}) %collective-permute-start.16) | collective-permute-done | bytes 196640 | tf_op jit(solution)/shard_map/ppermute | solution.py:203
  64.6 1.5 %edge_half1.5.second_ref.refs_2_ = bf16[4,8,32,128]{3,2,1,0:T(8,128)(2,1)S(1)} custom-call(s32[8,12]{1,0:T(8,128)S(1)} %fusion.5.refs_0_, bf16[4,8,64,768]{3,2,1,0:T(8,128)(2,1)S(1)} %halves_of_rows.1.refs_1_, bf16[4,8,32,128]{3,2,1,0:T(8,128)(2,1)S(1)} %edge_half1.4.second_ref.refs_2_, bf16[4,8,32,128]{3,2,1,0:T(8,128)(2,1)S(1)} %collective-permute-done.14.refs_3_, ...), custom_call_target="tpu_custom_call" | custom-call | flops 20132659200 | bytes 157286400 | tf_op jit(solution)/shard_map/edge_half1/pallas_call | solution.py:178
  66.1 3.6 %collective-permute-start.22 = (bf16[4,8,32,128]{3,2,1,0:T(8,128)(2,1)S(1)}, bf16[4,8,32,128]{3,2,1,0:T(8,128)(2,1)S(1)}, u32[]{:S(2)}, u32[]{:S(2)}) collective-permute-start(bf16[4,8,32,128]{3,2,1,0:T(8,128)(2,1)S(1)} %edge_half1.5.second_ref.refs_2_), channel_id=1, source_target_pairs={{1,0},{2,1},{3,2},{0,3},{5,4},{6,5},{7,6},{4,7},{9,8},{10,9},{11,1... | collective-permute-start | bytes 786440 | tf_op jit(solution)/shard_map/ppermute | solution.py:203
  69.8 1.3 %collective-permute-start.19 = (bf16[3,8,32,128]{3,2,1,0:T(8,128)(2,1)S(1)}, bf16[3,8,32,128]{3,2,1,0:T(8,128)(2,1)S(1)}, u32[]{:S(2)}, u32[]{:S(2)}) collective-permute-start(bf16[3,8,32,128]{3,2,1,0:T(8,128)(2,1)S(1)} %pad_maximum_fusion.11.refs_5_), channel_id=1, source_target_pairs={{4,0},{8,4},{12,8},{16,12},{20,16},{24,20},{28,24},{0,28},{5,1},{9... | collective-permute-start | bytes 589832 | tf_op jit(solution)/shard_map/ppermute | solution.py:203
  71.0 0.1 collective-permute-start.18
  71.1 1.5 %inner_half0.6.refs_1_.refs_7_ = bf16[2,8,32,128]{3,2,1,0:T(8,128)(2,1)S(1)} custom-call(s32[8,12]{1,0:T(8,128)S(1)} %fusion.5.refs_0_, bf16[4,8,64,768]{3,2,1,0:T(8,128)(2,1)S(1)} %halves_of_rows.1.refs_1_, bf16[4,8,32,128]{3,2,1,0:T(8,128)(2,1)S(1)} %edge_half0.5.refs_2_.first_ref, bf16[4,8,32,128]{3,2,1,0:T(8,128)(2,1)S(1)} %collective-permute-done.12.refs_3_, ...), custom_call_target="tpu_custom_call" | custom-call | flops 20132659200 | bytes 157286400 | tf_op jit(solution)/shard_map/inner_half0/pallas_call | solution.py:178
  72.6 0.9 unpack.5
  73.5 1.8 %collective-permute-done.19.refs_6_ = bf16[3,8,32,128]{3,2,1,0:T(8,128)(2,1)S(1)} collective-permute-done((bf16[3,8,32,128]{3,2,1,0:T(8,128)(2,1)S(1)}, bf16[3,8,32,128]{3,2,1,0:T(8,128)(2,1)S(1)}, u32[]{:S(2)}, u32[]{:S(2)}) %collective-permute-start.19) | collective-permute-done | bytes 196640 | tf_op jit(solution)/shard_map/ppermute | solution.py:203
  75.3 1.8 %collective-permute-done.18.refs_5_ = bf16[3,8,32,128]{3,2,1,0:T(8,128)(2,1)S(1)} collective-permute-done((bf16[3,8,32,128]{3,2,1,0:T(8,128)(2,1)S(1)}, bf16[3,8,32,128]{3,2,1,0:T(8,128)(2,1)S(1)}, u32[]{:S(2)}, u32[]{:S(2)}) %collective-permute-start.18) | collective-permute-done | bytes 196640 | tf_op jit(solution)/shard_map/ppermute | solution.py:203
  77.1 1.5 %edge_half0.6.refs_2_.first_ref = bf16[4,8,32,128]{3,2,1,0:T(8,128)(2,1)S(1)} custom-call(s32[8,12]{1,0:T(8,128)S(1)} %fusion.5.refs_0_, bf16[4,8,64,768]{3,2,1,0:T(8,128)(2,1)S(1)} %halves_of_rows.1.refs_1_, bf16[4,8,32,128]{3,2,1,0:T(8,128)(2,1)S(1)} %edge_half0.5.refs_2_.first_ref, bf16[4,8,32,128]{3,2,1,0:T(8,128)(2,1)S(1)} %collective-permute-done.12.refs_3_, ...), custom_call_target="tpu_custom_call" | custom-call | flops 20132659200 | bytes 157286400 | tf_op jit(solution)/shard_map/edge_half0/pallas_call | solution.py:178
  78.6 3.6 %collective-permute-start.20 = (bf16[4,8,32,128]{3,2,1,0:T(8,128)(2,1)S(1)}, bf16[4,8,32,128]{3,2,1,0:T(8,128)(2,1)S(1)}, u32[]{:S(2)}, u32[]{:S(2)}) collective-permute-start(bf16[4,8,32,128]{3,2,1,0:T(8,128)(2,1)S(1)} %edge_half0.6.refs_2_.first_ref), channel_id=1, source_target_pairs={{1,0},{2,1},{3,2},{0,3},{5,4},{6,5},{7,6},{4,7},{9,8},{10,9},{11,1... | collective-permute-start | bytes 786440 | tf_op jit(solution)/shard_map/ppermute | solution.py:203
  82.3 1.1 collective-permute-start.25
  83.4 0.1 collective-permute-start.24
  83.4 1.5 %inner_half1.6.refs_7_.refs_8_ = bf16[2,8,32,128]{3,2,1,0:T(8,128)(2,1)S(1)} custom-call(s32[8,12]{1,0:T(8,128)S(1)} %fusion.5.refs_0_, bf16[4,8,64,768]{3,2,1,0:T(8,128)(2,1)S(1)} %halves_of_rows.1.refs_1_, bf16[4,8,32,128]{3,2,1,0:T(8,128)(2,1)S(1)} %edge_half1.5.second_ref.refs_2_, bf16[4,8,32,128]{3,2,1,0:T(8,128)(2,1)S(1)} %collective-permute-done.22.refs_3_, ...), custom_call_target="tpu_custom_call" | custom-call | flops 20132659200 | bytes 157286400 | tf_op jit(solution)/shard_map/inner_half1/pallas_call | solution.py:178
  84.9 3.0 %collective-permute-done.25.refs_6_ = bf16[3,8,32,128]{3,2,1,0:T(8,128)(2,1)S(1)} collective-permute-done((bf16[3,8,32,128]{3,2,1,0:T(8,128)(2,1)S(1)}, bf16[3,8,32,128]{3,2,1,0:T(8,128)(2,1)S(1)}, u32[]{:S(2)}, u32[]{:S(2)}) %collective-permute-start.25) | collective-permute-done | bytes 196640 | tf_op jit(solution)/shard_map/ppermute | solution.py:203
  87.9 1.5 %collective-permute-done.24.refs_5_ = bf16[3,8,32,128]{3,2,1,0:T(8,128)(2,1)S(1)} collective-permute-done((bf16[3,8,32,128]{3,2,1,0:T(8,128)(2,1)S(1)}, bf16[3,8,32,128]{3,2,1,0:T(8,128)(2,1)S(1)}, u32[]{:S(2)}, u32[]{:S(2)}) %collective-permute-start.24) | collective-permute-done | bytes 196640 | tf_op jit(solution)/shard_map/ppermute | solution.py:203
  89.4 1.5 %edge_half1.6.refs_2_.second_ref = bf16[4,8,32,128]{3,2,1,0:T(8,128)(2,1)S(1)} custom-call(s32[8,12]{1,0:T(8,128)S(1)} %fusion.5.refs_0_, bf16[4,8,64,768]{3,2,1,0:T(8,128)(2,1)S(1)} %halves_of_rows.1.refs_1_, bf16[4,8,32,128]{3,2,1,0:T(8,128)(2,1)S(1)} %edge_half1.5.second_ref.refs_2_, bf16[4,8,32,128]{3,2,1,0:T(8,128)(2,1)S(1)} %collective-permute-done.22.refs_3_, ...), custom_call_target="tpu_custom_call" | custom-call | flops 20132659200 | bytes 157286400 | tf_op jit(solution)/shard_map/edge_half1/pallas_call | solution.py:178
  91.0 3.7 %collective-permute-start.28 = (bf16[2,8,32,128]{3,2,1,0:T(8,128)(2,1)S(1)}, bf16[2,8,32,128]{3,2,1,0:T(8,128)(2,1)S(1)}, u32[]{:S(2)}, u32[]{:S(2)}) collective-permute-start(bf16[2,8,32,128]{3,2,1,0:T(8,128)(2,1)S(1)} %pad_maximum_fusion.18), channel_id=1, source_target_pairs={{1,0},{2,1},{3,2},{0,3},{5,4},{6,5},{7,6},{4,7},{9,8},{10,9},{11,1... | collective-permute-start | bytes 393224 | tf_op jit(solution)/shard_map/ppermute | solution.py:203
  94.7 1.0 collective-permute-start.27
  95.7 0.1 collective-permute-start.26
  95.8 3.5 %collective-permute-start.30 = (bf16[2,8,32,128]{3,2,1,0:T(8,128)(2,1)S(1)}, bf16[2,8,32,128]{3,2,1,0:T(8,128)(2,1)S(1)}, u32[]{:S(2)}, u32[]{:S(2)}) collective-permute-start(bf16[2,8,32,128]{3,2,1,0:T(8,128)(2,1)S(1)} %slice.222), channel_id=1, source_target_pairs={{1,0},{2,1},{3,2},{0,3},{5,4},{6,5},{7,6},{4,7},{9,8},{10,9},{11,1... | collective-permute-start | bytes 393224 | tf_op jit(solution)/shard_map/ppermute | solution.py:203
  99.3 1.5 %inner_half0.7.refs_7_.refs_8_ = bf16[2,8,32,128]{3,2,1,0:T(8,128)(2,1)S(1)} custom-call(s32[8,12]{1,0:T(8,128)S(1)} %fusion.5.refs_0_, bf16[4,8,64,768]{3,2,1,0:T(8,128)(2,1)S(1)} %halves_of_rows.1.refs_1_, bf16[4,8,32,128]{3,2,1,0:T(8,128)(2,1)S(1)} %edge_half0.6.refs_2_.first_ref, bf16[4,8,32,128]{3,2,1,0:T(8,128)(2,1)S(1)} %collective-permute-done.20.refs_3_, ...), custom_call_target="tpu_custom_call" | custom-call | flops 20132659200 | bytes 157286400 | tf_op jit(solution)/shard_map/inner_half0/pallas_call | solution.py:178
  100.8 0.1 collective-permute-start.31
  100.9 1.7 %collective-permute-done.29 = bf16[2,8,32,128]{3,2,1,0:T(8,128)(2,1)S(1)} collective-permute-done((bf16[2,8,32,128]{3,2,1,0:T(8,128)(2,1)S(1)}, bf16[2,8,32,128]{3,2,1,0:T(8,128)(2,1)S(1)}, u32[]{:S(2)}, u32[]{:S(2)}) %collective-permute-start.29) | collective-permute-done | bytes 131104 | tf_op jit(solution)/shard_map/ppermute | solution.py:203
  102.7 0.6 collective-permute-start.33
  103.5 1.5 %edge_half0.7.refs_1_.first_ref = bf16[4,8,32,128]{3,2,1,0:T(8,128)(2,1)S(1)} custom-call(s32[8,12]{1,0:T(8,128)S(1)} %fusion.5.refs_0_, bf16[4,8,64,768]{3,2,1,0:T(8,128)(2,1)S(1)} %halves_of_rows.1.refs_1_, bf16[4,8,32,128]{3,2,1,0:T(8,128)(2,1)S(1)} %edge_half0.6.refs_2_.first_ref, bf16[4,8,32,128]{3,2,1,0:T(8,128)(2,1)S(1)} %collective-permute-done.20.refs_3_, ...), custom_call_target="tpu_custom_call" | custom-call | flops 20132659200 | bytes 157286400 | tf_op jit(solution)/shard_map/edge_half0/pallas_call | solution.py:178
  105.0 2.8 %collective-permute-done.31 = bf16[2,8,32,128]{3,2,1,0:T(8,128)(2,1)S(1)} collective-permute-done((bf16[2,8,32,128]{3,2,1,0:T(8,128)(2,1)S(1)}, bf16[2,8,32,128]{3,2,1,0:T(8,128)(2,1)S(1)}, u32[]{:S(2)}, u32[]{:S(2)}) %collective-permute-start.31) | collective-permute-done | bytes 131104 | tf_op jit(solution)/shard_map/ppermute | solution.py:203
  107.8 1.5 %inner_half1.7.refs_7_ = bf16[2,8,32,128]{3,2,1,0:T(8,128)(2,1)S(1)} custom-call(s32[8,12]{1,0:T(8,128)S(1)} %fusion.5.refs_0_, bf16[4,8,64,768]{3,2,1,0:T(8,128)(2,1)S(1)} %halves_of_rows.1.refs_1_, bf16[4,8,32,128]{3,2,1,0:T(8,128)(2,1)S(1)} %edge_half1.6.refs_2_.second_ref, bf16[4,8,32,128]{3,2,1,0:T(8,128)(2,1)S(1)} %pad_maximum_fusion.refs_3_, ...), custom_call_target="tpu_custom_call" | custom-call | flops 20132659200 | bytes 157286400 | tf_op jit(solution)/shard_map/inner_half1/pallas_call | solution.py:178
  109.3 0.9 unpack.6
  110.3 1.5 %edge_half1.7.second_ref = bf16[4,8,32,128]{3,2,1,0:T(8,128)(2,1)S(1)} custom-call(s32[8,12]{1,0:T(8,128)S(1)} %fusion.5.refs_0_, bf16[4,8,64,768]{3,2,1,0:T(8,128)(2,1)S(1)} %halves_of_rows.1.refs_1_, bf16[4,8,32,128]{3,2,1,0:T(8,128)(2,1)S(1)} %edge_half1.6.refs_2_.second_ref, bf16[4,8,32,128]{3,2,1,0:T(8,128)(2,1)S(1)} %pad_maximum_fusion.refs_3_, ...), custom_call_target="tpu_custom_call" | custom-call | flops 20132659200 | bytes 157286400 | tf_op jit(solution)/shard_map/edge_half1/pallas_call | solution.py:178
  111.8 1.5 %unpack.7 = (bf16[4,4,8,64,128]{4,3,2,1,0:T(8,128)(2,1)}, f32[8,128]{1,0:T(8,128)}) custom-call(bf16[4,8,32,128]{3,2,1,0:T(8,128)(2,1)S(1)} %edge_half0.7.refs_1_.first_ref, bf16[4,8,32,128]{3,2,1,0:T(8,128)(2,1)S(1)} %edge_half1.7.second_ref, bf16[4,4,8,64,128]{4,3,2,1,0:T(8,128)(2,1)} %get-tuple-element.79.refs_0_), custom_call_target="tpu_custom_call", output_to_operand_aliasing={{0}: (2, {})} | custom-call | tf_op jit(solution)/shard_map/unpack/pallas_call | solution.py:77
  (79 shorter events, 1.0 us)
Async XLA Ops:
  0.0 1.0 copy-start.1
  1.2 13.6 %collective-permute-start = (bf16[4,8,32,128]{3,2,1,0:T(8,128)(2,1)S(1)}, bf16[4,8,32,128]{3,2,1,0:T(8,128)(2,1)S(1)}, u32[]{:S(2)}, u32[]{:S(2)}) collective-permute-start(bf16[4,8,32,128]{3,2,1,0:T(8,128)(2,1)S(1)} %get-tuple-element.45.refs_2_), channel_id=1, source_target_pairs={{1,0},{2,1},{3,2},{0,3},{5,4},{6,5},{7,6},{4,7},{9,8},{10,9},{11,1... | collective-permute-start | bytes 786440 | tf_op jit(solution)/shard_map/ppermute | solution.py:203
  6.3 13.3 %collective-permute-start.1 = (bf16[4,8,32,128]{3,2,1,0:T(8,128)(2,1)S(1)}, bf16[4,8,32,128]{3,2,1,0:T(8,128)(2,1)S(1)}, u32[]{:S(2)}, u32[]{:S(2)}) collective-permute-start(bf16[4,8,32,128]{3,2,1,0:T(8,128)(2,1)S(1)} %get-tuple-element.45.refs_2_), channel_id=1, source_target_pairs={{0,1},{1,2},{2,3},{3,0},{4,5},{5,6},{6,7},{7,4},{8,9},{9,10},{10,1... | collective-permute-start | bytes 786440 | tf_op jit(solution)/shard_map/ppermute | solution.py:203
  6.3 26.1 %collective-permute-start.6 = (bf16[4,8,32,128]{3,2,1,0:T(8,128)(2,1)S(1)}, bf16[4,8,32,128]{3,2,1,0:T(8,128)(2,1)S(1)}, u32[]{:S(2)}, u32[]{:S(2)}) collective-permute-start(bf16[4,8,32,128]{3,2,1,0:T(8,128)(2,1)S(1)} %get-tuple-element.49.refs_2_), channel_id=1, source_target_pairs={{1,0},{2,1},{3,2},{0,3},{5,4},{6,5},{7,6},{4,7},{9,8},{10,9},{11,1... | collective-permute-start | bytes 786440 | tf_op jit(solution)/shard_map/ppermute | solution.py:203
  10.1 22.2 %collective-permute-start.7 = (bf16[4,8,32,128]{3,2,1,0:T(8,128)(2,1)S(1)}, bf16[4,8,32,128]{3,2,1,0:T(8,128)(2,1)S(1)}, u32[]{:S(2)}, u32[]{:S(2)}) collective-permute-start(bf16[4,8,32,128]{3,2,1,0:T(8,128)(2,1)S(1)} %get-tuple-element.49.refs_2_), channel_id=1, source_target_pairs={{0,1},{1,2},{2,3},{3,0},{4,5},{5,6},{6,7},{7,4},{8,9},{9,10},{10,1... | collective-permute-start | bytes 786440 | tf_op jit(solution)/shard_map/ppermute | solution.py:203
  10.1 1.9 %copy-start = (bf16[4,1,8,64,768]{4,3,2,1,0:T(8,128)(2,1)S(1)}, bf16[4,1,8,64,768]{4,3,2,1,0:T(8,128)(2,1)}, u32[]{:S(2)}) copy-start(bf16[4,1,8,64,768]{4,3,2,1,0:T(8,128)(2,1)} %param.4) | copy-start | bytes 9437188
  12.0 2.7 %copy-start.2 = (s32[1,8,12]{2,1,0:T(8,128)S(1)}, s32[1,8,12]{2,1,0:T(8,128)}, u32[]{:S(2)}) copy-start(s32[1,8,12]{2,1,0:T(8,128)} %param.5) | copy-start | bytes 1156
  19.7 4.3 %collective-permute-start.3 = (bf16[3,8,32,128]{3,2,1,0:T(8,128)(2,1)S(1)}, bf16[3,8,32,128]{3,2,1,0:T(8,128)(2,1)S(1)}, u32[]{:S(2)}, u32[]{:S(2)}) collective-permute-start(bf16[3,8,32,128]{3,2,1,0:T(8,128)(2,1)S(1)} %pad_maximum_fusion.3.refs_5_), channel_id=1, source_target_pairs={{4,0},{8,4},{12,8},{16,12},{20,16},{24,20},{28,24},{0,28},{5,1},{9... | collective-permute-start | bytes 589832 | tf_op jit(solution)/shard_map/ppermute | solution.py:203
  19.8 8.1 %collective-permute-start.2 = (bf16[3,8,32,128]{3,2,1,0:T(8,128)(2,1)S(1)}, bf16[3,8,32,128]{3,2,1,0:T(8,128)(2,1)S(1)}, u32[]{:S(2)}, u32[]{:S(2)}) collective-permute-start(bf16[3,8,32,128]{3,2,1,0:T(8,128)(2,1)S(1)} %pad_maximum_fusion.2.refs_6_), channel_id=1, source_target_pairs={{0,4},{4,8},{8,12},{12,16},{16,20},{20,24},{24,28},{28,0},{1,5},{5... | collective-permute-start | bytes 589832 | tf_op jit(solution)/shard_map/ppermute | solution.py:203
  29.4 15.4 %collective-permute-start.4 = (bf16[4,8,32,128]{3,2,1,0:T(8,128)(2,1)S(1)}, bf16[4,8,32,128]{3,2,1,0:T(8,128)(2,1)S(1)}, u32[]{:S(2)}, u32[]{:S(2)}) collective-permute-start(bf16[4,8,32,128]{3,2,1,0:T(8,128)(2,1)S(1)} %edge_half0.4.refs_2_.first_ref), channel_id=1, source_target_pairs={{1,0},{2,1},{3,2},{0,3},{5,4},{6,5},{7,6},{4,7},{9,8},{10,9},{11,1... | collective-permute-start | bytes 786440 | tf_op jit(solution)/shard_map/ppermute | solution.py:203
  32.4 12.5 %collective-permute-start.5 = (bf16[4,8,32,128]{3,2,1,0:T(8,128)(2,1)S(1)}, bf16[4,8,32,128]{3,2,1,0:T(8,128)(2,1)S(1)}, u32[]{:S(2)}, u32[]{:S(2)}) collective-permute-start(bf16[4,8,32,128]{3,2,1,0:T(8,128)(2,1)S(1)} %edge_half0.4.refs_2_.first_ref), channel_id=1, source_target_pairs={{0,1},{1,2},{2,3},{3,0},{4,5},{5,6},{6,7},{7,4},{8,9},{9,10},{10,1... | collective-permute-start | bytes 786440 | tf_op jit(solution)/shard_map/ppermute | solution.py:203
  32.5 5.3 %collective-permute-start.9 = (bf16[3,8,32,128]{3,2,1,0:T(8,128)(2,1)S(1)}, bf16[3,8,32,128]{3,2,1,0:T(8,128)(2,1)S(1)}, u32[]{:S(2)}, u32[]{:S(2)}) collective-permute-start(bf16[3,8,32,128]{3,2,1,0:T(8,128)(2,1)S(1)} %pad_maximum_fusion.5.refs_5_), channel_id=1, source_target_pairs={{4,0},{8,4},{12,8},{16,12},{20,16},{24,20},{28,24},{0,28},{5,1},{9... | collective-permute-start | bytes 589832 | tf_op jit(solution)/shard_map/ppermute | solution.py:203
  32.6 7.2 %collective-permute-start.8 = (bf16[3,8,32,128]{3,2,1,0:T(8,128)(2,1)S(1)}, bf16[3,8,32,128]{3,2,1,0:T(8,128)(2,1)S(1)}, u32[]{:S(2)}, u32[]{:S(2)}) collective-permute-start(bf16[3,8,32,128]{3,2,1,0:T(8,128)(2,1)S(1)} %pad_maximum_fusion.4.refs_6_), channel_id=1, source_target_pairs={{0,4},{4,8},{8,12},{12,16},{16,20},{20,24},{24,28},{28,0},{1,5},{5... | collective-permute-start | bytes 589832 | tf_op jit(solution)/shard_map/ppermute | solution.py:203
  41.2 15.7 %collective-permute-start.14 = (bf16[4,8,32,128]{3,2,1,0:T(8,128)(2,1)S(1)}, bf16[4,8,32,128]{3,2,1,0:T(8,128)(2,1)S(1)}, u32[]{:S(2)}, u32[]{:S(2)}) collective-permute-start(bf16[4,8,32,128]{3,2,1,0:T(8,128)(2,1)S(1)} %edge_half1.4.second_ref.refs_2_), channel_id=1, source_target_pairs={{1,0},{2,1},{3,2},{0,3},{5,4},{6,5},{7,6},{4,7},{9,8},{10,9},{11,1... | collective-permute-start | bytes 786440 | tf_op jit(solution)/shard_map/ppermute | solution.py:203
  44.8 12.1 %collective-permute-start.15 = (bf16[4,8,32,128]{3,2,1,0:T(8,128)(2,1)S(1)}, bf16[4,8,32,128]{3,2,1,0:T(8,128)(2,1)S(1)}, u32[]{:S(2)}, u32[]{:S(2)}) collective-permute-start(bf16[4,8,32,128]{3,2,1,0:T(8,128)(2,1)S(1)} %edge_half1.4.second_ref.refs_2_), channel_id=1, source_target_pairs={{0,1},{1,2},{2,3},{3,0},{4,5},{5,6},{6,7},{7,4},{8,9},{9,10},{10,1... | collective-permute-start | bytes 786440 | tf_op jit(solution)/shard_map/ppermute | solution.py:203
  44.9 5.5 %collective-permute-start.11 = (bf16[3,8,32,128]{3,2,1,0:T(8,128)(2,1)S(1)}, bf16[3,8,32,128]{3,2,1,0:T(8,128)(2,1)S(1)}, u32[]{:S(2)}, u32[]{:S(2)}) collective-permute-start(bf16[3,8,32,128]{3,2,1,0:T(8,128)(2,1)S(1)} %pad_maximum_fusion.7.refs_5_), channel_id=1, source_target_pairs={{4,0},{8,4},{12,8},{16,12},{20,16},{24,20},{28,24},{0,28},{5,1},{9... | collective-permute-start | bytes 589832 | tf_op jit(solution)/shard_map/ppermute | solution.py:203
  45.8 6.0 %collective-permute-start.10 = (bf16[3,8,32,128]{3,2,1,0:T(8,128)(2,1)S(1)}, bf16[3,8,32,128]{3,2,1,0:T(8,128)(2,1)S(1)}, u32[]{:S(2)}, u32[]{:S(2)}) collective-permute-start(bf16[3,8,32,128]{3,2,1,0:T(8,128)(2,1)S(1)} %pad_maximum_fusion.6.refs_6_), channel_id=1, source_target_pairs={{0,4},{4,8},{8,12},{12,16},{16,20},{20,24},{24,28},{28,0},{1,5},{5... | collective-permute-start | bytes 589832 | tf_op jit(solution)/shard_map/ppermute | solution.py:203
  53.3 16.3 %collective-permute-start.12 = (bf16[4,8,32,128]{3,2,1,0:T(8,128)(2,1)S(1)}, bf16[4,8,32,128]{3,2,1,0:T(8,128)(2,1)S(1)}, u32[]{:S(2)}, u32[]{:S(2)}) collective-permute-start(bf16[4,8,32,128]{3,2,1,0:T(8,128)(2,1)S(1)} %edge_half0.5.refs_2_.first_ref), channel_id=1, source_target_pairs={{1,0},{2,1},{3,2},{0,3},{5,4},{6,5},{7,6},{4,7},{9,8},{10,9},{11,1... | collective-permute-start | bytes 786440 | tf_op jit(solution)/shard_map/ppermute | solution.py:203
  57.0 12.7 %collective-permute-start.13 = (bf16[4,8,32,128]{3,2,1,0:T(8,128)(2,1)S(1)}, bf16[4,8,32,128]{3,2,1,0:T(8,128)(2,1)S(1)}, u32[]{:S(2)}, u32[]{:S(2)}) collective-permute-start(bf16[4,8,32,128]{3,2,1,0:T(8,128)(2,1)S(1)} %edge_half0.5.refs_2_.first_ref), channel_id=1, source_target_pairs={{0,1},{1,2},{2,3},{3,0},{4,5},{5,6},{6,7},{7,4},{8,9},{9,10},{10,1... | collective-permute-start | bytes 786440 | tf_op jit(solution)/shard_map/ppermute | solution.py:203
  57.1 5.9 %collective-permute-start.17 = (bf16[3,8,32,128]{3,2,1,0:T(8,128)(2,1)S(1)}, bf16[3,8,32,128]{3,2,1,0:T(8,128)(2,1)S(1)}, u32[]{:S(2)}, u32[]{:S(2)}) collective-permute-start(bf16[3,8,32,128]{3,2,1,0:T(8,128)(2,1)S(1)} %pad_maximum_fusion.9.refs_5_), channel_id=1, source_target_pairs={{4,0},{8,4},{12,8},{16,12},{20,16},{24,20},{28,24},{0,28},{5,1},{9... | collective-permute-start | bytes 589832 | tf_op jit(solution)/shard_map/ppermute | solution.py:203
  58.5 6.0 %collective-permute-start.16 = (bf16[3,8,32,128]{3,2,1,0:T(8,128)(2,1)S(1)}, bf16[3,8,32,128]{3,2,1,0:T(8,128)(2,1)S(1)}, u32[]{:S(2)}, u32[]{:S(2)}) collective-permute-start(bf16[3,8,32,128]{3,2,1,0:T(8,128)(2,1)S(1)} %pad_maximum_fusion.8.refs_6_), channel_id=1, source_target_pairs={{0,4},{4,8},{8,12},{12,16},{16,20},{20,24},{24,28},{28,0},{1,5},{5... | collective-permute-start | bytes 589832 | tf_op jit(solution)/shard_map/ppermute | solution.py:203
  66.1 16.1 %collective-permute-start.22 = (bf16[4,8,32,128]{3,2,1,0:T(8,128)(2,1)S(1)}, bf16[4,8,32,128]{3,2,1,0:T(8,128)(2,1)S(1)}, u32[]{:S(2)}, u32[]{:S(2)}) collective-permute-start(bf16[4,8,32,128]{3,2,1,0:T(8,128)(2,1)S(1)} %edge_half1.5.second_ref.refs_2_), channel_id=1, source_target_pairs={{1,0},{2,1},{3,2},{0,3},{5,4},{6,5},{7,6},{4,7},{9,8},{10,9},{11,1... | collective-permute-start | bytes 786440 | tf_op jit(solution)/shard_map/ppermute | solution.py:203
  69.6 12.5 %collective-permute-start.23 = (bf16[4,8,32,128]{3,2,1,0:T(8,128)(2,1)S(1)}, bf16[4,8,32,128]{3,2,1,0:T(8,128)(2,1)S(1)}, u32[]{:S(2)}, u32[]{:S(2)}) collective-permute-start(bf16[4,8,32,128]{3,2,1,0:T(8,128)(2,1)S(1)} %edge_half1.5.second_ref.refs_2_), channel_id=1, source_target_pairs={{0,1},{1,2},{2,3},{3,0},{4,5},{5,6},{6,7},{7,4},{8,9},{9,10},{10,1... | collective-permute-start | bytes 786440 | tf_op jit(solution)/shard_map/ppermute | solution.py:203
  69.8 5.6 %collective-permute-start.19 = (bf16[3,8,32,128]{3,2,1,0:T(8,128)(2,1)S(1)}, bf16[3,8,32,128]{3,2,1,0:T(8,128)(2,1)S(1)}, u32[]{:S(2)}, u32[]{:S(2)}) collective-permute-start(bf16[3,8,32,128]{3,2,1,0:T(8,128)(2,1)S(1)} %pad_maximum_fusion.11.refs_5_), channel_id=1, source_target_pairs={{4,0},{8,4},{12,8},{16,12},{20,16},{24,20},{28,24},{0,28},{5,1},{9... | collective-permute-start | bytes 589832 | tf_op jit(solution)/shard_map/ppermute | solution.py:203
  71.0 6.0 %collective-permute-start.18 = (bf16[3,8,32,128]{3,2,1,0:T(8,128)(2,1)S(1)}, bf16[3,8,32,128]{3,2,1,0:T(8,128)(2,1)S(1)}, u32[]{:S(2)}, u32[]{:S(2)}) collective-permute-start(bf16[3,8,32,128]{3,2,1,0:T(8,128)(2,1)S(1)} %pad_maximum_fusion.10.refs_6_), channel_id=1, source_target_pairs={{0,4},{4,8},{8,12},{12,16},{16,20},{20,24},{24,28},{28,0},{1,5},{5... | collective-permute-start | bytes 589832 | tf_op jit(solution)/shard_map/ppermute | solution.py:203
  78.6 16.1 %collective-permute-start.20 = (bf16[4,8,32,128]{3,2,1,0:T(8,128)(2,1)S(1)}, bf16[4,8,32,128]{3,2,1,0:T(8,128)(2,1)S(1)}, u32[]{:S(2)}, u32[]{:S(2)}) collective-permute-start(bf16[4,8,32,128]{3,2,1,0:T(8,128)(2,1)S(1)} %edge_half0.6.refs_2_.first_ref), channel_id=1, source_target_pairs={{1,0},{2,1},{3,2},{0,3},{5,4},{6,5},{7,6},{4,7},{9,8},{10,9},{11,1... | collective-permute-start | bytes 786440 | tf_op jit(solution)/shard_map/ppermute | solution.py:203
  82.2 12.5 %collective-permute-start.21 = (bf16[4,8,32,128]{3,2,1,0:T(8,128)(2,1)S(1)}, bf16[4,8,32,128]{3,2,1,0:T(8,128)(2,1)S(1)}, u32[]{:S(2)}, u32[]{:S(2)}) collective-permute-start(bf16[4,8,32,128]{3,2,1,0:T(8,128)(2,1)S(1)} %edge_half0.6.refs_2_.first_ref), channel_id=1, source_target_pairs={{0,1},{1,2},{2,3},{3,0},{4,5},{5,6},{6,7},{7,4},{8,9},{9,10},{10,1... | collective-permute-start | bytes 786440 | tf_op jit(solution)/shard_map/ppermute | solution.py:203
  82.3 5.6 %collective-permute-start.25 = (bf16[3,8,32,128]{3,2,1,0:T(8,128)(2,1)S(1)}, bf16[3,8,32,128]{3,2,1,0:T(8,128)(2,1)S(1)}, u32[]{:S(2)}, u32[]{:S(2)}) collective-permute-start(bf16[3,8,32,128]{3,2,1,0:T(8,128)(2,1)S(1)} %pad_maximum_fusion.13.refs_5_), channel_id=1, source_target_pairs={{4,0},{8,4},{12,8},{16,12},{20,16},{24,20},{28,24},{0,28},{5,1},{9... | collective-permute-start | bytes 589832 | tf_op jit(solution)/shard_map/ppermute | solution.py:203
  83.4 6.0 %collective-permute-start.24 = (bf16[3,8,32,128]{3,2,1,0:T(8,128)(2,1)S(1)}, bf16[3,8,32,128]{3,2,1,0:T(8,128)(2,1)S(1)}, u32[]{:S(2)}, u32[]{:S(2)}) collective-permute-start(bf16[3,8,32,128]{3,2,1,0:T(8,128)(2,1)S(1)} %pad_maximum_fusion.12.refs_6_), channel_id=1, source_target_pairs={{0,4},{4,8},{8,12},{12,16},{16,20},{20,24},{24,28},{28,0},{1,5},{5... | collective-permute-start | bytes 589832 | tf_op jit(solution)/shard_map/ppermute | solution.py:203
  91.0 9.9 %collective-permute-start.28 = (bf16[2,8,32,128]{3,2,1,0:T(8,128)(2,1)S(1)}, bf16[2,8,32,128]{3,2,1,0:T(8,128)(2,1)S(1)}, u32[]{:S(2)}, u32[]{:S(2)}) collective-permute-start(bf16[2,8,32,128]{3,2,1,0:T(8,128)(2,1)S(1)} %pad_maximum_fusion.18), channel_id=1, source_target_pairs={{1,0},{2,1},{3,2},{0,3},{5,4},{6,5},{7,6},{4,7},{9,8},{10,9},{11,1... | collective-permute-start | bytes 393224 | tf_op jit(solution)/shard_map/ppermute | solution.py:203
  94.6 8.0 %collective-permute-start.29 = (bf16[2,8,32,128]{3,2,1,0:T(8,128)(2,1)S(1)}, bf16[2,8,32,128]{3,2,1,0:T(8,128)(2,1)S(1)}, u32[]{:S(2)}, u32[]{:S(2)}) collective-permute-start(bf16[2,8,32,128]{3,2,1,0:T(8,128)(2,1)S(1)} %pad_maximum_fusion.18), channel_id=1, source_target_pairs={{0,1},{1,2},{2,3},{3,0},{4,5},{5,6},{6,7},{7,4},{8,9},{9,10},{10,1... | collective-permute-start | bytes 393224 | tf_op jit(solution)/shard_map/ppermute | solution.py:203
  94.7 8.6 %collective-permute-start.27 = (bf16[3,8,32,128]{3,2,1,0:T(8,128)(2,1)S(1)}, bf16[3,8,32,128]{3,2,1,0:T(8,128)(2,1)S(1)}, u32[]{:S(2)}, u32[]{:S(2)}) collective-permute-start(bf16[3,8,32,128]{3,2,1,0:T(8,128)(2,1)S(1)} %pad_maximum_fusion.15.refs_5_), channel_id=1, source_target_pairs={{4,0},{8,4},{12,8},{16,12},{20,16},{24,20},{28,24},{0,28},{5,1},{9... | collective-permute-start | bytes 589832 | tf_op jit(solution)/shard_map/ppermute | solution.py:203
  95.7 7.7 %collective-permute-start.26 = (bf16[3,8,32,128]{3,2,1,0:T(8,128)(2,1)S(1)}, bf16[3,8,32,128]{3,2,1,0:T(8,128)(2,1)S(1)}, u32[]{:S(2)}, u32[]{:S(2)}) collective-permute-start(bf16[3,8,32,128]{3,2,1,0:T(8,128)(2,1)S(1)} %pad_maximum_fusion.14.refs_6_), channel_id=1, source_target_pairs={{0,4},{4,8},{8,12},{12,16},{16,20},{20,24},{24,28},{28,0},{1,5},{5... | collective-permute-start | bytes 589832 | tf_op jit(solution)/shard_map/ppermute | solution.py:203
  95.8 9.2 %collective-permute-start.30 = (bf16[2,8,32,128]{3,2,1,0:T(8,128)(2,1)S(1)}, bf16[2,8,32,128]{3,2,1,0:T(8,128)(2,1)S(1)}, u32[]{:S(2)}, u32[]{:S(2)}) collective-permute-start(bf16[2,8,32,128]{3,2,1,0:T(8,128)(2,1)S(1)} %slice.222), channel_id=1, source_target_pairs={{1,0},{2,1},{3,2},{0,3},{5,4},{6,5},{7,6},{4,7},{9,8},{10,9},{11,1... | collective-permute-start | bytes 393224 | tf_op jit(solution)/shard_map/ppermute | solution.py:203
  100.8 6.9 %collective-permute-start.31 = (bf16[2,8,32,128]{3,2,1,0:T(8,128)(2,1)S(1)}, bf16[2,8,32,128]{3,2,1,0:T(8,128)(2,1)S(1)}, u32[]{:S(2)}, u32[]{:S(2)}) collective-permute-start(bf16[2,8,32,128]{3,2,1,0:T(8,128)(2,1)S(1)} %slice.222), channel_id=1, source_target_pairs={{0,1},{1,2},{2,3},{3,0},{4,5},{5,6},{6,7},{7,4},{8,9},{9,10},{10,1... | collective-permute-start | bytes 393224 | tf_op jit(solution)/shard_map/ppermute | solution.py:203
  102.7 7.5 %collective-permute-start.33 = (bf16[3,8,32,128]{3,2,1,0:T(8,128)(2,1)S(1)}, bf16[3,8,32,128]{3,2,1,0:T(8,128)(2,1)S(1)}, u32[]{:S(2)}, u32[]{:S(2)}) collective-permute-start(bf16[3,8,32,128]{3,2,1,0:T(8,128)(2,1)S(1)} %pad_maximum_fusion.17.refs_5_), channel_id=1, source_target_pairs={{4,0},{8,4},{12,8},{16,12},{20,16},{24,20},{28,24},{0,28},{5,1},{9... | collective-permute-start | bytes 589832 | tf_op jit(solution)/shard_map/ppermute | solution.py:203
  103.4 6.9 %collective-permute-start.32 = (bf16[3,8,32,128]{3,2,1,0:T(8,128)(2,1)S(1)}, bf16[3,8,32,128]{3,2,1,0:T(8,128)(2,1)S(1)}, u32[]{:S(2)}, u32[]{:S(2)}) collective-permute-start(bf16[3,8,32,128]{3,2,1,0:T(8,128)(2,1)S(1)} %pad_maximum_fusion.16.refs_6_), channel_id=1, source_target_pairs={{0,4},{4,8},{8,12},{12,16},{16,20},{20,24},{24,28},{28,0},{1,5},{5... | collective-permute-start | bytes 589832 | tf_op jit(solution)/shard_map/ppermute | solution.py:203

commit v16 on v11

--- a/solution.py
+++ b/solution.py
@@ -246,7 +246,8 @@
     start = start_vector.reshape(columns, faces, width, lanes)
     blocks = halves_of_rows(trace_blocks.reshape(columns, faces, width, -1))
     codes = neighbour.reshape(faces, -1)
-    table = (((codes // faces) % 3) * (columns + 2) + codes // (3 * faces)) * faces + codes % faces
+    around_shift = (codes // faces) % 3
+    table = (around_shift * (columns + 2) + codes // (3 * faces)) * faces + codes % faces
     every = tuple(range(columns))
     current = list(pack(start))
     basis = None
@@ -266,8 +267,8 @@
             stream = (shift(to_high, "stream", True), shift(to_low, "stream", False))
             middle = part(h, table, blocks, pieces[h], (to_low, to_high))
             after = middle
-            if h == 0 and index > 0:
-                basis, after = unpack(index - 1, every, *previous, basis, middle)
+            if index > 0 and h == (index == STEPS - 1):
+                basis, after = unpack(index - 1, every, *previous, basis, latest if h else middle)
             current[h] = latest = part(h, table, blocks, pieces[h], (*stream, middle, after))
             if index == STEPS - 2 and h == HALVES - 1:
                 outer = from_neighbours(jnp.stack([current[h][0], current[h][-1]]))

time: 116 us -> 113 us (0.974)
  starting transfers between devices: 58 us -> 43 us
  waiting for transfers between devices: 21.6 us -> 34.5 us
    ppermute x34, starting transfers between devices: 58 us -> 43 us  [shift(): return lax.ppermute(value, axis, pairs)]
    ppermute x34, waiting for transfers between devices: 21.6 us -> 34.5 us  [shift(): return lax.ppermute(value, axis, pairs)]
  transfers between devices with their start and end apart: 34 -> 34, of which waited for: 9 -> 17; matrix products, arithmetic and copies ran while one was open for 1% -> 1% of each run, Pallas kernels for 24% -> 24%
where the time goes in v16:
time: 113 us
  starting transfers between devices  43 us (38%)
  waiting for transfers between devices  34.5 us (31%)
  Pallas kernels  30.7 us (27%)
  local copies, waits for them, and re-layouts  3.23 us (3%)
    ppermute x34, starting transfers between devices, shift(): return lax.ppermute(value, axis, pairs)  43 us
    ppermute x34, waiting for transfers between devices, shift(): return lax.ppermute(value, axis, pairs)  34.5 us
    pallas_call x16, Pallas kernels, part(): pl.pallas_call(functools.partial(part_kernel, half), in_specs=in_specs, o...  23.6 us
    pallas_call x4, Pallas kernels, unpack(): pl.pallas_call(functools.partial(unpack_kernel, index, chosen, skipped),...  4.25 us
    unnamed x6, local copies, waits for them, and re-layouts  2.93 us
    pallas_call x1, Pallas kernels, halves_of_rows(): pl.pallas_call(halves_kernel, in_specs=[VMEM], out_specs=VMEM, out_shape=...  2.72 us
  transfers between devices with their start and end apart: 34, of which 17 were waited for; matrix products, arithmetic and copies ran while one was open for 1% of the time, Pallas kernels for 24%

profile of v16, /device:TPU:0, one launch (start us, length us, event | category | flops | bytes accessed | tf_op | source)
XLA Modules:
  0.0 112.6 jit_solution(10496884871440618611)
XLA Ops:
  0.0 1.0 copy-done.1
  1.0 0.2 pack.1
  1.2 3.1 %collective-permute-start = (bf16[4,8,32,128]{3,2,1,0:T(8,128)(2,1)S(1)}, bf16[4,8,32,128]{3,2,1,0:T(8,128)(2,1)S(1)}, u32[]{:S(2)}, u32[]{:S(2)}) collective-permute-start(bf16[4,8,32,128]{3,2,1,0:T(8,128)(2,1)S(1)} %get-tuple-element.45.refs_2_), channel_id=1, source_target_pairs={{0,1},{1,2},{2,3},{3,0},{4,5},{5,6},{6,7},{7,4},{8,9},{9,10},{10,1... | collective-permute-start | bytes 786440 | tf_op jit(solution)/shard_map/ppermute | solution.py:203
  4.3 2.1 %collective-permute-start.1 = (bf16[4,8,32,128]{3,2,1,0:T(8,128)(2,1)S(1)}, bf16[4,8,32,128]{3,2,1,0:T(8,128)(2,1)S(1)}, u32[]{:S(2)}, u32[]{:S(2)}) collective-permute-start(bf16[4,8,32,128]{3,2,1,0:T(8,128)(2,1)S(1)} %get-tuple-element.45.refs_2_), channel_id=1, source_target_pairs={{1,0},{2,1},{3,2},{0,3},{5,4},{6,5},{7,6},{4,7},{9,8},{10,9},{11,1... | collective-permute-start | bytes 786440 | tf_op jit(solution)/shard_map/ppermute | solution.py:203
  6.4 3.8 %collective-permute-start.7 = (bf16[4,8,32,128]{3,2,1,0:T(8,128)(2,1)S(1)}, bf16[4,8,32,128]{3,2,1,0:T(8,128)(2,1)S(1)}, u32[]{:S(2)}, u32[]{:S(2)}) collective-permute-start(bf16[4,8,32,128]{3,2,1,0:T(8,128)(2,1)S(1)} %get-tuple-element.49.refs_2_), channel_id=1, source_target_pairs={{1,0},{2,1},{3,2},{0,3},{5,4},{6,5},{7,6},{4,7},{9,8},{10,9},{11,1... | collective-permute-start | bytes 786440 | tf_op jit(solution)/shard_map/ppermute | solution.py:203
  10.2 1.9 %copy-done = bf16[4,1,8,64,768]{4,3,2,1,0:T(8,128)(2,1)S(1)} copy-done((bf16[4,1,8,64,768]{4,3,2,1,0:T(8,128)(2,1)S(1)}, bf16[4,1,8,64,768]{4,3,2,1,0:T(8,128)(2,1)}, u32[]{:S(2)}) %copy-start) | copy-done | bytes 3145752
  12.1 2.7 %halves_of_rows.1.refs_1_ = bf16[4,8,64,768]{3,2,1,0:T(8,128)(2,1)S(1)} custom-call(bf16[4,8,64,768]{3,2,1,0:T(8,128)(2,1)S(1)} %bitcast.29), custom_call_target="tpu_custom_call" | custom-call | tf_op jit(solution)/shard_map/halves_of_rows/pallas_call | solution.py:234
  14.9 4.4 %collective-permute-done.1.refs_4_ = bf16[4,8,32,128]{3,2,1,0:T(8,128)(2,1)S(1)} collective-permute-done((bf16[4,8,32,128]{3,2,1,0:T(8,128)(2,1)S(1)}, bf16[4,8,32,128]{3,2,1,0:T(8,128)(2,1)S(1)}, u32[]{:S(2)}, u32[]{:S(2)}) %collective-permute-start.1) | collective-permute-done | bytes 262176 | tf_op jit(solution)/shard_map/ppermute | solution.py:203
  19.5 0.5 collective-permute-start.2
  20.0 1.5 %inner_half0.4.refs_7_.refs_8_ = bf16[2,8,32,128]{3,2,1,0:T(8,128)(2,1)S(1)} custom-call(s32[8,12]{1,0:T(8,128)S(1)} %fusion.4.refs_0_, bf16[4,8,64,768]{3,2,1,0:T(8,128)(2,1)S(1)} %halves_of_rows.1.refs_1_, bf16[4,8,32,128]{3,2,1,0:T(8,128)(2,1)S(1)} %get-tuple-element.45.refs_2_, bf16[4,8,32,128]{3,2,1,0:T(8,128)(2,1)S(1)} %collective-permute-done.refs_3_, ...), custom_call_target="tpu_custom_call" | custom-call | flops 20132659200 | bytes 157286400 | tf_op jit(solution)/shard_map/inner_half0/pallas_call | solution.py:178
  21.5 1.9 %collective-permute-done.3.refs_6_ = bf16[3,8,32,128]{3,2,1,0:T(8,128)(2,1)S(1)} collective-permute-done((bf16[3,8,32,128]{3,2,1,0:T(8,128)(2,1)S(1)}, bf16[3,8,32,128]{3,2,1,0:T(8,128)(2,1)S(1)}, u32[]{:S(2)}, u32[]{:S(2)}) %collective-permute-start.3) | collective-permute-done | bytes 196640 | tf_op jit(solution)/shard_map/ppermute | solution.py:203
  23.4 4.2 %collective-permute-done.2.refs_5_ = bf16[3,8,32,128]{3,2,1,0:T(8,128)(2,1)S(1)} collective-permute-done((bf16[3,8,32,128]{3,2,1,0:T(8,128)(2,1)S(1)}, bf16[3,8,32,128]{3,2,1,0:T(8,128)(2,1)S(1)}, u32[]{:S(2)}, u32[]{:S(2)}) %collective-permute-start.2) | collective-permute-done | bytes 196640 | tf_op jit(solution)/shard_map/ppermute | solution.py:203
  27.7 1.5 %edge_half0.4.refs_2_.first_ref = bf16[4,8,32,128]{3,2,1,0:T(8,128)(2,1)S(1)} custom-call(s32[8,12]{1,0:T(8,128)S(1)} %fusion.4.refs_0_, bf16[4,8,64,768]{3,2,1,0:T(8,128)(2,1)S(1)} %halves_of_rows.1.refs_1_, bf16[4,8,32,128]{3,2,1,0:T(8,128)(2,1)S(1)} %get-tuple-element.45.refs_2_, bf16[4,8,32,128]{3,2,1,0:T(8,128)(2,1)S(1)} %collective-permute-done.refs_3_, ...), custom_call_target="tpu_custom_call" | custom-call | flops 20132659200 | bytes 157286400 | tf_op jit(solution)/shard_map/edge_half0/pallas_call | solution.py:178
  29.1 0.7 collective-permute-start.4
  29.9 3.2 %collective-permute-start.5 = (bf16[4,8,32,128]{3,2,1,0:T(8,128)(2,1)S(1)}, bf16[4,8,32,128]{3,2,1,0:T(8,128)(2,1)S(1)}, u32[]{:S(2)}, u32[]{:S(2)}) collective-permute-start(bf16[4,8,32,128]{3,2,1,0:T(8,128)(2,1)S(1)} %edge_half0.4.refs_2_.first_ref), channel_id=1, source_target_pairs={{1,0},{2,1},{3,2},{0,3},{5,4},{6,5},{7,6},{4,7},{9,8},{10,9},{11,1... | collective-permute-start | bytes 786440 | tf_op jit(solution)/shard_map/ppermute | solution.py:203
  33.2 0.5 collective-permute-start.8
  33.7 1.5 %inner_half1.4.refs_7_.refs_8_ = bf16[2,8,32,128]{3,2,1,0:T(8,128)(2,1)S(1)} custom-call(s32[8,12]{1,0:T(8,128)S(1)} %fusion.4.refs_0_, bf16[4,8,64,768]{3,2,1,0:T(8,128)(2,1)S(1)} %halves_of_rows.1.refs_1_, bf16[4,8,32,128]{3,2,1,0:T(8,128)(2,1)S(1)} %get-tuple-element.49.refs_2_, bf16[4,8,32,128]{3,2,1,0:T(8,128)(2,1)S(1)} %collective-permute-done.6.refs_3_, ...), custom_call_target="tpu_custom_call" | custom-call | flops 20132659200 | bytes 157286400 | tf_op jit(solution)/shard_map/inner_half1/pallas_call | solution.py:178
  35.2 3.1 %collective-permute-done.9.refs_6_ = bf16[3,8,32,128]{3,2,1,0:T(8,128)(2,1)S(1)} collective-permute-done((bf16[3,8,32,128]{3,2,1,0:T(8,128)(2,1)S(1)}, bf16[3,8,32,128]{3,2,1,0:T(8,128)(2,1)S(1)}, u32[]{:S(2)}, u32[]{:S(2)}) %collective-permute-start.9) | collective-permute-done | bytes 196640 | tf_op jit(solution)/shard_map/ppermute | solution.py:203
  38.4 1.8 %collective-permute-done.8.refs_5_ = bf16[3,8,32,128]{3,2,1,0:T(8,128)(2,1)S(1)} collective-permute-done((bf16[3,8,32,128]{3,2,1,0:T(8,128)(2,1)S(1)}, bf16[3,8,32,128]{3,2,1,0:T(8,128)(2,1)S(1)}, u32[]{:S(2)}, u32[]{:S(2)}) %collective-permute-start.8) | collective-permute-done | bytes 196640 | tf_op jit(solution)/shard_map/ppermute | solution.py:203
  40.2 1.5 %edge_half1.4.second_ref.refs_2_ = bf16[4,8,32,128]{3,2,1,0:T(8,128)(2,1)S(1)} custom-call(s32[8,12]{1,0:T(8,128)S(1)} %fusion.4.refs_0_, bf16[4,8,64,768]{3,2,1,0:T(8,128)(2,1)S(1)} %halves_of_rows.1.refs_1_, bf16[4,8,32,128]{3,2,1,0:T(8,128)(2,1)S(1)} %get-tuple-element.49.refs_2_, bf16[4,8,32,128]{3,2,1,0:T(8,128)(2,1)S(1)} %collective-permute-done.6.refs_3_, ...), custom_call_target="tpu_custom_call" | custom-call | flops 20132659200 | bytes 157286400 | tf_op jit(solution)/shard_map/edge_half1/pallas_call | solution.py:178
  41.7 0.1 collective-permute-start.14
  41.8 3.8 %collective-permute-start.15 = (bf16[4,8,32,128]{3,2,1,0:T(8,128)(2,1)S(1)}, bf16[4,8,32,128]{3,2,1,0:T(8,128)(2,1)S(1)}, u32[]{:S(2)}, u32[]{:S(2)}) collective-permute-start(bf16[4,8,32,128]{3,2,1,0:T(8,128)(2,1)S(1)} %edge_half1.4.second_ref.refs_2_), channel_id=1, source_target_pairs={{1,0},{2,1},{3,2},{0,3},{5,4},{6,5},{7,6},{4,7},{9,8},{10,9},{11,1... | collective-permute-start | bytes 786440 | tf_op jit(solution)/shard_map/ppermute | solution.py:203
  45.7 0.5 collective-permute-start.11
  46.1 0.2 collective-permute-start.10
  46.3 1.5 %inner_half0.5.refs_0_.refs_7_ = bf16[2,8,32,128]{3,2,1,0:T(8,128)(2,1)S(1)} custom-call(s32[8,12]{1,0:T(8,128)S(1)} %fusion.4.refs_0_, bf16[4,8,64,768]{3,2,1,0:T(8,128)(2,1)S(1)} %halves_of_rows.1.refs_1_, bf16[4,8,32,128]{3,2,1,0:T(8,128)(2,1)S(1)} %edge_half0.4.refs_2_.first_ref, bf16[4,8,32,128]{3,2,1,0:T(8,128)(2,1)S(1)} %collective-permute-done.4.refs_3_, ...), custom_call_target="tpu_custom_call" | custom-call | flops 20132659200 | bytes 157286400 | tf_op jit(solution)/shard_map/inner_half0/pallas_call | solution.py:178
  47.8 0.9 unpack.4
  48.7 2.4 %collective-permute-done.11.refs_6_ = bf16[3,8,32,128]{3,2,1,0:T(8,128)(2,1)S(1)} collective-permute-done((bf16[3,8,32,128]{3,2,1,0:T(8,128)(2,1)S(1)}, bf16[3,8,32,128]{3,2,1,0:T(8,128)(2,1)S(1)}, u32[]{:S(2)}, u32[]{:S(2)}) %collective-permute-start.11) | collective-permute-done | bytes 196640 | tf_op jit(solution)/shard_map/ppermute | solution.py:203
  51.1 1.3 %collective-permute-done.10.refs_5_ = bf16[3,8,32,128]{3,2,1,0:T(8,128)(2,1)S(1)} collective-permute-done((bf16[3,8,32,128]{3,2,1,0:T(8,128)(2,1)S(1)}, bf16[3,8,32,128]{3,2,1,0:T(8,128)(2,1)S(1)}, u32[]{:S(2)}, u32[]{:S(2)}) %collective-permute-start.10) | collective-permute-done | bytes 196640 | tf_op jit(solution)/shard_map/ppermute | solution.py:203
  52.3 1.5 %edge_half0.5.refs_2_.first_ref = bf16[4,8,32,128]{3,2,1,0:T(8,128)(2,1)S(1)} custom-call(s32[8,12]{1,0:T(8,128)S(1)} %fusion.4.refs_0_, bf16[4,8,64,768]{3,2,1,0:T(8,128)(2,1)S(1)} %halves_of_rows.1.refs_1_, bf16[4,8,32,128]{3,2,1,0:T(8,128)(2,1)S(1)} %edge_half0.4.refs_2_.first_ref, bf16[4,8,32,128]{3,2,1,0:T(8,128)(2,1)S(1)} %collective-permute-done.4.refs_3_, ...), custom_call_target="tpu_custom_call" | custom-call | flops 20132659200 | bytes 157286400 | tf_op jit(solution)/shard_map/edge_half0/pallas_call | solution.py:178
  53.8 0.1 collective-permute-start.12
  53.9 3.8 %collective-permute-start.13 = (bf16[4,8,32,128]{3,2,1,0:T(8,128)(2,1)S(1)}, bf16[4,8,32,128]{3,2,1,0:T(8,128)(2,1)S(1)}, u32[]{:S(2)}, u32[]{:S(2)}) collective-permute-start(bf16[4,8,32,128]{3,2,1,0:T(8,128)(2,1)S(1)} %edge_half0.5.refs_2_.first_ref), channel_id=1, source_target_pairs={{1,0},{2,1},{3,2},{0,3},{5,4},{6,5},{7,6},{4,7},{9,8},{10,9},{11,1... | collective-permute-start | bytes 786440 | tf_op jit(solution)/shard_map/ppermute | solution.py:203
  57.8 1.0 collective-permute-start.17
  58.9 1.5 %inner_half1.5.refs_7_.refs_8_ = bf16[2,8,32,128]{3,2,1,0:T(8,128)(2,1)S(1)} custom-call(s32[8,12]{1,0:T(8,128)S(1)} %fusion.4.refs_0_, bf16[4,8,64,768]{3,2,1,0:T(8,128)(2,1)S(1)} %halves_of_rows.1.refs_1_, bf16[4,8,32,128]{3,2,1,0:T(8,128)(2,1)S(1)} %edge_half1.4.second_ref.refs_2_, bf16[4,8,32,128]{3,2,1,0:T(8,128)(2,1)S(1)} %collective-permute-done.14.refs_3_, ...), custom_call_target="tpu_custom_call" | custom-call | flops 20132659200 | bytes 157286400 | tf_op jit(solution)/shard_map/inner_half1/pallas_call | solution.py:178
  60.4 3.1 %collective-permute-done.17.refs_6_ = bf16[3,8,32,128]{3,2,1,0:T(8,128)(2,1)S(1)} collective-permute-done((bf16[3,8,32,128]{3,2,1,0:T(8,128)(2,1)S(1)}, bf16[3,8,32,128]{3,2,1,0:T(8,128)(2,1)S(1)}, u32[]{:S(2)}, u32[]{:S(2)}) %collective-permute-start.17) | collective-permute-done | bytes 196640 | tf_op jit(solution)/shard_map/ppermute | solution.py:203
  63.5 1.4 %collective-permute-done.16.refs_5_ = bf16[3,8,32,128]{3,2,1,0:T(8,128)(2,1)S(1)} collective-permute-done((bf16[3,8,32,128]{3,2,1,0:T(8,128)(2,1)S(1)}, bf16[3,8,32,128]{3,2,1,0:T(8,128)(2,1)S(1)}, u32[]{:S(2)}, u32[]{:S(2)}) %collective-permute-start.16) | collective-permute-done | bytes 196640 | tf_op jit(solution)/shard_map/ppermute | solution.py:203
  64.9 1.5 %edge_half1.5.second_ref.refs_2_ = bf16[4,8,32,128]{3,2,1,0:T(8,128)(2,1)S(1)} custom-call(s32[8,12]{1,0:T(8,128)S(1)} %fusion.4.refs_0_, bf16[4,8,64,768]{3,2,1,0:T(8,128)(2,1)S(1)} %halves_of_rows.1.refs_1_, bf16[4,8,32,128]{3,2,1,0:T(8,128)(2,1)S(1)} %edge_half1.4.second_ref.refs_2_, bf16[4,8,32,128]{3,2,1,0:T(8,128)(2,1)S(1)} %collective-permute-done.14.refs_3_, ...), custom_call_target="tpu_custom_call" | custom-call | flops 20132659200 | bytes 157286400 | tf_op jit(solution)/shard_map/edge_half1/pallas_call | solution.py:178
  66.4 0.1 collective-permute-start.22
  66.4 3.8 %collective-permute-start.23 = (bf16[4,8,32,128]{3,2,1,0:T(8,128)(2,1)S(1)}, bf16[4,8,32,128]{3,2,1,0:T(8,128)(2,1)S(1)}, u32[]{:S(2)}, u32[]{:S(2)}) collective-permute-start(bf16[4,8,32,128]{3,2,1,0:T(8,128)(2,1)S(1)} %edge_half1.5.second_ref.refs_2_), channel_id=1, source_target_pairs={{1,0},{2,1},{3,2},{0,3},{5,4},{6,5},{7,6},{4,7},{9,8},{10,9},{11,1... | collective-permute-start | bytes 786440 | tf_op jit(solution)/shard_map/ppermute | solution.py:203
  70.3 0.9 collective-permute-start.19
  71.4 1.5 %inner_half0.6.refs_1_.refs_7_ = bf16[2,8,32,128]{3,2,1,0:T(8,128)(2,1)S(1)} custom-call(s32[8,12]{1,0:T(8,128)S(1)} %fusion.4.refs_0_, bf16[4,8,64,768]{3,2,1,0:T(8,128)(2,1)S(1)} %halves_of_rows.1.refs_1_, bf16[4,8,32,128]{3,2,1,0:T(8,128)(2,1)S(1)} %edge_half0.5.refs_2_.first_ref, bf16[4,8,32,128]{3,2,1,0:T(8,128)(2,1)S(1)} %collective-permute-done.12.refs_3_, ...), custom_call_target="tpu_custom_call" | custom-call | flops 20132659200 | bytes 157286400 | tf_op jit(solution)/shard_map/inner_half0/pallas_call | solution.py:178
  72.9 0.9 unpack.5
  73.8 2.0 %collective-permute-done.19.refs_6_ = bf16[3,8,32,128]{3,2,1,0:T(8,128)(2,1)S(1)} collective-permute-done((bf16[3,8,32,128]{3,2,1,0:T(8,128)(2,1)S(1)}, bf16[3,8,32,128]{3,2,1,0:T(8,128)(2,1)S(1)}, u32[]{:S(2)}, u32[]{:S(2)}) %collective-permute-start.19) | collective-permute-done | bytes 196640 | tf_op jit(solution)/shard_map/ppermute | solution.py:203
  75.8 1.5 %collective-permute-done.18.refs_5_ = bf16[3,8,32,128]{3,2,1,0:T(8,128)(2,1)S(1)} collective-permute-done((bf16[3,8,32,128]{3,2,1,0:T(8,128)(2,1)S(1)}, bf16[3,8,32,128]{3,2,1,0:T(8,128)(2,1)S(1)}, u32[]{:S(2)}, u32[]{:S(2)}) %collective-permute-start.18) | collective-permute-done | bytes 196640 | tf_op jit(solution)/shard_map/ppermute | solution.py:203
  77.4 1.5 %edge_half0.6.refs_2_.first_ref = bf16[4,8,32,128]{3,2,1,0:T(8,128)(2,1)S(1)} custom-call(s32[8,12]{1,0:T(8,128)S(1)} %fusion.4.refs_0_, bf16[4,8,64,768]{3,2,1,0:T(8,128)(2,1)S(1)} %halves_of_rows.1.refs_1_, bf16[4,8,32,128]{3,2,1,0:T(8,128)(2,1)S(1)} %edge_half0.5.refs_2_.first_ref, bf16[4,8,32,128]{3,2,1,0:T(8,128)(2,1)S(1)} %collective-permute-done.12.refs_3_, ...), custom_call_target="tpu_custom_call" | custom-call | flops 20132659200 | bytes 157286400 | tf_op jit(solution)/shard_map/edge_half0/pallas_call | solution.py:178
  78.9 3.8 %collective-permute-start.21 = (bf16[4,8,32,128]{3,2,1,0:T(8,128)(2,1)S(1)}, bf16[4,8,32,128]{3,2,1,0:T(8,128)(2,1)S(1)}, u32[]{:S(2)}, u32[]{:S(2)}) collective-permute-start(bf16[4,8,32,128]{3,2,1,0:T(8,128)(2,1)S(1)} %edge_half0.6.refs_2_.first_ref), channel_id=1, source_target_pairs={{1,0},{2,1},{3,2},{0,3},{5,4},{6,5},{7,6},{4,7},{9,8},{10,9},{11,1... | collective-permute-start | bytes 786440 | tf_op jit(solution)/shard_map/ppermute | solution.py:203
  82.8 0.8 collective-permute-start.25
  83.7 1.5 %inner_half1.6.refs_7_.refs_8_ = bf16[2,8,32,128]{3,2,1,0:T(8,128)(2,1)S(1)} custom-call(s32[8,12]{1,0:T(8,128)S(1)} %fusion.4.refs_0_, bf16[4,8,64,768]{3,2,1,0:T(8,128)(2,1)S(1)} %halves_of_rows.1.refs_1_, bf16[4,8,32,128]{3,2,1,0:T(8,128)(2,1)S(1)} %edge_half1.5.second_ref.refs_2_, bf16[4,8,32,128]{3,2,1,0:T(8,128)(2,1)S(1)} %collective-permute-done.22.refs_3_, ...), custom_call_target="tpu_custom_call" | custom-call | flops 20132659200 | bytes 157286400 | tf_op jit(solution)/shard_map/inner_half1/pallas_call | solution.py:178
  85.1 2.9 %collective-permute-done.25.refs_6_ = bf16[3,8,32,128]{3,2,1,0:T(8,128)(2,1)S(1)} collective-permute-done((bf16[3,8,32,128]{3,2,1,0:T(8,128)(2,1)S(1)}, bf16[3,8,32,128]{3,2,1,0:T(8,128)(2,1)S(1)}, u32[]{:S(2)}, u32[]{:S(2)}) %collective-permute-start.25) | collective-permute-done | bytes 196640 | tf_op jit(solution)/shard_map/ppermute | solution.py:203
  88.1 1.7 %collective-permute-done.24.refs_5_ = bf16[3,8,32,128]{3,2,1,0:T(8,128)(2,1)S(1)} collective-permute-done((bf16[3,8,32,128]{3,2,1,0:T(8,128)(2,1)S(1)}, bf16[3,8,32,128]{3,2,1,0:T(8,128)(2,1)S(1)}, u32[]{:S(2)}, u32[]{:S(2)}) %collective-permute-start.24) | collective-permute-done | bytes 196640 | tf_op jit(solution)/shard_map/ppermute | solution.py:203
  89.7 1.5 %edge_half1.6.refs_2_.second_ref = bf16[4,8,32,128]{3,2,1,0:T(8,128)(2,1)S(1)} custom-call(s32[8,12]{1,0:T(8,128)S(1)} %fusion.4.refs_0_, bf16[4,8,64,768]{3,2,1,0:T(8,128)(2,1)S(1)} %halves_of_rows.1.refs_1_, bf16[4,8,32,128]{3,2,1,0:T(8,128)(2,1)S(1)} %edge_half1.5.second_ref.refs_2_, bf16[4,8,32,128]{3,2,1,0:T(8,128)(2,1)S(1)} %collective-permute-done.22.refs_3_, ...), custom_call_target="tpu_custom_call" | custom-call | flops 20132659200 | bytes 157286400 | tf_op jit(solution)/shard_map/edge_half1/pallas_call | solution.py:178
  91.3 3.8 %collective-permute-start.29 = (bf16[2,8,32,128]{3,2,1,0:T(8,128)(2,1)S(1)}, bf16[2,8,32,128]{3,2,1,0:T(8,128)(2,1)S(1)}, u32[]{:S(2)}, u32[]{:S(2)}) collective-permute-start(bf16[2,8,32,128]{3,2,1,0:T(8,128)(2,1)S(1)} %pad_maximum_fusion.18), channel_id=1, source_target_pairs={{1,0},{2,1},{3,2},{0,3},{5,4},{6,5},{7,6},{4,7},{9,8},{10,9},{11,1... | collective-permute-start | bytes 393224 | tf_op jit(solution)/shard_map/ppermute | solution.py:203
  95.2 0.6 collective-permute-start.27
  96.0 1.5 %inner_half0.7.refs_7_.refs_8_ = bf16[2,8,32,128]{3,2,1,0:T(8,128)(2,1)S(1)} custom-call(s32[8,12]{1,0:T(8,128)S(1)} %fusion.4.refs_0_, bf16[4,8,64,768]{3,2,1,0:T(8,128)(2,1)S(1)} %halves_of_rows.1.refs_1_, bf16[4,8,32,128]{3,2,1,0:T(8,128)(2,1)S(1)} %edge_half0.6.refs_2_.first_ref, bf16[4,8,32,128]{3,2,1,0:T(8,128)(2,1)S(1)} %collective-permute-done.20.refs_3_, ...), custom_call_target="tpu_custom_call" | custom-call | flops 20132659200 | bytes 157286400 | tf_op jit(solution)/shard_map/inner_half0/pallas_call | solution.py:178
  97.5 0.6 collective-permute-done.28
  98.2 3.2 %collective-permute-start.31 = (bf16[2,8,32,128]{3,2,1,0:T(8,128)(2,1)S(1)}, bf16[2,8,32,128]{3,2,1,0:T(8,128)(2,1)S(1)}, u32[]{:S(2)}, u32[]{:S(2)}) collective-permute-start(bf16[2,8,32,128]{3,2,1,0:T(8,128)(2,1)S(1)} %slice.222), channel_id=1, source_target_pairs={{1,0},{2,1},{3,2},{0,3},{5,4},{6,5},{7,6},{4,7},{9,8},{10,9},{11,1... | collective-permute-start | bytes 393224 | tf_op jit(solution)/shard_map/ppermute | solution.py:203
  101.4 2.1 %collective-permute-start.33 = (bf16[3,8,32,128]{3,2,1,0:T(8,128)(2,1)S(1)}, bf16[3,8,32,128]{3,2,1,0:T(8,128)(2,1)S(1)}, u32[]{:S(2)}, u32[]{:S(2)}) collective-permute-start(bf16[3,8,32,128]{3,2,1,0:T(8,128)(2,1)S(1)} %pad_maximum_fusion.17.refs_5_), channel_id=1, source_target_pairs={{4,0},{8,4},{12,8},{16,12},{20,16},{24,20},{28,24},{0,28},{5,1},{9... | collective-permute-start | bytes 589832 | tf_op jit(solution)/shard_map/ppermute | solution.py:203
  103.7 1.5 %edge_half0.7.refs_1_.first_ref = bf16[4,8,32,128]{3,2,1,0:T(8,128)(2,1)S(1)} custom-call(s32[8,12]{1,0:T(8,128)S(1)} %fusion.4.refs_0_, bf16[4,8,64,768]{3,2,1,0:T(8,128)(2,1)S(1)} %halves_of_rows.1.refs_1_, bf16[4,8,32,128]{3,2,1,0:T(8,128)(2,1)S(1)} %edge_half0.6.refs_2_.first_ref, bf16[4,8,32,128]{3,2,1,0:T(8,128)(2,1)S(1)} %collective-permute-done.20.refs_3_, ...), custom_call_target="tpu_custom_call" | custom-call | flops 20132659200 | bytes 157286400 | tf_op jit(solution)/shard_map/edge_half0/pallas_call | solution.py:178
  105.2 0.5 collective-permute-done.30
  105.7 0.2 collective-permute-done.31
  106.1 1.5 %inner_half1.7.refs_7_ = bf16[2,8,32,128]{3,2,1,0:T(8,128)(2,1)S(1)} custom-call(s32[8,12]{1,0:T(8,128)S(1)} %fusion.4.refs_0_, bf16[4,8,64,768]{3,2,1,0:T(8,128)(2,1)S(1)} %halves_of_rows.1.refs_1_, bf16[4,8,32,128]{3,2,1,0:T(8,128)(2,1)S(1)} %edge_half1.6.refs_2_.second_ref, bf16[4,8,32,128]{3,2,1,0:T(8,128)(2,1)S(1)} %pad_maximum_fusion.refs_3_, ...), custom_call_target="tpu_custom_call" | custom-call | flops 20132659200 | bytes 157286400 | tf_op jit(solution)/shard_map/inner_half1/pallas_call | solution.py:178
  107.5 0.9 unpack.6
  108.5 1.2 %collective-permute-done.32.refs_5_ = bf16[3,8,32,128]{3,2,1,0:T(8,128)(2,1)S(1)} collective-permute-done((bf16[3,8,32,128]{3,2,1,0:T(8,128)(2,1)S(1)}, bf16[3,8,32,128]{3,2,1,0:T(8,128)(2,1)S(1)}, u32[]{:S(2)}, u32[]{:S(2)}) %collective-permute-start.32) | collective-permute-done | bytes 196640 | tf_op jit(solution)/shard_map/ppermute | solution.py:203
  109.6 1.5 %edge_half1.7.second_ref = bf16[4,8,32,128]{3,2,1,0:T(8,128)(2,1)S(1)} custom-call(s32[8,12]{1,0:T(8,128)S(1)} %fusion.4.refs_0_, bf16[4,8,64,768]{3,2,1,0:T(8,128)(2,1)S(1)} %halves_of_rows.1.refs_1_, bf16[4,8,32,128]{3,2,1,0:T(8,128)(2,1)S(1)} %edge_half1.6.refs_2_.second_ref, bf16[4,8,32,128]{3,2,1,0:T(8,128)(2,1)S(1)} %pad_maximum_fusion.refs_3_, ...), custom_call_target="tpu_custom_call" | custom-call | flops 20132659200 | bytes 157286400 | tf_op jit(solution)/shard_map/edge_half1/pallas_call | solution.py:178
  111.1 1.5 %unpack.7 = (bf16[4,4,8,64,128]{4,3,2,1,0:T(8,128)(2,1)}, f32[8,128]{1,0:T(8,128)}) custom-call(bf16[4,8,32,128]{3,2,1,0:T(8,128)(2,1)S(1)} %edge_half0.7.refs_1_.first_ref, bf16[4,8,32,128]{3,2,1,0:T(8,128)(2,1)S(1)} %edge_half1.7.second_ref, bf16[4,4,8,64,128]{4,3,2,1,0:T(8,128)(2,1)} %get-tuple-element.79.refs_0_), custom_call_target="tpu_custom_call", output_to_operand_aliasing={{0}: (2, {})} | custom-call | tf_op jit(solution)/shard_map/unpack/pallas_call | solution.py:77
  (79 shorter events, 1.4 us)
Async XLA Ops:
  0.0 1.0 copy-start.1
  1.2 13.7 %collective-permute-start = (bf16[4,8,32,128]{3,2,1,0:T(8,128)(2,1)S(1)}, bf16[4,8,32,128]{3,2,1,0:T(8,128)(2,1)S(1)}, u32[]{:S(2)}, u32[]{:S(2)}) collective-permute-start(bf16[4,8,32,128]{3,2,1,0:T(8,128)(2,1)S(1)} %get-tuple-element.45.refs_2_), channel_id=1, source_target_pairs={{0,1},{1,2},{2,3},{3,0},{4,5},{5,6},{6,7},{7,4},{8,9},{9,10},{10,1... | collective-permute-start | bytes 786440 | tf_op jit(solution)/shard_map/ppermute | solution.py:203
  4.3 15.0 %collective-permute-start.1 = (bf16[4,8,32,128]{3,2,1,0:T(8,128)(2,1)S(1)}, bf16[4,8,32,128]{3,2,1,0:T(8,128)(2,1)S(1)}, u32[]{:S(2)}, u32[]{:S(2)}) collective-permute-start(bf16[4,8,32,128]{3,2,1,0:T(8,128)(2,1)S(1)} %get-tuple-element.45.refs_2_), channel_id=1, source_target_pairs={{1,0},{2,1},{3,2},{0,3},{5,4},{6,5},{7,6},{4,7},{9,8},{10,9},{11,1... | collective-permute-start | bytes 786440 | tf_op jit(solution)/shard_map/ppermute | solution.py:203
  6.4 26.6 %collective-permute-start.6 = (bf16[4,8,32,128]{3,2,1,0:T(8,128)(2,1)S(1)}, bf16[4,8,32,128]{3,2,1,0:T(8,128)(2,1)S(1)}, u32[]{:S(2)}, u32[]{:S(2)}) collective-permute-start(bf16[4,8,32,128]{3,2,1,0:T(8,128)(2,1)S(1)} %get-tuple-element.49.refs_2_), channel_id=1, source_target_pairs={{0,1},{1,2},{2,3},{3,0},{4,5},{5,6},{6,7},{7,4},{8,9},{9,10},{10,1... | collective-permute-start | bytes 786440 | tf_op jit(solution)/shard_map/ppermute | solution.py:203
  6.4 26.6 %collective-permute-start.7 = (bf16[4,8,32,128]{3,2,1,0:T(8,128)(2,1)S(1)}, bf16[4,8,32,128]{3,2,1,0:T(8,128)(2,1)S(1)}, u32[]{:S(2)}, u32[]{:S(2)}) collective-permute-start(bf16[4,8,32,128]{3,2,1,0:T(8,128)(2,1)S(1)} %get-tuple-element.49.refs_2_), channel_id=1, source_target_pairs={{1,0},{2,1},{3,2},{0,3},{5,4},{6,5},{7,6},{4,7},{9,8},{10,9},{11,1... | collective-permute-start | bytes 786440 | tf_op jit(solution)/shard_map/ppermute | solution.py:203
  10.2 1.9 %copy-start = (bf16[4,1,8,64,768]{4,3,2,1,0:T(8,128)(2,1)S(1)}, bf16[4,1,8,64,768]{4,3,2,1,0:T(8,128)(2,1)}, u32[]{:S(2)}) copy-start(bf16[4,1,8,64,768]{4,3,2,1,0:T(8,128)(2,1)} %param.4) | copy-start | bytes 9437188
  12.1 2.7 %copy-start.2 = (s32[1,8,12]{2,1,0:T(8,128)S(1)}, s32[1,8,12]{2,1,0:T(8,128)}, u32[]{:S(2)}) copy-start(s32[1,8,12]{2,1,0:T(8,128)} %param.5) | copy-start | bytes 1156
  19.4 4.1 %collective-permute-start.3 = (bf16[3,8,32,128]{3,2,1,0:T(8,128)(2,1)S(1)}, bf16[3,8,32,128]{3,2,1,0:T(8,128)(2,1)S(1)}, u32[]{:S(2)}, u32[]{:S(2)}) collective-permute-start(bf16[3,8,32,128]{3,2,1,0:T(8,128)(2,1)S(1)} %pad_maximum_fusion.3.refs_5_), channel_id=1, source_target_pairs={{4,0},{8,4},{12,8},{16,12},{20,16},{24,20},{28,24},{0,28},{5,1},{9... | collective-permute-start | bytes 589832 | tf_op jit(solution)/shard_map/ppermute | solution.py:203
  19.5 8.2 %collective-permute-start.2 = (bf16[3,8,32,128]{3,2,1,0:T(8,128)(2,1)S(1)}, bf16[3,8,32,128]{3,2,1,0:T(8,128)(2,1)S(1)}, u32[]{:S(2)}, u32[]{:S(2)}) collective-permute-start(bf16[3,8,32,128]{3,2,1,0:T(8,128)(2,1)S(1)} %pad_maximum_fusion.2.refs_6_), channel_id=1, source_target_pairs={{0,4},{4,8},{8,12},{12,16},{16,20},{20,24},{24,28},{28,0},{1,5},{5... | collective-permute-start | bytes 589832 | tf_op jit(solution)/shard_map/ppermute | solution.py:203
  29.1 16.4 %collective-permute-start.4 = (bf16[4,8,32,128]{3,2,1,0:T(8,128)(2,1)S(1)}, bf16[4,8,32,128]{3,2,1,0:T(8,128)(2,1)S(1)}, u32[]{:S(2)}, u32[]{:S(2)}) collective-permute-start(bf16[4,8,32,128]{3,2,1,0:T(8,128)(2,1)S(1)} %edge_half0.4.refs_2_.first_ref), channel_id=1, source_target_pairs={{0,1},{1,2},{2,3},{3,0},{4,5},{5,6},{6,7},{7,4},{8,9},{9,10},{10,1... | collective-permute-start | bytes 786440 | tf_op jit(solution)/shard_map/ppermute | solution.py:203
  29.9 15.7 %collective-permute-start.5 = (bf16[4,8,32,128]{3,2,1,0:T(8,128)(2,1)S(1)}, bf16[4,8,32,128]{3,2,1,0:T(8,128)(2,1)S(1)}, u32[]{:S(2)}, u32[]{:S(2)}) collective-permute-start(bf16[4,8,32,128]{3,2,1,0:T(8,128)(2,1)S(1)} %edge_half0.4.refs_2_.first_ref), channel_id=1, source_target_pairs={{1,0},{2,1},{3,2},{0,3},{5,4},{6,5},{7,6},{4,7},{9,8},{10,9},{11,1... | collective-permute-start | bytes 786440 | tf_op jit(solution)/shard_map/ppermute | solution.py:203
  33.1 5.3 %collective-permute-start.9 = (bf16[3,8,32,128]{3,2,1,0:T(8,128)(2,1)S(1)}, bf16[3,8,32,128]{3,2,1,0:T(8,128)(2,1)S(1)}, u32[]{:S(2)}, u32[]{:S(2)}) collective-permute-start(bf16[3,8,32,128]{3,2,1,0:T(8,128)(2,1)S(1)} %pad_maximum_fusion.5.refs_5_), channel_id=1, source_target_pairs={{4,0},{8,4},{12,8},{16,12},{20,16},{24,20},{28,24},{0,28},{5,1},{9... | collective-permute-start | bytes 589832 | tf_op jit(solution)/shard_map/ppermute | solution.py:203
  33.2 7.0 %collective-permute-start.8 = (bf16[3,8,32,128]{3,2,1,0:T(8,128)(2,1)S(1)}, bf16[3,8,32,128]{3,2,1,0:T(8,128)(2,1)S(1)}, u32[]{:S(2)}, u32[]{:S(2)}) collective-permute-start(bf16[3,8,32,128]{3,2,1,0:T(8,128)(2,1)S(1)} %pad_maximum_fusion.4.refs_6_), channel_id=1, source_target_pairs={{0,4},{4,8},{8,12},{12,16},{16,20},{20,24},{24,28},{28,0},{1,5},{5... | collective-permute-start | bytes 589832 | tf_op jit(solution)/shard_map/ppermute | solution.py:203
  41.7 16.0 %collective-permute-start.14 = (bf16[4,8,32,128]{3,2,1,0:T(8,128)(2,1)S(1)}, bf16[4,8,32,128]{3,2,1,0:T(8,128)(2,1)S(1)}, u32[]{:S(2)}, u32[]{:S(2)}) collective-permute-start(bf16[4,8,32,128]{3,2,1,0:T(8,128)(2,1)S(1)} %edge_half1.4.second_ref.refs_2_), channel_id=1, source_target_pairs={{0,1},{1,2},{2,3},{3,0},{4,5},{5,6},{6,7},{7,4},{8,9},{9,10},{10,1... | collective-permute-start | bytes 786440 | tf_op jit(solution)/shard_map/ppermute | solution.py:203
  41.8 16.0 %collective-permute-start.15 = (bf16[4,8,32,128]{3,2,1,0:T(8,128)(2,1)S(1)}, bf16[4,8,32,128]{3,2,1,0:T(8,128)(2,1)S(1)}, u32[]{:S(2)}, u32[]{:S(2)}) collective-permute-start(bf16[4,8,32,128]{3,2,1,0:T(8,128)(2,1)S(1)} %edge_half1.4.second_ref.refs_2_), channel_id=1, source_target_pairs={{1,0},{2,1},{3,2},{0,3},{5,4},{6,5},{7,6},{4,7},{9,8},{10,9},{11,1... | collective-permute-start | bytes 786440 | tf_op jit(solution)/shard_map/ppermute | solution.py:203
  45.7 5.4 %collective-permute-start.11 = (bf16[3,8,32,128]{3,2,1,0:T(8,128)(2,1)S(1)}, bf16[3,8,32,128]{3,2,1,0:T(8,128)(2,1)S(1)}, u32[]{:S(2)}, u32[]{:S(2)}) collective-permute-start(bf16[3,8,32,128]{3,2,1,0:T(8,128)(2,1)S(1)} %pad_maximum_fusion.7.refs_5_), channel_id=1, source_target_pairs={{4,0},{8,4},{12,8},{16,12},{20,16},{24,20},{28,24},{0,28},{5,1},{9... | collective-permute-start | bytes 589832 | tf_op jit(solution)/shard_map/ppermute | solution.py:203
  46.1 6.2 %collective-permute-start.10 = (bf16[3,8,32,128]{3,2,1,0:T(8,128)(2,1)S(1)}, bf16[3,8,32,128]{3,2,1,0:T(8,128)(2,1)S(1)}, u32[]{:S(2)}, u32[]{:S(2)}) collective-permute-start(bf16[3,8,32,128]{3,2,1,0:T(8,128)(2,1)S(1)} %pad_maximum_fusion.6.refs_6_), channel_id=1, source_target_pairs={{0,4},{4,8},{8,12},{12,16},{16,20},{20,24},{24,28},{28,0},{1,5},{5... | collective-permute-start | bytes 589832 | tf_op jit(solution)/shard_map/ppermute | solution.py:203
  53.8 16.4 %collective-permute-start.12 = (bf16[4,8,32,128]{3,2,1,0:T(8,128)(2,1)S(1)}, bf16[4,8,32,128]{3,2,1,0:T(8,128)(2,1)S(1)}, u32[]{:S(2)}, u32[]{:S(2)}) collective-permute-start(bf16[4,8,32,128]{3,2,1,0:T(8,128)(2,1)S(1)} %edge_half0.5.refs_2_.first_ref), channel_id=1, source_target_pairs={{0,1},{1,2},{2,3},{3,0},{4,5},{5,6},{6,7},{7,4},{8,9},{9,10},{10,1... | collective-permute-start | bytes 786440 | tf_op jit(solution)/shard_map/ppermute | solution.py:203
  53.9 16.4 %collective-permute-start.13 = (bf16[4,8,32,128]{3,2,1,0:T(8,128)(2,1)S(1)}, bf16[4,8,32,128]{3,2,1,0:T(8,128)(2,1)S(1)}, u32[]{:S(2)}, u32[]{:S(2)}) collective-permute-start(bf16[4,8,32,128]{3,2,1,0:T(8,128)(2,1)S(1)} %edge_half0.5.refs_2_.first_ref), channel_id=1, source_target_pairs={{1,0},{2,1},{3,2},{0,3},{5,4},{6,5},{7,6},{4,7},{9,8},{10,9},{11,1... | collective-permute-start | bytes 786440 | tf_op jit(solution)/shard_map/ppermute | solution.py:203
  57.8 5.7 %collective-permute-start.17 = (bf16[3,8,32,128]{3,2,1,0:T(8,128)(2,1)S(1)}, bf16[3,8,32,128]{3,2,1,0:T(8,128)(2,1)S(1)}, u32[]{:S(2)}, u32[]{:S(2)}) collective-permute-start(bf16[3,8,32,128]{3,2,1,0:T(8,128)(2,1)S(1)} %pad_maximum_fusion.9.refs_5_), channel_id=1, source_target_pairs={{4,0},{8,4},{12,8},{16,12},{20,16},{24,20},{28,24},{0,28},{5,1},{9... | collective-permute-start | bytes 589832 | tf_op jit(solution)/shard_map/ppermute | solution.py:203
  58.8 6.0 %collective-permute-start.16 = (bf16[3,8,32,128]{3,2,1,0:T(8,128)(2,1)S(1)}, bf16[3,8,32,128]{3,2,1,0:T(8,128)(2,1)S(1)}, u32[]{:S(2)}, u32[]{:S(2)}) collective-permute-start(bf16[3,8,32,128]{3,2,1,0:T(8,128)(2,1)S(1)} %pad_maximum_fusion.8.refs_6_), channel_id=1, source_target_pairs={{0,4},{4,8},{8,12},{12,16},{16,20},{20,24},{24,28},{28,0},{1,5},{5... | collective-permute-start | bytes 589832 | tf_op jit(solution)/shard_map/ppermute | solution.py:203
  66.4 16.3 %collective-permute-start.22 = (bf16[4,8,32,128]{3,2,1,0:T(8,128)(2,1)S(1)}, bf16[4,8,32,128]{3,2,1,0:T(8,128)(2,1)S(1)}, u32[]{:S(2)}, u32[]{:S(2)}) collective-permute-start(bf16[4,8,32,128]{3,2,1,0:T(8,128)(2,1)S(1)} %edge_half1.5.second_ref.refs_2_), channel_id=1, source_target_pairs={{0,1},{1,2},{2,3},{3,0},{4,5},{5,6},{6,7},{7,4},{8,9},{9,10},{10,1... | collective-permute-start | bytes 786440 | tf_op jit(solution)/shard_map/ppermute | solution.py:203
  66.4 16.3 %collective-permute-start.23 = (bf16[4,8,32,128]{3,2,1,0:T(8,128)(2,1)S(1)}, bf16[4,8,32,128]{3,2,1,0:T(8,128)(2,1)S(1)}, u32[]{:S(2)}, u32[]{:S(2)}) collective-permute-start(bf16[4,8,32,128]{3,2,1,0:T(8,128)(2,1)S(1)} %edge_half1.5.second_ref.refs_2_), channel_id=1, source_target_pairs={{1,0},{2,1},{3,2},{0,3},{5,4},{6,5},{7,6},{4,7},{9,8},{10,9},{11,1... | collective-permute-start | bytes 786440 | tf_op jit(solution)/shard_map/ppermute | solution.py:203
  70.3 5.5 %collective-permute-start.19 = (bf16[3,8,32,128]{3,2,1,0:T(8,128)(2,1)S(1)}, bf16[3,8,32,128]{3,2,1,0:T(8,128)(2,1)S(1)}, u32[]{:S(2)}, u32[]{:S(2)}) collective-permute-start(bf16[3,8,32,128]{3,2,1,0:T(8,128)(2,1)S(1)} %pad_maximum_fusion.11.refs_5_), channel_id=1, source_target_pairs={{4,0},{8,4},{12,8},{16,12},{20,16},{24,20},{28,24},{0,28},{5,1},{9... | collective-permute-start | bytes 589832 | tf_op jit(solution)/shard_map/ppermute | solution.py:203
  71.3 6.0 %collective-permute-start.18 = (bf16[3,8,32,128]{3,2,1,0:T(8,128)(2,1)S(1)}, bf16[3,8,32,128]{3,2,1,0:T(8,128)(2,1)S(1)}, u32[]{:S(2)}, u32[]{:S(2)}) collective-permute-start(bf16[3,8,32,128]{3,2,1,0:T(8,128)(2,1)S(1)} %pad_maximum_fusion.10.refs_6_), channel_id=1, source_target_pairs={{0,4},{4,8},{8,12},{12,16},{16,20},{20,24},{24,28},{28,0},{1,5},{5... | collective-permute-start | bytes 589832 | tf_op jit(solution)/shard_map/ppermute | solution.py:203
  78.8 16.3 %collective-permute-start.20 = (bf16[4,8,32,128]{3,2,1,0:T(8,128)(2,1)S(1)}, bf16[4,8,32,128]{3,2,1,0:T(8,128)(2,1)S(1)}, u32[]{:S(2)}, u32[]{:S(2)}) collective-permute-start(bf16[4,8,32,128]{3,2,1,0:T(8,128)(2,1)S(1)} %edge_half0.6.refs_2_.first_ref), channel_id=1, source_target_pairs={{0,1},{1,2},{2,3},{3,0},{4,5},{5,6},{6,7},{7,4},{8,9},{9,10},{10,1... | collective-permute-start | bytes 786440 | tf_op jit(solution)/shard_map/ppermute | solution.py:203
  78.9 16.2 %collective-permute-start.21 = (bf16[4,8,32,128]{3,2,1,0:T(8,128)(2,1)S(1)}, bf16[4,8,32,128]{3,2,1,0:T(8,128)(2,1)S(1)}, u32[]{:S(2)}, u32[]{:S(2)}) collective-permute-start(bf16[4,8,32,128]{3,2,1,0:T(8,128)(2,1)S(1)} %edge_half0.6.refs_2_.first_ref), channel_id=1, source_target_pairs={{1,0},{2,1},{3,2},{0,3},{5,4},{6,5},{7,6},{4,7},{9,8},{10,9},{11,1... | collective-permute-start | bytes 786440 | tf_op jit(solution)/shard_map/ppermute | solution.py:203
  82.8 5.3 %collective-permute-start.25 = (bf16[3,8,32,128]{3,2,1,0:T(8,128)(2,1)S(1)}, bf16[3,8,32,128]{3,2,1,0:T(8,128)(2,1)S(1)}, u32[]{:S(2)}, u32[]{:S(2)}) collective-permute-start(bf16[3,8,32,128]{3,2,1,0:T(8,128)(2,1)S(1)} %pad_maximum_fusion.13.refs_5_), channel_id=1, source_target_pairs={{4,0},{8,4},{12,8},{16,12},{20,16},{24,20},{28,24},{0,28},{5,1},{9... | collective-permute-start | bytes 589832 | tf_op jit(solution)/shard_map/ppermute | solution.py:203
  83.6 6.1 %collective-permute-start.24 = (bf16[3,8,32,128]{3,2,1,0:T(8,128)(2,1)S(1)}, bf16[3,8,32,128]{3,2,1,0:T(8,128)(2,1)S(1)}, u32[]{:S(2)}, u32[]{:S(2)}) collective-permute-start(bf16[3,8,32,128]{3,2,1,0:T(8,128)(2,1)S(1)} %pad_maximum_fusion.12.refs_6_), channel_id=1, source_target_pairs={{0,4},{4,8},{8,12},{12,16},{16,20},{20,24},{24,28},{28,0},{1,5},{5... | collective-permute-start | bytes 589832 | tf_op jit(solution)/shard_map/ppermute | solution.py:203
  91.2 6.9 %collective-permute-start.28 = (bf16[2,8,32,128]{3,2,1,0:T(8,128)(2,1)S(1)}, bf16[2,8,32,128]{3,2,1,0:T(8,128)(2,1)S(1)}, u32[]{:S(2)}, u32[]{:S(2)}) collective-permute-start(bf16[2,8,32,128]{3,2,1,0:T(8,128)(2,1)S(1)} %pad_maximum_fusion.18), channel_id=1, source_target_pairs={{0,1},{1,2},{2,3},{3,0},{4,5},{5,6},{6,7},{7,4},{8,9},{9,10},{10,1... | collective-permute-start | bytes 393224 | tf_op jit(solution)/shard_map/ppermute | solution.py:203
  91.3 10.0 %collective-permute-start.29 = (bf16[2,8,32,128]{3,2,1,0:T(8,128)(2,1)S(1)}, bf16[2,8,32,128]{3,2,1,0:T(8,128)(2,1)S(1)}, u32[]{:S(2)}, u32[]{:S(2)}) collective-permute-start(bf16[2,8,32,128]{3,2,1,0:T(8,128)(2,1)S(1)} %pad_maximum_fusion.18), channel_id=1, source_target_pairs={{1,0},{2,1},{3,2},{0,3},{5,4},{6,5},{7,6},{4,7},{9,8},{10,9},{11,1... | collective-permute-start | bytes 393224 | tf_op jit(solution)/shard_map/ppermute | solution.py:203
  95.2 8.3 %collective-permute-start.27 = (bf16[3,8,32,128]{3,2,1,0:T(8,128)(2,1)S(1)}, bf16[3,8,32,128]{3,2,1,0:T(8,128)(2,1)S(1)}, u32[]{:S(2)}, u32[]{:S(2)}) collective-permute-start(bf16[3,8,32,128]{3,2,1,0:T(8,128)(2,1)S(1)} %pad_maximum_fusion.15.refs_5_), channel_id=1, source_target_pairs={{4,0},{8,4},{12,8},{16,12},{20,16},{24,20},{28,24},{0,28},{5,1},{9... | collective-permute-start | bytes 589832 | tf_op jit(solution)/shard_map/ppermute | solution.py:203
  95.9 7.7 %collective-permute-start.26 = (bf16[3,8,32,128]{3,2,1,0:T(8,128)(2,1)S(1)}, bf16[3,8,32,128]{3,2,1,0:T(8,128)(2,1)S(1)}, u32[]{:S(2)}, u32[]{:S(2)}) collective-permute-start(bf16[3,8,32,128]{3,2,1,0:T(8,128)(2,1)S(1)} %pad_maximum_fusion.14.refs_6_), channel_id=1, source_target_pairs={{0,4},{4,8},{8,12},{12,16},{16,20},{20,24},{24,28},{28,0},{1,5},{5... | collective-permute-start | bytes 589832 | tf_op jit(solution)/shard_map/ppermute | solution.py:203
  97.5 8.2 %collective-permute-start.30 = (bf16[2,8,32,128]{3,2,1,0:T(8,128)(2,1)S(1)}, bf16[2,8,32,128]{3,2,1,0:T(8,128)(2,1)S(1)}, u32[]{:S(2)}, u32[]{:S(2)}) collective-permute-start(bf16[2,8,32,128]{3,2,1,0:T(8,128)(2,1)S(1)} %slice.222), channel_id=1, source_target_pairs={{0,1},{1,2},{2,3},{3,0},{4,5},{5,6},{6,7},{7,4},{8,9},{9,10},{10,1... | collective-permute-start | bytes 393224 | tf_op jit(solution)/shard_map/ppermute | solution.py:203
  98.2 7.8 %collective-permute-start.31 = (bf16[2,8,32,128]{3,2,1,0:T(8,128)(2,1)S(1)}, bf16[2,8,32,128]{3,2,1,0:T(8,128)(2,1)S(1)}, u32[]{:S(2)}, u32[]{:S(2)}) collective-permute-start(bf16[2,8,32,128]{3,2,1,0:T(8,128)(2,1)S(1)} %slice.222), channel_id=1, source_target_pairs={{1,0},{2,1},{3,2},{0,3},{5,4},{6,5},{7,6},{4,7},{9,8},{10,9},{11,1... | collective-permute-start | bytes 393224 | tf_op jit(solution)/shard_map/ppermute | solution.py:203
  101.4 7.0 %collective-permute-start.33 = (bf16[3,8,32,128]{3,2,1,0:T(8,128)(2,1)S(1)}, bf16[3,8,32,128]{3,2,1,0:T(8,128)(2,1)S(1)}, u32[]{:S(2)}, u32[]{:S(2)}) collective-permute-start(bf16[3,8,32,128]{3,2,1,0:T(8,128)(2,1)S(1)} %pad_maximum_fusion.17.refs_5_), channel_id=1, source_target_pairs={{4,0},{8,4},{12,8},{16,12},{20,16},{24,20},{28,24},{0,28},{5,1},{9... | collective-permute-start | bytes 589832 | tf_op jit(solution)/shard_map/ppermute | solution.py:203
  103.6 6.0 %collective-permute-start.32 = (bf16[3,8,32,128]{3,2,1,0:T(8,128)(2,1)S(1)}, bf16[3,8,32,128]{3,2,1,0:T(8,128)(2,1)S(1)}, u32[]{:S(2)}, u32[]{:S(2)}) collective-permute-start(bf16[3,8,32,128]{3,2,1,0:T(8,128)(2,1)S(1)} %pad_maximum_fusion.16.refs_6_), channel_id=1, source_target_pairs={{0,4},{4,8},{8,12},{12,16},{16,20},{20,24},{24,28},{28,0},{1,5},{5... | collective-permute-start | bytes 589832 | tf_op jit(solution)/shard_map/ppermute | solution.py:203

commit v17 on v13

--- a/solution.py
+++ b/solution.py
@@ -98,7 +98,7 @@
 
 
 def from_neighbours(value, half):
-    return value, *(shift(value, "azim", up) for up in (half == 0, half > 0))
+    return value, *(shift(value, "azim", up) for up in (half > 0, half == 0))
 
 
 def joined(value, outer, inner, after):
@@ -129,7 +129,7 @@
 
     lax.fori_loop(0, columns, enter, 0)
     if edge:
-        high_st, low_st, before = refs[5:8]
+        low_st, high_st, before = refs[5:8]
 
         def enter_stream(face, carry):
             for azim in range(3):
@@ -249,7 +249,7 @@
     around_shift = (codes // faces) % 3
     tables = [
         (place * (columns + 2) + codes // (3 * faces)) * faces + codes % faces
-        for place in (around_shift, 2 - around_shift)
+        for place in (2 - around_shift, around_shift)
     ]
     every = tuple(range(columns))
     current = list(pack(start))
@@ -267,11 +267,11 @@
                 inner = from_neighbours(own_inner, h)
                 to_low, to_high = edges(*outer, middle)
                 pieces[h] = joined(current[h], outer, inner, latest)
-            stream = (shift(to_low, "stream", False), shift(to_high, "stream", True))
-            middle = part(h, tables[h], blocks, pieces[h], (to_high, to_low))
+            stream = (shift(to_high, "stream", True), shift(to_low, "stream", False))
+            middle = part(h, tables[h], blocks, pieces[h], (to_low, to_high))
             after = middle
-            if h == 0 and index > 0:
-                basis, after = unpack(index - 1, every, *previous, basis, middle)
+            if index > 0 and h == (index == STEPS - 1):
+                basis, after = unpack(index - 1, every, *previous, basis, latest if h else middle)
             current[h] = latest = part(h, tables[h], blocks, pieces[h], (*stream, middle, after))
             if index == STEPS - 2 and h == HALVES - 1:
                 outer = from_neighbours(jnp.stack([current[h][0], current[h][-1]]), h)

time: 117 us -> 116 us (level)
  starting transfers between devices: 41.5 us -> 39.4 us
    ppermute x34, starting transfers between devices: 41.5 us -> 39.4 us  [shift(): return lax.ppermute(value, axis, pairs)]
  transfers between devices with their start and end apart: 34 -> 34, of which waited for: 16 -> 17; matrix products, arithmetic and copies ran while one was open for 1% -> 1% of each run, Pallas kernels for 24% -> 24%
where the time goes in v17:
time: 116 us
  waiting for transfers between devices  41.4 us (36%)
  starting transfers between devices  39.4 us (34%)
  Pallas kernels  30.7 us (26%)
  local copies, waits for them, and re-layouts  3.23 us (3%)
    ppermute x34, waiting for transfers between devices, shift(): return lax.ppermute(value, axis, pairs)  41.4 us
    ppermute x34, starting transfers between devices, shift(): return lax.ppermute(value, axis, pairs)  39.4 us
    pallas_call x16, Pallas kernels, part(): pl.pallas_call(functools.partial(part_kernel, half), in_specs=in_specs, o...  23.6 us
    pallas_call x4, Pallas kernels, unpack(): pl.pallas_call(functools.partial(unpack_kernel, index, chosen, skipped),...  4.26 us
    unnamed x6, local copies, waits for them, and re-layouts  2.93 us
    pallas_call x1, Pallas kernels, halves_of_rows(): pl.pallas_call(halves_kernel, in_specs=[VMEM], out_specs=VMEM, out_shape=...  2.72 us
  transfers between devices with their start and end apart: 34, of which 17 were waited for; matrix products, arithmetic and copies ran while one was open for 1% of the time, Pallas kernels for 24%

profile of v17, /device:TPU:0, one launch (start us, length us, event | category | flops | bytes accessed | tf_op | source)
XLA Modules:
  0.0 115.9 jit_solution(14120319418159549696)
XLA Ops:
  0.0 1.0 copy-done.1
  1.0 0.2 pack.1
  1.2 5.1 %collective-permute-start = (bf16[4,8,32,128]{3,2,1,0:T(8,128)(2,1)S(1)}, bf16[4,8,32,128]{3,2,1,0:T(8,128)(2,1)S(1)}, u32[]{:S(2)}, u32[]{:S(2)}) collective-permute-start(bf16[4,8,32,128]{3,2,1,0:T(8,128)(2,1)S(1)} %get-tuple-element.45.refs_2_), channel_id=1, source_target_pairs={{1,0},{2,1},{3,2},{0,3},{5,4},{6,5},{7,6},{4,7},{9,8},{10,9},{11,1... | collective-permute-start | bytes 786440 | tf_op jit(solution)/shard_map/ppermute | solution.py:203
  6.3 3.9 %collective-permute-start.7 = (bf16[4,8,32,128]{3,2,1,0:T(8,128)(2,1)S(1)}, bf16[4,8,32,128]{3,2,1,0:T(8,128)(2,1)S(1)}, u32[]{:S(2)}, u32[]{:S(2)}) collective-permute-start(bf16[4,8,32,128]{3,2,1,0:T(8,128)(2,1)S(1)} %get-tuple-element.49.refs_2_), channel_id=1, source_target_pairs={{1,0},{2,1},{3,2},{0,3},{5,4},{6,5},{7,6},{4,7},{9,8},{10,9},{11,1... | collective-permute-start | bytes 786440 | tf_op jit(solution)/shard_map/ppermute | solution.py:203
  10.2 1.9 %copy-done = bf16[4,1,8,64,768]{4,3,2,1,0:T(8,128)(2,1)S(1)} copy-done((bf16[4,1,8,64,768]{4,3,2,1,0:T(8,128)(2,1)S(1)}, bf16[4,1,8,64,768]{4,3,2,1,0:T(8,128)(2,1)}, u32[]{:S(2)}) %copy-start) | copy-done | bytes 3145752
  12.1 2.7 %halves_of_rows.1.refs_1_ = bf16[4,8,64,768]{3,2,1,0:T(8,128)(2,1)S(1)} custom-call(bf16[4,8,64,768]{3,2,1,0:T(8,128)(2,1)S(1)} %bitcast.53), custom_call_target="tpu_custom_call" | custom-call | tf_op jit(solution)/shard_map/halves_of_rows/pallas_call | solution.py:234
  14.8 4.9 %collective-permute-done.1.refs_4_ = bf16[4,8,32,128]{3,2,1,0:T(8,128)(2,1)S(1)} collective-permute-done((bf16[4,8,32,128]{3,2,1,0:T(8,128)(2,1)S(1)}, bf16[4,8,32,128]{3,2,1,0:T(8,128)(2,1)S(1)}, u32[]{:S(2)}, u32[]{:S(2)}) %collective-permute-start.1) | collective-permute-done | bytes 262176 | tf_op jit(solution)/shard_map/ppermute | solution.py:203
  19.9 0.5 collective-permute-start.2
  20.4 1.5 %inner_half0.4.refs_7_.refs_8_ = bf16[2,8,32,128]{3,2,1,0:T(8,128)(2,1)S(1)} custom-call(s32[8,12]{1,0:T(8,128)S(1)} %get-tuple-element.136.refs_0_, bf16[4,8,64,768]{3,2,1,0:T(8,128)(2,1)S(1)} %halves_of_rows.1.refs_1_, bf16[4,8,32,128]{3,2,1,0:T(8,128)(2,1)S(1)} %get-tuple-element.45.refs_2_, bf16[4,8,32,128]{3,2,1,0:T(8,128)(2,1)S(1)} %collective-permute-done.refs_3_, ...), custom_call_target="tpu_custom_call" | custom-call | flops 20132659200 | bytes 157286400 | tf_op jit(solution)/shard_map/inner_half0/pallas_call | solution.py:178
  21.9 2.2 %collective-permute-done.3.refs_6_ = bf16[3,8,32,128]{3,2,1,0:T(8,128)(2,1)S(1)} collective-permute-done((bf16[3,8,32,128]{3,2,1,0:T(8,128)(2,1)S(1)}, bf16[3,8,32,128]{3,2,1,0:T(8,128)(2,1)S(1)}, u32[]{:S(2)}, u32[]{:S(2)}) %collective-permute-start.3) | collective-permute-done | bytes 196640 | tf_op jit(solution)/shard_map/ppermute | solution.py:203
  24.1 3.9 %collective-permute-done.2.refs_5_ = bf16[3,8,32,128]{3,2,1,0:T(8,128)(2,1)S(1)} collective-permute-done((bf16[3,8,32,128]{3,2,1,0:T(8,128)(2,1)S(1)}, bf16[3,8,32,128]{3,2,1,0:T(8,128)(2,1)S(1)}, u32[]{:S(2)}, u32[]{:S(2)}) %collective-permute-start.2) | collective-permute-done | bytes 196640 | tf_op jit(solution)/shard_map/ppermute | solution.py:203
  28.0 1.5 %edge_half0.4.refs_2_.first_ref = bf16[4,8,32,128]{3,2,1,0:T(8,128)(2,1)S(1)} custom-call(s32[8,12]{1,0:T(8,128)S(1)} %get-tuple-element.136.refs_0_, bf16[4,8,64,768]{3,2,1,0:T(8,128)(2,1)S(1)} %halves_of_rows.1.refs_1_, bf16[4,8,32,128]{3,2,1,0:T(8,128)(2,1)S(1)} %get-tuple-element.45.refs_2_, bf16[4,8,32,128]{3,2,1,0:T(8,128)(2,1)S(1)} %collective-permute-done.refs_3_, ...), custom_call_target="tpu_custom_call" | custom-call | flops 20132659200 | bytes 157286400 | tf_op jit(solution)/shard_map/edge_half0/pallas_call | solution.py:178
  29.5 2.0 %collective-permute-start.4 = (bf16[4,8,32,128]{3,2,1,0:T(8,128)(2,1)S(1)}, bf16[4,8,32,128]{3,2,1,0:T(8,128)(2,1)S(1)}, u32[]{:S(2)}, u32[]{:S(2)}) collective-permute-start(bf16[4,8,32,128]{3,2,1,0:T(8,128)(2,1)S(1)} %edge_half0.4.refs_2_.first_ref), channel_id=1, source_target_pairs={{1,0},{2,1},{3,2},{0,3},{5,4},{6,5},{7,6},{4,7},{9,8},{10,9},{11,1... | collective-permute-start | bytes 786440 | tf_op jit(solution)/shard_map/ppermute | solution.py:203
  31.5 2.1 %collective-permute-start.5 = (bf16[4,8,32,128]{3,2,1,0:T(8,128)(2,1)S(1)}, bf16[4,8,32,128]{3,2,1,0:T(8,128)(2,1)S(1)}, u32[]{:S(2)}, u32[]{:S(2)}) collective-permute-start(bf16[4,8,32,128]{3,2,1,0:T(8,128)(2,1)S(1)} %edge_half0.4.refs_2_.first_ref), channel_id=1, source_target_pairs={{0,1},{1,2},{2,3},{3,0},{4,5},{5,6},{6,7},{7,4},{8,9},{9,10},{10,1... | collective-permute-start | bytes 786440 | tf_op jit(solution)/shard_map/ppermute | solution.py:203
  33.8 0.5 collective-permute-start.8
  34.3 1.5 %inner_half1.4.refs_7_.refs_8_ = bf16[2,8,32,128]{3,2,1,0:T(8,128)(2,1)S(1)} custom-call(s32[8,12]{1,0:T(8,128)S(1)} %get-tuple-element.135.refs_0_, bf16[4,8,64,768]{3,2,1,0:T(8,128)(2,1)S(1)} %halves_of_rows.1.refs_1_, bf16[4,8,32,128]{3,2,1,0:T(8,128)(2,1)S(1)} %get-tuple-element.49.refs_2_, bf16[4,8,32,128]{3,2,1,0:T(8,128)(2,1)S(1)} %collective-permute-done.6.refs_3_, ...), custom_call_target="tpu_custom_call" | custom-call | flops 20132659200 | bytes 157286400 | tf_op jit(solution)/shard_map/inner_half1/pallas_call | solution.py:178
  35.8 3.1 %collective-permute-done.9.refs_6_ = bf16[3,8,32,128]{3,2,1,0:T(8,128)(2,1)S(1)} collective-permute-done((bf16[3,8,32,128]{3,2,1,0:T(8,128)(2,1)S(1)}, bf16[3,8,32,128]{3,2,1,0:T(8,128)(2,1)S(1)}, u32[]{:S(2)}, u32[]{:S(2)}) %collective-permute-start.9) | collective-permute-done | bytes 196640 | tf_op jit(solution)/shard_map/ppermute | solution.py:203
  38.9 2.0 %collective-permute-done.8.refs_5_ = bf16[3,8,32,128]{3,2,1,0:T(8,128)(2,1)S(1)} collective-permute-done((bf16[3,8,32,128]{3,2,1,0:T(8,128)(2,1)S(1)}, bf16[3,8,32,128]{3,2,1,0:T(8,128)(2,1)S(1)}, u32[]{:S(2)}, u32[]{:S(2)}) %collective-permute-start.8) | collective-permute-done | bytes 196640 | tf_op jit(solution)/shard_map/ppermute | solution.py:203
  40.9 1.5 %edge_half1.4.second_ref.refs_2_ = bf16[4,8,32,128]{3,2,1,0:T(8,128)(2,1)S(1)} custom-call(s32[8,12]{1,0:T(8,128)S(1)} %get-tuple-element.135.refs_0_, bf16[4,8,64,768]{3,2,1,0:T(8,128)(2,1)S(1)} %halves_of_rows.1.refs_1_, bf16[4,8,32,128]{3,2,1,0:T(8,128)(2,1)S(1)} %get-tuple-element.49.refs_2_, bf16[4,8,32,128]{3,2,1,0:T(8,128)(2,1)S(1)} %collective-permute-done.6.refs_3_, ...), custom_call_target="tpu_custom_call" | custom-call | flops 20132659200 | bytes 157286400 | tf_op jit(solution)/shard_map/edge_half1/pallas_call | solution.py:178
  42.4 1.7 %collective-permute-start.14 = (bf16[4,8,32,128]{3,2,1,0:T(8,128)(2,1)S(1)}, bf16[4,8,32,128]{3,2,1,0:T(8,128)(2,1)S(1)}, u32[]{:S(2)}, u32[]{:S(2)}) collective-permute-start(bf16[4,8,32,128]{3,2,1,0:T(8,128)(2,1)S(1)} %edge_half1.4.second_ref.refs_2_), channel_id=1, source_target_pairs={{0,1},{1,2},{2,3},{3,0},{4,5},{5,6},{6,7},{7,4},{8,9},{9,10},{10,1... | collective-permute-start | bytes 786440 | tf_op jit(solution)/shard_map/ppermute | solution.py:203
  44.1 2.1 %collective-permute-start.15 = (bf16[4,8,32,128]{3,2,1,0:T(8,128)(2,1)S(1)}, bf16[4,8,32,128]{3,2,1,0:T(8,128)(2,1)S(1)}, u32[]{:S(2)}, u32[]{:S(2)}) collective-permute-start(bf16[4,8,32,128]{3,2,1,0:T(8,128)(2,1)S(1)} %edge_half1.4.second_ref.refs_2_), channel_id=1, source_target_pairs={{1,0},{2,1},{3,2},{0,3},{5,4},{6,5},{7,6},{4,7},{9,8},{10,9},{11,1... | collective-permute-start | bytes 786440 | tf_op jit(solution)/shard_map/ppermute | solution.py:203
  46.4 0.6 collective-permute-start.11
  47.1 1.5 %inner_half0.5.refs_0_.refs_7_ = bf16[2,8,32,128]{3,2,1,0:T(8,128)(2,1)S(1)} custom-call(s32[8,12]{1,0:T(8,128)S(1)} %get-tuple-element.136.refs_0_, bf16[4,8,64,768]{3,2,1,0:T(8,128)(2,1)S(1)} %halves_of_rows.1.refs_1_, bf16[4,8,32,128]{3,2,1,0:T(8,128)(2,1)S(1)} %edge_half0.4.refs_2_.first_ref, bf16[4,8,32,128]{3,2,1,0:T(8,128)(2,1)S(1)} %collective-permute-done.4.refs_3_, ...), custom_call_target="tpu_custom_call" | custom-call | flops 20132659200 | bytes 157286400 | tf_op jit(solution)/shard_map/inner_half0/pallas_call | solution.py:178
  48.6 0.9 unpack.4
  49.5 2.2 %collective-permute-done.11.refs_6_ = bf16[3,8,32,128]{3,2,1,0:T(8,128)(2,1)S(1)} collective-permute-done((bf16[3,8,32,128]{3,2,1,0:T(8,128)(2,1)S(1)}, bf16[3,8,32,128]{3,2,1,0:T(8,128)(2,1)S(1)}, u32[]{:S(2)}, u32[]{:S(2)}) %collective-permute-start.11) | collective-permute-done | bytes 196640 | tf_op jit(solution)/shard_map/ppermute | solution.py:203
  51.7 1.4 %collective-permute-done.10.refs_5_ = bf16[3,8,32,128]{3,2,1,0:T(8,128)(2,1)S(1)} collective-permute-done((bf16[3,8,32,128]{3,2,1,0:T(8,128)(2,1)S(1)}, bf16[3,8,32,128]{3,2,1,0:T(8,128)(2,1)S(1)}, u32[]{:S(2)}, u32[]{:S(2)}) %collective-permute-start.10) | collective-permute-done | bytes 196640 | tf_op jit(solution)/shard_map/ppermute | solution.py:203
  53.1 1.5 %edge_half0.5.refs_2_.first_ref = bf16[4,8,32,128]{3,2,1,0:T(8,128)(2,1)S(1)} custom-call(s32[8,12]{1,0:T(8,128)S(1)} %get-tuple-element.136.refs_0_, bf16[4,8,64,768]{3,2,1,0:T(8,128)(2,1)S(1)} %halves_of_rows.1.refs_1_, bf16[4,8,32,128]{3,2,1,0:T(8,128)(2,1)S(1)} %edge_half0.4.refs_2_.first_ref, ...), custom_call_target="tpu_custom_call" | custom-call | flops 20132659200 | bytes 157286400 | tf_op jit(solution)/shard_map/edge_half0/pallas_call | solution.py:178
  54.6 1.8 %collective-permute-start.12 = (bf16[4,8,32,128]{3,2,1,0:T(8,128)(2,1)S(1)}, bf16[4,8,32,128]{3,2,1,0:T(8,128)(2,1)S(1)}, u32[]{:S(2)}, u32[]{:S(2)}) collective-permute-start(bf16[4,8,32,128]{3,2,1,0:T(8,128)(2,1)S(1)} %edge_half0.5.refs_2_.first_ref), channel_id=1, source_target_pairs={{1,0},{2,1},{3,2},{0,3},{5,4},{6,5},{7,6},{4,7},{9,8},{10,9},{11,1... | collective-permute-start | bytes 786440 | tf_op jit(solution)/shard_map/ppermute | solution.py:203
  56.3 0.4 collective-permute-start.13
  56.8 1.8 %collective-permute-start.17 = (bf16[3,8,32,128]{3,2,1,0:T(8,128)(2,1)S(1)}, bf16[3,8,32,128]{3,2,1,0:T(8,128)(2,1)S(1)}, u32[]{:S(2)}, u32[]{:S(2)}) collective-permute-start(bf16[3,8,32,128]{3,2,1,0:T(8,128)(2,1)S(1)} %pad_maximum_fusion.9.refs_5_), channel_id=1, source_target_pairs={{4,0},{8,4},{12,8},{16,12},{20,16},{24,20},{28,24},{0,28},{5,1},{9... | collective-permute-start | bytes 589832 | tf_op jit(solution)/shard_map/ppermute | solution.py:203
  58.7 1.5 %inner_half1.5.refs_7_.refs_8_ = bf16[2,8,32,128]{3,2,1,0:T(8,128)(2,1)S(1)} custom-call(s32[8,12]{1,0:T(8,128)S(1)} %get-tuple-element.135.refs_0_, bf16[4,8,64,768]{3,2,1,0:T(8,128)(2,1)S(1)} %halves_of_rows.1.refs_1_, bf16[4,8,32,128]{3,2,1,0:T(8,128)(2,1)S(1)} %edge_half1.4.second_ref.refs_2_, ...), custom_call_target="tpu_custom_call" | custom-call | flops 20132659200 | bytes 157286400 | tf_op jit(solution)/shard_map/inner_half1/pallas_call | solution.py:178
  60.2 3.0 %collective-permute-done.17.refs_6_ = bf16[3,8,32,128]{3,2,1,0:T(8,128)(2,1)S(1)} collective-permute-done((bf16[3,8,32,128]{3,2,1,0:T(8,128)(2,1)S(1)}, bf16[3,8,32,128]{3,2,1,0:T(8,128)(2,1)S(1)}, u32[]{:S(2)}, u32[]{:S(2)}) %collective-permute-start.17) | collective-permute-done | bytes 196640 | tf_op jit(solution)/shard_map/ppermute | solution.py:203
  63.2 5.7 %collective-permute-done.16.refs_5_ = bf16[3,8,32,128]{3,2,1,0:T(8,128)(2,1)S(1)} collective-permute-done((bf16[3,8,32,128]{3,2,1,0:T(8,128)(2,1)S(1)}, bf16[3,8,32,128]{3,2,1,0:T(8,128)(2,1)S(1)}, u32[]{:S(2)}, u32[]{:S(2)}) %collective-permute-start.16) | collective-permute-done | bytes 196640 | tf_op jit(solution)/shard_map/ppermute | solution.py:203
  68.9 1.5 %edge_half1.5.second_ref.refs_2_ = bf16[4,8,32,128]{3,2,1,0:T(8,128)(2,1)S(1)} custom-call(s32[8,12]{1,0:T(8,128)S(1)} %get-tuple-element.135.refs_0_, bf16[4,8,64,768]{3,2,1,0:T(8,128)(2,1)S(1)} %halves_of_rows.1.refs_1_, bf16[4,8,32,128]{3,2,1,0:T(8,128)(2,1)S(1)} %edge_half1.4.second_ref.refs_2_, ...), custom_call_target="tpu_custom_call" | custom-call | flops 20132659200 | bytes 157286400 | tf_op jit(solution)/shard_map/edge_half1/pallas_call | solution.py:178
  70.4 2.0 %collective-permute-start.22 = (bf16[4,8,32,128]{3,2,1,0:T(8,128)(2,1)S(1)}, bf16[4,8,32,128]{3,2,1,0:T(8,128)(2,1)S(1)}, u32[]{:S(2)}, u32[]{:S(2)}) collective-permute-start(bf16[4,8,32,128]{3,2,1,0:T(8,128)(2,1)S(1)} %edge_half1.5.second_ref.refs_2_), channel_id=1, source_target_pairs={{0,1},{1,2},{2,3},{3,0},{4,5},{5,6},{6,7},{7,4},{8,9},{9,10},{10,1... | collective-permute-start | bytes 786440 | tf_op jit(solution)/shard_map/ppermute | solution.py:203
  72.4 1.9 %collective-permute-start.23 = (bf16[4,8,32,128]{3,2,1,0:T(8,128)(2,1)S(1)}, bf16[4,8,32,128]{3,2,1,0:T(8,128)(2,1)S(1)}, u32[]{:S(2)}, u32[]{:S(2)}) collective-permute-start(bf16[4,8,32,128]{3,2,1,0:T(8,128)(2,1)S(1)} %edge_half1.5.second_ref.refs_2_), channel_id=1, source_target_pairs={{1,0},{2,1},{3,2},{0,3},{5,4},{6,5},{7,6},{4,7},{9,8},{10,9},{11,1... | collective-permute-start | bytes 786440 | tf_op jit(solution)/shard_map/ppermute | solution.py:203
  74.5 0.5 collective-permute-start.18
  75.0 1.5 %inner_half0.6.refs_1_.refs_7_ = bf16[2,8,32,128]{3,2,1,0:T(8,128)(2,1)S(1)} custom-call(s32[8,12]{1,0:T(8,128)S(1)} %get-tuple-element.136.refs_0_, bf16[4,8,64,768]{3,2,1,0:T(8,128)(2,1)S(1)} %halves_of_rows.1.refs_1_, bf16[4,8,32,128]{3,2,1,0:T(8,128)(2,1)S(1)} %edge_half0.5.refs_2_.first_ref, ...), custom_call_target="tpu_custom_call" | custom-call | flops 20132659200 | bytes 157286400 | tf_op jit(solution)/shard_map/inner_half0/pallas_call | solution.py:178
  76.5 0.9 unpack.5
  77.4 2.2 %collective-permute-done.19.refs_6_ = bf16[3,8,32,128]{3,2,1,0:T(8,128)(2,1)S(1)} collective-permute-done((bf16[3,8,32,128]{3,2,1,0:T(8,128)(2,1)S(1)}, bf16[3,8,32,128]{3,2,1,0:T(8,128)(2,1)S(1)}, u32[]{:S(2)}, u32[]{:S(2)}) %collective-permute-start.19) | collective-permute-done | bytes 196640 | tf_op jit(solution)/shard_map/ppermute | solution.py:203
  79.6 1.8 %collective-permute-done.18.refs_5_ = bf16[3,8,32,128]{3,2,1,0:T(8,128)(2,1)S(1)} collective-permute-done((bf16[3,8,32,128]{3,2,1,0:T(8,128)(2,1)S(1)}, bf16[3,8,32,128]{3,2,1,0:T(8,128)(2,1)S(1)}, u32[]{:S(2)}, u32[]{:S(2)}) %collective-permute-start.18) | collective-permute-done | bytes 196640 | tf_op jit(solution)/shard_map/ppermute | solution.py:203
  81.5 1.5 %edge_half0.6.refs_2_.first_ref = bf16[4,8,32,128]{3,2,1,0:T(8,128)(2,1)S(1)} custom-call(s32[8,12]{1,0:T(8,128)S(1)} %get-tuple-element.136.refs_0_, bf16[4,8,64,768]{3,2,1,0:T(8,128)(2,1)S(1)} %halves_of_rows.1.refs_1_, bf16[4,8,32,128]{3,2,1,0:T(8,128)(2,1)S(1)} %edge_half0.5.refs_2_.first_ref, ...), custom_call_target="tpu_custom_call" | custom-call | flops 20132659200 | bytes 157286400 | tf_op jit(solution)/shard_map/edge_half0/pallas_call | solution.py:178
  82.9 0.3 collective-permute-start.20
  83.3 1.7 %collective-permute-start.21 = (bf16[4,8,32,128]{3,2,1,0:T(8,128)(2,1)S(1)}, bf16[4,8,32,128]{3,2,1,0:T(8,128)(2,1)S(1)}, u32[]{:S(2)}, u32[]{:S(2)}) collective-permute-start(bf16[4,8,32,128]{3,2,1,0:T(8,128)(2,1)S(1)} %edge_half0.6.refs_2_.first_ref), channel_id=1, source_target_pairs={{0,1},{1,2},{2,3},{3,0},{4,5},{5,6},{6,7},{7,4},{8,9},{9,10},{10,1... | collective-permute-start | bytes 786440 | tf_op jit(solution)/shard_map/ppermute | solution.py:203
  85.1 0.5 collective-permute-start.25
  85.8 1.5 %inner_half1.6.refs_7_.refs_8_ = bf16[2,8,32,128]{3,2,1,0:T(8,128)(2,1)S(1)} custom-call(s32[8,12]{1,0:T(8,128)S(1)} %get-tuple-element.135.refs_0_, bf16[4,8,64,768]{3,2,1,0:T(8,128)(2,1)S(1)} %halves_of_rows.1.refs_1_, bf16[4,8,32,128]{3,2,1,0:T(8,128)(2,1)S(1)} %edge_half1.5.second_ref.refs_2_, ...), custom_call_target="tpu_custom_call" | custom-call | flops 20132659200 | bytes 157286400 | tf_op jit(solution)/shard_map/inner_half1/pallas_call | solution.py:178
  87.2 3.3 %collective-permute-done.25.refs_6_ = bf16[3,8,32,128]{3,2,1,0:T(8,128)(2,1)S(1)} collective-permute-done((bf16[3,8,32,128]{3,2,1,0:T(8,128)(2,1)S(1)}, bf16[3,8,32,128]{3,2,1,0:T(8,128)(2,1)S(1)}, u32[]{:S(2)}, u32[]{:S(2)}) %collective-permute-start.25) | collective-permute-done | bytes 196640 | tf_op jit(solution)/shard_map/ppermute | solution.py:203
  90.5 3.0 %collective-permute-done.24.refs_5_ = bf16[3,8,32,128]{3,2,1,0:T(8,128)(2,1)S(1)} collective-permute-done((bf16[3,8,32,128]{3,2,1,0:T(8,128)(2,1)S(1)}, bf16[3,8,32,128]{3,2,1,0:T(8,128)(2,1)S(1)}, u32[]{:S(2)}, u32[]{:S(2)}) %collective-permute-start.24) | collective-permute-done | bytes 196640 | tf_op jit(solution)/shard_map/ppermute | solution.py:203
  93.5 1.5 %edge_half1.6.refs_2_.second_ref = bf16[4,8,32,128]{3,2,1,0:T(8,128)(2,1)S(1)} custom-call(s32[8,12]{1,0:T(8,128)S(1)} %get-tuple-element.135.refs_0_, bf16[4,8,64,768]{3,2,1,0:T(8,128)(2,1)S(1)} %halves_of_rows.1.refs_1_, bf16[4,8,32,128]{3,2,1,0:T(8,128)(2,1)S(1)} %edge_half1.5.second_ref.refs_2_, ...), custom_call_target="tpu_custom_call" | custom-call | flops 20132659200 | bytes 157286400 | tf_op jit(solution)/shard_map/edge_half1/pallas_call | solution.py:178
  95.1 0.2 collective-permute-start.28
  95.3 3.7 %collective-permute-start.29 = (bf16[2,8,32,128]{3,2,1,0:T(8,128)(2,1)S(1)}, bf16[2,8,32,128]{3,2,1,0:T(8,128)(2,1)S(1)}, u32[]{:S(2)}, u32[]{:S(2)}) collective-permute-start(bf16[2,8,32,128]{3,2,1,0:T(8,128)(2,1)S(1)} %pad_maximum_fusion.18), channel_id=1, source_target_pairs={{1,0},{2,1},{3,2},{0,3},{5,4},{6,5},{7,6},{4,7},{9,8},{10,9},{11,1... | collective-permute-start | bytes 393224 | tf_op jit(solution)/shard_map/ppermute | solution.py:203
  99.2 0.5 collective-permute-start.26
  99.7 1.5 %inner_half0.7.refs_7_.refs_8_ = bf16[2,8,32,128]{3,2,1,0:T(8,128)(2,1)S(1)} custom-call(s32[8,12]{1,0:T(8,128)S(1)} %get-tuple-element.136.refs_0_, bf16[4,8,64,768]{3,2,1,0:T(8,128)(2,1)S(1)} %halves_of_rows.1.refs_1_, bf16[4,8,32,128]{3,2,1,0:T(8,128)(2,1)S(1)} %edge_half0.6.refs_2_.first_ref, ...), custom_call_target="tpu_custom_call" | custom-call | flops 20132659200 | bytes 157286400 | tf_op jit(solution)/shard_map/inner_half0/pallas_call | solution.py:178
  101.3 0.6 collective-permute-done.28
  101.9 3.2 %collective-permute-start.31 = (bf16[2,8,32,128]{3,2,1,0:T(8,128)(2,1)S(1)}, bf16[2,8,32,128]{3,2,1,0:T(8,128)(2,1)S(1)}, u32[]{:S(2)}, u32[]{:S(2)}) collective-permute-start(bf16[2,8,32,128]{3,2,1,0:T(8,128)(2,1)S(1)} %slice.222), channel_id=1, source_target_pairs={{1,0},{2,1},{3,2},{0,3},{5,4},{6,5},{7,6},{4,7},{9,8},{10,9},{11,1... | collective-permute-start | bytes 393224 | tf_op jit(solution)/shard_map/ppermute | solution.py:203
  105.2 1.6 %collective-permute-start.33 = (bf16[3,8,32,128]{3,2,1,0:T(8,128)(2,1)S(1)}, bf16[3,8,32,128]{3,2,1,0:T(8,128)(2,1)S(1)}, u32[]{:S(2)}, u32[]{:S(2)}) collective-permute-start(bf16[3,8,32,128]{3,2,1,0:T(8,128)(2,1)S(1)} %pad_maximum_fusion.17.refs_5_), channel_id=1, source_target_pairs={{4,0},{8,4},{12,8},{16,12},{20,16},{24,20},{28,24},{0,28},{5,1},{9... | collective-permute-start | bytes 589832 | tf_op jit(solution)/shard_map/ppermute | solution.py:203
  106.9 1.5 %edge_half0.7.refs_1_.first_ref = bf16[4,8,32,128]{3,2,1,0:T(8,128)(2,1)S(1)} custom-call(s32[8,12]{1,0:T(8,128)S(1)} %get-tuple-element.136.refs_0_, bf16[4,8,64,768]{3,2,1,0:T(8,128)(2,1)S(1)} %halves_of_rows.1.refs_1_, bf16[4,8,32,128]{3,2,1,0:T(8,128)(2,1)S(1)} %edge_half0.6.refs_2_.first_ref, ...), custom_call_target="tpu_custom_call" | custom-call | flops 20132659200 | bytes 157286400 | tf_op jit(solution)/shard_map/edge_half0/pallas_call | solution.py:178
  108.4 1.0 collective-permute-done.30
  109.4 0.2 collective-permute-done.31
  109.8 1.5 %inner_half1.7.refs_7_ = bf16[2,8,32,128]{3,2,1,0:T(8,128)(2,1)S(1)} custom-call(s32[8,12]{1,0:T(8,128)S(1)} %get-tuple-element.135.refs_0_, bf16[4,8,64,768]{3,2,1,0:T(8,128)(2,1)S(1)} %halves_of_rows.1.refs_1_, bf16[4,8,32,128]{3,2,1,0:T(8,128)(2,1)S(1)} %edge_half1.6.refs_2_.second_ref, bf16[4,8,32,128]{3,2,1,0:T(8,128)(2,1)S(1)} %pad_maximum_fusion.refs_3_, ...), custom_call_target="tpu_custom_call" | custom-call | flops 20132659200 | bytes 157286400 | tf_op jit(solution)/shard_map/inner_half1/pallas_call | solution.py:178
  111.3 0.9 unpack.6
  112.2 0.7 collective-permute-done.32.refs_5_
  112.9 1.5 %edge_half1.7.second_ref = bf16[4,8,32,128]{3,2,1,0:T(8,128)(2,1)S(1)} custom-call(s32[8,12]{1,0:T(8,128)S(1)} %get-tuple-element.135.refs_0_, bf16[4,8,64,768]{3,2,1,0:T(8,128)(2,1)S(1)} %halves_of_rows.1.refs_1_, bf16[4,8,32,128]{3,2,1,0:T(8,128)(2,1)S(1)} %edge_half1.6.refs_2_.second_ref, bf16[4,8,32,128]{3,2,1,0:T(8,128)(2,1)S(1)} %pad_maximum_fusion.refs_3_, ...), custom_call_target="tpu_custom_call" | custom-call | flops 20132659200 | bytes 157286400 | tf_op jit(solution)/shard_map/edge_half1/pallas_call | solution.py:178
  114.4 1.5 %unpack.7 = (bf16[4,4,8,64,128]{4,3,2,1,0:T(8,128)(2,1)}, f32[8,128]{1,0:T(8,128)}) custom-call(bf16[4,8,32,128]{3,2,1,0:T(8,128)(2,1)S(1)} %edge_half0.7.refs_1_.first_ref, bf16[4,8,32,128]{3,2,1,0:T(8,128)(2,1)S(1)} %edge_half1.7.second_ref, bf16[4,4,8,64,128]{4,3,2,1,0:T(8,128)(2,1)} %get-tuple-element.79.refs_0_), custom_call_target="tpu_custom_call", output_to_operand_aliasing={{0}: (2, {})} | custom-call | tf_op jit(solution)/shard_map/unpack/pallas_call | solution.py:77
  (79 shorter events, 1.5 us)
Async XLA Ops:
  0.0 1.0 copy-start.1
  1.2 13.6 %collective-permute-start = (bf16[4,8,32,128]{3,2,1,0:T(8,128)(2,1)S(1)}, bf16[4,8,32,128]{3,2,1,0:T(8,128)(2,1)S(1)}, u32[]{:S(2)}, u32[]{:S(2)}) collective-permute-start(bf16[4,8,32,128]{3,2,1,0:T(8,128)(2,1)S(1)} %get-tuple-element.45.refs_2_), channel_id=1, source_target_pairs={{1,0},{2,1},{3,2},{0,3},{5,4},{6,5},{7,6},{4,7},{9,8},{10,9},{11,1... | collective-permute-start | bytes 786440 | tf_op jit(solution)/shard_map/ppermute | solution.py:203
  6.3 13.4 %collective-permute-start.1 = (bf16[4,8,32,128]{3,2,1,0:T(8,128)(2,1)S(1)}, bf16[4,8,32,128]{3,2,1,0:T(8,128)(2,1)S(1)}, u32[]{:S(2)}, u32[]{:S(2)}) collective-permute-start(bf16[4,8,32,128]{3,2,1,0:T(8,128)(2,1)S(1)} %get-tuple-element.45.refs_2_), channel_id=1, source_target_pairs={{0,1},{1,2},{2,3},{3,0},{4,5},{5,6},{6,7},{7,4},{8,9},{9,10},{10,1... | collective-permute-start | bytes 786440 | tf_op jit(solution)/shard_map/ppermute | solution.py:203
  6.3 27.3 %collective-permute-start.6 = (bf16[4,8,32,128]{3,2,1,0:T(8,128)(2,1)S(1)}, bf16[4,8,32,128]{3,2,1,0:T(8,128)(2,1)S(1)}, u32[]{:S(2)}, u32[]{:S(2)}) collective-permute-start(bf16[4,8,32,128]{3,2,1,0:T(8,128)(2,1)S(1)} %get-tuple-element.49.refs_2_), channel_id=1, source_target_pairs={{0,1},{1,2},{2,3},{3,0},{4,5},{5,6},{6,7},{7,4},{8,9},{9,10},{10,1... | collective-permute-start | bytes 786440 | tf_op jit(solution)/shard_map/ppermute | solution.py:203
  6.3 27.3 %collective-permute-start.7 = (bf16[4,8,32,128]{3,2,1,0:T(8,128)(2,1)S(1)}, bf16[4,8,32,128]{3,2,1,0:T(8,128)(2,1)S(1)}, u32[]{:S(2)}, u32[]{:S(2)}) collective-permute-start(bf16[4,8,32,128]{3,2,1,0:T(8,128)(2,1)S(1)} %get-tuple-element.49.refs_2_), channel_id=1, source_target_pairs={{1,0},{2,1},{3,2},{0,3},{5,4},{6,5},{7,6},{4,7},{9,8},{10,9},{11,1... | collective-permute-start | bytes 786440 | tf_op jit(solution)/shard_map/ppermute | solution.py:203
  10.2 1.9 %copy-start = (bf16[4,1,8,64,768]{4,3,2,1,0:T(8,128)(2,1)S(1)}, bf16[4,1,8,64,768]{4,3,2,1,0:T(8,128)(2,1)}, u32[]{:S(2)}) copy-start(bf16[4,1,8,64,768]{4,3,2,1,0:T(8,128)(2,1)} %param.4) | copy-start | bytes 9437188
  12.1 2.7 %copy-start.2 = (s32[1,8,12]{2,1,0:T(8,128)S(1)}, s32[1,8,12]{2,1,0:T(8,128)}, u32[]{:S(2)}) copy-start(s32[1,8,12]{2,1,0:T(8,128)} %param.5) | copy-start | bytes 1156
  19.8 4.3 %collective-permute-start.3 = (bf16[3,8,32,128]{3,2,1,0:T(8,128)(2,1)S(1)}, bf16[3,8,32,128]{3,2,1,0:T(8,128)(2,1)S(1)}, u32[]{:S(2)}, u32[]{:S(2)}) collective-permute-start(bf16[3,8,32,128]{3,2,1,0:T(8,128)(2,1)S(1)} %pad_maximum_fusion.3.refs_5_), channel_id=1, source_target_pairs={{4,0},{8,4},{12,8},{16,12},{20,16},{24,20},{28,24},{0,28},{5,1},{9... | collective-permute-start | bytes 589832 | tf_op jit(solution)/shard_map/ppermute | solution.py:203
  19.9 8.1 %collective-permute-start.2 = (bf16[3,8,32,128]{3,2,1,0:T(8,128)(2,1)S(1)}, bf16[3,8,32,128]{3,2,1,0:T(8,128)(2,1)S(1)}, u32[]{:S(2)}, u32[]{:S(2)}) collective-permute-start(bf16[3,8,32,128]{3,2,1,0:T(8,128)(2,1)S(1)} %pad_maximum_fusion.2.refs_6_), channel_id=1, source_target_pairs={{0,4},{4,8},{8,12},{12,16},{16,20},{20,24},{24,28},{28,0},{1,5},{5... | collective-permute-start | bytes 589832 | tf_op jit(solution)/shard_map/ppermute | solution.py:203
  29.5 16.7 %collective-permute-start.4 = (bf16[4,8,32,128]{3,2,1,0:T(8,128)(2,1)S(1)}, bf16[4,8,32,128]{3,2,1,0:T(8,128)(2,1)S(1)}, u32[]{:S(2)}, u32[]{:S(2)}) collective-permute-start(bf16[4,8,32,128]{3,2,1,0:T(8,128)(2,1)S(1)} %edge_half0.4.refs_2_.first_ref), channel_id=1, source_target_pairs={{1,0},{2,1},{3,2},{0,3},{5,4},{6,5},{7,6},{4,7},{9,8},{10,9},{11,1... | collective-permute-start | bytes 786440 | tf_op jit(solution)/shard_map/ppermute | solution.py:203
  31.5 14.8 %collective-permute-start.5 = (bf16[4,8,32,128]{3,2,1,0:T(8,128)(2,1)S(1)}, bf16[4,8,32,128]{3,2,1,0:T(8,128)(2,1)S(1)}, u32[]{:S(2)}, u32[]{:S(2)}) collective-permute-start(bf16[4,8,32,128]{3,2,1,0:T(8,128)(2,1)S(1)} %edge_half0.4.refs_2_.first_ref), channel_id=1, source_target_pairs={{0,1},{1,2},{2,3},{3,0},{4,5},{5,6},{6,7},{7,4},{8,9},{9,10},{10,1... | collective-permute-start | bytes 786440 | tf_op jit(solution)/shard_map/ppermute | solution.py:203
  33.7 5.3 %collective-permute-start.9 = (bf16[3,8,32,128]{3,2,1,0:T(8,128)(2,1)S(1)}, bf16[3,8,32,128]{3,2,1,0:T(8,128)(2,1)S(1)}, u32[]{:S(2)}, u32[]{:S(2)}) collective-permute-start(bf16[3,8,32,128]{3,2,1,0:T(8,128)(2,1)S(1)} %pad_maximum_fusion.5.refs_5_), channel_id=1, source_target_pairs={{4,0},{8,4},{12,8},{16,12},{20,16},{24,20},{28,24},{0,28},{5,1},{9... | collective-permute-start | bytes 589832 | tf_op jit(solution)/shard_map/ppermute | solution.py:203
  33.8 7.1 %collective-permute-start.8 = (bf16[3,8,32,128]{3,2,1,0:T(8,128)(2,1)S(1)}, bf16[3,8,32,128]{3,2,1,0:T(8,128)(2,1)S(1)}, u32[]{:S(2)}, u32[]{:S(2)}) collective-permute-start(bf16[3,8,32,128]{3,2,1,0:T(8,128)(2,1)S(1)} %pad_maximum_fusion.4.refs_6_), channel_id=1, source_target_pairs={{0,4},{4,8},{8,12},{12,16},{16,20},{20,24},{24,28},{28,0},{1,5},{5... | collective-permute-start | bytes 589832 | tf_op jit(solution)/shard_map/ppermute | solution.py:203
  42.4 14.3 %collective-permute-start.14 = (bf16[4,8,32,128]{3,2,1,0:T(8,128)(2,1)S(1)}, bf16[4,8,32,128]{3,2,1,0:T(8,128)(2,1)S(1)}, u32[]{:S(2)}, u32[]{:S(2)}) collective-permute-start(bf16[4,8,32,128]{3,2,1,0:T(8,128)(2,1)S(1)} %edge_half1.4.second_ref.refs_2_), channel_id=1, source_target_pairs={{0,1},{1,2},{2,3},{3,0},{4,5},{5,6},{6,7},{7,4},{8,9},{9,10},{10,1... | collective-permute-start | bytes 786440 | tf_op jit(solution)/shard_map/ppermute | solution.py:203
  44.1 12.6 %collective-permute-start.15 = (bf16[4,8,32,128]{3,2,1,0:T(8,128)(2,1)S(1)}, bf16[4,8,32,128]{3,2,1,0:T(8,128)(2,1)S(1)}, u32[]{:S(2)}, u32[]{:S(2)}) collective-permute-start(bf16[4,8,32,128]{3,2,1,0:T(8,128)(2,1)S(1)} %edge_half1.4.second_ref.refs_2_), channel_id=1, source_target_pairs={{1,0},{2,1},{3,2},{0,3},{5,4},{6,5},{7,6},{4,7},{9,8},{10,9},{11,1... | collective-permute-start | bytes 786440 | tf_op jit(solution)/shard_map/ppermute | solution.py:203
  46.4 5.3 %collective-permute-start.11 = (bf16[3,8,32,128]{3,2,1,0:T(8,128)(2,1)S(1)}, bf16[3,8,32,128]{3,2,1,0:T(8,128)(2,1)S(1)}, u32[]{:S(2)}, u32[]{:S(2)}) collective-permute-start(bf16[3,8,32,128]{3,2,1,0:T(8,128)(2,1)S(1)} %pad_maximum_fusion.7.refs_5_), channel_id=1, source_target_pairs={{4,0},{8,4},{12,8},{16,12},{20,16},{24,20},{28,24},{0,28},{5,1},{9... | collective-permute-start | bytes 589832 | tf_op jit(solution)/shard_map/ppermute | solution.py:203
  47.0 6.0 %collective-permute-start.10 = (bf16[3,8,32,128]{3,2,1,0:T(8,128)(2,1)S(1)}, bf16[3,8,32,128]{3,2,1,0:T(8,128)(2,1)S(1)}, u32[]{:S(2)}, u32[]{:S(2)}) collective-permute-start(bf16[3,8,32,128]{3,2,1,0:T(8,128)(2,1)S(1)} %pad_maximum_fusion.6.refs_6_), channel_id=1, source_target_pairs={{0,4},{4,8},{8,12},{12,16},{16,20},{20,24},{24,28},{28,0},{1,5},{5... | collective-permute-start | bytes 589832 | tf_op jit(solution)/shard_map/ppermute | solution.py:203
  54.6 19.7 %collective-permute-start.12 = (bf16[4,8,32,128]{3,2,1,0:T(8,128)(2,1)S(1)}, bf16[4,8,32,128]{3,2,1,0:T(8,128)(2,1)S(1)}, u32[]{:S(2)}, u32[]{:S(2)}) collective-permute-start(bf16[4,8,32,128]{3,2,1,0:T(8,128)(2,1)S(1)} %edge_half0.5.refs_2_.first_ref), channel_id=1, source_target_pairs={{1,0},{2,1},{3,2},{0,3},{5,4},{6,5},{7,6},{4,7},{9,8},{10,9},{11,1... | collective-permute-start | bytes 786440 | tf_op jit(solution)/shard_map/ppermute | solution.py:203
  56.3 17.9 %collective-permute-start.13 = (bf16[4,8,32,128]{3,2,1,0:T(8,128)(2,1)S(1)}, bf16[4,8,32,128]{3,2,1,0:T(8,128)(2,1)S(1)}, u32[]{:S(2)}, u32[]{:S(2)}) collective-permute-start(bf16[4,8,32,128]{3,2,1,0:T(8,128)(2,1)S(1)} %edge_half0.5.refs_2_.first_ref), channel_id=1, source_target_pairs={{0,1},{1,2},{2,3},{3,0},{4,5},{5,6},{6,7},{7,4},{8,9},{9,10},{10,1... | collective-permute-start | bytes 786440 | tf_op jit(solution)/shard_map/ppermute | solution.py:203
  56.8 6.4 %collective-permute-start.17 = (bf16[3,8,32,128]{3,2,1,0:T(8,128)(2,1)S(1)}, bf16[3,8,32,128]{3,2,1,0:T(8,128)(2,1)S(1)}, u32[]{:S(2)}, u32[]{:S(2)}) collective-permute-start(bf16[3,8,32,128]{3,2,1,0:T(8,128)(2,1)S(1)} %pad_maximum_fusion.9.refs_5_), channel_id=1, source_target_pairs={{4,0},{8,4},{12,8},{16,12},{20,16},{24,20},{28,24},{0,28},{5,1},{9... | collective-permute-start | bytes 589832 | tf_op jit(solution)/shard_map/ppermute | solution.py:203
  58.6 10.3 %collective-permute-start.16 = (bf16[3,8,32,128]{3,2,1,0:T(8,128)(2,1)S(1)}, bf16[3,8,32,128]{3,2,1,0:T(8,128)(2,1)S(1)}, u32[]{:S(2)}, u32[]{:S(2)}) collective-permute-start(bf16[3,8,32,128]{3,2,1,0:T(8,128)(2,1)S(1)} %pad_maximum_fusion.8.refs_6_), channel_id=1, source_target_pairs={{0,4},{4,8},{8,12},{12,16},{16,20},{20,24},{24,28},{28,0},{1,5},{5... | collective-permute-start | bytes 589832 | tf_op jit(solution)/shard_map/ppermute | solution.py:203
  70.4 14.6 %collective-permute-start.22 = (bf16[4,8,32,128]{3,2,1,0:T(8,128)(2,1)S(1)}, bf16[4,8,32,128]{3,2,1,0:T(8,128)(2,1)S(1)}, u32[]{:S(2)}, u32[]{:S(2)}) collective-permute-start(bf16[4,8,32,128]{3,2,1,0:T(8,128)(2,1)S(1)} %edge_half1.5.second_ref.refs_2_), channel_id=1, source_target_pairs={{0,1},{1,2},{2,3},{3,0},{4,5},{5,6},{6,7},{7,4},{8,9},{9,10},{10,1... | collective-permute-start | bytes 786440 | tf_op jit(solution)/shard_map/ppermute | solution.py:203
  72.4 12.6 %collective-permute-start.23 = (bf16[4,8,32,128]{3,2,1,0:T(8,128)(2,1)S(1)}, bf16[4,8,32,128]{3,2,1,0:T(8,128)(2,1)S(1)}, u32[]{:S(2)}, u32[]{:S(2)}) collective-permute-start(bf16[4,8,32,128]{3,2,1,0:T(8,128)(2,1)S(1)} %edge_half1.5.second_ref.refs_2_), channel_id=1, source_target_pairs={{1,0},{2,1},{3,2},{0,3},{5,4},{6,5},{7,6},{4,7},{9,8},{10,9},{11,1... | collective-permute-start | bytes 786440 | tf_op jit(solution)/shard_map/ppermute | solution.py:203
  74.4 5.3 %collective-permute-start.19 = (bf16[3,8,32,128]{3,2,1,0:T(8,128)(2,1)S(1)}, bf16[3,8,32,128]{3,2,1,0:T(8,128)(2,1)S(1)}, u32[]{:S(2)}, u32[]{:S(2)}) collective-permute-start(bf16[3,8,32,128]{3,2,1,0:T(8,128)(2,1)S(1)} %pad_maximum_fusion.11.refs_5_), channel_id=1, source_target_pairs={{4,0},{8,4},{12,8},{16,12},{20,16},{24,20},{28,24},{0,28},{5,1},{9... | collective-permute-start | bytes 589832 | tf_op jit(solution)/shard_map/ppermute | solution.py:203
  74.5 7.0 %collective-permute-start.18 = (bf16[3,8,32,128]{3,2,1,0:T(8,128)(2,1)S(1)}, bf16[3,8,32,128]{3,2,1,0:T(8,128)(2,1)S(1)}, u32[]{:S(2)}, u32[]{:S(2)}) collective-permute-start(bf16[3,8,32,128]{3,2,1,0:T(8,128)(2,1)S(1)} %pad_maximum_fusion.10.refs_6_), channel_id=1, source_target_pairs={{0,4},{4,8},{8,12},{12,16},{16,20},{20,24},{24,28},{28,0},{1,5},{5... | collective-permute-start | bytes 589832 | tf_op jit(solution)/shard_map/ppermute | solution.py:203
  82.9 16.0 %collective-permute-start.20 = (bf16[4,8,32,128]{3,2,1,0:T(8,128)(2,1)S(1)}, bf16[4,8,32,128]{3,2,1,0:T(8,128)(2,1)S(1)}, u32[]{:S(2)}, u32[]{:S(2)}) collective-permute-start(bf16[4,8,32,128]{3,2,1,0:T(8,128)(2,1)S(1)} %edge_half0.6.refs_2_.first_ref), channel_id=1, source_target_pairs={{1,0},{2,1},{3,2},{0,3},{5,4},{6,5},{7,6},{4,7},{9,8},{10,9},{11,1... | collective-permute-start | bytes 786440 | tf_op jit(solution)/shard_map/ppermute | solution.py:203
  83.3 15.7 %collective-permute-start.21 = (bf16[4,8,32,128]{3,2,1,0:T(8,128)(2,1)S(1)}, bf16[4,8,32,128]{3,2,1,0:T(8,128)(2,1)S(1)}, u32[]{:S(2)}, u32[]{:S(2)}) collective-permute-start(bf16[4,8,32,128]{3,2,1,0:T(8,128)(2,1)S(1)} %edge_half0.6.refs_2_.first_ref), channel_id=1, source_target_pairs={{0,1},{1,2},{2,3},{3,0},{4,5},{5,6},{6,7},{7,4},{8,9},{9,10},{10,1... | collective-permute-start | bytes 786440 | tf_op jit(solution)/shard_map/ppermute | solution.py:203
  85.1 5.4 %collective-permute-start.25 = (bf16[3,8,32,128]{3,2,1,0:T(8,128)(2,1)S(1)}, bf16[3,8,32,128]{3,2,1,0:T(8,128)(2,1)S(1)}, u32[]{:S(2)}, u32[]{:S(2)}) collective-permute-start(bf16[3,8,32,128]{3,2,1,0:T(8,128)(2,1)S(1)} %pad_maximum_fusion.13.refs_5_), channel_id=1, source_target_pairs={{4,0},{8,4},{12,8},{16,12},{20,16},{24,20},{28,24},{0,28},{5,1},{9... | collective-permute-start | bytes 589832 | tf_op jit(solution)/shard_map/ppermute | solution.py:203
  85.6 7.9 %collective-permute-start.24 = (bf16[3,8,32,128]{3,2,1,0:T(8,128)(2,1)S(1)}, bf16[3,8,32,128]{3,2,1,0:T(8,128)(2,1)S(1)}, u32[]{:S(2)}, u32[]{:S(2)}) collective-permute-start(bf16[3,8,32,128]{3,2,1,0:T(8,128)(2,1)S(1)} %pad_maximum_fusion.12.refs_6_), channel_id=1, source_target_pairs={{0,4},{4,8},{8,12},{12,16},{16,20},{20,24},{24,28},{28,0},{1,5},{5... | collective-permute-start | bytes 589832 | tf_op jit(solution)/shard_map/ppermute | solution.py:203
  95.1 6.8 %collective-permute-start.28 = (bf16[2,8,32,128]{3,2,1,0:T(8,128)(2,1)S(1)}, bf16[2,8,32,128]{3,2,1,0:T(8,128)(2,1)S(1)}, u32[]{:S(2)}, u32[]{:S(2)}) collective-permute-start(bf16[2,8,32,128]{3,2,1,0:T(8,128)(2,1)S(1)} %pad_maximum_fusion.18), channel_id=1, source_target_pairs={{0,1},{1,2},{2,3},{3,0},{4,5},{5,6},{6,7},{7,4},{8,9},{9,10},{10,1... | collective-permute-start | bytes 393224 | tf_op jit(solution)/shard_map/ppermute | solution.py:203
  95.3 9.8 %collective-permute-start.29 = (bf16[2,8,32,128]{3,2,1,0:T(8,128)(2,1)S(1)}, bf16[2,8,32,128]{3,2,1,0:T(8,128)(2,1)S(1)}, u32[]{:S(2)}, u32[]{:S(2)}) collective-permute-start(bf16[2,8,32,128]{3,2,1,0:T(8,128)(2,1)S(1)} %pad_maximum_fusion.18), channel_id=1, source_target_pairs={{1,0},{2,1},{3,2},{0,3},{5,4},{6,5},{7,6},{4,7},{9,8},{10,9},{11,1... | collective-permute-start | bytes 393224 | tf_op jit(solution)/shard_map/ppermute | solution.py:203
  99.1 7.8 %collective-permute-start.27 = (bf16[3,8,32,128]{3,2,1,0:T(8,128)(2,1)S(1)}, bf16[3,8,32,128]{3,2,1,0:T(8,128)(2,1)S(1)}, u32[]{:S(2)}, u32[]{:S(2)}) collective-permute-start(bf16[3,8,32,128]{3,2,1,0:T(8,128)(2,1)S(1)} %pad_maximum_fusion.15.refs_5_), channel_id=1, source_target_pairs={{4,0},{8,4},{12,8},{16,12},{20,16},{24,20},{28,24},{0,28},{5,1},{9... | collective-permute-start | bytes 589832 | tf_op jit(solution)/shard_map/ppermute | solution.py:203
  99.2 7.7 %collective-permute-start.26 = (bf16[3,8,32,128]{3,2,1,0:T(8,128)(2,1)S(1)}, bf16[3,8,32,128]{3,2,1,0:T(8,128)(2,1)S(1)}, u32[]{:S(2)}, u32[]{:S(2)}) collective-permute-start(bf16[3,8,32,128]{3,2,1,0:T(8,128)(2,1)S(1)} %pad_maximum_fusion.14.refs_6_), channel_id=1, source_target_pairs={{0,4},{4,8},{8,12},{12,16},{16,20},{20,24},{24,28},{28,0},{1,5},{5... | collective-permute-start | bytes 589832 | tf_op jit(solution)/shard_map/ppermute | solution.py:203
  101.2 8.3 %collective-permute-start.30 = (bf16[2,8,32,128]{3,2,1,0:T(8,128)(2,1)S(1)}, bf16[2,8,32,128]{3,2,1,0:T(8,128)(2,1)S(1)}, u32[]{:S(2)}, u32[]{:S(2)}) collective-permute-start(bf16[2,8,32,128]{3,2,1,0:T(8,128)(2,1)S(1)} %slice.222), channel_id=1, source_target_pairs={{0,1},{1,2},{2,3},{3,0},{4,5},{5,6},{6,7},{7,4},{8,9},{9,10},{10,1... | collective-permute-start | bytes 393224 | tf_op jit(solution)/shard_map/ppermute | solution.py:203
  101.9 7.8 %collective-permute-start.31 = (bf16[2,8,32,128]{3,2,1,0:T(8,128)(2,1)S(1)}, bf16[2,8,32,128]{3,2,1,0:T(8,128)(2,1)S(1)}, u32[]{:S(2)}, u32[]{:S(2)}) collective-permute-start(bf16[2,8,32,128]{3,2,1,0:T(8,128)(2,1)S(1)} %slice.222), channel_id=1, source_target_pairs={{1,0},{2,1},{3,2},{0,3},{5,4},{6,5},{7,6},{4,7},{9,8},{10,9},{11,1... | collective-permute-start | bytes 393224 | tf_op jit(solution)/shard_map/ppermute | solution.py:203
  105.2 7.0 %collective-permute-start.33 = (bf16[3,8,32,128]{3,2,1,0:T(8,128)(2,1)S(1)}, bf16[3,8,32,128]{3,2,1,0:T(8,128)(2,1)S(1)}, u32[]{:S(2)}, u32[]{:S(2)}) collective-permute-start(bf16[3,8,32,128]{3,2,1,0:T(8,128)(2,1)S(1)} %pad_maximum_fusion.17.refs_5_), channel_id=1, source_target_pairs={{4,0},{8,4},{12,8},{16,12},{20,16},{24,20},{28,24},{0,28},{5,1},{9... | collective-permute-start | bytes 589832 | tf_op jit(solution)/shard_map/ppermute | solution.py:203
  106.8 6.0 %collective-permute-start.32 = (bf16[3,8,32,128]{3,2,1,0:T(8,128)(2,1)S(1)}, bf16[3,8,32,128]{3,2,1,0:T(8,128)(2,1)S(1)}, u32[]{:S(2)}, u32[]{:S(2)}) collective-permute-start(bf16[3,8,32,128]{3,2,1,0:T(8,128)(2,1)S(1)} %pad_maximum_fusion.16.refs_6_), channel_id=1, source_target_pairs={{0,4},{4,8},{8,12},{12,16},{16,20},{20,24},{24,28},{28,0},{1,5},{5... | collective-permute-start | bytes 589832 | tf_op jit(solution)/shard_map/ppermute | solution.py:203
